TPU v7x, 32 devices: a whole 2x2x4 slice. The times are simulated.
32 devices in a mesh: section: 4 (over y, core), block: 8 (over z, x).
Axes of the slice: x: 2, y: 2, z: 4, core: 2. Of those that a mesh axis runs over, the one named last changes fastest.
Arguments:
- inputs: bfloat16 [4, 16384, 128], P('section', 'block'), may hold values from -6 to 6
- cotangent: bfloat16 [4, 16384, 128], P('section', 'block'), may hold values from -6 to 6
- right_factor: bfloat16 [2, 4, 128, 128, 128], P(None, 'section', 'block'), may hold values from -0.5 to 0.5
- left_factor: bfloat16 [2, 4, 128, 128, 128], P(None, 'section', 'block'), may hold values from -0.5 to 0.5
Outputs:
- outputs: bfloat16 [4, 16384, 128], P('section', 'block')
- input_grad: bfloat16 [4, 16384, 128], P('section', 'block')
- right_grad: float32 [2, 4, 128, 128, 128], P(None, 'section', 'block')
- left_grad: float32 [2, 4, 128, 128, 128], P(None, 'section', 'block')
All inputs are finite; a program needn't handle non-finite values.
Results may differ from a plain program's by a relative error of at most 0.04.
Values may be sent and summed in bfloat16 or wider, within the bound.
No kernel may reach another device: no remote copies, remote signals or barrier semaphores. Data moves between devices by JAX's collectives and lax.ppermute only.
A program may use at most 64 MiB of HBM per device.

v0:
```python
import jax
import jax.numpy as jnp
from jax import lax
from jax.sharding import PartitionSpec as P


def shifted(x, axis, by):
    peers = lax.axis_size(axis)
    return lax.ppermute(x, axis, [(i, (i + by) % peers) for i in range(peers)])


def first_factor(right_block, acts):
    return jnp.einsum("bjk,bjr->bkr", right_block, acts, preferred_element_type=jnp.float32).astype(
        jnp.bfloat16
    )


def silu_slope(values):
    sigmoid = jax.nn.sigmoid(values)
    return sigmoid * (1.0 + values * (1.0 - sigmoid))


def body(inputs, cotangent, right_factor, left_factor):
    section_count = lax.axis_size("section")
    section_index = lax.axis_index("section")
    loop_count = right_factor.shape[0]
    own_blocks = right_factor.shape[2]
    block_size = right_factor.shape[3]
    row_count = inputs.shape[2]
    layer_count = loop_count * section_count
    tick_count = layer_count + section_count
    right_local = right_factor[:, 0]
    left_local = left_factor[:, 0]
    tick_list = jnp.arange(tick_count, dtype=jnp.int32)

    def pick_weights(loop_index):
        right_block = lax.dynamic_index_in_dim(right_local, loop_index, 0, keepdims=False)
        left_block = lax.dynamic_index_in_dim(left_local, loop_index, 0, keepdims=False)
        return (right_block, left_block)

    def forward_tick(carried, tick):
        micro_index = jnp.remainder(tick - section_index, section_count)
        layer_index = tick - micro_index
        active = (layer_index >= 0) & (layer_index < layer_count)
        loop_index = jnp.clip(layer_index // section_count, 0, loop_count - 1)
        right_block, left_block = pick_weights(loop_index)
        mixed = first_factor(right_block, carried)
        columns = lax.all_to_all(mixed, "block", split_axis=1, concat_axis=0, tiled=True)
        activated = jax.nn.silu(columns.astype(jnp.float32)).astype(jnp.bfloat16)
        second = jnp.einsum(
            "kbc,bkr->ckr", left_block, activated, preferred_element_type=jnp.float32
        ).astype(jnp.bfloat16)
        returned = lax.all_to_all(second, "block", split_axis=0, concat_axis=1, tiled=True)
        updated = (carried.astype(jnp.float32) + returned.astype(jnp.float32)).astype(jnp.bfloat16)
        updated = jnp.where(active, updated, carried)
        moved = shifted(updated, "section", 1)
        return (moved, (carried,))

    start = inputs[0].reshape(own_blocks, block_size, row_count)
    finished, stored = lax.scan(forward_tick, start, tick_list)
    stored_inputs = stored[0]

    def backward_tick(carry_all, tick):
        grad_carried, right_grad, left_grad = carry_all
        slot_index = jnp.remainder(section_index + tick, section_count)
        delay = jnp.remainder(slot_index + 1, section_count)
        layer_index = layer_count - 1 - tick + delay
        active = (tick >= delay) & (tick - delay <= layer_count - 1)
        loop_index = jnp.clip(layer_index // section_count, 0, loop_count - 1)
        right_block, left_block = pick_weights(loop_index)
        source_tick = jnp.clip(
            layer_index + jnp.remainder(-slot_index, section_count), 0, tick_count - 1
        )
        layer_input = lax.dynamic_index_in_dim(stored_inputs, source_tick, 0, keepdims=False)
        columns, grad_columns = (
            lax.all_to_all(
                first_factor(right_block, layer_input),
                "block",
                split_axis=1,
                concat_axis=0,
                tiled=True,
            ),
            lax.all_to_all(grad_carried, "block", split_axis=1, concat_axis=0, tiled=True),
        )
        column_wide = columns.astype(jnp.float32)
        activated = jax.nn.silu(column_wide).astype(jnp.bfloat16)
        left_term = jnp.einsum(
            "bkr,ckr->kbc", activated, grad_columns, preferred_element_type=jnp.float32
        )
        grad_act = jnp.einsum(
            "kbc,ckr->bkr", left_block, grad_columns, preferred_element_type=jnp.float32
        )
        grad_mixed = (grad_act * silu_slope(column_wide)).astype(jnp.bfloat16)
        grad_back = lax.all_to_all(grad_mixed, "block", split_axis=0, concat_axis=1, tiled=True)
        right_term = jnp.einsum(
            "bjr,bkr->bjk", layer_input, grad_back, preferred_element_type=jnp.float32
        )
        branch = jnp.einsum(
            "bjk,bkr->bjr", right_block, grad_back, preferred_element_type=jnp.float32
        )
        grad_in = (grad_carried.astype(jnp.float32) + branch).astype(jnp.bfloat16)
        grad_in = jnp.where(active, grad_in, grad_carried)
        selector = (jnp.arange(loop_count) == loop_index).astype(jnp.float32) * active.astype(
            jnp.float32
        )
        right_grad = right_grad + selector[:, None, None, None] * right_term[None]
        left_grad = left_grad + selector[:, None, None, None] * left_term[None]
        moved = shifted(grad_in, "section", -1)
        return ((moved, right_grad, left_grad), None)

    grad_start = cotangent[0].reshape(own_blocks, block_size, row_count)
    right_zero = jnp.zeros(right_local.shape, jnp.float32)
    left_zero = jnp.zeros(left_local.shape, jnp.float32)
    (grad_final, right_grad, left_grad), unused = lax.scan(
        backward_tick, (grad_start, right_zero, left_zero), tick_list
    )
    outputs = finished.reshape(1, own_blocks * block_size, row_count)
    input_grad = grad_final.reshape(1, own_blocks * block_size, row_count)
    return (outputs, input_grad, right_grad[:, None], left_grad[:, None])


def solution(mesh):
    in_specs = (
        P("section", "block", None),
        P("section", "block", None),
        P(None, "section", "block", None, None),
        P(None, "section", "block", None, None),
    )
    out_specs = (
        P("section", "block", None),
        P("section", "block", None),
        P(None, "section", "block", None, None),
        P(None, "section", "block", None, None),
    )
    return jax.shard_map(body, mesh=mesh, in_specs=in_specs, out_specs=out_specs, check_vma=False)
```

profile of v0, /device:TPU:0, one launch (start us, length us, event | category | flops | bytes accessed | tf_op | source)
XLA Modules:
  0.0 1484.2 jit_solution(3055339775748443303)
XLA Ops:
  2.6 596.1 %while.31 = (s32[]{:T(128)}, bf16[16,128,128]{2,1,0:T(8,128)(2,1)S(1)}, bf16[12,16,128,128]{3,2,1,0:T(8,128)(2,1)}, s32[12]{0:T(128)S(1)}, s32[]{:T(128)}, /*ind...) while((s32[]{:T(128)}, ...), condition=%wide.region_1.2_spmd, body=%wide.region_0.1_spmd.sunk | while | flops 137625632 | bytes 28312144 | solution.py:60
  5.2 21.6 %all_to_all.131 = bf16[16,128,128]{2,0,1:T(8,128)(2,1)S(1)} all-to-all(bf16[16,128,128]{2,0,1:T(8,128)(2,1)S(1)} %copy.74), channel_id=1, replica_groups=mesh['section'=4,'block'=8] {'block'}, dimensions={1} | all-to-all | bytes 1048576 | tf_op jit(solution)/shard_map/while/body/eval_jaxpr/all_to_all | solution.py:48
  33.4 14.2 all-to-all-done.1
  59.3 17.2 %all_to_all.131 = bf16[16,128,128]{2,0,1:T(8,128)(2,1)S(1)} all-to-all(bf16[16,128,128]{2,0,1:T(8,128)(2,1)S(1)} %copy.74), channel_id=1, replica_groups=mesh['section'=4,'block'=8] {'block'}, dimensions={1} | all-to-all | bytes 1048576 | tf_op jit(solution)/shard_map/while/body/eval_jaxpr/all_to_all | solution.py:48
  83.2 14.0 all-to-all-done.1
  108.9 15.9 %all_to_all.131 = bf16[16,128,128]{2,0,1:T(8,128)(2,1)S(1)} all-to-all(bf16[16,128,128]{2,0,1:T(8,128)(2,1)S(1)} %copy.74), channel_id=1, replica_groups=mesh['section'=4,'block'=8] {'block'}, dimensions={1} | all-to-all | bytes 1048576 | tf_op jit(solution)/shard_map/while/body/eval_jaxpr/all_to_all | solution.py:48
  131.5 13.4 all-to-all-done.1
  156.5 18.2 %all_to_all.131 = bf16[16,128,128]{2,0,1:T(8,128)(2,1)S(1)} all-to-all(bf16[16,128,128]{2,0,1:T(8,128)(2,1)S(1)} %copy.74), channel_id=1, replica_groups=mesh['section'=4,'block'=8] {'block'}, dimensions={1} | all-to-all | bytes 1048576 | tf_op jit(solution)/shard_map/while/body/eval_jaxpr/all_to_all | solution.py:48
  181.4 14.2 all-to-all-done.1
  207.3 15.4 %all_to_all.131 = bf16[16,128,128]{2,0,1:T(8,128)(2,1)S(1)} all-to-all(bf16[16,128,128]{2,0,1:T(8,128)(2,1)S(1)} %copy.74), channel_id=1, replica_groups=mesh['section'=4,'block'=8] {'block'}, dimensions={1} | all-to-all | bytes 1048576 | tf_op jit(solution)/shard_map/while/body/eval_jaxpr/all_to_all | solution.py:48
  229.4 13.3 all-to-all-done.1
  254.3 18.9 %all_to_all.131 = bf16[16,128,128]{2,0,1:T(8,128)(2,1)S(1)} all-to-all(bf16[16,128,128]{2,0,1:T(8,128)(2,1)S(1)} %copy.74), channel_id=1, replica_groups=mesh['section'=4,'block'=8] {'block'}, dimensions={1} | all-to-all | bytes 1048576 | tf_op jit(solution)/shard_map/while/body/eval_jaxpr/all_to_all | solution.py:48
  279.9 14.2 all-to-all-done.1
  305.8 15.4 %all_to_all.131 = bf16[16,128,128]{2,0,1:T(8,128)(2,1)S(1)} all-to-all(bf16[16,128,128]{2,0,1:T(8,128)(2,1)S(1)} %copy.74), channel_id=1, replica_groups=mesh['section'=4,'block'=8] {'block'}, dimensions={1} | all-to-all | bytes 1048576 | tf_op jit(solution)/shard_map/while/body/eval_jaxpr/all_to_all | solution.py:48
  327.9 13.3 all-to-all-done.1
  352.9 18.9 %all_to_all.131 = bf16[16,128,128]{2,0,1:T(8,128)(2,1)S(1)} all-to-all(bf16[16,128,128]{2,0,1:T(8,128)(2,1)S(1)} %copy.74), channel_id=1, replica_groups=mesh['section'=4,'block'=8] {'block'}, dimensions={1} | all-to-all | bytes 1048576 | tf_op jit(solution)/shard_map/while/body/eval_jaxpr/all_to_all | solution.py:48
  378.4 14.2 all-to-all-done.1
  404.3 15.4 %all_to_all.131 = bf16[16,128,128]{2,0,1:T(8,128)(2,1)S(1)} all-to-all(bf16[16,128,128]{2,0,1:T(8,128)(2,1)S(1)} %copy.74), channel_id=1, replica_groups=mesh['section'=4,'block'=8] {'block'}, dimensions={1} | all-to-all | bytes 1048576 | tf_op jit(solution)/shard_map/while/body/eval_jaxpr/all_to_all | solution.py:48
  426.4 13.3 all-to-all-done.1
  451.4 18.9 %all_to_all.131 = bf16[16,128,128]{2,0,1:T(8,128)(2,1)S(1)} all-to-all(bf16[16,128,128]{2,0,1:T(8,128)(2,1)S(1)} %copy.74), channel_id=1, replica_groups=mesh['section'=4,'block'=8] {'block'}, dimensions={1} | all-to-all | bytes 1048576 | tf_op jit(solution)/shard_map/while/body/eval_jaxpr/all_to_all | solution.py:48
  477.0 14.2 all-to-all-done.1
  502.8 15.4 %all_to_all.131 = bf16[16,128,128]{2,0,1:T(8,128)(2,1)S(1)} all-to-all(bf16[16,128,128]{2,0,1:T(8,128)(2,1)S(1)} %copy.74), channel_id=1, replica_groups=mesh['section'=4,'block'=8] {'block'}, dimensions={1} | all-to-all | bytes 1048576 | tf_op jit(solution)/shard_map/while/body/eval_jaxpr/all_to_all | solution.py:48
  524.9 13.3 all-to-all-done.1
  549.9 18.9 %all_to_all.131 = bf16[16,128,128]{2,0,1:T(8,128)(2,1)S(1)} all-to-all(bf16[16,128,128]{2,0,1:T(8,128)(2,1)S(1)} %copy.74), channel_id=1, replica_groups=mesh['section'=4,'block'=8] {'block'}, dimensions={1} | all-to-all | bytes 1048576 | tf_op jit(solution)/shard_map/while/body/eval_jaxpr/all_to_all | solution.py:48
  575.5 14.2 all-to-all-done.1
  599.6 883.9 %while.32 = (s32[]{:T(128)}, bf16[16,128,128]{2,1,0:T(8,128)(2,1)S(1)}, f32[2,16,128,128]{3,2,1,0:T(8,128)}, f32[2,16,128,128]{3,2,1,0:T(8,128)}, s32[12]{0:T(12...) while((s32[]{:T(128)}, ...), condition=%wide.region_3.4_spmd.clone, body=%wide.region_2.3_spmd.clone.sunk | while | flops 342884416 | bytes 70779976 | solution.py:114
  679.3 14.7 all-to-all-done.2
  699.6 13.5 all-to-all-done.3
  752.9 14.6 all-to-all-done.2
  773.1 13.7 all-to-all-done.3
  827.0 15.0 %all-to-all-done.2 = bf16[16,128,128]{2,0,1:T(8,128)(2,1)S(1)} async-done(((bf16[16,128,128]{2,0,1:T(8,128)(2,1)}), bf16[16,128,128]{2,0,1:T(8,128)(2,1)S(1)}, u32[]{:S(2)}, u32[]{:S(2)}) %all-to-all-start.2) | async-done | bytes 524320 | tf_op jit(solution)/shard_map/while/body/eval_jaxpr/all_to_all | solution.py:76
  847.5 13.6 all-to-all-done.3
  901.0 14.7 all-to-all-done.2
  921.2 13.7 all-to-all-done.3
  975.1 14.9 %all-to-all-done.2 = bf16[16,128,128]{2,0,1:T(8,128)(2,1)S(1)} async-done(((bf16[16,128,128]{2,0,1:T(8,128)(2,1)}), bf16[16,128,128]{2,0,1:T(8,128)(2,1)S(1)}, u32[]{:S(2)}, u32[]{:S(2)}) %all-to-all-start.2) | async-done | bytes 524320 | tf_op jit(solution)/shard_map/while/body/eval_jaxpr/all_to_all | solution.py:76
  995.5 13.6 all-to-all-done.3
  1049.0 14.7 all-to-all-done.2
  1069.2 13.7 all-to-all-done.3
  1123.2 14.9 %all-to-all-done.2 = bf16[16,128,128]{2,0,1:T(8,128)(2,1)S(1)} async-done(((bf16[16,128,128]{2,0,1:T(8,128)(2,1)}), bf16[16,128,128]{2,0,1:T(8,128)(2,1)S(1)}, u32[]{:S(2)}, u32[]{:S(2)}) %all-to-all-start.2) | async-done | bytes 524320 | tf_op jit(solution)/shard_map/while/body/eval_jaxpr/all_to_all | solution.py:76
  1143.6 13.6 all-to-all-done.3
  1197.0 14.7 all-to-all-done.2
  1217.3 13.7 all-to-all-done.3
  1271.2 14.9 %all-to-all-done.2 = bf16[16,128,128]{2,0,1:T(8,128)(2,1)S(1)} async-done(((bf16[16,128,128]{2,0,1:T(8,128)(2,1)}), bf16[16,128,128]{2,0,1:T(8,128)(2,1)S(1)}, u32[]{:S(2)}, u32[]{:S(2)}) %all-to-all-start.2) | async-done | bytes 524320 | tf_op jit(solution)/shard_map/while/body/eval_jaxpr/all_to_all | solution.py:76
  1291.6 13.6 all-to-all-done.3
  1345.1 14.7 all-to-all-done.2
  1365.3 13.7 all-to-all-done.3
  1419.3 14.8 %all-to-all-done.2 = bf16[16,128,128]{2,0,1:T(8,128)(2,1)S(1)} async-done(((bf16[16,128,128]{2,0,1:T(8,128)(2,1)}), bf16[16,128,128]{2,0,1:T(8,128)(2,1)S(1)}, u32[]{:S(2)}, u32[]{:S(2)}) %all-to-all-start.2) | async-done | bytes 524320 | tf_op jit(solution)/shard_map/while/body/eval_jaxpr/all_to_all | solution.py:76
  1439.6 13.5 all-to-all-done.3
  (593 shorter events, 741.8 us)
Async XLA Ops:
  29.8 17.8 %all-to-all-start.1 = ((bf16[128,16,128]{2,1,0:T(8,128)(2,1)}), bf16[128,16,128]{2,1,0:T(8,128)(2,1)S(1)}, u32[]{:S(2)}, u32[]{:S(2)}) async-start(bf16[128,16,128]{2,1,0:T(8,128)(2,1)} %copy.77), calls=%async_computation.1 | async-start | bytes 1048576 | tf_op jit(solution)/shard_map/while/body/eval_jaxpr/all_to_all | solution.py:53
  79.5 17.7 %all-to-all-start.1 = ((bf16[128,16,128]{2,1,0:T(8,128)(2,1)}), bf16[128,16,128]{2,1,0:T(8,128)(2,1)S(1)}, u32[]{:S(2)}, u32[]{:S(2)}) async-start(bf16[128,16,128]{2,1,0:T(8,128)(2,1)} %copy.77), calls=%async_computation.1 | async-start | bytes 1048576 | tf_op jit(solution)/shard_map/while/body/eval_jaxpr/all_to_all | solution.py:53
  127.8 17.0 %all-to-all-start.1 = ((bf16[128,16,128]{2,1,0:T(8,128)(2,1)}), bf16[128,16,128]{2,1,0:T(8,128)(2,1)S(1)}, u32[]{:S(2)}, u32[]{:S(2)}) async-start(bf16[128,16,128]{2,1,0:T(8,128)(2,1)} %copy.77), calls=%async_computation.1 | async-start | bytes 1048576 | tf_op jit(solution)/shard_map/while/body/eval_jaxpr/all_to_all | solution.py:53
  177.8 17.8 %all-to-all-start.1 = ((bf16[128,16,128]{2,1,0:T(8,128)(2,1)}), bf16[128,16,128]{2,1,0:T(8,128)(2,1)S(1)}, u32[]{:S(2)}, u32[]{:S(2)}) async-start(bf16[128,16,128]{2,1,0:T(8,128)(2,1)} %copy.77), calls=%async_computation.1 | async-start | bytes 1048576 | tf_op jit(solution)/shard_map/while/body/eval_jaxpr/all_to_all | solution.py:53
  225.7 17.0 %all-to-all-start.1 = ((bf16[128,16,128]{2,1,0:T(8,128)(2,1)}), bf16[128,16,128]{2,1,0:T(8,128)(2,1)S(1)}, u32[]{:S(2)}, u32[]{:S(2)}) async-start(bf16[128,16,128]{2,1,0:T(8,128)(2,1)} %copy.77), calls=%async_computation.1 | async-start | bytes 1048576 | tf_op jit(solution)/shard_map/while/body/eval_jaxpr/all_to_all | solution.py:53
  276.3 17.8 %all-to-all-start.1 = ((bf16[128,16,128]{2,1,0:T(8,128)(2,1)}), bf16[128,16,128]{2,1,0:T(8,128)(2,1)S(1)}, u32[]{:S(2)}, u32[]{:S(2)}) async-start(bf16[128,16,128]{2,1,0:T(8,128)(2,1)} %copy.77), calls=%async_computation.1 | async-start | bytes 1048576 | tf_op jit(solution)/shard_map/while/body/eval_jaxpr/all_to_all | solution.py:53
  324.2 17.0 %all-to-all-start.1 = ((bf16[128,16,128]{2,1,0:T(8,128)(2,1)}), bf16[128,16,128]{2,1,0:T(8,128)(2,1)S(1)}, u32[]{:S(2)}, u32[]{:S(2)}) async-start(bf16[128,16,128]{2,1,0:T(8,128)(2,1)} %copy.77), calls=%async_computation.1 | async-start | bytes 1048576 | tf_op jit(solution)/shard_map/while/body/eval_jaxpr/all_to_all | solution.py:53
  374.8 17.8 %all-to-all-start.1 = ((bf16[128,16,128]{2,1,0:T(8,128)(2,1)}), bf16[128,16,128]{2,1,0:T(8,128)(2,1)S(1)}, u32[]{:S(2)}, u32[]{:S(2)}) async-start(bf16[128,16,128]{2,1,0:T(8,128)(2,1)} %copy.77), calls=%async_computation.1 | async-start | bytes 1048576 | tf_op jit(solution)/shard_map/while/body/eval_jaxpr/all_to_all | solution.py:53
  422.7 17.0 %all-to-all-start.1 = ((bf16[128,16,128]{2,1,0:T(8,128)(2,1)}), bf16[128,16,128]{2,1,0:T(8,128)(2,1)S(1)}, u32[]{:S(2)}, u32[]{:S(2)}) async-start(bf16[128,16,128]{2,1,0:T(8,128)(2,1)} %copy.77), calls=%async_computation.1 | async-start | bytes 1048576 | tf_op jit(solution)/shard_map/while/body/eval_jaxpr/all_to_all | solution.py:53
  473.3 17.8 %all-to-all-start.1 = ((bf16[128,16,128]{2,1,0:T(8,128)(2,1)}), bf16[128,16,128]{2,1,0:T(8,128)(2,1)S(1)}, u32[]{:S(2)}, u32[]{:S(2)}) async-start(bf16[128,16,128]{2,1,0:T(8,128)(2,1)} %copy.77), calls=%async_computation.1 | async-start | bytes 1048576 | tf_op jit(solution)/shard_map/while/body/eval_jaxpr/all_to_all | solution.py:53
  521.2 17.0 %all-to-all-start.1 = ((bf16[128,16,128]{2,1,0:T(8,128)(2,1)}), bf16[128,16,128]{2,1,0:T(8,128)(2,1)S(1)}, u32[]{:S(2)}, u32[]{:S(2)}) async-start(bf16[128,16,128]{2,1,0:T(8,128)(2,1)} %copy.77), calls=%async_computation.1 | async-start | bytes 1048576 | tf_op jit(solution)/shard_map/while/body/eval_jaxpr/all_to_all | solution.py:53
  571.8 17.8 %all-to-all-start.1 = ((bf16[128,16,128]{2,1,0:T(8,128)(2,1)}), bf16[128,16,128]{2,1,0:T(8,128)(2,1)S(1)}, u32[]{:S(2)}, u32[]{:S(2)}) async-start(bf16[128,16,128]{2,1,0:T(8,128)(2,1)} %copy.77), calls=%async_computation.1 | async-start | bytes 1048576 | tf_op jit(solution)/shard_map/while/body/eval_jaxpr/all_to_all | solution.py:53
  604.2 15.6 %all-to-all-start.2 = ((bf16[16,128,128]{2,0,1:T(8,128)(2,1)}), bf16[16,128,128]{2,0,1:T(8,128)(2,1)S(1)}, u32[]{:S(2)}, u32[]{:S(2)}) async-start(bf16[16,128,128]{2,0,1:T(8,128)(2,1)} %copy.79), calls=%async_computation.2 | async-start | bytes 1048576 | tf_op jit(solution)/shard_map/while/body/eval_jaxpr/all_to_all | solution.py:76
  619.8 17.0 %all-to-all-start.3 = ((bf16[16,128,128]{2,0,1:T(8,128)(2,1)}), bf16[16,128,128]{2,0,1:T(8,128)(2,1)}, u32[]{:S(2)}, u32[]{:S(2)}) async-start(bf16[16,128,128]{2,0,1:T(8,128)(2,1)} %copy.81), calls=%async_computation.3 | async-start | bytes 1048576 | tf_op jit(solution)/shard_map/while/body/eval_jaxpr/all_to_all | solution.py:83
  640.4 17.5 %all-to-all-start.4 = ((bf16[128,16,128]{2,1,0:T(8,128)(2,1)}), bf16[128,16,128]{2,1,0:T(8,128)(2,1)}, u32[]{:S(2)}, u32[]{:S(2)}) async-start(bf16[128,16,128]{2,1,0:T(8,128)(2,1)} %copy.83), calls=%async_computation.4 | async-start | bytes 1048576 | tf_op jit(solution)/shard_map/while/body/eval_jaxpr/all_to_all | solution.py:94
  673.2 20.9 %all-to-all-start.2 = ((bf16[16,128,128]{2,0,1:T(8,128)(2,1)}), bf16[16,128,128]{2,0,1:T(8,128)(2,1)S(1)}, u32[]{:S(2)}, u32[]{:S(2)}) async-start(bf16[16,128,128]{2,0,1:T(8,128)(2,1)} %copy.79), calls=%async_computation.2 | async-start | bytes 1048576 | tf_op jit(solution)/shard_map/while/body/eval_jaxpr/all_to_all | solution.py:76
  694.1 19.0 %all-to-all-start.3 = ((bf16[16,128,128]{2,0,1:T(8,128)(2,1)}), bf16[16,128,128]{2,0,1:T(8,128)(2,1)}, u32[]{:S(2)}, u32[]{:S(2)}) async-start(bf16[16,128,128]{2,0,1:T(8,128)(2,1)} %copy.81), calls=%async_computation.3 | async-start | bytes 1048576 | tf_op jit(solution)/shard_map/while/body/eval_jaxpr/all_to_all | solution.py:83
  716.7 18.4 %all-to-all-start.4 = ((bf16[128,16,128]{2,1,0:T(8,128)(2,1)}), bf16[128,16,128]{2,1,0:T(8,128)(2,1)}, u32[]{:S(2)}, u32[]{:S(2)}) async-start(bf16[128,16,128]{2,1,0:T(8,128)(2,1)} %copy.83), calls=%async_computation.4 | async-start | bytes 1048576 | tf_op jit(solution)/shard_map/while/body/eval_jaxpr/all_to_all | solution.py:94
  748.0 19.6 %all-to-all-start.2 = ((bf16[16,128,128]{2,0,1:T(8,128)(2,1)}), bf16[16,128,128]{2,0,1:T(8,128)(2,1)S(1)}, u32[]{:S(2)}, u32[]{:S(2)}) async-start(bf16[16,128,128]{2,0,1:T(8,128)(2,1)} %copy.79), calls=%async_computation.2 | async-start | bytes 1048576 | tf_op jit(solution)/shard_map/while/body/eval_jaxpr/all_to_all | solution.py:76
  767.6 19.2 %all-to-all-start.3 = ((bf16[16,128,128]{2,0,1:T(8,128)(2,1)}), bf16[16,128,128]{2,0,1:T(8,128)(2,1)}, u32[]{:S(2)}, u32[]{:S(2)}) async-start(bf16[16,128,128]{2,0,1:T(8,128)(2,1)} %copy.81), calls=%async_computation.3 | async-start | bytes 1048576 | tf_op jit(solution)/shard_map/while/body/eval_jaxpr/all_to_all | solution.py:83
  790.3 18.4 %all-to-all-start.4 = ((bf16[128,16,128]{2,1,0:T(8,128)(2,1)}), bf16[128,16,128]{2,1,0:T(8,128)(2,1)}, u32[]{:S(2)}, u32[]{:S(2)}) async-start(bf16[128,16,128]{2,1,0:T(8,128)(2,1)} %copy.83), calls=%async_computation.4 | async-start | bytes 1048576 | tf_op jit(solution)/shard_map/while/body/eval_jaxpr/all_to_all | solution.py:94
  821.6 20.3 %all-to-all-start.2 = ((bf16[16,128,128]{2,0,1:T(8,128)(2,1)}), bf16[16,128,128]{2,0,1:T(8,128)(2,1)S(1)}, u32[]{:S(2)}, u32[]{:S(2)}) async-start(bf16[16,128,128]{2,0,1:T(8,128)(2,1)} %copy.79), calls=%async_computation.2 | async-start | bytes 1048576 | tf_op jit(solution)/shard_map/while/body/eval_jaxpr/all_to_all | solution.py:76
  842.0 19.1 %all-to-all-start.3 = ((bf16[16,128,128]{2,0,1:T(8,128)(2,1)}), bf16[16,128,128]{2,0,1:T(8,128)(2,1)}, u32[]{:S(2)}, u32[]{:S(2)}) async-start(bf16[16,128,128]{2,0,1:T(8,128)(2,1)} %copy.81), calls=%async_computation.3 | async-start | bytes 1048576 | tf_op jit(solution)/shard_map/while/body/eval_jaxpr/all_to_all | solution.py:83
  864.7 18.4 %all-to-all-start.4 = ((bf16[128,16,128]{2,1,0:T(8,128)(2,1)}), bf16[128,16,128]{2,1,0:T(8,128)(2,1)}, u32[]{:S(2)}, u32[]{:S(2)}) async-start(bf16[128,16,128]{2,1,0:T(8,128)(2,1)} %copy.83), calls=%async_computation.4 | async-start | bytes 1048576 | tf_op jit(solution)/shard_map/while/body/eval_jaxpr/all_to_all | solution.py:94
  896.0 19.7 %all-to-all-start.2 = ((bf16[16,128,128]{2,0,1:T(8,128)(2,1)}), bf16[16,128,128]{2,0,1:T(8,128)(2,1)S(1)}, u32[]{:S(2)}, u32[]{:S(2)}) async-start(bf16[16,128,128]{2,0,1:T(8,128)(2,1)} %copy.79), calls=%async_computation.2 | async-start | bytes 1048576 | tf_op jit(solution)/shard_map/while/body/eval_jaxpr/all_to_all | solution.py:76
  915.7 19.2 %all-to-all-start.3 = ((bf16[16,128,128]{2,0,1:T(8,128)(2,1)}), bf16[16,128,128]{2,0,1:T(8,128)(2,1)}, u32[]{:S(2)}, u32[]{:S(2)}) async-start(bf16[16,128,128]{2,0,1:T(8,128)(2,1)} %copy.81), calls=%async_computation.3 | async-start | bytes 1048576 | tf_op jit(solution)/shard_map/while/body/eval_jaxpr/all_to_all | solution.py:83
  938.4 18.4 %all-to-all-start.4 = ((bf16[128,16,128]{2,1,0:T(8,128)(2,1)}), bf16[128,16,128]{2,1,0:T(8,128)(2,1)}, u32[]{:S(2)}, u32[]{:S(2)}) async-start(bf16[128,16,128]{2,1,0:T(8,128)(2,1)} %copy.83), calls=%async_computation.4 | async-start | bytes 1048576 | tf_op jit(solution)/shard_map/while/body/eval_jaxpr/all_to_all | solution.py:94
  969.7 20.3 %all-to-all-start.2 = ((bf16[16,128,128]{2,0,1:T(8,128)(2,1)}), bf16[16,128,128]{2,0,1:T(8,128)(2,1)S(1)}, u32[]{:S(2)}, u32[]{:S(2)}) async-start(bf16[16,128,128]{2,0,1:T(8,128)(2,1)} %copy.79), calls=%async_computation.2 | async-start | bytes 1048576 | tf_op jit(solution)/shard_map/while/body/eval_jaxpr/all_to_all | solution.py:76
  990.0 19.1 %all-to-all-start.3 = ((bf16[16,128,128]{2,0,1:T(8,128)(2,1)}), bf16[16,128,128]{2,0,1:T(8,128)(2,1)}, u32[]{:S(2)}, u32[]{:S(2)}) async-start(bf16[16,128,128]{2,0,1:T(8,128)(2,1)} %copy.81), calls=%async_computation.3 | async-start | bytes 1048576 | tf_op jit(solution)/shard_map/while/body/eval_jaxpr/all_to_all | solution.py:83
  1012.7 18.4 %all-to-all-start.4 = ((bf16[128,16,128]{2,1,0:T(8,128)(2,1)}), bf16[128,16,128]{2,1,0:T(8,128)(2,1)}, u32[]{:S(2)}, u32[]{:S(2)}) async-start(bf16[128,16,128]{2,1,0:T(8,128)(2,1)} %copy.83), calls=%async_computation.4 | async-start | bytes 1048576 | tf_op jit(solution)/shard_map/while/body/eval_jaxpr/all_to_all | solution.py:94
  1044.0 19.7 %all-to-all-start.2 = ((bf16[16,128,128]{2,0,1:T(8,128)(2,1)}), bf16[16,128,128]{2,0,1:T(8,128)(2,1)S(1)}, u32[]{:S(2)}, u32[]{:S(2)}) async-start(bf16[16,128,128]{2,0,1:T(8,128)(2,1)} %copy.79), calls=%async_computation.2 | async-start | bytes 1048576 | tf_op jit(solution)/shard_map/while/body/eval_jaxpr/all_to_all | solution.py:76
  1063.7 19.2 %all-to-all-start.3 = ((bf16[16,128,128]{2,0,1:T(8,128)(2,1)}), bf16[16,128,128]{2,0,1:T(8,128)(2,1)}, u32[]{:S(2)}, u32[]{:S(2)}) async-start(bf16[16,128,128]{2,0,1:T(8,128)(2,1)} %copy.81), calls=%async_computation.3 | async-start | bytes 1048576 | tf_op jit(solution)/shard_map/while/body/eval_jaxpr/all_to_all | solution.py:83
  1086.5 18.4 %all-to-all-start.4 = ((bf16[128,16,128]{2,1,0:T(8,128)(2,1)}), bf16[128,16,128]{2,1,0:T(8,128)(2,1)}, u32[]{:S(2)}, u32[]{:S(2)}) async-start(bf16[128,16,128]{2,1,0:T(8,128)(2,1)} %copy.83), calls=%async_computation.4 | async-start | bytes 1048576 | tf_op jit(solution)/shard_map/while/body/eval_jaxpr/all_to_all | solution.py:94
  1117.8 20.3 %all-to-all-start.2 = ((bf16[16,128,128]{2,0,1:T(8,128)(2,1)}), bf16[16,128,128]{2,0,1:T(8,128)(2,1)S(1)}, u32[]{:S(2)}, u32[]{:S(2)}) async-start(bf16[16,128,128]{2,0,1:T(8,128)(2,1)} %copy.79), calls=%async_computation.2 | async-start | bytes 1048576 | tf_op jit(solution)/shard_map/while/body/eval_jaxpr/all_to_all | solution.py:76
  1138.1 19.1 %all-to-all-start.3 = ((bf16[16,128,128]{2,0,1:T(8,128)(2,1)}), bf16[16,128,128]{2,0,1:T(8,128)(2,1)}, u32[]{:S(2)}, u32[]{:S(2)}) async-start(bf16[16,128,128]{2,0,1:T(8,128)(2,1)} %copy.81), calls=%async_computation.3 | async-start | bytes 1048576 | tf_op jit(solution)/shard_map/while/body/eval_jaxpr/all_to_all | solution.py:83
  1160.7 18.4 %all-to-all-start.4 = ((bf16[128,16,128]{2,1,0:T(8,128)(2,1)}), bf16[128,16,128]{2,1,0:T(8,128)(2,1)}, u32[]{:S(2)}, u32[]{:S(2)}) async-start(bf16[128,16,128]{2,1,0:T(8,128)(2,1)} %copy.83), calls=%async_computation.4 | async-start | bytes 1048576 | tf_op jit(solution)/shard_map/while/body/eval_jaxpr/all_to_all | solution.py:94
  1192.0 19.8 %all-to-all-start.2 = ((bf16[16,128,128]{2,0,1:T(8,128)(2,1)}), bf16[16,128,128]{2,0,1:T(8,128)(2,1)S(1)}, u32[]{:S(2)}, u32[]{:S(2)}) async-start(bf16[16,128,128]{2,0,1:T(8,128)(2,1)} %copy.79), calls=%async_computation.2 | async-start | bytes 1048576 | tf_op jit(solution)/shard_map/while/body/eval_jaxpr/all_to_all | solution.py:76
  1211.8 19.2 %all-to-all-start.3 = ((bf16[16,128,128]{2,0,1:T(8,128)(2,1)}), bf16[16,128,128]{2,0,1:T(8,128)(2,1)}, u32[]{:S(2)}, u32[]{:S(2)}) async-start(bf16[16,128,128]{2,0,1:T(8,128)(2,1)} %copy.81), calls=%async_computation.3 | async-start | bytes 1048576 | tf_op jit(solution)/shard_map/while/body/eval_jaxpr/all_to_all | solution.py:83
  1234.5 18.4 %all-to-all-start.4 = ((bf16[128,16,128]{2,1,0:T(8,128)(2,1)}), bf16[128,16,128]{2,1,0:T(8,128)(2,1)}, u32[]{:S(2)}, u32[]{:S(2)}) async-start(bf16[128,16,128]{2,1,0:T(8,128)(2,1)} %copy.83), calls=%async_computation.4 | async-start | bytes 1048576 | tf_op jit(solution)/shard_map/while/body/eval_jaxpr/all_to_all | solution.py:94
  1265.8 20.3 %all-to-all-start.2 = ((bf16[16,128,128]{2,0,1:T(8,128)(2,1)}), bf16[16,128,128]{2,0,1:T(8,128)(2,1)S(1)}, u32[]{:S(2)}, u32[]{:S(2)}) async-start(bf16[16,128,128]{2,0,1:T(8,128)(2,1)} %copy.79), calls=%async_computation.2 | async-start | bytes 1048576 | tf_op jit(solution)/shard_map/while/body/eval_jaxpr/all_to_all | solution.py:76
  1286.1 19.1 %all-to-all-start.3 = ((bf16[16,128,128]{2,0,1:T(8,128)(2,1)}), bf16[16,128,128]{2,0,1:T(8,128)(2,1)}, u32[]{:S(2)}, u32[]{:S(2)}) async-start(bf16[16,128,128]{2,0,1:T(8,128)(2,1)} %copy.81), calls=%async_computation.3 | async-start | bytes 1048576 | tf_op jit(solution)/shard_map/while/body/eval_jaxpr/all_to_all | solution.py:83
  1308.7 18.4 %all-to-all-start.4 = ((bf16[128,16,128]{2,1,0:T(8,128)(2,1)}), bf16[128,16,128]{2,1,0:T(8,128)(2,1)}, u32[]{:S(2)}, u32[]{:S(2)}) async-start(bf16[128,16,128]{2,1,0:T(8,128)(2,1)} %copy.83), calls=%async_computation.4 | async-start | bytes 1048576 | tf_op jit(solution)/shard_map/while/body/eval_jaxpr/all_to_all | solution.py:94
  1340.0 19.8 %all-to-all-start.2 = ((bf16[16,128,128]{2,0,1:T(8,128)(2,1)}), bf16[16,128,128]{2,0,1:T(8,128)(2,1)S(1)}, u32[]{:S(2)}, u32[]{:S(2)}) async-start(bf16[16,128,128]{2,0,1:T(8,128)(2,1)} %copy.79), calls=%async_computation.2 | async-start | bytes 1048576 | tf_op jit(solution)/shard_map/while/body/eval_jaxpr/all_to_all | solution.py:76
  1359.8 19.2 %all-to-all-start.3 = ((bf16[16,128,128]{2,0,1:T(8,128)(2,1)}), bf16[16,128,128]{2,0,1:T(8,128)(2,1)}, u32[]{:S(2)}, u32[]{:S(2)}) async-start(bf16[16,128,128]{2,0,1:T(8,128)(2,1)} %copy.81), calls=%async_computation.3 | async-start | bytes 1048576 | tf_op jit(solution)/shard_map/while/body/eval_jaxpr/all_to_all | solution.py:83
  1382.6 18.4 %all-to-all-start.4 = ((bf16[128,16,128]{2,1,0:T(8,128)(2,1)}), bf16[128,16,128]{2,1,0:T(8,128)(2,1)}, u32[]{:S(2)}, u32[]{:S(2)}) async-start(bf16[128,16,128]{2,1,0:T(8,128)(2,1)} %copy.83), calls=%async_computation.4 | async-start | bytes 1048576 | tf_op jit(solution)/shard_map/while/body/eval_jaxpr/all_to_all | solution.py:94
  1413.9 20.3 %all-to-all-start.2 = ((bf16[16,128,128]{2,0,1:T(8,128)(2,1)}), bf16[16,128,128]{2,0,1:T(8,128)(2,1)S(1)}, u32[]{:S(2)}, u32[]{:S(2)}) async-start(bf16[16,128,128]{2,0,1:T(8,128)(2,1)} %copy.79), calls=%async_computation.2 | async-start | bytes 1048576 | tf_op jit(solution)/shard_map/while/body/eval_jaxpr/all_to_all | solution.py:76
  1434.1 19.0 %all-to-all-start.3 = ((bf16[16,128,128]{2,0,1:T(8,128)(2,1)}), bf16[16,128,128]{2,0,1:T(8,128)(2,1)}, u32[]{:S(2)}, u32[]{:S(2)}) async-start(bf16[16,128,128]{2,0,1:T(8,128)(2,1)} %copy.81), calls=%async_computation.3 | async-start | bytes 1048576 | tf_op jit(solution)/shard_map/while/body/eval_jaxpr/all_to_all | solution.py:83
  1456.8 18.4 %all-to-all-start.4 = ((bf16[128,16,128]{2,1,0:T(8,128)(2,1)}), bf16[128,16,128]{2,1,0:T(8,128)(2,1)}, u32[]{:S(2)}, u32[]{:S(2)}) async-start(bf16[128,16,128]{2,1,0:T(8,128)(2,1)} %copy.83), calls=%async_computation.4 | async-start | bytes 1048576 | tf_op jit(solution)/shard_map/while/body/eval_jaxpr/all_to_all | solution.py:94
  (88 other events, 941.2 us)
where the time goes:
time: 1490 us; the launch traced here: 1480 us
  waiting for transfers between devices  768 us (52%)
  blocking collectives  210 us (14%)
  starting transfers between devices  196 us (13%)
  local copies, waits for them, and re-layouts  132 us (9%)
  matrix products  83.1 us (6%)
  loops' own time  53.3 us (4%)
  other arithmetic  40.4 us (3%)
    all_to_all x12, blocking collectives, forward_tick(): lax.all_to_all(mixed, 'block', split_axis=1, concat_axis=0, tiled=True)  210 us
    all_to_all x12, waiting for transfers between devices, backward_tick(): lax.all_to_all(first_factor(right_block, layer_input), 'block', split_axi...  174 us
    all_to_all x12, waiting for transfers between devices, forward_tick(): lax.all_to_all(second, 'block', split_axis=0, concat_axis=1, tiled=True)  166 us
    all_to_all x12, waiting for transfers between devices, backward_tick(): lax.all_to_all(grad_carried, 'block', split_axis=1, concat_axis=0, tiled=...  161 us
    all_to_all x12, waiting for transfers between devices, backward_tick(): lax.all_to_all(grad_mixed, 'block', split_axis=0, concat_axis=1, tiled=True)  135 us
    ppermute x24, waiting for transfers between devices, shifted(): return lax.ppermute(x, axis, [(i, (i + by) % peers) for i in range(peers)])  132 us
    all_to_all x12, starting transfers between devices, backward_tick(): lax.all_to_all(grad_carried, 'block', split_axis=1, concat_axis=0, tiled=...  49.7 us
    all_to_all x12, starting transfers between devices, backward_tick(): lax.all_to_all(grad_mixed, 'block', split_axis=0, concat_axis=1, tiled=True)  49.7 us
  transfers between devices with their start and end apart: 72, of which 72 were waited for; matrix products, arithmetic and copies ran while one was open for 7% of the time, Pallas kernels for 0%

commit v1 on v0

v1 whole, which is shorter than its diff:
```python
import jax
import jax.numpy as jnp
from jax import lax
from jax.sharding import Mesh, PartitionSpec as P

F32 = jnp.float32
BF16 = jnp.bfloat16
PLANE = ("s", "x")


def swap(chunks, axes):
    return lax.all_to_all(chunks, axes, split_axis=0, concat_axis=0, tiled=True)


def silu_slope(values):
    sigmoid = jax.nn.sigmoid(values)
    return sigmoid * (1.0 + values * (1.0 - sigmoid))


def plane_order(size, sections, peers):
    sub = size // (sections * sections * peers)
    natural = jnp.arange(size).reshape(sections, peers, sections, sub)
    order = natural.transpose(2, 1, 0, 3).reshape(size)
    return (order[:, None] == jnp.arange(size)[None, :]).astype(BF16)


def to_columns(values):
    own, full, rows = values.shape
    moved = swap(values.transpose(1, 0, 2), PLANE)
    return moved.reshape(full // own, own, own, rows).transpose(1, 0, 2, 3).reshape(own, full, rows)


def body(inputs, cotangent, right_factor, left_factor):
    sections = lax.axis_size("s")
    peers = lax.axis_size("x")
    loops, _, own, size, _ = right_factor.shape
    rows = inputs.shape[2]
    sub = own // sections
    layers = loops * sections
    order = plane_order(size, sections, peers)

    def permuted(blocks):
        return jnp.einsum("aj,bjr->bar", order, blocks, preferred_element_type=F32).astype(BF16)

    def natural(blocks, kind):
        return jnp.einsum("aj,bar->bjr", order, blocks, preferred_element_type=F32).astype(kind)

    def enter(acts):
        parts = permuted(acts.reshape(own, size, rows)).reshape(sections, sub, size, rows)
        return swap(swap(parts, "s"), "t").reshape(own, size, rows)

    def leave(acts):
        parts = swap(swap(acts.reshape(sections, sub, size, rows), "t"), "s")
        return natural(parts.reshape(own, size, rows), BF16).reshape(1, own * size, rows)

    both = jnp.stack([right_factor[:, 0], left_factor[:, 0]], axis=1)
    both = jnp.einsum("aj,lfbjk,ck->lfbac", order, both, order, preferred_element_type=F32).astype(BF16)
    both = both.reshape(loops, 2, sections, sub, size, size).transpose(0, 2, 1, 3, 4, 5)
    weights = []
    for loop in range(loops):
        moved = swap(both[loop], "s")
        for section in range(sections):
            full = lax.all_gather(moved[section], "t", axis=0, tiled=False)
            weights.append((full[:, 0].reshape(own, size, size), full[:, 1].reshape(own, size, size)))

    current = enter(inputs)
    grad = enter(cotangent)
    stored = []
    for right, left in weights:
        mixed = jnp.einsum("bjk,bjr->bkr", right, current, preferred_element_type=F32).astype(BF16)
        columns = to_columns(mixed)
        stored.append((current, columns))
        activated = jax.nn.silu(columns.astype(F32)).astype(BF16)
        second = jnp.einsum("kbc,kbr->kcr", left, activated, preferred_element_type=F32).astype(BF16)
        returned = to_columns(second)
        current = (current.astype(F32) + returned.astype(F32)).astype(BF16)
    outputs = leave(current)

    sums = [None] * layers
    for layer in reversed(range(layers)):
        right, left = weights[layer]
        acts, columns = stored[layer]
        grad_columns = to_columns(grad)
        wide = columns.astype(F32)
        activated = jax.nn.silu(wide).astype(BF16)
        left_term = jnp.einsum("kbr,kcr->kbc", activated, grad_columns, preferred_element_type=F32)
        grad_act = jnp.einsum("kbc,kcr->kbr", left, grad_columns, preferred_element_type=F32)
        grad_mixed = to_columns((grad_act * silu_slope(wide)).astype(BF16))
        right_term = jnp.einsum("bjr,bkr->bjk", acts, grad_mixed, preferred_element_type=F32)
        branch = jnp.einsum("bjk,bkr->bjr", right, grad_mixed, preferred_element_type=F32)
        grad = (grad.astype(F32) + branch).astype(BF16)
        terms = jnp.stack(
            [
                right_term.astype(BF16).reshape(sections, sub, size, size),
                left_term.astype(BF16).reshape(sections, sub, size, size),
            ],
            axis=1,
        )
        sums[layer] = lax.psum_scatter(terms, "t", scatter_dimension=0, tiled=False)
    input_grad = leave(grad)

    halves = []
    for loop in range(loops):
        moved = swap(jnp.stack(sums[loop * sections : (loop + 1) * sections]), "s")
        blocks = moved.transpose(1, 0, 2, 3, 4).reshape(2, own, size, size)
        halves.append(
            jnp.einsum("aj,fbac,ck->fbjk", order, blocks, order, preferred_element_type=F32)
        )
    grads = jnp.stack(halves)
    return (outputs, input_grad, grads[:, 0][:, None], grads[:, 1][:, None])


def solution(mesh):
    sections = mesh.shape["section"]
    peers = mesh.shape["block"] // sections
    planes = Mesh(mesh.devices.reshape(sections, sections, peers), ("s", "t", "x"))
    acts = P("s", ("t", "x"), None)
    factor = P(None, "s", ("t", "x"), None, None)
    return jax.shard_map(
        body,
        mesh=planes,
        in_specs=(acts, acts, factor, factor),
        out_specs=(acts, acts, factor, factor),
        check_vma=False,
    )
```

time: 1490 us -> 994 us (0.67)
  waiting for transfers between devices: 768 us -> 375 us
  starting transfers between devices: 196 us -> 103 us
  blocking collectives: 210 us -> 278 us
  loops' own time: 53.3 us -> 0 us
  local copies, waits for them, and re-layouts: 132 us -> 109 us
  matrix products: 83.1 us -> 60.1 us
  between operations: 0.74 us -> 16.2 us
    all_to_all x48 -> x25, waiting for transfers between devices: 636 us -> 123 us  [swap(): return lax.all_to_all(chunks, axes, split_axis=0, concat_axis=0, tiled=True)]
    unnamed x0 -> x10, waiting for transfers between devices: none -> 218 us
    ppermute x24 -> x0, waiting for transfers between devices: 132 us -> none  [shifted(): return lax.ppermute(x, axis, [(i, (i + by) % peers) for i in range(peers)])]
    all_to_all x48 -> x25, starting transfers between devices: 193 us -> 102 us  [swap(): return lax.all_to_all(chunks, axes, split_axis=0, concat_axis=0, tiled=True)]
    all_to_all x12 -> x19, blocking collectives: 210 us -> 278 us  [swap(): return lax.all_to_all(chunks, axes, split_axis=0, concat_axis=0, tiled=True)]
    another operation x2 -> x0, loops' own time: 53.3 us -> none  [the longest x1 35.8 us: body(): lax.scan(backward_tick, (grad_start, right_zero, left_zero), tick_list)]
    all_gather x0 -> x8, waiting for transfers between devices: none -> 34.3 us  [body(): full = lax.all_gather(moved[section], 't', axis=0, tiled=False)]
    unnamed x10 -> x193, local copies, waits for them, and re-layouts: 3.46 us -> 32.1 us
  transfers between devices with their start and end apart: 72 -> 34, of which waited for: 72 -> 26; matrix products, arithmetic and copies ran while one was open for 7% -> 13% of each run, Pallas kernels for 0% -> 0%
where the time goes in v1:
time: 994 us; the launch traced here: 981 us
  waiting for transfers between devices  375 us (38%)
  blocking collectives  278 us (28%)
  local copies, waits for them, and re-layouts  109 us (11%)
  starting transfers between devices  103 us (10%)
  matrix products  60.1 us (6%)
  other arithmetic  40.1 us (4%)
  between operations  16.2 us (2%)
    all_to_all x19, blocking collectives, swap(): return lax.all_to_all(chunks, axes, split_axis=0, concat_axis=0, tiled=True)  278 us
    unnamed x10, waiting for transfers between devices  218 us
    all_to_all x25, waiting for transfers between devices, swap(): return lax.all_to_all(chunks, axes, split_axis=0, concat_axis=0, tiled=True)  123 us
    all_to_all x25, starting transfers between devices, swap(): return lax.all_to_all(chunks, axes, split_axis=0, concat_axis=0, tiled=True)  102 us
    all_gather x8, waiting for transfers between devices, body(): full = lax.all_gather(moved[section], 't', axis=0, tiled=False)  34.3 us
    unnamed x193, local copies, waits for them, and re-layouts  32.1 us
  transfers between devices with their start and end apart: 34, of which 26 were waited for; matrix products, arithmetic and copies ran while one was open for 13% of the time, Pallas kernels for 0%

profile of v1, /device:TPU:0, one launch (start us, length us, event | category | flops | bytes accessed | tf_op | source)
XLA Modules:
  0.0 981.5 jit_solution(17011925008401213793)
XLA Ops:
  17.3 18.5 %all_to_all.220 = bf16[4,2,4,128,128]{4,3,2,1,0:T(8,128)(2,1)S(1)} all-to-all(bf16[4,2,4,128,128]{4,3,2,1,0:T(8,128)(2,1)S(1)} %get-tuple-element.14), channel_id=1, replica_groups=mesh['s'=4,'t'=4,'x'=2] {'s'}, dimensions={0} | all-to-all | bytes 2097152 | tf_op jit(solution)/shard_map/all_to_all | solution.py:12
  37.2 11.9 %all_to_all.221 = bf16[4,4,128,128]{3,2,1,0:T(8,128)(2,1)} all-to-all(bf16[4,4,128,128]{3,2,1,0:T(8,128)(2,1)S(1)} %bitcast.785), channel_id=1, replica_groups=mesh['s'=4,'t'=4,'x'=2] {'s'}, dimensions={0} | all-to-all | bytes 1048576 | tf_op jit(solution)/shard_map/all_to_all | solution.py:12
  49.1 4.9 all-to-all-start.1
  54.7 20.7 %all-gather.9.cloned.1.call-done = bf16[4,2,4,128,128]{4,3,2,1,0:T(8,128)(2,1)} async-done(((bf16[1,2,4,128,128]{4,3,2,1,0:T(8,128)(2,1)}), bf16[4,2,4,128,128]{4,3,2,1,0:T(8,128)(2,1)}) %all-gather.9.cloned.1.call-update) | async-done | bytes 1048592 | tf_op jit(solution)/shard_map/all_gather | solution.py:63
  77.4 13.1 %all_to_all.222 = bf16[128,16,128]{2,1,0:T(8,128)(2,1)S(1)} all-to-all(bf16[128,16,128]{2,1,0:T(8,128)(2,1)S(1)} %copy.291), channel_id=1, replica_groups=mesh['s'=4,'t'=4,'x'=2] {'s','x'}, dimensions={0} | all-to-all | bytes 1048576 | tf_op jit(solution)/shard_map/all_to_all | solution.py:12
  97.8 6.3 all-gather.11.cloned.1.call-done
  107.3 12.0 %all_to_all.223 = bf16[128,16,128]{2,1,0:T(8,128)(2,1)S(1)} all-to-all(bf16[128,16,128]{2,1,0:T(8,128)(2,1)S(1)} %copy.297), channel_id=1, replica_groups=mesh['s'=4,'t'=4,'x'=2] {'s','x'}, dimensions={0} | all-to-all | bytes 1048576 | tf_op jit(solution)/shard_map/all_to_all | solution.py:12
  126.5 7.3 all-gather.13.cloned.1.call-done
  139.7 12.8 %all_to_all.224 = bf16[128,16,128]{2,1,0:T(8,128)(2,1)} all-to-all(bf16[128,16,128]{2,1,0:T(8,128)(2,1)S(1)} %copy.303), channel_id=1, replica_groups=mesh['s'=4,'t'=4,'x'=2] {'s','x'}, dimensions={0} | all-to-all | bytes 1048576 | tf_op jit(solution)/shard_map/all_to_all | solution.py:12
  152.5 4.3 all-to-all-start.11
  161.7 9.6 all-to-all-done.11
  171.3 4.2 all-to-all-start.8
  180.5 4.2 all-to-all-done.8
  188.3 11.7 %all_to_all.225 = bf16[128,16,128]{2,1,0:T(8,128)(2,1)S(1)} all-to-all(bf16[128,16,128]{2,1,0:T(8,128)(2,1)S(1)} %copy.309), channel_id=1, replica_groups=mesh['s'=4,'t'=4,'x'=2] {'s','x'}, dimensions={0} | all-to-all | bytes 1048576 | tf_op jit(solution)/shard_map/all_to_all | solution.py:12
  203.8 4.1 all-to-all-start.10
  210.9 6.3 all-to-all-done.10
  220.7 11.7 %all_to_all.226 = bf16[128,16,128]{2,1,0:T(8,128)(2,1)S(1)} all-to-all(bf16[128,16,128]{2,1,0:T(8,128)(2,1)S(1)} %copy.315), channel_id=1, replica_groups=mesh['s'=4,'t'=4,'x'=2] {'s','x'}, dimensions={0} | all-to-all | bytes 1048576 | tf_op jit(solution)/shard_map/all_to_all | solution.py:12
  236.2 4.1 all-to-all-start.13
  243.5 6.1 all-to-all-done.13
  253.2 11.7 %all_to_all.227 = bf16[128,16,128]{2,1,0:T(8,128)(2,1)S(1)} all-to-all(bf16[128,16,128]{2,1,0:T(8,128)(2,1)S(1)} %copy.321), channel_id=1, replica_groups=mesh['s'=4,'t'=4,'x'=2] {'s','x'}, dimensions={0} | all-to-all | bytes 1048576 | tf_op jit(solution)/shard_map/all_to_all | solution.py:12
  277.5 4.6 all-to-all-done.15
  295.2 13.4 %all_to_all.228 = bf16[128,16,128]{2,1,0:T(8,128)(2,1)} all-to-all(bf16[128,16,128]{2,1,0:T(8,128)(2,1)} %copy.327), channel_id=1, replica_groups=mesh['s'=4,'t'=4,'x'=2] {'s','x'}, dimensions={0} | all-to-all | bytes 1048576 | tf_op jit(solution)/shard_map/all_to_all | solution.py:12
  317.7 10.1 %all-to-all-done.23 = bf16[4,4,128,128]{3,2,1,0:T(8,128)(2,1)} async-done(((bf16[4,4,128,128]{3,2,1,0:T(8,128)(2,1)}), bf16[4,4,128,128]{3,2,1,0:T(8,128)(2,1)}, u32[]{:S(2)}, u32[]{:S(2)}) %all-to-all-start.23) | async-done | bytes 524320 | tf_op jit(solution)/shard_map/all_to_all | solution.py:12
  327.8 4.3 all-to-all-start.17
  336.6 4.8 all-to-all-done.17
  354.8 4.1 all-to-all-start.18
  360.9 7.3 all-to-all-done.18
  371.4 11.7 %all_to_all.229 = bf16[128,16,128]{2,1,0:T(8,128)(2,1)S(1)} all-to-all(bf16[128,16,128]{2,1,0:T(8,128)(2,1)S(1)} %copy.341), channel_id=1, replica_groups=mesh['s'=4,'t'=4,'x'=2] {'s','x'}, dimensions={0} | all-to-all | bytes 1048576 | tf_op jit(solution)/shard_map/all_to_all | solution.py:12
  385.1 11.8 %all_to_all.230 = bf16[128,16,128]{2,1,0:T(8,128)(2,1)S(1)} all-to-all(bf16[128,16,128]{2,1,0:T(8,128)(2,1)S(1)} %copy.344), channel_id=1, replica_groups=mesh['s'=4,'t'=4,'x'=2] {'s','x'}, dimensions={0} | all-to-all | bytes 1048576 | tf_op jit(solution)/shard_map/all_to_all | solution.py:12
  397.6 11.7 %all_to_all.231 = bf16[128,16,128]{2,1,0:T(8,128)(2,1)S(1)} all-to-all(bf16[128,16,128]{2,1,0:T(8,128)(2,1)S(1)} %copy.347), channel_id=1, replica_groups=mesh['s'=4,'t'=4,'x'=2] {'s','x'}, dimensions={0} | all-to-all | bytes 1048576 | tf_op jit(solution)/shard_map/all_to_all | solution.py:12
  410.0 11.8 %all_to_all.232 = bf16[128,16,128]{2,1,0:T(8,128)(2,1)S(1)} all-to-all(bf16[128,16,128]{2,1,0:T(8,128)(2,1)S(1)} %copy.350), channel_id=1, replica_groups=mesh['s'=4,'t'=4,'x'=2] {'s','x'}, dimensions={0} | all-to-all | bytes 1048576 | tf_op jit(solution)/shard_map/all_to_all | solution.py:12
  422.6 11.7 %all_to_all.233 = bf16[128,16,128]{2,1,0:T(8,128)(2,1)S(1)} all-to-all(bf16[128,16,128]{2,1,0:T(8,128)(2,1)S(1)} %copy.353), channel_id=1, replica_groups=mesh['s'=4,'t'=4,'x'=2] {'s','x'}, dimensions={0} | all-to-all | bytes 1048576 | tf_op jit(solution)/shard_map/all_to_all | solution.py:12
  435.0 11.8 %all_to_all.234 = bf16[128,16,128]{2,1,0:T(8,128)(2,1)S(1)} all-to-all(bf16[128,16,128]{2,1,0:T(8,128)(2,1)S(1)} %copy.356), channel_id=1, replica_groups=mesh['s'=4,'t'=4,'x'=2] {'s','x'}, dimensions={0} | all-to-all | bytes 1048576 | tf_op jit(solution)/shard_map/all_to_all | solution.py:12
  447.6 11.7 %all_to_all.235 = bf16[128,16,128]{2,1,0:T(8,128)(2,1)S(1)} all-to-all(bf16[128,16,128]{2,1,0:T(8,128)(2,1)S(1)} %copy.359), channel_id=1, replica_groups=mesh['s'=4,'t'=4,'x'=2] {'s','x'}, dimensions={0} | all-to-all | bytes 1048576 | tf_op jit(solution)/shard_map/all_to_all | solution.py:12
  462.3 4.2 all-to-all-start.32
  469.0 6.8 all-to-all-done.32
  499.2 4.4 all-to-all-start.34
  554.4 4.2 all-to-all-start.37
  573.2 4.1 all-to-all-start.38
  600.6 4.2 all-to-all-done.39
  610.3 11.9 %all_to_all.236 = bf16[128,16,128]{2,1,0:T(8,128)(2,1)S(1)} all-to-all(bf16[128,16,128]{2,1,0:T(8,128)(2,1)S(1)} %copy.335), channel_id=1, replica_groups=mesh['s'=4,'t'=4,'x'=2] {'s','x'}, dimensions={0} | all-to-all | bytes 1048576 | tf_op jit(solution)/shard_map/all_to_all | solution.py:12
  625.0 32.6 %all_to_all.237 = bf16[4,4,128,128]{3,2,1,0:T(8,128)(2,1)} all-to-all(bf16[4,4,128,128]{3,2,1,0:T(8,128)(2,1)S(1)} %add_convert_fusion), channel_id=1, replica_groups=mesh['s'=4,'t'=4,'x'=2] {'t'}, dimensions={0} | all-to-all | bytes 1048576 | tf_op jit(solution)/shard_map/all_to_all | solution.py:12
  661.5 8.5 all-to-all-done.21
  670.0 34.1 %all_to_all.238 = bf16[4,4,128,128]{3,2,1,0:T(8,128)(2,1)} all-to-all(bf16[4,4,128,128]{3,2,1,0:T(8,128)(2,1)S(1)} %bitcast.786), channel_id=1, replica_groups=mesh['s'=4,'t'=4,'x'=2] {'t'}, dimensions={0} | all-to-all | bytes 1048576 | tf_op jit(solution)/shard_map/all_to_all | solution.py:12
  708.4 214.8 %all-reduce.11.cloned.1.call-done = (bf16[4,2,4,128,128]{4,3,2,0,1:T(8,128)(2,1)}, bf16[4,2,4,128,128]{4,3,2,0,1:T(8,128)(2,1)}, bf16[4,2,4,128,128]{4,3,2,0,1:T...) async-done(((bf16[4,2,4,128,128]{4,3,2,0,1:T(8,128)(2,1)}, ...) | async-done | bytes 8388624
  936.2 9.8 all-to-all-done.42
  945.9 4.2 all-to-all-start.43
  955.7 9.0 all-to-all-done.43
  (406 shorter events, 296.2 us)
Async XLA Ops:
  7.2 29.6 %copy-start = (bf16[1,2048,128]{2,1,0:T(8,128)(2,1)S(1)}, bf16[1,2048,128]{2,1,0:T(8,128)(2,1)}, u32[]{:S(2)}) copy-start(bf16[1,2048,128]{2,1,0:T(8,128)(2,1)} %param.4) | copy-start | bytes 1572868
  7.2 68.2 %all-gather.9.cloned.1.call-start = ((), (), s32[]{:S(2)}) async-start(), calls=%async_computation.44 | async-start | bytes 1310720 | tf_op jit(solution)/shard_map/all_gather | solution.py:63
  49.1 27.6 %all-to-all-start.1 = ((bf16[4,4,128,128]{3,2,1,0:T(8,128)(2,1)}), bf16[4,4,128,128]{3,2,1,0:T(8,128)(2,1)S(1)}, u32[]{:S(2)}, u32[]{:S(2)}) async-start(bf16[4,4,128,128]{3,2,1,0:T(8,128)(2,1)} %all_to_all.221), calls=%async_computation.1 | async-start | bytes 1048576 | tf_op jit(solution)/shard_map/all_to_all | solution.py:12
  54.0 50.2 %all-gather.11.cloned.1.call-start = ((), (), s32[]{:S(2)}) async-start(), calls=%async_computation.45 | async-start | bytes 1310720 | tf_op jit(solution)/shard_map/all_gather | solution.py:63
  76.7 13.9 %copy-start.68 = (bf16[4,1,4,128,128]{4,3,2,1,0:T(8,128)(2,1)}, bf16[4,1,4,128,128]{4,3,2,1,0:T(8,128)(2,1)S(1)}, u32[]{:S(2)}) copy-start(bf16[4,1,4,128,128]{4,3,2,1,0:T(8,128)(2,1)S(1)} %get-tuple-element.32) | copy-start | bytes 1572868
  76.7 15.4 %copy-start.47 = (bf16[4,1,4,128,128]{4,3,2,1,0:T(8,128)(2,1)}, bf16[4,1,4,128,128]{4,3,2,1,0:T(8,128)(2,1)S(1)}, u32[]{:S(2)}) copy-start(bf16[4,1,4,128,128]{4,3,2,1,0:T(8,128)(2,1)S(1)} %get-tuple-element.33) | copy-start | bytes 1572868
  92.1 13.3 %copy-start.17 = (bf16[16,128,128]{2,1,0:T(8,128)(2,1)}, bf16[16,128,128]{2,1,0:T(8,128)(2,1)S(1)}, u32[]{:S(2)}) copy-start(bf16[16,128,128]{2,1,0:T(8,128)(2,1)S(1)} %get-tuple-element.31) | copy-start | bytes 1572868
  93.6 12.7 %all-to-all-start.4 = ((bf16[128,16,128]{2,1,0:T(8,128)(2,1)}), bf16[128,16,128]{2,1,0:T(8,128)(2,1)S(1)}, u32[]{:S(2)}, u32[]{:S(2)}) async-start(bf16[128,16,128]{2,1,0:T(8,128)(2,1)} %copy.293), calls=%async_computation.4 | async-start | bytes 1048576 | tf_op jit(solution)/shard_map/all_to_all | solution.py:12
  97.1 36.6 %all-gather.13.cloned.1.call-start = ((), (), s32[]{:S(2)}) async-start(), calls=%async_computation.46 | async-start | bytes 1310720 | tf_op jit(solution)/shard_map/all_gather | solution.py:63
  105.5 15.4 %copy-start.48 = (bf16[4,1,4,128,128]{4,3,2,1,0:T(8,128)(2,1)}, bf16[4,1,4,128,128]{4,3,2,1,0:T(8,128)(2,1)S(1)}, u32[]{:S(2)}) copy-start(bf16[4,1,4,128,128]{4,3,2,1,0:T(8,128)(2,1)S(1)} %get-tuple-element.39) | copy-start | bytes 1572868
  120.9 15.1 %copy-start.19 = (bf16[16,128,128]{2,1,0:T(8,128)(2,1)}, bf16[16,128,128]{2,1,0:T(8,128)(2,1)S(1)}, u32[]{:S(2)}) copy-start(bf16[16,128,128]{2,1,0:T(8,128)(2,1)S(1)} %get-tuple-element.29) | copy-start | bytes 1572868
  122.4 13.6 %all-to-all-start.6 = ((bf16[128,16,128]{2,1,0:T(8,128)(2,1)}), bf16[128,16,128]{2,1,0:T(8,128)(2,1)S(1)}, u32[]{:S(2)}, u32[]{:S(2)}) async-start(bf16[128,16,128]{2,1,0:T(8,128)(2,1)} %copy.299), calls=%async_computation.6 | async-start | bytes 1048576 | tf_op jit(solution)/shard_map/all_to_all | solution.py:12
  125.9 52.3 %all-gather.15.cloned.1.call-start = ((), (), s32[]{:S(2)}) async-start(), calls=%async_computation.47 | async-start | bytes 1310720 | tf_op jit(solution)/shard_map/all_gather | solution.py:63
  152.5 18.8 %all-to-all-start.11 = ((bf16[4,2,4,128,128]{4,3,2,1,0:T(8,128)(2,1)}), bf16[4,2,4,128,128]{4,3,2,1,0:T(8,128)(2,1)}, u32[]{:S(2)}, u32[]{:S(2)}) async-start(bf16[4,2,4,128,128]{4,3,2,1,0:T(8,128)(2,1)} %get-tuple-element.15), calls=%async_computation.11 | async-start | bytes 2097152 | tf_op jit(solution)/shard_map/all_to_all | solution.py:12
  171.3 13.4 %all-to-all-start.8 = ((bf16[128,16,128]{2,1,0:T(8,128)(2,1)}), bf16[128,16,128]{2,1,0:T(8,128)(2,1)}, u32[]{:S(2)}, u32[]{:S(2)}) async-start(bf16[128,16,128]{2,1,0:T(8,128)(2,1)} %copy.305), calls=%async_computation.8 | async-start | bytes 1048576 | tf_op jit(solution)/shard_map/all_to_all | solution.py:12
  175.5 33.1 %all-gather.17.cloned.1.call-start = ((), (), s32[]{:S(2)}) async-start(), calls=%async_computation.48 | async-start | bytes 1310720 | tf_op jit(solution)/shard_map/all_gather | solution.py:63
  187.5 12.5 %copy-start.13 = (bf16[16,128,128]{2,1,0:T(8,128)(2,1)}, bf16[16,128,128]{2,1,0:T(8,128)(2,1)S(1)}, u32[]{:S(2)}) copy-start(bf16[16,128,128]{2,1,0:T(8,128)(2,1)S(1)} %fusion.63) | copy-start | bytes 1572868
  203.8 13.4 %all-to-all-start.10 = ((bf16[128,16,128]{2,1,0:T(8,128)(2,1)}), bf16[128,16,128]{2,1,0:T(8,128)(2,1)}, u32[]{:S(2)}, u32[]{:S(2)}) async-start(bf16[128,16,128]{2,1,0:T(8,128)(2,1)} %copy.311), calls=%async_computation.10 | async-start | bytes 1048576 | tf_op jit(solution)/shard_map/all_to_all | solution.py:12
  207.9 33.2 %all-gather.19.cloned.1.call-start = ((), (), s32[]{:S(2)}) async-start(), calls=%async_computation.49 | async-start | bytes 1310720 | tf_op jit(solution)/shard_map/all_gather | solution.py:63
  236.2 13.4 %all-to-all-start.13 = ((bf16[128,16,128]{2,1,0:T(8,128)(2,1)}), bf16[128,16,128]{2,1,0:T(8,128)(2,1)}, u32[]{:S(2)}, u32[]{:S(2)}) async-start(bf16[128,16,128]{2,1,0:T(8,128)(2,1)} %copy.317), calls=%async_computation.13 | async-start | bytes 1048576 | tf_op jit(solution)/shard_map/all_to_all | solution.py:12
  240.4 34.8 %all-gather.21.cloned.1.call-start = ((), (), s32[]{:S(2)}) async-start(), calls=%async_computation.50 | async-start | bytes 1310720 | tf_op jit(solution)/shard_map/all_gather | solution.py:63
  252.5 12.5 %copy-start.15 = (bf16[16,128,128]{2,1,0:T(8,128)(2,1)}, bf16[16,128,128]{2,1,0:T(8,128)(2,1)S(1)}, u32[]{:S(2)}) copy-start(bf16[16,128,128]{2,1,0:T(8,128)(2,1)S(1)} %fusion.61) | copy-start | bytes 1572868
  268.7 13.4 %all-to-all-start.15 = ((bf16[128,16,128]{2,1,0:T(8,128)(2,1)}), bf16[128,16,128]{2,1,0:T(8,128)(2,1)}, u32[]{:S(2)}, u32[]{:S(2)}) async-start(bf16[128,16,128]{2,1,0:T(8,128)(2,1)} %copy.323), calls=%async_computation.15 | async-start | bytes 1048576 | tf_op jit(solution)/shard_map/all_to_all | solution.py:12
  272.9 61.5 %all-gather.23.cloned.1.call-start = ((), (), s32[]{:S(2)}) async-start(), calls=%async_computation.51 | async-start | bytes 1310720 | tf_op jit(solution)/shard_map/all_gather | solution.py:63
  282.1 13.1 %all-to-all-start.22 = ((bf16[4,4,128,128]{3,2,1,0:T(8,128)(2,1)}), bf16[4,4,128,128]{3,2,1,0:T(8,128)(2,1)}, u32[]{:S(2)}, u32[]{:S(2)}) async-start(bf16[4,4,128,128]{3,2,1,0:T(8,128)(2,1)} %bitcast.761), calls=%async_computation.22 | async-start | bytes 1048576 | tf_op jit(solution)/shard_map/all_to_all | solution.py:12
  308.6 19.2 %all-to-all-start.23 = ((bf16[4,4,128,128]{3,2,1,0:T(8,128)(2,1)}), bf16[4,4,128,128]{3,2,1,0:T(8,128)(2,1)}, u32[]{:S(2)}, u32[]{:S(2)}) async-start(bf16[4,4,128,128]{3,2,1,0:T(8,128)(2,1)} %all-to-all-done.22), calls=%async_computation.23 | async-start | bytes 1048576 | tf_op jit(solution)/shard_map/all_to_all | solution.py:12
  327.8 13.6 %all-to-all-start.17 = ((bf16[128,16,128]{2,1,0:T(8,128)(2,1)}), bf16[128,16,128]{2,1,0:T(8,128)(2,1)}, u32[]{:S(2)}, u32[]{:S(2)}) async-start(bf16[128,16,128]{2,1,0:T(8,128)(2,1)} %copy.329), calls=%async_computation.17 | async-start | bytes 1048576 | tf_op jit(solution)/shard_map/all_to_all | solution.py:12
  341.4 13.4 %all-to-all-start.24 = ((bf16[128,16,128]{2,1,0:T(8,128)(2,1)}), bf16[128,16,128]{2,1,0:T(8,128)(2,1)}, u32[]{:S(2)}, u32[]{:S(2)}) async-start(bf16[128,16,128]{2,1,0:T(8,128)(2,1)} %copy.338), calls=%async_computation.24 | async-start | bytes 1048576 | tf_op jit(solution)/shard_map/all_to_all | solution.py:12
  354.8 13.4 %all-to-all-start.18 = ((bf16[128,16,128]{2,1,0:T(8,128)(2,1)}), bf16[128,16,128]{2,1,0:T(8,128)(2,1)}, u32[]{:S(2)}, u32[]{:S(2)}) async-start(bf16[128,16,128]{2,1,0:T(8,128)(2,1)} %copy.333), calls=%async_computation.18 | async-start | bytes 1048576 | tf_op jit(solution)/shard_map/all_to_all | solution.py:12
  383.1 13.7 %copy-start.63 = (bf16[8,16,16,128]{3,2,0,1:T(8,128)(2,1)}, bf16[8,16,16,128]{3,2,0,1:T(8,128)(2,1)S(1)}, u32[]{:S(2)}) copy-start(bf16[8,16,16,128]{3,2,0,1:T(8,128)(2,1)S(1)} %copy.342) | copy-start | bytes 1572868
  447.2 12.9 %copy-start.74 = (bf16[4,1,4,128,128]{4,3,2,1,0:T(8,128)(2,1)S(1)}, bf16[4,1,4,128,128]{4,3,2,1,0:T(8,128)(2,1)}, u32[]{:S(2)}) copy-start(bf16[4,1,4,128,128]{4,3,2,1,0:T(8,128)(2,1)} %get-tuple-element.44) | copy-start | bytes 1572868
  462.3 13.4 %all-to-all-start.32 = ((bf16[128,16,128]{2,1,0:T(8,128)(2,1)}), bf16[128,16,128]{2,1,0:T(8,128)(2,1)}, u32[]{:S(2)}, u32[]{:S(2)}) async-start(bf16[128,16,128]{2,1,0:T(8,128)(2,1)} %copy.362), calls=%async_computation.32 | async-start | bytes 1048576 | tf_op jit(solution)/shard_map/all_to_all | solution.py:12
  480.5 13.4 %all-to-all-start.33 = ((bf16[128,16,128]{2,1,0:T(8,128)(2,1)}), bf16[128,16,128]{2,1,0:T(8,128)(2,1)}, u32[]{:S(2)}, u32[]{:S(2)}) async-start(bf16[128,16,128]{2,1,0:T(8,128)(2,1)} %copy.365), calls=%async_computation.33 | async-start | bytes 1048576 | tf_op jit(solution)/shard_map/all_to_all | solution.py:12
  499.2 13.6 %all-to-all-start.34 = ((bf16[128,16,128]{2,1,0:T(8,128)(2,1)}), bf16[128,16,128]{2,1,0:T(8,128)(2,1)}, u32[]{:S(2)}, u32[]{:S(2)}) async-start(bf16[128,16,128]{2,1,0:T(8,128)(2,1)} %copy.368), calls=%async_computation.34 | async-start | bytes 1048576 | tf_op jit(solution)/shard_map/all_to_all | solution.py:12
  517.6 13.4 %all-to-all-start.35 = ((bf16[128,16,128]{2,1,0:T(8,128)(2,1)}), bf16[128,16,128]{2,1,0:T(8,128)(2,1)}, u32[]{:S(2)}, u32[]{:S(2)}) async-start(bf16[128,16,128]{2,1,0:T(8,128)(2,1)} %copy.371), calls=%async_computation.35 | async-start | bytes 1048576 | tf_op jit(solution)/shard_map/all_to_all | solution.py:12
  536.3 13.4 %all-to-all-start.36 = ((bf16[128,16,128]{2,1,0:T(8,128)(2,1)}), bf16[128,16,128]{2,1,0:T(8,128)(2,1)}, u32[]{:S(2)}, u32[]{:S(2)}) async-start(bf16[128,16,128]{2,1,0:T(8,128)(2,1)} %copy.374), calls=%async_computation.36 | async-start | bytes 1048576 | tf_op jit(solution)/shard_map/all_to_all | solution.py:12
  554.4 13.4 %all-to-all-start.37 = ((bf16[128,16,128]{2,1,0:T(8,128)(2,1)}), bf16[128,16,128]{2,1,0:T(8,128)(2,1)}, u32[]{:S(2)}, u32[]{:S(2)}) async-start(bf16[128,16,128]{2,1,0:T(8,128)(2,1)} %copy.377), calls=%async_computation.37 | async-start | bytes 1048576 | tf_op jit(solution)/shard_map/all_to_all | solution.py:12
  573.2 13.4 %all-to-all-start.38 = ((bf16[128,16,128]{2,1,0:T(8,128)(2,1)}), bf16[128,16,128]{2,1,0:T(8,128)(2,1)}, u32[]{:S(2)}, u32[]{:S(2)}) async-start(bf16[128,16,128]{2,1,0:T(8,128)(2,1)} %copy.380), calls=%async_computation.38 | async-start | bytes 1048576 | tf_op jit(solution)/shard_map/all_to_all | solution.py:12
  591.3 13.4 %all-to-all-start.39 = ((bf16[128,16,128]{2,1,0:T(8,128)(2,1)}), bf16[128,16,128]{2,1,0:T(8,128)(2,1)}, u32[]{:S(2)}, u32[]{:S(2)}) async-start(bf16[128,16,128]{2,1,0:T(8,128)(2,1)} %copy.383), calls=%async_computation.39 | async-start | bytes 1048576 | tf_op jit(solution)/shard_map/all_to_all | solution.py:12
  595.5 327.8 %all-reduce.11.cloned.1.call-start = ((), (), s32[]{:S(2)}) async-start(), calls=%async_computation.52 | async-start | bytes 16777216
  625.0 36.1 %copy-start.66 = (bf16[8,16,16,128]{3,2,0,1:T(8,128)(2,1)S(1)}, bf16[8,16,16,128]{3,2,0,1:T(8,128)(2,1)}, u32[]{:S(2)}) copy-start(bf16[8,16,16,128]{3,2,0,1:T(8,128)(2,1)} %copy-done.65) | copy-start | bytes 1572868
  625.0 36.1 %copy-start.69 = (bf16[4,1,4,128,128]{4,3,2,1,0:T(8,128)(2,1)S(1)}, bf16[4,1,4,128,128]{4,3,2,1,0:T(8,128)(2,1)}, u32[]{:S(2)}) copy-start(bf16[4,1,4,128,128]{4,3,2,1,0:T(8,128)(2,1)} %copy-done.68) | copy-start | bytes 1572868
  625.0 36.1 %copy-start.82 = (bf16[16,128,128]{2,1,0:T(8,128)(2,1)S(1)}, bf16[16,128,128]{2,1,0:T(8,128)(2,1)}, u32[]{:S(2)}) copy-start(bf16[16,128,128]{2,1,0:T(8,128)(2,1)} %copy-done.81) | copy-start | bytes 1572868
  657.7 12.3 %all-to-all-start.21 = ((bf16[4,4,128,128]{3,2,1,0:T(8,128)(2,1)}), bf16[4,4,128,128]{3,2,1,0:T(8,128)(2,1)S(1)}, u32[]{:S(2)}, u32[]{:S(2)}) async-start(bf16[4,4,128,128]{3,2,1,0:T(8,128)(2,1)} %all_to_all.237), calls=%async_computation.21 | async-start | bytes 1048576 | tf_op jit(solution)/shard_map/all_to_all | solution.py:12
  661.2 46.7 %copy-start.92 = (u32[32]{0:T(128)S(1)}, u32[32]{0:T(128)}, u32[]{:S(2)}) copy-start(u32[32]{0:T(128)} %constant.31) | copy-start | bytes 388
  704.1 223.9 %all-to-all-start.41 = ((bf16[4,4,128,128]{3,2,1,0:T(8,128)(2,1)}), bf16[4,4,128,128]{3,2,1,0:T(8,128)(2,1)S(1)}, u32[]{:S(2)}, u32[]{:S(2)}) async-start(bf16[4,4,128,128]{3,2,1,0:T(8,128)(2,1)} %all_to_all.238), calls=%async_computation.41 | async-start | bytes 1048576 | tf_op jit(solution)/shard_map/all_to_all | solution.py:12
  928.0 18.0 %all-to-all-start.42 = ((bf16[4,2,4,128,128]{4,3,2,1,0:T(8,128)(2,1)}), bf16[4,2,4,128,128]{4,3,2,1,0:T(8,128)(2,1)S(1)}, u32[]{:S(2)}, u32[]{:S(2)}) async-start(bf16[4,2,4,128,128]{4,3,2,1,0:T(8,128)(2,1)} %copy.387), calls=%async_computation.42 | async-start | bytes 2097152 | tf_op jit(solution)/shard_map/all_to_all | solution.py:12
  945.9 18.8 %all-to-all-start.43 = ((bf16[4,2,4,128,128]{4,3,2,1,0:T(8,128)(2,1)}), bf16[4,2,4,128,128]{4,3,2,1,0:T(8,128)(2,1)}, u32[]{:S(2)}, u32[]{:S(2)}) async-start(bf16[4,2,4,128,128]{4,3,2,1,0:T(8,128)(2,1)} %copy.391), calls=%async_computation.43 | async-start | bytes 2097152 | tf_op jit(solution)/shard_map/all_to_all | solution.py:12
  (79 other events, 343.8 us)
Sparse Core Ops, SparseCore 0:
  36.9 38.3 all-gather.8
  76.9 27.1 all-gather.10
  106.3 27.4 all-gather.12
  135.2 27.4 all-gather.14
  178.3 27.8 all-gather.16
  210.0 27.8 all-gather.18
  242.8 27.8 all-gather.20
  275.3 27.8 all-gather.22
  607.7 315.5 all-reduce.10

commit v2 on v1

v2 whole, which is shorter than its diff:
```python
import jax
import jax.numpy as jnp
from jax import lax
from jax.sharding import Mesh, PartitionSpec as P

F32 = jnp.float32
BF16 = jnp.bfloat16
PLANE = ("s", "x")
MOST_PAIRWISE = 8


def pairwise(value, axes, count, mask):
    return lax.ppermute(value, axes, [(i, i ^ mask) for i in range(count)])


def silu_slope(values):
    sigmoid = jax.nn.sigmoid(values)
    return sigmoid * (1.0 + values * (1.0 - sigmoid))


def plane_orders(size, sections, peers):
    sub = size // (sections * sections * peers)
    count = sections * peers
    natural = jnp.arange(size).reshape(sections, peers, sections, sub)
    by_peer = natural.transpose(2, 1, 0, 3).reshape(count, size // count)
    me = jnp.arange(sections)[:, None] * peers + lax.axis_index("x")
    if count > MOST_PAIRWISE:
        me = jnp.zeros_like(me)
    order = by_peer[me ^ jnp.arange(count)[None, :]].reshape(sections, size)
    return (order[:, :, None] == jnp.arange(size)[None, None, :]).astype(BF16)


def exchange(values):
    own, full, rows = values.shape
    count = full // own
    pieces = values.transpose(1, 0, 2).reshape(count, own, own, rows)
    if count > MOST_PAIRWISE:
        moved = lax.all_to_all(pieces, PLANE, split_axis=0, concat_axis=0, tiled=True)
        return moved.transpose(1, 0, 2, 3).reshape(own, full, rows)
    moved = [pieces[0]] + [pairwise(pieces[m], PLANE, count, m) for m in range(1, count)]
    return jnp.concatenate(moved, axis=1)


def body(inputs, cotangent, right_factor, left_factor):
    sections = lax.axis_size("s")
    peers = lax.axis_size("x")
    loops, _, own, size, _ = right_factor.shape
    rows = inputs.shape[2]
    sub = own // sections
    layers = loops * sections
    s_index = lax.axis_index("s")
    t_index = lax.axis_index("t")
    orders = plane_orders(size, sections, peers)
    my_order = lax.dynamic_index_in_dim(orders, s_index, 0, keepdims=False)

    def turned(parts, send_by, place_by, target):
        moved = []
        for mask in range(sections):
            value = lax.dynamic_index_in_dim(parts, send_by ^ mask, 0, keepdims=False)
            pairs = [
                (s * sections + t, target(s, t, mask)) for s in range(sections) for t in range(sections)
            ]
            moved.append(lax.ppermute(value, ("s", "t"), pairs))
        moved = jnp.stack(moved)
        return jnp.stack(
            [
                lax.dynamic_index_in_dim(moved, place_by ^ part, 0, keepdims=False)
                for part in range(sections)
            ]
        )

    def enter(acts):
        parts = acts.reshape(sections, sub, size, rows)
        parts = turned(parts, t_index, s_index, lambda s, t, mask: (t ^ mask) * sections + s)
        parts = parts.reshape(own, size, rows)
        return jnp.einsum("aj,bjr->bar", my_order, parts, preferred_element_type=F32).astype(BF16)

    def leave(acts):
        acts = jnp.einsum("aj,bar->bjr", my_order, acts, preferred_element_type=F32).astype(BF16)
        parts = acts.reshape(sections, sub, size, rows)
        parts = turned(parts, s_index, t_index, lambda s, t, mask: t * sections + (s ^ mask))
        return parts.reshape(1, own * size, rows)

    both = jnp.stack([right_factor[:, 0], left_factor[:, 0]], axis=1)
    both = both.reshape(loops, 2, sections, sub, size, size)
    both = jnp.einsum("saj,lfsbjk,sck->lsfbac", orders, both, orders, preferred_element_type=F32)
    both = both.astype(BF16)
    weights = []
    for loop in range(loops):
        moved = lax.all_to_all(both[loop], "s", split_axis=0, concat_axis=0, tiled=True)
        for section in range(sections):
            full = lax.all_gather(moved[section], "t", axis=0, tiled=False)
            weights.append((full[:, 0].reshape(own, size, size), full[:, 1].reshape(own, size, size)))

    current = enter(inputs)
    grad = enter(cotangent)
    stored = []
    for right, left in weights:
        mixed = jnp.einsum("bjk,bjr->bkr", right, current, preferred_element_type=F32).astype(BF16)
        columns = exchange(mixed)
        stored.append((current, columns))
        activated = jax.nn.silu(columns.astype(F32)).astype(BF16)
        second = jnp.einsum("kbc,kbr->kcr", left, activated, preferred_element_type=F32).astype(BF16)
        returned = exchange(second)
        current = (current.astype(F32) + returned.astype(F32)).astype(BF16)
    outputs = leave(current)

    def reduced(terms):
        step = 1
        parts = terms
        while step < sections:
            pairs = parts.reshape((parts.shape[0] // 2, 2) + parts.shape[1:])
            bit = (t_index // step) % 2
            keep = lax.dynamic_index_in_dim(pairs, bit, 1, keepdims=False)
            give = lax.dynamic_index_in_dim(pairs, 1 - bit, 1, keepdims=False)
            got = pairwise(give, "t", sections, step)
            parts = (keep.astype(F32) + got.astype(F32)).astype(BF16)
            step *= 2
        return parts[0]

    sums = [None] * layers
    for layer in reversed(range(layers)):
        right, left = weights[layer]
        acts, columns = stored[layer]
        grad_columns = exchange(grad)
        wide = columns.astype(F32)
        activated = jax.nn.silu(wide).astype(BF16)
        left_term = jnp.einsum("kbr,kcr->kbc", activated, grad_columns, preferred_element_type=F32)
        grad_act = jnp.einsum("kbc,kcr->kbr", left, grad_columns, preferred_element_type=F32)
        grad_mixed = exchange((grad_act * silu_slope(wide)).astype(BF16))
        right_term = jnp.einsum("bjr,bkr->bjk", acts, grad_mixed, preferred_element_type=F32)
        branch = jnp.einsum("bjk,bkr->bjr", right, grad_mixed, preferred_element_type=F32)
        grad = (grad.astype(F32) + branch).astype(BF16)
        terms = jnp.stack(
            [
                right_term.astype(BF16).reshape(sections, sub, size, size),
                left_term.astype(BF16).reshape(sections, sub, size, size),
            ],
            axis=1,
        )
        sums[layer] = reduced(terms)
    input_grad = leave(grad)

    halves = []
    for loop in range(loops):
        mine = jnp.stack(sums[loop * sections : (loop + 1) * sections])
        moved = lax.all_to_all(mine, "s", split_axis=0, concat_axis=0, tiled=True)
        halves.append(
            jnp.einsum("saj,sfbac,sck->fsbjk", orders, moved, orders, preferred_element_type=F32)
        )
    grads = jnp.stack(halves).reshape(loops, 2, 1, own, size, size)
    return (outputs, input_grad, grads[:, 0], grads[:, 1])


def solution(mesh):
    sections = mesh.shape["section"]
    peers = mesh.shape["block"] // sections
    planes = Mesh(mesh.devices.reshape(sections, sections, peers), ("s", "t", "x"))
    acts = P("s", ("t", "x"), None)
    factor = P(None, "s", ("t", "x"), None, None)
    return jax.shard_map(
        body,
        mesh=planes,
        in_specs=(acts, acts, factor, factor),
        out_specs=(acts, acts, factor, factor),
        check_vma=False,
    )
```

time: 994 us -> 1060 us (1.066)
  blocking collectives: 278 us -> 18.6 us
  waiting for transfers between devices: 375 us -> 565 us
  starting transfers between devices: 103 us -> 265 us
  matrix products: 60.1 us -> 45.7 us
    ppermute x0 -> x256, waiting for transfers between devices: none -> 557 us  [the longest x240 532 us: pairwise(): return lax.ppermute(value, axes, [(i, i ^ mask) for i in range(count)])]
    all_to_all x19 -> x1, blocking collectives: 278 us -> 18.6 us  [body(): lax.all_to_all(both[loop], 's', split_axis=0, concat_axis=0, tiled=True)]
    ppermute x0 -> x256, starting transfers between devices: none -> 246 us  [the longest x240 208 us: pairwise(): return lax.ppermute(value, axes, [(i, i ^ mask) for i in range(count)])]
    unnamed x10 -> x8, waiting for transfers between devices: 218 us -> 0.13 us
    all_to_all x25 -> x3, waiting for transfers between devices: 123 us -> 8 us  [the longest x2 8 us: body(): moved = lax.all_to_all(mine, 's', split_axis=0, concat_axis=0, tiled=True)]
    all_to_all x25 -> x3, starting transfers between devices: 102 us -> 18.1 us  [the longest x2 13.5 us: body(): moved = lax.all_to_all(mine, 's', split_axis=0, concat_axis=0, tiled=True)]
    all_gather x8, waiting for transfers between devices: 34.3 us -> 0.01 us  [body(): full = lax.all_gather(moved[section], 't', axis=0, tiled=False)]
    unnamed x193 -> x382, local copies, waits for them, and re-layouts: 32.1 us -> 61.5 us
  transfers between devices with their start and end apart: 34 -> 267, of which waited for: 26 -> 175; matrix products, arithmetic and copies ran while one was open for 13% -> 15% of each run, Pallas kernels for 0% -> 0%
where the time goes in v2:
time: 1060 us; the launch traced here: 1050 us
  waiting for transfers between devices  565 us (53%)
  starting transfers between devices  265 us (25%)
  local copies, waits for them, and re-layouts  101 us (10%)
  matrix products  45.7 us (4%)
  other arithmetic  36.8 us (3%)
  blocking collectives  18.6 us (2%)
  between operations  17.3 us (2%)
    ppermute x240, waiting for transfers between devices, pairwise(): return lax.ppermute(value, axes, [(i, i ^ mask) for i in range(count)])  532 us
    ppermute x240, starting transfers between devices, pairwise(): return lax.ppermute(value, axes, [(i, i ^ mask) for i in range(count)])  208 us
    unnamed x382, local copies, waits for them, and re-layouts  61.5 us
    ppermute x16, starting transfers between devices, turned(): moved.append(lax.ppermute(value, ('s', 't'), pairs))  37.6 us
    ppermute x16, waiting for transfers between devices, turned(): moved.append(lax.ppermute(value, ('s', 't'), pairs))  24.6 us
  transfers between devices with their start and end apart: 267, of which 175 were waited for; matrix products, arithmetic and copies ran while one was open for 15% of the time, Pallas kernels for 0%

profile of v2, /device:TPU:0, one launch (start us, length us, event | category | flops | bytes accessed | tf_op | source)
XLA Modules:
  0.0 1048.9 jit_solution(17282073370722608628)
XLA Ops:
  15.9 18.6 %all_to_all.20 = bf16[4,2,4,128,128]{4,3,2,1,0:T(8,128)(2,1)S(1)} all-to-all(bf16[4,2,4,128,128]{4,3,2,1,0:T(8,128)(2,1)S(1)} %get-tuple-element.22), channel_id=1, replica_groups=mesh['s'=4,'t'=4,'x'=2] {'s'}, dimensions={0} | all-to-all | bytes 2097152 | tf_op jit(solution)/shard_map/all_to_all | solution.py:90
  36.6 6.1 collective-permute-start.123
  42.7 4.6 all-to-all-start.1
  47.9 18.3 %collective-permute-start.2 = (bf16[4,128,128]{1,2,0:T(8,128)(2,1)S(1)}, bf16[4,128,128]{1,2,0:T(8,128)(2,1)S(1)}, u32[]{:S(2)}, u32[]{:S(2)}) collective-permute-start(bf16[4,128,128]{1,2,0:T(8,128)(2,1)S(1)} %bitcast.444), channel_id=1, source_target_pairs={{0,16},{2,24},{4,0},{6,8},{8,18},{10,26},{12,2},{14,10},{16,20},{1... | collective-permute-start | bytes 393224 | tf_op jit(solution)/shard_map/ppermute | solution.py:63
  66.2 20.3 %collective-permute-done.122 = bf16[4,128,128]{2,1,0:T(8,128)(2,1)S(1)} collective-permute-done((bf16[4,128,128]{2,1,0:T(8,128)(2,1)S(1)}, bf16[4,128,128]{2,1,0:T(8,128)(2,1)S(1)}, u32[]{:S(2)}, u32[]{:S(2)}) %collective-permute-start.122) | collective-permute-done | bytes 131104 | tf_op jit(solution)/shard_map/ppermute | solution.py:63
  90.1 4.3 collective-permute-done.2
  98.1 8.1 collective-permute-start.128
  130.4 4.1 collective-permute-done.9
  135.1 4.4 collective-permute-done.10
  194.2 4.2 collective-permute-done.23
  198.6 4.9 collective-permute-done.24
  260.9 3.9 collective-permute-done.38
  283.2 4.1 collective-permute-done.43
  316.6 4.0 collective-permute-done.51
  502.2 3.9 collective-permute-done.136
  506.2 5.0 collective-permute-done.137
  554.8 3.7 collective-permute-done.144
  580.7 4.2 collective-permute-done.150
  585.7 4.2 collective-permute-done.151
  612.0 4.2 collective-permute-done.156
  632.3 4.2 collective-permute-done.163
  652.7 4.2 collective-permute-done.170
  673.0 4.2 collective-permute-done.177
  694.2 4.2 collective-permute-done.184
  702.7 4.2 collective-permute-done.186
  727.4 4.3 collective-permute-done.192
  732.4 4.3 collective-permute-done.193
  771.0 3.9 collective-permute-done.201
  776.1 4.0 collective-permute-done.203
  785.6 4.0 collective-permute-done.205
  813.7 3.9 collective-permute-done.213
  817.7 5.2 collective-permute-done.214
  838.7 4.5 collective-permute-done.219
  843.2 3.9 collective-permute-done.220
  847.9 4.5 collective-permute-done.221
  859.3 4.0 collective-permute-done.224
  868.4 4.3 collective-permute-done.226
  872.7 3.9 collective-permute-done.227
  876.7 5.2 collective-permute-done.228
  913.8 4.3 convolution_convert_fusion.32
  936.7 9.1 all-to-all-start.3
  950.4 9.1 collective-permute-done.240
  961.8 14.5 %collective-permute-done.242 = bf16[2,2,4,128,128]{4,3,2,1,0:T(8,128)(2,1)S(1)} collective-permute-done((bf16[2,2,4,128,128]{4,3,2,1,0:T(8,128)(2,1)}, bf16[2,2,4,128,128]{4,3,2,1,0:T(8,128)(2,1)S(1)}, u32[]{:S(2)}, u32[]{:S(2)}) %collective-permute-start.242) | collective-permute-done | bytes 524320 | tf_op jit(solution)/shard_map/ppermute | solution.py:13
  979.6 17.7 %collective-permute-done.247 = bf16[1,2,4,128,128]{4,3,2,1,0:T(8,128)(2,1)S(1)} collective-permute-done((bf16[1,2,4,128,128]{4,3,2,1,0:T(8,128)(2,1)S(1)}, bf16[1,2,4,128,128]{4,3,2,1,0:T(8,128)(2,1)S(1)}, u32[]{:S(2)}, u32[]{:S(2)}) %collective-permute-start.247) | collective-permute-done | bytes 262176 | tf_op jit(solution)/shard_map/ppermute | solution.py:13
  997.3 11.2 %collective-permute-done.241 = bf16[1,2,4,128,128]{4,3,2,1,0:T(8,128)(2,1)S(1)} collective-permute-done((bf16[1,2,4,128,128]{4,3,2,1,0:T(8,128)(2,1)S(1)}, bf16[1,2,4,128,128]{4,3,2,1,0:T(8,128)(2,1)S(1)}, u32[]{:S(2)}, u32[]{:S(2)}) %collective-permute-start.241) | collective-permute-done | bytes 262176 | tf_op jit(solution)/shard_map/ppermute | solution.py:13
  1009.2 6.4 collective-permute-done.243
  1016.8 4.4 all-to-all-start.2
  1027.7 8.0 all-to-all-done.2
  (1099 shorter events, 730.9 us)
Async XLA Ops:
  7.2 99.7 %all-gather.9.cloned.1.call-start = ((), (), s32[]{:S(2)}) async-start(), calls=%async_computation.4 | async-start | bytes 1310720 | tf_op jit(solution)/shard_map/all_gather | solution.py:92
  35.7 54.3 %collective-permute-start.1 = (bf16[4,128,128]{1,2,0:T(8,128)(2,1)S(1)}, bf16[4,128,128]{1,2,0:T(8,128)(2,1)S(1)}, u32[]{:S(2)}, u32[]{:S(2)}) collective-permute-start(bf16[4,128,128]{1,2,0:T(8,128)(2,1)S(1)} %bitcast.438), channel_id=1, source_target_pairs={{0,8},{2,0},{4,24},{6,16},{8,10},{10,2},{12,26},{14,18},{16,12},{1... | collective-permute-start | bytes 393224 | tf_op jit(solution)/shard_map/ppermute | solution.py:63
  36.6 29.7 %collective-permute-start.123 = (bf16[4,128,128]{2,1,0:T(8,128)(2,1)S(1)}, bf16[4,128,128]{2,1,0:T(8,128)(2,1)S(1)}, u32[]{:S(2)}, u32[]{:S(2)}) collective-permute-start(bf16[4,128,128]{2,1,0:T(8,128)(2,1)S(1)} %get-tuple-element.207), channel_id=1, source_target_pairs={{0,24},{2,16},{4,8},{6,0},{8,26},{10,18},{12,10},{14,2},{16,28},{1... | collective-permute-start | bytes 393224 | tf_op jit(solution)/shard_map/ppermute | solution.py:63
  42.6 43.8 %collective-permute-start.122 = (bf16[4,128,128]{2,1,0:T(8,128)(2,1)S(1)}, bf16[4,128,128]{2,1,0:T(8,128)(2,1)S(1)}, u32[]{:S(2)}, u32[]{:S(2)}) collective-permute-start(bf16[4,128,128]{2,1,0:T(8,128)(2,1)S(1)} %get-tuple-element.208), channel_id=1, source_target_pairs={{0,16},{2,24},{4,0},{6,8},{8,18},{10,26},{12,2},{14,10},{16,20},{1... | collective-permute-start | bytes 393224 | tf_op jit(solution)/shard_map/ppermute | solution.py:63
  42.6 44.5 %collective-permute-start.121 = (bf16[4,128,128]{2,1,0:T(8,128)(2,1)S(1)}, bf16[4,128,128]{2,1,0:T(8,128)(2,1)S(1)}, u32[]{:S(2)}, u32[]{:S(2)}) collective-permute-start(bf16[4,128,128]{2,1,0:T(8,128)(2,1)S(1)} %get-tuple-element.209), channel_id=1, source_target_pairs={{0,8},{2,0},{4,24},{6,16},{8,10},{10,2},{12,26},{14,18},{16,12},{1... | collective-permute-start | bytes 393224 | tf_op jit(solution)/shard_map/ppermute | solution.py:63
  42.7 194.3 %all-to-all-start.1 = ((bf16[4,2,4,128,128]{4,3,2,1,0:T(8,128)(2,1)}), bf16[4,2,4,128,128]{4,3,2,1,0:T(8,128)(2,1)S(1)}, u32[]{:S(2)}, u32[]{:S(2)}) async-start(bf16[4,2,4,128,128]{4,3,2,1,0:T(8,128)(2,1)} %get-tuple-element.23), calls=%async_computation.1 | async-start | bytes 2097152 | tf_op jit(solution)/shard_map/all_to_all | solution.py:90
  47.3 95.9 %all-gather.11.cloned.1.call-start = ((), (), s32[]{:S(2)}) async-start(), calls=%async_computation.5 | async-start | bytes 1310720 | tf_op jit(solution)/shard_map/all_gather | solution.py:92
  47.9 46.5 %collective-permute-start.2 = (bf16[4,128,128]{1,2,0:T(8,128)(2,1)S(1)}, bf16[4,128,128]{1,2,0:T(8,128)(2,1)S(1)}, u32[]{:S(2)}, u32[]{:S(2)}) collective-permute-start(bf16[4,128,128]{1,2,0:T(8,128)(2,1)S(1)} %bitcast.444), channel_id=1, source_target_pairs={{0,16},{2,24},{4,0},{6,8},{8,18},{10,26},{12,2},{14,10},{16,20},{1... | collective-permute-start | bytes 393224 | tf_op jit(solution)/shard_map/ppermute | solution.py:63
  66.2 28.2 %collective-permute-start.3 = (bf16[4,128,128]{1,2,0:T(8,128)(2,1)S(1)}, bf16[4,128,128]{1,2,0:T(8,128)(2,1)S(1)}, u32[]{:S(2)}, u32[]{:S(2)}) collective-permute-start(bf16[4,128,128]{1,2,0:T(8,128)(2,1)S(1)} %bitcast.443), channel_id=1, source_target_pairs={{0,24},{2,16},{4,8},{6,0},{8,26},{10,18},{12,10},{14,2},{16,28},{1... | collective-permute-start | bytes 393224 | tf_op jit(solution)/shard_map/ppermute | solution.py:63
  90.0 115.7 %all-gather.13.cloned.1.call-start = ((), (), s32[]{:S(2)}) async-start(), calls=%async_computation.6 | async-start | bytes 1310720 | tf_op jit(solution)/shard_map/all_gather | solution.py:92
  95.4 342.9 %collective-permute-start.130 = (bf16[16,16,128]{2,0,1:T(8,128)(2,1)S(1)}, bf16[16,16,128]{2,0,1:T(8,128)(2,1)}, u32[]{:S(2)}, u32[]{:S(2)}) collective-permute-start(bf16[16,16,128]{2,0,1:T(8,128)(2,1)S(1)} %get-tuple-element.194), channel_id=1, source_target_pairs={{0,25},{1,24},{8,17},{9,16},{16,9},{17,8},{24,1},{25,0},{2,27},{3,... | collective-permute-start | bytes 196616 | tf_op jit(solution)/shard_map/ppermute | solution.py:13
  96.2 303.9 %collective-permute-start.129 = (bf16[16,16,128]{2,0,1:T(8,128)(2,1)}, bf16[16,16,128]{2,0,1:T(8,128)(2,1)}, u32[]{:S(2)}, u32[]{:S(2)}) collective-permute-start(bf16[16,16,128]{2,0,1:T(8,128)(2,1)} %get-tuple-element.195), channel_id=1, source_target_pairs={{0,24},{1,25},{8,16},{9,17},{16,8},{17,9},{24,0},{25,1},{2,26},{3,... | collective-permute-start | bytes 196616 | tf_op jit(solution)/shard_map/ppermute | solution.py:13
  98.1 252.3 %collective-permute-start.128 = (bf16[16,16,128]{2,0,1:T(8,128)(2,1)}, bf16[16,16,128]{2,0,1:T(8,128)(2,1)}, u32[]{:S(2)}, u32[]{:S(2)}) collective-permute-start(bf16[16,16,128]{2,0,1:T(8,128)(2,1)} %get-tuple-element.196), channel_id=1, source_target_pairs={{0,17},{1,16},{8,25},{9,24},{16,1},{17,0},{24,9},{25,8},{2,19},{3,... | collective-permute-start | bytes 196616 | tf_op jit(solution)/shard_map/ppermute | solution.py:13
  106.2 191.8 %collective-permute-start.127 = (bf16[16,16,128]{2,0,1:T(8,128)(2,1)}, bf16[16,16,128]{2,0,1:T(8,128)(2,1)}, u32[]{:S(2)}, u32[]{:S(2)}) collective-permute-start(bf16[16,16,128]{2,0,1:T(8,128)(2,1)} %get-tuple-element.197), channel_id=1, source_target_pairs={{0,16},{1,17},{8,24},{9,25},{16,0},{17,1},{24,8},{25,9},{2,18},{3,... | collective-permute-start | bytes 196616 | tf_op jit(solution)/shard_map/ppermute | solution.py:13
  113.0 156.2 %all-gather.15.cloned.1.call-start = ((), (), s32[]{:S(2)}) async-start(), calls=%async_computation.7 | async-start | bytes 1310720 | tf_op jit(solution)/shard_map/all_gather | solution.py:92
  175.7 148.5 %all-gather.17.cloned.1.call-start = ((), (), s32[]{:S(2)}) async-start(), calls=%async_computation.8 | async-start | bytes 1310720 | tf_op jit(solution)/shard_map/all_gather | solution.py:92
  238.0 137.8 %all-gather.19.cloned.1.call-start = ((), (), s32[]{:S(2)}) async-start(), calls=%async_computation.9 | async-start | bytes 1310720 | tf_op jit(solution)/shard_map/all_gather | solution.py:92
  299.4 122.5 %all-gather.21.cloned.1.call-start = ((), (), s32[]{:S(2)}) async-start(), calls=%async_computation.10 | async-start | bytes 1310720 | tf_op jit(solution)/shard_map/all_gather | solution.py:92
  352.0 101.3 %all-gather.23.cloned.1.call-start = ((), (), s32[]{:S(2)}) async-start(), calls=%async_computation.11 | async-start | bytes 1310720 | tf_op jit(solution)/shard_map/all_gather | solution.py:92
  482.7 38.2 %collective-permute-start.115 = (bf16[16,16,128]{2,0,1:T(8,128)(2,1)S(1)}, bf16[16,16,128]{2,0,1:T(8,128)(2,1)S(1)}, u32[]{:S(2)}, u32[]{:S(2)}) collective-permute-start(bf16[16,16,128]{2,0,1:T(8,128)(2,1)S(1)} %get-tuple-element.218), channel_id=1, source_target_pairs={{0,25},{1,24},{8,17},{9,16},{16,9},{17,8},{24,1},{25,0},{2,27},{3,... | collective-permute-start | bytes 196616 | tf_op jit(solution)/shard_map/ppermute | solution.py:13
  483.9 37.0 %collective-permute-start.114 = (bf16[16,16,128]{2,0,1:T(8,128)(2,1)S(1)}, bf16[16,16,128]{2,0,1:T(8,128)(2,1)S(1)}, u32[]{:S(2)}, u32[]{:S(2)}) collective-permute-start(bf16[16,16,128]{2,0,1:T(8,128)(2,1)S(1)} %get-tuple-element.219), channel_id=1, source_target_pairs={{0,24},{1,25},{8,16},{9,17},{16,8},{17,9},{24,0},{25,1},{2,26},{3,... | collective-permute-start | bytes 196616 | tf_op jit(solution)/shard_map/ppermute | solution.py:13
  484.9 36.0 %collective-permute-start.113 = (bf16[16,16,128]{2,0,1:T(8,128)(2,1)S(1)}, bf16[16,16,128]{2,0,1:T(8,128)(2,1)S(1)}, u32[]{:S(2)}, u32[]{:S(2)}) collective-permute-start(bf16[16,16,128]{2,0,1:T(8,128)(2,1)S(1)} %get-tuple-element.220), channel_id=1, source_target_pairs={{0,17},{1,16},{8,25},{9,24},{16,1},{17,0},{24,9},{25,8},{2,19},{3,... | collective-permute-start | bytes 196616 | tf_op jit(solution)/shard_map/ppermute | solution.py:13
  486.4 34.5 %collective-permute-start.112 = (bf16[16,16,128]{2,0,1:T(8,128)(2,1)S(1)}, bf16[16,16,128]{2,0,1:T(8,128)(2,1)S(1)}, u32[]{:S(2)}, u32[]{:S(2)}) collective-permute-start(bf16[16,16,128]{2,0,1:T(8,128)(2,1)S(1)} %get-tuple-element.221), channel_id=1, source_target_pairs={{0,16},{1,17},{8,24},{9,25},{16,0},{17,1},{24,8},{25,9},{2,18},{3,... | collective-permute-start | bytes 196616 | tf_op jit(solution)/shard_map/ppermute | solution.py:13
  526.9 66.2 %collective-permute-start.119 = (bf16[4,128,128]{2,1,0:T(8,128)(2,1)S(1)}, bf16[4,128,128]{2,1,0:T(8,128)(2,1)S(1)}, u32[]{:S(2)}, u32[]{:S(2)}) collective-permute-start(bf16[4,128,128]{2,1,0:T(8,128)(2,1)S(1)} %bitcast.440), channel_id=1, source_target_pairs={{0,6},{2,14},{4,22},{6,30},{8,4},{10,12},{12,20},{14,28},{16,2},{1... | collective-permute-start | bytes 393224 | tf_op jit(solution)/shard_map/ppermute | solution.py:63
  529.8 64.5 %collective-permute-start.117 = (bf16[4,128,128]{2,1,0:T(8,128)(2,1)S(1)}, bf16[4,128,128]{2,1,0:T(8,128)(2,1)S(1)}, u32[]{:S(2)}, u32[]{:S(2)}) collective-permute-start(bf16[4,128,128]{2,1,0:T(8,128)(2,1)S(1)} %bitcast.439), channel_id=1, source_target_pairs={{0,2},{2,10},{4,18},{6,26},{8,0},{10,8},{12,16},{14,24},{16,6},{18... | collective-permute-start | bytes 393224 | tf_op jit(solution)/shard_map/ppermute | solution.py:63
  529.8 65.0 %collective-permute-start.118 = (bf16[4,128,128]{2,1,0:T(8,128)(2,1)}, bf16[4,128,128]{2,1,0:T(8,128)(2,1)S(1)}, u32[]{:S(2)}, u32[]{:S(2)}) collective-permute-start(bf16[4,128,128]{2,1,0:T(8,128)(2,1)} %bitcast.437), channel_id=1, source_target_pairs={{0,4},{2,12},{4,20},{6,28},{8,6},{10,14},{12,22},{14,30},{16,0},{1... | collective-permute-start | bytes 393224 | tf_op jit(solution)/shard_map/ppermute | solution.py:63
  531.1 65.9 %collective-permute-start.116 = (bf16[4,128,128]{2,1,0:T(8,128)(2,1)}, bf16[4,128,128]{2,1,0:T(8,128)(2,1)S(1)}, u32[]{:S(2)}, u32[]{:S(2)}) collective-permute-start(bf16[4,128,128]{2,1,0:T(8,128)(2,1)} %bitcast.436), channel_id=1, source_target_pairs={{0,0},{2,8},{4,16},{6,24},{8,2},{10,10},{12,18},{14,26},{16,4},{18... | collective-permute-start | bytes 393224 | tf_op jit(solution)/shard_map/ppermute | solution.py:63
  592.0 177.2 %collective-permute-start.252 = (bf16[2,2,4,128,128]{4,3,2,1,0:T(8,128)(2,1)S(1)}, bf16[2,2,4,128,128]{4,3,2,1,0:T(8,128)(2,1)S(1)}, u32[]{:S(2)}, u32[]{:S(2)}) collective-permute-start(bf16[2,2,4,128,128]{4,3,2,1,0:T(8,128)(2,1)S(1)} %bitcast.430), channel_id=1, source_target_pairs={{0,2},{2,0},{4,6},{6,4},{1,3},{3,1},{5,7},{7,5},{8,10},{10,8},{12,... | collective-permute-start | bytes 1572872 | tf_op jit(solution)/shard_map/ppermute | solution.py:13
  593.1 177.4 %collective-permute-start.254 = (bf16[2,2,4,128,128]{4,3,2,1,0:T(8,128)(2,1)S(1)}, bf16[2,2,4,128,128]{4,3,2,1,0:T(8,128)(2,1)S(1)}, u32[]{:S(2)}, u32[]{:S(2)}) collective-permute-start(bf16[2,2,4,128,128]{4,3,2,1,0:T(8,128)(2,1)S(1)} %bitcast.429), channel_id=1, source_target_pairs={{0,2},{2,0},{4,6},{6,4},{1,3},{3,1},{5,7},{7,5},{8,10},{10,8},{12,... | collective-permute-start | bytes 1572872 | tf_op jit(solution)/shard_map/ppermute | solution.py:13
  594.2 21.9 %collective-permute-start.158 = (bf16[16,16,128]{2,0,1:T(8,128)(2,1)S(1)}, bf16[16,16,128]{2,0,1:T(8,128)(2,1)S(1)}, u32[]{:S(2)}, u32[]{:S(2)}) collective-permute-start(bf16[16,16,128]{2,0,1:T(8,128)(2,1)S(1)} %get-tuple-element.160), channel_id=1, source_target_pairs={{0,25},{1,24},{8,17},{9,16},{16,9},{17,8},{24,1},{25,0},{2,27},{3,... | collective-permute-start | bytes 196616 | tf_op jit(solution)/shard_map/ppermute | solution.py:13
  594.8 21.3 %collective-permute-start.157 = (bf16[16,16,128]{2,0,1:T(8,128)(2,1)S(1)}, bf16[16,16,128]{2,0,1:T(8,128)(2,1)S(1)}, u32[]{:S(2)}, u32[]{:S(2)}) collective-permute-start(bf16[16,16,128]{2,0,1:T(8,128)(2,1)S(1)} %get-tuple-element.161), channel_id=1, source_target_pairs={{0,24},{1,25},{8,16},{9,17},{16,8},{17,9},{24,0},{25,1},{2,26},{3,... | collective-permute-start | bytes 196616 | tf_op jit(solution)/shard_map/ppermute | solution.py:13
  680.0 204.6 %collective-permute-start.248 = (bf16[2,2,4,128,128]{4,3,2,1,0:T(8,128)(2,1)S(1)}, bf16[2,2,4,128,128]{4,3,2,1,0:T(8,128)(2,1)S(1)}, u32[]{:S(2)}, u32[]{:S(2)}) collective-permute-start(bf16[2,2,4,128,128]{4,3,2,1,0:T(8,128)(2,1)S(1)} %bitcast.431), channel_id=1, source_target_pairs={{0,2},{2,0},{4,6},{6,4},{1,3},{3,1},{5,7},{7,5},{8,10},{10,8},{12,... | collective-permute-start | bytes 1572872 | tf_op jit(solution)/shard_map/ppermute | solution.py:13
  681.1 209.1 %collective-permute-start.250 = (bf16[2,2,4,128,128]{4,3,2,1,0:T(8,128)(2,1)S(1)}, bf16[2,2,4,128,128]{4,3,2,1,0:T(8,128)(2,1)S(1)}, u32[]{:S(2)}, u32[]{:S(2)}) collective-permute-start(bf16[2,2,4,128,128]{4,3,2,1,0:T(8,128)(2,1)S(1)} %bitcast.428), channel_id=1, source_target_pairs={{0,2},{2,0},{4,6},{6,4},{1,3},{3,1},{5,7},{7,5},{8,10},{10,8},{12,... | collective-permute-start | bytes 1572872 | tf_op jit(solution)/shard_map/ppermute | solution.py:13
  766.7 25.9 %collective-permute-start.207 = (bf16[16,16,128]{2,1,0:T(8,128)(2,1)S(1)}, bf16[16,16,128]{2,1,0:T(8,128)(2,1)S(1)}, u32[]{:S(2)}, u32[]{:S(2)}) collective-permute-start(bf16[16,16,128]{2,1,0:T(8,128)(2,1)S(1)} %get-tuple-element.104), channel_id=1, source_target_pairs={{0,25},{1,24},{8,17},{9,16},{16,9},{17,8},{24,1},{25,0},{2,27},{3,... | collective-permute-start | bytes 196616 | tf_op jit(solution)/shard_map/ppermute | solution.py:13
  769.2 22.9 %collective-permute-start.206 = (bf16[16,16,128]{2,1,0:T(8,128)(2,1)S(1)}, bf16[16,16,128]{2,1,0:T(8,128)(2,1)S(1)}, u32[]{:S(2)}, u32[]{:S(2)}) collective-permute-start(bf16[16,16,128]{2,1,0:T(8,128)(2,1)S(1)} %get-tuple-element.105), channel_id=1, source_target_pairs={{0,24},{1,25},{8,16},{9,17},{16,8},{17,9},{24,0},{25,1},{2,26},{3,... | collective-permute-start | bytes 196616 | tf_op jit(solution)/shard_map/ppermute | solution.py:13
  789.6 98.0 %collective-permute-start.253 = (bf16[1,2,4,128,128]{4,3,2,1,0:T(8,128)(2,1)S(1)}, bf16[1,2,4,128,128]{4,3,2,1,0:T(8,128)(2,1)S(1)}, u32[]{:S(2)}, u32[]{:S(2)}) collective-permute-start(bf16[1,2,4,128,128]{4,3,2,1,0:T(8,128)(2,1)S(1)} %constant_dynamic-slice_fusion.1), channel_id=1, source_target_pairs={{0,4},{2,6},{4,0},{6,2},{1,5},{3,7},{5,1},{7,3},{8,12},{10,14},{12... | collective-permute-start | bytes 786440 | tf_op jit(solution)/shard_map/ppermute | solution.py:13
  792.1 95.6 %collective-permute-start.255 = (bf16[1,2,4,128,128]{4,3,2,1,0:T(8,128)(2,1)S(1)}, bf16[1,2,4,128,128]{4,3,2,1,0:T(8,128)(2,1)S(1)}, u32[]{:S(2)}, u32[]{:S(2)}) collective-permute-start(bf16[1,2,4,128,128]{4,3,2,1,0:T(8,128)(2,1)S(1)} %constant_dynamic-slice_fusion), channel_id=1, source_target_pairs={{0,4},{2,6},{4,0},{6,2},{1,5},{3,7},{5,1},{7,3},{8,12},{10,14},{12... | collective-permute-start | bytes 786440 | tf_op jit(solution)/shard_map/ppermute | solution.py:13
  881.9 63.9 %collective-permute-start.244 = (bf16[2,2,4,128,128]{4,3,2,1,0:T(8,128)(2,1)}, bf16[2,2,4,128,128]{4,3,2,1,0:T(8,128)(2,1)}, u32[]{:S(2)}, u32[]{:S(2)}) collective-permute-start(bf16[2,2,4,128,128]{4,3,2,1,0:T(8,128)(2,1)} %bitcast.367), channel_id=1, source_target_pairs={{0,2},{2,0},{4,6},{6,4},{1,3},{3,1},{5,7},{7,5},{8,10},{10,8},{12,... | collective-permute-start | bytes 1572872 | tf_op jit(solution)/shard_map/ppermute | solution.py:13
  884.7 62.4 %collective-permute-start.246 = (bf16[2,2,4,128,128]{4,3,2,1,0:T(8,128)(2,1)}, bf16[2,2,4,128,128]{4,3,2,1,0:T(8,128)(2,1)}, u32[]{:S(2)}, u32[]{:S(2)}) collective-permute-start(bf16[2,2,4,128,128]{4,3,2,1,0:T(8,128)(2,1)} %bitcast.366), channel_id=1, source_target_pairs={{0,2},{2,0},{4,6},{6,4},{1,3},{3,1},{5,7},{7,5},{8,10},{10,8},{12,... | collective-permute-start | bytes 1572872 | tf_op jit(solution)/shard_map/ppermute | solution.py:13
  887.6 24.8 %collective-permute-start.235 = (bf16[16,16,128]{2,1,0:T(8,128)(2,1)S(1)}, bf16[16,16,128]{2,1,0:T(8,128)(2,1)S(1)}, u32[]{:S(2)}, u32[]{:S(2)}) collective-permute-start(bf16[16,16,128]{2,1,0:T(8,128)(2,1)S(1)} %get-tuple-element.72), channel_id=1, source_target_pairs={{0,25},{1,24},{8,17},{9,16},{16,9},{17,8},{24,1},{25,0},{2,27},{3,... | collective-permute-start | bytes 196616 | tf_op jit(solution)/shard_map/ppermute | solution.py:13
  887.7 24.2 %collective-permute-start.234 = (bf16[16,16,128]{2,1,0:T(8,128)(2,1)S(1)}, bf16[16,16,128]{2,1,0:T(8,128)(2,1)S(1)}, u32[]{:S(2)}, u32[]{:S(2)}) collective-permute-start(bf16[16,16,128]{2,1,0:T(8,128)(2,1)S(1)} %get-tuple-element.73), channel_id=1, source_target_pairs={{0,24},{1,25},{8,16},{9,17},{16,8},{17,9},{24,0},{25,1},{2,26},{3,... | collective-permute-start | bytes 196616 | tf_op jit(solution)/shard_map/ppermute | solution.py:13
  911.9 22.7 %collective-permute-start.251 = (bf16[1,2,4,128,128]{4,3,2,1,0:T(8,128)(2,1)}, bf16[1,2,4,128,128]{4,3,2,1,0:T(8,128)(2,1)}, u32[]{:S(2)}, u32[]{:S(2)}) collective-permute-start(bf16[1,2,4,128,128]{4,3,2,1,0:T(8,128)(2,1)} %constant_dynamic-slice_fusion.2), channel_id=1, source_target_pairs={{0,4},{2,6},{4,0},{6,2},{1,5},{3,7},{5,1},{7,3},{8,12},{10,14},{12... | collective-permute-start | bytes 786440 | tf_op jit(solution)/shard_map/ppermute | solution.py:13
  921.9 99.3 %collective-permute-start.239 = (bf16[4,128,128]{2,1,0:T(8,128)(2,1)}, bf16[4,128,128]{2,1,0:T(8,128)(2,1)}, u32[]{:S(2)}, u32[]{:S(2)}) collective-permute-start(bf16[4,128,128]{2,1,0:T(8,128)(2,1)} %bitcast.100), channel_id=1, source_target_pairs={{0,6},{2,14},{4,22},{6,30},{8,4},{10,12},{12,20},{14,28},{16,2},{1... | collective-permute-start | bytes 393224 | tf_op jit(solution)/shard_map/ppermute | solution.py:63
  929.4 91.8 %collective-permute-start.237 = (bf16[4,128,128]{2,1,0:T(8,128)(2,1)}, bf16[4,128,128]{2,1,0:T(8,128)(2,1)}, u32[]{:S(2)}, u32[]{:S(2)}) collective-permute-start(bf16[4,128,128]{2,1,0:T(8,128)(2,1)} %bitcast.96), channel_id=1, source_target_pairs={{0,2},{2,10},{4,18},{6,26},{8,0},{10,8},{12,16},{14,24},{16,6},{18... | collective-permute-start | bytes 393224 | tf_op jit(solution)/shard_map/ppermute | solution.py:63
  934.6 86.7 %collective-permute-start.238 = (bf16[4,128,128]{2,1,0:T(8,128)(2,1)}, bf16[4,128,128]{2,1,0:T(8,128)(2,1)}, u32[]{:S(2)}, u32[]{:S(2)}) collective-permute-start(bf16[4,128,128]{2,1,0:T(8,128)(2,1)} %bitcast.98), channel_id=1, source_target_pairs={{0,4},{2,12},{4,20},{6,28},{8,6},{10,14},{12,22},{14,30},{16,0},{1... | collective-permute-start | bytes 393224 | tf_op jit(solution)/shard_map/ppermute | solution.py:63
  936.7 80.1 %all-to-all-start.3 = ((bf16[4,2,4,128,128]{4,3,2,1,0:T(8,128)(2,1)}), bf16[4,2,4,128,128]{4,3,2,1,0:T(8,128)(2,1)S(1)}, u32[]{:S(2)}, u32[]{:S(2)}) async-start(bf16[4,2,4,128,128]{4,3,2,1,0:T(8,128)(2,1)} %pad_maximum_fusion.3), calls=%async_computation.3 | async-start | bytes 2097152 | tf_op jit(solution)/shard_map/all_to_all | solution.py:147
  947.1 29.3 %collective-permute-start.242 = (bf16[2,2,4,128,128]{4,3,2,1,0:T(8,128)(2,1)}, bf16[2,2,4,128,128]{4,3,2,1,0:T(8,128)(2,1)S(1)}, u32[]{:S(2)}, u32[]{:S(2)}) collective-permute-start(bf16[2,2,4,128,128]{4,3,2,1,0:T(8,128)(2,1)} %bitcast.432), channel_id=1, source_target_pairs={{0,2},{2,0},{4,6},{6,4},{1,3},{3,1},{5,7},{7,5},{8,10},{10,8},{12,... | collective-permute-start | bytes 1572872 | tf_op jit(solution)/shard_map/ppermute | solution.py:13
  977.7 30.7 %collective-permute-start.241 = (bf16[1,2,4,128,128]{4,3,2,1,0:T(8,128)(2,1)S(1)}, bf16[1,2,4,128,128]{4,3,2,1,0:T(8,128)(2,1)S(1)}, u32[]{:S(2)}, u32[]{:S(2)}) collective-permute-start(bf16[1,2,4,128,128]{4,3,2,1,0:T(8,128)(2,1)S(1)} %constant_dynamic-slice_fusion.7), channel_id=1, source_target_pairs={{0,4},{2,6},{4,0},{6,2},{1,5},{3,7},{5,1},{7,3},{8,12},{10,14},{12... | collective-permute-start | bytes 786440 | tf_op jit(solution)/shard_map/ppermute | solution.py:13
  (306 other events, 3110.7 us)
Sparse Core Ops, SparseCore 0:
  35.6 52.8 all-gather.8
  90.1 33.6 all-gather.10
  126.0 27.4 all-gather.12
  175.9 28.0 all-gather.14
  238.1 27.8 all-gather.16
  299.6 28.2 all-gather.18
  352.1 28.0 all-gather.20
  401.6 28.0 all-gather.22

commit v3 on v1

v3 whole, which is shorter than its diff:
```python
import jax
import jax.numpy as jnp
from jax import lax
from jax.sharding import Mesh, PartitionSpec as P

F32 = jnp.float32
BF16 = jnp.bfloat16
WIDE = ("s", "x")
GROUPS = 2
CHAINS = 1


def silu_slope(values):
    sigmoid = jax.nn.sigmoid(values)
    return sigmoid * (1.0 + values * (1.0 - sigmoid))


def group_order(size, sections, groups, peers):
    natural = jnp.arange(size).reshape(groups, peers, sections, -1)
    order = natural.transpose(2, 1, 0, 3).reshape(size)
    return (order[:, None] == jnp.arange(size)[None, :]).astype(BF16)


def exchange(values):
    own, full, rows = values.shape
    pieces = values.transpose(1, 0, 2).reshape(full // own, own, own, rows)
    moved = lax.all_to_all(pieces, WIDE, split_axis=0, concat_axis=0, tiled=True)
    return moved.transpose(1, 0, 2, 3).reshape(own, full, rows)


def body(inputs, cotangent, right_factor, left_factor):
    sections = lax.axis_size("s")
    groups = lax.axis_size("t")
    peers = lax.axis_size("x")
    loops, _, held, size, _ = right_factor.shape
    rows = inputs.shape[2]
    sub = held // sections
    own = sub * groups
    layers = loops * sections
    micros = sections // groups
    s_index = lax.axis_index("s")
    t_index = lax.axis_index("t")
    line = (s_index % micros) * groups + t_index
    order = group_order(size, sections, groups, peers)

    def turned(parts, send_by, place_by, target):
        moved = []
        for mask in range(sections):
            value = lax.dynamic_index_in_dim(parts, send_by ^ mask, 0, keepdims=False)
            pairs = [(s * groups + t, target(s, t, mask)) for s in range(sections) for t in range(groups)]
            moved.append(lax.ppermute(value, ("s", "t"), pairs))
        moved = jnp.stack(moved)
        return jnp.stack(
            [
                lax.dynamic_index_in_dim(moved, place_by ^ part, 0, keepdims=False)
                for part in range(sections)
            ]
        )

    def into(s, t, mask):
        return (((s % micros) * groups + t) ^ mask) * groups + s // micros

    def outof(s, t, mask):
        line_to = s ^ mask
        return (t * micros + line_to // groups) * groups + line_to % groups

    def enter(acts):
        parts = turned(acts.reshape(sections, sub, size, rows), line, s_index, into)
        parts = parts.reshape(micros, own, size, rows).transpose(1, 2, 0, 3)
        parts = parts.reshape(own, size, micros * rows)
        return jnp.einsum("aj,bjr->bar", order, parts, preferred_element_type=F32).astype(BF16)

    def leave(acts):
        acts = jnp.einsum("aj,bar->bjr", order, acts, preferred_element_type=F32).astype(BF16)
        parts = acts.reshape(own, size, micros, rows).transpose(2, 0, 1, 3)
        parts = turned(parts.reshape(sections, sub, size, rows), s_index, line, outof)
        return parts.reshape(1, held * size, rows)

    def split(acts):
        return jnp.split(acts, CHAINS, axis=2)

    def merge(chains):
        return jnp.concatenate(chains, axis=2)

    both = jnp.stack([right_factor[:, 0], left_factor[:, 0]], axis=1)
    both = jnp.einsum("aj,lfbjk,ck->lfbac", order, both, order, preferred_element_type=F32).astype(BF16)
    both = both.reshape(loops, 2, sections, sub, size, size).transpose(0, 2, 1, 3, 4, 5)
    weights = []
    for loop in range(loops):
        moved = [lax.dynamic_index_in_dim(both[loop], s_index, 0, keepdims=False)]
        for mask in range(1, sections):
            value = lax.dynamic_index_in_dim(both[loop], s_index ^ mask, 0, keepdims=False)
            moved.append(lax.ppermute(value, "s", [(s, s ^ mask) for s in range(sections)]))
        moved = jnp.stack(moved)
        for section in range(sections):
            part = lax.dynamic_index_in_dim(moved, s_index ^ section, 0, keepdims=False)
            full = lax.all_gather(part, "t", axis=0, tiled=False)
            weights.append((full[:, 0].reshape(own, size, size), full[:, 1].reshape(own, size, size)))

    current = split(enter(inputs))
    grad = split(enter(cotangent))
    stored = []
    for right, left in weights:
        columns = []
        following = []
        for acts in current:
            mixed = jnp.einsum("bjk,bjr->bkr", right, acts, preferred_element_type=F32).astype(BF16)
            columns.append(exchange(mixed))
        for acts, column in zip(current, columns):
            activated = jax.nn.silu(column.astype(F32)).astype(BF16)
            second = jnp.einsum("kbc,kbr->kcr", left, activated, preferred_element_type=F32).astype(BF16)
            following.append((acts.astype(F32) + exchange(second).astype(F32)).astype(BF16))
        stored.append((current, columns))
        current = following
    outputs = leave(merge(current))

    sums = [None] * layers
    for layer in reversed(range(layers)):
        right, left = weights[layer]
        right_term = 0.0
        left_term = 0.0
        following = []
        for acts, column, grad_out in zip(*stored[layer], grad):
            grad_columns = exchange(grad_out)
            wide = column.astype(F32)
            activated = jax.nn.silu(wide).astype(BF16)
            left_term += jnp.einsum("kbr,kcr->kbc", activated, grad_columns, preferred_element_type=F32)
            grad_act = jnp.einsum("kbc,kcr->kbr", left, grad_columns, preferred_element_type=F32)
            grad_mixed = exchange((grad_act * silu_slope(wide)).astype(BF16))
            right_term += jnp.einsum("bjr,bkr->bjk", acts, grad_mixed, preferred_element_type=F32)
            branch = jnp.einsum("bjk,bkr->bjr", right, grad_mixed, preferred_element_type=F32)
            following.append((grad_out.astype(F32) + branch).astype(BF16))
        grad = following
        terms = jnp.stack(
            [
                right_term.astype(BF16).reshape(groups, sub, size, size),
                left_term.astype(BF16).reshape(groups, sub, size, size),
            ],
            axis=1,
        )
        terms = terms.reshape(2 * own, size, size)
        terms = lax.psum_scatter(terms, "t", scatter_dimension=0, tiled=True)
        sums[layer] = terms.reshape(2, sub, size, size)
    input_grad = leave(merge(grad))

    halves = []
    for loop in range(loops):
        mine = jnp.stack(sums[loop * sections : (loop + 1) * sections])
        moved = lax.all_to_all(mine, "s", split_axis=0, concat_axis=0, tiled=True)
        halves.append(jnp.einsum("aj,sfbac,ck->fsbjk", order, moved, order, preferred_element_type=F32))
    grads = jnp.stack(halves).reshape(loops, 2, 1, held, size, size)
    return (outputs, input_grad, grads[:, 0], grads[:, 1])


def solution(mesh):
    sections = mesh.shape["section"]
    peers = mesh.shape["block"] // GROUPS
    grouped = Mesh(mesh.devices.reshape(sections, GROUPS, peers), ("s", "t", "x"))
    acts = P("s", ("t", "x"), None)
    factor = P(None, "s", ("t", "x"), None, None)
    return jax.shard_map(
        body,
        mesh=grouped,
        in_specs=(acts, acts, factor, factor),
        out_specs=(acts, acts, factor, factor),
        check_vma=False,
    )
```

time: 994 us -> 781 us (0.79)
  waiting for transfers between devices: 375 us -> 126 us
  blocking collectives: 278 us -> 321 us
  local copies, waits for them, and re-layouts: 109 us -> 76.2 us
  starting transfers between devices: 103 us -> 123 us
    unnamed x10 -> x8, waiting for transfers between devices: 218 us -> 0.13 us
    all_gather x0 -> x8, blocking collectives: none -> 104 us  [body(): full = lax.all_gather(part, 't', axis=0, tiled=False)]
    all_to_all x25 -> x18, waiting for transfers between devices: 123 us -> 57.4 us  [the longest x16 57.4 us: exchange(): lax.all_to_all(pieces, WIDE, split_axis=0, concat_axis=0, tiled=True)]
    all_to_all x19 -> x16, blocking collectives: 278 us -> 216 us  [exchange(): lax.all_to_all(pieces, WIDE, split_axis=0, concat_axis=0, tiled=True)]
    ppermute x0 -> x22, waiting for transfers between devices: none -> 57.8 us  [the longest x16 35.9 us: turned(): moved.append(lax.ppermute(value, ('s', 't'), pairs))]
    ppermute x0 -> x22, starting transfers between devices: none -> 44.5 us  [the longest x16 37.4 us: turned(): moved.append(lax.ppermute(value, ('s', 't'), pairs))]
    all_gather x8 -> x0, waiting for transfers between devices: 34.3 us -> none  [body(): full = lax.all_gather(moved[section], 't', axis=0, tiled=False)]
    all_to_all x25 -> x18, starting transfers between devices: 102 us -> 77.6 us  [the longest x16 67.4 us: exchange(): lax.all_to_all(pieces, WIDE, split_axis=0, concat_axis=0, tiled=True)]
  transfers between devices with their start and end apart: 34 -> 48, of which waited for: 26 -> 24; matrix products, arithmetic and copies ran while one was open for 13% -> 16% of each run, Pallas kernels for 0% -> 0%
where the time goes in v3:
time: 781 us; the launch traced here: 768 us
  blocking collectives  321 us (41%)
  waiting for transfers between devices  126 us (16%)
  starting transfers between devices  123 us (16%)
  local copies, waits for them, and re-layouts  76.2 us (10%)
  matrix products  65 us (8%)
  other arithmetic  41.5 us (5%)
  between operations  16.1 us (2%)
    all_to_all x16, blocking collectives, exchange(): lax.all_to_all(pieces, WIDE, split_axis=0, concat_axis=0, tiled=True)  216 us
    all_gather x8, blocking collectives, body(): full = lax.all_gather(part, 't', axis=0, tiled=False)  104 us
    all_to_all x16, starting transfers between devices, exchange(): lax.all_to_all(pieces, WIDE, split_axis=0, concat_axis=0, tiled=True)  67.4 us
    all_to_all x16, waiting for transfers between devices, exchange(): lax.all_to_all(pieces, WIDE, split_axis=0, concat_axis=0, tiled=True)  57.4 us
    ppermute x16, starting transfers between devices, turned(): moved.append(lax.ppermute(value, ('s', 't'), pairs))  37.4 us
    ppermute x16, waiting for transfers between devices, turned(): moved.append(lax.ppermute(value, ('s', 't'), pairs))  35.9 us
    ppermute x6, waiting for transfers between devices, body(): lax.ppermute(value, 's', [(s, s ^ mask) for s in range(sections)])  21.9 us
    unnamed x148, local copies, waits for them, and re-layouts  17.4 us
  transfers between devices with their start and end apart: 48, of which 24 were waited for; matrix products, arithmetic and copies ran while one was open for 16% of the time, Pallas kernels for 0%

profile of v3, /device:TPU:0, one launch (start us, length us, event | category | flops | bytes accessed | tf_op | source)
XLA Modules:
  0.0 768.2 jit_solution(5983318591185704464)
XLA Ops:
  10.7 7.5 collective-permute-start.3
  33.8 5.4 collective-permute-done.1
  46.2 15.4 %all_gather.32 = bf16[2,2,4,128,128]{4,3,2,1,0:T(8,128)(2,1)S(1)} all-gather(bf16[1,2,4,128,128]{4,3,2,1,0:T(8,128)(2,1)S(1)} %get-tuple-element.16), channel_id=1, replica_groups=mesh['s'=4,'t'=2,'x'=4] {'t'}, dimensions={0}, use_global_device_ids=true | all-gather | bytes 786432 | tf_op jit(solution)/shard_map/all_gather | solution.py:97
  62.0 12.4 %all_to_all.170 = bf16[16,8,8,256]{3,1,2,0:T(8,128)(2,1)S(1)} all-to-all(bf16[16,8,8,256]{3,1,2,0:T(8,128)(2,1)S(1)} %copy.190), channel_id=1, replica_groups=mesh['s'=4,'t'=2,'x'=4] {'s','x'}, dimensions={0} | all-to-all | bytes 1048576 | tf_op jit(solution)/shard_map/all_to_all | solution.py:27
  80.8 12.2 %all_gather.33 = bf16[2,2,4,128,128]{4,3,2,1,0:T(8,128)(2,1)S(1)} all-gather(bf16[1,2,4,128,128]{4,3,2,1,0:T(8,128)(2,1)S(1)} %get-tuple-element.19), channel_id=1, replica_groups=mesh['s'=4,'t'=2,'x'=4] {'t'}, dimensions={0}, use_global_device_ids=true | all-gather | bytes 786432 | tf_op jit(solution)/shard_map/all_gather | solution.py:97
  96.6 15.5 %all_to_all.171 = bf16[16,8,8,256]{3,1,2,0:T(8,128)(2,1)S(1)} all-to-all(bf16[16,8,8,256]{3,1,2,0:T(8,128)(2,1)S(1)} %copy.198), channel_id=1, replica_groups=mesh['s'=4,'t'=2,'x'=4] {'s','x'}, dimensions={0} | all-to-all | bytes 1048576 | tf_op jit(solution)/shard_map/all_to_all | solution.py:27
  118.4 12.2 %all_gather.34 = bf16[2,2,4,128,128]{4,3,2,1,0:T(8,128)(2,1)S(1)} all-gather(bf16[1,2,4,128,128]{4,3,2,1,0:T(8,128)(2,1)S(1)} %get-tuple-element.18), channel_id=1, replica_groups=mesh['s'=4,'t'=2,'x'=4] {'t'}, dimensions={0}, use_global_device_ids=true | all-gather | bytes 786432 | tf_op jit(solution)/shard_map/all_gather | solution.py:97
  135.1 15.9 %all_to_all.172 = bf16[16,8,8,256]{3,1,2,0:T(8,128)(2,1)S(1)} all-to-all(bf16[16,8,8,256]{3,1,2,0:T(8,128)(2,1)S(1)} %copy.206), channel_id=1, replica_groups=mesh['s'=4,'t'=2,'x'=4] {'s','x'}, dimensions={0} | all-to-all | bytes 1048576 | tf_op jit(solution)/shard_map/all_to_all | solution.py:27
  157.3 12.2 %all_gather.35 = bf16[2,2,4,128,128]{4,3,2,1,0:T(8,128)(2,1)S(1)} all-gather(bf16[1,2,4,128,128]{4,3,2,1,0:T(8,128)(2,1)S(1)} %copy-done.58), channel_id=1, replica_groups=mesh['s'=4,'t'=2,'x'=4] {'t'}, dimensions={0}, use_global_device_ids=true | all-gather | bytes 786432 | tf_op jit(solution)/shard_map/all_gather | solution.py:97
  173.1 16.1 %all_to_all.173 = bf16[16,8,8,256]{3,1,2,0:T(8,128)(2,1)S(1)} all-to-all(bf16[16,8,8,256]{3,1,2,0:T(8,128)(2,1)S(1)} %copy.214), channel_id=1, replica_groups=mesh['s'=4,'t'=2,'x'=4] {'s','x'}, dimensions={0} | all-to-all | bytes 1048576 | tf_op jit(solution)/shard_map/all_to_all | solution.py:27
  197.7 11.7 %collective-permute-done.9 = bf16[2,4,128,128]{3,2,1,0:T(8,128)(2,1)S(1)} collective-permute-done((bf16[2,4,128,128]{3,2,1,0:T(8,128)(2,1)S(1)}, bf16[2,4,128,128]{3,2,1,0:T(8,128)(2,1)S(1)}, u32[]{:S(2)}, u32[]{:S(2)}) %collective-permute-start.9) | collective-permute-done | bytes 262176 | tf_op jit(solution)/shard_map/ppermute | solution.py:93
  209.4 6.1 collective-permute-done.8
  216.6 15.6 %all_gather.36 = bf16[2,2,4,128,128]{4,3,2,1,0:T(8,128)(2,1)S(1)} all-gather(bf16[1,2,4,128,128]{4,3,2,1,0:T(8,128)(2,1)S(1)} %get-tuple-element.24), channel_id=1, replica_groups=mesh['s'=4,'t'=2,'x'=4] {'t'}, dimensions={0}, use_global_device_ids=true | all-gather | bytes 786432 | tf_op jit(solution)/shard_map/all_gather | solution.py:97
  236.2 12.4 %all_to_all.174 = bf16[16,8,8,256]{3,1,2,0:T(8,128)(2,1)S(1)} all-to-all(bf16[16,8,8,256]{3,1,2,0:T(8,128)(2,1)S(1)} %copy.222), channel_id=1, replica_groups=mesh['s'=4,'t'=2,'x'=4] {'s','x'}, dimensions={0} | all-to-all | bytes 1048576 | tf_op jit(solution)/shard_map/all_to_all | solution.py:27
  255.6 12.3 %all_gather.37 = bf16[2,2,4,128,128]{4,3,2,1,0:T(8,128)(2,1)S(1)} all-gather(bf16[1,2,4,128,128]{4,3,2,1,0:T(8,128)(2,1)} %get-tuple-element.27), channel_id=1, replica_groups=mesh['s'=4,'t'=2,'x'=4] {'t'}, dimensions={0}, use_global_device_ids=true | all-gather | bytes 786432 | tf_op jit(solution)/shard_map/all_gather | solution.py:97
  274.6 16.1 %all_to_all.175 = bf16[16,8,8,256]{3,1,2,0:T(8,128)(2,1)S(1)} all-to-all(bf16[16,8,8,256]{3,1,2,0:T(8,128)(2,1)S(1)} %copy.230), channel_id=1, replica_groups=mesh['s'=4,'t'=2,'x'=4] {'s','x'}, dimensions={0} | all-to-all | bytes 1048576 | tf_op jit(solution)/shard_map/all_to_all | solution.py:27
  297.2 12.3 %all_gather.38 = bf16[2,2,4,128,128]{4,3,2,1,0:T(8,128)(2,1)S(1)} all-gather(bf16[1,2,4,128,128]{4,3,2,1,0:T(8,128)(2,1)} %get-tuple-element.26), channel_id=1, replica_groups=mesh['s'=4,'t'=2,'x'=4] {'t'}, dimensions={0}, use_global_device_ids=true | all-gather | bytes 786432 | tf_op jit(solution)/shard_map/all_gather | solution.py:97
  315.2 16.1 %all_to_all.176 = bf16[16,8,8,256]{3,1,2,0:T(8,128)(2,1)S(1)} all-to-all(bf16[16,8,8,256]{3,1,2,0:T(8,128)(2,1)S(1)} %copy.238), channel_id=1, replica_groups=mesh['s'=4,'t'=2,'x'=4] {'s','x'}, dimensions={0} | all-to-all | bytes 1048576 | tf_op jit(solution)/shard_map/all_to_all | solution.py:27
  334.1 4.2 all-to-all-start.13
  338.4 12.2 %all_gather.39 = bf16[2,2,4,128,128]{4,3,2,1,0:T(8,128)(2,1)S(1)} all-gather(bf16[1,2,4,128,128]{4,3,2,1,0:T(8,128)(2,1)S(1)} %copy-done.57), channel_id=1, replica_groups=mesh['s'=4,'t'=2,'x'=4] {'t'}, dimensions={0}, use_global_device_ids=true | all-gather | bytes 786432 | tf_op jit(solution)/shard_map/all_gather | solution.py:97
  359.0 6.6 all-to-all-start.14
  366.3 8.0 %collective-permute-start.17 = (bf16[4,128,128]{2,1,0:T(8,128)(2,1)S(1)}, bf16[4,128,128]{2,1,0:T(8,128)(2,1)S(1)}, u32[]{:S(2)}, u32[]{:S(2)}) collective-permute-start(bf16[4,128,128]{2,1,0:T(8,128)(2,1)S(1)} %get-tuple-element.45), channel_id=1, source_target_pairs={{0,24},{4,16},{8,8},{12,0},{16,28},{20,20},{24,12},{28,4},{1,25},{... | collective-permute-start | bytes 393224 | tf_op jit(solution)/shard_map/ppermute | solution.py:51
  379.5 15.3 %collective-permute-done.15 = bf16[4,128,128]{2,1,0:T(8,128)(2,1)S(1)} collective-permute-done((bf16[4,128,128]{2,1,0:T(8,128)(2,1)S(1)}, bf16[4,128,128]{2,1,0:T(8,128)(2,1)S(1)}, u32[]{:S(2)}, u32[]{:S(2)}) %collective-permute-start.15) | collective-permute-done | bytes 131104 | tf_op jit(solution)/shard_map/ppermute | solution.py:51
  397.1 4.7 all-to-all-start.16
  403.0 8.1 %all-to-all-done.16 = bf16[16,8,8,256]{3,1,2,0:T(8,128)(2,1)} async-done(((bf16[16,8,8,256]{3,1,2,0:T(8,128)(2,1)}), bf16[16,8,8,256]{3,1,2,0:T(8,128)(2,1)}, u32[]{:S(2)}, u32[]{:S(2)}) %all-to-all-start.16) | async-done | bytes 524320 | tf_op jit(solution)/shard_map/all_to_all | solution.py:27
  412.9 12.4 %all_to_all.177 = bf16[16,8,8,256]{3,1,2,0:T(8,128)(2,1)S(1)} all-to-all(bf16[16,8,8,256]{3,1,2,0:T(8,128)(2,1)S(1)} %copy.256), channel_id=1, replica_groups=mesh['s'=4,'t'=2,'x'=4] {'s','x'}, dimensions={0} | all-to-all | bytes 1048576 | tf_op jit(solution)/shard_map/all_to_all | solution.py:27
  426.6 12.5 %all_to_all.178 = bf16[16,8,8,256]{3,1,2,0:T(8,128)(2,1)S(1)} all-to-all(bf16[16,8,8,256]{3,1,2,0:T(8,128)(2,1)S(1)} %copy.259), channel_id=1, replica_groups=mesh['s'=4,'t'=2,'x'=4] {'s','x'}, dimensions={0} | all-to-all | bytes 1048576 | tf_op jit(solution)/shard_map/all_to_all | solution.py:27
  439.9 12.3 %all_to_all.179 = bf16[16,8,8,256]{3,1,2,0:T(8,128)(2,1)S(1)} all-to-all(bf16[16,8,8,256]{3,1,2,0:T(8,128)(2,1)S(1)} %copy.262), channel_id=1, replica_groups=mesh['s'=4,'t'=2,'x'=4] {'s','x'}, dimensions={0} | all-to-all | bytes 1048576 | tf_op jit(solution)/shard_map/all_to_all | solution.py:27
  453.6 12.3 %all_to_all.180 = bf16[16,8,8,256]{3,1,2,0:T(8,128)(2,1)S(1)} all-to-all(bf16[16,8,8,256]{3,1,2,0:T(8,128)(2,1)S(1)} %copy.265), channel_id=1, replica_groups=mesh['s'=4,'t'=2,'x'=4] {'s','x'}, dimensions={0} | all-to-all | bytes 1048576 | tf_op jit(solution)/shard_map/all_to_all | solution.py:27
  466.8 12.5 %all_to_all.181 = bf16[16,8,8,256]{3,1,2,0:T(8,128)(2,1)S(1)} all-to-all(bf16[16,8,8,256]{3,1,2,0:T(8,128)(2,1)S(1)} %copy.268), channel_id=1, replica_groups=mesh['s'=4,'t'=2,'x'=4] {'s','x'}, dimensions={0} | all-to-all | bytes 1048576 | tf_op jit(solution)/shard_map/all_to_all | solution.py:27
  480.6 12.5 %all_to_all.182 = bf16[16,8,8,256]{3,1,2,0:T(8,128)(2,1)S(1)} all-to-all(bf16[16,8,8,256]{3,1,2,0:T(8,128)(2,1)S(1)} %copy.271), channel_id=1, replica_groups=mesh['s'=4,'t'=2,'x'=4] {'s','x'}, dimensions={0} | all-to-all | bytes 1048576 | tf_op jit(solution)/shard_map/all_to_all | solution.py:27
  493.9 12.5 %all_to_all.183 = bf16[16,8,8,256]{3,1,2,0:T(8,128)(2,1)S(1)} all-to-all(bf16[16,8,8,256]{3,1,2,0:T(8,128)(2,1)S(1)} %copy.274), channel_id=1, replica_groups=mesh['s'=4,'t'=2,'x'=4] {'s','x'}, dimensions={0} | all-to-all | bytes 1048576 | tf_op jit(solution)/shard_map/all_to_all | solution.py:27
  507.8 12.3 %all_to_all.184 = bf16[16,8,8,256]{3,1,2,0:T(8,128)(2,1)S(1)} all-to-all(bf16[16,8,8,256]{3,1,2,0:T(8,128)(2,1)S(1)} %copy.277), channel_id=1, replica_groups=mesh['s'=4,'t'=2,'x'=4] {'s','x'}, dimensions={0} | all-to-all | bytes 1048576 | tf_op jit(solution)/shard_map/all_to_all | solution.py:27
  521.0 12.5 %all_to_all.185 = bf16[16,8,8,256]{3,1,2,0:T(8,128)(2,1)S(1)} all-to-all(bf16[16,8,8,256]{3,1,2,0:T(8,128)(2,1)S(1)} %copy.280), channel_id=1, replica_groups=mesh['s'=4,'t'=2,'x'=4] {'s','x'}, dimensions={0} | all-to-all | bytes 1048576 | tf_op jit(solution)/shard_map/all_to_all | solution.py:27
  535.5 4.2 all-to-all-start.26
  544.4 4.6 all-to-all-done.26
  551.9 4.2 all-to-all-start.27
  560.2 9.9 %all-to-all-done.27 = bf16[16,8,8,256]{3,1,2,0:T(8,128)(2,1)} async-done(((bf16[16,8,8,256]{3,1,2,0:T(8,128)(2,1)}), bf16[16,8,8,256]{3,1,2,0:T(8,128)(2,1)}, u32[]{:S(2)}, u32[]{:S(2)}) %all-to-all-start.27) | async-done | bytes 524320 | tf_op jit(solution)/shard_map/all_to_all | solution.py:27
  574.2 4.3 all-to-all-start.28
  582.7 9.7 %all-to-all-done.28 = bf16[16,8,8,256]{3,1,2,0:T(8,128)(2,1)} async-done(((bf16[16,8,8,256]{3,1,2,0:T(8,128)(2,1)}), bf16[16,8,8,256]{3,1,2,0:T(8,128)(2,1)}, u32[]{:S(2)}, u32[]{:S(2)}) %all-to-all-start.28) | async-done | bytes 524320 | tf_op jit(solution)/shard_map/all_to_all | solution.py:27
  595.3 4.2 all-to-all-start.29
  608.0 5.3 all-to-all-done.29
  629.8 5.0 all-to-all-done.30
  652.3 4.3 all-to-all-start.31
  671.8 6.2 collective-permute-start.13
  697.0 6.7 all-to-all-start.33
  716.6 10.8 %reduce-scatter.9.cloned.1.call-done = bf16[8,128,128]{2,1,0:T(8,128)(2,1)} async-done(((bf16[16,128,128]{2,1,0:T(8,128)(2,1)}), bf16[8,128,128]{2,1,0:T(8,128)(2,1)}) %reduce-scatter.9.cloned.1.call-update) | async-done | bytes 262160 | tf_op jit(solution)/shard_map/reduce_scatter | solution.py:142
  746.8 4.3 collective-permute-done.21
  (415 shorter events, 270.3 us)
Async XLA Ops:
  9.1 20.0 %collective-permute-start = (bf16[4,128,128]{2,1,0:T(8,128)(2,1)}, bf16[4,128,128]{2,1,0:T(8,128)(2,1)S(1)}, u32[]{:S(2)}, u32[]{:S(2)}) collective-permute-start(bf16[4,128,128]{2,1,0:T(8,128)(2,1)} %get-tuple-element.60), channel_id=1, source_target_pairs={{0,0},{4,8},{8,16},{12,24},{16,4},{20,12},{24,20},{28,28},{1,1},{5... | collective-permute-start | bytes 393224 | tf_op jit(solution)/shard_map/ppermute | solution.py:51
  10.7 23.1 %collective-permute-start.3 = (bf16[4,128,128]{2,1,0:T(8,128)(2,1)}, bf16[4,128,128]{2,1,0:T(8,128)(2,1)S(1)}, u32[]{:S(2)}, u32[]{:S(2)}) collective-permute-start(bf16[4,128,128]{2,1,0:T(8,128)(2,1)} %get-tuple-element.61), channel_id=1, source_target_pairs={{0,24},{4,16},{8,8},{12,0},{16,28},{20,20},{24,12},{28,4},{1,25},{... | collective-permute-start | bytes 393224 | tf_op jit(solution)/shard_map/ppermute | solution.py:51
  18.2 15.6 %collective-permute-start.2 = (bf16[4,128,128]{2,1,0:T(8,128)(2,1)}, bf16[4,128,128]{2,1,0:T(8,128)(2,1)}, u32[]{:S(2)}, u32[]{:S(2)}) collective-permute-start(bf16[4,128,128]{2,1,0:T(8,128)(2,1)} %get-tuple-element.62), channel_id=1, source_target_pairs={{0,16},{4,24},{8,0},{12,8},{16,20},{20,28},{24,4},{28,12},{1,17},{... | collective-permute-start | bytes 393224 | tf_op jit(solution)/shard_map/ppermute | solution.py:51
  18.5 20.7 %collective-permute-start.1 = (bf16[4,128,128]{2,1,0:T(8,128)(2,1)S(1)}, bf16[4,128,128]{2,1,0:T(8,128)(2,1)}, u32[]{:S(2)}, u32[]{:S(2)}) collective-permute-start(bf16[4,128,128]{2,1,0:T(8,128)(2,1)S(1)} %get-tuple-element.63), channel_id=1, source_target_pairs={{0,8},{4,0},{8,24},{12,16},{16,12},{20,4},{24,28},{28,20},{1,9},{5... | collective-permute-start | bytes 393224 | tf_op jit(solution)/shard_map/ppermute | solution.py:51
  25.8 15.3 %collective-permute-start.6 = (bf16[2,4,128,128]{3,2,1,0:T(8,128)(2,1)S(1)}, bf16[2,4,128,128]{3,2,1,0:T(8,128)(2,1)S(1)}, u32[]{:S(2)}, u32[]{:S(2)}) collective-permute-start(bf16[2,4,128,128]{3,2,1,0:T(8,128)(2,1)S(1)} %get-tuple-element.21), channel_id=1, source_target_pairs={{0,24},{8,16},{16,8},{24,0},{1,25},{9,17},{17,9},{25,1},{2,26},{10... | collective-permute-start | bytes 786440 | tf_op jit(solution)/shard_map/ppermute | solution.py:93
  29.1 16.1 %collective-permute-start.5 = (bf16[2,4,128,128]{3,2,1,0:T(8,128)(2,1)S(1)}, bf16[2,4,128,128]{3,2,1,0:T(8,128)(2,1)S(1)}, u32[]{:S(2)}, u32[]{:S(2)}) collective-permute-start(bf16[2,4,128,128]{3,2,1,0:T(8,128)(2,1)S(1)} %get-tuple-element.22), channel_id=1, source_target_pairs={{0,16},{8,24},{16,0},{24,8},{1,17},{9,25},{17,1},{25,9},{2,18},{10... | collective-permute-start | bytes 786440 | tf_op jit(solution)/shard_map/ppermute | solution.py:93
  33.8 11.4 %collective-permute-start.4 = (bf16[2,4,128,128]{3,2,1,0:T(8,128)(2,1)S(1)}, bf16[2,4,128,128]{3,2,1,0:T(8,128)(2,1)S(1)}, u32[]{:S(2)}, u32[]{:S(2)}) collective-permute-start(bf16[2,4,128,128]{3,2,1,0:T(8,128)(2,1)S(1)} %get-tuple-element.23), channel_id=1, source_target_pairs={{0,8},{8,0},{16,24},{24,16},{1,9},{9,1},{17,25},{25,17},{2,10},{10... | collective-permute-start | bytes 786440 | tf_op jit(solution)/shard_map/ppermute | solution.py:93
  77.2 18.4 %all-to-all-start.1 = ((bf16[16,8,8,256]{3,2,1,0:T(8,128)(2,1)}), bf16[16,8,8,256]{3,2,1,0:T(8,128)(2,1)S(1)}, u32[]{:S(2)}, u32[]{:S(2)}) async-start(bf16[16,8,8,256]{3,2,1,0:T(8,128)(2,1)} %copy.192), calls=%async_computation.1 | async-start | bytes 1048576 | tf_op jit(solution)/shard_map/all_to_all | solution.py:27
  114.9 18.4 %all-to-all-start.3 = ((bf16[16,8,8,256]{3,2,1,0:T(8,128)(2,1)}), bf16[16,8,8,256]{3,2,1,0:T(8,128)(2,1)S(1)}, u32[]{:S(2)}, u32[]{:S(2)}) async-start(bf16[16,8,8,256]{3,2,1,0:T(8,128)(2,1)} %copy.200), calls=%async_computation.3 | async-start | bytes 1048576 | tf_op jit(solution)/shard_map/all_to_all | solution.py:27
  153.8 18.4 %all-to-all-start.5 = ((bf16[16,8,8,256]{3,2,1,0:T(8,128)(2,1)}), bf16[16,8,8,256]{3,2,1,0:T(8,128)(2,1)S(1)}, u32[]{:S(2)}, u32[]{:S(2)}) async-start(bf16[16,8,8,256]{3,2,1,0:T(8,128)(2,1)} %copy.208), calls=%async_computation.5 | async-start | bytes 1048576 | tf_op jit(solution)/shard_map/all_to_all | solution.py:27
  192.0 41.0 %all-to-all-start.7 = ((bf16[16,8,8,256]{3,2,1,0:T(8,128)(2,1)}), bf16[16,8,8,256]{3,2,1,0:T(8,128)(2,1)S(1)}, u32[]{:S(2)}, u32[]{:S(2)}) async-start(bf16[16,8,8,256]{3,2,1,0:T(8,128)(2,1)} %copy.216), calls=%async_computation.7 | async-start | bytes 1048576 | tf_op jit(solution)/shard_map/all_to_all | solution.py:27
  195.7 13.7 %collective-permute-start.9 = (bf16[2,4,128,128]{3,2,1,0:T(8,128)(2,1)S(1)}, bf16[2,4,128,128]{3,2,1,0:T(8,128)(2,1)S(1)}, u32[]{:S(2)}, u32[]{:S(2)}) collective-permute-start(bf16[2,4,128,128]{3,2,1,0:T(8,128)(2,1)S(1)} %get-tuple-element.29), channel_id=1, source_target_pairs={{0,24},{8,16},{16,8},{24,0},{1,25},{9,17},{17,9},{25,1},{2,26},{10... | collective-permute-start | bytes 786440 | tf_op jit(solution)/shard_map/ppermute | solution.py:93
  197.4 18.1 %collective-permute-start.8 = (bf16[2,4,128,128]{3,2,1,0:T(8,128)(2,1)S(1)}, bf16[2,4,128,128]{3,2,1,0:T(8,128)(2,1)S(1)}, u32[]{:S(2)}, u32[]{:S(2)}) collective-permute-start(bf16[2,4,128,128]{3,2,1,0:T(8,128)(2,1)S(1)} %get-tuple-element.30), channel_id=1, source_target_pairs={{0,16},{8,24},{16,0},{24,8},{1,17},{9,25},{17,1},{25,9},{2,18},{10... | collective-permute-start | bytes 786440 | tf_op jit(solution)/shard_map/ppermute | solution.py:93
  197.7 17.8 %collective-permute-start.7 = (bf16[2,4,128,128]{3,2,1,0:T(8,128)(2,1)S(1)}, bf16[2,4,128,128]{3,2,1,0:T(8,128)(2,1)S(1)}, u32[]{:S(2)}, u32[]{:S(2)}) collective-permute-start(bf16[2,4,128,128]{3,2,1,0:T(8,128)(2,1)S(1)} %get-tuple-element.31), channel_id=1, source_target_pairs={{0,8},{8,0},{16,24},{24,16},{1,9},{9,1},{17,25},{25,17},{2,10},{10... | collective-permute-start | bytes 786440 | tf_op jit(solution)/shard_map/ppermute | solution.py:93
  251.3 19.1 %all-to-all-start.9 = ((bf16[16,8,8,256]{3,2,1,0:T(8,128)(2,1)}), bf16[16,8,8,256]{3,2,1,0:T(8,128)(2,1)}, u32[]{:S(2)}, u32[]{:S(2)}) async-start(bf16[16,8,8,256]{3,2,1,0:T(8,128)(2,1)} %copy.224), calls=%async_computation.9 | async-start | bytes 1048576 | tf_op jit(solution)/shard_map/all_to_all | solution.py:27
  293.6 18.4 %all-to-all-start.11 = ((bf16[16,8,8,256]{3,2,1,0:T(8,128)(2,1)}), bf16[16,8,8,256]{3,2,1,0:T(8,128)(2,1)S(1)}, u32[]{:S(2)}, u32[]{:S(2)}) async-start(bf16[16,8,8,256]{3,2,1,0:T(8,128)(2,1)} %copy.232), calls=%async_computation.11 | async-start | bytes 1048576 | tf_op jit(solution)/shard_map/all_to_all | solution.py:27
  334.1 19.1 %all-to-all-start.13 = ((bf16[16,8,8,256]{3,2,1,0:T(8,128)(2,1)}), bf16[16,8,8,256]{3,2,1,0:T(8,128)(2,1)}, u32[]{:S(2)}, u32[]{:S(2)}) async-start(bf16[16,8,8,256]{3,2,1,0:T(8,128)(2,1)} %copy.240), calls=%async_computation.13 | async-start | bytes 1048576 | tf_op jit(solution)/shard_map/all_to_all | solution.py:27
  359.0 37.4 %all-to-all-start.14 = ((bf16[16,8,8,256]{3,1,2,0:T(8,128)(2,1)}), bf16[16,8,8,256]{3,1,2,0:T(8,128)(2,1)S(1)}, u32[]{:S(2)}, u32[]{:S(2)}) async-start(bf16[16,8,8,256]{3,1,2,0:T(8,128)(2,1)} %copy.246), calls=%async_computation.14 | async-start | bytes 1048576 | tf_op jit(solution)/shard_map/all_to_all | solution.py:27
  365.7 9.2 %collective-permute-start.14 = (bf16[4,128,128]{2,1,0:T(8,128)(2,1)S(1)}, bf16[4,128,128]{2,1,0:T(8,128)(2,1)S(1)}, u32[]{:S(2)}, u32[]{:S(2)}) collective-permute-start(bf16[4,128,128]{2,1,0:T(8,128)(2,1)S(1)} %get-tuple-element.44), channel_id=1, source_target_pairs={{0,0},{4,8},{8,16},{12,24},{16,4},{20,12},{24,20},{28,28},{1,1},{5... | collective-permute-start | bytes 393224 | tf_op jit(solution)/shard_map/ppermute | solution.py:51
  366.3 10.5 %collective-permute-start.17 = (bf16[4,128,128]{2,1,0:T(8,128)(2,1)S(1)}, bf16[4,128,128]{2,1,0:T(8,128)(2,1)S(1)}, u32[]{:S(2)}, u32[]{:S(2)}) collective-permute-start(bf16[4,128,128]{2,1,0:T(8,128)(2,1)S(1)} %get-tuple-element.45), channel_id=1, source_target_pairs={{0,24},{4,16},{8,8},{12,0},{16,28},{20,20},{24,12},{28,4},{1,25},{... | collective-permute-start | bytes 393224 | tf_op jit(solution)/shard_map/ppermute | solution.py:51
  374.3 5.2 collective-permute-start.16
  374.4 20.4 %collective-permute-start.15 = (bf16[4,128,128]{2,1,0:T(8,128)(2,1)S(1)}, bf16[4,128,128]{2,1,0:T(8,128)(2,1)S(1)}, u32[]{:S(2)}, u32[]{:S(2)}) collective-permute-start(bf16[4,128,128]{2,1,0:T(8,128)(2,1)S(1)} %get-tuple-element.47), channel_id=1, source_target_pairs={{0,8},{4,0},{8,24},{12,16},{16,12},{20,4},{24,28},{28,20},{1,9},{5... | collective-permute-start | bytes 393224 | tf_op jit(solution)/shard_map/ppermute | solution.py:51
  397.1 13.9 %all-to-all-start.16 = ((bf16[16,8,8,256]{3,1,2,0:T(8,128)(2,1)}), bf16[16,8,8,256]{3,1,2,0:T(8,128)(2,1)}, u32[]{:S(2)}, u32[]{:S(2)}) async-start(bf16[16,8,8,256]{3,1,2,0:T(8,128)(2,1)} %copy.253), calls=%async_computation.16 | async-start | bytes 1048576 | tf_op jit(solution)/shard_map/all_to_all | solution.py:27
  535.5 13.5 %all-to-all-start.26 = ((bf16[16,8,8,256]{3,1,2,0:T(8,128)(2,1)}), bf16[16,8,8,256]{3,1,2,0:T(8,128)(2,1)}, u32[]{:S(2)}, u32[]{:S(2)}) async-start(bf16[16,8,8,256]{3,1,2,0:T(8,128)(2,1)} %copy.283), calls=%async_computation.26 | async-start | bytes 1048576 | tf_op jit(solution)/shard_map/all_to_all | solution.py:27
  539.8 147.7 %reduce-scatter.23.cloned.1.call-start = ((), (), s32[]{:S(2)}) async-start(), calls=%async_computation.49 | async-start | bytes 786432 | tf_op jit(solution)/shard_map/reduce_scatter | solution.py:142
  551.9 18.1 %all-to-all-start.27 = ((bf16[16,8,8,256]{3,1,2,0:T(8,128)(2,1)}), bf16[16,8,8,256]{3,1,2,0:T(8,128)(2,1)}, u32[]{:S(2)}, u32[]{:S(2)}) async-start(bf16[16,8,8,256]{3,1,2,0:T(8,128)(2,1)} %copy.286), calls=%async_computation.27 | async-start | bytes 1048576 | tf_op jit(solution)/shard_map/all_to_all | solution.py:27
  556.2 133.1 %reduce-scatter.21.cloned.1.call-start = ((), (), s32[]{:S(2)}) async-start(), calls=%async_computation.48 | async-start | bytes 786432 | tf_op jit(solution)/shard_map/reduce_scatter | solution.py:142
  574.2 18.1 %all-to-all-start.28 = ((bf16[16,8,8,256]{3,1,2,0:T(8,128)(2,1)}), bf16[16,8,8,256]{3,1,2,0:T(8,128)(2,1)}, u32[]{:S(2)}, u32[]{:S(2)}) async-start(bf16[16,8,8,256]{3,1,2,0:T(8,128)(2,1)} %copy.289), calls=%async_computation.28 | async-start | bytes 1048576 | tf_op jit(solution)/shard_map/all_to_all | solution.py:27
  578.5 112.6 %reduce-scatter.19.cloned.1.call-start = ((), (), s32[]{:S(2)}) async-start(), calls=%async_computation.47 | async-start | bytes 786432 | tf_op jit(solution)/shard_map/reduce_scatter | solution.py:142
  595.3 18.1 %all-to-all-start.29 = ((bf16[16,8,8,256]{3,1,2,0:T(8,128)(2,1)}), bf16[16,8,8,256]{3,1,2,0:T(8,128)(2,1)}, u32[]{:S(2)}, u32[]{:S(2)}) async-start(bf16[16,8,8,256]{3,1,2,0:T(8,128)(2,1)} %copy.292), calls=%async_computation.29 | async-start | bytes 1048576 | tf_op jit(solution)/shard_map/all_to_all | solution.py:27
  599.5 93.4 %reduce-scatter.17.cloned.1.call-start = ((), (), s32[]{:S(2)}) async-start(), calls=%async_computation.46 | async-start | bytes 786432 | tf_op jit(solution)/shard_map/reduce_scatter | solution.py:142
  616.8 18.1 %all-to-all-start.30 = ((bf16[16,8,8,256]{3,1,2,0:T(8,128)(2,1)}), bf16[16,8,8,256]{3,1,2,0:T(8,128)(2,1)}, u32[]{:S(2)}, u32[]{:S(2)}) async-start(bf16[16,8,8,256]{3,1,2,0:T(8,128)(2,1)} %copy.295), calls=%async_computation.30 | async-start | bytes 1048576 | tf_op jit(solution)/shard_map/all_to_all | solution.py:27
  621.0 84.7 %reduce-scatter.15.cloned.1.call-start = ((), (), s32[]{:S(2)}) async-start(), calls=%async_computation.45 | async-start | bytes 786432 | tf_op jit(solution)/shard_map/reduce_scatter | solution.py:142
  634.9 17.4 %all-to-all-start.15 = ((bf16[16,8,8,256]{3,2,1,0:T(8,128)(2,1)}), bf16[16,8,8,256]{3,2,1,0:T(8,128)(2,1)}, u32[]{:S(2)}, u32[]{:S(2)}) async-start(bf16[16,8,8,256]{3,2,1,0:T(8,128)(2,1)} %copy.248), calls=%async_computation.15 | async-start | bytes 1048576 | tf_op jit(solution)/shard_map/all_to_all | solution.py:27
  639.1 68.4 %reduce-scatter.13.cloned.1.call-start = ((), (), s32[]{:S(2)}) async-start(), calls=%async_computation.44 | async-start | bytes 786432 | tf_op jit(solution)/shard_map/reduce_scatter | solution.py:142
  652.3 29.9 %all-to-all-start.31 = ((bf16[16,8,8,256]{3,1,2,0:T(8,128)(2,1)}), bf16[16,8,8,256]{3,1,2,0:T(8,128)(2,1)}, u32[]{:S(2)}, u32[]{:S(2)}) async-start(bf16[16,8,8,256]{3,1,2,0:T(8,128)(2,1)} %copy.298), calls=%async_computation.31 | async-start | bytes 1048576 | tf_op jit(solution)/shard_map/all_to_all | solution.py:27
  656.5 52.8 %reduce-scatter.11.cloned.1.call-start = ((), (), s32[]{:S(2)}) async-start(), calls=%async_computation.43 | async-start | bytes 786432 | tf_op jit(solution)/shard_map/reduce_scatter | solution.py:142
  658.5 68.9 %reduce-scatter.9.cloned.1.call-start = ((), (), s32[]{:S(2)}) async-start(), calls=%async_computation.42 | async-start | bytes 786432 | tf_op jit(solution)/shard_map/reduce_scatter | solution.py:142
  669.6 15.9 %collective-permute-start.10 = (bf16[4,128,128]{2,1,0:T(8,128)(2,1)}, bf16[4,128,128]{2,1,0:T(8,128)(2,1)}, u32[]{:S(2)}, u32[]{:S(2)}) collective-permute-start(bf16[4,128,128]{2,1,0:T(8,128)(2,1)} %get-tuple-element.52), channel_id=1, source_target_pairs={{0,0},{4,16},{8,4},{12,20},{16,8},{20,24},{24,12},{28,28},{1,1},{5... | collective-permute-start | bytes 393224 | tf_op jit(solution)/shard_map/ppermute | solution.py:51
  671.8 13.8 %collective-permute-start.13 = (bf16[4,128,128]{2,1,0:T(8,128)(2,1)}, bf16[4,128,128]{2,1,0:T(8,128)(2,1)}, u32[]{:S(2)}, u32[]{:S(2)}) collective-permute-start(bf16[4,128,128]{2,1,0:T(8,128)(2,1)} %get-tuple-element.53), channel_id=1, source_target_pairs={{0,12},{4,28},{8,8},{12,24},{16,4},{20,20},{24,0},{28,16},{1,13},{... | collective-permute-start | bytes 393224 | tf_op jit(solution)/shard_map/ppermute | solution.py:51
  677.9 7.6 collective-permute-start.12
  678.0 7.5 collective-permute-start.11
  697.0 33.7 %all-to-all-start.33 = ((bf16[4,2,4,128,128]{3,4,2,1,0:T(8,128)(2,1)}), bf16[4,2,4,128,128]{3,4,2,1,0:T(8,128)(2,1)}, u32[]{:S(2)}, u32[]{:S(2)}) async-start(bf16[4,2,4,128,128]{3,4,2,1,0:T(8,128)(2,1)} %pad_maximum_fusion.4), calls=%async_computation.41 | async-start | bytes 2097152 | tf_op jit(solution)/shard_map/all_to_all | solution.py:149
  730.8 25.7 %all-to-all-start.32 = ((bf16[4,2,4,128,128]{3,4,2,1,0:T(8,128)(2,1)}), bf16[4,2,4,128,128]{3,4,2,1,0:T(8,128)(2,1)S(1)}, u32[]{:S(2)}, u32[]{:S(2)}) async-start(bf16[4,2,4,128,128]{3,4,2,1,0:T(8,128)(2,1)} %pad_maximum_fusion.3), calls=%async_computation.36 | async-start | bytes 2097152 | tf_op jit(solution)/shard_map/all_to_all | solution.py:149
  735.0 11.8 %collective-permute-start.18 = (bf16[4,128,128]{2,1,0:T(8,128)(2,1)}, bf16[4,128,128]{2,1,0:T(8,128)(2,1)S(1)}, u32[]{:S(2)}, u32[]{:S(2)}) collective-permute-start(bf16[4,128,128]{2,1,0:T(8,128)(2,1)} %get-tuple-element.36), channel_id=1, source_target_pairs={{0,0},{4,16},{8,4},{12,20},{16,8},{20,24},{24,12},{28,28},{1,1},{5... | collective-permute-start | bytes 393224 | tf_op jit(solution)/shard_map/ppermute | solution.py:51
  736.6 14.6 %collective-permute-start.21 = (bf16[4,128,128]{2,1,0:T(8,128)(2,1)}, bf16[4,128,128]{2,1,0:T(8,128)(2,1)}, u32[]{:S(2)}, u32[]{:S(2)}) collective-permute-start(bf16[4,128,128]{2,1,0:T(8,128)(2,1)} %get-tuple-element.37), channel_id=1, source_target_pairs={{0,12},{4,28},{8,8},{12,24},{16,4},{20,20},{24,0},{28,16},{1,13},{... | collective-permute-start | bytes 393224 | tf_op jit(solution)/shard_map/ppermute | solution.py:51
  739.3 15.2 %collective-permute-start.20 = (bf16[4,128,128]{2,1,0:T(8,128)(2,1)S(1)}, bf16[4,128,128]{2,1,0:T(8,128)(2,1)}, u32[]{:S(2)}, u32[]{:S(2)}) collective-permute-start(bf16[4,128,128]{2,1,0:T(8,128)(2,1)S(1)} %get-tuple-element.38), channel_id=1, source_target_pairs={{0,8},{4,24},{8,12},{12,28},{16,0},{20,16},{24,4},{28,20},{1,9},{5... | collective-permute-start | bytes 393224 | tf_op jit(solution)/shard_map/ppermute | solution.py:51
  739.6 14.9 %collective-permute-start.19 = (bf16[4,128,128]{2,1,0:T(8,128)(2,1)S(1)}, bf16[4,128,128]{2,1,0:T(8,128)(2,1)}, u32[]{:S(2)}, u32[]{:S(2)}) collective-permute-start(bf16[4,128,128]{2,1,0:T(8,128)(2,1)S(1)} %get-tuple-element.39), channel_id=1, source_target_pairs={{0,4},{4,20},{8,0},{12,16},{16,12},{20,28},{24,8},{28,24},{1,5},{5... | collective-permute-start | bytes 393224 | tf_op jit(solution)/shard_map/ppermute | solution.py:51
  (73 other events, 761.9 us)
Sparse Core Ops, SparseCore 0:
  544.5 22.6 reduce-scatter.22
  569.6 20.0 reduce-scatter.20
  591.9 20.0 reduce-scatter.18
  614.2 20.0 reduce-scatter.16
  636.4 20.0 reduce-scatter.14
  658.7 20.3 reduce-scatter.12
  681.4 22.9 reduce-scatter.10
  707.3 20.0 reduce-scatter.8

commit v4 on v3

--- a/solution.py
+++ b/solution.py
@@ -8,6 +8,7 @@
 WIDE = ("s", "x")
 GROUPS = 2
 CHAINS = 1
+LAG = 3
 
 
 def silu_slope(values):
@@ -82,20 +83,43 @@
     def merge(chains):
         return jnp.concatenate(chains, axis=2)
 
-    both = jnp.stack([right_factor[:, 0], left_factor[:, 0]], axis=1)
-    both = jnp.einsum("aj,lfbjk,ck->lfbac", order, both, order, preferred_element_type=F32).astype(BF16)
-    both = both.reshape(loops, 2, sections, sub, size, size).transpose(0, 2, 1, 3, 4, 5)
+    def scattered(parts):
+        moved = [lax.dynamic_index_in_dim(parts, s_index, 0, keepdims=False)]
+        for mask in range(1, sections):
+            value = lax.dynamic_index_in_dim(parts, s_index ^ mask, 0, keepdims=False)
+            moved.append(lax.ppermute(value, "s", [(s, s ^ mask) for s in range(sections)]))
+        moved = jnp.stack(moved)
+        return [
+            lax.dynamic_index_in_dim(moved, s_index ^ section, 0, keepdims=False) for section in range(sections)
+        ]
+
+    def gathered(part):
+        moved = [part]
+        step = 1
+        while step < groups:
+            other = [lax.ppermute(one, "t", [(t, t ^ step) for t in range(groups)]) for one in moved]
+            low = (t_index // step) % 2 == 0
+            moved = [jnp.where(low, x, y) for x, y in zip(moved, other)] + [
+                jnp.where(low, y, x) for x, y in zip(moved, other)
+            ]
+            step *= 2
+        full = jnp.concatenate(moved, axis=1)
+        return jnp.einsum("aj,fbjk,ck->fbac", order, full, order, preferred_element_type=F32).astype(BF16)
+
+    right_parts = right_factor[:, 0].reshape(loops, sections, 1, sub, size, size)
+    left_parts = left_factor[:, 0].reshape(loops, sections, 1, sub, size, size)
     weights = []
     for loop in range(loops):
-        moved = [lax.dynamic_index_in_dim(both[loop], s_index, 0, keepdims=False)]
-        for mask in range(1, sections):
-            value = lax.dynamic_index_in_dim(both[loop], s_index ^ mask, 0, keepdims=False)
-            moved.append(lax.ppermute(value, "s", [(s, s ^ mask) for s in range(sections)]))
-        moved = jnp.stack(moved)
-        for section in range(sections):
-            part = lax.dynamic_index_in_dim(moved, s_index ^ section, 0, keepdims=False)
-            full = lax.all_gather(part, "t", axis=0, tiled=False)
-            weights.append((full[:, 0].reshape(own, size, size), full[:, 1].reshape(own, size, size)))
+        if loop == 0:
+            rights = scattered(right_parts[loop])
+            lefts = scattered(left_parts[loop])
+            weights.append((gathered(rights[0])[0], gathered(lefts[0])[0]))
+            parts = [jnp.concatenate(pair) for pair in zip(rights[1:], lefts[1:])]
+        else:
+            parts = scattered(jnp.concatenate([right_parts[loop], left_parts[loop]], axis=1))
+        for part in parts:
+            full = gathered(part)
+            weights.append((full[0], full[1]))
 
     current = split(enter(inputs))
     grad = split(enter(cotangent))
@@ -113,6 +137,18 @@
         stored.append((current, columns))
         current = following
     outputs = leave(merge(current))
+
+    def summed(parts):
+        step = 1
+        while step < groups:
+            pairs = parts.reshape((parts.shape[0] // 2, 2) + parts.shape[1:])
+            bit = (t_index // step) % 2
+            keep = lax.dynamic_index_in_dim(pairs, bit, 1, keepdims=False)
+            give = lax.dynamic_index_in_dim(pairs, 1 - bit, 1, keepdims=False)
+            got = lax.ppermute(give, "t", [(t, t ^ step) for t in range(groups)])
+            parts = (keep.astype(F32) + got.astype(F32)).astype(BF16)
+            step *= 2
+        return parts[0]
 
     sums = [None] * layers
     for layer in reversed(range(layers)):
@@ -131,25 +167,28 @@
             branch = jnp.einsum("bjk,bkr->bjr", right, grad_mixed, preferred_element_type=F32)
             following.append((grad_out.astype(F32) + branch).astype(BF16))
         grad = following
-        terms = jnp.stack(
-            [
-                right_term.astype(BF16).reshape(groups, sub, size, size),
-                left_term.astype(BF16).reshape(groups, sub, size, size),
-            ],
-            axis=1,
-        )
-        terms = terms.reshape(2 * own, size, size)
-        terms = lax.psum_scatter(terms, "t", scatter_dimension=0, tiled=True)
-        sums[layer] = terms.reshape(2, sub, size, size)
+        terms = jnp.stack([right_term.astype(BF16), left_term.astype(BF16)])
+        terms = jnp.einsum("aj,fbac,ck->fbjk", order, terms, order, preferred_element_type=F32).astype(BF16)
+        if layer:
+            grad, terms = lax.optimization_barrier((grad, terms))
+            terms = terms.reshape(2, groups, sub, size, size).transpose(1, 0, 2, 3, 4)
+            terms = terms.reshape(2 * own, size, size)
+            terms = lax.psum_scatter(terms, "t", scatter_dimension=0, tiled=True)
+            sums[layer] = terms.reshape(2, sub, size, size)
+        else:
+            sums[layer] = [summed(terms[f].reshape(groups, sub, size, size)) for f in range(2)]
+        if layer + LAG < layers:
+            grad, sums[layer + LAG] = lax.optimization_barrier((grad, sums[layer + LAG]))
     input_grad = leave(merge(grad))
 
-    halves = []
-    for loop in range(loops):
-        mine = jnp.stack(sums[loop * sections : (loop + 1) * sections])
-        moved = lax.all_to_all(mine, "s", split_axis=0, concat_axis=0, tiled=True)
-        halves.append(jnp.einsum("aj,sfbac,ck->fsbjk", order, moved, order, preferred_element_type=F32))
-    grads = jnp.stack(halves).reshape(loops, 2, 1, held, size, size)
-    return (outputs, input_grad, grads[:, 0], grads[:, 1])
+    grads = []
+    for factor in (1, 0):
+        halves = []
+        for loop in reversed(range(loops)):
+            mine = jnp.stack([sums[loop * sections + section][factor] for section in range(sections)])
+            halves.insert(0, jnp.stack(scattered(mine)).reshape(1, held, size, size))
+        grads.insert(0, jnp.stack(halves).astype(F32))
+    return (outputs, input_grad, grads[0], grads[1])
 
 
 def solution(mesh):

time: 781 us -> 828 us (1.060)
  blocking collectives: 321 us -> 138 us
  waiting for transfers between devices: 126 us -> 282 us
  starting transfers between devices: 123 us -> 178 us
  matrix products: 65 us -> 83.7 us
    all_gather x8 -> x0, blocking collectives: 104 us -> none  [body(): full = lax.all_gather(part, 't', axis=0, tiled=False)]
    ppermute x6 -> x32, waiting for transfers between devices: 21.9 us -> 122 us  [the longest x9 85.9 us: gathered(): lax.ppermute(one, 't', [(t, t ^ step) for t in range(groups)])]
    all_to_all x16 -> x10, blocking collectives: 216 us -> 138 us  [exchange(): lax.all_to_all(pieces, WIDE, split_axis=0, concat_axis=0, tiled=True)]
    ppermute x6 -> x32, starting transfers between devices: 7.1 us -> 43.4 us  [the longest x21 24.3 us: scattered(): lax.ppermute(value, 's', [(s, s ^ mask) for s in range(sections)])]
    all_to_all x16 -> x22, starting transfers between devices: 67.4 us -> 103 us  [exchange(): lax.all_to_all(pieces, WIDE, split_axis=0, concat_axis=0, tiled=True)]
    all_to_all x16 -> x22, waiting for transfers between devices: 57.4 us -> 86.4 us  [exchange(): lax.all_to_all(pieces, WIDE, split_axis=0, concat_axis=0, tiled=True)]
    reduce_scatter x8 -> x7, waiting for transfers between devices: 10.8 us -> 38.3 us  [body(): terms = lax.psum_scatter(terms, 't', scatter_dimension=0, tiled=True)]
    dot_general x3 -> x17, matrix products: 5.38 us -> 28.8 us  [the longest x8 16.2 us: body(): jnp.einsum('aj,fbac,ck->fbjk', order, terms, order, preferred_element_typ...]
  transfers between devices with their start and end apart: 48 -> 77, of which waited for: 24 -> 42; matrix products, arithmetic and copies ran while one was open for 16% -> 13% of each run, Pallas kernels for 0% -> 0%
where the time goes in v4:
time: 828 us; the launch traced here: 815 us
  waiting for transfers between devices  282 us (34%)
  starting transfers between devices  178 us (21%)
  blocking collectives  138 us (17%)
  matrix products  83.7 us (10%)
  local copies, waits for them, and re-layouts  77.1 us (9%)
  other arithmetic  39.3 us (5%)
  between operations  16.7 us (2%)
    all_to_all x10, blocking collectives, exchange(): lax.all_to_all(pieces, WIDE, split_axis=0, concat_axis=0, tiled=True)  138 us
    all_to_all x22, starting transfers between devices, exchange(): lax.all_to_all(pieces, WIDE, split_axis=0, concat_axis=0, tiled=True)  103 us
    all_to_all x22, waiting for transfers between devices, exchange(): lax.all_to_all(pieces, WIDE, split_axis=0, concat_axis=0, tiled=True)  86.4 us
    ppermute x9, waiting for transfers between devices, gathered(): lax.ppermute(one, 't', [(t, t ^ step) for t in range(groups)])  85.9 us
    reduce_scatter x7, waiting for transfers between devices, body(): terms = lax.psum_scatter(terms, 't', scatter_dimension=0, tiled=True)  38.3 us
    ppermute x16, waiting for transfers between devices, turned(): moved.append(lax.ppermute(value, ('s', 't'), pairs))  34.6 us
    ppermute x16, starting transfers between devices, turned(): moved.append(lax.ppermute(value, ('s', 't'), pairs))  31.2 us
    ppermute x21, waiting for transfers between devices, scattered(): lax.ppermute(value, 's', [(s, s ^ mask) for s in range(sections)])  26.9 us
  transfers between devices with their start and end apart: 77, of which 42 were waited for; matrix products, arithmetic and copies ran while one was open for 13% of the time, Pallas kernels for 0%

profile of v4, /device:TPU:0, one launch (start us, length us, event | category | flops | bytes accessed | tf_op | source)
XLA Modules:
  0.0 814.6 jit_solution(9726387639221421431)
XLA Ops:
  9.1 8.4 %collective-permute-start.3 = (bf16[4,128,128]{2,1,0:T(8,128)(2,1)S(1)}, bf16[4,128,128]{2,1,0:T(8,128)(2,1)S(1)}, u32[]{:S(2)}, u32[]{:S(2)}) collective-permute-start(bf16[4,128,128]{2,1,0:T(8,128)(2,1)S(1)} %get-tuple-element.149), channel_id=1, source_target_pairs={{0,24},{4,16},{8,8},{12,0},{16,28},{20,20},{24,12},{28,4},{1,25},{... | collective-permute-start | bytes 393224 | tf_op jit(solution)/shard_map/ppermute | solution.py:52
  26.2 6.7 collective-permute-done.3
  50.3 5.8 collective-permute-done.7
  61.8 8.7 %all-to-all-done = bf16[16,8,8,256]{3,1,2,0:T(8,128)(2,1)S(1)} async-done(((bf16[16,8,8,256]{3,1,2,0:T(8,128)(2,1)}), bf16[16,8,8,256]{3,1,2,0:T(8,128)(2,1)S(1)}, u32[]{:S(2)}, u32[]{:S(2)}) %all-to-all-start) | async-done | bytes 524320 | tf_op jit(solution)/shard_map/all_to_all | solution.py:28
  78.1 14.0 %collective-permute-done.12 = bf16[2,4,128,128]{2,3,1,0:T(8,128)(2,1)S(1)} collective-permute-done((bf16[2,4,128,128]{2,3,1,0:T(8,128)(2,1)S(1)}, bf16[2,4,128,128]{2,3,1,0:T(8,128)(2,1)S(1)}, u32[]{:S(2)}, u32[]{:S(2)}) %collective-permute-start.12) | collective-permute-done | bytes 262176 | tf_op jit(solution)/shard_map/ppermute | solution.py:100
  93.7 13.1 %all_to_all.160 = bf16[16,8,8,256]{3,1,2,0:T(8,128)(2,1)S(1)} all-to-all(bf16[16,8,8,256]{3,1,2,0:T(8,128)(2,1)S(1)} %copy.176), channel_id=1, replica_groups=mesh['s'=4,'t'=2,'x'=4] {'s','x'}, dimensions={0} | all-to-all | bytes 1048576 | tf_op jit(solution)/shard_map/all_to_all | solution.py:28
  116.2 9.4 %collective-permute-done.13 = bf16[2,4,128,128]{2,3,1,0:T(8,128)(2,1)S(1)} collective-permute-done((bf16[2,4,128,128]{2,3,1,0:T(8,128)(2,1)S(1)}, bf16[2,4,128,128]{2,3,1,0:T(8,128)(2,1)S(1)}, u32[]{:S(2)}, u32[]{:S(2)}) %collective-permute-start.13) | collective-permute-done | bytes 262176 | tf_op jit(solution)/shard_map/ppermute | solution.py:100
  125.6 13.9 %collective-permute-done.14 = bf16[2,4,128,128]{2,3,1,0:T(8,128)(2,1)S(1)} collective-permute-done((bf16[2,4,128,128]{2,3,1,0:T(8,128)(2,1)S(1)}, bf16[2,4,128,128]{2,3,1,0:T(8,128)(2,1)S(1)}, u32[]{:S(2)}, u32[]{:S(2)}) %collective-permute-start.14) | collective-permute-done | bytes 262176 | tf_op jit(solution)/shard_map/ppermute | solution.py:100
  143.6 13.1 %all_to_all.161 = bf16[16,8,8,256]{3,1,2,0:T(8,128)(2,1)S(1)} all-to-all(bf16[16,8,8,256]{3,1,2,0:T(8,128)(2,1)S(1)} %copy.185), channel_id=1, replica_groups=mesh['s'=4,'t'=2,'x'=4] {'s','x'}, dimensions={0} | all-to-all | bytes 1048576 | tf_op jit(solution)/shard_map/all_to_all | solution.py:28
  165.0 7.8 all-to-all-done.5
  196.5 7.7 collective-permute-done.17
  209.3 12.0 %collective-permute-done.18 = bf16[2,4,128,128]{2,3,1,0:T(8,128)(2,1)S(1)} collective-permute-done((bf16[2,4,128,128]{2,3,1,0:T(8,128)(2,1)S(1)}, bf16[2,4,128,128]{2,3,1,0:T(8,128)(2,1)S(1)}, u32[]{:S(2)}, u32[]{:S(2)}) %collective-permute-start.18) | collective-permute-done | bytes 262176 | tf_op jit(solution)/shard_map/ppermute | solution.py:100
  227.0 13.5 %all_to_all.162 = bf16[16,8,8,256]{3,1,2,0:T(8,128)(2,1)S(1)} all-to-all(bf16[16,8,8,256]{3,1,2,0:T(8,128)(2,1)S(1)} %copy.205), channel_id=1, replica_groups=mesh['s'=4,'t'=2,'x'=4] {'s','x'}, dimensions={0} | all-to-all | bytes 1048576 | tf_op jit(solution)/shard_map/all_to_all | solution.py:28
  251.2 8.8 %collective-permute-done.19 = bf16[2,4,128,128]{2,3,1,0:T(8,128)(2,1)S(1)} collective-permute-done((bf16[2,4,128,128]{2,3,1,0:T(8,128)(2,1)}, bf16[2,4,128,128]{2,3,1,0:T(8,128)(2,1)S(1)}, u32[]{:S(2)}, u32[]{:S(2)}) %collective-permute-start.19) | collective-permute-done | bytes 262176 | tf_op jit(solution)/shard_map/ppermute | solution.py:100
  270.7 17.6 %all_to_all.163 = bf16[16,8,8,256]{3,1,2,0:T(8,128)(2,1)S(1)} all-to-all(bf16[16,8,8,256]{3,1,2,0:T(8,128)(2,1)S(1)} %copy.214), channel_id=1, replica_groups=mesh['s'=4,'t'=2,'x'=4] {'s','x'}, dimensions={0} | all-to-all | bytes 1048576 | tf_op jit(solution)/shard_map/all_to_all | solution.py:28
  298.2 9.5 %collective-permute-done.20 = bf16[2,4,128,128]{2,3,1,0:T(8,128)(2,1)S(1)} collective-permute-done((bf16[2,4,128,128]{2,3,1,0:T(8,128)(2,1)}, bf16[2,4,128,128]{2,3,1,0:T(8,128)(2,1)S(1)}, u32[]{:S(2)}, u32[]{:S(2)}) %collective-permute-start.20) | collective-permute-done | bytes 262176 | tf_op jit(solution)/shard_map/ppermute | solution.py:100
  318.3 17.1 %all_to_all.164 = bf16[16,8,8,256]{3,1,2,0:T(8,128)(2,1)S(1)} all-to-all(bf16[16,8,8,256]{3,1,2,0:T(8,128)(2,1)S(1)} %copy.223), channel_id=1, replica_groups=mesh['s'=4,'t'=2,'x'=4] {'s','x'}, dimensions={0} | all-to-all | bytes 1048576 | tf_op jit(solution)/shard_map/all_to_all | solution.py:28
  345.0 9.4 %collective-permute-done.21 = bf16[2,4,128,128]{2,3,1,0:T(8,128)(2,1)S(1)} collective-permute-done((bf16[2,4,128,128]{2,3,1,0:T(8,128)(2,1)S(1)}, bf16[2,4,128,128]{2,3,1,0:T(8,128)(2,1)S(1)}, u32[]{:S(2)}, u32[]{:S(2)}) %collective-permute-start.21) | collective-permute-done | bytes 262176 | tf_op jit(solution)/shard_map/ppermute | solution.py:100
  365.0 8.0 all-to-all-start.14
  374.8 7.2 collective-permute-start.29
  382.6 14.2 %collective-permute-done.29 = bf16[4,128,128]{2,1,0:T(8,128)(2,1)S(1)} collective-permute-done((bf16[4,128,128]{2,1,0:T(8,128)(2,1)S(1)}, bf16[4,128,128]{2,1,0:T(8,128)(2,1)S(1)}, u32[]{:S(2)}, u32[]{:S(2)}) %collective-permute-start.29) | collective-permute-done | bytes 131104 | tf_op jit(solution)/shard_map/ppermute | solution.py:52
  396.9 6.1 collective-permute-done.27
  411.6 7.1 all-to-all-done.16
  429.7 5.4 all-to-all-done.17
  443.2 12.4 %all_to_all.165 = bf16[16,8,8,256]{3,1,2,0:T(8,128)(2,1)S(1)} all-to-all(bf16[16,8,8,256]{3,1,2,0:T(8,128)(2,1)S(1)} %copy.247), channel_id=1, replica_groups=mesh['s'=4,'t'=2,'x'=4] {'s','x'}, dimensions={0} | all-to-all | bytes 1048576 | tf_op jit(solution)/shard_map/all_to_all | solution.py:28
  463.0 7.7 all-to-all-done.19
  478.9 12.4 %all_to_all.166 = bf16[16,8,8,256]{3,1,2,0:T(8,128)(2,1)S(1)} all-to-all(bf16[16,8,8,256]{3,1,2,0:T(8,128)(2,1)S(1)} %copy.254), channel_id=1, replica_groups=mesh['s'=4,'t'=2,'x'=4] {'s','x'}, dimensions={0} | all-to-all | bytes 1048576 | tf_op jit(solution)/shard_map/all_to_all | solution.py:28
  492.9 4.5 all-to-all-start.21
  498.9 7.7 all-to-all-done.21
  514.8 12.4 %all_to_all.167 = bf16[16,8,8,256]{3,1,2,0:T(8,128)(2,1)S(1)} all-to-all(bf16[16,8,8,256]{3,1,2,0:T(8,128)(2,1)S(1)} %copy.261), channel_id=1, replica_groups=mesh['s'=4,'t'=2,'x'=4] {'s','x'}, dimensions={0} | all-to-all | bytes 1048576 | tf_op jit(solution)/shard_map/all_to_all | solution.py:28
  536.7 5.7 all-to-all-done.23
  548.4 10.1 %reduce-scatter.8.cloned.1.call-done = bf16[8,128,128]{2,1,0:T(8,128)(2,1)} async-done(((bf16[16,128,128]{2,1,0:T(8,128)(2,1)}), bf16[8,128,128]{2,1,0:T(8,128)(2,1)}) %reduce-scatter.8.cloned.1.call-update) | async-done | bytes 262160 | tf_op jit(solution)/shard_map/reduce_scatter | solution.py:176
  558.5 13.0 %all_to_all.168 = bf16[16,8,8,256]{3,1,2,0:T(8,128)(2,1)S(1)} all-to-all(bf16[16,8,8,256]{3,1,2,0:T(8,128)(2,1)S(1)} %copy.269), channel_id=1, replica_groups=mesh['s'=4,'t'=2,'x'=4] {'s','x'}, dimensions={0} | all-to-all | bytes 1048576 | tf_op jit(solution)/shard_map/all_to_all | solution.py:28
  573.2 4.3 all-to-all-start.25
  580.9 5.8 all-to-all-done.25
  592.6 9.9 %reduce-scatter.10.cloned.1.call-done = bf16[8,128,128]{2,1,0:T(8,128)(2,1)} async-done(((bf16[16,128,128]{2,1,0:T(8,128)(2,1)}), bf16[8,128,128]{2,1,0:T(8,128)(2,1)}) %reduce-scatter.10.cloned.1.call-update) | async-done | bytes 262160 | tf_op jit(solution)/shard_map/reduce_scatter | solution.py:176
  602.6 13.0 %all_to_all.169 = bf16[16,8,8,256]{3,1,2,0:T(8,128)(2,1)S(1)} all-to-all(bf16[16,8,8,256]{3,1,2,0:T(8,128)(2,1)S(1)} %copy.277), channel_id=1, replica_groups=mesh['s'=4,'t'=2,'x'=4] {'s','x'}, dimensions={0} | all-to-all | bytes 1048576 | tf_op jit(solution)/shard_map/all_to_all | solution.py:28
  624.8 5.9 all-to-all-done.27
  635.1 11.4 %reduce-scatter.12.cloned.1.call-done = bf16[8,128,128]{2,1,0:T(8,128)(2,1)} async-done(((bf16[16,128,128]{2,1,0:T(8,128)(2,1)}), bf16[8,128,128]{2,1,0:T(8,128)(2,1)}) %reduce-scatter.12.cloned.1.call-update) | async-done | bytes 262160 | tf_op jit(solution)/shard_map/reduce_scatter | solution.py:176
  653.5 6.9 all-to-all-done.28
  669.6 4.3 all-to-all-done.15
  697.6 4.3 collective-permute-start.25
  705.0 5.0 collective-permute-done.24
  712.8 15.3 %all-to-all-start.30 = ((bf16[16,8,8,256]{3,1,2,0:T(8,128)(2,1)}), bf16[16,8,8,256]{3,1,2,0:T(8,128)(2,1)S(1)}, u32[]{:S(2)}, u32[]{:S(2)}) async-start(bf16[16,8,8,256]{3,1,2,0:T(8,128)(2,1)} %copy.293), calls=%async_computation.34 | async-start | bytes 1048576 | tf_op jit(solution)/shard_map/all_to_all | solution.py:28
  752.5 7.7 all-to-all-done.31
  761.5 6.8 reduce-scatter.16.cloned.1.call-done
  772.8 4.4 collective-permute-start.33
  777.3 9.7 %collective-permute-done.34 = bf16[1,4,128,128]{3,2,1,0:T(8,128)(2,1)S(1)} collective-permute-done((bf16[1,4,128,128]{3,2,1,0:T(8,128)(2,1)S(1)}, bf16[1,4,128,128]{3,2,1,0:T(8,128)(2,1)S(1)}, u32[]{:S(2)}, u32[]{:S(2)}) %collective-permute-start.34) | collective-permute-done | bytes 131104 | tf_op jit(solution)/shard_map/ppermute | solution.py:148
  (490 shorter events, 352.8 us)
Async XLA Ops:
  8.4 17.4 %collective-permute-start = (bf16[4,128,128]{2,1,0:T(8,128)(2,1)S(1)}, bf16[4,128,128]{2,1,0:T(8,128)(2,1)S(1)}, u32[]{:S(2)}, u32[]{:S(2)}) collective-permute-start(bf16[4,128,128]{2,1,0:T(8,128)(2,1)S(1)} %get-tuple-element.148), channel_id=1, source_target_pairs={{0,0},{4,8},{8,16},{12,24},{16,4},{20,12},{24,20},{28,28},{1,1},{5... | collective-permute-start | bytes 393224 | tf_op jit(solution)/shard_map/ppermute | solution.py:52
  9.1 23.8 %collective-permute-start.3 = (bf16[4,128,128]{2,1,0:T(8,128)(2,1)S(1)}, bf16[4,128,128]{2,1,0:T(8,128)(2,1)S(1)}, u32[]{:S(2)}, u32[]{:S(2)}) collective-permute-start(bf16[4,128,128]{2,1,0:T(8,128)(2,1)S(1)} %get-tuple-element.149), channel_id=1, source_target_pairs={{0,24},{4,16},{8,8},{12,0},{16,28},{20,20},{24,12},{28,4},{1,25},{... | collective-permute-start | bytes 393224 | tf_op jit(solution)/shard_map/ppermute | solution.py:52
  17.5 15.4 %collective-permute-start.2 = (bf16[4,128,128]{2,1,0:T(8,128)(2,1)S(1)}, bf16[4,128,128]{2,1,0:T(8,128)(2,1)S(1)}, u32[]{:S(2)}, u32[]{:S(2)}) collective-permute-start(bf16[4,128,128]{2,1,0:T(8,128)(2,1)S(1)} %get-tuple-element.150), channel_id=1, source_target_pairs={{0,16},{4,24},{8,0},{12,8},{16,20},{20,28},{24,4},{28,12},{1,17},{... | collective-permute-start | bytes 393224 | tf_op jit(solution)/shard_map/ppermute | solution.py:52
  17.8 20.4 %collective-permute-start.1 = (bf16[4,128,128]{2,1,0:T(8,128)(2,1)S(1)}, bf16[4,128,128]{2,1,0:T(8,128)(2,1)S(1)}, u32[]{:S(2)}, u32[]{:S(2)}) collective-permute-start(bf16[4,128,128]{2,1,0:T(8,128)(2,1)S(1)} %get-tuple-element.151), channel_id=1, source_target_pairs={{0,8},{4,0},{8,24},{12,16},{16,12},{20,4},{24,28},{28,20},{1,9},{5... | collective-permute-start | bytes 393224 | tf_op jit(solution)/shard_map/ppermute | solution.py:52
  20.4 19.7 %collective-permute-start.8 = (bf16[1,4,128,128]{2,3,1,0:T(8,128)(2,1)S(1)}, bf16[1,4,128,128]{2,3,1,0:T(8,128)(2,1)S(1)}, u32[]{:S(2)}, u32[]{:S(2)}) collective-permute-start(bf16[1,4,128,128]{2,3,1,0:T(8,128)(2,1)S(1)} %bitcast.909), channel_id=1, source_target_pairs={{0,8},{8,0},{16,24},{24,16},{1,9},{9,1},{17,25},{25,17},{2,10},{10... | collective-permute-start | bytes 393224 | tf_op jit(solution)/shard_map/ppermute | solution.py:90
  25.9 14.3 %collective-permute-start.9 = (bf16[1,4,128,128]{2,3,1,0:T(8,128)(2,1)S(1)}, bf16[1,4,128,128]{2,3,1,0:T(8,128)(2,1)S(1)}, u32[]{:S(2)}, u32[]{:S(2)}) collective-permute-start(bf16[1,4,128,128]{2,3,1,0:T(8,128)(2,1)S(1)} %bitcast.914), channel_id=1, source_target_pairs={{0,16},{8,24},{16,0},{24,8},{1,17},{9,25},{17,1},{25,9},{2,18},{10... | collective-permute-start | bytes 393224 | tf_op jit(solution)/shard_map/ppermute | solution.py:90
  57.7 12.8 %all-to-all-start = ((bf16[16,8,8,256]{3,1,2,0:T(8,128)(2,1)}), bf16[16,8,8,256]{3,1,2,0:T(8,128)(2,1)S(1)}, u32[]{:S(2)}, u32[]{:S(2)}) async-start(bf16[16,8,8,256]{3,1,2,0:T(8,128)(2,1)} %copy.167), calls=%async_computation | async-start | bytes 1048576 | tf_op jit(solution)/shard_map/all_to_all | solution.py:28
  73.3 19.4 %all-to-all-start.1 = ((bf16[16,8,8,256]{3,2,1,0:T(8,128)(2,1)}), bf16[16,8,8,256]{3,2,1,0:T(8,128)(2,1)S(1)}, u32[]{:S(2)}, u32[]{:S(2)}) async-start(bf16[16,8,8,256]{3,2,1,0:T(8,128)(2,1)} %copy.170), calls=%async_computation.1 | async-start | bytes 1048576 | tf_op jit(solution)/shard_map/all_to_all | solution.py:28
  77.0 15.1 %collective-permute-start.12 = (bf16[2,4,128,128]{2,3,1,0:T(8,128)(2,1)S(1)}, bf16[2,4,128,128]{2,3,1,0:T(8,128)(2,1)S(1)}, u32[]{:S(2)}, u32[]{:S(2)}) collective-permute-start(bf16[2,4,128,128]{2,3,1,0:T(8,128)(2,1)S(1)} %pad_maximum_fusion.23), channel_id=1, source_target_pairs={{0,4},{4,0},{1,5},{5,1},{2,6},{6,2},{3,7},{7,3},{8,12},{12,8},{9,1... | collective-permute-start | bytes 786440 | tf_op jit(solution)/shard_map/ppermute | solution.py:100
  109.5 32.2 %all-to-all-start.3 = ((bf16[16,8,8,256]{3,2,1,0:T(8,128)(2,1)}), bf16[16,8,8,256]{3,2,1,0:T(8,128)(2,1)S(1)}, u32[]{:S(2)}, u32[]{:S(2)}) async-start(bf16[16,8,8,256]{3,2,1,0:T(8,128)(2,1)} %copy.179), calls=%async_computation.3 | async-start | bytes 1048576 | tf_op jit(solution)/shard_map/all_to_all | solution.py:28
  115.3 24.3 %collective-permute-start.14 = (bf16[2,4,128,128]{2,3,1,0:T(8,128)(2,1)S(1)}, bf16[2,4,128,128]{2,3,1,0:T(8,128)(2,1)S(1)}, u32[]{:S(2)}, u32[]{:S(2)}) collective-permute-start(bf16[2,4,128,128]{2,3,1,0:T(8,128)(2,1)S(1)} %pad_maximum_fusion.25), channel_id=1, source_target_pairs={{0,4},{4,0},{1,5},{5,1},{2,6},{6,2},{3,7},{7,3},{8,12},{12,8},{9,1... | collective-permute-start | bytes 786440 | tf_op jit(solution)/shard_map/ppermute | solution.py:100
  159.5 13.2 %all-to-all-start.5 = ((bf16[16,8,8,256]{3,2,1,0:T(8,128)(2,1)}), bf16[16,8,8,256]{3,2,1,0:T(8,128)(2,1)S(1)}, u32[]{:S(2)}, u32[]{:S(2)}) async-start(bf16[16,8,8,256]{3,2,1,0:T(8,128)(2,1)} %copy.188), calls=%async_computation.5 | async-start | bytes 1048576 | tf_op jit(solution)/shard_map/all_to_all | solution.py:28
  176.7 12.8 %all-to-all-start.6 = ((bf16[16,8,8,256]{3,1,2,0:T(8,128)(2,1)}), bf16[16,8,8,256]{3,1,2,0:T(8,128)(2,1)S(1)}, u32[]{:S(2)}, u32[]{:S(2)}) async-start(bf16[16,8,8,256]{3,1,2,0:T(8,128)(2,1)} %copy.194), calls=%async_computation.6 | async-start | bytes 1048576 | tf_op jit(solution)/shard_map/all_to_all | solution.py:28
  187.7 16.6 %collective-permute-start.17 = (bf16[2,4,128,128]{2,3,1,0:T(8,128)(2,1)}, bf16[2,4,128,128]{2,3,1,0:T(8,128)(2,1)}, u32[]{:S(2)}, u32[]{:S(2)}) collective-permute-start(bf16[2,4,128,128]{2,3,1,0:T(8,128)(2,1)} %get-tuple-element.59), channel_id=1, source_target_pairs={{0,24},{8,16},{16,8},{24,0},{1,25},{9,17},{17,9},{25,1},{2,26},{10... | collective-permute-start | bytes 786440 | tf_op jit(solution)/shard_map/ppermute | solution.py:90
  192.3 30.5 %all-to-all-start.7 = ((bf16[16,8,8,256]{3,2,1,0:T(8,128)(2,1)}), bf16[16,8,8,256]{3,2,1,0:T(8,128)(2,1)}, u32[]{:S(2)}, u32[]{:S(2)}) async-start(bf16[16,8,8,256]{3,2,1,0:T(8,128)(2,1)} %copy.197), calls=%async_computation.7 | async-start | bytes 1048576 | tf_op jit(solution)/shard_map/all_to_all | solution.py:28
  206.4 14.9 %collective-permute-start.18 = (bf16[2,4,128,128]{2,3,1,0:T(8,128)(2,1)S(1)}, bf16[2,4,128,128]{2,3,1,0:T(8,128)(2,1)S(1)}, u32[]{:S(2)}, u32[]{:S(2)}) collective-permute-start(bf16[2,4,128,128]{2,3,1,0:T(8,128)(2,1)S(1)} %get-tuple-element.55), channel_id=1, source_target_pairs={{0,4},{4,0},{1,5},{5,1},{2,6},{6,2},{3,7},{7,3},{8,12},{12,8},{9,1... | collective-permute-start | bytes 786440 | tf_op jit(solution)/shard_map/ppermute | solution.py:100
  243.5 20.7 %all-to-all-start.9 = ((bf16[16,8,8,256]{3,2,1,0:T(8,128)(2,1)}), bf16[16,8,8,256]{3,2,1,0:T(8,128)(2,1)}, u32[]{:S(2)}, u32[]{:S(2)}) async-start(bf16[16,8,8,256]{3,2,1,0:T(8,128)(2,1)} %copy.208), calls=%async_computation.9 | async-start | bytes 1048576 | tf_op jit(solution)/shard_map/all_to_all | solution.py:28
  291.1 20.7 %all-to-all-start.11 = ((bf16[16,8,8,256]{3,2,1,0:T(8,128)(2,1)}), bf16[16,8,8,256]{3,2,1,0:T(8,128)(2,1)}, u32[]{:S(2)}, u32[]{:S(2)}) async-start(bf16[16,8,8,256]{3,2,1,0:T(8,128)(2,1)} %copy.217), calls=%async_computation.11 | async-start | bytes 1048576 | tf_op jit(solution)/shard_map/all_to_all | solution.py:28
  338.0 19.7 %all-to-all-start.13 = ((bf16[16,8,8,256]{3,2,1,0:T(8,128)(2,1)}), bf16[16,8,8,256]{3,2,1,0:T(8,128)(2,1)}, u32[]{:S(2)}, u32[]{:S(2)}) async-start(bf16[16,8,8,256]{3,2,1,0:T(8,128)(2,1)} %copy.226), calls=%async_computation.13 | async-start | bytes 1048576 | tf_op jit(solution)/shard_map/all_to_all | solution.py:28
  365.0 40.2 %all-to-all-start.14 = ((bf16[16,8,8,256]{3,1,2,0:T(8,128)(2,1)}), bf16[16,8,8,256]{3,1,2,0:T(8,128)(2,1)}, u32[]{:S(2)}, u32[]{:S(2)}) async-start(bf16[16,8,8,256]{3,1,2,0:T(8,128)(2,1)} %copy.232), calls=%async_computation.14 | async-start | bytes 1048576 | tf_op jit(solution)/shard_map/all_to_all | solution.py:28
  374.8 22.1 %collective-permute-start.29 = (bf16[4,128,128]{2,1,0:T(8,128)(2,1)S(1)}, bf16[4,128,128]{2,1,0:T(8,128)(2,1)S(1)}, u32[]{:S(2)}, u32[]{:S(2)}) collective-permute-start(bf16[4,128,128]{2,1,0:T(8,128)(2,1)S(1)} %get-tuple-element.111), channel_id=1, source_target_pairs={{0,24},{4,16},{8,8},{12,0},{16,28},{20,20},{24,12},{28,4},{1,25},{... | collective-permute-start | bytes 393224 | tf_op jit(solution)/shard_map/ppermute | solution.py:52
  382.1 14.8 %collective-permute-start.28 = (bf16[4,128,128]{2,1,0:T(8,128)(2,1)S(1)}, bf16[4,128,128]{2,1,0:T(8,128)(2,1)S(1)}, u32[]{:S(2)}, u32[]{:S(2)}) collective-permute-start(bf16[4,128,128]{2,1,0:T(8,128)(2,1)S(1)} %get-tuple-element.112), channel_id=1, source_target_pairs={{0,16},{4,24},{8,0},{12,8},{16,20},{20,28},{24,4},{28,12},{1,17},{... | collective-permute-start | bytes 393224 | tf_op jit(solution)/shard_map/ppermute | solution.py:52
  382.1 20.8 %collective-permute-start.27 = (bf16[4,128,128]{2,1,0:T(8,128)(2,1)S(1)}, bf16[4,128,128]{2,1,0:T(8,128)(2,1)S(1)}, u32[]{:S(2)}, u32[]{:S(2)}) collective-permute-start(bf16[4,128,128]{2,1,0:T(8,128)(2,1)S(1)} %get-tuple-element.113), channel_id=1, source_target_pairs={{0,8},{4,0},{8,24},{12,16},{16,12},{20,4},{24,28},{28,20},{1,9},{5... | collective-permute-start | bytes 393224 | tf_op jit(solution)/shard_map/ppermute | solution.py:52
  405.2 13.5 %all-to-all-start.16 = ((bf16[16,8,8,256]{3,1,2,0:T(8,128)(2,1)}), bf16[16,8,8,256]{3,1,2,0:T(8,128)(2,1)}, u32[]{:S(2)}, u32[]{:S(2)}) async-start(bf16[16,8,8,256]{3,1,2,0:T(8,128)(2,1)} %copy.240), calls=%async_computation.16 | async-start | bytes 1048576 | tf_op jit(solution)/shard_map/all_to_all | solution.py:28
  421.6 13.5 %all-to-all-start.17 = ((bf16[16,8,8,256]{3,1,2,0:T(8,128)(2,1)}), bf16[16,8,8,256]{3,1,2,0:T(8,128)(2,1)}, u32[]{:S(2)}, u32[]{:S(2)}) async-start(bf16[16,8,8,256]{3,1,2,0:T(8,128)(2,1)} %copy.242), calls=%async_computation.17 | async-start | bytes 1048576 | tf_op jit(solution)/shard_map/all_to_all | solution.py:28
  457.2 13.5 %all-to-all-start.19 = ((bf16[16,8,8,256]{3,1,2,0:T(8,128)(2,1)}), bf16[16,8,8,256]{3,1,2,0:T(8,128)(2,1)}, u32[]{:S(2)}, u32[]{:S(2)}) async-start(bf16[16,8,8,256]{3,1,2,0:T(8,128)(2,1)} %copy.249), calls=%async_computation.19 | async-start | bytes 1048576 | tf_op jit(solution)/shard_map/all_to_all | solution.py:28
  492.9 13.7 %all-to-all-start.21 = ((bf16[16,8,8,256]{3,1,2,0:T(8,128)(2,1)}), bf16[16,8,8,256]{3,1,2,0:T(8,128)(2,1)}, u32[]{:S(2)}, u32[]{:S(2)}) async-start(bf16[16,8,8,256]{3,1,2,0:T(8,128)(2,1)} %copy.256), calls=%async_computation.21 | async-start | bytes 1048576 | tf_op jit(solution)/shard_map/all_to_all | solution.py:28
  528.9 13.5 %all-to-all-start.23 = ((bf16[16,8,8,256]{3,1,2,0:T(8,128)(2,1)}), bf16[16,8,8,256]{3,1,2,0:T(8,128)(2,1)}, u32[]{:S(2)}, u32[]{:S(2)}) async-start(bf16[16,8,8,256]{3,1,2,0:T(8,128)(2,1)} %copy.263), calls=%async_computation.23 | async-start | bytes 1048576 | tf_op jit(solution)/shard_map/all_to_all | solution.py:28
  533.1 25.3 %reduce-scatter.8.cloned.1.call-start = ((), (), s32[]{:S(2)}) async-start(), calls=%async_computation.39 | async-start | bytes 786432 | tf_op jit(solution)/shard_map/reduce_scatter | solution.py:176
  573.2 13.5 %all-to-all-start.25 = ((bf16[16,8,8,256]{3,1,2,0:T(8,128)(2,1)}), bf16[16,8,8,256]{3,1,2,0:T(8,128)(2,1)}, u32[]{:S(2)}, u32[]{:S(2)}) async-start(bf16[16,8,8,256]{3,1,2,0:T(8,128)(2,1)} %copy.271), calls=%async_computation.26 | async-start | bytes 1048576 | tf_op jit(solution)/shard_map/all_to_all | solution.py:28
  577.4 25.1 %reduce-scatter.10.cloned.1.call-start = ((), (), s32[]{:S(2)}) async-start(), calls=%async_computation.40 | async-start | bytes 786432 | tf_op jit(solution)/shard_map/reduce_scatter | solution.py:176
  617.2 13.5 %all-to-all-start.27 = ((bf16[16,8,8,256]{3,1,2,0:T(8,128)(2,1)}), bf16[16,8,8,256]{3,1,2,0:T(8,128)(2,1)}, u32[]{:S(2)}, u32[]{:S(2)}) async-start(bf16[16,8,8,256]{3,1,2,0:T(8,128)(2,1)} %copy.279), calls=%async_computation.29 | async-start | bytes 1048576 | tf_op jit(solution)/shard_map/all_to_all | solution.py:28
  621.5 25.0 %reduce-scatter.12.cloned.1.call-start = ((), (), s32[]{:S(2)}) async-start(), calls=%async_computation.41 | async-start | bytes 786432 | tf_op jit(solution)/shard_map/reduce_scatter | solution.py:176
  647.3 13.1 %all-to-all-start.28 = ((bf16[16,8,8,256]{3,1,2,0:T(8,128)(2,1)}), bf16[16,8,8,256]{3,1,2,0:T(8,128)(2,1)S(1)}, u32[]{:S(2)}, u32[]{:S(2)}) async-start(bf16[16,8,8,256]{3,1,2,0:T(8,128)(2,1)} %copy.285), calls=%async_computation.31 | async-start | bytes 1048576 | tf_op jit(solution)/shard_map/all_to_all | solution.py:28
  664.8 47.2 %reduce-scatter.14.cloned.1.call-start = ((), (), s32[]{:S(2)}) async-start(), calls=%async_computation.42 | async-start | bytes 786432 | tf_op jit(solution)/shard_map/reduce_scatter | solution.py:176
  674.0 17.4 %all-to-all-start.29 = ((bf16[16,8,8,256]{3,1,2,0:T(8,128)(2,1)}), bf16[16,8,8,256]{3,1,2,0:T(8,128)(2,1)S(1)}, u32[]{:S(2)}, u32[]{:S(2)}) async-start(bf16[16,8,8,256]{3,1,2,0:T(8,128)(2,1)} %copy.287), calls=%async_computation.32 | async-start | bytes 1048576 | tf_op jit(solution)/shard_map/all_to_all | solution.py:28
  677.5 50.6 %reduce-scatter.20.cloned.1.call-start = ((), (), s32[]{:S(2)}) async-start(), calls=%async_computation.45 | async-start | bytes 786432 | tf_op jit(solution)/shard_map/reduce_scatter | solution.py:176
  682.1 68.7 %reduce-scatter.18.cloned.1.call-start = ((), (), s32[]{:S(2)}) async-start(), calls=%async_computation.44 | async-start | bytes 786432 | tf_op jit(solution)/shard_map/reduce_scatter | solution.py:176
  696.7 71.7 %reduce-scatter.16.cloned.1.call-start = ((), (), s32[]{:S(2)}) async-start(), calls=%async_computation.43 | async-start | bytes 786432 | tf_op jit(solution)/shard_map/reduce_scatter | solution.py:176
  712.8 30.2 %all-to-all-start.30 = ((bf16[16,8,8,256]{3,1,2,0:T(8,128)(2,1)}), bf16[16,8,8,256]{3,1,2,0:T(8,128)(2,1)S(1)}, u32[]{:S(2)}, u32[]{:S(2)}) async-start(bf16[16,8,8,256]{3,1,2,0:T(8,128)(2,1)} %copy.293), calls=%async_computation.34 | async-start | bytes 1048576 | tf_op jit(solution)/shard_map/all_to_all | solution.py:28
  732.9 16.1 %collective-permute-start.47 = (bf16[4,128,128]{2,1,0:T(8,128)(2,1)}, bf16[4,128,128]{2,1,0:T(8,128)(2,1)}, u32[]{:S(2)}, u32[]{:S(2)}) collective-permute-start(bf16[4,128,128]{2,1,0:T(8,128)(2,1)} %get-tuple-element.79), channel_id=1, source_target_pairs={{0,24},{8,16},{16,8},{24,0},{1,25},{9,17},{17,9},{25,1},{2,26},{10... | collective-permute-start | bytes 393224 | tf_op jit(solution)/shard_map/ppermute | solution.py:90
  734.7 14.3 %collective-permute-start.46 = (bf16[4,128,128]{2,1,0:T(8,128)(2,1)}, bf16[4,128,128]{2,1,0:T(8,128)(2,1)}, u32[]{:S(2)}, u32[]{:S(2)}) collective-permute-start(bf16[4,128,128]{2,1,0:T(8,128)(2,1)} %get-tuple-element.80), channel_id=1, source_target_pairs={{0,16},{8,24},{16,0},{24,8},{1,17},{9,25},{17,1},{25,9},{2,18},{10... | collective-permute-start | bytes 393224 | tf_op jit(solution)/shard_map/ppermute | solution.py:90
  745.4 14.8 %all-to-all-start.31 = ((bf16[16,8,8,256]{3,1,2,0:T(8,128)(2,1)}), bf16[16,8,8,256]{3,1,2,0:T(8,128)(2,1)S(1)}, u32[]{:S(2)}, u32[]{:S(2)}) async-start(bf16[16,8,8,256]{3,1,2,0:T(8,128)(2,1)} %copy.295), calls=%async_computation.35 | async-start | bytes 1048576 | tf_op jit(solution)/shard_map/all_to_all | solution.py:28
  769.1 22.3 %collective-permute-start.41 = (bf16[1,4,128,128]{3,2,1,0:T(8,128)(2,1)S(1)}, bf16[1,4,128,128]{3,2,1,0:T(8,128)(2,1)S(1)}, u32[]{:S(2)}, u32[]{:S(2)}) collective-permute-start(bf16[1,4,128,128]{3,2,1,0:T(8,128)(2,1)S(1)} %dynamic-slice_bitcast_fusion.10), channel_id=1, source_target_pairs={{0,4},{4,0},{1,5},{5,1},{2,6},{6,2},{3,7},{7,3},{8,12},{12,8},{9,1... | collective-permute-start | bytes 393224 | tf_op jit(solution)/shard_map/ppermute | solution.py:148
  769.2 17.8 %collective-permute-start.34 = (bf16[1,4,128,128]{3,2,1,0:T(8,128)(2,1)S(1)}, bf16[1,4,128,128]{3,2,1,0:T(8,128)(2,1)S(1)}, u32[]{:S(2)}, u32[]{:S(2)}) collective-permute-start(bf16[1,4,128,128]{3,2,1,0:T(8,128)(2,1)S(1)} %dynamic-slice_bitcast_fusion.17), channel_id=1, source_target_pairs={{0,4},{4,0},{1,5},{5,1},{2,6},{6,2},{3,7},{7,3},{8,12},{12,8},{9,1... | collective-permute-start | bytes 393224 | tf_op jit(solution)/shard_map/ppermute | solution.py:148
  772.1 15.1 %collective-permute-start.30 = (bf16[4,128,128]{2,1,0:T(8,128)(2,1)S(1)}, bf16[4,128,128]{2,1,0:T(8,128)(2,1)S(1)}, u32[]{:S(2)}, u32[]{:S(2)}) collective-permute-start(bf16[4,128,128]{2,1,0:T(8,128)(2,1)S(1)} %get-tuple-element.102), channel_id=1, source_target_pairs={{0,0},{4,16},{8,4},{12,20},{16,8},{20,24},{24,12},{28,28},{1,1},{5... | collective-permute-start | bytes 393224 | tf_op jit(solution)/shard_map/ppermute | solution.py:52
  772.8 18.0 %collective-permute-start.33 = (bf16[4,128,128]{2,1,0:T(8,128)(2,1)S(1)}, bf16[4,128,128]{2,1,0:T(8,128)(2,1)S(1)}, u32[]{:S(2)}, u32[]{:S(2)}) collective-permute-start(bf16[4,128,128]{2,1,0:T(8,128)(2,1)S(1)} %get-tuple-element.103), channel_id=1, source_target_pairs={{0,12},{4,28},{8,8},{12,24},{16,4},{20,20},{24,0},{28,16},{1,13},{... | collective-permute-start | bytes 393224 | tf_op jit(solution)/shard_map/ppermute | solution.py:52
  777.2 14.0 %collective-permute-start.32 = (bf16[4,128,128]{2,1,0:T(8,128)(2,1)S(1)}, bf16[4,128,128]{2,1,0:T(8,128)(2,1)S(1)}, u32[]{:S(2)}, u32[]{:S(2)}) collective-permute-start(bf16[4,128,128]{2,1,0:T(8,128)(2,1)S(1)} %get-tuple-element.104), channel_id=1, source_target_pairs={{0,8},{4,24},{8,12},{12,28},{16,0},{20,16},{24,4},{28,20},{1,9},{5... | collective-permute-start | bytes 393224 | tf_op jit(solution)/shard_map/ppermute | solution.py:52
  (96 other events, 783.7 us)
Sparse Core Ops, SparseCore 0:
  536.2 22.2 reduce-scatter.7
  581.2 21.3 reduce-scatter.9
  625.1 21.2 reduce-scatter.11
  667.6 21.3 reduce-scatter.13
  691.1 30.5 reduce-scatter.19
  724.5 20.8 reduce-scatter.17
  748.2 20.1 reduce-scatter.15

commit v5 on v3

v5 whole, which is shorter than its diff:
```python
import jax
import jax.numpy as jnp
from jax import lax
from jax.sharding import PartitionSpec as P

F32 = jnp.float32
BF16 = jnp.bfloat16
ALL = ("section", "block")
CHAINS = 2
LAG = 2


def swap(parts, axes):
    return lax.all_to_all(parts, axes, split_axis=0, concat_axis=0, tiled=True)


def silu_slope(values):
    sigmoid = jax.nn.sigmoid(values)
    return sigmoid * (1.0 + values * (1.0 - sigmoid))


def device_order(size, sections, peers):
    natural = jnp.arange(size).reshape(peers, sections, -1)
    order = natural.transpose(1, 0, 2).reshape(size)
    return (order[:, None] == jnp.arange(size)[None, :]).astype(BF16)


def exchange(values):
    own, full, rows = values.shape
    pieces = values.transpose(1, 0, 2).reshape(full // own, own, own, rows)
    moved = swap(pieces, ALL)
    return moved.transpose(1, 0, 2, 3).reshape(own, full, rows)


def body(inputs, cotangent, right_factor, left_factor):
    sections = lax.axis_size("section")
    peers = lax.axis_size("block")
    loops, _, held, size, _ = right_factor.shape
    rows = inputs.shape[2]
    own = held // sections
    layers = loops * sections
    order = device_order(size, sections, peers)

    def enter(acts):
        parts = swap(acts.reshape(sections, own, size, rows), "section")
        parts = parts.transpose(1, 2, 0, 3).reshape(own, size, sections * rows)
        return jnp.einsum("aj,bjr->bar", order, parts, preferred_element_type=F32).astype(BF16)

    def leave(acts):
        acts = jnp.einsum("aj,bar->bjr", order, acts, preferred_element_type=F32).astype(BF16)
        parts = acts.reshape(own, size, sections, rows).transpose(2, 0, 1, 3)
        return swap(parts, "section").reshape(1, held * size, rows)

    def split(acts):
        return jnp.split(acts, CHAINS, axis=2)

    def merge(chains):
        return jnp.concatenate(chains, axis=2)

    weights = []
    for loop in range(loops):
        parts = jnp.stack([right_factor[loop, 0], left_factor[loop, 0]])
        parts = parts.reshape(2, sections, own, size, size).transpose(1, 0, 2, 3, 4)
        moved = swap(parts, "section")
        for section in range(sections):
            full = jnp.einsum(
                "aj,fbjk,ck->fbac", order, moved[section], order, preferred_element_type=F32
            ).astype(BF16)
            weights.append((full[0], full[1]))

    current = split(enter(inputs))
    grad = split(enter(cotangent))
    stored = []
    for right, left in weights:
        columns = []
        following = []
        for acts in current:
            mixed = jnp.einsum("bjk,bjr->bkr", right, acts, preferred_element_type=F32).astype(BF16)
            columns.append(exchange(mixed))
        for acts, column in zip(current, columns):
            activated = jax.nn.silu(column.astype(F32)).astype(BF16)
            second = jnp.einsum("kbc,kbr->kcr", left, activated, preferred_element_type=F32).astype(BF16)
            following.append((acts.astype(F32) + exchange(second).astype(F32)).astype(BF16))
        stored.append((current, columns))
        current = following
    outputs = leave(merge(current))

    sums = [None] * layers
    for layer in reversed(range(layers)):
        right, left = weights[layer]
        right_term = 0.0
        left_term = 0.0
        following = []
        for acts, column, grad_out in zip(*stored[layer], grad):
            grad_columns = exchange(grad_out)
            wide = column.astype(F32)
            activated = jax.nn.silu(wide).astype(BF16)
            left_term += jnp.einsum("kbr,kcr->kbc", activated, grad_columns, preferred_element_type=F32)
            grad_act = jnp.einsum("kbc,kcr->kbr", left, grad_columns, preferred_element_type=F32)
            grad_mixed = exchange((grad_act * silu_slope(wide)).astype(BF16))
            right_term += jnp.einsum("bjr,bkr->bjk", acts, grad_mixed, preferred_element_type=F32)
            branch = jnp.einsum("bjk,bkr->bjr", right, grad_mixed, preferred_element_type=F32)
            following.append((grad_out.astype(F32) + branch).astype(BF16))
        grad = following
        terms = jnp.stack([right_term.astype(BF16), left_term.astype(BF16)])
        sums[layer] = jnp.einsum(
            "aj,fbac,ck->fbjk", order, terms, order, preferred_element_type=F32
        ).astype(BF16)
        if layer + LAG < layers:
            grad, sums[layer + LAG] = lax.optimization_barrier((grad, sums[layer + LAG]))
    input_grad = leave(merge(grad))

    halves = []
    for loop in range(loops):
        moved = swap(jnp.stack(sums[loop * sections : (loop + 1) * sections]), "section")
        halves.append(moved.transpose(1, 0, 2, 3, 4).reshape(2, 1, held, size, size).astype(F32))
    grads = jnp.stack(halves)
    return (outputs, input_grad, grads[:, 0], grads[:, 1])


def solution(mesh):
    acts = P("section", "block", None)
    factor = P(None, "section", "block", None, None)
    return jax.shard_map(
        body,
        mesh=mesh,
        in_specs=(acts, acts, factor, factor),
        out_specs=(acts, acts, factor, factor),
        check_vma=False,
    )
```

time: 781 us -> 1060 us (1.36)
  blocking collectives: 321 us -> 0 us
  waiting for transfers between devices: 126 us -> 395 us
  starting transfers between devices: 123 us -> 250 us
  local copies, waits for them, and re-layouts: 76.2 us -> 194 us
  matrix products: 65 us -> 137 us
  other arithmetic: 41.5 us -> 58.3 us
  between operations: 16.1 us -> 3.46 us
    all_to_all x18 -> x72, waiting for transfers between devices: 57.4 us -> 395 us  [swap(): return lax.all_to_all(parts, axes, split_axis=0, concat_axis=0, tiled=True)]
    all_to_all x16 -> x0, blocking collectives: 216 us -> none  [exchange(): lax.all_to_all(pieces, WIDE, split_axis=0, concat_axis=0, tiled=True)]
    all_to_all x18 -> x72, starting transfers between devices: 77.6 us -> 250 us  [swap(): return lax.all_to_all(parts, axes, split_axis=0, concat_axis=0, tiled=True)]
    reshape x32 -> x112, local copies, waits for them, and re-layouts: 16.3 us -> 127 us  [exchange(): pieces = values.transpose(1, 0, 2).reshape(full // own, own, own, rows)]
    all_gather x8 -> x0, blocking collectives: 104 us -> none  [body(): full = lax.all_gather(part, 't', axis=0, tiled=False)]
    ppermute x22 -> x0, waiting for transfers between devices: 57.8 us -> none  [the longest x16 35.9 us: turned(): moved.append(lax.ppermute(value, ('s', 't'), pairs))]
    ppermute x22 -> x0, starting transfers between devices: 44.5 us -> none  [the longest x16 37.4 us: turned(): moved.append(lax.ppermute(value, ('s', 't'), pairs))]
    convert_element_type x8 -> x32, local copies, waits for them, and re-layouts: 8.73 us -> 41.8 us  [body(): exchange(second).astype(F32)]
  transfers between devices with their start and end apart: 48 -> 72, of which waited for: 24 -> 69; matrix products, arithmetic and copies ran while one was open for 16% -> 35% of each run, Pallas kernels for 0% -> 0%
where the time goes in v5:
time: 1060 us; the launch traced here: 1040 us
  waiting for transfers between devices  395 us (37%)
  starting transfers between devices  250 us (24%)
  local copies, waits for them, and re-layouts  194 us (18%)
  matrix products  137 us (13%)
  other arithmetic  58.3 us (6%)
    all_to_all x72, waiting for transfers between devices, swap(): return lax.all_to_all(parts, axes, split_axis=0, concat_axis=0, tiled=True)  395 us
    all_to_all x72, starting transfers between devices, swap(): return lax.all_to_all(parts, axes, split_axis=0, concat_axis=0, tiled=True)  250 us
    reshape x112, local copies, waits for them, and re-layouts, exchange(): pieces = values.transpose(1, 0, 2).reshape(full // own, own, own, rows)  127 us
    convert_element_type x32, local copies, waits for them, and re-layouts, body(): exchange(second).astype(F32)  41.8 us
    dot_general x16, matrix products, body(): jnp.einsum('kbc,kcr->kbr', left, grad_columns, preferred_element_type=F32)  29 us
    dot_general x16, matrix products, body(): jnp.einsum('kbr,kcr->kbc', activated, grad_columns, preferred_element_typ...  24.4 us
  transfers between devices with their start and end apart: 72, of which 69 were waited for; matrix products, arithmetic and copies ran while one was open for 35% of the time, Pallas kernels for 0%

profile of v5, /device:TPU:0, one launch (start us, length us, event | category | flops | bytes accessed | tf_op | source)
XLA Modules:
  0.0 1037.7 jit_solution(6380192854752662483)
XLA Ops:
  8.3 5.6 all-to-all-done
  17.9 14.0 %all-to-all-done.1 = bf16[4,2,4,128,128]{4,3,2,1,0:T(8,128)(2,1)S(1)} async-done(((bf16[4,2,4,128,128]{4,3,2,1,0:T(8,128)(2,1)}), bf16[4,2,4,128,128]{4,3,2,1,0:T(8,128)(2,1)S(1)}, u32[]{:S(2)}, u32[]{:S(2)}) %all-to-all-start.1) | async-done | bytes 1048608 | tf_op jit(solution)/shard_map/all_to_all | solution.py:14
  36.9 7.2 all-to-all-done.36
  44.1 5.5 all-to-all-start.19
  52.5 7.9 all-to-all-done.19
  64.8 8.8 all-to-all-done.2
  79.3 8.2 all-to-all-done.20
  93.4 8.0 all-to-all-done.3
  114.0 5.3 all-to-all-done.10
  127.2 6.2 all-to-all-done.4
  139.9 7.4 all-to-all-done.21
  153.4 7.8 all-to-all-done.5
  227.4 6.6 all-to-all-done.6
  241.9 6.0 all-to-all-done.24
  279.9 8.8 all-to-all-done.8
  294.4 8.3 all-to-all-done.26
  338.3 7.5 all-to-all-done.11
  353.1 6.5 all-to-all-done.28
  373.6 5.6 all-to-all-start.29
  390.5 6.3 all-to-all-start.13
  400.8 6.6 all-to-all-done.13
  416.0 5.4 all-to-all-done.30
  435.7 5.9 all-to-all-start.31
  452.8 5.9 all-to-all-start.15
  462.7 6.6 all-to-all-done.15
  477.8 5.4 all-to-all-done.32
  511.1 5.6 all-to-all-start.17
  550.0 5.2 all-to-all-done.38
  562.3 6.9 all-to-all-done.45
  605.0 5.3 all-to-all-done.40
  617.6 6.8 all-to-all-done.47
  663.0 5.3 all-to-all-done.42
  677.3 8.8 all-to-all-done.51
  720.0 7.7 all-to-all-done.50
  735.8 5.9 all-to-all-done.18
  746.8 8.1 all-to-all-done.53
  788.3 7.0 all-to-all-done.56
  856.8 7.0 all-to-all-done.58
  885.4 6.8 all-to-all-done.61
  898.5 6.9 all-to-all-done.64
  909.8 8.8 all-to-all-done.62
  924.2 7.6 all-to-all-done.35
  939.8 6.0 all-to-all-done.67
  966.7 6.3 all-to-all-done.68
  979.2 7.0 all-to-all-done.66
  991.8 12.5 %all-to-all-done.71 = bf16[4,2,4,128,128]{4,3,2,1,0:T(8,128)(2,1)S(1)} async-done(((bf16[4,2,4,128,128]{4,3,2,1,0:T(8,128)(2,1)}), bf16[4,2,4,128,128]{4,3,2,1,0:T(8,128)(2,1)S(1)}, u32[]{:S(2)}, u32[]{:S(2)}) %all-to-all-start.71) | async-done | bytes 1048608 | tf_op jit(solution)/shard_map/all_to_all | solution.py:14
  1010.7 6.0 all-to-all-done.69
  1024.3 10.3 all-to-all-done.70
  (619 shorter events, 693.1 us)
Async XLA Ops:
  13.9 18.0 %all-to-all-start.1 = ((bf16[4,2,4,128,128]{4,3,2,1,0:T(8,128)(2,1)}), bf16[4,2,4,128,128]{4,3,2,1,0:T(8,128)(2,1)S(1)}, u32[]{:S(2)}, u32[]{:S(2)}) async-start(bf16[4,2,4,128,128]{4,3,2,1,0:T(8,128)(2,1)} %maximum_bitcast_fusion), calls=%async_computation.1 | async-start | bytes 2097152 | tf_op jit(solution)/shard_map/all_to_all | solution.py:14
  44.1 16.2 %all-to-all-start.19 = ((bf16[32,4,4,256]{3,1,2,0:T(4,128)(2,1)}), bf16[32,4,4,256]{3,1,2,0:T(4,128)(2,1)S(1)}, u32[]{:S(2)}, u32[]{:S(2)}) async-start(bf16[32,4,4,256]{3,1,2,0:T(4,128)(2,1)} %copy.484), calls=%async_computation.19 | async-start | bytes 524288 | tf_op jit(solution)/shard_map/all_to_all | solution.py:14
  87.5 13.9 %all-to-all-start.3 = ((bf16[32,4,4,256]{3,2,1,0:T(4,128)(2,1)}), bf16[32,4,4,256]{3,2,1,0:T(4,128)(2,1)}, u32[]{:S(2)}, u32[]{:S(2)}) async-start(bf16[32,4,4,256]{3,2,1,0:T(4,128)(2,1)} %bitcast.17), calls=%async_computation.3 | async-start | bytes 524288 | tf_op jit(solution)/shard_map/all_to_all | solution.py:14
  101.4 18.0 %all-to-all-start.10 = ((bf16[4,2,4,128,128]{4,3,2,1,0:T(8,128)(2,1)}), bf16[4,2,4,128,128]{4,3,2,1,0:T(8,128)(2,1)S(1)}, u32[]{:S(2)}, u32[]{:S(2)}) async-start(bf16[4,2,4,128,128]{4,3,2,1,0:T(8,128)(2,1)} %maximum_bitcast_fusion.1), calls=%async_computation.10 | async-start | bytes 2097152 | tf_op jit(solution)/shard_map/all_to_all | solution.py:14
  119.4 13.9 %all-to-all-start.4 = ((bf16[32,4,4,256]{3,1,2,0:T(4,128)(2,1)}), bf16[32,4,4,256]{3,1,2,0:T(4,128)(2,1)}, u32[]{:S(2)}, u32[]{:S(2)}) async-start(bf16[32,4,4,256]{3,1,2,0:T(4,128)(2,1)} %copy.430), calls=%async_computation.4 | async-start | bytes 524288 | tf_op jit(solution)/shard_map/all_to_all | solution.py:14
  133.3 13.9 %all-to-all-start.21 = ((bf16[32,4,4,256]{3,1,2,0:T(4,128)(2,1)}), bf16[32,4,4,256]{3,1,2,0:T(4,128)(2,1)}, u32[]{:S(2)}, u32[]{:S(2)}) async-start(bf16[32,4,4,256]{3,1,2,0:T(4,128)(2,1)} %copy.490), calls=%async_computation.21 | async-start | bytes 524288 | tf_op jit(solution)/shard_map/all_to_all | solution.py:14
  147.3 13.9 %all-to-all-start.5 = ((bf16[32,4,4,256]{3,2,1,0:T(4,128)(2,1)}), bf16[32,4,4,256]{3,2,1,0:T(4,128)(2,1)}, u32[]{:S(2)}, u32[]{:S(2)}) async-start(bf16[32,4,4,256]{3,2,1,0:T(4,128)(2,1)} %bitcast.805), calls=%async_computation.5 | async-start | bytes 524288 | tf_op jit(solution)/shard_map/all_to_all | solution.py:14
  175.2 15.0 %all-to-all-start.37 = ((bf16[32,4,4,256]{3,1,2,0:T(4,128)(2,1)}), bf16[32,4,4,256]{3,1,2,0:T(4,128)(2,1)S(1)}, u32[]{:S(2)}, u32[]{:S(2)}) async-start(bf16[32,4,4,256]{3,1,2,0:T(4,128)(2,1)} %copy.535), calls=%async_computation.37 | async-start | bytes 524288 | tf_op jit(solution)/shard_map/all_to_all | solution.py:14
  190.8 15.0 %all-to-all-start.43 = ((bf16[32,4,4,256]{3,1,2,0:T(4,128)(2,1)}), bf16[32,4,4,256]{3,1,2,0:T(4,128)(2,1)}, u32[]{:S(2)}, u32[]{:S(2)}) async-start(bf16[32,4,4,256]{3,1,2,0:T(4,128)(2,1)} %copy.547), calls=%async_computation.43 | async-start | bytes 524288 | tf_op jit(solution)/shard_map/all_to_all | solution.py:14
  205.8 13.9 %all-to-all-start.23 = ((bf16[32,4,4,256]{3,1,2,0:T(4,128)(2,1)}), bf16[32,4,4,256]{3,1,2,0:T(4,128)(2,1)}, u32[]{:S(2)}, u32[]{:S(2)}) async-start(bf16[32,4,4,256]{3,1,2,0:T(4,128)(2,1)} %copy.496), calls=%async_computation.23 | async-start | bytes 524288 | tf_op jit(solution)/shard_map/all_to_all | solution.py:14
  219.8 14.1 %all-to-all-start.6 = ((bf16[32,4,4,256]{3,1,2,0:T(4,128)(2,1)}), bf16[32,4,4,256]{3,1,2,0:T(4,128)(2,1)}, u32[]{:S(2)}, u32[]{:S(2)}) async-start(bf16[32,4,4,256]{3,1,2,0:T(4,128)(2,1)} %copy.438), calls=%async_computation.6 | async-start | bytes 524288 | tf_op jit(solution)/shard_map/all_to_all | solution.py:14
  233.9 13.9 %all-to-all-start.24 = ((bf16[32,4,4,256]{3,2,1,0:T(4,128)(2,1)}), bf16[32,4,4,256]{3,2,1,0:T(4,128)(2,1)}, u32[]{:S(2)}, u32[]{:S(2)}) async-start(bf16[32,4,4,256]{3,2,1,0:T(4,128)(2,1)} %bitcast.801), calls=%async_computation.24 | async-start | bytes 524288 | tf_op jit(solution)/shard_map/all_to_all | solution.py:14
  247.9 13.9 %all-to-all-start.7 = ((bf16[32,4,4,256]{3,2,1,0:T(4,128)(2,1)}), bf16[32,4,4,256]{3,2,1,0:T(4,128)(2,1)}, u32[]{:S(2)}, u32[]{:S(2)}) async-start(bf16[32,4,4,256]{3,2,1,0:T(4,128)(2,1)} %bitcast.38), calls=%async_computation.7 | async-start | bytes 524288 | tf_op jit(solution)/shard_map/all_to_all | solution.py:14
  288.7 13.9 %all-to-all-start.26 = ((bf16[32,4,4,256]{3,2,1,0:T(4,128)(2,1)}), bf16[32,4,4,256]{3,2,1,0:T(4,128)(2,1)}, u32[]{:S(2)}, u32[]{:S(2)}) async-start(bf16[32,4,4,256]{3,2,1,0:T(4,128)(2,1)} %bitcast.119), calls=%async_computation.26 | async-start | bytes 524288 | tf_op jit(solution)/shard_map/all_to_all | solution.py:14
  315.9 15.4 %all-to-all-start.27 = ((bf16[32,4,4,256]{3,1,2,0:T(4,128)(2,1)}), bf16[32,4,4,256]{3,1,2,0:T(4,128)(2,1)}, u32[]{:S(2)}, u32[]{:S(2)}) async-start(bf16[32,4,4,256]{3,1,2,0:T(4,128)(2,1)} %copy.508), calls=%async_computation.27 | async-start | bytes 524288 | tf_op jit(solution)/shard_map/all_to_all | solution.py:14
  331.3 14.4 %all-to-all-start.11 = ((bf16[32,4,4,256]{3,1,2,0:T(4,128)(2,1)}), bf16[32,4,4,256]{3,1,2,0:T(4,128)(2,1)}, u32[]{:S(2)}, u32[]{:S(2)}) async-start(bf16[32,4,4,256]{3,1,2,0:T(4,128)(2,1)} %copy.454), calls=%async_computation.11 | async-start | bytes 524288 | tf_op jit(solution)/shard_map/all_to_all | solution.py:14
  345.8 13.9 %all-to-all-start.28 = ((bf16[32,4,4,256]{3,2,1,0:T(4,128)(2,1)}), bf16[32,4,4,256]{3,2,1,0:T(4,128)(2,1)}, u32[]{:S(2)}, u32[]{:S(2)}) async-start(bf16[32,4,4,256]{3,2,1,0:T(4,128)(2,1)} %bitcast.803), calls=%async_computation.28 | async-start | bytes 524288 | tf_op jit(solution)/shard_map/all_to_all | solution.py:14
  359.7 13.9 %all-to-all-start.12 = ((bf16[32,4,4,256]{3,2,1,0:T(4,128)(2,1)}), bf16[32,4,4,256]{3,2,1,0:T(4,128)(2,1)}, u32[]{:S(2)}, u32[]{:S(2)}) async-start(bf16[32,4,4,256]{3,2,1,0:T(4,128)(2,1)} %bitcast.61), calls=%async_computation.12 | async-start | bytes 524288 | tf_op jit(solution)/shard_map/all_to_all | solution.py:14
  373.6 16.9 %all-to-all-start.29 = ((bf16[32,4,4,256]{3,1,2,0:T(4,128)(2,1)}), bf16[32,4,4,256]{3,1,2,0:T(4,128)(2,1)}, u32[]{:S(2)}, u32[]{:S(2)}) async-start(bf16[32,4,4,256]{3,1,2,0:T(4,128)(2,1)} %copy.514), calls=%async_computation.29 | async-start | bytes 524288 | tf_op jit(solution)/shard_map/all_to_all | solution.py:14
  390.5 16.9 %all-to-all-start.13 = ((bf16[32,4,4,256]{3,1,2,0:T(4,128)(2,1)}), bf16[32,4,4,256]{3,1,2,0:T(4,128)(2,1)}, u32[]{:S(2)}, u32[]{:S(2)}) async-start(bf16[32,4,4,256]{3,1,2,0:T(4,128)(2,1)} %copy.462), calls=%async_computation.13 | async-start | bytes 524288 | tf_op jit(solution)/shard_map/all_to_all | solution.py:14
  407.4 13.9 %all-to-all-start.30 = ((bf16[32,4,4,256]{3,2,1,0:T(4,128)(2,1)}), bf16[32,4,4,256]{3,2,1,0:T(4,128)(2,1)}, u32[]{:S(2)}, u32[]{:S(2)}) async-start(bf16[32,4,4,256]{3,2,1,0:T(4,128)(2,1)} %bitcast.804), calls=%async_computation.30 | async-start | bytes 524288 | tf_op jit(solution)/shard_map/all_to_all | solution.py:14
  421.3 14.4 %all-to-all-start.14 = ((bf16[32,4,4,256]{3,2,1,0:T(4,128)(2,1)}), bf16[32,4,4,256]{3,2,1,0:T(4,128)(2,1)}, u32[]{:S(2)}, u32[]{:S(2)}) async-start(bf16[32,4,4,256]{3,2,1,0:T(4,128)(2,1)} %bitcast.800), calls=%async_computation.14 | async-start | bytes 524288 | tf_op jit(solution)/shard_map/all_to_all | solution.py:14
  435.7 17.0 %all-to-all-start.31 = ((bf16[32,4,4,256]{3,1,2,0:T(4,128)(2,1)}), bf16[32,4,4,256]{3,1,2,0:T(4,128)(2,1)}, u32[]{:S(2)}, u32[]{:S(2)}) async-start(bf16[32,4,4,256]{3,1,2,0:T(4,128)(2,1)} %copy.520), calls=%async_computation.31 | async-start | bytes 524288 | tf_op jit(solution)/shard_map/all_to_all | solution.py:14
  452.8 16.5 %all-to-all-start.15 = ((bf16[32,4,4,256]{3,1,2,0:T(4,128)(2,1)}), bf16[32,4,4,256]{3,1,2,0:T(4,128)(2,1)}, u32[]{:S(2)}, u32[]{:S(2)}) async-start(bf16[32,4,4,256]{3,1,2,0:T(4,128)(2,1)} %copy.470), calls=%async_computation.15 | async-start | bytes 524288 | tf_op jit(solution)/shard_map/all_to_all | solution.py:14
  469.3 13.9 %all-to-all-start.32 = ((bf16[32,4,4,256]{3,2,1,0:T(4,128)(2,1)}), bf16[32,4,4,256]{3,2,1,0:T(4,128)(2,1)}, u32[]{:S(2)}, u32[]{:S(2)}) async-start(bf16[32,4,4,256]{3,2,1,0:T(4,128)(2,1)} %bitcast.802), calls=%async_computation.32 | async-start | bytes 524288 | tf_op jit(solution)/shard_map/all_to_all | solution.py:14
  483.2 13.9 %all-to-all-start.16 = ((bf16[32,4,4,256]{3,2,1,0:T(4,128)(2,1)}), bf16[32,4,4,256]{3,2,1,0:T(4,128)(2,1)}, u32[]{:S(2)}, u32[]{:S(2)}) async-start(bf16[32,4,4,256]{3,2,1,0:T(4,128)(2,1)} %bitcast.81), calls=%async_computation.16 | async-start | bytes 524288 | tf_op jit(solution)/shard_map/all_to_all | solution.py:14
  497.2 13.9 %all-to-all-start.33 = ((bf16[32,4,4,256]{3,1,2,0:T(4,128)(2,1)}), bf16[32,4,4,256]{3,1,2,0:T(4,128)(2,1)}, u32[]{:S(2)}, u32[]{:S(2)}) async-start(bf16[32,4,4,256]{3,1,2,0:T(4,128)(2,1)} %copy.526), calls=%async_computation.33 | async-start | bytes 524288 | tf_op jit(solution)/shard_map/all_to_all | solution.py:14
  511.1 16.3 %all-to-all-start.17 = ((bf16[32,4,4,256]{3,1,2,0:T(4,128)(2,1)}), bf16[32,4,4,256]{3,1,2,0:T(4,128)(2,1)}, u32[]{:S(2)}, u32[]{:S(2)}) async-start(bf16[32,4,4,256]{3,1,2,0:T(4,128)(2,1)} %copy.478), calls=%async_computation.17 | async-start | bytes 524288 | tf_op jit(solution)/shard_map/all_to_all | solution.py:14
  527.4 13.9 %all-to-all-start.44 = ((bf16[32,4,4,256]{3,1,2,0:T(4,128)(2,1)}), bf16[32,4,4,256]{3,1,2,0:T(4,128)(2,1)}, u32[]{:S(2)}, u32[]{:S(2)}) async-start(bf16[32,4,4,256]{3,1,2,0:T(4,128)(2,1)} %copy.549), calls=%async_computation.44 | async-start | bytes 524288 | tf_op jit(solution)/shard_map/all_to_all | solution.py:14
  541.3 13.9 %all-to-all-start.38 = ((bf16[32,4,4,256]{3,1,2,0:T(4,128)(2,1)}), bf16[32,4,4,256]{3,1,2,0:T(4,128)(2,1)}, u32[]{:S(2)}, u32[]{:S(2)}) async-start(bf16[32,4,4,256]{3,1,2,0:T(4,128)(2,1)} %copy.537), calls=%async_computation.38 | async-start | bytes 524288 | tf_op jit(solution)/shard_map/all_to_all | solution.py:14
  555.3 13.9 %all-to-all-start.45 = ((bf16[32,4,4,256]{3,1,2,0:T(4,128)(2,1)}), bf16[32,4,4,256]{3,1,2,0:T(4,128)(2,1)}, u32[]{:S(2)}, u32[]{:S(2)}) async-start(bf16[32,4,4,256]{3,1,2,0:T(4,128)(2,1)} %copy.551), calls=%async_computation.45 | async-start | bytes 524288 | tf_op jit(solution)/shard_map/all_to_all | solution.py:14
  596.4 13.9 %all-to-all-start.40 = ((bf16[32,4,4,256]{3,1,2,0:T(4,128)(2,1)}), bf16[32,4,4,256]{3,1,2,0:T(4,128)(2,1)}, u32[]{:S(2)}, u32[]{:S(2)}) async-start(bf16[32,4,4,256]{3,1,2,0:T(4,128)(2,1)} %copy.541), calls=%async_computation.40 | async-start | bytes 524288 | tf_op jit(solution)/shard_map/all_to_all | solution.py:14
  610.3 14.1 %all-to-all-start.47 = ((bf16[32,4,4,256]{3,1,2,0:T(4,128)(2,1)}), bf16[32,4,4,256]{3,1,2,0:T(4,128)(2,1)}, u32[]{:S(2)}, u32[]{:S(2)}) async-start(bf16[32,4,4,256]{3,1,2,0:T(4,128)(2,1)} %copy.555), calls=%async_computation.47 | async-start | bytes 524288 | tf_op jit(solution)/shard_map/all_to_all | solution.py:14
  624.4 13.9 %all-to-all-start.41 = ((bf16[32,4,4,256]{3,1,2,0:T(4,128)(2,1)}), bf16[32,4,4,256]{3,1,2,0:T(4,128)(2,1)}, u32[]{:S(2)}, u32[]{:S(2)}) async-start(bf16[32,4,4,256]{3,1,2,0:T(4,128)(2,1)} %copy.543), calls=%async_computation.41 | async-start | bytes 524288 | tf_op jit(solution)/shard_map/all_to_all | solution.py:14
  638.4 14.6 %all-to-all-start.48 = ((bf16[32,4,4,256]{3,1,2,0:T(4,128)(2,1)}), bf16[32,4,4,256]{3,1,2,0:T(4,128)(2,1)S(1)}, u32[]{:S(2)}, u32[]{:S(2)}) async-start(bf16[32,4,4,256]{3,1,2,0:T(4,128)(2,1)} %copy.557), calls=%async_computation.48 | async-start | bytes 524288 | tf_op jit(solution)/shard_map/all_to_all | solution.py:14
  652.9 15.4 %all-to-all-start.42 = ((bf16[32,4,4,256]{3,1,2,0:T(4,128)(2,1)}), bf16[32,4,4,256]{3,1,2,0:T(4,128)(2,1)}, u32[]{:S(2)}, u32[]{:S(2)}) async-start(bf16[32,4,4,256]{3,1,2,0:T(4,128)(2,1)} %copy.545), calls=%async_computation.42 | async-start | bytes 524288 | tf_op jit(solution)/shard_map/all_to_all | solution.py:14
  672.1 13.9 %all-to-all-start.51 = ((bf16[32,4,4,256]{3,1,2,0:T(4,128)(2,1)}), bf16[32,4,4,256]{3,1,2,0:T(4,128)(2,1)}, u32[]{:S(2)}, u32[]{:S(2)}) async-start(bf16[32,4,4,256]{3,1,2,0:T(4,128)(2,1)} %copy.565), calls=%async_computation.51 | async-start | bytes 524288 | tf_op jit(solution)/shard_map/all_to_all | solution.py:14
  686.0 13.9 %all-to-all-start.49 = ((bf16[32,4,4,256]{3,1,2,0:T(4,128)(2,1)}), bf16[32,4,4,256]{3,1,2,0:T(4,128)(2,1)}, u32[]{:S(2)}, u32[]{:S(2)}) async-start(bf16[32,4,4,256]{3,1,2,0:T(4,128)(2,1)} %copy.561), calls=%async_computation.49 | async-start | bytes 524288 | tf_op jit(solution)/shard_map/all_to_all | solution.py:14
  700.0 13.9 %all-to-all-start.52 = ((bf16[32,4,4,256]{3,1,2,0:T(4,128)(2,1)}), bf16[32,4,4,256]{3,1,2,0:T(4,128)(2,1)}, u32[]{:S(2)}, u32[]{:S(2)}) async-start(bf16[32,4,4,256]{3,1,2,0:T(4,128)(2,1)} %copy.567), calls=%async_computation.52 | async-start | bytes 524288 | tf_op jit(solution)/shard_map/all_to_all | solution.py:14
  727.7 13.9 %all-to-all-start.18 = ((bf16[32,4,4,256]{3,2,1,0:T(4,128)(2,1)}), bf16[32,4,4,256]{3,2,1,0:T(4,128)(2,1)}, u32[]{:S(2)}, u32[]{:S(2)}) async-start(bf16[32,4,4,256]{3,2,1,0:T(4,128)(2,1)} %bitcast.796), calls=%async_computation.18 | async-start | bytes 524288 | tf_op jit(solution)/shard_map/all_to_all | solution.py:14
  754.9 13.9 %all-to-all-start.55 = ((bf16[32,4,4,256]{3,1,2,0:T(4,128)(2,1)}), bf16[32,4,4,256]{3,1,2,0:T(4,128)(2,1)}, u32[]{:S(2)}, u32[]{:S(2)}) async-start(bf16[32,4,4,256]{3,1,2,0:T(4,128)(2,1)} %copy.575), calls=%async_computation.55 | async-start | bytes 524288 | tf_op jit(solution)/shard_map/all_to_all | solution.py:14
  795.3 13.9 %all-to-all-start.34 = ((bf16[32,4,4,256]{3,2,1,0:T(4,128)(2,1)}), bf16[32,4,4,256]{3,2,1,0:T(4,128)(2,1)}, u32[]{:S(2)}, u32[]{:S(2)}) async-start(bf16[32,4,4,256]{3,2,1,0:T(4,128)(2,1)} %bitcast.797), calls=%async_computation.34 | async-start | bytes 524288 | tf_op jit(solution)/shard_map/all_to_all | solution.py:14
  809.3 14.1 %all-to-all-start.59 = ((bf16[32,4,4,256]{3,1,2,0:T(4,128)(2,1)}), bf16[32,4,4,256]{3,1,2,0:T(4,128)(2,1)}, u32[]{:S(2)}, u32[]{:S(2)}) async-start(bf16[32,4,4,256]{3,1,2,0:T(4,128)(2,1)} %copy.585), calls=%async_computation.59 | async-start | bytes 524288 | tf_op jit(solution)/shard_map/all_to_all | solution.py:14
  836.7 13.9 %all-to-all-start.60 = ((bf16[32,4,4,256]{3,1,2,0:T(4,128)(2,1)}), bf16[32,4,4,256]{3,1,2,0:T(4,128)(2,1)S(1)}, u32[]{:S(2)}, u32[]{:S(2)}) async-start(bf16[32,4,4,256]{3,1,2,0:T(4,128)(2,1)} %copy.587), calls=%async_computation.60 | async-start | bytes 524288 | tf_op jit(solution)/shard_map/all_to_all | solution.py:14
  864.9 13.9 %all-to-all-start.63 = ((bf16[32,4,4,256]{3,1,2,0:T(4,128)(2,1)}), bf16[32,4,4,256]{3,1,2,0:T(4,128)(2,1)}, u32[]{:S(2)}, u32[]{:S(2)}) async-start(bf16[32,4,4,256]{3,1,2,0:T(4,128)(2,1)} %copy.595), calls=%async_computation.63 | async-start | bytes 524288 | tf_op jit(solution)/shard_map/all_to_all | solution.py:14
  931.8 13.9 %all-to-all-start.67 = ((bf16[32,4,4,256]{3,1,2,0:T(4,128)(2,1)}), bf16[32,4,4,256]{3,1,2,0:T(4,128)(2,1)}, u32[]{:S(2)}, u32[]{:S(2)}) async-start(bf16[32,4,4,256]{3,1,2,0:T(4,128)(2,1)} %copy.605), calls=%async_computation.67 | async-start | bytes 524288 | tf_op jit(solution)/shard_map/all_to_all | solution.py:14
  986.2 18.2 %all-to-all-start.71 = ((bf16[4,2,4,128,128]{4,3,2,1,0:T(8,128)(2,1)}), bf16[4,2,4,128,128]{4,3,2,1,0:T(8,128)(2,1)S(1)}, u32[]{:S(2)}, u32[]{:S(2)}) async-start(bf16[4,2,4,128,128]{4,3,2,1,0:T(8,128)(2,1)} %pad_maximum_fusion.1), calls=%async_computation.71 | async-start | bytes 2097152 | tf_op jit(solution)/shard_map/all_to_all | solution.py:14
  1016.7 18.0 %all-to-all-start.70 = ((bf16[4,2,4,128,128]{4,3,2,1,0:T(8,128)(2,1)}), bf16[4,2,4,128,128]{4,3,2,1,0:T(8,128)(2,1)S(1)}, u32[]{:S(2)}, u32[]{:S(2)}) async-start(bf16[4,2,4,128,128]{4,3,2,1,0:T(8,128)(2,1)} %pad_maximum_fusion), calls=%async_computation.70 | async-start | bytes 2097152 | tf_op jit(solution)/shard_map/all_to_all | solution.py:14
  (120 other events, 1430.7 us)

commit v6 on v3

v6 whole, which is shorter than its diff:
```python
import jax
import jax.numpy as jnp
from jax import lax
from jax.sharding import Mesh, PartitionSpec as P

F32 = jnp.float32
BF16 = jnp.bfloat16
WIDE = ("s", "x")
GROUPS = 2
STRETCH = 2


def silu_slope(values):
    sigmoid = jax.nn.sigmoid(values)
    return sigmoid * (1.0 + values * (1.0 - sigmoid))


def group_order(size, sections, groups, peers):
    natural = jnp.arange(size).reshape(groups, peers, sections, -1)
    order = natural.transpose(2, 1, 0, 3).reshape(size)
    return (order[:, None] == jnp.arange(size)[None, :]).astype(BF16)


def exchange(values):
    own, full, rows = values.shape
    pieces = values.transpose(1, 0, 2).reshape(full // own, own, own, rows)
    moved = lax.all_to_all(pieces, WIDE, split_axis=0, concat_axis=0, tiled=True)
    return moved.transpose(1, 0, 2, 3).reshape(own, full, rows)


def forward_layer(acts, factors):
    mixed = jnp.einsum("bjk,bjr->bkr", factors[0], acts, preferred_element_type=F32).astype(BF16)
    columns = exchange(mixed)
    activated = jax.nn.silu(columns.astype(F32)).astype(BF16)
    second = jnp.einsum("kbc,kbr->kcr", factors[1], activated, preferred_element_type=F32).astype(BF16)
    following = (acts.astype(F32) + exchange(second).astype(F32)).astype(BF16)
    return following, (acts, columns)


def backward_layer(grad, saved):
    factors, (acts, columns) = saved
    grad_columns = exchange(grad)
    wide = columns.astype(F32)
    activated = jax.nn.silu(wide).astype(BF16)
    left_term = jnp.einsum("kbr,kcr->kbc", activated, grad_columns, preferred_element_type=F32)
    grad_act = jnp.einsum("kbc,kcr->kbr", factors[1], grad_columns, preferred_element_type=F32)
    grad_mixed = exchange((grad_act * silu_slope(wide)).astype(BF16))
    right_term = jnp.einsum("bjr,bkr->bjk", acts, grad_mixed, preferred_element_type=F32)
    branch = jnp.einsum("bjk,bkr->bjr", factors[0], grad_mixed, preferred_element_type=F32)
    following = (grad.astype(F32) + branch).astype(BF16)
    return following, jnp.stack([right_term.astype(BF16), left_term.astype(BF16)])


def body(inputs, cotangent, right_factor, left_factor):
    sections = lax.axis_size("s")
    groups = lax.axis_size("t")
    peers = lax.axis_size("x")
    loops, _, held, size, _ = right_factor.shape
    rows = inputs.shape[2]
    sub = held // sections
    own = sub * groups
    layers = loops * sections
    micros = sections // groups
    s_index = lax.axis_index("s")
    t_index = lax.axis_index("t")
    line = (s_index % micros) * groups + t_index
    order = group_order(size, sections, groups, peers)

    def pick(parts, index):
        return lax.dynamic_index_in_dim(parts, index, 0, keepdims=False)

    def turned(parts, send_by, place_by, target):
        moved = []
        for mask in range(sections):
            pairs = [(s * groups + t, target(s, t, mask)) for s in range(sections) for t in range(groups)]
            moved.append(lax.ppermute(pick(parts, send_by ^ mask), ("s", "t"), pairs))
        moved = jnp.stack(moved)
        return jnp.stack([pick(moved, place_by ^ part) for part in range(sections)])

    def into(s, t, mask):
        return (((s % micros) * groups + t) ^ mask) * groups + s // micros

    def outof(s, t, mask):
        line_to = s ^ mask
        return (t * micros + line_to // groups) * groups + line_to % groups

    def enter(acts):
        parts = turned(acts.reshape(sections, sub, size, rows), line, s_index, into)
        parts = parts.reshape(micros, own, size, rows).transpose(1, 2, 0, 3)
        parts = parts.reshape(own, size, micros * rows)
        return jnp.einsum("aj,bjr->bar", order, parts, preferred_element_type=F32).astype(BF16)

    def leave(acts):
        acts = jnp.einsum("aj,bar->bjr", order, acts, preferred_element_type=F32).astype(BF16)
        parts = acts.reshape(own, size, micros, rows).transpose(2, 0, 1, 3)
        parts = turned(parts.reshape(sections, sub, size, rows), s_index, line, outof)
        return parts.reshape(1, held * size, rows)

    def scattered(parts):
        moved = [pick(parts, s_index)]
        for mask in range(1, sections):
            pairs = [(s, s ^ mask) for s in range(sections)]
            moved.append(lax.ppermute(pick(parts, s_index ^ mask), "s", pairs))
        moved = jnp.stack(moved)
        return jnp.stack([pick(moved, s_index ^ section) for section in range(sections)])

    def gathered(part):
        moved = [part]
        step = 1
        while step < groups:
            pairs = [(t, t ^ step) for t in range(groups)]
            other = [lax.ppermute(one, "t", pairs) for one in moved]
            low = (t_index // step) % 2 == 0
            moved = [jnp.where(low, x, y) for x, y in zip(moved, other)] + [
                jnp.where(low, y, x) for x, y in zip(moved, other)
            ]
            step *= 2
        return jnp.concatenate(moved, axis=2)

    def summed(terms):
        parts = terms.reshape(terms.shape[:2] + (groups, sub, size, size)).transpose(2, 0, 1, 3, 4, 5)
        step = 1
        while step < groups:
            pairs = [(t, t ^ step) for t in range(groups)]
            parts = parts.reshape((parts.shape[0] // 2, 2) + parts.shape[1:])
            bit = (t_index // step) % 2
            keep = lax.dynamic_index_in_dim(parts, bit, 1, keepdims=False)
            give = lax.dynamic_index_in_dim(parts, 1 - bit, 1, keepdims=False)
            parts = (keep.astype(F32) + lax.ppermute(give, "t", pairs).astype(F32)).astype(BF16)
            step *= 2
        return parts[0]

    def ordered(factors):
        return jnp.einsum("aj,lfbjk,ck->lfbac", order, factors, order, preferred_element_type=F32).astype(BF16)

    def unordered(terms):
        return jnp.einsum("aj,lfbac,ck->lfbjk", order, terms, order, preferred_element_type=F32).astype(BF16)

    both = jnp.stack([right_factor[:, 0], left_factor[:, 0]], axis=1)
    both = both.reshape(loops, 2, sections, sub, size, size).transpose(0, 2, 1, 3, 4, 5)
    stretches = layers // STRETCH
    arrived = [scattered(both[0])]

    def fetch(stretch):
        loop, start = divmod(stretch * STRETCH, sections)
        return gathered(arrived[loop][start : start + STRETCH])

    current = enter(inputs)
    stored = []
    weights = [ordered(fetch(0))]
    later, weights[0], cotangent = lax.optimization_barrier((both[1:], weights[0], cotangent))
    arrived.extend(scattered(later[loop]) for loop in range(loops - 1))
    for stretch in range(stretches):
        coming = fetch(stretch + 1) if stretch + 1 < stretches else None
        if stretch + 1 == stretches:
            current, cotangent = lax.optimization_barrier((current, cotangent))
            grad = enter(cotangent)
        current, saved = lax.scan(forward_layer, current, weights[stretch])
        stored.append(saved)
        if coming is not None:
            current, coming = lax.optimization_barrier((current, coming))
            weights.append(ordered(coming))
    outputs = leave(current)

    per_loop = stretches // loops

    def returned(loop):
        mine = jnp.concatenate(sums[loop * per_loop : (loop + 1) * per_loop])
        return scattered(mine).transpose(1, 0, 2, 3, 4).reshape(2, 1, held, size, size)

    sums = [None] * stretches
    halves = [None] * loops
    beside = {"outputs": outputs}
    for stretch in reversed(range(stretches)):
        grad, terms = lax.scan(backward_layer, grad, (weights[stretch], stored[stretch]), reverse=True)
        grad, terms, beside = lax.optimization_barrier((grad, terms, beside))
        outputs = beside.get("outputs", outputs)
        ready = beside.get("half")
        if "sum" in beside:
            sums[stretch + 1] = beside["sum"]
        beside = {"sum": summed(unordered(terms))}
        loop = (stretch + 1) // per_loop
        if (stretch + 1) % per_loop == 0 and loop < loops:
            beside["half"] = returned(loop)
            owed = loop
        if ready is not None:
            halves[owed] = ready
    sums[0] = beside["sum"]
    halves[0] = returned(0)
    input_grad = leave(grad)
    grads = jnp.stack(halves).astype(F32)
    return (outputs, input_grad, grads[:, 0], grads[:, 1])


def solution(mesh):
    sections = mesh.shape["section"]
    peers = mesh.shape["block"] // GROUPS
    grouped = Mesh(mesh.devices.reshape(sections, GROUPS, peers), ("s", "t", "x"))
    acts = P("s", ("t", "x"), None)
    factor = P(None, "s", ("t", "x"), None, None)
    return jax.shard_map(
        body,
        mesh=grouped,
        in_specs=(acts, acts, factor, factor),
        out_specs=(acts, acts, factor, factor),
        check_vma=False,
    )
```

time: 781 us -> 873 us (1.12)
  waiting for transfers between devices: 126 us -> 490 us
  blocking collectives: 321 us -> 0 us
  starting transfers between devices: 123 us -> 180 us
  between operations: 16.1 us -> 1.79 us
  other arithmetic: 41.5 us -> 27.5 us
  matrix products: 65 us -> 74.3 us
  local copies, waits for them, and re-layouts: 76.2 us -> 85.2 us
    all_to_all x16 -> x32, waiting for transfers between devices: 57.4 us -> 295 us  [exchange(): lax.all_to_all(pieces, WIDE, split_axis=0, concat_axis=0, tiled=True)]
    all_to_all x16 -> x0, blocking collectives: 216 us -> none  [exchange(): lax.all_to_all(pieces, WIDE, split_axis=0, concat_axis=0, tiled=True)]
    ppermute x22 -> x36, waiting for transfers between devices: 57.8 us -> 195 us  [the longest x4 88.4 us: summed(): lax.ppermute(give, 't', pairs).astype(F32)]
    all_gather x8 -> x0, blocking collectives: 104 us -> none  [body(): full = lax.all_gather(part, 't', axis=0, tiled=False)]
    all_to_all x16 -> x32, starting transfers between devices: 67.4 us -> 116 us  [exchange(): lax.all_to_all(pieces, WIDE, split_axis=0, concat_axis=0, tiled=True)]
    ppermute x22 -> x36, starting transfers between devices: 44.5 us -> 64.5 us  [the longest x16 49 us: turned(): moved.append(lax.ppermute(pick(parts, send_by ^ mask), ('s', 't'), pairs))]
    dot_general x50 -> x56, matrix products: 57.6 us -> 72.9 us  [the longest x8 12.7 us: forward_layer(): jnp.einsum('kbc,kbr->kcr', factors[1], activated, preferred_element_type=...]
    unnamed x148 -> x25, local copies, waits for them, and re-layouts: 17.4 us -> 2.22 us
  transfers between devices with their start and end apart: 48 -> 68, of which waited for: 24 -> 48; matrix products, arithmetic and copies ran while one was open for 16% -> 8% of each run, Pallas kernels for 0% -> 0%
where the time goes in v6:
time: 873 us; the launch traced here: 861 us
  waiting for transfers between devices  490 us (56%)
  starting transfers between devices  180 us (21%)
  local copies, waits for them, and re-layouts  85.2 us (10%)
  matrix products  74.3 us (9%)
  other arithmetic  27.5 us (3%)
    all_to_all x32, waiting for transfers between devices, exchange(): lax.all_to_all(pieces, WIDE, split_axis=0, concat_axis=0, tiled=True)  295 us
    all_to_all x32, starting transfers between devices, exchange(): lax.all_to_all(pieces, WIDE, split_axis=0, concat_axis=0, tiled=True)  116 us
    ppermute x4, waiting for transfers between devices, summed(): lax.ppermute(give, 't', pairs).astype(F32)  88.4 us
    ppermute x16, waiting for transfers between devices, turned(): moved.append(lax.ppermute(pick(parts, send_by ^ mask), ('s', 't'), pairs))  63.1 us
    ppermute x16, starting transfers between devices, turned(): moved.append(lax.ppermute(pick(parts, send_by ^ mask), ('s', 't'), pairs))  49 us
    ppermute x12, waiting for transfers between devices, scattered(): moved.append(lax.ppermute(pick(parts, s_index ^ mask), 's', pairs))  43.3 us
    reshape x24, local copies, waits for them, and re-layouts, exchange(): pieces = values.transpose(1, 0, 2).reshape(full // own, own, own, rows)  20.3 us
  transfers between devices with their start and end apart: 68, of which 48 were waited for; matrix products, arithmetic and copies ran while one was open for 8% of the time, Pallas kernels for 0%

profile of v6, /device:TPU:0, one launch (start us, length us, event | category | flops | bytes accessed | tf_op | source)
XLA Modules:
  0.0 860.6 jit_solution(622623379590905721)
XLA Ops:
  19.5 6.5 collective-permute-done.6
  37.0 50.9 %collective-permute-done.1 = bf16[4,128,128]{2,1,0:T(8,128)(2,1)S(1)} collective-permute-done((bf16[4,128,128]{2,1,0:T(8,128)(2,1)}, bf16[4,128,128]{2,1,0:T(8,128)(2,1)S(1)}, u32[]{:S(2)}, u32[]{:S(2)}) %collective-permute-start.1) | collective-permute-done | bytes 131104 | tf_op jit(solution)/shard_map/ppermute | solution.py:76
  116.0 74.2 %while.120 = (s32[]{:T(128)}, bf16[8,128,256]{2,1,0:T(8,128)(2,1)S(1)}, bf16[2,8,128,256]{3,2,1,0:T(8,128)(2,1)S(1)}, bf16[2,8,128,256]{3,1,2,0:T(8,128)(2,1)}, ...) while((s32[]{:T(128)}, bf16[8,128,256]{2,1,0:T(8,128)(2,1)S(1)}, ...), condition=%wide.region_1.2_spmd, body=%wide.region_0.1_spmd.sunk | while | flops 137363456 | bytes 15728829 | solution.py:158
  123.2 20.4 %all-to-all-done = bf16[16,8,8,256]{3,1,2,0:T(8,128)(2,1)S(1)} async-done(((bf16[16,8,8,256]{3,1,2,0:T(8,128)(2,1)}), bf16[16,8,8,256]{3,1,2,0:T(8,128)(2,1)S(1)}, u32[]{:S(2)}, u32[]{:S(2)}) %all-to-all-start) | async-done | bytes 524320 | tf_op jit(solution)/shard_map/while/body/eval_jaxpr/all_to_all | solution.py:27
  150.7 8.3 all-to-all-done.1
  165.2 9.2 %all-to-all-done = bf16[16,8,8,256]{3,1,2,0:T(8,128)(2,1)S(1)} async-done(((bf16[16,8,8,256]{3,1,2,0:T(8,128)(2,1)}), bf16[16,8,8,256]{3,1,2,0:T(8,128)(2,1)S(1)}, u32[]{:S(2)}, u32[]{:S(2)}) %all-to-all-start) | async-done | bytes 524320 | tf_op jit(solution)/shard_map/while/body/eval_jaxpr/all_to_all | solution.py:27
  181.4 8.3 all-to-all-done.1
  199.4 72.4 %while.121 = (s32[]{:T(128)}, bf16[8,128,256]{2,1,0:T(8,128)(2,1)S(1)}, bf16[2,8,128,256]{3,2,1,0:T(8,128)(2,1)S(1)}, bf16[2,8,128,256]{3,1,2,0:T(8,128)(2,1)}, ...) while((s32[]{:T(128)}, bf16[8,128,256]{2,1,0:T(8,128)(2,1)S(1)}, ...), condition=%wide.region_3.4_spmd, body=%wide.region_2.3_spmd.sunk | while | flops 137363456 | bytes 15728829 | solution.py:158
  205.1 20.0 %all-to-all-done.2 = bf16[16,8,8,256]{3,1,2,0:T(8,128)(2,1)S(1)} async-done(((bf16[16,8,8,256]{3,1,2,0:T(8,128)(2,1)}), bf16[16,8,8,256]{3,1,2,0:T(8,128)(2,1)S(1)}, u32[]{:S(2)}, u32[]{:S(2)}) %all-to-all-start.2) | async-done | bytes 524320 | tf_op jit(solution)/shard_map/while/body/eval_jaxpr/all_to_all | solution.py:27
  232.2 8.3 all-to-all-done.3
  246.7 9.2 %all-to-all-done.2 = bf16[16,8,8,256]{3,1,2,0:T(8,128)(2,1)S(1)} async-done(((bf16[16,8,8,256]{3,1,2,0:T(8,128)(2,1)}), bf16[16,8,8,256]{3,1,2,0:T(8,128)(2,1)S(1)}, u32[]{:S(2)}, u32[]{:S(2)}) %all-to-all-start.2) | async-done | bytes 524320 | tf_op jit(solution)/shard_map/while/body/eval_jaxpr/all_to_all | solution.py:27
  263.0 8.3 all-to-all-done.3
  278.5 61.5 %while.122 = (s32[]{:T(128)}, bf16[8,128,256]{2,1,0:T(8,128)(2,1)S(1)}, bf16[2,8,128,256]{3,2,1,0:T(8,128)(2,1)S(1)}, bf16[2,8,128,256]{3,1,2,0:T(8,128)(2,1)}, ...) while((s32[]{:T(128)}, bf16[8,128,256]{2,1,0:T(8,128)(2,1)S(1)}, ...), condition=%wide.region_5.6_spmd, body=%wide.region_4.5_spmd.sunk | while | flops 137363456 | bytes 15728829 | solution.py:158
  284.2 9.2 %all-to-all-done.4 = bf16[16,8,8,256]{3,1,2,0:T(8,128)(2,1)S(1)} async-done(((bf16[16,8,8,256]{3,1,2,0:T(8,128)(2,1)}), bf16[16,8,8,256]{3,1,2,0:T(8,128)(2,1)S(1)}, u32[]{:S(2)}, u32[]{:S(2)}) %all-to-all-start.4) | async-done | bytes 524320 | tf_op jit(solution)/shard_map/while/body/eval_jaxpr/all_to_all | solution.py:27
  300.5 8.3 all-to-all-done.5
  315.0 9.2 %all-to-all-done.4 = bf16[16,8,8,256]{3,1,2,0:T(8,128)(2,1)S(1)} async-done(((bf16[16,8,8,256]{3,1,2,0:T(8,128)(2,1)}), bf16[16,8,8,256]{3,1,2,0:T(8,128)(2,1)S(1)}, u32[]{:S(2)}, u32[]{:S(2)}) %all-to-all-start.4) | async-done | bytes 524320 | tf_op jit(solution)/shard_map/while/body/eval_jaxpr/all_to_all | solution.py:27
  331.2 8.3 all-to-all-done.5
  345.2 61.5 %while.123 = (s32[]{:T(128)}, bf16[8,128,256]{2,1,0:T(8,128)(2,1)S(1)}, bf16[2,8,128,256]{3,2,1,0:T(8,128)(2,1)}, bf16[2,8,128,256]{3,1,2,0:T(8,128)(2,1)}, bf16...) while((s32[]{:T(128)}, bf16[8,128,256]{2,1,0:T(8,128)(2,1)S(1)}, ...), condition=%wide.region_7.8_spmd, body=%wide.region_6.7_spmd.sunk | while | flops 137363456 | bytes 15728829 | solution.py:158
  350.9 9.2 %all-to-all-done.6 = bf16[16,8,8,256]{3,1,2,0:T(8,128)(2,1)S(1)} async-done(((bf16[16,8,8,256]{3,1,2,0:T(8,128)(2,1)}), bf16[16,8,8,256]{3,1,2,0:T(8,128)(2,1)S(1)}, u32[]{:S(2)}, u32[]{:S(2)}) %all-to-all-start.6) | async-done | bytes 524320 | tf_op jit(solution)/shard_map/while/body/eval_jaxpr/all_to_all | solution.py:27
  367.9 7.5 all-to-all-done.7
  381.7 9.2 %all-to-all-done.6 = bf16[16,8,8,256]{3,1,2,0:T(8,128)(2,1)S(1)} async-done(((bf16[16,8,8,256]{3,1,2,0:T(8,128)(2,1)}), bf16[16,8,8,256]{3,1,2,0:T(8,128)(2,1)S(1)}, u32[]{:S(2)}, u32[]{:S(2)}) %all-to-all-start.6) | async-done | bytes 524320 | tf_op jit(solution)/shard_map/while/body/eval_jaxpr/all_to_all | solution.py:27
  398.8 7.4 all-to-all-done.7
  419.7 14.8 %collective-permute-start.16 = (bf16[4,128,128]{2,1,0:T(8,128)(2,1)S(1)}, bf16[4,128,128]{2,1,0:T(8,128)(2,1)S(1)}, u32[]{:S(2)}, u32[]{:S(2)}) collective-permute-start(bf16[4,128,128]{2,1,0:T(8,128)(2,1)S(1)} %get-tuple-element.930), channel_id=1, source_target_pairs={{0,16},{4,24},{8,0},{12,8},{16,20},{20,28},{24,4},{28,12},{1,17},{... | collective-permute-start | bytes 393224 | tf_op jit(solution)/shard_map/ppermute | solution.py:76
  451.2 65.4 %while.124 = (s32[]{:T(128)}, bf16[8,128,256]{2,1,0:T(8,128)(2,1)S(1)}, bf16[2,2,8,128,128]{4,3,2,1,0:T(8,128)(2,1)}, bf16[2,2,8,128,128]{4,3,2,1,0:T(8,128)(2,1...) while((s32[]{:T(128)}, ...), condition=%wide.region_9.10_spmd, body=%wide.region_8.9_spmd.sunk | while | flops 274726912 | bytes 22020356 | solution.py:175
  457.0 8.1 all-to-all-done.8
  471.4 8.8 %all-to-all-done.9 = bf16[16,8,8,256]{3,1,2,0:T(8,128)(2,1)S(1)} async-done(((bf16[16,8,8,256]{3,1,2,0:T(8,128)(2,1)}), bf16[16,8,8,256]{3,1,2,0:T(8,128)(2,1)S(1)}, u32[]{:S(2)}, u32[]{:S(2)}) %all-to-all-start.9) | async-done | bytes 524320 | tf_op jit(solution)/shard_map/while/body/eval_jaxpr/all_to_all | solution.py:27
  489.7 8.1 all-to-all-done.8
  504.1 8.8 %all-to-all-done.9 = bf16[16,8,8,256]{3,1,2,0:T(8,128)(2,1)S(1)} async-done(((bf16[16,8,8,256]{3,1,2,0:T(8,128)(2,1)}), bf16[16,8,8,256]{3,1,2,0:T(8,128)(2,1)S(1)}, u32[]{:S(2)}, u32[]{:S(2)}) %all-to-all-start.9) | async-done | bytes 524320 | tf_op jit(solution)/shard_map/while/body/eval_jaxpr/all_to_all | solution.py:27
  519.5 26.4 %collective-permute-done.22 = bf16[1,2,2,4,128,128]{5,4,3,2,1,0:T(8,128)(2,1)S(1)} collective-permute-done((bf16[1,2,2,4,128,128]{5,4,3,2,1,0:T(8,128)(2,1)}, bf16[1,2,2,4,128,128]{5,4,3,2,1,0:T(8,128)(2,1)S(1)}, u32[]{:S(2)}, u32[]{:S(2)}) %collective-permute-start.22) | collective-permute-done | bytes 524320 | tf_op jit(solution)/shard_map/ppermute | solution.py:129
  548.1 63.4 %while.125 = (s32[]{:T(128)}, bf16[8,128,256]{2,1,0:T(8,128)(2,1)S(1)}, bf16[2,2,8,128,128]{4,3,2,1,0:T(8,128)(2,1)}, bf16[2,2,8,128,128]{4,3,2,1,0:T(8,128)(2,1...) while((s32[]{:T(128)}, ...), condition=%wide.region_11.12_spmd, body=%wide.region_10.11_spmd.sunk | while | flops 274726912 | bytes 22020356 | solution.py:175
  553.8 8.1 all-to-all-done.10
  568.2 8.8 %all-to-all-done.11 = bf16[16,8,8,256]{3,1,2,0:T(8,128)(2,1)S(1)} async-done(((bf16[16,8,8,256]{3,1,2,0:T(8,128)(2,1)}), bf16[16,8,8,256]{3,1,2,0:T(8,128)(2,1)S(1)}, u32[]{:S(2)}, u32[]{:S(2)}) %all-to-all-start.11) | async-done | bytes 524320 | tf_op jit(solution)/shard_map/while/body/eval_jaxpr/all_to_all | solution.py:27
  585.5 8.1 all-to-all-done.10
  599.9 8.8 %all-to-all-done.11 = bf16[16,8,8,256]{3,1,2,0:T(8,128)(2,1)S(1)} async-done(((bf16[16,8,8,256]{3,1,2,0:T(8,128)(2,1)}), bf16[16,8,8,256]{3,1,2,0:T(8,128)(2,1)S(1)}, u32[]{:S(2)}, u32[]{:S(2)}) %all-to-all-start.11) | async-done | bytes 524320 | tf_op jit(solution)/shard_map/while/body/eval_jaxpr/all_to_all | solution.py:27
  614.3 26.3 %collective-permute-done.23 = bf16[1,2,2,4,128,128]{5,4,3,2,1,0:T(8,128)(2,1)S(1)} collective-permute-done((bf16[1,2,2,4,128,128]{5,4,3,2,1,0:T(8,128)(2,1)}, bf16[1,2,2,4,128,128]{5,4,3,2,1,0:T(8,128)(2,1)S(1)}, u32[]{:S(2)}, u32[]{:S(2)}) %collective-permute-start.23) | collective-permute-done | bytes 524320 | tf_op jit(solution)/shard_map/ppermute | solution.py:129
  642.9 63.4 %while.126 = (s32[]{:T(128)}, bf16[8,128,256]{2,1,0:T(8,128)(2,1)S(1)}, bf16[2,2,8,128,128]{4,3,2,1,0:T(8,128)(2,1)}, bf16[2,2,8,128,128]{4,3,2,1,0:T(8,128)(2,1...) while((s32[]{:T(128)}, ...), condition=%wide.region_13.14_spmd, body=%wide.region_12.13_spmd.sunk | while | flops 274726912 | bytes 22020356 | solution.py:175
  648.6 8.1 all-to-all-done.12
  663.0 8.8 %all-to-all-done.13 = bf16[16,8,8,256]{3,1,2,0:T(8,128)(2,1)S(1)} async-done(((bf16[16,8,8,256]{3,1,2,0:T(8,128)(2,1)}), bf16[16,8,8,256]{3,1,2,0:T(8,128)(2,1)S(1)}, u32[]{:S(2)}, u32[]{:S(2)}) %all-to-all-start.13) | async-done | bytes 524320 | tf_op jit(solution)/shard_map/while/body/eval_jaxpr/all_to_all | solution.py:27
  680.3 8.1 all-to-all-done.12
  694.7 8.8 %all-to-all-done.13 = bf16[16,8,8,256]{3,1,2,0:T(8,128)(2,1)S(1)} async-done(((bf16[16,8,8,256]{3,1,2,0:T(8,128)(2,1)}), bf16[16,8,8,256]{3,1,2,0:T(8,128)(2,1)S(1)}, u32[]{:S(2)}, u32[]{:S(2)}) %all-to-all-start.13) | async-done | bytes 524320 | tf_op jit(solution)/shard_map/while/body/eval_jaxpr/all_to_all | solution.py:27
  726.1 13.6 %collective-permute-done.27 = bf16[1,2,2,4,128,128]{5,4,3,2,1,0:T(8,128)(2,1)S(1)} collective-permute-done((bf16[1,2,2,4,128,128]{5,4,3,2,1,0:T(8,128)(2,1)}, bf16[1,2,2,4,128,128]{5,4,3,2,1,0:T(8,128)(2,1)S(1)}, u32[]{:S(2)}, u32[]{:S(2)}) %collective-permute-start.27) | collective-permute-done | bytes 524320 | tf_op jit(solution)/shard_map/ppermute | solution.py:129
  741.8 63.6 %while.127 = (s32[]{:T(128)}, bf16[8,128,256]{2,1,0:T(8,128)(2,1)S(1)}, bf16[2,2,8,128,128]{4,3,2,1,0:T(8,128)(2,1)}, bf16[2,2,8,128,128]{4,3,2,1,0:T(8,128)(2,1...) while((s32[]{:T(128)}, ...), condition=%wide.region_15.16_spmd, body=%wide.region_14.15_spmd.sunk | while | flops 274726912 | bytes 22020356 | solution.py:175
  747.8 8.1 all-to-all-done.14
  762.2 8.8 %all-to-all-done.15 = bf16[16,8,8,256]{3,1,2,0:T(8,128)(2,1)S(1)} async-done(((bf16[16,8,8,256]{3,1,2,0:T(8,128)(2,1)}), bf16[16,8,8,256]{3,1,2,0:T(8,128)(2,1)S(1)}, u32[]{:S(2)}, u32[]{:S(2)}) %all-to-all-start.15) | async-done | bytes 524320 | tf_op jit(solution)/shard_map/while/body/eval_jaxpr/all_to_all | solution.py:27
  779.5 8.1 all-to-all-done.14
  793.9 8.8 %all-to-all-done.15 = bf16[16,8,8,256]{3,1,2,0:T(8,128)(2,1)S(1)} async-done(((bf16[16,8,8,256]{3,1,2,0:T(8,128)(2,1)}), bf16[16,8,8,256]{3,1,2,0:T(8,128)(2,1)S(1)}, u32[]{:S(2)}, u32[]{:S(2)}) %all-to-all-start.15) | async-done | bytes 524320 | tf_op jit(solution)/shard_map/while/body/eval_jaxpr/all_to_all | solution.py:27
  818.9 22.1 %collective-permute-done.32 = bf16[1,2,2,4,128,128]{5,4,3,2,1,0:T(8,128)(2,1)S(1)} collective-permute-done((bf16[1,2,2,4,128,128]{5,4,3,2,1,0:T(8,128)(2,1)}, bf16[1,2,2,4,128,128]{5,4,3,2,1,0:T(8,128)(2,1)S(1)}, u32[]{:S(2)}, u32[]{:S(2)}) %collective-permute-start.32) | collective-permute-done | bytes 524320 | tf_op jit(solution)/shard_map/ppermute | solution.py:129
  846.3 6.2 collective-permute-done.34
  (377 shorter events, 395.2 us)
Async XLA Ops:
  12.3 13.6 %collective-permute-start.6 = (bf16[2,4,128,128]{2,3,1,0:T(8,128)(2,1)S(1)}, bf16[2,4,128,128]{2,3,1,0:T(8,128)(2,1)S(1)}, u32[]{:S(2)}, u32[]{:S(2)}) collective-permute-start(bf16[2,4,128,128]{2,3,1,0:T(8,128)(2,1)S(1)} %get-tuple-element.905), channel_id=1, source_target_pairs={{0,24},{8,16},{16,8},{24,0},{1,25},{9,17},{17,9},{25,1},{2,26},{10... | collective-permute-start | bytes 786440 | tf_op jit(solution)/shard_map/ppermute | solution.py:103
  13.1 21.1 %collective-permute-start = (bf16[4,128,128]{2,1,0:T(8,128)(2,1)S(1)}, bf16[4,128,128]{2,1,0:T(8,128)(2,1)S(1)}, u32[]{:S(2)}, u32[]{:S(2)}) collective-permute-start(bf16[4,128,128]{2,1,0:T(8,128)(2,1)S(1)} %get-tuple-element.936), channel_id=1, source_target_pairs={{0,0},{4,8},{8,16},{12,24},{16,4},{20,12},{24,20},{28,28},{1,1},{5... | collective-permute-start | bytes 393224 | tf_op jit(solution)/shard_map/ppermute | solution.py:76
  27.1 65.6 %collective-permute-start.7 = (bf16[2,2,4,128,128]{3,4,2,1,0:T(8,128)(2,1)}, bf16[2,2,4,128,128]{3,4,2,1,0:T(8,128)(2,1)}, u32[]{:S(2)}, u32[]{:S(2)}) collective-permute-start(bf16[2,2,4,128,128]{3,4,2,1,0:T(8,128)(2,1)} %pad_maximum_fusion.10), channel_id=1, source_target_pairs={{0,4},{4,0},{1,5},{5,1},{2,6},{6,2},{3,7},{7,3},{8,12},{12,8},{9,1... | collective-permute-start | bytes 1572872 | tf_op jit(solution)/shard_map/ppermute | solution.py:112
  30.5 62.2 %collective-permute-start.8 = (bf16[2,2,4,128,128]{3,4,2,1,0:T(8,128)(2,1)}, bf16[2,2,4,128,128]{3,4,2,1,0:T(8,128)(2,1)}, u32[]{:S(2)}, u32[]{:S(2)}) collective-permute-start(bf16[2,2,4,128,128]{3,4,2,1,0:T(8,128)(2,1)} %pad_maximum_fusion.11), channel_id=1, source_target_pairs={{0,4},{4,0},{1,5},{5,1},{2,6},{6,2},{3,7},{7,3},{8,12},{12,8},{9,1... | collective-permute-start | bytes 1572872 | tf_op jit(solution)/shard_map/ppermute | solution.py:112
  30.8 57.0 %collective-permute-start.1 = (bf16[4,128,128]{2,1,0:T(8,128)(2,1)}, bf16[4,128,128]{2,1,0:T(8,128)(2,1)S(1)}, u32[]{:S(2)}, u32[]{:S(2)}) collective-permute-start(bf16[4,128,128]{2,1,0:T(8,128)(2,1)} %get-tuple-element.939), channel_id=1, source_target_pairs={{0,8},{4,0},{8,24},{12,16},{16,12},{20,4},{24,28},{28,20},{1,9},{5... | collective-permute-start | bytes 393224 | tf_op jit(solution)/shard_map/ppermute | solution.py:76
  30.8 57.0 %collective-permute-start.2 = (bf16[4,128,128]{2,1,0:T(8,128)(2,1)}, bf16[4,128,128]{2,1,0:T(8,128)(2,1)S(1)}, u32[]{:S(2)}, u32[]{:S(2)}) collective-permute-start(bf16[4,128,128]{2,1,0:T(8,128)(2,1)} %get-tuple-element.938), channel_id=1, source_target_pairs={{0,16},{4,24},{8,0},{12,8},{16,20},{20,28},{24,4},{28,12},{1,17},{... | collective-permute-start | bytes 393224 | tf_op jit(solution)/shard_map/ppermute | solution.py:76
  34.3 57.9 %collective-permute-start.3 = (bf16[4,128,128]{2,1,0:T(8,128)(2,1)}, bf16[4,128,128]{2,1,0:T(8,128)(2,1)S(1)}, u32[]{:S(2)}, u32[]{:S(2)}) collective-permute-start(bf16[4,128,128]{2,1,0:T(8,128)(2,1)} %get-tuple-element.937), channel_id=1, source_target_pairs={{0,24},{4,16},{8,8},{12,0},{16,28},{20,20},{24,12},{28,4},{1,25},{... | collective-permute-start | bytes 393224 | tf_op jit(solution)/shard_map/ppermute | solution.py:76
  114.9 81.2 %collective-permute-start.12 = (bf16[2,2,4,128,128]{3,4,2,1,0:T(8,128)(2,1)}, bf16[2,2,4,128,128]{3,4,2,1,0:T(8,128)(2,1)}, u32[]{:S(2)}, u32[]{:S(2)}) collective-permute-start(bf16[2,2,4,128,128]{3,4,2,1,0:T(8,128)(2,1)} %pad_maximum_fusion.12), channel_id=1, source_target_pairs={{0,4},{4,0},{1,5},{5,1},{2,6},{6,2},{3,7},{7,3},{8,12},{12,8},{9,1... | collective-permute-start | bytes 1572872 | tf_op jit(solution)/shard_map/ppermute | solution.py:112
  118.3 25.3 %all-to-all-start = ((bf16[16,8,8,256]{3,1,2,0:T(8,128)(2,1)}), bf16[16,8,8,256]{3,1,2,0:T(8,128)(2,1)S(1)}, u32[]{:S(2)}, u32[]{:S(2)}) async-start(bf16[16,8,8,256]{3,1,2,0:T(8,128)(2,1)} %copy.340), calls=%async_computation | async-start | bytes 1048576 | tf_op jit(solution)/shard_map/while/body/eval_jaxpr/all_to_all | solution.py:27
  146.2 12.8 %all-to-all-start.1 = ((bf16[16,8,8,256]{3,1,2,0:T(8,128)(2,1)}), bf16[16,8,8,256]{3,1,2,0:T(8,128)(2,1)S(1)}, u32[]{:S(2)}, u32[]{:S(2)}) async-start(bf16[16,8,8,256]{3,1,2,0:T(8,128)(2,1)} %copy.341), calls=%async_computation.1 | async-start | bytes 1048576 | tf_op jit(solution)/shard_map/while/body/eval_jaxpr/all_to_all | solution.py:27
  161.6 12.8 %all-to-all-start = ((bf16[16,8,8,256]{3,1,2,0:T(8,128)(2,1)}), bf16[16,8,8,256]{3,1,2,0:T(8,128)(2,1)S(1)}, u32[]{:S(2)}, u32[]{:S(2)}) async-start(bf16[16,8,8,256]{3,1,2,0:T(8,128)(2,1)} %copy.340), calls=%async_computation | async-start | bytes 1048576 | tf_op jit(solution)/shard_map/while/body/eval_jaxpr/all_to_all | solution.py:27
  177.0 12.8 %all-to-all-start.1 = ((bf16[16,8,8,256]{3,1,2,0:T(8,128)(2,1)}), bf16[16,8,8,256]{3,1,2,0:T(8,128)(2,1)S(1)}, u32[]{:S(2)}, u32[]{:S(2)}) async-start(bf16[16,8,8,256]{3,1,2,0:T(8,128)(2,1)} %copy.341), calls=%async_computation.1 | async-start | bytes 1048576 | tf_op jit(solution)/shard_map/while/body/eval_jaxpr/all_to_all | solution.py:27
  194.5 80.7 %collective-permute-start.13 = (bf16[2,2,4,128,128]{3,4,2,1,0:T(8,128)(2,1)}, bf16[2,2,4,128,128]{3,4,2,1,0:T(8,128)(2,1)}, u32[]{:S(2)}, u32[]{:S(2)}) collective-permute-start(bf16[2,2,4,128,128]{3,4,2,1,0:T(8,128)(2,1)} %pad_maximum_fusion.13), channel_id=1, source_target_pairs={{0,4},{4,0},{1,5},{5,1},{2,6},{6,2},{3,7},{7,3},{8,12},{12,8},{9,1... | collective-permute-start | bytes 1572872 | tf_op jit(solution)/shard_map/ppermute | solution.py:112
  201.6 23.6 %all-to-all-start.2 = ((bf16[16,8,8,256]{3,1,2,0:T(8,128)(2,1)}), bf16[16,8,8,256]{3,1,2,0:T(8,128)(2,1)S(1)}, u32[]{:S(2)}, u32[]{:S(2)}) async-start(bf16[16,8,8,256]{3,1,2,0:T(8,128)(2,1)} %copy.344), calls=%async_computation.2 | async-start | bytes 1048576 | tf_op jit(solution)/shard_map/while/body/eval_jaxpr/all_to_all | solution.py:27
  227.7 12.8 %all-to-all-start.3 = ((bf16[16,8,8,256]{3,1,2,0:T(8,128)(2,1)}), bf16[16,8,8,256]{3,1,2,0:T(8,128)(2,1)S(1)}, u32[]{:S(2)}, u32[]{:S(2)}) async-start(bf16[16,8,8,256]{3,1,2,0:T(8,128)(2,1)} %copy.345), calls=%async_computation.3 | async-start | bytes 1048576 | tf_op jit(solution)/shard_map/while/body/eval_jaxpr/all_to_all | solution.py:27
  243.2 12.8 %all-to-all-start.2 = ((bf16[16,8,8,256]{3,1,2,0:T(8,128)(2,1)}), bf16[16,8,8,256]{3,1,2,0:T(8,128)(2,1)S(1)}, u32[]{:S(2)}, u32[]{:S(2)}) async-start(bf16[16,8,8,256]{3,1,2,0:T(8,128)(2,1)} %copy.344), calls=%async_computation.2 | async-start | bytes 1048576 | tf_op jit(solution)/shard_map/while/body/eval_jaxpr/all_to_all | solution.py:27
  258.5 12.8 %all-to-all-start.3 = ((bf16[16,8,8,256]{3,1,2,0:T(8,128)(2,1)}), bf16[16,8,8,256]{3,1,2,0:T(8,128)(2,1)S(1)}, u32[]{:S(2)}, u32[]{:S(2)}) async-start(bf16[16,8,8,256]{3,1,2,0:T(8,128)(2,1)} %copy.345), calls=%async_computation.3 | async-start | bytes 1048576 | tf_op jit(solution)/shard_map/while/body/eval_jaxpr/all_to_all | solution.py:27
  280.6 12.8 %all-to-all-start.4 = ((bf16[16,8,8,256]{3,1,2,0:T(8,128)(2,1)}), bf16[16,8,8,256]{3,1,2,0:T(8,128)(2,1)S(1)}, u32[]{:S(2)}, u32[]{:S(2)}) async-start(bf16[16,8,8,256]{3,1,2,0:T(8,128)(2,1)} %copy.348), calls=%async_computation.4 | async-start | bytes 1048576 | tf_op jit(solution)/shard_map/while/body/eval_jaxpr/all_to_all | solution.py:27
  296.0 12.8 %all-to-all-start.5 = ((bf16[16,8,8,256]{3,1,2,0:T(8,128)(2,1)}), bf16[16,8,8,256]{3,1,2,0:T(8,128)(2,1)S(1)}, u32[]{:S(2)}, u32[]{:S(2)}) async-start(bf16[16,8,8,256]{3,1,2,0:T(8,128)(2,1)} %copy.349), calls=%async_computation.5 | async-start | bytes 1048576 | tf_op jit(solution)/shard_map/while/body/eval_jaxpr/all_to_all | solution.py:27
  311.4 12.8 %all-to-all-start.4 = ((bf16[16,8,8,256]{3,1,2,0:T(8,128)(2,1)}), bf16[16,8,8,256]{3,1,2,0:T(8,128)(2,1)S(1)}, u32[]{:S(2)}, u32[]{:S(2)}) async-start(bf16[16,8,8,256]{3,1,2,0:T(8,128)(2,1)} %copy.348), calls=%async_computation.4 | async-start | bytes 1048576 | tf_op jit(solution)/shard_map/while/body/eval_jaxpr/all_to_all | solution.py:27
  326.7 12.8 %all-to-all-start.5 = ((bf16[16,8,8,256]{3,1,2,0:T(8,128)(2,1)}), bf16[16,8,8,256]{3,1,2,0:T(8,128)(2,1)S(1)}, u32[]{:S(2)}, u32[]{:S(2)}) async-start(bf16[16,8,8,256]{3,1,2,0:T(8,128)(2,1)} %copy.349), calls=%async_computation.5 | async-start | bytes 1048576 | tf_op jit(solution)/shard_map/while/body/eval_jaxpr/all_to_all | solution.py:27
  347.3 12.8 %all-to-all-start.6 = ((bf16[16,8,8,256]{3,1,2,0:T(8,128)(2,1)}), bf16[16,8,8,256]{3,1,2,0:T(8,128)(2,1)S(1)}, u32[]{:S(2)}, u32[]{:S(2)}) async-start(bf16[16,8,8,256]{3,1,2,0:T(8,128)(2,1)} %copy.352), calls=%async_computation.6 | async-start | bytes 1048576 | tf_op jit(solution)/shard_map/while/body/eval_jaxpr/all_to_all | solution.py:27
  362.7 12.8 %all-to-all-start.7 = ((bf16[16,8,8,256]{3,1,2,0:T(8,128)(2,1)}), bf16[16,8,8,256]{3,1,2,0:T(8,128)(2,1)S(1)}, u32[]{:S(2)}, u32[]{:S(2)}) async-start(bf16[16,8,8,256]{3,1,2,0:T(8,128)(2,1)} %copy.353), calls=%async_computation.7 | async-start | bytes 1048576 | tf_op jit(solution)/shard_map/while/body/eval_jaxpr/all_to_all | solution.py:27
  378.1 12.8 %all-to-all-start.6 = ((bf16[16,8,8,256]{3,1,2,0:T(8,128)(2,1)}), bf16[16,8,8,256]{3,1,2,0:T(8,128)(2,1)S(1)}, u32[]{:S(2)}, u32[]{:S(2)}) async-start(bf16[16,8,8,256]{3,1,2,0:T(8,128)(2,1)} %copy.352), calls=%async_computation.6 | async-start | bytes 1048576 | tf_op jit(solution)/shard_map/while/body/eval_jaxpr/all_to_all | solution.py:27
  393.4 12.8 %all-to-all-start.7 = ((bf16[16,8,8,256]{3,1,2,0:T(8,128)(2,1)}), bf16[16,8,8,256]{3,1,2,0:T(8,128)(2,1)S(1)}, u32[]{:S(2)}, u32[]{:S(2)}) async-start(bf16[16,8,8,256]{3,1,2,0:T(8,128)(2,1)} %copy.353), calls=%async_computation.7 | async-start | bytes 1048576 | tf_op jit(solution)/shard_map/while/body/eval_jaxpr/all_to_all | solution.py:27
  413.3 21.2 %collective-permute-start.20 = (bf16[4,128,128]{2,1,0:T(8,128)(2,1)S(1)}, bf16[4,128,128]{2,1,0:T(8,128)(2,1)S(1)}, u32[]{:S(2)}, u32[]{:S(2)}) collective-permute-start(bf16[4,128,128]{2,1,0:T(8,128)(2,1)S(1)} %get-tuple-element.922), channel_id=1, source_target_pairs={{0,8},{4,24},{8,12},{12,28},{16,0},{20,16},{24,4},{28,20},{1,9},{5... | collective-permute-start | bytes 393224 | tf_op jit(solution)/shard_map/ppermute | solution.py:76
  413.6 26.5 %collective-permute-start.21 = (bf16[4,128,128]{2,1,0:T(8,128)(2,1)S(1)}, bf16[4,128,128]{2,1,0:T(8,128)(2,1)S(1)}, u32[]{:S(2)}, u32[]{:S(2)}) collective-permute-start(bf16[4,128,128]{2,1,0:T(8,128)(2,1)S(1)} %get-tuple-element.921), channel_id=1, source_target_pairs={{0,12},{4,28},{8,8},{12,24},{16,4},{20,20},{24,0},{28,16},{1,13},{... | collective-permute-start | bytes 393224 | tf_op jit(solution)/shard_map/ppermute | solution.py:76
  415.6 24.7 %collective-permute-start.14 = (bf16[4,128,128]{2,1,0:T(8,128)(2,1)S(1)}, bf16[4,128,128]{2,1,0:T(8,128)(2,1)S(1)}, u32[]{:S(2)}, u32[]{:S(2)}) collective-permute-start(bf16[4,128,128]{2,1,0:T(8,128)(2,1)S(1)} %get-tuple-element.928), channel_id=1, source_target_pairs={{0,0},{4,8},{8,16},{12,24},{16,4},{20,12},{24,20},{28,28},{1,1},{5... | collective-permute-start | bytes 393224 | tf_op jit(solution)/shard_map/ppermute | solution.py:76
  416.3 26.6 %collective-permute-start.15 = (bf16[4,128,128]{2,1,0:T(8,128)(2,1)S(1)}, bf16[4,128,128]{2,1,0:T(8,128)(2,1)S(1)}, u32[]{:S(2)}, u32[]{:S(2)}) collective-permute-start(bf16[4,128,128]{2,1,0:T(8,128)(2,1)S(1)} %get-tuple-element.931), channel_id=1, source_target_pairs={{0,8},{4,0},{8,24},{12,16},{16,12},{20,4},{24,28},{28,20},{1,9},{5... | collective-permute-start | bytes 393224 | tf_op jit(solution)/shard_map/ppermute | solution.py:76
  419.7 23.2 %collective-permute-start.16 = (bf16[4,128,128]{2,1,0:T(8,128)(2,1)S(1)}, bf16[4,128,128]{2,1,0:T(8,128)(2,1)S(1)}, u32[]{:S(2)}, u32[]{:S(2)}) collective-permute-start(bf16[4,128,128]{2,1,0:T(8,128)(2,1)S(1)} %get-tuple-element.930), channel_id=1, source_target_pairs={{0,16},{4,24},{8,0},{12,8},{16,20},{20,28},{24,4},{28,12},{1,17},{... | collective-permute-start | bytes 393224 | tf_op jit(solution)/shard_map/ppermute | solution.py:76
  434.5 13.6 %collective-permute-start.17 = (bf16[4,128,128]{2,1,0:T(8,128)(2,1)S(1)}, bf16[4,128,128]{2,1,0:T(8,128)(2,1)S(1)}, u32[]{:S(2)}, u32[]{:S(2)}) collective-permute-start(bf16[4,128,128]{2,1,0:T(8,128)(2,1)S(1)} %get-tuple-element.929), channel_id=1, source_target_pairs={{0,24},{4,16},{8,8},{12,0},{16,28},{20,20},{24,12},{28,4},{1,25},{... | collective-permute-start | bytes 393224 | tf_op jit(solution)/shard_map/ppermute | solution.py:76
  452.3 12.8 %all-to-all-start.8 = ((bf16[16,8,8,256]{3,2,1,0:T(8,128)(2,1)}), bf16[16,8,8,256]{3,2,1,0:T(8,128)(2,1)S(1)}, u32[]{:S(2)}, u32[]{:S(2)}) async-start(bf16[16,8,8,256]{3,2,1,0:T(8,128)(2,1)} %bitcast.682), calls=%async_computation.8 | async-start | bytes 1048576 | tf_op jit(solution)/shard_map/while/body/eval_jaxpr/all_to_all | solution.py:27
  467.4 12.8 %all-to-all-start.9 = ((bf16[16,8,8,256]{3,1,2,0:T(8,128)(2,1)}), bf16[16,8,8,256]{3,1,2,0:T(8,128)(2,1)S(1)}, u32[]{:S(2)}, u32[]{:S(2)}) async-start(bf16[16,8,8,256]{3,1,2,0:T(8,128)(2,1)} %copy.361), calls=%async_computation.9 | async-start | bytes 1048576 | tf_op jit(solution)/shard_map/while/body/eval_jaxpr/all_to_all | solution.py:27
  485.0 12.8 %all-to-all-start.8 = ((bf16[16,8,8,256]{3,2,1,0:T(8,128)(2,1)}), bf16[16,8,8,256]{3,2,1,0:T(8,128)(2,1)S(1)}, u32[]{:S(2)}, u32[]{:S(2)}) async-start(bf16[16,8,8,256]{3,2,1,0:T(8,128)(2,1)} %bitcast.682), calls=%async_computation.8 | async-start | bytes 1048576 | tf_op jit(solution)/shard_map/while/body/eval_jaxpr/all_to_all | solution.py:27
  500.1 12.8 %all-to-all-start.9 = ((bf16[16,8,8,256]{3,1,2,0:T(8,128)(2,1)}), bf16[16,8,8,256]{3,1,2,0:T(8,128)(2,1)S(1)}, u32[]{:S(2)}, u32[]{:S(2)}) async-start(bf16[16,8,8,256]{3,1,2,0:T(8,128)(2,1)} %copy.361), calls=%async_computation.9 | async-start | bytes 1048576 | tf_op jit(solution)/shard_map/while/body/eval_jaxpr/all_to_all | solution.py:27
  519.5 26.4 %collective-permute-start.22 = (bf16[1,2,2,4,128,128]{5,4,3,2,1,0:T(8,128)(2,1)}, bf16[1,2,2,4,128,128]{5,4,3,2,1,0:T(8,128)(2,1)S(1)}, u32[]{:S(2)}, u32[]{:S(2)}) collective-permute-start(bf16[1,2,2,4,128,128]{5,4,3,2,1,0:T(8,128)(2,1)} %dynamic-slice_bitcast_fusion.35), channel_id=1, source_target_pairs={{0,4},{4,0},{1,5},{5,1},{2,6},{6,2},{3,7},{7,3},{8,12},{12,8},{9,1... | collective-permute-start | bytes 1572872 | tf_op jit(solution)/shard_map/ppermute | solution.py:129
  580.8 12.8 %all-to-all-start.10 = ((bf16[16,8,8,256]{3,2,1,0:T(8,128)(2,1)}), bf16[16,8,8,256]{3,2,1,0:T(8,128)(2,1)S(1)}, u32[]{:S(2)}, u32[]{:S(2)}) async-start(bf16[16,8,8,256]{3,2,1,0:T(8,128)(2,1)} %bitcast.700), calls=%async_computation.10 | async-start | bytes 1048576 | tf_op jit(solution)/shard_map/while/body/eval_jaxpr/all_to_all | solution.py:27
  595.9 12.8 %all-to-all-start.11 = ((bf16[16,8,8,256]{3,1,2,0:T(8,128)(2,1)}), bf16[16,8,8,256]{3,1,2,0:T(8,128)(2,1)S(1)}, u32[]{:S(2)}, u32[]{:S(2)}) async-start(bf16[16,8,8,256]{3,1,2,0:T(8,128)(2,1)} %copy.369), calls=%async_computation.11 | async-start | bytes 1048576 | tf_op jit(solution)/shard_map/while/body/eval_jaxpr/all_to_all | solution.py:27
  614.3 26.4 %collective-permute-start.23 = (bf16[1,2,2,4,128,128]{5,4,3,2,1,0:T(8,128)(2,1)}, bf16[1,2,2,4,128,128]{5,4,3,2,1,0:T(8,128)(2,1)S(1)}, u32[]{:S(2)}, u32[]{:S(2)}) collective-permute-start(bf16[1,2,2,4,128,128]{5,4,3,2,1,0:T(8,128)(2,1)} %dynamic-slice_bitcast_fusion.34), channel_id=1, source_target_pairs={{0,4},{4,0},{1,5},{5,1},{2,6},{6,2},{3,7},{7,3},{8,12},{12,8},{9,1... | collective-permute-start | bytes 1572872 | tf_op jit(solution)/shard_map/ppermute | solution.py:129
  713.0 26.7 %collective-permute-start.27 = (bf16[1,2,2,4,128,128]{5,4,3,2,1,0:T(8,128)(2,1)}, bf16[1,2,2,4,128,128]{5,4,3,2,1,0:T(8,128)(2,1)S(1)}, u32[]{:S(2)}, u32[]{:S(2)}) collective-permute-start(bf16[1,2,2,4,128,128]{5,4,3,2,1,0:T(8,128)(2,1)} %dynamic-slice_bitcast_fusion.33), channel_id=1, source_target_pairs={{0,4},{4,0},{1,5},{5,1},{2,6},{6,2},{3,7},{7,3},{8,12},{12,8},{9,1... | collective-permute-start | bytes 1572872 | tf_op jit(solution)/shard_map/ppermute | solution.py:129
  743.2 12.8 %all-to-all-start.14 = ((bf16[16,8,8,256]{3,2,1,0:T(8,128)(2,1)}), bf16[16,8,8,256]{3,2,1,0:T(8,128)(2,1)S(1)}, u32[]{:S(2)}, u32[]{:S(2)}) async-start(bf16[16,8,8,256]{3,2,1,0:T(8,128)(2,1)} %bitcast.736), calls=%async_computation.14 | async-start | bytes 1048576 | tf_op jit(solution)/shard_map/while/body/eval_jaxpr/all_to_all | solution.py:27
  758.2 12.8 %all-to-all-start.15 = ((bf16[16,8,8,256]{3,1,2,0:T(8,128)(2,1)}), bf16[16,8,8,256]{3,1,2,0:T(8,128)(2,1)S(1)}, u32[]{:S(2)}, u32[]{:S(2)}) async-start(bf16[16,8,8,256]{3,1,2,0:T(8,128)(2,1)} %copy.385), calls=%async_computation.15 | async-start | bytes 1048576 | tf_op jit(solution)/shard_map/while/body/eval_jaxpr/all_to_all | solution.py:27
  774.8 12.8 %all-to-all-start.14 = ((bf16[16,8,8,256]{3,2,1,0:T(8,128)(2,1)}), bf16[16,8,8,256]{3,2,1,0:T(8,128)(2,1)S(1)}, u32[]{:S(2)}, u32[]{:S(2)}) async-start(bf16[16,8,8,256]{3,2,1,0:T(8,128)(2,1)} %bitcast.736), calls=%async_computation.14 | async-start | bytes 1048576 | tf_op jit(solution)/shard_map/while/body/eval_jaxpr/all_to_all | solution.py:27
  808.3 32.7 %collective-permute-start.32 = (bf16[1,2,2,4,128,128]{5,4,3,2,1,0:T(8,128)(2,1)}, bf16[1,2,2,4,128,128]{5,4,3,2,1,0:T(8,128)(2,1)S(1)}, u32[]{:S(2)}, u32[]{:S(2)}) collective-permute-start(bf16[1,2,2,4,128,128]{5,4,3,2,1,0:T(8,128)(2,1)} %dynamic-slice_bitcast_fusion.32), channel_id=1, source_target_pairs={{0,4},{4,0},{1,5},{5,1},{2,6},{6,2},{3,7},{7,3},{8,12},{12,8},{9,1... | collective-permute-start | bytes 1572872 | tf_op jit(solution)/shard_map/ppermute | solution.py:129
  809.0 32.6 %collective-permute-start.28 = (bf16[4,128,128]{2,1,0:T(8,128)(2,1)S(1)}, bf16[4,128,128]{2,1,0:T(8,128)(2,1)S(1)}, u32[]{:S(2)}, u32[]{:S(2)}) collective-permute-start(bf16[4,128,128]{2,1,0:T(8,128)(2,1)S(1)} %get-tuple-element.912), channel_id=1, source_target_pairs={{0,0},{4,16},{8,4},{12,20},{16,8},{20,24},{24,12},{28,28},{1,1},{5... | collective-permute-start | bytes 393224 | tf_op jit(solution)/shard_map/ppermute | solution.py:76
  809.7 35.5 %collective-permute-start.29 = (bf16[4,128,128]{2,1,0:T(8,128)(2,1)S(1)}, bf16[4,128,128]{2,1,0:T(8,128)(2,1)S(1)}, u32[]{:S(2)}, u32[]{:S(2)}) collective-permute-start(bf16[4,128,128]{2,1,0:T(8,128)(2,1)S(1)} %get-tuple-element.915), channel_id=1, source_target_pairs={{0,4},{4,20},{8,0},{12,16},{16,12},{20,28},{24,8},{28,24},{1,5},{5... | collective-permute-start | bytes 393224 | tf_op jit(solution)/shard_map/ppermute | solution.py:76
  814.9 30.4 %collective-permute-start.30 = (bf16[4,128,128]{2,1,0:T(8,128)(2,1)S(1)}, bf16[4,128,128]{2,1,0:T(8,128)(2,1)S(1)}, u32[]{:S(2)}, u32[]{:S(2)}) collective-permute-start(bf16[4,128,128]{2,1,0:T(8,128)(2,1)S(1)} %get-tuple-element.914), channel_id=1, source_target_pairs={{0,8},{4,24},{8,12},{12,28},{16,0},{20,16},{24,4},{28,20},{1,9},{5... | collective-permute-start | bytes 393224 | tf_op jit(solution)/shard_map/ppermute | solution.py:76
  814.9 30.4 %collective-permute-start.31 = (bf16[4,128,128]{2,1,0:T(8,128)(2,1)S(1)}, bf16[4,128,128]{2,1,0:T(8,128)(2,1)S(1)}, u32[]{:S(2)}, u32[]{:S(2)}) collective-permute-start(bf16[4,128,128]{2,1,0:T(8,128)(2,1)S(1)} %get-tuple-element.913), channel_id=1, source_target_pairs={{0,12},{4,28},{8,8},{12,24},{16,4},{20,20},{24,0},{28,16},{1,13},{... | collective-permute-start | bytes 393224 | tf_op jit(solution)/shard_map/ppermute | solution.py:76
  (48 other events, 346.5 us)

commit v7 on v6

--- a/solution.py
+++ b/solution.py
@@ -96,13 +96,14 @@
         parts = turned(parts.reshape(sections, sub, size, rows), s_index, line, outof)
         return parts.reshape(1, held * size, rows)
 
-    def scattered(parts):
-        moved = [pick(parts, s_index)]
+    def scattered(*kinds):
+        moved = [jnp.stack([pick(parts, s_index) for parts in kinds])]
         for mask in range(1, sections):
             pairs = [(s, s ^ mask) for s in range(sections)]
-            moved.append(lax.ppermute(pick(parts, s_index ^ mask), "s", pairs))
+            value = jnp.stack([pick(parts, s_index ^ mask) for parts in kinds])
+            moved.append(lax.ppermute(value, "s", pairs))
         moved = jnp.stack(moved)
-        return jnp.stack([pick(moved, s_index ^ section) for section in range(sections)])
+        return [pick(moved, s_index ^ section) for section in range(sections)]
 
     def gathered(part):
         moved = [part]
@@ -136,56 +137,60 @@
     def unordered(terms):
         return jnp.einsum("aj,lfbac,ck->lfbjk", order, terms, order, preferred_element_type=F32).astype(BF16)
 
-    both = jnp.stack([right_factor[:, 0], left_factor[:, 0]], axis=1)
-    both = both.reshape(loops, 2, sections, sub, size, size).transpose(0, 2, 1, 3, 4, 5)
     stretches = layers // STRETCH
-    arrived = [scattered(both[0])]
-
-    def fetch(stretch):
-        loop, start = divmod(stretch * STRETCH, sections)
-        return gathered(arrived[loop][start : start + STRETCH])
-
+    per_loop = stretches // loops
+    rights = right_factor[:, 0].reshape(loops, sections, sub, size, size)
+    lefts = left_factor[:, 0].reshape(loops, sections, sub, size, size)
+
+    def part_of(arrived, stretch):
+        start = stretch * STRETCH % sections
+        return jnp.stack(arrived[start : start + STRETCH])
+
+    arrived = scattered(rights[0], lefts[0])
+    parts = [part_of(arrived, stretch) for stretch in range(per_loop)]
     current = enter(inputs)
+    weights = [ordered(gathered(parts[0]))]
+    later = (parts[1:], rights[1:], lefts[1:], cotangent)
+    current, weights[0], later = lax.optimization_barrier((current, weights[0], later))
+    parts[1:], rights, lefts, cotangent = later
+    for loop in range(loops - 1):
+        arrived = scattered(rights[loop], lefts[loop])
+        parts.extend(part_of(arrived, stretch + loop * per_loop) for stretch in range(per_loop))
     stored = []
-    weights = [ordered(fetch(0))]
-    later, weights[0], cotangent = lax.optimization_barrier((both[1:], weights[0], cotangent))
-    arrived.extend(scattered(later[loop]) for loop in range(loops - 1))
     for stretch in range(stretches):
-        coming = fetch(stretch + 1) if stretch + 1 < stretches else None
-        if stretch + 1 == stretches:
+        coming = None
+        if stretch + 1 < stretches:
+            coming = gathered(parts[stretch + 1])
+        if stretch + 2 == stretches:
             current, cotangent = lax.optimization_barrier((current, cotangent))
             grad = enter(cotangent)
         current, saved = lax.scan(forward_layer, current, weights[stretch])
         stored.append(saved)
         if coming is not None:
-            current, coming = lax.optimization_barrier((current, coming))
             weights.append(ordered(coming))
-    outputs = leave(current)
-
-    per_loop = stretches // loops
+    current, grad = lax.optimization_barrier((current, grad))
 
     def returned(loop):
         mine = jnp.concatenate(sums[loop * per_loop : (loop + 1) * per_loop])
-        return scattered(mine).transpose(1, 0, 2, 3, 4).reshape(2, 1, held, size, size)
+        moved = jnp.stack(scattered(mine))
+        return moved.reshape(sections, 2, sub, size, size).transpose(1, 0, 2, 3, 4).reshape(2, 1, held, size, size)
 
     sums = [None] * stretches
     halves = [None] * loops
-    beside = {"outputs": outputs}
+    outputs = leave(current)
     for stretch in reversed(range(stretches)):
         grad, terms = lax.scan(backward_layer, grad, (weights[stretch], stored[stretch]), reverse=True)
-        grad, terms, beside = lax.optimization_barrier((grad, terms, beside))
-        outputs = beside.get("outputs", outputs)
-        ready = beside.get("half")
-        if "sum" in beside:
-            sums[stretch + 1] = beside["sum"]
-        beside = {"sum": summed(unordered(terms))}
-        loop = (stretch + 1) // per_loop
-        if (stretch + 1) % per_loop == 0 and loop < loops:
-            beside["half"] = returned(loop)
-            owed = loop
-        if ready is not None:
-            halves[owed] = ready
-    sums[0] = beside["sum"]
+        two_ago = sums[stretch + 2] if stretch + 2 < stretches else outputs
+        if stretch + 1 < stretches:
+            grad, terms, two_ago = lax.optimization_barrier((grad, terms, two_ago))
+            if stretch + 2 < stretches:
+                sums[stretch + 2] = two_ago
+            else:
+                outputs = two_ago
+        sums[stretch] = summed(unordered(terms))
+        loop = (stretch + 2) // per_loop
+        if (stretch + 2) % per_loop == 0 and 0 < loop < loops:
+            halves[loop] = returned(loop)
     halves[0] = returned(0)
     input_grad = leave(grad)
     grads = jnp.stack(halves).astype(F32)

time: 873 us -> 834 us (0.955)
  waiting for transfers between devices: 490 us -> 419 us
  starting transfers between devices: 180 us -> 215 us
    ppermute x4, waiting for transfers between devices: 88.4 us -> 0.01 us  [summed(): lax.ppermute(give, 't', pairs).astype(F32)]
    ppermute x4, waiting for transfers between devices: 0.01 us -> 49.9 us  [gathered(): other = [lax.ppermute(one, 't', pairs) for one in moved]]
    ppermute x16, waiting for transfers between devices: 63.1 us -> 28.9 us  [turned(): moved.append(lax.ppermute(pick(parts, send_by ^ mask), ('s', 't'), pairs))]
    ppermute x4, starting transfers between devices: 4.53 us -> 29.1 us  [gathered(): other = [lax.ppermute(one, 't', pairs) for one in moved]]
    ppermute x4, starting transfers between devices: 0.01 us -> 21 us  [summed(): lax.ppermute(give, 't', pairs).astype(F32)]
    ppermute x16, starting transfers between devices: 49 us -> 35.3 us  [turned(): moved.append(lax.ppermute(pick(parts, send_by ^ mask), ('s', 't'), pairs))]
    all_to_all x32, waiting for transfers between devices: 295 us -> 306 us  [exchange(): lax.all_to_all(pieces, WIDE, split_axis=0, concat_axis=0, tiled=True)]
    ppermute x12, waiting for transfers between devices: 43.3 us -> 34.1 us  [scattered(): moved.append(lax.ppermute(value, 's', pairs))]
  transfers between devices with their start and end apart: 68 -> 68, of which waited for: 48 -> 47; matrix products, arithmetic and copies ran while one was open for 8% -> 13% of each run, Pallas kernels for 0% -> 0%
where the time goes in v7:
time: 834 us; the launch traced here: 821 us
  waiting for transfers between devices  419 us (50%)
  starting transfers between devices  215 us (26%)
  local copies, waits for them, and re-layouts  84.9 us (10%)
  matrix products  73.7 us (9%)
  other arithmetic  25.5 us (3%)
    all_to_all x32, waiting for transfers between devices, exchange(): lax.all_to_all(pieces, WIDE, split_axis=0, concat_axis=0, tiled=True)  306 us
    all_to_all x32, starting transfers between devices, exchange(): lax.all_to_all(pieces, WIDE, split_axis=0, concat_axis=0, tiled=True)  115 us
    ppermute x4, waiting for transfers between devices, gathered(): other = [lax.ppermute(one, 't', pairs) for one in moved]  49.9 us
    ppermute x16, starting transfers between devices, turned(): moved.append(lax.ppermute(pick(parts, send_by ^ mask), ('s', 't'), pairs))  35.3 us
    ppermute x12, waiting for transfers between devices, scattered(): moved.append(lax.ppermute(value, 's', pairs))  34.1 us
    ppermute x4, starting transfers between devices, gathered(): other = [lax.ppermute(one, 't', pairs) for one in moved]  29.1 us
    ppermute x16, waiting for transfers between devices, turned(): moved.append(lax.ppermute(pick(parts, send_by ^ mask), ('s', 't'), pairs))  28.9 us
    ppermute x4, starting transfers between devices, summed(): lax.ppermute(give, 't', pairs).astype(F32)  21 us
  transfers between devices with their start and end apart: 68, of which 47 were waited for; matrix products, arithmetic and copies ran while one was open for 13% of the time, Pallas kernels for 0%

profile of v7, /device:TPU:0, one launch (start us, length us, event | category | flops | bytes accessed | tf_op | source)
XLA Modules:
  0.0 820.8 jit_solution(9417311518988766091)
XLA Ops:
  16.5 8.6 %collective-permute-done.1 = bf16[4,128,128]{2,1,0:T(8,128)(2,1)S(1)} collective-permute-done((bf16[4,128,128]{2,1,0:T(8,128)(2,1)S(1)}, bf16[4,128,128]{2,1,0:T(8,128)(2,1)S(1)}, u32[]{:S(2)}, u32[]{:S(2)}) %collective-permute-start.1) | collective-permute-done | bytes 131104 | tf_op jit(solution)/shard_map/ppermute | solution.py:76
  40.5 20.3 %collective-permute-done.7 = bf16[2,2,4,128,128]{3,4,2,1,0:T(8,128)(2,1)} collective-permute-done((bf16[2,2,4,128,128]{3,4,2,1,0:T(8,128)(2,1)}, bf16[2,2,4,128,128]{3,4,2,1,0:T(8,128)(2,1)}, u32[]{:S(2)}, u32[]{:S(2)}) %collective-permute-start.7) | collective-permute-done | bytes 524320 | tf_op jit(solution)/shard_map/ppermute | solution.py:113
  84.1 11.4 %collective-permute-done.8 = bf16[2,2,4,128,128]{3,4,2,1,0:T(8,128)(2,1)S(1)} collective-permute-done((bf16[2,2,4,128,128]{3,4,2,1,0:T(8,128)(2,1)S(1)}, bf16[2,2,4,128,128]{3,4,2,1,0:T(8,128)(2,1)S(1)}, u32[]{:S(2)}, u32[]{:S(2)}) %collective-permute-start.8) | collective-permute-done | bytes 524320 | tf_op jit(solution)/shard_map/ppermute | solution.py:113
  98.4 61.7 %while.120 = (s32[]{:T(128)}, bf16[8,128,256]{2,1,0:T(8,128)(2,1)S(1)}, bf16[2,8,128,256]{3,2,1,0:T(8,128)(2,1)S(1)}, bf16[2,8,128,256]{3,1,2,0:T(8,128)(2,1)}, ...) while((s32[]{:T(128)}, bf16[8,128,256]{2,1,0:T(8,128)(2,1)S(1)}, ...), condition=%wide.region_1.2_spmd, body=%wide.region_0.1_spmd.sunk | while | flops 137363456 | bytes 15728829 | solution.py:167
  104.3 9.3 %all-to-all-done = bf16[16,8,8,256]{3,1,2,0:T(8,128)(2,1)S(1)} async-done(((bf16[16,8,8,256]{3,1,2,0:T(8,128)(2,1)}), bf16[16,8,8,256]{3,1,2,0:T(8,128)(2,1)S(1)}, u32[]{:S(2)}, u32[]{:S(2)}) %all-to-all-start) | async-done | bytes 524320 | tf_op jit(solution)/shard_map/while/body/eval_jaxpr/all_to_all | solution.py:27
  120.6 8.3 %all-to-all-done.1 = bf16[16,8,8,256]{3,1,2,0:T(8,128)(2,1)S(1)} async-done(((bf16[16,8,8,256]{3,1,2,0:T(8,128)(2,1)}), bf16[16,8,8,256]{3,1,2,0:T(8,128)(2,1)S(1)}, u32[]{:S(2)}, u32[]{:S(2)}) %all-to-all-start.1) | async-done | bytes 524320 | tf_op jit(solution)/shard_map/while/body/eval_jaxpr/all_to_all | solution.py:27
  135.1 9.2 %all-to-all-done = bf16[16,8,8,256]{3,1,2,0:T(8,128)(2,1)S(1)} async-done(((bf16[16,8,8,256]{3,1,2,0:T(8,128)(2,1)}), bf16[16,8,8,256]{3,1,2,0:T(8,128)(2,1)S(1)}, u32[]{:S(2)}, u32[]{:S(2)}) %all-to-all-start) | async-done | bytes 524320 | tf_op jit(solution)/shard_map/while/body/eval_jaxpr/all_to_all | solution.py:27
  151.3 8.3 %all-to-all-done.1 = bf16[16,8,8,256]{3,1,2,0:T(8,128)(2,1)S(1)} async-done(((bf16[16,8,8,256]{3,1,2,0:T(8,128)(2,1)}), bf16[16,8,8,256]{3,1,2,0:T(8,128)(2,1)S(1)}, u32[]{:S(2)}, u32[]{:S(2)}) %all-to-all-start.1) | async-done | bytes 524320 | tf_op jit(solution)/shard_map/while/body/eval_jaxpr/all_to_all | solution.py:27
  161.5 61.5 %while.121 = (s32[]{:T(128)}, bf16[8,128,256]{2,1,0:T(8,128)(2,1)S(1)}, bf16[2,8,128,256]{3,2,1,0:T(8,128)(2,1)S(1)}, bf16[2,8,128,256]{3,1,2,0:T(8,128)(2,1)}, ...) while((s32[]{:T(128)}, bf16[8,128,256]{2,1,0:T(8,128)(2,1)S(1)}, ...), condition=%wide.region_3.4_spmd, body=%wide.region_2.3_spmd.sunk | while | flops 137363456 | bytes 15728829 | solution.py:167
  167.2 9.2 %all-to-all-done.2 = bf16[16,8,8,256]{3,1,2,0:T(8,128)(2,1)S(1)} async-done(((bf16[16,8,8,256]{3,1,2,0:T(8,128)(2,1)}), bf16[16,8,8,256]{3,1,2,0:T(8,128)(2,1)S(1)}, u32[]{:S(2)}, u32[]{:S(2)}) %all-to-all-start.2) | async-done | bytes 524320 | tf_op jit(solution)/shard_map/while/body/eval_jaxpr/all_to_all | solution.py:27
  183.4 8.3 %all-to-all-done.3 = bf16[16,8,8,256]{3,1,2,0:T(8,128)(2,1)S(1)} async-done(((bf16[16,8,8,256]{3,1,2,0:T(8,128)(2,1)}), bf16[16,8,8,256]{3,1,2,0:T(8,128)(2,1)S(1)}, u32[]{:S(2)}, u32[]{:S(2)}) %all-to-all-start.3) | async-done | bytes 524320 | tf_op jit(solution)/shard_map/while/body/eval_jaxpr/all_to_all | solution.py:27
  198.0 9.2 %all-to-all-done.2 = bf16[16,8,8,256]{3,1,2,0:T(8,128)(2,1)S(1)} async-done(((bf16[16,8,8,256]{3,1,2,0:T(8,128)(2,1)}), bf16[16,8,8,256]{3,1,2,0:T(8,128)(2,1)S(1)}, u32[]{:S(2)}, u32[]{:S(2)}) %all-to-all-start.2) | async-done | bytes 524320 | tf_op jit(solution)/shard_map/while/body/eval_jaxpr/all_to_all | solution.py:27
  214.2 8.3 %all-to-all-done.3 = bf16[16,8,8,256]{3,1,2,0:T(8,128)(2,1)S(1)} async-done(((bf16[16,8,8,256]{3,1,2,0:T(8,128)(2,1)}), bf16[16,8,8,256]{3,1,2,0:T(8,128)(2,1)S(1)}, u32[]{:S(2)}, u32[]{:S(2)}) %all-to-all-start.3) | async-done | bytes 524320 | tf_op jit(solution)/shard_map/while/body/eval_jaxpr/all_to_all | solution.py:27
  238.4 22.8 %collective-permute-start.12 = (bf16[2,2,4,128,128]{3,4,2,1,0:T(8,128)(2,1)}, bf16[2,2,4,128,128]{3,4,2,1,0:T(8,128)(2,1)}, u32[]{:S(2)}, u32[]{:S(2)}) collective-permute-start(bf16[2,2,4,128,128]{3,4,2,1,0:T(8,128)(2,1)} %pad_maximum_fusion.8), channel_id=1, source_target_pairs={{0,4},{4,0},{1,5},{5,1},{2,6},{6,2},{3,7},{7,3},{8,12},{12,8},{9,1... | collective-permute-start | bytes 1572872 | tf_op jit(solution)/shard_map/ppermute | solution.py:113
  264.4 10.7 %collective-permute-done.17 = bf16[4,128,128]{2,1,0:T(8,128)(2,1)S(1)} collective-permute-done((bf16[4,128,128]{2,1,0:T(8,128)(2,1)S(1)}, bf16[4,128,128]{2,1,0:T(8,128)(2,1)S(1)}, u32[]{:S(2)}, u32[]{:S(2)}) %collective-permute-start.17) | collective-permute-done | bytes 131104 | tf_op jit(solution)/shard_map/ppermute | solution.py:76
  276.9 10.1 %collective-permute-done.13 = bf16[2,2,4,128,128]{3,4,2,1,0:T(8,128)(2,1)} collective-permute-done((bf16[2,2,4,128,128]{3,4,2,1,0:T(8,128)(2,1)}, bf16[2,2,4,128,128]{3,4,2,1,0:T(8,128)(2,1)}, u32[]{:S(2)}, u32[]{:S(2)}) %collective-permute-start.13) | collective-permute-done | bytes 524320 | tf_op jit(solution)/shard_map/ppermute | solution.py:113
  289.9 8.1 collective-permute-done.12
  302.0 61.5 %while.122 = (s32[]{:T(128)}, bf16[8,128,256]{2,1,0:T(8,128)(2,1)S(1)}, bf16[2,8,128,256]{3,2,1,0:T(8,128)(2,1)S(1)}, bf16[2,8,128,256]{3,1,2,0:T(8,128)(2,1)}, ...) while((s32[]{:T(128)}, bf16[8,128,256]{2,1,0:T(8,128)(2,1)S(1)}, ...), condition=%wide.region_5.6_spmd, body=%wide.region_4.5_spmd.sunk | while | flops 137363456 | bytes 15728829 | solution.py:167
  307.7 9.2 %all-to-all-done.4 = bf16[16,8,8,256]{3,1,2,0:T(8,128)(2,1)S(1)} async-done(((bf16[16,8,8,256]{3,1,2,0:T(8,128)(2,1)}), bf16[16,8,8,256]{3,1,2,0:T(8,128)(2,1)S(1)}, u32[]{:S(2)}, u32[]{:S(2)}) %all-to-all-start.4) | async-done | bytes 524320 | tf_op jit(solution)/shard_map/while/body/eval_jaxpr/all_to_all | solution.py:27
  323.9 8.3 %all-to-all-done.5 = bf16[16,8,8,256]{3,1,2,0:T(8,128)(2,1)S(1)} async-done(((bf16[16,8,8,256]{3,1,2,0:T(8,128)(2,1)}), bf16[16,8,8,256]{3,1,2,0:T(8,128)(2,1)S(1)}, u32[]{:S(2)}, u32[]{:S(2)}) %all-to-all-start.5) | async-done | bytes 524320 | tf_op jit(solution)/shard_map/while/body/eval_jaxpr/all_to_all | solution.py:27
  338.5 9.2 %all-to-all-done.4 = bf16[16,8,8,256]{3,1,2,0:T(8,128)(2,1)S(1)} async-done(((bf16[16,8,8,256]{3,1,2,0:T(8,128)(2,1)}), bf16[16,8,8,256]{3,1,2,0:T(8,128)(2,1)S(1)}, u32[]{:S(2)}, u32[]{:S(2)}) %all-to-all-start.4) | async-done | bytes 524320 | tf_op jit(solution)/shard_map/while/body/eval_jaxpr/all_to_all | solution.py:27
  354.7 8.3 %all-to-all-done.5 = bf16[16,8,8,256]{3,1,2,0:T(8,128)(2,1)S(1)} async-done(((bf16[16,8,8,256]{3,1,2,0:T(8,128)(2,1)}), bf16[16,8,8,256]{3,1,2,0:T(8,128)(2,1)S(1)}, u32[]{:S(2)}, u32[]{:S(2)}) %all-to-all-start.5) | async-done | bytes 524320 | tf_op jit(solution)/shard_map/while/body/eval_jaxpr/all_to_all | solution.py:27
  365.7 61.6 %while.123 = (s32[]{:T(128)}, bf16[8,128,256]{2,1,0:T(8,128)(2,1)S(1)}, bf16[2,8,128,256]{3,2,1,0:T(8,128)(2,1)}, bf16[2,8,128,256]{3,1,2,0:T(8,128)(2,1)}, bf16...) while((s32[]{:T(128)}, bf16[8,128,256]{2,1,0:T(8,128)(2,1)S(1)}, ...), condition=%wide.region_7.8_spmd, body=%wide.region_6.7_spmd.sunk | while | flops 137363456 | bytes 15728829 | solution.py:167
  371.5 9.2 %all-to-all-done.6 = bf16[16,8,8,256]{3,1,2,0:T(8,128)(2,1)S(1)} async-done(((bf16[16,8,8,256]{3,1,2,0:T(8,128)(2,1)}), bf16[16,8,8,256]{3,1,2,0:T(8,128)(2,1)S(1)}, u32[]{:S(2)}, u32[]{:S(2)}) %all-to-all-start.6) | async-done | bytes 524320 | tf_op jit(solution)/shard_map/while/body/eval_jaxpr/all_to_all | solution.py:27
  388.5 7.5 all-to-all-done.7
  402.3 9.2 %all-to-all-done.6 = bf16[16,8,8,256]{3,1,2,0:T(8,128)(2,1)S(1)} async-done(((bf16[16,8,8,256]{3,1,2,0:T(8,128)(2,1)}), bf16[16,8,8,256]{3,1,2,0:T(8,128)(2,1)S(1)}, u32[]{:S(2)}, u32[]{:S(2)}) %all-to-all-start.6) | async-done | bytes 524320 | tf_op jit(solution)/shard_map/while/body/eval_jaxpr/all_to_all | solution.py:27
  419.4 7.5 all-to-all-done.7
  439.5 66.1 %while.124 = (s32[]{:T(128)}, bf16[8,128,256]{2,1,0:T(8,128)(2,1)S(1)}, bf16[2,2,8,128,128]{4,3,2,1,0:T(8,128)(2,1)}, bf16[2,2,8,128,128]{4,3,2,1,0:T(8,128)(2,1...) while((s32[]{:T(128)}, ...), condition=%wide.region_9.10_spmd, body=%wide.region_8.9_spmd.sunk | while | flops 274726912 | bytes 22020356 | solution.py:182
  445.8 8.2 all-to-all-done.8
  460.4 8.8 %all-to-all-done.9 = bf16[16,8,8,256]{3,1,2,0:T(8,128)(2,1)S(1)} async-done(((bf16[16,8,8,256]{3,1,2,0:T(8,128)(2,1)}), bf16[16,8,8,256]{3,1,2,0:T(8,128)(2,1)S(1)}, u32[]{:S(2)}, u32[]{:S(2)}) %all-to-all-start.9) | async-done | bytes 524320 | tf_op jit(solution)/shard_map/while/body/eval_jaxpr/all_to_all | solution.py:27
  478.7 8.1 all-to-all-done.8
  493.1 8.8 %all-to-all-done.9 = bf16[16,8,8,256]{3,1,2,0:T(8,128)(2,1)S(1)} async-done(((bf16[16,8,8,256]{3,1,2,0:T(8,128)(2,1)}), bf16[16,8,8,256]{3,1,2,0:T(8,128)(2,1)S(1)}, u32[]{:S(2)}, u32[]{:S(2)}) %all-to-all-start.9) | async-done | bytes 524320 | tf_op jit(solution)/shard_map/while/body/eval_jaxpr/all_to_all | solution.py:27
  512.9 74.2 %while.125 = (s32[]{:T(128)}, bf16[8,128,256]{2,1,0:T(8,128)(2,1)S(1)}, bf16[2,2,8,128,128]{4,3,2,1,0:T(8,128)(2,1)}, bf16[2,2,8,128,128]{4,3,2,1,0:T(8,128)(2,1...) while((s32[]{:T(128)}, ...), condition=%wide.region_11.12_spmd, body=%wide.region_10.11_spmd.sunk | while | flops 274726912 | bytes 22020356 | solution.py:182
  518.7 18.9 %all-to-all-done.10 = bf16[16,8,8,256]{3,2,1,0:T(8,128)(2,1)S(1)} async-done(((bf16[16,8,8,256]{3,2,1,0:T(8,128)(2,1)}), bf16[16,8,8,256]{3,2,1,0:T(8,128)(2,1)S(1)}, u32[]{:S(2)}, u32[]{:S(2)}) %all-to-all-start.10) | async-done | bytes 524320 | tf_op jit(solution)/shard_map/while/body/eval_jaxpr/all_to_all | solution.py:27
  543.9 8.8 %all-to-all-done.11 = bf16[16,8,8,256]{3,1,2,0:T(8,128)(2,1)S(1)} async-done(((bf16[16,8,8,256]{3,1,2,0:T(8,128)(2,1)}), bf16[16,8,8,256]{3,1,2,0:T(8,128)(2,1)S(1)}, u32[]{:S(2)}, u32[]{:S(2)}) %all-to-all-start.11) | async-done | bytes 524320 | tf_op jit(solution)/shard_map/while/body/eval_jaxpr/all_to_all | solution.py:27
  561.2 8.1 all-to-all-done.10
  575.6 8.8 %all-to-all-done.11 = bf16[16,8,8,256]{3,1,2,0:T(8,128)(2,1)S(1)} async-done(((bf16[16,8,8,256]{3,1,2,0:T(8,128)(2,1)}), bf16[16,8,8,256]{3,1,2,0:T(8,128)(2,1)S(1)}, u32[]{:S(2)}, u32[]{:S(2)}) %all-to-all-start.11) | async-done | bytes 524320 | tf_op jit(solution)/shard_map/while/body/eval_jaxpr/all_to_all | solution.py:27
  596.5 74.1 %while.126 = (s32[]{:T(128)}, bf16[8,128,256]{2,1,0:T(8,128)(2,1)S(1)}, bf16[2,2,8,128,128]{4,3,2,1,0:T(8,128)(2,1)}, bf16[2,2,8,128,128]{4,3,2,1,0:T(8,128)(2,1...) while((s32[]{:T(128)}, ...), condition=%wide.region_13.14_spmd, body=%wide.region_12.13_spmd.sunk | while | flops 274726912 | bytes 22020356 | solution.py:182
  602.3 18.9 %all-to-all-done.12 = bf16[16,8,8,256]{3,2,1,0:T(8,128)(2,1)S(1)} async-done(((bf16[16,8,8,256]{3,2,1,0:T(8,128)(2,1)}), bf16[16,8,8,256]{3,2,1,0:T(8,128)(2,1)S(1)}, u32[]{:S(2)}, u32[]{:S(2)}) %all-to-all-start.12) | async-done | bytes 524320 | tf_op jit(solution)/shard_map/while/body/eval_jaxpr/all_to_all | solution.py:27
  627.5 8.8 %all-to-all-done.13 = bf16[16,8,8,256]{3,1,2,0:T(8,128)(2,1)S(1)} async-done(((bf16[16,8,8,256]{3,1,2,0:T(8,128)(2,1)}), bf16[16,8,8,256]{3,1,2,0:T(8,128)(2,1)S(1)}, u32[]{:S(2)}, u32[]{:S(2)}) %all-to-all-start.13) | async-done | bytes 524320 | tf_op jit(solution)/shard_map/while/body/eval_jaxpr/all_to_all | solution.py:27
  644.7 8.1 all-to-all-done.12
  659.2 8.8 %all-to-all-done.13 = bf16[16,8,8,256]{3,1,2,0:T(8,128)(2,1)S(1)} async-done(((bf16[16,8,8,256]{3,1,2,0:T(8,128)(2,1)}), bf16[16,8,8,256]{3,1,2,0:T(8,128)(2,1)S(1)}, u32[]{:S(2)}, u32[]{:S(2)}) %all-to-all-start.13) | async-done | bytes 524320 | tf_op jit(solution)/shard_map/while/body/eval_jaxpr/all_to_all | solution.py:27
  677.9 74.5 %while.127 = (s32[]{:T(128)}, bf16[8,128,256]{2,1,0:T(8,128)(2,1)S(1)}, bf16[2,2,8,128,128]{4,3,2,1,0:T(8,128)(2,1)}, bf16[2,2,8,128,128]{4,3,2,1,0:T(8,128)(2,1...) while((s32[]{:T(128)}, ...), condition=%wide.region_15.16_spmd, body=%wide.region_14.15_spmd.sunk | while | flops 274726912 | bytes 22020356 | solution.py:182
  683.9 18.9 %all-to-all-done.14 = bf16[16,8,8,256]{3,2,1,0:T(8,128)(2,1)S(1)} async-done(((bf16[16,8,8,256]{3,2,1,0:T(8,128)(2,1)}), bf16[16,8,8,256]{3,2,1,0:T(8,128)(2,1)S(1)}, u32[]{:S(2)}, u32[]{:S(2)}) %all-to-all-start.14) | async-done | bytes 524320 | tf_op jit(solution)/shard_map/while/body/eval_jaxpr/all_to_all | solution.py:27
  709.1 8.8 %all-to-all-done.15 = bf16[16,8,8,256]{3,1,2,0:T(8,128)(2,1)S(1)} async-done(((bf16[16,8,8,256]{3,1,2,0:T(8,128)(2,1)}), bf16[16,8,8,256]{3,1,2,0:T(8,128)(2,1)S(1)}, u32[]{:S(2)}, u32[]{:S(2)}) %all-to-all-start.15) | async-done | bytes 524320 | tf_op jit(solution)/shard_map/while/body/eval_jaxpr/all_to_all | solution.py:27
  726.4 8.1 all-to-all-done.14
  740.8 8.8 %all-to-all-done.15 = bf16[16,8,8,256]{3,1,2,0:T(8,128)(2,1)S(1)} async-done(((bf16[16,8,8,256]{3,1,2,0:T(8,128)(2,1)}), bf16[16,8,8,256]{3,1,2,0:T(8,128)(2,1)S(1)}, u32[]{:S(2)}, u32[]{:S(2)}) %all-to-all-start.15) | async-done | bytes 524320 | tf_op jit(solution)/shard_map/while/body/eval_jaxpr/all_to_all | solution.py:27
  767.6 18.0 %collective-permute-start.28 = (bf16[1,2,2,4,128,128]{5,4,3,2,1,0:T(8,128)(2,1)S(1)}, bf16[1,2,2,4,128,128]{5,4,3,2,1,0:T(8,128)(2,1)S(1)}, u32[]{:S(2)}, u32[]{:S(2)}) collective-permute-start(bf16[1,2,2,4,128,128]{5,4,3,2,1,0:T(8,128)(2,1)S(1)} %copy-done.20), channel_id=1, source_target_pairs={{0,4},{4,0},{1,5},{5,1},{2,6},{6,2},{3,7},{7,3},{8,12},{12,8},{9,1... | collective-permute-start | bytes 1572872 | tf_op jit(solution)/shard_map/ppermute | solution.py:130
  (389 shorter events, 401.6 us)
Async XLA Ops:
  4.0 29.6 %collective-permute-start.4 = (bf16[2,4,128,128]{2,3,1,0:T(8,128)(2,1)S(1)}, bf16[2,4,128,128]{2,3,1,0:T(8,128)(2,1)S(1)}, u32[]{:S(2)}, u32[]{:S(2)}) collective-permute-start(bf16[2,4,128,128]{2,3,1,0:T(8,128)(2,1)S(1)} %pad_maximum_fusion.16), channel_id=1, source_target_pairs={{0,8},{8,0},{16,24},{24,16},{1,9},{9,1},{17,25},{25,17},{2,10},{10... | collective-permute-start | bytes 786440 | tf_op jit(solution)/shard_map/ppermute | solution.py:104
  5.9 19.1 %collective-permute-start.1 = (bf16[4,128,128]{2,1,0:T(8,128)(2,1)S(1)}, bf16[4,128,128]{2,1,0:T(8,128)(2,1)S(1)}, u32[]{:S(2)}, u32[]{:S(2)}) collective-permute-start(bf16[4,128,128]{2,1,0:T(8,128)(2,1)S(1)} %get-tuple-element.939), channel_id=1, source_target_pairs={{0,8},{4,0},{8,24},{12,16},{16,12},{20,4},{24,28},{28,20},{1,9},{5... | collective-permute-start | bytes 393224 | tf_op jit(solution)/shard_map/ppermute | solution.py:76
  10.3 23.2 %collective-permute-start.5 = (bf16[2,4,128,128]{2,3,1,0:T(8,128)(2,1)S(1)}, bf16[2,4,128,128]{2,3,1,0:T(8,128)(2,1)S(1)}, u32[]{:S(2)}, u32[]{:S(2)}) collective-permute-start(bf16[2,4,128,128]{2,3,1,0:T(8,128)(2,1)S(1)} %pad_maximum_fusion.17), channel_id=1, source_target_pairs={{0,16},{8,24},{16,0},{24,8},{1,17},{9,25},{17,1},{25,9},{2,18},{10... | collective-permute-start | bytes 786440 | tf_op jit(solution)/shard_map/ppermute | solution.py:104
  13.5 20.1 %collective-permute-start.6 = (bf16[2,4,128,128]{2,3,1,0:T(8,128)(2,1)S(1)}, bf16[2,4,128,128]{2,3,1,0:T(8,128)(2,1)S(1)}, u32[]{:S(2)}, u32[]{:S(2)}) collective-permute-start(bf16[2,4,128,128]{2,3,1,0:T(8,128)(2,1)S(1)} %pad_maximum_fusion.18), channel_id=1, source_target_pairs={{0,24},{8,16},{16,8},{24,0},{1,25},{9,17},{17,9},{25,1},{2,26},{10... | collective-permute-start | bytes 786440 | tf_op jit(solution)/shard_map/ppermute | solution.py:104
  14.2 16.8 %collective-permute-start.2 = (bf16[4,128,128]{2,1,0:T(8,128)(2,1)}, bf16[4,128,128]{2,1,0:T(8,128)(2,1)S(1)}, u32[]{:S(2)}, u32[]{:S(2)}) collective-permute-start(bf16[4,128,128]{2,1,0:T(8,128)(2,1)} %get-tuple-element.938), channel_id=1, source_target_pairs={{0,16},{4,24},{8,0},{12,8},{16,20},{20,28},{24,4},{28,12},{1,17},{... | collective-permute-start | bytes 393224 | tf_op jit(solution)/shard_map/ppermute | solution.py:76
  35.3 25.5 %collective-permute-start.7 = (bf16[2,2,4,128,128]{3,4,2,1,0:T(8,128)(2,1)}, bf16[2,2,4,128,128]{3,4,2,1,0:T(8,128)(2,1)}, u32[]{:S(2)}, u32[]{:S(2)}) collective-permute-start(bf16[2,2,4,128,128]{3,4,2,1,0:T(8,128)(2,1)} %pad_maximum_fusion.6), channel_id=1, source_target_pairs={{0,4},{4,0},{1,5},{5,1},{2,6},{6,2},{3,7},{7,3},{8,12},{12,8},{9,1... | collective-permute-start | bytes 1572872 | tf_op jit(solution)/shard_map/ppermute | solution.py:113
  69.8 25.6 %collective-permute-start.8 = (bf16[2,2,4,128,128]{3,4,2,1,0:T(8,128)(2,1)S(1)}, bf16[2,2,4,128,128]{3,4,2,1,0:T(8,128)(2,1)S(1)}, u32[]{:S(2)}, u32[]{:S(2)}) collective-permute-start(bf16[2,2,4,128,128]{3,4,2,1,0:T(8,128)(2,1)S(1)} %pad_maximum_fusion.7), channel_id=1, source_target_pairs={{0,4},{4,0},{1,5},{5,1},{2,6},{6,2},{3,7},{7,3},{8,12},{12,8},{9,1... | collective-permute-start | bytes 1572872 | tf_op jit(solution)/shard_map/ppermute | solution.py:113
  100.6 13.0 %all-to-all-start = ((bf16[16,8,8,256]{3,1,2,0:T(8,128)(2,1)}), bf16[16,8,8,256]{3,1,2,0:T(8,128)(2,1)S(1)}, u32[]{:S(2)}, u32[]{:S(2)}) async-start(bf16[16,8,8,256]{3,1,2,0:T(8,128)(2,1)} %copy.349), calls=%async_computation | async-start | bytes 1048576 | tf_op jit(solution)/shard_map/while/body/eval_jaxpr/all_to_all | solution.py:27
  116.1 12.8 %all-to-all-start.1 = ((bf16[16,8,8,256]{3,1,2,0:T(8,128)(2,1)}), bf16[16,8,8,256]{3,1,2,0:T(8,128)(2,1)S(1)}, u32[]{:S(2)}, u32[]{:S(2)}) async-start(bf16[16,8,8,256]{3,1,2,0:T(8,128)(2,1)} %copy.350), calls=%async_computation.1 | async-start | bytes 1048576 | tf_op jit(solution)/shard_map/while/body/eval_jaxpr/all_to_all | solution.py:27
  131.5 12.8 %all-to-all-start = ((bf16[16,8,8,256]{3,1,2,0:T(8,128)(2,1)}), bf16[16,8,8,256]{3,1,2,0:T(8,128)(2,1)S(1)}, u32[]{:S(2)}, u32[]{:S(2)}) async-start(bf16[16,8,8,256]{3,1,2,0:T(8,128)(2,1)} %copy.349), calls=%async_computation | async-start | bytes 1048576 | tf_op jit(solution)/shard_map/while/body/eval_jaxpr/all_to_all | solution.py:27
  146.9 12.8 %all-to-all-start.1 = ((bf16[16,8,8,256]{3,1,2,0:T(8,128)(2,1)}), bf16[16,8,8,256]{3,1,2,0:T(8,128)(2,1)S(1)}, u32[]{:S(2)}, u32[]{:S(2)}) async-start(bf16[16,8,8,256]{3,1,2,0:T(8,128)(2,1)} %copy.350), calls=%async_computation.1 | async-start | bytes 1048576 | tf_op jit(solution)/shard_map/while/body/eval_jaxpr/all_to_all | solution.py:27
  163.6 12.8 %all-to-all-start.2 = ((bf16[16,8,8,256]{3,1,2,0:T(8,128)(2,1)}), bf16[16,8,8,256]{3,1,2,0:T(8,128)(2,1)S(1)}, u32[]{:S(2)}, u32[]{:S(2)}) async-start(bf16[16,8,8,256]{3,1,2,0:T(8,128)(2,1)} %copy.353), calls=%async_computation.2 | async-start | bytes 1048576 | tf_op jit(solution)/shard_map/while/body/eval_jaxpr/all_to_all | solution.py:27
  179.0 12.8 %all-to-all-start.3 = ((bf16[16,8,8,256]{3,1,2,0:T(8,128)(2,1)}), bf16[16,8,8,256]{3,1,2,0:T(8,128)(2,1)S(1)}, u32[]{:S(2)}, u32[]{:S(2)}) async-start(bf16[16,8,8,256]{3,1,2,0:T(8,128)(2,1)} %copy.354), calls=%async_computation.3 | async-start | bytes 1048576 | tf_op jit(solution)/shard_map/while/body/eval_jaxpr/all_to_all | solution.py:27
  194.4 12.8 %all-to-all-start.2 = ((bf16[16,8,8,256]{3,1,2,0:T(8,128)(2,1)}), bf16[16,8,8,256]{3,1,2,0:T(8,128)(2,1)S(1)}, u32[]{:S(2)}, u32[]{:S(2)}) async-start(bf16[16,8,8,256]{3,1,2,0:T(8,128)(2,1)} %copy.353), calls=%async_computation.2 | async-start | bytes 1048576 | tf_op jit(solution)/shard_map/while/body/eval_jaxpr/all_to_all | solution.py:27
  209.7 12.8 %all-to-all-start.3 = ((bf16[16,8,8,256]{3,1,2,0:T(8,128)(2,1)}), bf16[16,8,8,256]{3,1,2,0:T(8,128)(2,1)S(1)}, u32[]{:S(2)}, u32[]{:S(2)}) async-start(bf16[16,8,8,256]{3,1,2,0:T(8,128)(2,1)} %copy.354), calls=%async_computation.3 | async-start | bytes 1048576 | tf_op jit(solution)/shard_map/while/body/eval_jaxpr/all_to_all | solution.py:27
  224.6 13.8 %collective-permute-start.14 = (bf16[4,128,128]{2,1,0:T(8,128)(2,1)S(1)}, bf16[4,128,128]{2,1,0:T(8,128)(2,1)S(1)}, u32[]{:S(2)}, u32[]{:S(2)}) collective-permute-start(bf16[4,128,128]{2,1,0:T(8,128)(2,1)S(1)} %get-tuple-element.912), channel_id=1, source_target_pairs={{0,0},{4,8},{8,16},{12,24},{16,4},{20,12},{24,20},{28,28},{1,1},{5... | collective-permute-start | bytes 393224 | tf_op jit(solution)/shard_map/ppermute | solution.py:76
  225.2 39.2 %collective-permute-start.15 = (bf16[4,128,128]{2,1,0:T(8,128)(2,1)S(1)}, bf16[4,128,128]{2,1,0:T(8,128)(2,1)S(1)}, u32[]{:S(2)}, u32[]{:S(2)}) collective-permute-start(bf16[4,128,128]{2,1,0:T(8,128)(2,1)S(1)} %get-tuple-element.915), channel_id=1, source_target_pairs={{0,8},{4,0},{8,24},{12,16},{16,12},{20,4},{24,28},{28,20},{1,9},{5... | collective-permute-start | bytes 393224 | tf_op jit(solution)/shard_map/ppermute | solution.py:76
  228.2 36.2 %collective-permute-start.16 = (bf16[4,128,128]{2,1,0:T(8,128)(2,1)S(1)}, bf16[4,128,128]{2,1,0:T(8,128)(2,1)S(1)}, u32[]{:S(2)}, u32[]{:S(2)}) collective-permute-start(bf16[4,128,128]{2,1,0:T(8,128)(2,1)S(1)} %get-tuple-element.914), channel_id=1, source_target_pairs={{0,16},{4,24},{8,0},{12,8},{16,20},{20,28},{24,4},{28,12},{1,17},{... | collective-permute-start | bytes 393224 | tf_op jit(solution)/shard_map/ppermute | solution.py:76
  230.8 44.4 %collective-permute-start.17 = (bf16[4,128,128]{2,1,0:T(8,128)(2,1)S(1)}, bf16[4,128,128]{2,1,0:T(8,128)(2,1)S(1)}, u32[]{:S(2)}, u32[]{:S(2)}) collective-permute-start(bf16[4,128,128]{2,1,0:T(8,128)(2,1)S(1)} %get-tuple-element.913), channel_id=1, source_target_pairs={{0,24},{4,16},{8,8},{12,0},{16,28},{20,20},{24,12},{28,4},{1,25},{... | collective-permute-start | bytes 393224 | tf_op jit(solution)/shard_map/ppermute | solution.py:76
  234.7 52.3 %collective-permute-start.13 = (bf16[2,2,4,128,128]{3,4,2,1,0:T(8,128)(2,1)}, bf16[2,2,4,128,128]{3,4,2,1,0:T(8,128)(2,1)}, u32[]{:S(2)}, u32[]{:S(2)}) collective-permute-start(bf16[2,2,4,128,128]{3,4,2,1,0:T(8,128)(2,1)} %pad_maximum_fusion.9), channel_id=1, source_target_pairs={{0,4},{4,0},{1,5},{5,1},{2,6},{6,2},{3,7},{7,3},{8,12},{12,8},{9,1... | collective-permute-start | bytes 1572872 | tf_op jit(solution)/shard_map/ppermute | solution.py:113
  238.4 59.6 %collective-permute-start.12 = (bf16[2,2,4,128,128]{3,4,2,1,0:T(8,128)(2,1)}, bf16[2,2,4,128,128]{3,4,2,1,0:T(8,128)(2,1)}, u32[]{:S(2)}, u32[]{:S(2)}) collective-permute-start(bf16[2,2,4,128,128]{3,4,2,1,0:T(8,128)(2,1)} %pad_maximum_fusion.8), channel_id=1, source_target_pairs={{0,4},{4,0},{1,5},{5,1},{2,6},{6,2},{3,7},{7,3},{8,12},{12,8},{9,1... | collective-permute-start | bytes 1572872 | tf_op jit(solution)/shard_map/ppermute | solution.py:113
  304.1 12.8 %all-to-all-start.4 = ((bf16[16,8,8,256]{3,1,2,0:T(8,128)(2,1)}), bf16[16,8,8,256]{3,1,2,0:T(8,128)(2,1)S(1)}, u32[]{:S(2)}, u32[]{:S(2)}) async-start(bf16[16,8,8,256]{3,1,2,0:T(8,128)(2,1)} %copy.357), calls=%async_computation.4 | async-start | bytes 1048576 | tf_op jit(solution)/shard_map/while/body/eval_jaxpr/all_to_all | solution.py:27
  319.5 12.8 %all-to-all-start.5 = ((bf16[16,8,8,256]{3,1,2,0:T(8,128)(2,1)}), bf16[16,8,8,256]{3,1,2,0:T(8,128)(2,1)S(1)}, u32[]{:S(2)}, u32[]{:S(2)}) async-start(bf16[16,8,8,256]{3,1,2,0:T(8,128)(2,1)} %copy.358), calls=%async_computation.5 | async-start | bytes 1048576 | tf_op jit(solution)/shard_map/while/body/eval_jaxpr/all_to_all | solution.py:27
  334.9 12.8 %all-to-all-start.4 = ((bf16[16,8,8,256]{3,1,2,0:T(8,128)(2,1)}), bf16[16,8,8,256]{3,1,2,0:T(8,128)(2,1)S(1)}, u32[]{:S(2)}, u32[]{:S(2)}) async-start(bf16[16,8,8,256]{3,1,2,0:T(8,128)(2,1)} %copy.357), calls=%async_computation.4 | async-start | bytes 1048576 | tf_op jit(solution)/shard_map/while/body/eval_jaxpr/all_to_all | solution.py:27
  350.2 12.8 %all-to-all-start.5 = ((bf16[16,8,8,256]{3,1,2,0:T(8,128)(2,1)}), bf16[16,8,8,256]{3,1,2,0:T(8,128)(2,1)S(1)}, u32[]{:S(2)}, u32[]{:S(2)}) async-start(bf16[16,8,8,256]{3,1,2,0:T(8,128)(2,1)} %copy.358), calls=%async_computation.5 | async-start | bytes 1048576 | tf_op jit(solution)/shard_map/while/body/eval_jaxpr/all_to_all | solution.py:27
  367.9 12.8 %all-to-all-start.6 = ((bf16[16,8,8,256]{3,1,2,0:T(8,128)(2,1)}), bf16[16,8,8,256]{3,1,2,0:T(8,128)(2,1)S(1)}, u32[]{:S(2)}, u32[]{:S(2)}) async-start(bf16[16,8,8,256]{3,1,2,0:T(8,128)(2,1)} %copy.361), calls=%async_computation.6 | async-start | bytes 1048576 | tf_op jit(solution)/shard_map/while/body/eval_jaxpr/all_to_all | solution.py:27
  383.3 12.8 %all-to-all-start.7 = ((bf16[16,8,8,256]{3,1,2,0:T(8,128)(2,1)}), bf16[16,8,8,256]{3,1,2,0:T(8,128)(2,1)S(1)}, u32[]{:S(2)}, u32[]{:S(2)}) async-start(bf16[16,8,8,256]{3,1,2,0:T(8,128)(2,1)} %copy.362), calls=%async_computation.7 | async-start | bytes 1048576 | tf_op jit(solution)/shard_map/while/body/eval_jaxpr/all_to_all | solution.py:27
  398.7 12.8 %all-to-all-start.6 = ((bf16[16,8,8,256]{3,1,2,0:T(8,128)(2,1)}), bf16[16,8,8,256]{3,1,2,0:T(8,128)(2,1)S(1)}, u32[]{:S(2)}, u32[]{:S(2)}) async-start(bf16[16,8,8,256]{3,1,2,0:T(8,128)(2,1)} %copy.361), calls=%async_computation.6 | async-start | bytes 1048576 | tf_op jit(solution)/shard_map/while/body/eval_jaxpr/all_to_all | solution.py:27
  429.0 80.6 %collective-permute-start.18 = (bf16[4,128,128]{2,1,0:T(8,128)(2,1)}, bf16[4,128,128]{2,1,0:T(8,128)(2,1)}, u32[]{:S(2)}, u32[]{:S(2)}) collective-permute-start(bf16[4,128,128]{2,1,0:T(8,128)(2,1)} %get-tuple-element.904), channel_id=1, source_target_pairs={{0,0},{4,16},{8,4},{12,20},{16,8},{20,24},{24,12},{28,28},{1,1},{5... | collective-permute-start | bytes 393224 | tf_op jit(solution)/shard_map/ppermute | solution.py:76
  431.2 78.4 %collective-permute-start.19 = (bf16[4,128,128]{2,1,0:T(8,128)(2,1)}, bf16[4,128,128]{2,1,0:T(8,128)(2,1)}, u32[]{:S(2)}, u32[]{:S(2)}) collective-permute-start(bf16[4,128,128]{2,1,0:T(8,128)(2,1)} %get-tuple-element.907), channel_id=1, source_target_pairs={{0,4},{4,20},{8,0},{12,16},{16,12},{20,28},{24,8},{28,24},{1,5},{5... | collective-permute-start | bytes 393224 | tf_op jit(solution)/shard_map/ppermute | solution.py:76
  434.8 74.8 %collective-permute-start.20 = (bf16[4,128,128]{2,1,0:T(8,128)(2,1)}, bf16[4,128,128]{2,1,0:T(8,128)(2,1)}, u32[]{:S(2)}, u32[]{:S(2)}) collective-permute-start(bf16[4,128,128]{2,1,0:T(8,128)(2,1)} %get-tuple-element.906), channel_id=1, source_target_pairs={{0,8},{4,24},{8,12},{12,28},{16,0},{20,16},{24,4},{28,20},{1,9},{5... | collective-permute-start | bytes 393224 | tf_op jit(solution)/shard_map/ppermute | solution.py:76
  434.8 74.8 %collective-permute-start.21 = (bf16[4,128,128]{2,1,0:T(8,128)(2,1)S(1)}, bf16[4,128,128]{2,1,0:T(8,128)(2,1)}, u32[]{:S(2)}, u32[]{:S(2)}) collective-permute-start(bf16[4,128,128]{2,1,0:T(8,128)(2,1)S(1)} %get-tuple-element.905), channel_id=1, source_target_pairs={{0,12},{4,28},{8,8},{12,24},{16,4},{20,20},{24,0},{28,16},{1,13},{... | collective-permute-start | bytes 393224 | tf_op jit(solution)/shard_map/ppermute | solution.py:76
  440.6 13.5 %all-to-all-start.8 = ((bf16[16,8,8,256]{3,2,1,0:T(8,128)(2,1)}), bf16[16,8,8,256]{3,2,1,0:T(8,128)(2,1)S(1)}, u32[]{:S(2)}, u32[]{:S(2)}) async-start(bf16[16,8,8,256]{3,2,1,0:T(8,128)(2,1)} %bitcast.680), calls=%async_computation.8 | async-start | bytes 1048576 | tf_op jit(solution)/shard_map/while/body/eval_jaxpr/all_to_all | solution.py:27
  456.4 12.8 %all-to-all-start.9 = ((bf16[16,8,8,256]{3,1,2,0:T(8,128)(2,1)}), bf16[16,8,8,256]{3,1,2,0:T(8,128)(2,1)S(1)}, u32[]{:S(2)}, u32[]{:S(2)}) async-start(bf16[16,8,8,256]{3,1,2,0:T(8,128)(2,1)} %copy.370), calls=%async_computation.9 | async-start | bytes 1048576 | tf_op jit(solution)/shard_map/while/body/eval_jaxpr/all_to_all | solution.py:27
  489.1 12.8 %all-to-all-start.9 = ((bf16[16,8,8,256]{3,1,2,0:T(8,128)(2,1)}), bf16[16,8,8,256]{3,1,2,0:T(8,128)(2,1)S(1)}, u32[]{:S(2)}, u32[]{:S(2)}) async-start(bf16[16,8,8,256]{3,1,2,0:T(8,128)(2,1)} %copy.370), calls=%async_computation.9 | async-start | bytes 1048576 | tf_op jit(solution)/shard_map/while/body/eval_jaxpr/all_to_all | solution.py:27
  508.7 84.7 %collective-permute-start.22 = (bf16[1,2,2,4,128,128]{5,4,3,2,1,0:T(8,128)(2,1)}, bf16[1,2,2,4,128,128]{5,4,3,2,1,0:T(8,128)(2,1)}, u32[]{:S(2)}, u32[]{:S(2)}) collective-permute-start(bf16[1,2,2,4,128,128]{5,4,3,2,1,0:T(8,128)(2,1)} %dynamic-slice_bitcast_fusion.35), channel_id=1, source_target_pairs={{0,4},{4,0},{1,5},{5,1},{2,6},{6,2},{3,7},{7,3},{8,12},{12,8},{9,1... | collective-permute-start | bytes 1572872 | tf_op jit(solution)/shard_map/ppermute | solution.py:130
  514.0 23.6 %all-to-all-start.10 = ((bf16[16,8,8,256]{3,2,1,0:T(8,128)(2,1)}), bf16[16,8,8,256]{3,2,1,0:T(8,128)(2,1)S(1)}, u32[]{:S(2)}, u32[]{:S(2)}) async-start(bf16[16,8,8,256]{3,2,1,0:T(8,128)(2,1)} %bitcast.698), calls=%async_computation.10 | async-start | bytes 1048576 | tf_op jit(solution)/shard_map/while/body/eval_jaxpr/all_to_all | solution.py:27
  539.9 12.8 %all-to-all-start.11 = ((bf16[16,8,8,256]{3,1,2,0:T(8,128)(2,1)}), bf16[16,8,8,256]{3,1,2,0:T(8,128)(2,1)S(1)}, u32[]{:S(2)}, u32[]{:S(2)}) async-start(bf16[16,8,8,256]{3,1,2,0:T(8,128)(2,1)} %copy.378), calls=%async_computation.11 | async-start | bytes 1048576 | tf_op jit(solution)/shard_map/while/body/eval_jaxpr/all_to_all | solution.py:27
  556.5 12.8 %all-to-all-start.10 = ((bf16[16,8,8,256]{3,2,1,0:T(8,128)(2,1)}), bf16[16,8,8,256]{3,2,1,0:T(8,128)(2,1)S(1)}, u32[]{:S(2)}, u32[]{:S(2)}) async-start(bf16[16,8,8,256]{3,2,1,0:T(8,128)(2,1)} %bitcast.698), calls=%async_computation.10 | async-start | bytes 1048576 | tf_op jit(solution)/shard_map/while/body/eval_jaxpr/all_to_all | solution.py:27
  571.6 12.8 %all-to-all-start.11 = ((bf16[16,8,8,256]{3,1,2,0:T(8,128)(2,1)}), bf16[16,8,8,256]{3,1,2,0:T(8,128)(2,1)S(1)}, u32[]{:S(2)}, u32[]{:S(2)}) async-start(bf16[16,8,8,256]{3,1,2,0:T(8,128)(2,1)} %copy.378), calls=%async_computation.11 | async-start | bytes 1048576 | tf_op jit(solution)/shard_map/while/body/eval_jaxpr/all_to_all | solution.py:27
  592.2 82.3 %collective-permute-start.23 = (bf16[1,2,2,4,128,128]{5,4,3,2,1,0:T(8,128)(2,1)}, bf16[1,2,2,4,128,128]{5,4,3,2,1,0:T(8,128)(2,1)}, u32[]{:S(2)}, u32[]{:S(2)}) collective-permute-start(bf16[1,2,2,4,128,128]{5,4,3,2,1,0:T(8,128)(2,1)} %dynamic-slice_bitcast_fusion.34), channel_id=1, source_target_pairs={{0,4},{4,0},{1,5},{5,1},{2,6},{6,2},{3,7},{7,3},{8,12},{12,8},{9,1... | collective-permute-start | bytes 1572872 | tf_op jit(solution)/shard_map/ppermute | solution.py:130
  597.6 23.6 %all-to-all-start.12 = ((bf16[16,8,8,256]{3,2,1,0:T(8,128)(2,1)}), bf16[16,8,8,256]{3,2,1,0:T(8,128)(2,1)S(1)}, u32[]{:S(2)}, u32[]{:S(2)}) async-start(bf16[16,8,8,256]{3,2,1,0:T(8,128)(2,1)} %bitcast.716), calls=%async_computation.12 | async-start | bytes 1048576 | tf_op jit(solution)/shard_map/while/body/eval_jaxpr/all_to_all | solution.py:27
  673.6 127.6 %collective-permute-start.29 = (bf16[1,2,2,4,128,128]{5,4,3,2,1,0:T(8,128)(2,1)}, bf16[1,2,2,4,128,128]{5,4,3,2,1,0:T(8,128)(2,1)}, u32[]{:S(2)}, u32[]{:S(2)}) collective-permute-start(bf16[1,2,2,4,128,128]{5,4,3,2,1,0:T(8,128)(2,1)} %dynamic-slice_bitcast_fusion.32), channel_id=1, source_target_pairs={{0,4},{4,0},{1,5},{5,1},{2,6},{6,2},{3,7},{7,3},{8,12},{12,8},{9,1... | collective-permute-start | bytes 1572872 | tf_op jit(solution)/shard_map/ppermute | solution.py:130
  679.2 23.6 %all-to-all-start.14 = ((bf16[16,8,8,256]{3,2,1,0:T(8,128)(2,1)}), bf16[16,8,8,256]{3,2,1,0:T(8,128)(2,1)S(1)}, u32[]{:S(2)}, u32[]{:S(2)}) async-start(bf16[16,8,8,256]{3,2,1,0:T(8,128)(2,1)} %bitcast.734), calls=%async_computation.14 | async-start | bytes 1048576 | tf_op jit(solution)/shard_map/while/body/eval_jaxpr/all_to_all | solution.py:27
  759.7 25.8 %collective-permute-start.25 = (bf16[4,128,128]{2,1,0:T(8,128)(2,1)S(1)}, bf16[4,128,128]{2,1,0:T(8,128)(2,1)S(1)}, u32[]{:S(2)}, u32[]{:S(2)}) collective-permute-start(bf16[4,128,128]{2,1,0:T(8,128)(2,1)S(1)} %get-tuple-element.899), channel_id=1, source_target_pairs={{0,4},{4,20},{8,0},{12,16},{16,12},{20,28},{24,8},{28,24},{1,5},{5... | collective-permute-start | bytes 393224 | tf_op jit(solution)/shard_map/ppermute | solution.py:76
  764.9 20.7 %collective-permute-start.26 = (bf16[4,128,128]{2,1,0:T(8,128)(2,1)S(1)}, bf16[4,128,128]{2,1,0:T(8,128)(2,1)S(1)}, u32[]{:S(2)}, u32[]{:S(2)}) collective-permute-start(bf16[4,128,128]{2,1,0:T(8,128)(2,1)S(1)} %get-tuple-element.898), channel_id=1, source_target_pairs={{0,8},{4,24},{8,12},{12,28},{16,0},{20,16},{24,4},{28,20},{1,9},{5... | collective-permute-start | bytes 393224 | tf_op jit(solution)/shard_map/ppermute | solution.py:76
  764.9 23.3 %collective-permute-start.27 = (bf16[4,128,128]{2,1,0:T(8,128)(2,1)S(1)}, bf16[4,128,128]{2,1,0:T(8,128)(2,1)S(1)}, u32[]{:S(2)}, u32[]{:S(2)}) collective-permute-start(bf16[4,128,128]{2,1,0:T(8,128)(2,1)S(1)} %get-tuple-element.897), channel_id=1, source_target_pairs={{0,12},{4,28},{8,8},{12,24},{16,4},{20,20},{24,0},{28,16},{1,13},{... | collective-permute-start | bytes 393224 | tf_op jit(solution)/shard_map/ppermute | solution.py:76
  767.6 34.7 %collective-permute-start.28 = (bf16[1,2,2,4,128,128]{5,4,3,2,1,0:T(8,128)(2,1)S(1)}, bf16[1,2,2,4,128,128]{5,4,3,2,1,0:T(8,128)(2,1)S(1)}, u32[]{:S(2)}, u32[]{:S(2)}) collective-permute-start(bf16[1,2,2,4,128,128]{5,4,3,2,1,0:T(8,128)(2,1)S(1)} %copy-done.20), channel_id=1, source_target_pairs={{0,4},{4,0},{1,5},{5,1},{2,6},{6,2},{3,7},{7,3},{8,12},{12,8},{9,1... | collective-permute-start | bytes 1572872 | tf_op jit(solution)/shard_map/ppermute | solution.py:130
  (49 other events, 415.9 us)

commit v8 on v7

--- a/solution.py
+++ b/solution.py
@@ -6,7 +6,7 @@
 F32 = jnp.float32
 BF16 = jnp.bfloat16
 WIDE = ("s", "x")
-GROUPS = 2
+GROUPS = 4
 STRETCH = 2
 
 
@@ -106,36 +106,15 @@
         return [pick(moved, s_index ^ section) for section in range(sections)]
 
     def gathered(part):
-        moved = [part]
-        step = 1
-        while step < groups:
-            pairs = [(t, t ^ step) for t in range(groups)]
-            other = [lax.ppermute(one, "t", pairs) for one in moved]
-            low = (t_index // step) % 2 == 0
-            moved = [jnp.where(low, x, y) for x, y in zip(moved, other)] + [
-                jnp.where(low, y, x) for x, y in zip(moved, other)
-            ]
-            step *= 2
-        return jnp.concatenate(moved, axis=2)
+        part = jnp.einsum("aj,lfbjk,ck->lfbac", order, part, order, preferred_element_type=F32).astype(BF16)
+        full = lax.all_gather(part, "t", axis=0, tiled=False)
+        return full.transpose(1, 2, 0, 3, 4, 5).reshape(part.shape[:2] + (own, size, size))
 
     def summed(terms):
         parts = terms.reshape(terms.shape[:2] + (groups, sub, size, size)).transpose(2, 0, 1, 3, 4, 5)
-        step = 1
-        while step < groups:
-            pairs = [(t, t ^ step) for t in range(groups)]
-            parts = parts.reshape((parts.shape[0] // 2, 2) + parts.shape[1:])
-            bit = (t_index // step) % 2
-            keep = lax.dynamic_index_in_dim(parts, bit, 1, keepdims=False)
-            give = lax.dynamic_index_in_dim(parts, 1 - bit, 1, keepdims=False)
-            parts = (keep.astype(F32) + lax.ppermute(give, "t", pairs).astype(F32)).astype(BF16)
-            step *= 2
-        return parts[0]
-
-    def ordered(factors):
-        return jnp.einsum("aj,lfbjk,ck->lfbac", order, factors, order, preferred_element_type=F32).astype(BF16)
-
-    def unordered(terms):
-        return jnp.einsum("aj,lfbac,ck->lfbjk", order, terms, order, preferred_element_type=F32).astype(BF16)
+        total = lax.psum_scatter(parts.reshape(-1, size, size), "t", scatter_dimension=0, tiled=True)
+        total = total.reshape(terms.shape[:2] + (sub, size, size))
+        return jnp.einsum("aj,lfbac,ck->lfbjk", order, total, order, preferred_element_type=F32).astype(BF16)
 
     stretches = layers // STRETCH
     per_loop = stretches // loops
@@ -149,7 +128,7 @@
     arrived = scattered(rights[0], lefts[0])
     parts = [part_of(arrived, stretch) for stretch in range(per_loop)]
     current = enter(inputs)
-    weights = [ordered(gathered(parts[0]))]
+    weights = [gathered(parts[0])]
     later = (parts[1:], rights[1:], lefts[1:], cotangent)
     current, weights[0], later = lax.optimization_barrier((current, weights[0], later))
     parts[1:], rights, lefts, cotangent = later
@@ -167,7 +146,7 @@
         current, saved = lax.scan(forward_layer, current, weights[stretch])
         stored.append(saved)
         if coming is not None:
-            weights.append(ordered(coming))
+            weights.append(coming)
     current, grad = lax.optimization_barrier((current, grad))
 
     def returned(loop):
@@ -187,7 +166,7 @@
                 sums[stretch + 2] = two_ago
             else:
                 outputs = two_ago
-        sums[stretch] = summed(unordered(terms))
+        sums[stretch] = summed(terms)
         loop = (stretch + 2) // per_loop
         if (stretch + 2) % per_loop == 0 and 0 < loop < loops:
             halves[loop] = returned(loop)

time: 834 us -> 844 us (1.012)
  starting transfers between devices: 215 us -> 169 us
  waiting for transfers between devices: 419 us -> 451 us
  local copies, waits for them, and re-layouts: 84.9 us -> 108 us
  other arithmetic: 25.5 us -> 9.61 us
  between operations: 1.86 us -> 15.4 us
    all_gather x0 -> x4, waiting for transfers between devices: none -> 53 us  [gathered(): full = lax.all_gather(part, 't', axis=0, tiled=False)]
    ppermute x8 -> x0, starting transfers between devices: 50 us -> none  [the longest x4 29.1 us: gathered(): other = [lax.ppermute(one, 't', pairs) for one in moved]]
    ppermute x8 -> x0, waiting for transfers between devices: 49.9 us -> none  [the longest x4 49.9 us: gathered(): other = [lax.ppermute(one, 't', pairs) for one in moved]]
    all_to_all x32, waiting for transfers between devices: 306 us -> 273 us  [exchange(): lax.all_to_all(pieces, WIDE, split_axis=0, concat_axis=0, tiled=True)]
    ppermute x16, waiting for transfers between devices: 28.9 us -> 61.3 us  [turned(): moved.append(lax.ppermute(pick(parts, send_by ^ mask), ('s', 't'), pairs))]
    transpose x2 -> x24, local copies, waits for them, and re-layouts: 0.56 us -> 26.7 us  [the longest x4 12.7 us: summed(): terms.reshape(terms.shape[:2] + (groups, sub, size, size))]
    reduce_scatter x0 -> x4, waiting for transfers between devices: none -> 23 us  [summed(): lax.psum_scatter(parts.reshape(-1, size, size), 't', scatter_dimension=0,...]
    ppermute x16, starting transfers between devices: 35.3 us -> 13.2 us  [turned(): moved.append(lax.ppermute(pick(parts, send_by ^ mask), ('s', 't'), pairs))]
  transfers between devices with their start and end apart: 68 -> 68, of which waited for: 47 -> 49; matrix products, arithmetic and copies ran while one was open for 13% -> 15% of each run, Pallas kernels for 0% -> 0%
where the time goes in v8:
time: 844 us; the launch traced here: 830 us
  waiting for transfers between devices  451 us (53%)
  starting transfers between devices  169 us (20%)
  local copies, waits for them, and re-layouts  108 us (13%)
  matrix products  76.5 us (9%)
  between operations  15.4 us (2%)
  other arithmetic  9.61 us (1%)
    all_to_all x32, waiting for transfers between devices, exchange(): lax.all_to_all(pieces, WIDE, split_axis=0, concat_axis=0, tiled=True)  273 us
    all_to_all x32, starting transfers between devices, exchange(): lax.all_to_all(pieces, WIDE, split_axis=0, concat_axis=0, tiled=True)  133 us
    ppermute x16, waiting for transfers between devices, turned(): moved.append(lax.ppermute(pick(parts, send_by ^ mask), ('s', 't'), pairs))  61.3 us
    all_gather x4, waiting for transfers between devices, gathered(): full = lax.all_gather(part, 't', axis=0, tiled=False)  53 us
    ppermute x12, waiting for transfers between devices, scattered(): moved.append(lax.ppermute(value, 's', pairs))  40 us
    ppermute x12, starting transfers between devices, scattered(): moved.append(lax.ppermute(value, 's', pairs))  23.1 us
    reduce_scatter x4, waiting for transfers between devices, summed(): lax.psum_scatter(parts.reshape(-1, size, size), 't', scatter_dimension=0,...  23 us
    reshape x24, local copies, waits for them, and re-layouts, exchange(): pieces = values.transpose(1, 0, 2).reshape(full // own, own, own, rows)  20 us
  transfers between devices with their start and end apart: 68, of which 49 were waited for; matrix products, arithmetic and copies ran while one was open for 15% of the time, Pallas kernels for 0%

profile of v8, /device:TPU:0, one launch (start us, length us, event | category | flops | bytes accessed | tf_op | source)
XLA Modules:
  0.0 830.4 jit_solution(11971860850801415003)
XLA Ops:
  36.3 27.2 %collective-permute-done.2 = bf16[4,128,128]{1,2,0:T(8,128)(2,1)S(1)} collective-permute-done((bf16[4,128,128]{1,2,0:T(8,128)(2,1)S(1)}, bf16[4,128,128]{1,2,0:T(8,128)(2,1)S(1)}, u32[]{:S(2)}, u32[]{:S(2)}) %collective-permute-start.2) | collective-permute-done | bytes 131104 | tf_op jit(solution)/shard_map/ppermute | solution.py:76
  64.2 24.3 %all-gather.9.cloned.1.call-done = bf16[8,2,4,128,128]{4,3,2,1,0:T(8,128)(2,1)} async-done(((bf16[2,2,4,128,128]{4,3,2,1,0:T(8,128)(2,1)}), bf16[8,2,4,128,128]{4,3,2,1,0:T(8,128)(2,1)}) %all-gather.9.cloned.1.call-update) | async-done | bytes 2097168 | tf_op jit(solution)/shard_map/all_gather | solution.py:110
  111.4 28.7 %all-gather.11.cloned.1.call-done = bf16[8,2,4,128,128]{4,3,2,1,0:T(8,128)(2,1)} async-done(((bf16[2,2,4,128,128]{4,3,2,1,0:T(8,128)(2,1)}), bf16[8,2,4,128,128]{4,3,2,1,0:T(8,128)(2,1)}) %all-gather.11.cloned.1.call-update) | async-done | bytes 2097168 | tf_op jit(solution)/shard_map/all_gather | solution.py:110
  144.6 61.7 %while.120 = (s32[]{:T(128)}, bf16[16,128,128]{2,1,0:T(8,128)(2,1)S(1)}, bf16[2,16,128,128]{3,2,1,0:T(8,128)(2,1)S(1)}, bf16[2,16,128,128]{3,1,2,0:T(8,128)(2,1)...) while((s32[]{:T(128)}, bf16[16,128,128]{2,1,0:T(8,128)(2,1)S(1)}, ...), condition=%wide.region_1.2_spmd, body=%wide.region_0.1_spmd.sunk | while | flops 137363456 | bytes 16253117 | solution.py:146
  150.5 9.3 %all-to-all-done = bf16[8,16,16,128]{3,1,2,0:T(8,128)(2,1)S(1)} async-done(((bf16[8,16,16,128]{3,1,2,0:T(8,128)(2,1)}), bf16[8,16,16,128]{3,1,2,0:T(8,128)(2,1)S(1)}, u32[]{:S(2)}, u32[]{:S(2)}) %all-to-all-start) | async-done | bytes 524320 | tf_op jit(solution)/shard_map/while/body/eval_jaxpr/all_to_all | solution.py:27
  166.8 8.3 all-to-all-done.1
  181.3 9.2 %all-to-all-done = bf16[8,16,16,128]{3,1,2,0:T(8,128)(2,1)S(1)} async-done(((bf16[8,16,16,128]{3,1,2,0:T(8,128)(2,1)}), bf16[8,16,16,128]{3,1,2,0:T(8,128)(2,1)S(1)}, u32[]{:S(2)}, u32[]{:S(2)}) %all-to-all-start) | async-done | bytes 524320 | tf_op jit(solution)/shard_map/while/body/eval_jaxpr/all_to_all | solution.py:27
  197.5 8.3 all-to-all-done.1
  207.7 61.5 %while.121 = (s32[]{:T(128)}, bf16[16,128,128]{2,1,0:T(8,128)(2,1)S(1)}, bf16[2,16,128,128]{3,2,1,0:T(8,128)(2,1)S(1)}, bf16[2,16,128,128]{3,1,2,0:T(8,128)(2,1)...) while((s32[]{:T(128)}, bf16[16,128,128]{2,1,0:T(8,128)(2,1)S(1)}, ...), condition=%wide.region_3.4_spmd, body=%wide.region_2.3_spmd.sunk | while | flops 137363456 | bytes 16253117 | solution.py:146
  213.5 9.2 %all-to-all-done.2 = bf16[8,16,16,128]{3,1,2,0:T(8,128)(2,1)S(1)} async-done(((bf16[8,16,16,128]{3,1,2,0:T(8,128)(2,1)}), bf16[8,16,16,128]{3,1,2,0:T(8,128)(2,1)S(1)}, u32[]{:S(2)}, u32[]{:S(2)}) %all-to-all-start.2) | async-done | bytes 524320 | tf_op jit(solution)/shard_map/while/body/eval_jaxpr/all_to_all | solution.py:27
  229.7 8.3 all-to-all-done.3
  244.2 9.2 %all-to-all-done.2 = bf16[8,16,16,128]{3,1,2,0:T(8,128)(2,1)S(1)} async-done(((bf16[8,16,16,128]{3,1,2,0:T(8,128)(2,1)}), bf16[8,16,16,128]{3,1,2,0:T(8,128)(2,1)S(1)}, u32[]{:S(2)}, u32[]{:S(2)}) %all-to-all-start.2) | async-done | bytes 524320 | tf_op jit(solution)/shard_map/while/body/eval_jaxpr/all_to_all | solution.py:27
  260.4 8.3 all-to-all-done.3
  277.8 11.7 %collective-permute-done.12 = bf16[4,128,128]{1,2,0:T(8,128)(2,1)S(1)} collective-permute-done((bf16[4,128,128]{1,2,0:T(8,128)(2,1)S(1)}, bf16[4,128,128]{1,2,0:T(8,128)(2,1)S(1)}, u32[]{:S(2)}, u32[]{:S(2)}) %collective-permute-start.12) | collective-permute-done | bytes 131104 | tf_op jit(solution)/shard_map/ppermute | solution.py:76
  297.8 65.5 %while.122 = (s32[]{:T(128)}, bf16[16,128,128]{2,1,0:T(8,128)(2,1)S(1)}, bf16[2,16,128,128]{3,2,1,0:T(8,128)(2,1)S(1)}, bf16[2,16,128,128]{3,1,2,0:T(8,128)(2,1)...) while((s32[]{:T(128)}, bf16[16,128,128]{2,1,0:T(8,128)(2,1)S(1)}, ...), condition=%wide.region_5.6_spmd, body=%wide.region_4.5_spmd.sunk | while | flops 137363456 | bytes 16253117 | solution.py:146
  300.1 7.5 all-to-all-start.4
  307.6 9.3 %all-to-all-done.4 = bf16[8,16,16,128]{3,1,2,0:T(8,128)(2,1)S(1)} async-done(((bf16[8,16,16,128]{3,1,2,0:T(8,128)(2,1)}), bf16[8,16,16,128]{3,1,2,0:T(8,128)(2,1)S(1)}, u32[]{:S(2)}, u32[]{:S(2)}) %all-to-all-start.4) | async-done | bytes 524320 | tf_op jit(solution)/shard_map/while/body/eval_jaxpr/all_to_all | solution.py:27
  323.9 8.3 all-to-all-done.5
  338.4 9.2 %all-to-all-done.4 = bf16[8,16,16,128]{3,1,2,0:T(8,128)(2,1)S(1)} async-done(((bf16[8,16,16,128]{3,1,2,0:T(8,128)(2,1)}), bf16[8,16,16,128]{3,1,2,0:T(8,128)(2,1)S(1)}, u32[]{:S(2)}, u32[]{:S(2)}) %all-to-all-start.4) | async-done | bytes 524320 | tf_op jit(solution)/shard_map/while/body/eval_jaxpr/all_to_all | solution.py:27
  354.6 8.3 all-to-all-done.5
  365.9 61.5 %while.123 = (s32[]{:T(128)}, bf16[16,128,128]{2,1,0:T(8,128)(2,1)S(1)}, bf16[2,16,128,128]{3,2,1,0:T(8,128)(2,1)}, bf16[2,16,128,128]{3,1,2,0:T(8,128)(2,1)}, b...) while((s32[]{:T(128)}, bf16[16,128,128]{2,1,0:T(8,128)(2,1)S(1)}, ...), condition=%wide.region_7.8_spmd, body=%wide.region_6.7_spmd.sunk | while | flops 137363456 | bytes 16253117 | solution.py:146
  371.6 9.2 %all-to-all-done.6 = bf16[8,16,16,128]{3,1,2,0:T(8,128)(2,1)S(1)} async-done(((bf16[8,16,16,128]{3,1,2,0:T(8,128)(2,1)}), bf16[8,16,16,128]{3,1,2,0:T(8,128)(2,1)S(1)}, u32[]{:S(2)}, u32[]{:S(2)}) %all-to-all-start.6) | async-done | bytes 524320 | tf_op jit(solution)/shard_map/while/body/eval_jaxpr/all_to_all | solution.py:27
  388.6 7.5 all-to-all-done.7
  402.3 9.2 %all-to-all-done.6 = bf16[8,16,16,128]{3,1,2,0:T(8,128)(2,1)S(1)} async-done(((bf16[8,16,16,128]{3,1,2,0:T(8,128)(2,1)}), bf16[8,16,16,128]{3,1,2,0:T(8,128)(2,1)S(1)}, u32[]{:S(2)}, u32[]{:S(2)}) %all-to-all-start.6) | async-done | bytes 524320 | tf_op jit(solution)/shard_map/while/body/eval_jaxpr/all_to_all | solution.py:27
  419.4 7.5 all-to-all-done.7
  429.5 68.2 %while.124 = (s32[]{:T(128)}, bf16[16,128,128]{2,1,0:T(8,128)(2,1)S(1)}, bf16[2,2,16,128,128]{4,3,2,1,0:T(8,128)(2,1)}, bf16[2,2,16,128,128]{4,3,2,1,0:T(8,128)(...) while((s32[]{:T(128)}, ...), condition=%wide.region_9.10_spmd, body=%wide.region_8.9_spmd.sunk | while | flops 276037632 | bytes 34603268 | solution.py:161
  435.2 8.1 all-to-all-done.8
  449.7 8.8 %all-to-all-done.9 = bf16[8,16,16,128]{3,1,2,0:T(8,128)(2,1)S(1)} async-done(((bf16[8,16,16,128]{3,1,2,0:T(8,128)(2,1)}), bf16[8,16,16,128]{3,1,2,0:T(8,128)(2,1)S(1)}, u32[]{:S(2)}, u32[]{:S(2)}) %all-to-all-start.9) | async-done | bytes 524320 | tf_op jit(solution)/shard_map/while/body/eval_jaxpr/all_to_all | solution.py:27
  469.3 8.1 all-to-all-done.8
  483.8 8.8 %all-to-all-done.9 = bf16[8,16,16,128]{3,1,2,0:T(8,128)(2,1)S(1)} async-done(((bf16[8,16,16,128]{3,1,2,0:T(8,128)(2,1)}), bf16[8,16,16,128]{3,1,2,0:T(8,128)(2,1)S(1)}, u32[]{:S(2)}, u32[]{:S(2)}) %all-to-all-start.9) | async-done | bytes 524320 | tf_op jit(solution)/shard_map/while/body/eval_jaxpr/all_to_all | solution.py:27
  522.1 82.9 %while.125 = (s32[]{:T(128)}, bf16[16,128,128]{2,1,0:T(8,128)(2,1)S(1)}, bf16[2,2,16,128,128]{4,3,2,1,0:T(8,128)(2,1)}, bf16[2,2,16,128,128]{4,3,2,1,0:T(8,128)(...) while((s32[]{:T(128)}, ...), condition=%wide.region_11.12_spmd, body=%wide.region_10.11_spmd.sunk | while | flops 276037632 | bytes 38797600 | solution.py:161
  523.3 20.1 %all-to-all-start.10 = ((bf16[8,16,16,128]{3,2,1,0:T(8,128)(2,1)}), bf16[8,16,16,128]{3,2,1,0:T(8,128)(2,1)S(1)}, u32[]{:S(2)}, u32[]{:S(2)}) async-start(bf16[8,16,16,128]{3,2,1,0:T(8,128)(2,1)} %bitcast.625), calls=%async_computation.10 | async-start | bytes 1048576 | tf_op jit(solution)/shard_map/while/body/eval_jaxpr/all_to_all | solution.py:27
  544.5 8.2 all-to-all-done.10
  559.1 8.8 %all-to-all-done.11 = bf16[8,16,16,128]{3,1,2,0:T(8,128)(2,1)S(1)} async-done(((bf16[8,16,16,128]{3,1,2,0:T(8,128)(2,1)}), bf16[8,16,16,128]{3,1,2,0:T(8,128)(2,1)S(1)}, u32[]{:S(2)}, u32[]{:S(2)}) %all-to-all-start.11) | async-done | bytes 524320 | tf_op jit(solution)/shard_map/while/body/eval_jaxpr/all_to_all | solution.py:27
  577.6 8.1 all-to-all-done.10
  592.2 8.8 %all-to-all-done.11 = bf16[8,16,16,128]{3,1,2,0:T(8,128)(2,1)S(1)} async-done(((bf16[8,16,16,128]{3,1,2,0:T(8,128)(2,1)}), bf16[8,16,16,128]{3,1,2,0:T(8,128)(2,1)S(1)}, u32[]{:S(2)}, u32[]{:S(2)}) %all-to-all-start.11) | async-done | bytes 524320 | tf_op jit(solution)/shard_map/while/body/eval_jaxpr/all_to_all | solution.py:27
  611.7 66.2 %while.126 = (s32[]{:T(128)}, bf16[16,128,128]{2,1,0:T(8,128)(2,1)S(1)}, bf16[2,2,16,128,128]{4,3,2,1,0:T(8,128)(2,1)}, bf16[2,2,16,128,128]{4,3,2,1,0:T(8,128)(...) while((s32[]{:T(128)}, ...), condition=%wide.region_13.14_spmd, body=%wide.region_12.13_spmd.sunk | while | flops 276037632 | bytes 38797600 | solution.py:161
  617.4 8.1 all-to-all-done.12
  632.0 8.8 %all-to-all-done.13 = bf16[8,16,16,128]{3,1,2,0:T(8,128)(2,1)S(1)} async-done(((bf16[8,16,16,128]{3,1,2,0:T(8,128)(2,1)}), bf16[8,16,16,128]{3,1,2,0:T(8,128)(2,1)S(1)}, u32[]{:S(2)}, u32[]{:S(2)}) %all-to-all-start.13) | async-done | bytes 524320 | tf_op jit(solution)/shard_map/while/body/eval_jaxpr/all_to_all | solution.py:27
  650.5 8.1 all-to-all-done.12
  665.1 8.8 %all-to-all-done.13 = bf16[8,16,16,128]{3,1,2,0:T(8,128)(2,1)S(1)} async-done(((bf16[8,16,16,128]{3,1,2,0:T(8,128)(2,1)}), bf16[8,16,16,128]{3,1,2,0:T(8,128)(2,1)S(1)}, u32[]{:S(2)}, u32[]{:S(2)}) %all-to-all-start.13) | async-done | bytes 524320 | tf_op jit(solution)/shard_map/while/body/eval_jaxpr/all_to_all | solution.py:27
  685.4 66.2 %while.127 = (s32[]{:T(128)}, bf16[16,128,128]{2,1,0:T(8,128)(2,1)S(1)}, bf16[2,2,16,128,128]{4,3,2,1,0:T(8,128)(2,1)}, bf16[2,2,16,128,128]{4,3,2,1,0:T(8,128)(...) while((s32[]{:T(128)}, ...), condition=%wide.region_16.17_spmd, body=%wide.region_15.16_spmd.sunk | while | flops 276037632 | bytes 38797600 | solution.py:161
  691.2 8.1 all-to-all-done.14
  705.8 8.8 %all-to-all-done.15 = bf16[8,16,16,128]{3,1,2,0:T(8,128)(2,1)S(1)} async-done(((bf16[8,16,16,128]{3,1,2,0:T(8,128)(2,1)}), bf16[8,16,16,128]{3,1,2,0:T(8,128)(2,1)S(1)}, u32[]{:S(2)}, u32[]{:S(2)}) %all-to-all-start.15) | async-done | bytes 524320 | tf_op jit(solution)/shard_map/while/body/eval_jaxpr/all_to_all | solution.py:27
  724.3 8.1 all-to-all-done.14
  738.9 8.8 %all-to-all-done.15 = bf16[8,16,16,128]{3,1,2,0:T(8,128)(2,1)S(1)} async-done(((bf16[8,16,16,128]{3,1,2,0:T(8,128)(2,1)}), bf16[8,16,16,128]{3,1,2,0:T(8,128)(2,1)S(1)}, u32[]{:S(2)}, u32[]{:S(2)}) %all-to-all-start.15) | async-done | bytes 524320 | tf_op jit(solution)/shard_map/while/body/eval_jaxpr/all_to_all | solution.py:27
  764.0 9.7 %collective-permute-start.26 = (bf16[1,2,4,128,128]{4,3,2,1,0:T(8,128)(2,1)S(1)}, bf16[1,2,4,128,128]{4,3,2,1,0:T(8,128)(2,1)S(1)}, u32[]{:S(2)}, u32[]{:S(2)}) collective-permute-start(bf16[1,2,4,128,128]{4,3,2,1,0:T(8,128)(2,1)S(1)} %get-tuple-element.908), channel_id=1, source_target_pairs={{0,16},{8,24},{16,0},{24,8},{1,17},{9,25},{17,1},{25,9},{2,18},{10... | collective-permute-start | bytes 786440 | tf_op jit(solution)/shard_map/ppermute | solution.py:104
  780.8 22.9 %reduce-scatter.9.cloned.1.call-done = bf16[16,128,128]{2,1,0:T(8,128)(2,1)} async-done(((bf16[64,128,128]{2,1,0:T(8,128)(2,1)}), bf16[16,128,128]{2,1,0:T(8,128)(2,1)}) %reduce-scatter.9.cloned.1.call-update) | async-done | bytes 524304 | tf_op jit(solution)/shard_map/reduce_scatter | solution.py:115
  (416 shorter events, 388.4 us)
Async XLA Ops:
  7.2 81.3 %all-gather.9.cloned.1.call-start = ((), (), s32[]{:S(2)}) async-start(), calls=%async_computation.24 | async-start | bytes 2621440 | tf_op jit(solution)/shard_map/all_gather | solution.py:110
  27.1 113.0 %all-gather.11.cloned.1.call-start = ((), (), s32[]{:S(2)}) async-start(), calls=%async_computation.25 | async-start | bytes 2621440 | tf_op jit(solution)/shard_map/all_gather | solution.py:110
  29.6 33.9 %collective-permute-start.2 = (bf16[4,128,128]{1,2,0:T(8,128)(2,1)S(1)}, bf16[4,128,128]{1,2,0:T(8,128)(2,1)S(1)}, u32[]{:S(2)}, u32[]{:S(2)}) collective-permute-start(bf16[4,128,128]{1,2,0:T(8,128)(2,1)S(1)} %bitcast.769), channel_id=1, source_target_pairs={{0,16},{2,24},{4,0},{6,8},{8,18},{10,26},{12,2},{14,10},{16,20},{1... | collective-permute-start | bytes 393224 | tf_op jit(solution)/shard_map/ppermute | solution.py:76
  32.4 31.1 %collective-permute-start.1 = (bf16[4,128,128]{1,2,0:T(8,128)(2,1)S(1)}, bf16[4,128,128]{1,2,0:T(8,128)(2,1)S(1)}, u32[]{:S(2)}, u32[]{:S(2)}) collective-permute-start(bf16[4,128,128]{1,2,0:T(8,128)(2,1)S(1)} %bitcast.771), channel_id=1, source_target_pairs={{0,8},{2,0},{4,24},{6,16},{8,10},{10,2},{12,26},{14,18},{16,12},{1... | collective-permute-start | bytes 393224 | tf_op jit(solution)/shard_map/ppermute | solution.py:76
  33.0 30.5 %collective-permute-start = (bf16[4,128,128]{1,2,0:T(8,128)(2,1)S(1)}, bf16[4,128,128]{1,2,0:T(8,128)(2,1)S(1)}, u32[]{:S(2)}, u32[]{:S(2)}) collective-permute-start(bf16[4,128,128]{1,2,0:T(8,128)(2,1)S(1)} %bitcast.774), channel_id=1, source_target_pairs={{0,0},{2,8},{4,16},{6,24},{8,2},{10,10},{12,18},{14,26},{16,4},{18... | collective-permute-start | bytes 393224 | tf_op jit(solution)/shard_map/ppermute | solution.py:76
  93.0 197.2 %all-gather.13.cloned.1.call-start = ((), (), s32[]{:S(2)}) async-start(), calls=%async_computation.26 | async-start | bytes 2621440 | tf_op jit(solution)/shard_map/all_gather | solution.py:110
  93.8 14.2 %collective-permute-start.8 = (bf16[2,4,128,128]{2,3,1,0:T(8,128)(2,1)S(1)}, bf16[2,4,128,128]{2,3,1,0:T(8,128)(2,1)S(1)}, u32[]{:S(2)}, u32[]{:S(2)}) collective-permute-start(bf16[2,4,128,128]{2,3,1,0:T(8,128)(2,1)S(1)} %pad_maximum_fusion.17), channel_id=1, source_target_pairs={{0,16},{8,24},{16,0},{24,8},{1,17},{9,25},{17,1},{25,9},{2,18},{10... | collective-permute-start | bytes 786440 | tf_op jit(solution)/shard_map/ppermute | solution.py:104
  109.6 183.7 %all-gather.15.cloned.1.call-start = ((), (), s32[]{:S(2)}) async-start(), calls=%async_computation.27 | async-start | bytes 2621440 | tf_op jit(solution)/shard_map/all_gather | solution.py:110
  111.4 496.9 %reduce-scatter.5.cloned.1.call-start = ((), (), s32[]{:S(2)}) async-start(), calls=%async_computation.20 | async-start | bytes 2621440 | tf_op jit(solution)/shard_map/reduce_scatter | solution.py:115
  146.8 12.9 %all-to-all-start = ((bf16[8,16,16,128]{3,1,2,0:T(8,128)(2,1)}), bf16[8,16,16,128]{3,1,2,0:T(8,128)(2,1)S(1)}, u32[]{:S(2)}, u32[]{:S(2)}) async-start(bf16[8,16,16,128]{3,1,2,0:T(8,128)(2,1)} %copy.405), calls=%async_computation | async-start | bytes 1048576 | tf_op jit(solution)/shard_map/while/body/eval_jaxpr/all_to_all | solution.py:27
  162.4 12.7 %all-to-all-start.1 = ((bf16[8,16,16,128]{3,1,2,0:T(8,128)(2,1)}), bf16[8,16,16,128]{3,1,2,0:T(8,128)(2,1)S(1)}, u32[]{:S(2)}, u32[]{:S(2)}) async-start(bf16[8,16,16,128]{3,1,2,0:T(8,128)(2,1)} %copy.406), calls=%async_computation.1 | async-start | bytes 1048576 | tf_op jit(solution)/shard_map/while/body/eval_jaxpr/all_to_all | solution.py:27
  177.8 12.7 %all-to-all-start = ((bf16[8,16,16,128]{3,1,2,0:T(8,128)(2,1)}), bf16[8,16,16,128]{3,1,2,0:T(8,128)(2,1)S(1)}, u32[]{:S(2)}, u32[]{:S(2)}) async-start(bf16[8,16,16,128]{3,1,2,0:T(8,128)(2,1)} %copy.405), calls=%async_computation | async-start | bytes 1048576 | tf_op jit(solution)/shard_map/while/body/eval_jaxpr/all_to_all | solution.py:27
  193.1 12.7 %all-to-all-start.1 = ((bf16[8,16,16,128]{3,1,2,0:T(8,128)(2,1)}), bf16[8,16,16,128]{3,1,2,0:T(8,128)(2,1)S(1)}, u32[]{:S(2)}, u32[]{:S(2)}) async-start(bf16[8,16,16,128]{3,1,2,0:T(8,128)(2,1)} %copy.406), calls=%async_computation.1 | async-start | bytes 1048576 | tf_op jit(solution)/shard_map/while/body/eval_jaxpr/all_to_all | solution.py:27
  210.0 12.7 %all-to-all-start.2 = ((bf16[8,16,16,128]{3,1,2,0:T(8,128)(2,1)}), bf16[8,16,16,128]{3,1,2,0:T(8,128)(2,1)S(1)}, u32[]{:S(2)}, u32[]{:S(2)}) async-start(bf16[8,16,16,128]{3,1,2,0:T(8,128)(2,1)} %copy.409), calls=%async_computation.2 | async-start | bytes 1048576 | tf_op jit(solution)/shard_map/while/body/eval_jaxpr/all_to_all | solution.py:27
  225.3 12.7 %all-to-all-start.3 = ((bf16[8,16,16,128]{3,1,2,0:T(8,128)(2,1)}), bf16[8,16,16,128]{3,1,2,0:T(8,128)(2,1)S(1)}, u32[]{:S(2)}, u32[]{:S(2)}) async-start(bf16[8,16,16,128]{3,1,2,0:T(8,128)(2,1)} %copy.410), calls=%async_computation.3 | async-start | bytes 1048576 | tf_op jit(solution)/shard_map/while/body/eval_jaxpr/all_to_all | solution.py:27
  240.7 12.7 %all-to-all-start.2 = ((bf16[8,16,16,128]{3,1,2,0:T(8,128)(2,1)}), bf16[8,16,16,128]{3,1,2,0:T(8,128)(2,1)S(1)}, u32[]{:S(2)}, u32[]{:S(2)}) async-start(bf16[8,16,16,128]{3,1,2,0:T(8,128)(2,1)} %copy.409), calls=%async_computation.2 | async-start | bytes 1048576 | tf_op jit(solution)/shard_map/while/body/eval_jaxpr/all_to_all | solution.py:27
  256.0 12.7 %all-to-all-start.3 = ((bf16[8,16,16,128]{3,1,2,0:T(8,128)(2,1)}), bf16[8,16,16,128]{3,1,2,0:T(8,128)(2,1)S(1)}, u32[]{:S(2)}, u32[]{:S(2)}) async-start(bf16[8,16,16,128]{3,1,2,0:T(8,128)(2,1)} %copy.410), calls=%async_computation.3 | async-start | bytes 1048576 | tf_op jit(solution)/shard_map/while/body/eval_jaxpr/all_to_all | solution.py:27
  270.1 19.4 %collective-permute-start.12 = (bf16[4,128,128]{1,2,0:T(8,128)(2,1)S(1)}, bf16[4,128,128]{1,2,0:T(8,128)(2,1)S(1)}, u32[]{:S(2)}, u32[]{:S(2)}) collective-permute-start(bf16[4,128,128]{1,2,0:T(8,128)(2,1)S(1)} %bitcast.764), channel_id=1, source_target_pairs={{0,16},{2,24},{4,0},{6,8},{8,18},{10,26},{12,2},{14,10},{16,20},{1... | collective-permute-start | bytes 393224 | tf_op jit(solution)/shard_map/ppermute | solution.py:76
  271.3 18.2 %collective-permute-start.11 = (bf16[4,128,128]{1,2,0:T(8,128)(2,1)S(1)}, bf16[4,128,128]{1,2,0:T(8,128)(2,1)S(1)}, u32[]{:S(2)}, u32[]{:S(2)}) collective-permute-start(bf16[4,128,128]{1,2,0:T(8,128)(2,1)S(1)} %bitcast.767), channel_id=1, source_target_pairs={{0,8},{2,0},{4,24},{6,16},{8,10},{10,2},{12,26},{14,18},{16,12},{1... | collective-permute-start | bytes 393224 | tf_op jit(solution)/shard_map/ppermute | solution.py:76
  271.9 17.6 %collective-permute-start.10 = (bf16[4,128,128]{1,2,0:T(8,128)(2,1)S(1)}, bf16[4,128,128]{1,2,0:T(8,128)(2,1)S(1)}, u32[]{:S(2)}, u32[]{:S(2)}) collective-permute-start(bf16[4,128,128]{1,2,0:T(8,128)(2,1)S(1)} %bitcast.772), channel_id=1, source_target_pairs={{0,0},{2,8},{4,16},{6,24},{8,2},{10,10},{12,18},{14,26},{16,4},{18... | collective-permute-start | bytes 393224 | tf_op jit(solution)/shard_map/ppermute | solution.py:76
  300.1 16.8 %all-to-all-start.4 = ((bf16[8,16,16,128]{3,1,2,0:T(8,128)(2,1)}), bf16[8,16,16,128]{3,1,2,0:T(8,128)(2,1)S(1)}, u32[]{:S(2)}, u32[]{:S(2)}) async-start(bf16[8,16,16,128]{3,1,2,0:T(8,128)(2,1)} %copy.413), calls=%async_computation.4 | async-start | bytes 1048576 | tf_op jit(solution)/shard_map/while/body/eval_jaxpr/all_to_all | solution.py:27
  319.5 12.7 %all-to-all-start.5 = ((bf16[8,16,16,128]{3,1,2,0:T(8,128)(2,1)}), bf16[8,16,16,128]{3,1,2,0:T(8,128)(2,1)S(1)}, u32[]{:S(2)}, u32[]{:S(2)}) async-start(bf16[8,16,16,128]{3,1,2,0:T(8,128)(2,1)} %copy.414), calls=%async_computation.5 | async-start | bytes 1048576 | tf_op jit(solution)/shard_map/while/body/eval_jaxpr/all_to_all | solution.py:27
  334.9 12.7 %all-to-all-start.4 = ((bf16[8,16,16,128]{3,1,2,0:T(8,128)(2,1)}), bf16[8,16,16,128]{3,1,2,0:T(8,128)(2,1)S(1)}, u32[]{:S(2)}, u32[]{:S(2)}) async-start(bf16[8,16,16,128]{3,1,2,0:T(8,128)(2,1)} %copy.413), calls=%async_computation.4 | async-start | bytes 1048576 | tf_op jit(solution)/shard_map/while/body/eval_jaxpr/all_to_all | solution.py:27
  350.2 12.7 %all-to-all-start.5 = ((bf16[8,16,16,128]{3,1,2,0:T(8,128)(2,1)}), bf16[8,16,16,128]{3,1,2,0:T(8,128)(2,1)S(1)}, u32[]{:S(2)}, u32[]{:S(2)}) async-start(bf16[8,16,16,128]{3,1,2,0:T(8,128)(2,1)} %copy.414), calls=%async_computation.5 | async-start | bytes 1048576 | tf_op jit(solution)/shard_map/while/body/eval_jaxpr/all_to_all | solution.py:27
  368.1 12.7 %all-to-all-start.6 = ((bf16[8,16,16,128]{3,1,2,0:T(8,128)(2,1)}), bf16[8,16,16,128]{3,1,2,0:T(8,128)(2,1)S(1)}, u32[]{:S(2)}, u32[]{:S(2)}) async-start(bf16[8,16,16,128]{3,1,2,0:T(8,128)(2,1)} %copy.417), calls=%async_computation.6 | async-start | bytes 1048576 | tf_op jit(solution)/shard_map/while/body/eval_jaxpr/all_to_all | solution.py:27
  383.4 12.7 %all-to-all-start.7 = ((bf16[8,16,16,128]{3,1,2,0:T(8,128)(2,1)}), bf16[8,16,16,128]{3,1,2,0:T(8,128)(2,1)S(1)}, u32[]{:S(2)}, u32[]{:S(2)}) async-start(bf16[8,16,16,128]{3,1,2,0:T(8,128)(2,1)} %copy.418), calls=%async_computation.7 | async-start | bytes 1048576 | tf_op jit(solution)/shard_map/while/body/eval_jaxpr/all_to_all | solution.py:27
  398.8 12.7 %all-to-all-start.6 = ((bf16[8,16,16,128]{3,1,2,0:T(8,128)(2,1)}), bf16[8,16,16,128]{3,1,2,0:T(8,128)(2,1)S(1)}, u32[]{:S(2)}, u32[]{:S(2)}) async-start(bf16[8,16,16,128]{3,1,2,0:T(8,128)(2,1)} %copy.417), calls=%async_computation.6 | async-start | bytes 1048576 | tf_op jit(solution)/shard_map/while/body/eval_jaxpr/all_to_all | solution.py:27
  414.2 12.7 %all-to-all-start.7 = ((bf16[8,16,16,128]{3,1,2,0:T(8,128)(2,1)}), bf16[8,16,16,128]{3,1,2,0:T(8,128)(2,1)S(1)}, u32[]{:S(2)}, u32[]{:S(2)}) async-start(bf16[8,16,16,128]{3,1,2,0:T(8,128)(2,1)} %copy.418), calls=%async_computation.7 | async-start | bytes 1048576 | tf_op jit(solution)/shard_map/while/body/eval_jaxpr/all_to_all | solution.py:27
  430.6 12.7 %all-to-all-start.8 = ((bf16[8,16,16,128]{3,2,1,0:T(8,128)(2,1)}), bf16[8,16,16,128]{3,2,1,0:T(8,128)(2,1)S(1)}, u32[]{:S(2)}, u32[]{:S(2)}) async-start(bf16[8,16,16,128]{3,2,1,0:T(8,128)(2,1)} %bitcast.606), calls=%async_computation.8 | async-start | bytes 1048576 | tf_op jit(solution)/shard_map/while/body/eval_jaxpr/all_to_all | solution.py:27
  445.8 12.7 %all-to-all-start.9 = ((bf16[8,16,16,128]{3,1,2,0:T(8,128)(2,1)}), bf16[8,16,16,128]{3,1,2,0:T(8,128)(2,1)S(1)}, u32[]{:S(2)}, u32[]{:S(2)}) async-start(bf16[8,16,16,128]{3,1,2,0:T(8,128)(2,1)} %copy.423), calls=%async_computation.9 | async-start | bytes 1048576 | tf_op jit(solution)/shard_map/while/body/eval_jaxpr/all_to_all | solution.py:27
  464.7 12.7 %all-to-all-start.8 = ((bf16[8,16,16,128]{3,2,1,0:T(8,128)(2,1)}), bf16[8,16,16,128]{3,2,1,0:T(8,128)(2,1)S(1)}, u32[]{:S(2)}, u32[]{:S(2)}) async-start(bf16[8,16,16,128]{3,2,1,0:T(8,128)(2,1)} %bitcast.606), calls=%async_computation.8 | async-start | bytes 1048576 | tf_op jit(solution)/shard_map/while/body/eval_jaxpr/all_to_all | solution.py:27
  479.9 12.7 %all-to-all-start.9 = ((bf16[8,16,16,128]{3,1,2,0:T(8,128)(2,1)}), bf16[8,16,16,128]{3,1,2,0:T(8,128)(2,1)S(1)}, u32[]{:S(2)}, u32[]{:S(2)}) async-start(bf16[8,16,16,128]{3,1,2,0:T(8,128)(2,1)} %copy.423), calls=%async_computation.9 | async-start | bytes 1048576 | tf_op jit(solution)/shard_map/while/body/eval_jaxpr/all_to_all | solution.py:27
  500.9 180.3 %reduce-scatter.7.cloned.1.call-start = ((), (), s32[]{:S(2)}) async-start(), calls=%async_computation.21 | async-start | bytes 2621440 | tf_op jit(solution)/shard_map/reduce_scatter | solution.py:115
  503.7 15.6 %collective-permute-start.15 = (bf16[4,128,128]{2,1,0:T(8,128)(2,1)S(1)}, bf16[4,128,128]{2,1,0:T(8,128)(2,1)S(1)}, u32[]{:S(2)}, u32[]{:S(2)}) collective-permute-start(bf16[4,128,128]{2,1,0:T(8,128)(2,1)S(1)} %bitcast.770), channel_id=1, source_target_pairs={{0,2},{2,10},{4,18},{6,26},{8,0},{10,8},{12,16},{14,24},{16,6},{18... | collective-permute-start | bytes 393224 | tf_op jit(solution)/shard_map/ppermute | solution.py:76
  503.9 15.4 %collective-permute-start.14 = (bf16[4,128,128]{2,1,0:T(8,128)(2,1)S(1)}, bf16[4,128,128]{2,1,0:T(8,128)(2,1)S(1)}, u32[]{:S(2)}, u32[]{:S(2)}) collective-permute-start(bf16[4,128,128]{2,1,0:T(8,128)(2,1)S(1)} %bitcast.773), channel_id=1, source_target_pairs={{0,0},{2,8},{4,16},{6,24},{8,2},{10,10},{12,18},{14,26},{16,4},{18... | collective-permute-start | bytes 393224 | tf_op jit(solution)/shard_map/ppermute | solution.py:76
  523.3 29.4 %all-to-all-start.10 = ((bf16[8,16,16,128]{3,2,1,0:T(8,128)(2,1)}), bf16[8,16,16,128]{3,2,1,0:T(8,128)(2,1)S(1)}, u32[]{:S(2)}, u32[]{:S(2)}) async-start(bf16[8,16,16,128]{3,2,1,0:T(8,128)(2,1)} %bitcast.625), calls=%async_computation.10 | async-start | bytes 1048576 | tf_op jit(solution)/shard_map/while/body/eval_jaxpr/all_to_all | solution.py:27
  555.2 12.7 %all-to-all-start.11 = ((bf16[8,16,16,128]{3,1,2,0:T(8,128)(2,1)}), bf16[8,16,16,128]{3,1,2,0:T(8,128)(2,1)S(1)}, u32[]{:S(2)}, u32[]{:S(2)}) async-start(bf16[8,16,16,128]{3,1,2,0:T(8,128)(2,1)} %copy.429), calls=%async_computation.11 | async-start | bytes 1048576 | tf_op jit(solution)/shard_map/while/body/eval_jaxpr/all_to_all | solution.py:27
  573.1 12.7 %all-to-all-start.10 = ((bf16[8,16,16,128]{3,2,1,0:T(8,128)(2,1)}), bf16[8,16,16,128]{3,2,1,0:T(8,128)(2,1)S(1)}, u32[]{:S(2)}, u32[]{:S(2)}) async-start(bf16[8,16,16,128]{3,2,1,0:T(8,128)(2,1)} %bitcast.625), calls=%async_computation.10 | async-start | bytes 1048576 | tf_op jit(solution)/shard_map/while/body/eval_jaxpr/all_to_all | solution.py:27
  588.3 12.7 %all-to-all-start.11 = ((bf16[8,16,16,128]{3,1,2,0:T(8,128)(2,1)}), bf16[8,16,16,128]{3,1,2,0:T(8,128)(2,1)S(1)}, u32[]{:S(2)}, u32[]{:S(2)}) async-start(bf16[8,16,16,128]{3,1,2,0:T(8,128)(2,1)} %copy.429), calls=%async_computation.11 | async-start | bytes 1048576 | tf_op jit(solution)/shard_map/while/body/eval_jaxpr/all_to_all | solution.py:27
  608.1 171.0 %reduce-scatter.11.cloned.1.call-start = ((), (), s32[]{:S(2)}) async-start(), calls=%async_computation.23 | async-start | bytes 2621440 | tf_op jit(solution)/shard_map/reduce_scatter | solution.py:115
  645.9 12.7 %all-to-all-start.12 = ((bf16[8,16,16,128]{3,2,1,0:T(8,128)(2,1)}), bf16[8,16,16,128]{3,2,1,0:T(8,128)(2,1)S(1)}, u32[]{:S(2)}, u32[]{:S(2)}) async-start(bf16[8,16,16,128]{3,2,1,0:T(8,128)(2,1)} %bitcast.644), calls=%async_computation.12 | async-start | bytes 1048576 | tf_op jit(solution)/shard_map/while/body/eval_jaxpr/all_to_all | solution.py:27
  681.1 122.7 %reduce-scatter.9.cloned.1.call-start = ((), (), s32[]{:S(2)}) async-start(), calls=%async_computation.22 | async-start | bytes 2621440 | tf_op jit(solution)/shard_map/reduce_scatter | solution.py:115
  755.9 17.7 %collective-permute-start.20 = (bf16[4,128,128]{2,1,0:T(8,128)(2,1)S(1)}, bf16[4,128,128]{2,1,0:T(8,128)(2,1)S(1)}, u32[]{:S(2)}, u32[]{:S(2)}) collective-permute-start(bf16[4,128,128]{2,1,0:T(8,128)(2,1)S(1)} %bitcast.760), channel_id=1, source_target_pairs={{0,4},{2,12},{4,20},{6,28},{8,6},{10,14},{12,22},{14,30},{16,0},{1... | collective-permute-start | bytes 393224 | tf_op jit(solution)/shard_map/ppermute | solution.py:76
  756.1 17.5 %collective-permute-start.19 = (bf16[4,128,128]{2,1,0:T(8,128)(2,1)S(1)}, bf16[4,128,128]{2,1,0:T(8,128)(2,1)S(1)}, u32[]{:S(2)}, u32[]{:S(2)}) collective-permute-start(bf16[4,128,128]{2,1,0:T(8,128)(2,1)S(1)} %bitcast.759), channel_id=1, source_target_pairs={{0,2},{2,10},{4,18},{6,26},{8,0},{10,8},{12,16},{14,24},{16,6},{18... | collective-permute-start | bytes 393224 | tf_op jit(solution)/shard_map/ppermute | solution.py:76
  756.9 16.8 %collective-permute-start.18 = (bf16[4,128,128]{2,1,0:T(8,128)(2,1)S(1)}, bf16[4,128,128]{2,1,0:T(8,128)(2,1)S(1)}, u32[]{:S(2)}, u32[]{:S(2)}) collective-permute-start(bf16[4,128,128]{2,1,0:T(8,128)(2,1)S(1)} %bitcast.761), channel_id=1, source_target_pairs={{0,0},{2,8},{4,16},{6,24},{8,2},{10,10},{12,18},{14,26},{16,4},{18... | collective-permute-start | bytes 393224 | tf_op jit(solution)/shard_map/ppermute | solution.py:76
  757.8 16.9 %collective-permute-start.27 = (bf16[1,2,4,128,128]{4,3,2,1,0:T(8,128)(2,1)S(1)}, bf16[1,2,4,128,128]{4,3,2,1,0:T(8,128)(2,1)S(1)}, u32[]{:S(2)}, u32[]{:S(2)}) collective-permute-start(bf16[1,2,4,128,128]{4,3,2,1,0:T(8,128)(2,1)S(1)} %get-tuple-element.907), channel_id=1, source_target_pairs={{0,24},{8,16},{16,8},{24,0},{1,25},{9,17},{17,9},{25,1},{2,26},{10... | collective-permute-start | bytes 786440 | tf_op jit(solution)/shard_map/ppermute | solution.py:104
  764.0 15.1 %collective-permute-start.26 = (bf16[1,2,4,128,128]{4,3,2,1,0:T(8,128)(2,1)S(1)}, bf16[1,2,4,128,128]{4,3,2,1,0:T(8,128)(2,1)S(1)}, u32[]{:S(2)}, u32[]{:S(2)}) collective-permute-start(bf16[1,2,4,128,128]{4,3,2,1,0:T(8,128)(2,1)S(1)} %get-tuple-element.908), channel_id=1, source_target_pairs={{0,16},{8,24},{16,0},{24,8},{1,17},{9,25},{17,1},{25,9},{2,18},{10... | collective-permute-start | bytes 786440 | tf_op jit(solution)/shard_map/ppermute | solution.py:104
  805.9 14.2 %collective-permute-start.23 = (bf16[1,2,4,128,128]{4,3,2,1,0:T(8,128)(2,1)S(1)}, bf16[1,2,4,128,128]{4,3,2,1,0:T(8,128)(2,1)S(1)}, u32[]{:S(2)}, u32[]{:S(2)}) collective-permute-start(bf16[1,2,4,128,128]{4,3,2,1,0:T(8,128)(2,1)S(1)} %get-tuple-element.900), channel_id=1, source_target_pairs={{0,16},{8,24},{16,0},{24,8},{1,17},{9,25},{17,1},{25,9},{2,18},{10... | collective-permute-start | bytes 786440 | tf_op jit(solution)/shard_map/ppermute | solution.py:104
  (48 other events, 349.3 us)
Sparse Core Ops, SparseCore 0:
  27.2 61.1 all-gather.8
  93.1 46.9 all-gather.10
  142.3 44.6 all-gather.12
  188.4 44.5 all-gather.14
  501.0 48.7 reduce-scatter.4
  608.3 40.6 reduce-scatter.6
  681.2 40.6 reduce-scatter.10
  755.0 48.7 reduce-scatter.8

commit v9 on v8

v9 whole, which is shorter than its diff:
```python
import jax
import jax.numpy as jnp
from jax import lax
from jax.sharding import Mesh, PartitionSpec as P

F32 = jnp.float32
BF16 = jnp.bfloat16
WIDE = ("s", "x")
GROUPS = 4
PAIRED = 2


def silu_slope(values):
    sigmoid = jax.nn.sigmoid(values)
    return sigmoid * (1.0 + values * (1.0 - sigmoid))


def group_order(size, sections, groups, peers):
    natural = jnp.arange(size).reshape(groups, peers, sections, -1)
    order = natural.transpose(2, 1, 0, 3).reshape(size)
    return (order[:, None] == jnp.arange(size)[None, :]).astype(BF16)


def exchange(values):
    own, full, rows = values.shape
    pieces = values.transpose(1, 0, 2).reshape(full // own, own, own, rows)
    moved = lax.all_to_all(pieces, WIDE, split_axis=0, concat_axis=0, tiled=True)
    return moved.transpose(1, 0, 2, 3).reshape(own, full, rows)


def forward_layer(acts, right, left):
    mixed = jnp.einsum("bjk,bjr->bkr", right, acts, preferred_element_type=F32).astype(BF16)
    columns = exchange(mixed)
    activated = jax.nn.silu(columns.astype(F32)).astype(BF16)
    second = jnp.einsum("kbc,kbr->kcr", left, activated, preferred_element_type=F32).astype(BF16)
    following = (acts.astype(F32) + exchange(second).astype(F32)).astype(BF16)
    return following, (acts, columns)


def backward_layer(grad, right, left, saved):
    acts, columns = saved
    grad_columns = exchange(grad)
    wide = columns.astype(F32)
    activated = jax.nn.silu(wide).astype(BF16)
    left_term = jnp.einsum("kbr,kcr->kbc", activated, grad_columns, preferred_element_type=F32)
    grad_act = jnp.einsum("kbc,kcr->kbr", left, grad_columns, preferred_element_type=F32)
    grad_mixed = exchange((grad_act * silu_slope(wide)).astype(BF16))
    right_term = jnp.einsum("bjr,bkr->bjk", acts, grad_mixed, preferred_element_type=F32)
    branch = jnp.einsum("bjk,bkr->bjr", right, grad_mixed, preferred_element_type=F32)
    following = (grad.astype(F32) + branch).astype(BF16)
    return following, right_term.astype(BF16), left_term.astype(BF16)


def body(inputs, cotangent, right_factor, left_factor):
    sections = lax.axis_size("s")
    groups = lax.axis_size("t")
    peers = lax.axis_size("x")
    loops, _, held, size, _ = right_factor.shape
    rows = inputs.shape[2]
    sub = held // sections
    own = sub * groups
    layers = loops * sections
    micros = sections // groups
    s_index = lax.axis_index("s")
    t_index = lax.axis_index("t")
    line = (s_index % micros) * groups + t_index
    order = group_order(size, sections, groups, peers)

    def pick(parts, index):
        return lax.dynamic_index_in_dim(parts, index, 0, keepdims=False)

    def turned(parts, send_by, place_by, target):
        moved = []
        for mask in range(sections):
            pairs = [(s * groups + t, target(s, t, mask)) for s in range(sections) for t in range(groups)]
            moved.append(lax.ppermute(pick(parts, send_by ^ mask), ("s", "t"), pairs))
        moved = jnp.stack(moved)
        return jnp.stack([pick(moved, place_by ^ part) for part in range(sections)])

    def into(s, t, mask):
        return (((s % micros) * groups + t) ^ mask) * groups + s // micros

    def outof(s, t, mask):
        line_to = s ^ mask
        return (t * micros + line_to // groups) * groups + line_to % groups

    def arriving(acts):
        parts = turned(acts.reshape(sections, sub, size, rows), line, s_index, into)
        parts = parts.reshape(micros, own, size, rows).transpose(1, 2, 0, 3)
        return parts.reshape(own, size, micros * rows)

    def settled(parts):
        return jnp.einsum("aj,bjr->bar", order, parts, preferred_element_type=F32).astype(BF16)

    def leave(acts):
        acts = jnp.einsum("aj,bar->bjr", order, acts, preferred_element_type=F32).astype(BF16)
        parts = acts.reshape(own, size, micros, rows).transpose(2, 0, 1, 3)
        parts = turned(parts.reshape(sections, sub, size, rows), s_index, line, outof)
        return parts.reshape(1, held * size, rows)

    def scattered(*kinds):
        moved = [jnp.stack([pick(parts, s_index) for parts in kinds])]
        for mask in range(1, sections):
            pairs = [(s, s ^ mask) for s in range(sections)]
            value = jnp.stack([pick(parts, s_index ^ mask) for parts in kinds])
            moved.append(lax.ppermute(value, "s", pairs))
        moved = jnp.stack(moved)
        return [pick(moved, s_index ^ section) for section in range(sections)]

    def ordered(part):
        return jnp.einsum("aj,fbjk,ck->fbac", order, part, order, preferred_element_type=F32).astype(BF16)

    def gathered(part):
        full = lax.all_gather(part, "t", axis=0, tiled=False)
        return [full[:, f].reshape(own, size, size) for f in range(part.shape[0])]

    def summed(terms):
        total = lax.psum_scatter(terms, "t", scatter_dimension=0, tiled=True)
        return jnp.einsum("aj,bac,ck->bjk", order, total, order, preferred_element_type=F32).astype(BF16)

    rights = right_factor[:, 0].reshape(loops, sections, sub, size, size)
    lefts = left_factor[:, 0].reshape(loops, sections, sub, size, size)
    parts = [ordered(part) for part in scattered(rights[0], lefts[0])]
    current = arriving(inputs)
    current, parts[0] = lax.optimization_barrier((current, parts[0]))
    weights = [(gathered(parts[0][:1])[0], gathered(parts[0][1:])[0])]
    later, weights[0] = lax.optimization_barrier(((rights[1:], lefts[1:], cotangent), weights[0]))
    rights, lefts, cotangent = later
    for loop in range(loops - 1):
        parts.extend(ordered(part) for part in scattered(rights[loop], lefts[loop]))

    current = settled(current)
    grad = settled(arriving(cotangent))
    stored = []
    for layer in range(layers):
        if layer + 1 < layers:
            current, parts[layer + 1] = lax.optimization_barrier((current, parts[layer + 1]))
            weights.append(tuple(gathered(parts[layer + 1])))
        current, saved = forward_layer(current, *weights[layer])
        stored.append(saved)
    outputs = leave(current)

    def returned(loop, factor):
        mine = jnp.stack([sums[loop * sections + section][factor] for section in range(sections)])
        return jnp.stack(scattered(mine)).reshape(1, held, size, size)

    once = 1 + s_index // sections
    sums = [None] * layers

    def backward_pair(first):
        def run(_, carry):
            grad, *factors = carry
            terms = []
            for step in range(PAIRED):
                right, left = factors[2 * step : 2 * step + 2]
                grad, right_term, left_term = backward_layer(grad, right, left, stored[first - step])
                terms += [right_term, left_term]
            return (grad, *terms)

        return run

    layer = layers - 1
    while layer >= PAIRED:
        factors = [factor for step in range(PAIRED) for factor in weights[layer - step]]
        grad, *terms = lax.fori_loop(0, once, backward_pair(layer), (grad, *factors))
        for step in range(PAIRED):
            sums[layer - step] = [summed(term) for term in terms[2 * step : 2 * step + 2]]
        layer -= PAIRED
    while layer >= 0:
        grad, right_term, left_term = backward_layer(grad, *weights[layer], stored[layer])
        sums[layer] = [summed(right_term), summed(left_term)]
        layer -= 1
    input_grad = leave(grad)
    halves = [jnp.stack([returned(loop, factor) for factor in range(2)]) for loop in range(loops)]
    grads = jnp.stack(halves).astype(F32)
    return (outputs, input_grad, grads[:, 0], grads[:, 1])


def solution(mesh):
    sections = mesh.shape["section"]
    peers = mesh.shape["block"] // GROUPS
    grouped = Mesh(mesh.devices.reshape(sections, GROUPS, peers), ("s", "t", "x"))
    acts = P("s", ("t", "x"), None)
    factor = P(None, "s", ("t", "x"), None, None)
    return jax.shard_map(
        body,
        mesh=grouped,
        in_specs=(acts, acts, factor, factor),
        out_specs=(acts, acts, factor, factor),
        check_vma=False,
    )
```

time: 844 us -> 845 us (level)
  blocking collectives: 0 us -> 128 us
  waiting for transfers between devices: 451 us -> 323 us
  starting transfers between devices: 169 us -> 149 us
  other arithmetic: 9.61 us -> 27.8 us
    all_to_all x32 -> x24, waiting for transfers between devices: 273 us -> 114 us  [exchange(): lax.all_to_all(pieces, WIDE, split_axis=0, concat_axis=0, tiled=True)]
    all_to_all x0 -> x8, blocking collectives: none -> 96.9 us  [exchange(): lax.all_to_all(pieces, WIDE, split_axis=0, concat_axis=0, tiled=True)]
    reduce_scatter x4 -> x16, waiting for transfers between devices: 23 us -> 119 us  [summed(): total = lax.psum_scatter(terms, 't', scatter_dimension=0, tiled=True)]
    all_gather x0 -> x2, blocking collectives: none -> 31.5 us  [gathered(): full = lax.all_gather(part, 't', axis=0, tiled=False)]
    all_to_all x32 -> x24, starting transfers between devices: 133 us -> 104 us  [exchange(): lax.all_to_all(pieces, WIDE, split_axis=0, concat_axis=0, tiled=True)]
    all_gather x4 -> x7, waiting for transfers between devices: 53 us -> 27.3 us  [gathered(): full = lax.all_gather(part, 't', axis=0, tiled=False)]
    transpose x10 -> x0, local copies, waits for them, and re-layouts: 25.4 us -> none  [the longest x4 12.7 us: summed(): terms.reshape(terms.shape[:2] + (groups, sub, size, size))]
    ppermute x16, waiting for transfers between devices: 61.3 us -> 38.5 us  [turned(): moved.append(lax.ppermute(pick(parts, send_by ^ mask), ('s', 't'), pairs))]
  transfers between devices with their start and end apart: 68 -> 81, of which waited for: 49 -> 43; matrix products, arithmetic and copies ran while one was open for 15% -> 20% of each run, Pallas kernels for 0% -> 0%
where the time goes in v9:
time: 845 us; the launch traced here: 833 us
  waiting for transfers between devices  323 us (38%)
  starting transfers between devices  149 us (18%)
  blocking collectives  128 us (15%)
  local copies, waits for them, and re-layouts  103 us (12%)
  matrix products  83.3 us (10%)
  other arithmetic  27.8 us (3%)
  between operations  16.6 us (2%)
    reduce_scatter x16, waiting for transfers between devices, summed(): total = lax.psum_scatter(terms, 't', scatter_dimension=0, tiled=True)  119 us
    all_to_all x24, waiting for transfers between devices, exchange(): lax.all_to_all(pieces, WIDE, split_axis=0, concat_axis=0, tiled=True)  114 us
    all_to_all x24, starting transfers between devices, exchange(): lax.all_to_all(pieces, WIDE, split_axis=0, concat_axis=0, tiled=True)  104 us
    all_to_all x8, blocking collectives, exchange(): lax.all_to_all(pieces, WIDE, split_axis=0, concat_axis=0, tiled=True)  96.9 us
    ppermute x16, waiting for transfers between devices, turned(): moved.append(lax.ppermute(pick(parts, send_by ^ mask), ('s', 't'), pairs))  38.5 us
    all_gather x2, blocking collectives, gathered(): full = lax.all_gather(part, 't', axis=0, tiled=False)  31.5 us
    all_gather x7, waiting for transfers between devices, gathered(): full = lax.all_gather(part, 't', axis=0, tiled=False)  27.3 us
    reshape x28, local copies, waits for them, and re-layouts, exchange(): pieces = values.transpose(1, 0, 2).reshape(full // own, own, own, rows)  23.1 us
  transfers between devices with their start and end apart: 81, of which 43 were waited for; matrix products, arithmetic and copies ran while one was open for 20% of the time, Pallas kernels for 0%

profile of v9, /device:TPU:0, one launch (start us, length us, event | category | flops | bytes accessed | tf_op | source)
XLA Modules:
  0.0 832.6 jit_solution(7524333427461105011)
XLA Ops:
  9.1 7.5 collective-permute-start.3
  24.7 7.9 collective-permute-start.5
  32.6 4.3 collective-permute-done.2
  42.5 16.2 %all-gather.1 = bf16[4,4,128,128]{3,2,1,0:T(8,128)(2,1)S(1)} all-gather(bf16[1,4,128,128]{3,2,1,0:T(8,128)(2,1)S(1)} %get-tuple-element.516), channel_id=3, replica_groups=mesh['s'=4,'t'=4,'x'=2] {'t'}, dimensions={0}, use_global_device_ids=true | all-gather | bytes 655360 | tf_op jit(solution)/shard_map/all_gather | solution.py:114
  58.7 15.3 %all-gather = bf16[4,4,128,128]{3,2,1,0:T(8,128)(2,1)S(1)} all-gather(bf16[1,4,128,128]{3,2,1,0:T(8,128)(2,1)S(1)} %get-tuple-element.517), channel_id=2, replica_groups=mesh['s'=4,'t'=4,'x'=2] {'t'}, dimensions={0}, use_global_device_ids=true | all-gather | bytes 655360 | tf_op jit(solution)/shard_map/all_gather | solution.py:114
  76.2 4.2 all-to-all-start.12
  81.1 8.5 %all-to-all-done.12 = bf16[8,16,16,128]{3,1,2,0:T(8,128)(2,1)S(1)} async-done(((bf16[8,16,16,128]{3,1,2,0:T(8,128)(2,1)}), bf16[8,16,16,128]{3,1,2,0:T(8,128)(2,1)S(1)}, u32[]{:S(2)}, u32[]{:S(2)}) %all-to-all-start.12) | async-done | bytes 524320 | tf_op jit(solution)/shard_map/all_to_all | solution.py:27
  98.1 8.0 all-to-all-done.13
  119.9 7.5 all-to-all-done.14
  155.9 5.3 all-to-all-done.16
  166.9 4.7 collective-permute-done.9
  184.1 12.7 %all_to_all.172 = bf16[8,16,16,128]{3,1,2,0:T(8,128)(2,1)S(1)} all-to-all(bf16[8,16,16,128]{3,1,2,0:T(8,128)(2,1)S(1)} %copy.293), channel_id=1, replica_groups=mesh['s'=4,'t'=4,'x'=2] {'s','x'}, dimensions={0} | all-to-all | bytes 1048576 | tf_op jit(solution)/shard_map/all_to_all | solution.py:27
  203.6 8.1 all-gather.23.cloned.1.call-done
  223.7 8.7 %all-to-all-done.20 = bf16[8,16,16,128]{3,1,2,0:T(8,128)(2,1)S(1)} async-done(((bf16[8,16,16,128]{3,1,2,0:T(8,128)(2,1)}), bf16[8,16,16,128]{3,1,2,0:T(8,128)(2,1)S(1)}, u32[]{:S(2)}, u32[]{:S(2)}) %all-to-all-start.20) | async-done | bytes 524320 | tf_op jit(solution)/shard_map/all_to_all | solution.py:27
  239.2 8.0 all-to-all-done.21
  255.1 12.7 %all_to_all.173 = bf16[8,16,16,128]{3,1,2,0:T(8,128)(2,1)S(1)} all-to-all(bf16[8,16,16,128]{3,1,2,0:T(8,128)(2,1)S(1)} %copy.311), channel_id=1, replica_groups=mesh['s'=4,'t'=4,'x'=2] {'s','x'}, dimensions={0} | all-to-all | bytes 1048576 | tf_op jit(solution)/shard_map/all_to_all | solution.py:27
  274.6 8.1 all-gather.27.cloned.1.call-done
  293.3 8.5 %all-to-all-done.24 = bf16[8,16,16,128]{3,1,2,0:T(8,128)(2,1)S(1)} async-done(((bf16[8,16,16,128]{3,1,2,0:T(8,128)(2,1)}), bf16[8,16,16,128]{3,1,2,0:T(8,128)(2,1)S(1)}, u32[]{:S(2)}, u32[]{:S(2)}) %all-to-all-start.24) | async-done | bytes 524320 | tf_op jit(solution)/shard_map/all_to_all | solution.py:27
  313.8 5.2 collective-permute-done.15
  319.0 21.1 %collective-permute-done.16 = bf16[4,128,128]{1,2,0:T(8,128)(2,1)S(1)} collective-permute-done((bf16[4,128,128]{1,2,0:T(8,128)(2,1)S(1)}, bf16[4,128,128]{1,2,0:T(8,128)(2,1)S(1)}, u32[]{:S(2)}, u32[]{:S(2)}) %collective-permute-start.16) | collective-permute-done | bytes 131104 | tf_op jit(solution)/shard_map/ppermute | solution.py:76
  348.2 9.2 %all-to-all-start.26 = ((bf16[8,16,16,128]{3,1,2,0:T(8,128)(2,1)}), bf16[8,16,16,128]{3,1,2,0:T(8,128)(2,1)}, u32[]{:S(2)}, u32[]{:S(2)}) async-start(bf16[8,16,16,128]{3,1,2,0:T(8,128)(2,1)} %copy.328), calls=%async_computation.26 | async-start | bytes 1048576 | tf_op jit(solution)/shard_map/all_to_all | solution.py:27
  368.7 58.1 %while.54 = (s32[]{:T(128)}, bf16[16,128,128]{2,1,0:T(8,128)(2,1)S(1)}, bf16[16,128,128]{1,2,0:T(8,128)(2,1)S(1)}, bf16[16,128,128]{2,1,0:T(8,128)(2,1)}, bf16[1...) while((s32[]{:T(128)}, ...), condition=%wide.region_1.2_spmd, body=%wide.region_0.1_spmd.sunk | while | flops 547880960 | bytes 34603272 | solution.py:165
  369.1 13.1 %all_to_all.174 = bf16[8,16,16,128]{3,2,1,0:T(8,128)(2,1)S(1)} all-to-all(bf16[8,16,16,128]{3,2,1,0:T(8,128)(2,1)S(1)} %bitcast.1009), channel_id=1, replica_groups=mesh['s'=4,'t'=4,'x'=2] {'s','x'}, dimensions={0} | all-to-all | bytes 1048576 | tf_op jit(solution)/shard_map/while/body/all_to_all | solution.py:27
  384.3 11.7 %all_to_all.175 = bf16[8,16,16,128]{3,1,2,0:T(8,128)(2,1)S(1)} all-to-all(bf16[8,16,16,128]{3,1,2,0:T(8,128)(2,1)S(1)} %copy.528), channel_id=1, replica_groups=mesh['s'=4,'t'=4,'x'=2] {'s','x'}, dimensions={0} | all-to-all | bytes 1048576 | tf_op jit(solution)/shard_map/while/body/all_to_all | solution.py:27
  403.0 6.9 all-to-all-done.2
  420.7 5.3 all-to-all-done.3
  437.7 56.8 %while.55 = (s32[]{:T(128)}, bf16[16,128,128]{2,1,0:T(8,128)(2,1)S(1)}, bf16[16,128,128]{1,2,0:T(8,128)(2,1)S(1)}, bf16[16,128,128]{2,1,0:T(8,128)(2,1)}, bf16[1...) while((s32[]{:T(128)}, ...), condition=%wide.region_3.4_spmd, body=%wide.region_2.3_spmd.sunk | while | flops 547880960 | bytes 36700460 | solution.py:165
  438.1 11.7 %all_to_all.176 = bf16[8,16,16,128]{3,2,1,0:T(8,128)(2,1)S(1)} all-to-all(bf16[8,16,16,128]{3,2,1,0:T(8,128)(2,1)S(1)} %bitcast.1010), channel_id=1, replica_groups=mesh['s'=4,'t'=4,'x'=2] {'s','x'}, dimensions={0} | all-to-all | bytes 1048576 | tf_op jit(solution)/shard_map/while/body/all_to_all | solution.py:27
  451.7 11.7 %all_to_all.177 = bf16[8,16,16,128]{3,1,2,0:T(8,128)(2,1)S(1)} all-to-all(bf16[8,16,16,128]{3,1,2,0:T(8,128)(2,1)S(1)} %copy.536), channel_id=1, replica_groups=mesh['s'=4,'t'=4,'x'=2] {'s','x'}, dimensions={0} | all-to-all | bytes 1048576 | tf_op jit(solution)/shard_map/while/body/all_to_all | solution.py:27
  470.5 6.9 all-to-all-done.6
  488.1 5.2 all-to-all-done.7
  505.7 57.0 %while.56 = (s32[]{:T(128)}, bf16[16,128,128]{2,1,0:T(8,128)(2,1)S(1)}, bf16[16,128,128]{1,2,0:T(8,128)(2,1)S(1)}, bf16[16,128,128]{2,1,0:T(8,128)(2,1)}, bf16[1...) while((s32[]{:T(128)}, ...), condition=%wide.region_5.6_spmd, body=%wide.region_4.5_spmd.sunk | while | flops 547880960 | bytes 36700460 | solution.py:165
  506.3 11.7 %all_to_all.178 = bf16[8,16,16,128]{3,2,1,0:T(8,128)(2,1)S(1)} all-to-all(bf16[8,16,16,128]{3,2,1,0:T(8,128)(2,1)S(1)} %bitcast.1011), channel_id=1, replica_groups=mesh['s'=4,'t'=4,'x'=2] {'s','x'}, dimensions={0} | all-to-all | bytes 1048576 | tf_op jit(solution)/shard_map/while/body/all_to_all | solution.py:27
  519.9 11.7 %all_to_all.179 = bf16[8,16,16,128]{3,1,2,0:T(8,128)(2,1)S(1)} all-to-all(bf16[8,16,16,128]{3,1,2,0:T(8,128)(2,1)S(1)} %copy.544), channel_id=1, replica_groups=mesh['s'=4,'t'=4,'x'=2] {'s','x'}, dimensions={0} | all-to-all | bytes 1048576 | tf_op jit(solution)/shard_map/while/body/all_to_all | solution.py:27
  538.7 6.9 all-to-all-done.10
  556.3 5.2 all-to-all-done.11
  572.4 7.3 all-to-all-done.27
  584.3 8.8 %all-to-all-done.28 = bf16[8,16,16,128]{3,2,1,0:T(8,128)(2,1)} async-done(((bf16[8,16,16,128]{3,2,1,0:T(8,128)(2,1)}), bf16[8,16,16,128]{3,2,1,0:T(8,128)(2,1)}, u32[]{:S(2)}, u32[]{:S(2)}) %all-to-all-start.28) | async-done | bytes 524320 | tf_op jit(solution)/shard_map/all_to_all | solution.py:27
  596.7 4.1 all-to-all-start.29
  607.3 7.4 collective-permute-done.13
  618.4 15.3 %all-to-all-start.30 = ((bf16[8,16,16,128]{3,1,2,0:T(8,128)(2,1)}), bf16[8,16,16,128]{3,1,2,0:T(8,128)(2,1)}, u32[]{:S(2)}, u32[]{:S(2)}) async-start(bf16[8,16,16,128]{3,1,2,0:T(8,128)(2,1)} %copy.360), calls=%async_computation.30 | async-start | bytes 1048576 | tf_op jit(solution)/shard_map/all_to_all | solution.py:27
  653.4 19.2 %reduce-scatter.23.cloned.1.call-done = bf16[4,128,128]{1,2,0:T(8,128)(2,1)} async-done(((bf16[16,128,128]{1,2,0:T(8,128)(2,1)}), bf16[4,128,128]{1,2,0:T(8,128)(2,1)}) %reduce-scatter.23.cloned.1.call-update) | async-done | bytes 131088 | tf_op jit(solution)/shard_map/reduce_scatter | solution.py:118
  673.9 20.7 %reduce-scatter.31.cloned.1.call-done = bf16[4,128,128]{2,1,0:T(8,128)(2,1)} async-done(((bf16[16,128,128]{2,1,0:T(8,128)(2,1)}), bf16[4,128,128]{2,1,0:T(8,128)(2,1)}) %reduce-scatter.31.cloned.1.call-update) | async-done | bytes 131088 | tf_op jit(solution)/shard_map/reduce_scatter | solution.py:118
  696.6 20.2 %reduce-scatter.21.cloned.1.call-done = bf16[4,128,128]{1,2,0:T(8,128)(2,1)} async-done(((bf16[16,128,128]{1,2,0:T(8,128)(2,1)}), bf16[4,128,128]{1,2,0:T(8,128)(2,1)}) %reduce-scatter.21.cloned.1.call-update) | async-done | bytes 131088 | tf_op jit(solution)/shard_map/reduce_scatter | solution.py:118
  732.8 6.1 reduce-scatter.27.cloned.1.call-done
  746.6 18.6 %reduce-scatter.19.cloned.1.call-done = bf16[4,128,128]{2,1,0:T(8,128)(2,1)} async-done(((bf16[16,128,128]{2,1,0:T(8,128)(2,1)}), bf16[4,128,128]{2,1,0:T(8,128)(2,1)}) %reduce-scatter.19.cloned.1.call-update) | async-done | bytes 131088 | tf_op jit(solution)/shard_map/reduce_scatter | solution.py:118
  767.9 22.0 %reduce-scatter.25.cloned.1.call-done = bf16[4,128,128]{2,1,0:T(8,128)(2,1)} async-done(((bf16[16,128,128]{2,1,0:T(8,128)(2,1)}), bf16[4,128,128]{2,1,0:T(8,128)(2,1)}) %reduce-scatter.25.cloned.1.call-update) | async-done | bytes 131088 | tf_op jit(solution)/shard_map/reduce_scatter | solution.py:118
  800.1 12.6 %reduce-scatter.17.cloned.1.call-done = bf16[4,128,128]{2,1,0:T(8,128)(2,1)} async-done(((bf16[16,128,128]{2,1,0:T(8,128)(2,1)}), bf16[4,128,128]{2,1,0:T(8,128)(2,1)}) %reduce-scatter.17.cloned.1.call-update) | async-done | bytes 131088 | tf_op jit(solution)/shard_map/reduce_scatter | solution.py:118
  (589 shorter events, 353.6 us)
Async XLA Ops:
  8.4 15.0 %collective-permute-start = (bf16[4,128,128]{2,1,0:T(8,128)(2,1)S(1)}, bf16[4,128,128]{2,1,0:T(8,128)(2,1)S(1)}, u32[]{:S(2)}, u32[]{:S(2)}) collective-permute-start(bf16[4,128,128]{2,1,0:T(8,128)(2,1)S(1)} %get-tuple-element.512), channel_id=1, source_target_pairs={{0,0},{2,8},{4,16},{6,24},{8,2},{10,10},{12,18},{14,26},{16,4},{18... | collective-permute-start | bytes 393224 | tf_op jit(solution)/shard_map/ppermute | solution.py:76
  9.1 15.6 %collective-permute-start.3 = (bf16[4,128,128]{2,1,0:T(8,128)(2,1)S(1)}, bf16[4,128,128]{2,1,0:T(8,128)(2,1)S(1)}, u32[]{:S(2)}, u32[]{:S(2)}) collective-permute-start(bf16[4,128,128]{2,1,0:T(8,128)(2,1)S(1)} %get-tuple-element.513), channel_id=1, source_target_pairs={{0,24},{2,16},{4,8},{6,0},{8,26},{10,18},{12,10},{14,2},{16,28},{1... | collective-permute-start | bytes 393224 | tf_op jit(solution)/shard_map/ppermute | solution.py:76
  16.6 20.2 %collective-permute-start.2 = (bf16[4,128,128]{2,1,0:T(8,128)(2,1)S(1)}, bf16[4,128,128]{2,1,0:T(8,128)(2,1)}, u32[]{:S(2)}, u32[]{:S(2)}) collective-permute-start(bf16[4,128,128]{2,1,0:T(8,128)(2,1)S(1)} %get-tuple-element.514), channel_id=1, source_target_pairs={{0,16},{2,24},{4,0},{6,8},{8,18},{10,26},{12,2},{14,10},{16,20},{1... | collective-permute-start | bytes 393224 | tf_op jit(solution)/shard_map/ppermute | solution.py:76
  17.3 19.6 %collective-permute-start.1 = (bf16[4,128,128]{2,1,0:T(8,128)(2,1)S(1)}, bf16[4,128,128]{2,1,0:T(8,128)(2,1)}, u32[]{:S(2)}, u32[]{:S(2)}) collective-permute-start(bf16[4,128,128]{2,1,0:T(8,128)(2,1)S(1)} %get-tuple-element.515), channel_id=1, source_target_pairs={{0,8},{2,0},{4,24},{6,16},{8,10},{10,2},{12,26},{14,18},{16,12},{1... | collective-permute-start | bytes 393224 | tf_op jit(solution)/shard_map/ppermute | solution.py:76
  20.7 17.4 %collective-permute-start.6 = (bf16[2,4,128,128]{2,3,1,0:T(8,128)(2,1)S(1)}, bf16[2,4,128,128]{2,3,1,0:T(8,128)(2,1)S(1)}, u32[]{:S(2)}, u32[]{:S(2)}) collective-permute-start(bf16[2,4,128,128]{2,3,1,0:T(8,128)(2,1)S(1)} %pad_maximum_fusion.24), channel_id=1, source_target_pairs={{0,24},{8,16},{16,8},{24,0},{1,25},{9,17},{17,9},{25,1},{2,26},{10... | collective-permute-start | bytes 786440 | tf_op jit(solution)/shard_map/ppermute | solution.py:106
  24.7 15.6 %collective-permute-start.5 = (bf16[2,4,128,128]{2,3,1,0:T(8,128)(2,1)S(1)}, bf16[2,4,128,128]{2,3,1,0:T(8,128)(2,1)S(1)}, u32[]{:S(2)}, u32[]{:S(2)}) collective-permute-start(bf16[2,4,128,128]{2,3,1,0:T(8,128)(2,1)S(1)} %pad_maximum_fusion.23), channel_id=1, source_target_pairs={{0,16},{8,24},{16,0},{24,8},{1,17},{9,25},{17,1},{25,9},{2,18},{10... | collective-permute-start | bytes 786440 | tf_op jit(solution)/shard_map/ppermute | solution.py:106
  80.3 30.7 %all-gather.17.cloned.1.call-start = ((), (), s32[]{:S(2)}) async-start(), calls=%async_computation.64 | async-start | bytes 1310720 | tf_op jit(solution)/shard_map/all_gather | solution.py:114
  96.9 43.1 %all-gather.19.cloned.1.call-start = ((), (), s32[]{:S(2)}) async-start(), calls=%async_computation.65 | async-start | bytes 1310720 | tf_op jit(solution)/shard_map/all_gather | solution.py:114
  151.9 30.3 %all-gather.21.cloned.1.call-start = ((), (), s32[]{:S(2)}) async-start(), calls=%async_computation.66 | async-start | bytes 1310720 | tf_op jit(solution)/shard_map/all_gather | solution.py:114
  155.8 15.7 %collective-permute-start.9 = (bf16[2,4,128,128]{2,3,1,0:T(8,128)(2,1)S(1)}, bf16[2,4,128,128]{2,3,1,0:T(8,128)(2,1)}, u32[]{:S(2)}, u32[]{:S(2)}) collective-permute-start(bf16[2,4,128,128]{2,3,1,0:T(8,128)(2,1)S(1)} %pad_maximum_fusion.27), channel_id=1, source_target_pairs={{0,24},{8,16},{16,8},{24,0},{1,25},{9,17},{17,9},{25,1},{2,26},{10... | collective-permute-start | bytes 786440 | tf_op jit(solution)/shard_map/ppermute | solution.py:106
  166.7 45.0 %all-gather.23.cloned.1.call-start = ((), (), s32[]{:S(2)}) async-start(), calls=%async_computation.67 | async-start | bytes 1310720 | tf_op jit(solution)/shard_map/all_gather | solution.py:114
  223.1 30.1 %all-gather.25.cloned.1.call-start = ((), (), s32[]{:S(2)}) async-start(), calls=%async_computation.68 | async-start | bytes 1310720 | tf_op jit(solution)/shard_map/all_gather | solution.py:114
  238.0 44.7 %all-gather.27.cloned.1.call-start = ((), (), s32[]{:S(2)}) async-start(), calls=%async_computation.69 | async-start | bytes 1310720 | tf_op jit(solution)/shard_map/all_gather | solution.py:114
  269.9 14.9 %all-to-all-start.23 = ((bf16[8,16,16,128]{3,2,1,0:T(8,128)(2,1)}), bf16[8,16,16,128]{3,2,1,0:T(8,128)(2,1)S(1)}, u32[]{:S(2)}, u32[]{:S(2)}) async-start(bf16[8,16,16,128]{3,2,1,0:T(8,128)(2,1)} %copy.313), calls=%async_computation.23 | async-start | bytes 1048576 | tf_op jit(solution)/shard_map/all_to_all | solution.py:27
  292.5 51.3 %all-gather.29.cloned.1.call-start = ((), (), s32[]{:S(2)}) async-start(), calls=%async_computation.70 | async-start | bytes 1310720 | tf_op jit(solution)/shard_map/all_gather | solution.py:114
  303.9 37.0 %all-to-all-start.25 = ((bf16[8,16,16,128]{3,2,1,0:T(8,128)(2,1)}), bf16[8,16,16,128]{3,2,1,0:T(8,128)(2,1)S(1)}, u32[]{:S(2)}, u32[]{:S(2)}) async-start(bf16[8,16,16,128]{3,2,1,0:T(8,128)(2,1)} %copy.322), calls=%async_computation.25 | async-start | bytes 1048576 | tf_op jit(solution)/shard_map/all_to_all | solution.py:27
  308.5 31.6 %collective-permute-start.16 = (bf16[4,128,128]{1,2,0:T(8,128)(2,1)S(1)}, bf16[4,128,128]{1,2,0:T(8,128)(2,1)S(1)}, u32[]{:S(2)}, u32[]{:S(2)}) collective-permute-start(bf16[4,128,128]{1,2,0:T(8,128)(2,1)S(1)} %bitcast.1153), channel_id=1, source_target_pairs={{0,16},{2,24},{4,0},{6,8},{8,18},{10,26},{12,2},{14,10},{16,20},{1... | collective-permute-start | bytes 393224 | tf_op jit(solution)/shard_map/ppermute | solution.py:76
  311.5 28.6 %collective-permute-start.17 = (bf16[4,128,128]{1,2,0:T(8,128)(2,1)S(1)}, bf16[4,128,128]{1,2,0:T(8,128)(2,1)S(1)}, u32[]{:S(2)}, u32[]{:S(2)}) collective-permute-start(bf16[4,128,128]{1,2,0:T(8,128)(2,1)S(1)} %bitcast.1152), channel_id=1, source_target_pairs={{0,24},{2,16},{4,8},{6,0},{8,26},{10,18},{12,10},{14,2},{16,28},{1... | collective-permute-start | bytes 393224 | tf_op jit(solution)/shard_map/ppermute | solution.py:76
  313.1 27.0 %collective-permute-start.14 = (bf16[4,128,128]{1,2,0:T(8,128)(2,1)S(1)}, bf16[4,128,128]{1,2,0:T(8,128)(2,1)S(1)}, u32[]{:S(2)}, u32[]{:S(2)}) collective-permute-start(bf16[4,128,128]{1,2,0:T(8,128)(2,1)S(1)} %bitcast.1151), channel_id=1, source_target_pairs={{0,0},{2,8},{4,16},{6,24},{8,2},{10,10},{12,18},{14,26},{16,4},{18... | collective-permute-start | bytes 393224 | tf_op jit(solution)/shard_map/ppermute | solution.py:76
  348.2 18.5 %all-to-all-start.26 = ((bf16[8,16,16,128]{3,1,2,0:T(8,128)(2,1)}), bf16[8,16,16,128]{3,1,2,0:T(8,128)(2,1)}, u32[]{:S(2)}, u32[]{:S(2)}) async-start(bf16[8,16,16,128]{3,1,2,0:T(8,128)(2,1)} %copy.328), calls=%async_computation.26 | async-start | bytes 1048576 | tf_op jit(solution)/shard_map/all_to_all | solution.py:27
  357.4 278.0 %reduce-scatter.45.cloned.1.call-start = ((), (), s32[]{:S(2)}) async-start(), calls=%async_computation.62 | async-start | bytes 655360 | tf_op jit(solution)/shard_map/reduce_scatter | solution.py:118
  426.9 209.9 %reduce-scatter.47.cloned.1.call-start = ((), (), s32[]{:S(2)}) async-start(), calls=%async_computation.63 | async-start | bytes 655360 | tf_op jit(solution)/shard_map/reduce_scatter | solution.py:118
  437.6 200.5 %reduce-scatter.41.cloned.1.call-start = ((), (), s32[]{:S(2)}) async-start(), calls=%async_computation.60 | async-start | bytes 655360 | tf_op jit(solution)/shard_map/reduce_scatter | solution.py:118
  494.5 145.1 %reduce-scatter.43.cloned.1.call-start = ((), (), s32[]{:S(2)}) async-start(), calls=%async_computation.61 | async-start | bytes 655360 | tf_op jit(solution)/shard_map/reduce_scatter | solution.py:118
  495.2 146.5 %reduce-scatter.39.cloned.1.call-start = ((), (), s32[]{:S(2)}) async-start(), calls=%async_computation.59 | async-start | bytes 655360 | tf_op jit(solution)/shard_map/reduce_scatter | solution.py:118
  495.8 147.3 %reduce-scatter.37.cloned.1.call-start = ((), (), s32[]{:S(2)}) async-start(), calls=%async_computation.58 | async-start | bytes 655360 | tf_op jit(solution)/shard_map/reduce_scatter | solution.py:118
  496.6 147.9 %reduce-scatter.35.cloned.1.call-start = ((), (), s32[]{:S(2)}) async-start(), calls=%async_computation.57 | async-start | bytes 655360 | tf_op jit(solution)/shard_map/reduce_scatter | solution.py:118
  497.1 148.7 %reduce-scatter.33.cloned.1.call-start = ((), (), s32[]{:S(2)}) async-start(), calls=%async_computation.56 | async-start | bytes 655360 | tf_op jit(solution)/shard_map/reduce_scatter | solution.py:118
  505.6 146.4 %reduce-scatter.29.cloned.1.call-start = ((), (), s32[]{:S(2)}) async-start(), calls=%async_computation.54 | async-start | bytes 655360 | tf_op jit(solution)/shard_map/reduce_scatter | solution.py:118
  562.7 109.9 %reduce-scatter.23.cloned.1.call-start = ((), (), s32[]{:S(2)}) async-start(), calls=%async_computation.51 | async-start | bytes 655360 | tf_op jit(solution)/shard_map/reduce_scatter | solution.py:118
  563.5 131.1 %reduce-scatter.31.cloned.1.call-start = ((), (), s32[]{:S(2)}) async-start(), calls=%async_computation.55 | async-start | bytes 655360 | tf_op jit(solution)/shard_map/reduce_scatter | solution.py:118
  570.5 146.3 %reduce-scatter.21.cloned.1.call-start = ((), (), s32[]{:S(2)}) async-start(), calls=%async_computation.50 | async-start | bytes 655360 | tf_op jit(solution)/shard_map/reduce_scatter | solution.py:118
  596.7 19.4 %all-to-all-start.29 = ((bf16[8,16,16,128]{3,1,2,0:T(8,128)(2,1)}), bf16[8,16,16,128]{3,1,2,0:T(8,128)(2,1)}, u32[]{:S(2)}, u32[]{:S(2)}) async-start(bf16[8,16,16,128]{3,1,2,0:T(8,128)(2,1)} %copy.357), calls=%async_computation.29 | async-start | bytes 1048576 | tf_op jit(solution)/shard_map/all_to_all | solution.py:27
  600.8 138.0 %reduce-scatter.27.cloned.1.call-start = ((), (), s32[]{:S(2)}) async-start(), calls=%async_computation.53 | async-start | bytes 655360 | tf_op jit(solution)/shard_map/reduce_scatter | solution.py:118
  618.4 104.5 %all-to-all-start.30 = ((bf16[8,16,16,128]{3,1,2,0:T(8,128)(2,1)}), bf16[8,16,16,128]{3,1,2,0:T(8,128)(2,1)}, u32[]{:S(2)}, u32[]{:S(2)}) async-start(bf16[8,16,16,128]{3,1,2,0:T(8,128)(2,1)} %copy.360), calls=%async_computation.30 | async-start | bytes 1048576 | tf_op jit(solution)/shard_map/all_to_all | solution.py:27
  633.7 131.6 %reduce-scatter.19.cloned.1.call-start = ((), (), s32[]{:S(2)}) async-start(), calls=%async_computation.49 | async-start | bytes 655360 | tf_op jit(solution)/shard_map/reduce_scatter | solution.py:118
  647.4 70.8 %collective-permute-start.30 = (bf16[1,4,128,128]{3,2,1,0:T(8,128)(2,1)S(1)}, bf16[1,4,128,128]{3,2,1,0:T(8,128)(2,1)S(1)}, u32[]{:S(2)}, u32[]{:S(2)}) collective-permute-start(bf16[1,4,128,128]{3,2,1,0:T(8,128)(2,1)S(1)} %get-tuple-element.457), channel_id=1, source_target_pairs={{0,24},{8,16},{16,8},{24,0},{1,25},{9,17},{17,9},{25,1},{2,26},{10... | collective-permute-start | bytes 393224 | tf_op jit(solution)/shard_map/ppermute | solution.py:106
  649.2 69.1 %collective-permute-start.29 = (bf16[1,4,128,128]{3,2,1,0:T(8,128)(2,1)S(1)}, bf16[1,4,128,128]{3,2,1,0:T(8,128)(2,1)S(1)}, u32[]{:S(2)}, u32[]{:S(2)}) collective-permute-start(bf16[1,4,128,128]{3,2,1,0:T(8,128)(2,1)S(1)} %get-tuple-element.458), channel_id=1, source_target_pairs={{0,16},{8,24},{16,0},{24,8},{1,17},{9,25},{17,1},{25,9},{2,18},{10... | collective-permute-start | bytes 393224 | tf_op jit(solution)/shard_map/ppermute | solution.py:106
  649.9 68.4 %collective-permute-start.28 = (bf16[1,4,128,128]{3,2,1,0:T(8,128)(2,1)S(1)}, bf16[1,4,128,128]{3,2,1,0:T(8,128)(2,1)S(1)}, u32[]{:S(2)}, u32[]{:S(2)}) collective-permute-start(bf16[1,4,128,128]{3,2,1,0:T(8,128)(2,1)S(1)} %get-tuple-element.459), channel_id=1, source_target_pairs={{0,8},{8,0},{16,24},{24,16},{1,9},{9,1},{17,25},{25,17},{2,10},{10... | collective-permute-start | bytes 393224 | tf_op jit(solution)/shard_map/ppermute | solution.py:106
  649.9 71.1 %collective-permute-start.33 = (bf16[1,4,128,128]{3,2,1,0:T(8,128)(2,1)}, bf16[1,4,128,128]{3,2,1,0:T(8,128)(2,1)}, u32[]{:S(2)}, u32[]{:S(2)}) collective-permute-start(bf16[1,4,128,128]{3,2,1,0:T(8,128)(2,1)} %get-tuple-element.465), channel_id=1, source_target_pairs={{0,24},{8,16},{16,8},{24,0},{1,25},{9,17},{17,9},{25,1},{2,26},{10... | collective-permute-start | bytes 393224 | tf_op jit(solution)/shard_map/ppermute | solution.py:106
  651.3 69.7 %collective-permute-start.32 = (bf16[1,4,128,128]{3,2,1,0:T(8,128)(2,1)S(1)}, bf16[1,4,128,128]{3,2,1,0:T(8,128)(2,1)}, u32[]{:S(2)}, u32[]{:S(2)}) collective-permute-start(bf16[1,4,128,128]{3,2,1,0:T(8,128)(2,1)S(1)} %get-tuple-element.466), channel_id=1, source_target_pairs={{0,16},{8,24},{16,0},{24,8},{1,17},{9,25},{17,1},{25,9},{2,18},{10... | collective-permute-start | bytes 393224 | tf_op jit(solution)/shard_map/ppermute | solution.py:106
  725.5 15.3 %all-to-all-start.31 = ((bf16[8,16,16,128]{3,2,1,0:T(8,128)(2,1)}), bf16[8,16,16,128]{3,2,1,0:T(8,128)(2,1)S(1)}, u32[]{:S(2)}, u32[]{:S(2)}) async-start(bf16[8,16,16,128]{3,2,1,0:T(8,128)(2,1)} %copy.362), calls=%async_computation.31 | async-start | bytes 1048576 | tf_op jit(solution)/shard_map/all_to_all | solution.py:27
  729.2 60.6 %reduce-scatter.25.cloned.1.call-start = ((), (), s32[]{:S(2)}) async-start(), calls=%async_computation.52 | async-start | bytes 655360 | tf_op jit(solution)/shard_map/reduce_scatter | solution.py:118
  730.6 82.1 %reduce-scatter.17.cloned.1.call-start = ((), (), s32[]{:S(2)}) async-start(), calls=%async_computation.48 | async-start | bytes 655360 | tf_op jit(solution)/shard_map/reduce_scatter | solution.py:118
  742.1 24.5 %collective-permute-start.21 = (bf16[4,128,128]{2,1,0:T(8,128)(2,1)S(1)}, bf16[4,128,128]{2,1,0:T(8,128)(2,1)S(1)}, u32[]{:S(2)}, u32[]{:S(2)}) collective-permute-start(bf16[4,128,128]{2,1,0:T(8,128)(2,1)S(1)} %bitcast.1159), channel_id=1, source_target_pairs={{0,6},{2,14},{4,22},{6,30},{8,4},{10,12},{12,20},{14,28},{16,2},{1... | collective-permute-start | bytes 393224 | tf_op jit(solution)/shard_map/ppermute | solution.py:76
  742.5 24.1 %collective-permute-start.19 = (bf16[4,128,128]{2,1,0:T(8,128)(2,1)S(1)}, bf16[4,128,128]{2,1,0:T(8,128)(2,1)}, u32[]{:S(2)}, u32[]{:S(2)}) collective-permute-start(bf16[4,128,128]{2,1,0:T(8,128)(2,1)S(1)} %bitcast.1157), channel_id=1, source_target_pairs={{0,2},{2,10},{4,18},{6,26},{8,0},{10,8},{12,16},{14,24},{16,6},{18... | collective-permute-start | bytes 393224 | tf_op jit(solution)/shard_map/ppermute | solution.py:76
  742.5 24.1 %collective-permute-start.20 = (bf16[4,128,128]{2,1,0:T(8,128)(2,1)S(1)}, bf16[4,128,128]{2,1,0:T(8,128)(2,1)}, u32[]{:S(2)}, u32[]{:S(2)}) collective-permute-start(bf16[4,128,128]{2,1,0:T(8,128)(2,1)S(1)} %bitcast.1156), channel_id=1, source_target_pairs={{0,4},{2,12},{4,20},{6,28},{8,6},{10,14},{12,22},{14,30},{16,0},{1... | collective-permute-start | bytes 393224 | tf_op jit(solution)/shard_map/ppermute | solution.py:76
  744.0 22.7 %collective-permute-start.18 = (bf16[4,128,128]{2,1,0:T(8,128)(2,1)S(1)}, bf16[4,128,128]{2,1,0:T(8,128)(2,1)}, u32[]{:S(2)}, u32[]{:S(2)}) collective-permute-start(bf16[4,128,128]{2,1,0:T(8,128)(2,1)S(1)} %bitcast.1154), channel_id=1, source_target_pairs={{0,0},{2,8},{4,16},{6,24},{8,2},{10,10},{12,18},{14,26},{16,4},{18... | collective-permute-start | bytes 393224 | tf_op jit(solution)/shard_map/ppermute | solution.py:76
  (115 other events, 1500.6 us)
Sparse Core Ops, SparseCore 0:
  82.7 28.2 all-gather.16
  112.6 27.4 all-gather.18
  154.3 27.8 all-gather.20
  184.2 27.4 all-gather.22
  225.2 27.9 all-gather.24
  255.2 27.4 all-gather.26
  294.9 44.7 all-gather.28
  427.0 18.4 reduce-scatter.44
  448.4 19.9 reduce-scatter.46
  494.6 18.4 reduce-scatter.40
  515.4 19.8 reduce-scatter.42
  537.5 19.7 reduce-scatter.38
  559.6 19.9 reduce-scatter.36
  581.7 19.7 reduce-scatter.34
  603.6 24.5 reduce-scatter.32
  630.3 20.0 reduce-scatter.28
  652.6 19.9 reduce-scatter.22
  674.7 19.8 reduce-scatter.30
  696.9 19.8 reduce-scatter.20
  718.9 19.8 reduce-scatter.26
  741.1 24.1 reduce-scatter.18
  768.1 21.6 reduce-scatter.24
  792.7 19.9 reduce-scatter.16

commit v10 on v9

--- a/solution.py
+++ b/solution.py
@@ -114,64 +114,98 @@
         full = lax.all_gather(part, "t", axis=0, tiled=False)
         return [full[:, f].reshape(own, size, size) for f in range(part.shape[0])]
 
+    def around(value_of):
+        moved = [value_of(0)]
+        for mask in range(1, groups):
+            moved.append(lax.ppermute(value_of(mask), "t", [(t, t ^ mask) for t in range(groups)]))
+        return moved
+
+    def gathered_directly(part):
+        moved = jnp.stack(around(lambda mask: part))
+        return jnp.concatenate([pick(moved, t_index ^ group) for group in range(groups)])
+
+    def unordered(total):
+        return jnp.einsum("aj,fbac,ck->fbjk", order, total, order, preferred_element_type=F32).astype(BF16)
+
     def summed(terms):
-        total = lax.psum_scatter(terms, "t", scatter_dimension=0, tiled=True)
-        return jnp.einsum("aj,bac,ck->bjk", order, total, order, preferred_element_type=F32).astype(BF16)
+        total = lax.psum_scatter(terms.reshape(-1, size, size), "t", scatter_dimension=0, tiled=True)
+        return unordered(total.reshape(terms.shape[1:]))
+
+    def summed_directly(term):
+        parts = term.reshape(groups, sub, size, size)
+        moved = around(lambda mask: pick(parts, t_index ^ mask))
+        return unordered(sum(one.astype(F32) for one in moved).astype(BF16)[None])
+
+    def laid_out(*terms):
+        return jnp.stack([term.reshape(groups, sub, size, size) for term in terms], axis=1)
 
     rights = right_factor[:, 0].reshape(loops, sections, sub, size, size)
     lefts = left_factor[:, 0].reshape(loops, sections, sub, size, size)
     parts = [ordered(part) for part in scattered(rights[0], lefts[0])]
     current = arriving(inputs)
     current, parts[0] = lax.optimization_barrier((current, parts[0]))
-    weights = [(gathered(parts[0][:1])[0], gathered(parts[0][1:])[0])]
-    later, weights[0] = lax.optimization_barrier(((rights[1:], lefts[1:], cotangent), weights[0]))
-    rights, lefts, cotangent = later
+    weights = [(gathered_directly(parts[0][0]), gathered_directly(parts[0][1]))]
+    later, right = lax.optimization_barrier(((rights[1:], lefts[1:]), weights[0][0]))
+    rights, lefts = later
+    weights[0] = (right, weights[0][1])
     for loop in range(loops - 1):
         parts.extend(ordered(part) for part in scattered(rights[loop], lefts[loop]))
 
     current = settled(current)
-    grad = settled(arriving(cotangent))
     stored = []
     for layer in range(layers):
         if layer + 1 < layers:
             current, parts[layer + 1] = lax.optimization_barrier((current, parts[layer + 1]))
             weights.append(tuple(gathered(parts[layer + 1])))
+        else:
+            current, cotangent = lax.optimization_barrier((current, cotangent))
+            grad = settled(arriving(cotangent))
         current, saved = forward_layer(current, *weights[layer])
         stored.append(saved)
     outputs = leave(current)
 
-    def returned(loop, factor):
-        mine = jnp.stack([sums[loop * sections + section][factor] for section in range(sections)])
-        return jnp.stack(scattered(mine)).reshape(1, held, size, size)
-
     once = 1 + s_index // sections
     sums = [None] * layers
 
     def backward_pair(first):
         def run(_, carry):
-            grad, *factors = carry
+            grad, _ = carry
             terms = []
-            for step in range(PAIRED):
-                right, left = factors[2 * step : 2 * step + 2]
-                grad, right_term, left_term = backward_layer(grad, right, left, stored[first - step])
-                terms += [right_term, left_term]
-            return (grad, *terms)
+            for layer in range(first, first - PAIRED, -1):
+                grad, *pair = backward_layer(grad, *weights[layer], stored[layer])
+                terms += pair
+            return grad, laid_out(*terms)
 
         return run
 
     layer = layers - 1
     while layer >= PAIRED:
-        factors = [factor for step in range(PAIRED) for factor in weights[layer - step]]
-        grad, *terms = lax.fori_loop(0, once, backward_pair(layer), (grad, *factors))
+        blank = jnp.zeros((groups, 2 * PAIRED, sub, size, size), BF16)
+        grad, terms = lax.fori_loop(0, once, backward_pair(layer), (grad, blank))
+        total = summed(terms)
         for step in range(PAIRED):
-            sums[layer - step] = [summed(term) for term in terms[2 * step : 2 * step + 2]]
+            sums[layer - step] = [total[2 * step], total[2 * step + 1]]
         layer -= PAIRED
     while layer >= 0:
         grad, right_term, left_term = backward_layer(grad, *weights[layer], stored[layer])
-        sums[layer] = [summed(right_term), summed(left_term)]
+        if layer:
+            total = summed(laid_out(right_term, left_term))
+            sums[layer] = [total[0], total[1]]
+        else:
+            sums[layer] = [summed_directly(right_term)[0], summed(laid_out(left_term))[0]]
         layer -= 1
     input_grad = leave(grad)
-    halves = [jnp.stack([returned(loop, factor) for factor in range(2)]) for loop in range(loops)]
+
+    def of_loop(loop, factor):
+        return jnp.stack([sums[loop * sections + section][factor] for section in range(sections)])
+
+    halves = []
+    for loop in range(loops):
+        if loop:
+            moved = jnp.stack(scattered(of_loop(loop, 0), of_loop(loop, 1)), axis=1)
+        else:
+            moved = jnp.stack([jnp.stack(scattered(of_loop(loop, factor)))[:, 0] for factor in range(2)])
+        halves.append(moved.reshape(2, 1, held, size, size))
     grads = jnp.stack(halves).astype(F32)
     return (outputs, input_grad, grads[:, 0], grads[:, 1])
 

time: 845 us -> 867 us (1.026)
  local copies, waits for them, and re-layouts: 103 us -> 131 us
  starting transfers between devices: 149 us -> 161 us
  blocking collectives: 128 us -> 117 us
    ppermute x0 -> x9, waiting for transfers between devices: none -> 37.2 us  [around(): lax.ppermute(value_of(mask), 't', [(t, t ^ mask) for t in range(groups)])]
    ppermute x0 -> x9, starting transfers between devices: none -> 34.6 us  [around(): lax.ppermute(value_of(mask), 't', [(t, t ^ mask) for t in range(groups)])]
    all_gather x2 -> x0, blocking collectives: 31.5 us -> none  [gathered(): full = lax.all_gather(part, 't', axis=0, tiled=False)]
    reduce_scatter x16 -> x5, waiting for transfers between devices: 119 us -> 90.9 us  [summed(): lax.psum_scatter(terms.reshape(-1, size, size), 't', scatter_dimension=0,...]
    all_to_all x24 -> x22, waiting for transfers between devices: 114 us -> 141 us  [exchange(): lax.all_to_all(pieces, WIDE, split_axis=0, concat_axis=0, tiled=True)]
    ppermute x16, waiting for transfers between devices: 38.5 us -> 12.6 us  [turned(): moved.append(lax.ppermute(pick(parts, send_by ^ mask), ('s', 't'), pairs))]
    all_to_all x8 -> x10, blocking collectives: 96.9 us -> 117 us  [exchange(): lax.all_to_all(pieces, WIDE, split_axis=0, concat_axis=0, tiled=True)]
    all_gather x7, waiting for transfers between devices: 27.3 us -> 9.49 us  [gathered(): full = lax.all_gather(part, 't', axis=0, tiled=False)]
  transfers between devices with their start and end apart: 81 -> 74, of which waited for: 43 -> 40; matrix products, arithmetic and copies ran while one was open for 20% -> 19% of each run, Pallas kernels for 0% -> 0%
where the time goes in v10:
time: 867 us; the launch traced here: 854 us
  waiting for transfers between devices  319 us (37%)
  starting transfers between devices  161 us (19%)
  local copies, waits for them, and re-layouts  131 us (15%)
  blocking collectives  117 us (13%)
  matrix products  75 us (9%)
  other arithmetic  33.5 us (4%)
  between operations  16.6 us (2%)
    all_to_all x22, waiting for transfers between devices, exchange(): lax.all_to_all(pieces, WIDE, split_axis=0, concat_axis=0, tiled=True)  141 us
    all_to_all x10, blocking collectives, exchange(): lax.all_to_all(pieces, WIDE, split_axis=0, concat_axis=0, tiled=True)  117 us
    reduce_scatter x5, waiting for transfers between devices, summed(): lax.psum_scatter(terms.reshape(-1, size, size), 't', scatter_dimension=0,...  90.9 us
    all_to_all x22, starting transfers between devices, exchange(): lax.all_to_all(pieces, WIDE, split_axis=0, concat_axis=0, tiled=True)  87.3 us
    ppermute x9, waiting for transfers between devices, around(): lax.ppermute(value_of(mask), 't', [(t, t ^ mask) for t in range(groups)])  37.2 us
    ppermute x9, starting transfers between devices, around(): lax.ppermute(value_of(mask), 't', [(t, t ^ mask) for t in range(groups)])  34.6 us
    while x22, local copies, waits for them, and re-layouts, body(): grad, terms = lax.fori_loop(0, once, backward_pair(layer), (grad, blank))  29.1 us
    unnamed x151, local copies, waits for them, and re-layouts  24.8 us
  transfers between devices with their start and end apart: 74, of which 40 were waited for; matrix products, arithmetic and copies ran while one was open for 19% of the time, Pallas kernels for 0%

profile of v10, /device:TPU:0, one launch (start us, length us, event | category | flops | bytes accessed | tf_op | source)
XLA Modules:
  0.0 853.6 jit_solution(3202678656791276856)
XLA Ops:
  19.4 5.0 collective-permute-start.6
  26.1 5.3 collective-permute-done.2
  32.7 7.1 collective-permute-done.5
  53.4 6.7 collective-permute-done.11
  60.2 5.1 collective-permute-done.8
  72.8 7.9 all-to-all-done.12
  84.1 4.1 all-to-all-start.13
  89.4 8.1 all-to-all-done.13
  110.2 8.5 all-to-all-done.14
  128.4 7.2 all-to-all-done.15
  136.2 4.2 all-gather.17.cloned.1.call-done
  162.5 6.9 collective-permute-done.14
  186.4 8.7 %all-to-all-done.18 = bf16[8,16,16,128]{3,1,2,0:T(8,128)(2,1)S(1)} async-done(((bf16[8,16,16,128]{3,1,2,0:T(8,128)(2,1)}), bf16[8,16,16,128]{3,1,2,0:T(8,128)(2,1)S(1)}, u32[]{:S(2)}, u32[]{:S(2)}) %all-to-all-start.18) | async-done | bytes 524320 | tf_op jit(solution)/shard_map/all_to_all | solution.py:27
  203.6 8.0 all-to-all-done.19
  225.0 8.6 %all-to-all-done.20 = bf16[8,16,16,128]{3,1,2,0:T(8,128)(2,1)S(1)} async-done(((bf16[8,16,16,128]{3,1,2,0:T(8,128)(2,1)}), bf16[8,16,16,128]{3,1,2,0:T(8,128)(2,1)S(1)}, u32[]{:S(2)}, u32[]{:S(2)}) %all-to-all-start.20) | async-done | bytes 524320 | tf_op jit(solution)/shard_map/all_to_all | solution.py:27
  241.4 8.0 all-to-all-done.21
  262.1 8.7 %all-to-all-done.22 = bf16[8,16,16,128]{3,1,2,0:T(8,128)(2,1)S(1)} async-done(((bf16[8,16,16,128]{3,1,2,0:T(8,128)(2,1)}), bf16[8,16,16,128]{3,1,2,0:T(8,128)(2,1)S(1)}, u32[]{:S(2)}, u32[]{:S(2)}) %all-to-all-start.22) | async-done | bytes 524320 | tf_op jit(solution)/shard_map/all_to_all | solution.py:27
  280.1 7.1 all-to-all-done.23
  300.7 8.4 all-to-all-done.24
  311.4 11.7 %all_to_all.172 = bf16[8,16,16,128]{3,2,1,0:T(8,128)(2,1)S(1)} all-to-all(bf16[8,16,16,128]{3,2,1,0:T(8,128)(2,1)S(1)} %copy.346), channel_id=1, replica_groups=mesh['s'=4,'t'=4,'x'=2] {'s','x'}, dimensions={0} | all-to-all | bytes 1048576 | tf_op jit(solution)/shard_map/all_to_all | solution.py:27
  370.8 8.6 %all-to-all-start.26 = ((bf16[8,16,16,128]{3,1,2,0:T(8,128)(2,1)}), bf16[8,16,16,128]{3,1,2,0:T(8,128)(2,1)S(1)}, u32[]{:S(2)}, u32[]{:S(2)}) async-start(bf16[8,16,16,128]{3,1,2,0:T(8,128)(2,1)} %copy.352), calls=%async_computation.26 | async-start | bytes 1048576 | tf_op jit(solution)/shard_map/all_to_all | solution.py:27
  382.9 5.8 all-to-all-done.26
  391.4 60.2 %while.36 = (s32[]{:T(128)}, bf16[16,128,128]{2,1,0:T(8,128)(2,1)S(1)}, bf16[4,4,4,128,128]{3,4,2,0,1:T(8,128)(2,1)}, s32[]{:T(128)}, bf16[16,128,128]{2,1,0:T(8...) while((s32[]{:T(128)}, ...), condition=%wide.region_1.2_spmd, body=%wide.region_0.1_spmd.sunk | while | flops 551026688 | bytes 38797556 | solution.py:184
  391.9 11.7 %all_to_all.176 = bf16[8,16,16,128]{3,2,1,0:T(8,128)(2,1)S(1)} all-to-all(bf16[8,16,16,128]{3,2,1,0:T(8,128)(2,1)S(1)} %bitcast.1014), channel_id=1, replica_groups=mesh['s'=4,'t'=4,'x'=2] {'s','x'}, dimensions={0} | all-to-all | bytes 1048576 | tf_op jit(solution)/shard_map/while/body/all_to_all | solution.py:27
  405.5 11.7 %all_to_all.177 = bf16[8,16,16,128]{3,1,2,0:T(8,128)(2,1)S(1)} all-to-all(bf16[8,16,16,128]{3,1,2,0:T(8,128)(2,1)S(1)} %copy.537), channel_id=1, replica_groups=mesh['s'=4,'t'=4,'x'=2] {'s','x'}, dimensions={0} | all-to-all | bytes 1048576 | tf_op jit(solution)/shard_map/while/body/all_to_all | solution.py:27
  424.7 7.4 all-to-all-done.2
  444.2 3.9 all-to-all-done.3
  453.5 60.0 %while.37 = (s32[]{:T(128)}, bf16[16,128,128]{2,1,0:T(8,128)(2,1)S(1)}, bf16[4,4,4,128,128]{3,4,2,0,1:T(8,128)(2,1)}, s32[]{:T(128)}, bf16[16,128,128]{2,1,0:T(8...) while((s32[]{:T(128)}, ...), condition=%wide.region_3.4_spmd, body=%wide.region_2.3_spmd.sunk | while | flops 551026688 | bytes 36700376 | solution.py:184
  453.8 11.7 %all_to_all.178 = bf16[8,16,16,128]{3,2,1,0:T(8,128)(2,1)S(1)} all-to-all(bf16[8,16,16,128]{3,2,1,0:T(8,128)(2,1)S(1)} %bitcast.1015), channel_id=1, replica_groups=mesh['s'=4,'t'=4,'x'=2] {'s','x'}, dimensions={0} | all-to-all | bytes 1048576 | tf_op jit(solution)/shard_map/while/body/all_to_all | solution.py:27
  467.4 11.7 %all_to_all.179 = bf16[8,16,16,128]{3,1,2,0:T(8,128)(2,1)S(1)} all-to-all(bf16[8,16,16,128]{3,1,2,0:T(8,128)(2,1)S(1)} %copy.547), channel_id=1, replica_groups=mesh['s'=4,'t'=4,'x'=2] {'s','x'}, dimensions={0} | all-to-all | bytes 1048576 | tf_op jit(solution)/shard_map/while/body/all_to_all | solution.py:27
  486.6 7.4 all-to-all-done.6
  515.4 60.2 %while.38 = (s32[]{:T(128)}, bf16[16,128,128]{2,1,0:T(8,128)(2,1)S(1)}, bf16[4,4,4,128,128]{3,4,2,0,1:T(8,128)(2,1)}, s32[]{:T(128)}, bf16[16,128,128]{2,1,0:T(8...) while((s32[]{:T(128)}, ...), condition=%wide.region_5.6_spmd, body=%wide.region_4.5_spmd.sunk | while | flops 551026688 | bytes 36700376 | solution.py:184
  515.9 11.7 %all_to_all.180 = bf16[8,16,16,128]{3,2,1,0:T(8,128)(2,1)S(1)} all-to-all(bf16[8,16,16,128]{3,2,1,0:T(8,128)(2,1)S(1)} %bitcast.1016), channel_id=1, replica_groups=mesh['s'=4,'t'=4,'x'=2] {'s','x'}, dimensions={0} | all-to-all | bytes 1048576 | tf_op jit(solution)/shard_map/while/body/all_to_all | solution.py:27
  529.5 11.7 %all_to_all.181 = bf16[8,16,16,128]{3,1,2,0:T(8,128)(2,1)S(1)} all-to-all(bf16[8,16,16,128]{3,1,2,0:T(8,128)(2,1)S(1)} %copy.557), channel_id=1, replica_groups=mesh['s'=4,'t'=4,'x'=2] {'s','x'}, dimensions={0} | all-to-all | bytes 1048576 | tf_op jit(solution)/shard_map/while/body/all_to_all | solution.py:27
  548.7 7.4 all-to-all-done.10
  575.9 11.8 %all_to_all.173 = bf16[8,16,16,128]{3,2,1,0:T(8,128)(2,1)S(1)} all-to-all(bf16[8,16,16,128]{3,2,1,0:T(8,128)(2,1)S(1)} %bitcast.1121), channel_id=1, replica_groups=mesh['s'=4,'t'=4,'x'=2] {'s','x'}, dimensions={0} | all-to-all | bytes 1048576 | tf_op jit(solution)/shard_map/all_to_all | solution.py:27
  588.2 11.8 %all_to_all.174 = bf16[8,16,16,128]{3,1,2,0:T(8,128)(2,1)S(1)} all-to-all(bf16[8,16,16,128]{3,1,2,0:T(8,128)(2,1)S(1)} %copy.387), channel_id=1, replica_groups=mesh['s'=4,'t'=4,'x'=2] {'s','x'}, dimensions={0} | all-to-all | bytes 1048576 | tf_op jit(solution)/shard_map/all_to_all | solution.py:27
  600.5 11.8 %all_to_all.175 = bf16[8,16,16,128]{3,1,2,0:T(8,128)(2,1)S(1)} all-to-all(bf16[8,16,16,128]{3,1,2,0:T(8,128)(2,1)S(1)} %copy.390), channel_id=1, replica_groups=mesh['s'=4,'t'=4,'x'=2] {'s','x'}, dimensions={0} | all-to-all | bytes 1048576 | tf_op jit(solution)/shard_map/all_to_all | solution.py:27
  627.3 4.1 all-to-all-start.27
  633.9 6.8 all-to-all-done.27
  647.7 6.7 all-to-all-start.31
  656.7 5.0 collective-permute-done.17
  665.5 4.8 collective-permute-start.27
  677.1 9.2 %collective-permute-start.30 = (bf16[4,128,128]{1,2,0:T(8,128)(2,1)S(1)}, bf16[4,128,128]{1,2,0:T(8,128)(2,1)S(1)}, u32[]{:S(2)}, u32[]{:S(2)}) collective-permute-start(bf16[4,128,128]{1,2,0:T(8,128)(2,1)S(1)} %bitcast.1178), channel_id=1, source_target_pairs={{0,6},{2,4},{4,2},{6,0},{1,7},{3,5},{5,3},{7,1},{8,14},{10,12},{12... | collective-permute-start | bytes 393224 | tf_op jit(solution)/shard_map/ppermute | solution.py:120
  686.8 14.0 %collective-permute-start.28 = (bf16[4,128,128]{1,2,0:T(8,128)(2,1)S(1)}, bf16[4,128,128]{1,2,0:T(8,128)(2,1)S(1)}, u32[]{:S(2)}, u32[]{:S(2)}) collective-permute-start(bf16[4,128,128]{1,2,0:T(8,128)(2,1)S(1)} %bitcast.1179), channel_id=1, source_target_pairs={{0,2},{2,0},{4,6},{6,4},{1,3},{3,1},{5,7},{7,5},{8,10},{10,8},{12,... | collective-permute-start | bytes 393224 | tf_op jit(solution)/shard_map/ppermute | solution.py:120
  701.9 25.3 %collective-permute-done.29 = bf16[4,128,128]{1,2,0:T(8,128)(2,1)S(1)} collective-permute-done((bf16[4,128,128]{1,2,0:T(8,128)(2,1)S(1)}, bf16[4,128,128]{1,2,0:T(8,128)(2,1)S(1)}, u32[]{:S(2)}, u32[]{:S(2)}) %collective-permute-start.29) | collective-permute-done | bytes 131104 | tf_op jit(solution)/shard_map/ppermute | solution.py:120
  735.7 45.5 %reduce-scatter.12.cloned.1.call-done = bf16[16,128,128]{2,1,0:T(8,128)(2,1)} async-done(((bf16[64,128,128]{2,1,0:T(8,128)(2,1)}), bf16[16,128,128]{2,1,0:T(8,128)(2,1)}) %reduce-scatter.12.cloned.1.call-update) | async-done | bytes 524304 | tf_op jit(solution)/shard_map/reduce_scatter | solution.py:131
  784.9 41.8 %reduce-scatter.8.cloned.1.call-done = bf16[16,128,128]{2,1,0:T(8,128)(2,1)} async-done(((bf16[64,128,128]{2,1,0:T(8,128)(2,1)}), bf16[16,128,128]{2,1,0:T(8,128)(2,1)}) %reduce-scatter.8.cloned.1.call-update) | async-done | bytes 524304 | tf_op jit(solution)/shard_map/reduce_scatter | solution.py:131
  (560 shorter events, 381.2 us)
Async XLA Ops:
  9.1 16.5 %collective-permute-start.3 = (bf16[4,128,128]{2,1,0:T(8,128)(2,1)S(1)}, bf16[4,128,128]{2,1,0:T(8,128)(2,1)S(1)}, u32[]{:S(2)}, u32[]{:S(2)}) collective-permute-start(bf16[4,128,128]{2,1,0:T(8,128)(2,1)S(1)} %get-tuple-element.542), channel_id=1, source_target_pairs={{0,24},{2,16},{4,8},{6,0},{8,26},{10,18},{12,10},{14,2},{16,28},{1... | collective-permute-start | bytes 393224 | tf_op jit(solution)/shard_map/ppermute | solution.py:76
  11.5 20.0 %collective-permute-start.2 = (bf16[4,128,128]{2,1,0:T(8,128)(2,1)}, bf16[4,128,128]{2,1,0:T(8,128)(2,1)S(1)}, u32[]{:S(2)}, u32[]{:S(2)}) collective-permute-start(bf16[4,128,128]{2,1,0:T(8,128)(2,1)} %get-tuple-element.543), channel_id=1, source_target_pairs={{0,16},{2,24},{4,0},{6,8},{8,18},{10,26},{12,2},{14,10},{16,20},{1... | collective-permute-start | bytes 393224 | tf_op jit(solution)/shard_map/ppermute | solution.py:76
  14.1 17.4 %collective-permute-start.1 = (bf16[4,128,128]{2,1,0:T(8,128)(2,1)S(1)}, bf16[4,128,128]{2,1,0:T(8,128)(2,1)}, u32[]{:S(2)}, u32[]{:S(2)}) collective-permute-start(bf16[4,128,128]{2,1,0:T(8,128)(2,1)S(1)} %get-tuple-element.544), channel_id=1, source_target_pairs={{0,8},{2,0},{4,24},{6,16},{8,10},{10,2},{12,26},{14,18},{16,12},{1... | collective-permute-start | bytes 393224 | tf_op jit(solution)/shard_map/ppermute | solution.py:76
  14.8 16.7 %collective-permute-start = (bf16[4,128,128]{2,1,0:T(8,128)(2,1)S(1)}, bf16[4,128,128]{2,1,0:T(8,128)(2,1)}, u32[]{:S(2)}, u32[]{:S(2)}) collective-permute-start(bf16[4,128,128]{2,1,0:T(8,128)(2,1)S(1)} %get-tuple-element.541), channel_id=1, source_target_pairs={{0,0},{2,8},{4,16},{6,24},{8,2},{10,10},{12,18},{14,26},{16,4},{18... | collective-permute-start | bytes 393224 | tf_op jit(solution)/shard_map/ppermute | solution.py:76
  19.4 13.2 %collective-permute-start.6 = (bf16[2,4,128,128]{2,3,1,0:T(8,128)(2,1)S(1)}, bf16[2,4,128,128]{2,3,1,0:T(8,128)(2,1)S(1)}, u32[]{:S(2)}, u32[]{:S(2)}) collective-permute-start(bf16[2,4,128,128]{2,3,1,0:T(8,128)(2,1)S(1)} %pad_maximum_fusion.30), channel_id=1, source_target_pairs={{0,24},{8,16},{16,8},{24,0},{1,25},{9,17},{17,9},{25,1},{2,26},{10... | collective-permute-start | bytes 786440 | tf_op jit(solution)/shard_map/ppermute | solution.py:106
  25.5 14.2 %collective-permute-start.5 = (bf16[2,4,128,128]{2,3,1,0:T(8,128)(2,1)S(1)}, bf16[2,4,128,128]{2,3,1,0:T(8,128)(2,1)S(1)}, u32[]{:S(2)}, u32[]{:S(2)}) collective-permute-start(bf16[2,4,128,128]{2,3,1,0:T(8,128)(2,1)S(1)} %pad_maximum_fusion.29), channel_id=1, source_target_pairs={{0,16},{8,24},{16,0},{24,8},{1,17},{9,25},{17,1},{25,9},{2,18},{10... | collective-permute-start | bytes 786440 | tf_op jit(solution)/shard_map/ppermute | solution.py:106
  44.2 15.9 %collective-permute-start.11 = (bf16[4,128,128]{2,1,0:T(8,128)(2,1)S(1)}, bf16[4,128,128]{2,1,0:T(8,128)(2,1)S(1)}, u32[]{:S(2)}, u32[]{:S(2)}) collective-permute-start(bf16[4,128,128]{2,1,0:T(8,128)(2,1)S(1)} %get-tuple-element.549), channel_id=1, source_target_pairs={{0,4},{2,6},{4,0},{6,2},{1,5},{3,7},{5,1},{7,3},{8,12},{10,14},{12... | collective-permute-start | bytes 393224 | tf_op jit(solution)/shard_map/ppermute | solution.py:120
  44.2 15.9 %collective-permute-start.10 = (bf16[4,128,128]{2,1,0:T(8,128)(2,1)S(1)}, bf16[4,128,128]{2,1,0:T(8,128)(2,1)S(1)}, u32[]{:S(2)}, u32[]{:S(2)}) collective-permute-start(bf16[4,128,128]{2,1,0:T(8,128)(2,1)S(1)} %get-tuple-element.549), channel_id=1, source_target_pairs={{0,2},{2,0},{4,6},{6,4},{1,3},{3,1},{5,7},{7,5},{8,10},{10,8},{12,... | collective-permute-start | bytes 393224 | tf_op jit(solution)/shard_map/ppermute | solution.py:120
  44.9 15.3 %collective-permute-start.9 = (bf16[4,128,128]{2,1,0:T(8,128)(2,1)S(1)}, bf16[4,128,128]{2,1,0:T(8,128)(2,1)S(1)}, u32[]{:S(2)}, u32[]{:S(2)}) collective-permute-start(bf16[4,128,128]{2,1,0:T(8,128)(2,1)S(1)} %get-tuple-element.548), channel_id=1, source_target_pairs={{0,6},{2,4},{4,2},{6,0},{1,7},{3,5},{5,3},{7,1},{8,14},{10,12},{12... | collective-permute-start | bytes 393224 | tf_op jit(solution)/shard_map/ppermute | solution.py:120
  48.6 16.8 %collective-permute-start.8 = (bf16[4,128,128]{2,1,0:T(8,128)(2,1)S(1)}, bf16[4,128,128]{2,1,0:T(8,128)(2,1)S(1)}, u32[]{:S(2)}, u32[]{:S(2)}) collective-permute-start(bf16[4,128,128]{2,1,0:T(8,128)(2,1)S(1)} %get-tuple-element.548), channel_id=1, source_target_pairs={{0,4},{2,6},{4,0},{6,2},{1,5},{3,7},{5,1},{7,3},{8,12},{10,14},{12... | collective-permute-start | bytes 393224 | tf_op jit(solution)/shard_map/ppermute | solution.py:120
  49.0 16.4 %collective-permute-start.7 = (bf16[4,128,128]{2,1,0:T(8,128)(2,1)S(1)}, bf16[4,128,128]{2,1,0:T(8,128)(2,1)S(1)}, u32[]{:S(2)}, u32[]{:S(2)}) collective-permute-start(bf16[4,128,128]{2,1,0:T(8,128)(2,1)S(1)} %get-tuple-element.548), channel_id=1, source_target_pairs={{0,2},{2,0},{4,6},{6,4},{1,3},{3,1},{5,7},{7,5},{8,10},{10,8},{12,... | collective-permute-start | bytes 393224 | tf_op jit(solution)/shard_map/ppermute | solution.py:120
  71.4 30.9 %all-gather.15.cloned.1.call-start = ((), (), s32[]{:S(2)}) async-start(), calls=%async_computation.42 | async-start | bytes 1310720 | tf_op jit(solution)/shard_map/all_gather | solution.py:114
  84.1 13.4 %all-to-all-start.13 = ((bf16[8,16,16,128]{3,2,1,0:T(8,128)(2,1)}), bf16[8,16,16,128]{3,2,1,0:T(8,128)(2,1)}, u32[]{:S(2)}, u32[]{:S(2)}) async-start(bf16[8,16,16,128]{3,2,1,0:T(8,128)(2,1)} %copy.284), calls=%async_computation.13 | async-start | bytes 1048576 | tf_op jit(solution)/shard_map/all_to_all | solution.py:27
  105.8 12.9 %all-to-all-start.14 = ((bf16[8,16,16,128]{3,1,2,0:T(8,128)(2,1)}), bf16[8,16,16,128]{3,1,2,0:T(8,128)(2,1)S(1)}, u32[]{:S(2)}, u32[]{:S(2)}) async-start(bf16[8,16,16,128]{3,1,2,0:T(8,128)(2,1)} %copy.291), calls=%async_computation.14 | async-start | bytes 1048576 | tf_op jit(solution)/shard_map/all_to_all | solution.py:27
  109.5 31.0 %all-gather.17.cloned.1.call-start = ((), (), s32[]{:S(2)}) async-start(), calls=%async_computation.43 | async-start | bytes 1310720 | tf_op jit(solution)/shard_map/all_gather | solution.py:114
  143.9 13.0 %all-to-all-start.16 = ((bf16[8,16,16,128]{3,1,2,0:T(8,128)(2,1)}), bf16[8,16,16,128]{3,1,2,0:T(8,128)(2,1)S(1)}, u32[]{:S(2)}, u32[]{:S(2)}) async-start(bf16[8,16,16,128]{3,1,2,0:T(8,128)(2,1)} %copy.300), calls=%async_computation.16 | async-start | bytes 1048576 | tf_op jit(solution)/shard_map/all_to_all | solution.py:27
  147.5 30.4 %all-gather.19.cloned.1.call-start = ((), (), s32[]{:S(2)}) async-start(), calls=%async_computation.44 | async-start | bytes 1310720 | tf_op jit(solution)/shard_map/all_gather | solution.py:114
  149.0 13.5 %collective-permute-start.15 = (bf16[2,4,128,128]{2,3,1,0:T(8,128)(2,1)}, bf16[2,4,128,128]{2,3,1,0:T(8,128)(2,1)}, u32[]{:S(2)}, u32[]{:S(2)}) collective-permute-start(bf16[2,4,128,128]{2,3,1,0:T(8,128)(2,1)} %pad_maximum_fusion.33), channel_id=1, source_target_pairs={{0,24},{8,16},{16,8},{24,0},{1,25},{9,17},{17,9},{25,1},{2,26},{10... | collective-permute-start | bytes 786440 | tf_op jit(solution)/shard_map/ppermute | solution.py:106
  151.8 17.6 %collective-permute-start.14 = (bf16[2,4,128,128]{2,3,1,0:T(8,128)(2,1)}, bf16[2,4,128,128]{2,3,1,0:T(8,128)(2,1)}, u32[]{:S(2)}, u32[]{:S(2)}) collective-permute-start(bf16[2,4,128,128]{2,3,1,0:T(8,128)(2,1)} %pad_maximum_fusion.32), channel_id=1, source_target_pairs={{0,16},{8,24},{16,0},{24,8},{1,17},{9,25},{17,1},{25,9},{2,18},{10... | collective-permute-start | bytes 786440 | tf_op jit(solution)/shard_map/ppermute | solution.py:106
  153.1 16.2 %collective-permute-start.13 = (bf16[2,4,128,128]{2,3,1,0:T(8,128)(2,1)}, bf16[2,4,128,128]{2,3,1,0:T(8,128)(2,1)}, u32[]{:S(2)}, u32[]{:S(2)}) collective-permute-start(bf16[2,4,128,128]{2,3,1,0:T(8,128)(2,1)} %pad_maximum_fusion.31), channel_id=1, source_target_pairs={{0,8},{8,0},{16,24},{24,16},{1,9},{9,1},{17,25},{25,17},{2,10},{10... | collective-permute-start | bytes 786440 | tf_op jit(solution)/shard_map/ppermute | solution.py:106
  158.9 14.3 %all-to-all-start.17 = ((bf16[8,16,16,128]{3,2,1,0:T(8,128)(2,1)}), bf16[8,16,16,128]{3,2,1,0:T(8,128)(2,1)S(1)}, u32[]{:S(2)}, u32[]{:S(2)}) async-start(bf16[8,16,16,128]{3,2,1,0:T(8,128)(2,1)} %copy.302), calls=%async_computation.17 | async-start | bytes 1048576 | tf_op jit(solution)/shard_map/all_to_all | solution.py:27
  185.8 30.9 %all-gather.21.cloned.1.call-start = ((), (), s32[]{:S(2)}) async-start(), calls=%async_computation.45 | async-start | bytes 1310720 | tf_op jit(solution)/shard_map/all_gather | solution.py:114
  224.4 30.0 %all-gather.23.cloned.1.call-start = ((), (), s32[]{:S(2)}) async-start(), calls=%async_computation.46 | async-start | bytes 1310720 | tf_op jit(solution)/shard_map/all_gather | solution.py:114
  261.6 30.6 %all-gather.25.cloned.1.call-start = ((), (), s32[]{:S(2)}) async-start(), calls=%async_computation.47 | async-start | bytes 1310720 | tf_op jit(solution)/shard_map/all_gather | solution.py:114
  299.9 68.2 %all-gather.27.cloned.1.call-start = ((), (), s32[]{:S(2)}) async-start(), calls=%async_computation.48 | async-start | bytes 1310720 | tf_op jit(solution)/shard_map/all_gather | solution.py:114
  330.6 36.4 %collective-permute-start.23 = (bf16[4,128,128]{1,2,0:T(8,128)(2,1)}, bf16[4,128,128]{1,2,0:T(8,128)(2,1)}, u32[]{:S(2)}, u32[]{:S(2)}) collective-permute-start(bf16[4,128,128]{1,2,0:T(8,128)(2,1)} %bitcast.1174), channel_id=1, source_target_pairs={{0,24},{2,16},{4,8},{6,0},{8,26},{10,18},{12,10},{14,2},{16,28},{1... | collective-permute-start | bytes 393224 | tf_op jit(solution)/shard_map/ppermute | solution.py:76
  332.2 34.8 %collective-permute-start.22 = (bf16[4,128,128]{1,2,0:T(8,128)(2,1)}, bf16[4,128,128]{1,2,0:T(8,128)(2,1)}, u32[]{:S(2)}, u32[]{:S(2)}) collective-permute-start(bf16[4,128,128]{1,2,0:T(8,128)(2,1)} %bitcast.1175), channel_id=1, source_target_pairs={{0,16},{2,24},{4,0},{6,8},{8,18},{10,26},{12,2},{14,10},{16,20},{1... | collective-permute-start | bytes 393224 | tf_op jit(solution)/shard_map/ppermute | solution.py:76
  334.3 32.7 %collective-permute-start.21 = (bf16[4,128,128]{1,2,0:T(8,128)(2,1)S(1)}, bf16[4,128,128]{1,2,0:T(8,128)(2,1)}, u32[]{:S(2)}, u32[]{:S(2)}) collective-permute-start(bf16[4,128,128]{1,2,0:T(8,128)(2,1)S(1)} %bitcast.1176), channel_id=1, source_target_pairs={{0,8},{2,0},{4,24},{6,16},{8,10},{10,2},{12,26},{14,18},{16,12},{1... | collective-permute-start | bytes 393224 | tf_op jit(solution)/shard_map/ppermute | solution.py:76
  334.5 32.5 %collective-permute-start.20 = (bf16[4,128,128]{1,2,0:T(8,128)(2,1)S(1)}, bf16[4,128,128]{1,2,0:T(8,128)(2,1)S(1)}, u32[]{:S(2)}, u32[]{:S(2)}) collective-permute-start(bf16[4,128,128]{1,2,0:T(8,128)(2,1)S(1)} %bitcast.1177), channel_id=1, source_target_pairs={{0,0},{2,8},{4,16},{6,24},{8,2},{10,10},{12,18},{14,26},{16,4},{18... | collective-permute-start | bytes 393224 | tf_op jit(solution)/shard_map/ppermute | solution.py:76
  370.8 17.9 %all-to-all-start.26 = ((bf16[8,16,16,128]{3,1,2,0:T(8,128)(2,1)}), bf16[8,16,16,128]{3,1,2,0:T(8,128)(2,1)S(1)}, u32[]{:S(2)}, u32[]{:S(2)}) async-start(bf16[8,16,16,128]{3,1,2,0:T(8,128)(2,1)} %copy.352), calls=%async_computation.26 | async-start | bytes 1048576 | tf_op jit(solution)/shard_map/all_to_all | solution.py:27
  379.4 348.2 %reduce-scatter.10.cloned.1.call-start = ((), (), s32[]{:S(2)}) async-start(), calls=%async_computation.39 | async-start | bytes 655360 | tf_op jit(solution)/shard_map/reduce_scatter | solution.py:131
  613.8 115.2 %reduce-scatter.6.cloned.1.call-start = ((), (), s32[]{:S(2)}) async-start(), calls=%async_computation.37 | async-start | bytes 1310720 | tf_op jit(solution)/shard_map/reduce_scatter | solution.py:131
  617.2 116.8 %reduce-scatter.14.cloned.1.call-start = ((), (), s32[]{:S(2)}) async-start(), calls=%async_computation.41 | async-start | bytes 2621440 | tf_op jit(solution)/shard_map/reduce_scatter | solution.py:131
  619.6 161.6 %reduce-scatter.12.cloned.1.call-start = ((), (), s32[]{:S(2)}) async-start(), calls=%async_computation.40 | async-start | bytes 2621440 | tf_op jit(solution)/shard_map/reduce_scatter | solution.py:131
  627.3 13.4 %all-to-all-start.27 = ((bf16[8,16,16,128]{3,2,1,0:T(8,128)(2,1)}), bf16[8,16,16,128]{3,2,1,0:T(8,128)(2,1)}, u32[]{:S(2)}, u32[]{:S(2)}) async-start(bf16[8,16,16,128]{3,2,1,0:T(8,128)(2,1)} %copy.354), calls=%async_computation.27 | async-start | bytes 1048576 | tf_op jit(solution)/shard_map/all_to_all | solution.py:27
  631.4 195.3 %reduce-scatter.8.cloned.1.call-start = ((), (), s32[]{:S(2)}) async-start(), calls=%async_computation.38 | async-start | bytes 2621440 | tf_op jit(solution)/shard_map/reduce_scatter | solution.py:131
  645.3 16.4 %collective-permute-start.17 = (bf16[4,128,128]{2,1,0:T(8,128)(2,1)S(1)}, bf16[4,128,128]{2,1,0:T(8,128)(2,1)S(1)}, u32[]{:S(2)}, u32[]{:S(2)}) collective-permute-start(bf16[4,128,128]{2,1,0:T(8,128)(2,1)S(1)} %bitcast.1187), channel_id=1, source_target_pairs={{0,2},{2,10},{4,18},{6,26},{8,0},{10,8},{12,16},{14,24},{16,6},{18... | collective-permute-start | bytes 393224 | tf_op jit(solution)/shard_map/ppermute | solution.py:76
  645.5 16.2 %collective-permute-start.16 = (bf16[4,128,128]{2,1,0:T(8,128)(2,1)S(1)}, bf16[4,128,128]{2,1,0:T(8,128)(2,1)S(1)}, u32[]{:S(2)}, u32[]{:S(2)}) collective-permute-start(bf16[4,128,128]{2,1,0:T(8,128)(2,1)S(1)} %bitcast.1188), channel_id=1, source_target_pairs={{0,0},{2,8},{4,16},{6,24},{8,2},{10,10},{12,18},{14,26},{16,4},{18... | collective-permute-start | bytes 393224 | tf_op jit(solution)/shard_map/ppermute | solution.py:76
  647.7 16.9 %all-to-all-start.31 = ((bf16[8,16,16,128]{3,1,2,0:T(8,128)(2,1)}), bf16[8,16,16,128]{3,1,2,0:T(8,128)(2,1)S(1)}, u32[]{:S(2)}, u32[]{:S(2)}) async-start(bf16[8,16,16,128]{3,1,2,0:T(8,128)(2,1)} %copy.393), calls=%async_computation.31 | async-start | bytes 1048576 | tf_op jit(solution)/shard_map/all_to_all | solution.py:27
  665.5 21.2 %collective-permute-start.27 = (bf16[4,128,128]{2,1,0:T(8,128)(2,1)S(1)}, bf16[4,128,128]{2,1,0:T(8,128)(2,1)S(1)}, u32[]{:S(2)}, u32[]{:S(2)}) collective-permute-start(bf16[4,128,128]{2,1,0:T(8,128)(2,1)S(1)} %bitcast.1184), channel_id=1, source_target_pairs={{0,6},{2,14},{4,22},{6,30},{8,4},{10,12},{12,20},{14,28},{16,2},{1... | collective-permute-start | bytes 393224 | tf_op jit(solution)/shard_map/ppermute | solution.py:76
  670.5 16.3 %collective-permute-start.26 = (bf16[4,128,128]{2,1,0:T(8,128)(2,1)S(1)}, bf16[4,128,128]{2,1,0:T(8,128)(2,1)S(1)}, u32[]{:S(2)}, u32[]{:S(2)}) collective-permute-start(bf16[4,128,128]{2,1,0:T(8,128)(2,1)S(1)} %bitcast.1182), channel_id=1, source_target_pairs={{0,4},{2,12},{4,20},{6,28},{8,6},{10,14},{12,22},{14,30},{16,0},{1... | collective-permute-start | bytes 393224 | tf_op jit(solution)/shard_map/ppermute | solution.py:76
  673.7 27.2 %collective-permute-start.25 = (bf16[4,128,128]{2,1,0:T(8,128)(2,1)S(1)}, bf16[4,128,128]{2,1,0:T(8,128)(2,1)S(1)}, u32[]{:S(2)}, u32[]{:S(2)}) collective-permute-start(bf16[4,128,128]{2,1,0:T(8,128)(2,1)S(1)} %bitcast.1181), channel_id=1, source_target_pairs={{0,2},{2,10},{4,18},{6,26},{8,0},{10,8},{12,16},{14,24},{16,6},{18... | collective-permute-start | bytes 393224 | tf_op jit(solution)/shard_map/ppermute | solution.py:76
  675.7 25.1 %collective-permute-start.24 = (bf16[4,128,128]{2,1,0:T(8,128)(2,1)S(1)}, bf16[4,128,128]{2,1,0:T(8,128)(2,1)S(1)}, u32[]{:S(2)}, u32[]{:S(2)}) collective-permute-start(bf16[4,128,128]{2,1,0:T(8,128)(2,1)S(1)} %bitcast.1183), channel_id=1, source_target_pairs={{0,0},{2,8},{4,16},{6,24},{8,2},{10,10},{12,18},{14,26},{16,4},{18... | collective-permute-start | bytes 393224 | tf_op jit(solution)/shard_map/ppermute | solution.py:76
  677.1 24.8 %collective-permute-start.30 = (bf16[4,128,128]{1,2,0:T(8,128)(2,1)S(1)}, bf16[4,128,128]{1,2,0:T(8,128)(2,1)S(1)}, u32[]{:S(2)}, u32[]{:S(2)}) collective-permute-start(bf16[4,128,128]{1,2,0:T(8,128)(2,1)S(1)} %bitcast.1178), channel_id=1, source_target_pairs={{0,6},{2,4},{4,2},{6,0},{1,7},{3,5},{5,3},{7,1},{8,14},{10,12},{12... | collective-permute-start | bytes 393224 | tf_op jit(solution)/shard_map/ppermute | solution.py:120
  686.7 40.4 %collective-permute-start.29 = (bf16[4,128,128]{1,2,0:T(8,128)(2,1)S(1)}, bf16[4,128,128]{1,2,0:T(8,128)(2,1)S(1)}, u32[]{:S(2)}, u32[]{:S(2)}) collective-permute-start(bf16[4,128,128]{1,2,0:T(8,128)(2,1)S(1)} %bitcast.1180), channel_id=1, source_target_pairs={{0,4},{2,6},{4,0},{6,2},{1,5},{3,7},{5,1},{7,3},{8,12},{10,14},{12... | collective-permute-start | bytes 393224 | tf_op jit(solution)/shard_map/ppermute | solution.py:120
  686.8 40.3 %collective-permute-start.28 = (bf16[4,128,128]{1,2,0:T(8,128)(2,1)S(1)}, bf16[4,128,128]{1,2,0:T(8,128)(2,1)S(1)}, u32[]{:S(2)}, u32[]{:S(2)}) collective-permute-start(bf16[4,128,128]{1,2,0:T(8,128)(2,1)S(1)} %bitcast.1179), channel_id=1, source_target_pairs={{0,2},{2,0},{4,6},{6,4},{1,3},{3,1},{5,7},{7,5},{8,10},{10,8},{12,... | collective-permute-start | bytes 393224 | tf_op jit(solution)/shard_map/ppermute | solution.py:120
  783.2 60.1 %collective-permute-start.39 = (bf16[2,4,128,128]{3,2,1,0:T(8,128)(2,1)S(1)}, bf16[2,4,128,128]{3,2,1,0:T(8,128)(2,1)S(1)}, u32[]{:S(2)}, u32[]{:S(2)}) collective-permute-start(bf16[2,4,128,128]{3,2,1,0:T(8,128)(2,1)S(1)} %pad_maximum_fusion.36), channel_id=1, source_target_pairs={{0,24},{8,16},{16,8},{24,0},{1,25},{9,17},{17,9},{25,1},{2,26},{10... | collective-permute-start | bytes 786440 | tf_op jit(solution)/shard_map/ppermute | solution.py:106
  784.1 59.2 %collective-permute-start.38 = (bf16[2,4,128,128]{3,2,1,0:T(8,128)(2,1)S(1)}, bf16[2,4,128,128]{3,2,1,0:T(8,128)(2,1)S(1)}, u32[]{:S(2)}, u32[]{:S(2)}) collective-permute-start(bf16[2,4,128,128]{3,2,1,0:T(8,128)(2,1)S(1)} %pad_maximum_fusion.35), channel_id=1, source_target_pairs={{0,16},{8,24},{16,0},{24,8},{1,17},{9,25},{17,1},{25,9},{2,18},{10... | collective-permute-start | bytes 786440 | tf_op jit(solution)/shard_map/ppermute | solution.py:106
  (91 other events, 1164.9 us)
Sparse Core Ops, SparseCore 0:
  73.8 28.4 all-gather.14
  112.4 27.9 all-gather.16
  149.9 27.9 all-gather.18
  188.5 27.9 all-gather.20
  226.5 27.8 all-gather.22
  263.7 27.9 all-gather.24
  302.3 27.8 all-gather.26
  613.9 19.4 reduce-scatter.9
  635.7 33.8 reduce-scatter.5
  672.4 61.5 reduce-scatter.13
  736.9 44.3 reduce-scatter.11
  783.5 43.1 reduce-scatter.7

commit v11 on v10

--- a/solution.py
+++ b/solution.py
@@ -111,8 +111,10 @@
         return jnp.einsum("aj,fbjk,ck->fbac", order, part, order, preferred_element_type=F32).astype(BF16)
 
     def gathered(part):
-        full = lax.all_gather(part, "t", axis=0, tiled=False)
-        return [full[:, f].reshape(own, size, size) for f in range(part.shape[0])]
+        return lax.all_gather(part, "t", axis=0, tiled=False)
+
+    def pair_of(full):
+        return [full[:, f].reshape(own, size, size) for f in range(2)]
 
     def around(value_of):
         moved = [value_of(0)]
@@ -122,7 +124,7 @@
 
     def gathered_directly(part):
         moved = jnp.stack(around(lambda mask: part))
-        return jnp.concatenate([pick(moved, t_index ^ group) for group in range(groups)])
+        return jnp.stack([pick(moved, t_index ^ group) for group in range(groups)])
 
     def unordered(total):
         return jnp.einsum("aj,fbac,ck->fbjk", order, total, order, preferred_element_type=F32).astype(BF16)
@@ -130,11 +132,6 @@
     def summed(terms):
         total = lax.psum_scatter(terms.reshape(-1, size, size), "t", scatter_dimension=0, tiled=True)
         return unordered(total.reshape(terms.shape[1:]))
-
-    def summed_directly(term):
-        parts = term.reshape(groups, sub, size, size)
-        moved = around(lambda mask: pick(parts, t_index ^ mask))
-        return unordered(sum(one.astype(F32) for one in moved).astype(BF16)[None])
 
     def laid_out(*terms):
         return jnp.stack([term.reshape(groups, sub, size, size) for term in terms], axis=1)
@@ -144,56 +141,54 @@
     parts = [ordered(part) for part in scattered(rights[0], lefts[0])]
     current = arriving(inputs)
     current, parts[0] = lax.optimization_barrier((current, parts[0]))
-    weights = [(gathered_directly(parts[0][0]), gathered_directly(parts[0][1]))]
-    later, right = lax.optimization_barrier(((rights[1:], lefts[1:]), weights[0][0]))
+    first = [gathered_directly(parts[0][f]) for f in range(2)]
+    later, first[0] = lax.optimization_barrier(((rights[1:], lefts[1:]), first[0]))
     rights, lefts = later
-    weights[0] = (right, weights[0][1])
+    weights = [jnp.stack(first, axis=1)]
     for loop in range(loops - 1):
         parts.extend(ordered(part) for part in scattered(rights[loop], lefts[loop]))
 
     current = settled(current)
-    stored = []
+    kept = [jnp.zeros((layers, own, size, micros * rows), BF16) for _ in range(2)]
     for layer in range(layers):
         if layer + 1 < layers:
             current, parts[layer + 1] = lax.optimization_barrier((current, parts[layer + 1]))
-            weights.append(tuple(gathered(parts[layer + 1])))
+            weights.append(gathered(parts[layer + 1]))
         else:
             current, cotangent = lax.optimization_barrier((current, cotangent))
             grad = settled(arriving(cotangent))
-        current, saved = forward_layer(current, *weights[layer])
-        stored.append(saved)
+        factors = pair_of(weights[layer]) if layer else [one.reshape(own, size, size) for one in first]
+        current, saved = forward_layer(current, *factors)
+        kept = [lax.dynamic_update_index_in_dim(all_of, one, layer, 0) for all_of, one in zip(kept, saved)]
+        current, kept = lax.optimization_barrier((current, kept))
     outputs = leave(current)
 
     once = 1 + s_index // sections
     sums = [None] * layers
 
-    def backward_pair(first):
+    def backward_pair(top):
         def run(_, carry):
             grad, _ = carry
             terms = []
-            for layer in range(first, first - PAIRED, -1):
-                grad, *pair = backward_layer(grad, *weights[layer], stored[layer])
+            for layer in range(top, top - PAIRED, -1):
+                saved = [all_of[layer] for all_of in kept]
+                grad, *pair = backward_layer(grad, *pair_of(weights[layer]), saved)
                 terms += pair
             return grad, laid_out(*terms)
 
         return run
 
-    layer = layers - 1
-    while layer >= PAIRED:
+    totals = {}
+    for top in range(layers - 1, 0, -PAIRED):
         blank = jnp.zeros((groups, 2 * PAIRED, sub, size, size), BF16)
-        grad, terms = lax.fori_loop(0, once, backward_pair(layer), (grad, blank))
-        total = summed(terms)
+        grad, terms = lax.fori_loop(0, once, backward_pair(top), (grad, blank))
+        if top + 2 * PAIRED in totals:
+            asked = totals[top + 2 * PAIRED]
+            grad, terms, totals[top + 2 * PAIRED] = lax.optimization_barrier((grad, terms, asked))
+        totals[top] = summed(terms)
+    for top, total in totals.items():
         for step in range(PAIRED):
-            sums[layer - step] = [total[2 * step], total[2 * step + 1]]
-        layer -= PAIRED
-    while layer >= 0:
-        grad, right_term, left_term = backward_layer(grad, *weights[layer], stored[layer])
-        if layer:
-            total = summed(laid_out(right_term, left_term))
-            sums[layer] = [total[0], total[1]]
-        else:
-            sums[layer] = [summed_directly(right_term)[0], summed(laid_out(left_term))[0]]
-        layer -= 1
+            sums[top - step] = [total[2 * step], total[2 * step + 1]]
     input_grad = leave(grad)
 
     def of_loop(loop, factor):

time: 867 us -> 799 us (0.922)
  blocking collectives: 117 us -> 46.7 us
  starting transfers between devices: 161 us -> 197 us
  waiting for transfers between devices: 319 us -> 292 us
  other arithmetic: 33.5 us -> 24.3 us
    all_to_all x10 -> x4, blocking collectives: 117 us -> 46.7 us  [exchange(): lax.all_to_all(pieces, WIDE, split_axis=0, concat_axis=0, tiled=True)]
    reduce_scatter x5 -> x4, waiting for transfers between devices: 90.9 us -> 36.4 us  [summed(): lax.psum_scatter(terms.reshape(-1, size, size), 't', scatter_dimension=0,...]
    ppermute x9 -> x6, waiting for transfers between devices: 37.2 us -> 6.53 us  [around(): lax.ppermute(value_of(mask), 't', [(t, t ^ mask) for t in range(groups)])]
    all_gather x7, waiting for transfers between devices: 9.49 us -> 37.5 us  [gathered(): return lax.all_gather(part, 't', axis=0, tiled=False)]
    ppermute x9 -> x6, starting transfers between devices: 34.6 us -> 10.2 us  [around(): lax.ppermute(value_of(mask), 't', [(t, t ^ mask) for t in range(groups)])]
    all_to_all x22 -> x28, waiting for transfers between devices: 141 us -> 164 us  [exchange(): lax.all_to_all(pieces, WIDE, split_axis=0, concat_axis=0, tiled=True)]
    ppermute x15, starting transfers between devices: 13.7 us -> 36 us  [scattered(): moved.append(lax.ppermute(value, 's', pairs))]
    ppermute x16, starting transfers between devices: 24.1 us -> 46.1 us  [turned(): moved.append(lax.ppermute(pick(parts, send_by ^ mask), ('s', 't'), pairs))]
  transfers between devices with their start and end apart: 74 -> 76, of which waited for: 40 -> 48; matrix products, arithmetic and copies ran while one was open for 19% -> 20% of each run, Pallas kernels for 0% -> 0%
where the time goes in v11:
time: 799 us; the launch traced here: 786 us
  waiting for transfers between devices  292 us (37%)
  starting transfers between devices  197 us (25%)
  local copies, waits for them, and re-layouts  136 us (17%)
  matrix products  73.5 us (9%)
  blocking collectives  46.7 us (6%)
  other arithmetic  24.3 us (3%)
  between operations  15.8 us (2%)
    all_to_all x28, waiting for transfers between devices, exchange(): lax.all_to_all(pieces, WIDE, split_axis=0, concat_axis=0, tiled=True)  164 us
    all_to_all x28, starting transfers between devices, exchange(): lax.all_to_all(pieces, WIDE, split_axis=0, concat_axis=0, tiled=True)  104 us
    all_to_all x4, blocking collectives, exchange(): lax.all_to_all(pieces, WIDE, split_axis=0, concat_axis=0, tiled=True)  46.7 us
    ppermute x16, starting transfers between devices, turned(): moved.append(lax.ppermute(pick(parts, send_by ^ mask), ('s', 't'), pairs))  46.1 us
    all_gather x7, waiting for transfers between devices, gathered(): return lax.all_gather(part, 't', axis=0, tiled=False)  37.5 us
    reduce_scatter x4, waiting for transfers between devices, summed(): lax.psum_scatter(terms.reshape(-1, size, size), 't', scatter_dimension=0,...  36.4 us
    ppermute x15, starting transfers between devices, scattered(): moved.append(lax.ppermute(value, 's', pairs))  36 us
    ppermute x16, waiting for transfers between devices, turned(): moved.append(lax.ppermute(pick(parts, send_by ^ mask), ('s', 't'), pairs))  24.6 us
  transfers between devices with their start and end apart: 76, of which 48 were waited for; matrix products, arithmetic and copies ran while one was open for 20% of the time, Pallas kernels for 0%

profile of v11, /device:TPU:0, one launch (start us, length us, event | category | flops | bytes accessed | tf_op | source)
XLA Modules:
  0.0 786.1 jit_solution(16722041515329770351)
XLA Ops:
  22.3 14.0 %collective-permute-start.5 = (bf16[2,4,128,128]{2,3,1,0:T(8,128)(2,1)S(1)}, bf16[2,4,128,128]{2,3,1,0:T(8,128)(2,1)S(1)}, u32[]{:S(2)}, u32[]{:S(2)}) collective-permute-start(bf16[2,4,128,128]{2,3,1,0:T(8,128)(2,1)S(1)} %pad_maximum_fusion.29), channel_id=1, source_target_pairs={{0,16},{8,24},{16,0},{24,8},{1,17},{9,25},{17,1},{25,9},{2,18},{10... | collective-permute-start | bytes 786440 | tf_op jit(solution)/shard_map/ppermute | solution.py:106
  58.0 4.2 collective-permute-done.12
  72.3 5.9 all-to-all-done.16
  80.1 4.1 all-to-all-start.17
  95.2 12.6 %all-gather.15.cloned.1.call-done = bf16[8,4,128,128]{3,2,1,0:T(8,128)(2,1)} async-done(((bf16[2,4,128,128]{3,2,1,0:T(8,128)(2,1)}), bf16[8,4,128,128]{3,2,1,0:T(8,128)(2,1)}) %all-gather.15.cloned.1.call-update) | async-done | bytes 1048592 | tf_op jit(solution)/shard_map/all_gather | solution.py:114
  130.8 9.0 %all-to-all-done.19 = bf16[8,16,16,128]{3,2,1,0:T(8,128)(2,1)S(1)} async-done(((bf16[8,16,16,128]{3,2,1,0:T(8,128)(2,1)}), bf16[8,16,16,128]{3,2,1,0:T(8,128)(2,1)S(1)}, u32[]{:S(2)}, u32[]{:S(2)}) %all-to-all-start.19) | async-done | bytes 524320 | tf_op jit(solution)/shard_map/all_to_all | solution.py:27
  140.4 7.1 all-gather.17.cloned.1.call-done
  156.2 6.7 all-to-all-done.20
  170.2 7.4 all-to-all-done.21
  191.8 8.0 %all-to-all-done.22 = bf16[8,16,16,128]{3,1,2,0:T(8,128)(2,1)S(1)} async-done(((bf16[8,16,16,128]{3,1,2,0:T(8,128)(2,1)}), bf16[8,16,16,128]{3,1,2,0:T(8,128)(2,1)S(1)}, u32[]{:S(2)}, u32[]{:S(2)}) %all-to-all-start.22) | async-done | bytes 524320 | tf_op jit(solution)/shard_map/all_to_all | solution.py:27
  207.1 7.3 all-to-all-done.23
  228.8 8.0 %all-to-all-done.24 = bf16[8,16,16,128]{3,1,2,0:T(8,128)(2,1)S(1)} async-done(((bf16[8,16,16,128]{3,1,2,0:T(8,128)(2,1)}), bf16[8,16,16,128]{3,1,2,0:T(8,128)(2,1)S(1)}, u32[]{:S(2)}, u32[]{:S(2)}) %all-to-all-start.24) | async-done | bytes 524320 | tf_op jit(solution)/shard_map/all_to_all | solution.py:27
  244.0 7.4 all-to-all-done.25
  265.7 8.0 %all-to-all-done.26 = bf16[8,16,16,128]{3,1,2,0:T(8,128)(2,1)S(1)} async-done(((bf16[8,16,16,128]{3,1,2,0:T(8,128)(2,1)}), bf16[8,16,16,128]{3,1,2,0:T(8,128)(2,1)S(1)}, u32[]{:S(2)}, u32[]{:S(2)}) %all-to-all-start.26) | async-done | bytes 524320 | tf_op jit(solution)/shard_map/all_to_all | solution.py:27
  281.3 7.4 all-to-all-done.27
  289.3 5.8 all-gather.25.cloned.1.call-done
  313.4 4.2 all-to-all-start.29
  320.4 6.4 all-to-all-done.29
  339.8 5.2 all-to-all-start.30
  345.8 9.9 %collective-permute-done.22 = bf16[4,128,128]{1,2,0:T(8,128)(2,1)S(1)} collective-permute-done((bf16[4,128,128]{1,2,0:T(8,128)(2,1)S(1)}, bf16[4,128,128]{1,2,0:T(8,128)(2,1)S(1)}, u32[]{:S(2)}, u32[]{:S(2)}) %collective-permute-start.22) | collective-permute-done | bytes 131104 | tf_op jit(solution)/shard_map/ppermute | solution.py:76
  357.9 4.7 all-to-all-start.31
  365.3 6.7 all-to-all-done.31
  374.4 6.4 copy.391
  382.7 61.3 %while.48 = (s32[]{:T(128)}, bf16[16,128,128]{2,1,0:T(8,128)(2,1)S(1)}, bf16[4,4,4,128,128]{3,4,2,0,1:T(8,128)(2,1)}, s32[]{:T(128)}, bf16[4,2,4,128,128]{4,3,2,...) while((s32[]{:T(128)}, ...), condition=%wide.region_1.2_spmd, body=%wide.region_0.1_spmd.sunk | while | flops 551026688 | bytes 41418968 | solution.py:184
  390.0 6.7 all-to-all-done
  398.4 11.7 %all_to_all.176 = bf16[8,16,16,128]{3,1,2,0:T(8,128)(2,1)S(1)} all-to-all(bf16[8,16,16,128]{3,1,2,0:T(8,128)(2,1)S(1)} %copy.559), channel_id=1, replica_groups=mesh['s'=4,'t'=4,'x'=2] {'s','x'}, dimensions={0} | all-to-all | bytes 1048576 | tf_op jit(solution)/shard_map/while/body/all_to_all | solution.py:27
  418.4 5.6 all-to-all-done.2
  444.0 4.1 copy.398
  450.1 61.4 %while.49 = (s32[]{:T(128)}, bf16[16,128,128]{2,1,0:T(8,128)(2,1)S(1)}, bf16[4,4,4,128,128]{3,4,2,0,1:T(8,128)(2,1)}, s32[]{:T(128)}, bf16[4,2,4,128,128]{4,3,2,...) while((s32[]{:T(128)}, ...), condition=%wide.region_3.4_spmd, body=%wide.region_2.3_spmd.sunk | while | flops 551026688 | bytes 41418968 | solution.py:184
  457.4 6.7 all-to-all-done.4
  465.8 11.7 %all_to_all.177 = bf16[8,16,16,128]{3,1,2,0:T(8,128)(2,1)S(1)} all-to-all(bf16[8,16,16,128]{3,1,2,0:T(8,128)(2,1)S(1)} %copy.569), channel_id=1, replica_groups=mesh['s'=4,'t'=4,'x'=2] {'s','x'}, dimensions={0} | all-to-all | bytes 1048576 | tf_op jit(solution)/shard_map/while/body/all_to_all | solution.py:27
  485.9 5.6 all-to-all-done.6
  511.5 4.2 copy.403
  520.0 61.4 %while.50 = (s32[]{:T(128)}, bf16[16,128,128]{2,1,0:T(8,128)(2,1)S(1)}, bf16[4,4,4,128,128]{3,4,2,0,1:T(8,128)(2,1)}, s32[]{:T(128)}, bf16[4,2,4,128,128]{4,3,2,...) while((s32[]{:T(128)}, ...), condition=%wide.region_5.6_spmd, body=%wide.region_4.5_spmd.sunk | while | flops 551026688 | bytes 41418968 | solution.py:184
  527.4 6.7 all-to-all-done.8
  535.8 11.7 %all_to_all.178 = bf16[8,16,16,128]{3,1,2,0:T(8,128)(2,1)S(1)} all-to-all(bf16[8,16,16,128]{3,1,2,0:T(8,128)(2,1)S(1)} %copy.579), channel_id=1, replica_groups=mesh['s'=4,'t'=4,'x'=2] {'s','x'}, dimensions={0} | all-to-all | bytes 1048576 | tf_op jit(solution)/shard_map/while/body/all_to_all | solution.py:27
  555.9 5.6 all-to-all-done.10
  585.7 61.5 %while.51 = (s32[]{:T(128)}, bf16[16,128,128]{2,1,0:T(8,128)(2,1)S(1)}, bf16[4,4,4,128,128]{3,4,2,0,1:T(8,128)(2,1)}, s32[]{:T(128)}, bf16[4,2,4,128,128]{4,3,2,...) while((s32[]{:T(128)}, ...), condition=%wide.region_8.9_spmd, body=%wide.region_7.8_spmd.sunk | while | flops 551026688 | bytes 41419004 | solution.py:184
  591.9 7.9 %all-to-all-done.12 = bf16[8,16,16,128]{3,2,1,0:T(8,128)(2,1)S(1)} async-done(((bf16[8,16,16,128]{3,2,1,0:T(8,128)(2,1)}), bf16[8,16,16,128]{3,2,1,0:T(8,128)(2,1)S(1)}, u32[]{:S(2)}, u32[]{:S(2)}) %all-to-all-start.12) | async-done | bytes 524320 | tf_op jit(solution)/shard_map/while/body/all_to_all | solution.py:27
  601.5 11.7 %all_to_all.179 = bf16[8,16,16,128]{3,1,2,0:T(8,128)(2,1)S(1)} all-to-all(bf16[8,16,16,128]{3,1,2,0:T(8,128)(2,1)S(1)} %copy.589), channel_id=1, replica_groups=mesh['s'=4,'t'=4,'x'=2] {'s','x'}, dimensions={0} | all-to-all | bytes 1048576 | tf_op jit(solution)/shard_map/while/body/all_to_all | solution.py:27
  619.7 7.4 all-to-all-done.14
  647.2 4.3 copy.411
  664.3 5.6 collective-permute-done.18
  669.9 5.2 collective-permute-done.19
  678.5 15.3 %collective-permute-start.25 = (bf16[4,128,128]{2,1,0:T(8,128)(2,1)S(1)}, bf16[4,128,128]{2,1,0:T(8,128)(2,1)S(1)}, u32[]{:S(2)}, u32[]{:S(2)}) collective-permute-start(bf16[4,128,128]{2,1,0:T(8,128)(2,1)S(1)} %bitcast.1256), channel_id=1, source_target_pairs={{0,2},{2,10},{4,18},{6,26},{8,0},{10,8},{12,16},{14,24},{16,6},{18... | collective-permute-start | bytes 393224 | tf_op jit(solution)/shard_map/ppermute | solution.py:76
  693.9 6.3 collective-permute-start.26
  700.9 11.7 %collective-permute-start.35 = (bf16[2,4,128,128]{3,2,1,0:T(8,128)(2,1)S(1)}, bf16[2,4,128,128]{3,2,1,0:T(8,128)(2,1)S(1)}, u32[]{:S(2)}, u32[]{:S(2)}) collective-permute-start(bf16[2,4,128,128]{3,2,1,0:T(8,128)(2,1)S(1)} %pad_maximum_fusion.35), channel_id=1, source_target_pairs={{0,16},{8,24},{16,0},{24,8},{1,17},{9,25},{17,1},{25,9},{2,18},{10... | collective-permute-start | bytes 786440 | tf_op jit(solution)/shard_map/ppermute | solution.py:106
  723.9 36.3 %reduce-scatter.11.cloned.1.call-done = bf16[16,128,128]{2,1,0:T(8,128)(2,1)} async-done(((bf16[64,128,128]{2,1,0:T(8,128)(2,1)}), bf16[16,128,128]{2,1,0:T(8,128)(2,1)}) %reduce-scatter.11.cloned.1.call-update) | async-done | bytes 524304 | tf_op jit(solution)/shard_map/reduce_scatter | solution.py:133
  (465 shorter events, 410.4 us)
Async XLA Ops:
  11.0 29.6 %collective-permute-start.4 = (bf16[2,4,128,128]{2,3,1,0:T(8,128)(2,1)S(1)}, bf16[2,4,128,128]{2,3,1,0:T(8,128)(2,1)S(1)}, u32[]{:S(2)}, u32[]{:S(2)}) collective-permute-start(bf16[2,4,128,128]{2,3,1,0:T(8,128)(2,1)S(1)} %pad_maximum_fusion.28), channel_id=1, source_target_pairs={{0,8},{8,0},{16,24},{24,16},{1,9},{9,1},{17,25},{25,17},{2,10},{10... | collective-permute-start | bytes 786440 | tf_op jit(solution)/shard_map/ppermute | solution.py:106
  13.9 22.4 %collective-permute-start.1 = (bf16[4,128,128]{2,1,0:T(8,128)(2,1)}, bf16[4,128,128]{2,1,0:T(8,128)(2,1)S(1)}, u32[]{:S(2)}, u32[]{:S(2)}) collective-permute-start(bf16[4,128,128]{2,1,0:T(8,128)(2,1)} %get-tuple-element.595), channel_id=1, source_target_pairs={{0,8},{2,0},{4,24},{6,16},{8,10},{10,2},{12,26},{14,18},{16,12},{1... | collective-permute-start | bytes 393224 | tf_op jit(solution)/shard_map/ppermute | solution.py:76
  17.0 23.4 %collective-permute-start.2 = (bf16[4,128,128]{2,1,0:T(8,128)(2,1)}, bf16[4,128,128]{2,1,0:T(8,128)(2,1)S(1)}, u32[]{:S(2)}, u32[]{:S(2)}) collective-permute-start(bf16[4,128,128]{2,1,0:T(8,128)(2,1)} %get-tuple-element.594), channel_id=1, source_target_pairs={{0,16},{2,24},{4,0},{6,8},{8,18},{10,26},{12,2},{14,10},{16,20},{1... | collective-permute-start | bytes 393224 | tf_op jit(solution)/shard_map/ppermute | solution.py:76
  20.5 20.0 %collective-permute-start.3 = (bf16[4,128,128]{2,1,0:T(8,128)(2,1)S(1)}, bf16[4,128,128]{2,1,0:T(8,128)(2,1)S(1)}, u32[]{:S(2)}, u32[]{:S(2)}) collective-permute-start(bf16[4,128,128]{2,1,0:T(8,128)(2,1)S(1)} %get-tuple-element.593), channel_id=1, source_target_pairs={{0,24},{2,16},{4,8},{6,0},{8,26},{10,18},{12,10},{14,2},{16,28},{1... | collective-permute-start | bytes 393224 | tf_op jit(solution)/shard_map/ppermute | solution.py:76
  22.3 20.2 %collective-permute-start.5 = (bf16[2,4,128,128]{2,3,1,0:T(8,128)(2,1)S(1)}, bf16[2,4,128,128]{2,3,1,0:T(8,128)(2,1)S(1)}, u32[]{:S(2)}, u32[]{:S(2)}) collective-permute-start(bf16[2,4,128,128]{2,3,1,0:T(8,128)(2,1)S(1)} %pad_maximum_fusion.29), channel_id=1, source_target_pairs={{0,16},{8,24},{16,0},{24,8},{1,17},{9,25},{17,1},{25,9},{2,18},{10... | collective-permute-start | bytes 786440 | tf_op jit(solution)/shard_map/ppermute | solution.py:106
  52.0 17.7 %collective-permute-start.7 = (bf16[4,128,128]{2,1,0:T(8,128)(2,1)S(1)}, bf16[4,128,128]{2,1,0:T(8,128)(2,1)S(1)}, u32[]{:S(2)}, u32[]{:S(2)}) collective-permute-start(bf16[4,128,128]{2,1,0:T(8,128)(2,1)S(1)} %get-tuple-element.597), channel_id=1, source_target_pairs={{0,2},{2,0},{4,6},{6,4},{1,3},{3,1},{5,7},{7,5},{8,10},{10,8},{12,... | collective-permute-start | bytes 393224 | tf_op jit(solution)/shard_map/ppermute | solution.py:122
  52.6 19.5 %collective-permute-start.8 = (bf16[4,128,128]{2,1,0:T(8,128)(2,1)S(1)}, bf16[4,128,128]{2,1,0:T(8,128)(2,1)S(1)}, u32[]{:S(2)}, u32[]{:S(2)}) collective-permute-start(bf16[4,128,128]{2,1,0:T(8,128)(2,1)S(1)} %get-tuple-element.597), channel_id=1, source_target_pairs={{0,4},{2,6},{4,0},{6,2},{1,5},{3,7},{5,1},{7,3},{8,12},{10,14},{12... | collective-permute-start | bytes 393224 | tf_op jit(solution)/shard_map/ppermute | solution.py:122
  56.6 15.5 %collective-permute-start.9 = (bf16[4,128,128]{2,1,0:T(8,128)(2,1)S(1)}, bf16[4,128,128]{2,1,0:T(8,128)(2,1)S(1)}, u32[]{:S(2)}, u32[]{:S(2)}) collective-permute-start(bf16[4,128,128]{2,1,0:T(8,128)(2,1)S(1)} %get-tuple-element.597), channel_id=1, source_target_pairs={{0,6},{2,4},{4,2},{6,0},{1,7},{3,5},{5,3},{7,1},{8,14},{10,12},{12... | collective-permute-start | bytes 393224 | tf_op jit(solution)/shard_map/ppermute | solution.py:122
  65.5 12.7 %all-to-all-start.16 = ((bf16[8,16,16,128]{3,1,2,0:T(8,128)(2,1)}), bf16[8,16,16,128]{3,1,2,0:T(8,128)(2,1)S(1)}, u32[]{:S(2)}, u32[]{:S(2)}) async-start(bf16[8,16,16,128]{3,1,2,0:T(8,128)(2,1)} %copy.288), calls=%async_computation.16 | async-start | bytes 1048576 | tf_op jit(solution)/shard_map/all_to_all | solution.py:27
  69.0 38.8 %all-gather.15.cloned.1.call-start = ((), (), s32[]{:S(2)}) async-start(), calls=%async_computation.40 | async-start | bytes 1310720 | tf_op jit(solution)/shard_map/all_gather | solution.py:114
  80.1 13.5 %all-to-all-start.17 = ((bf16[8,16,16,128]{3,2,1,0:T(8,128)(2,1)}), bf16[8,16,16,128]{3,2,1,0:T(8,128)(2,1)}, u32[]{:S(2)}, u32[]{:S(2)}) async-start(bf16[8,16,16,128]{3,2,1,0:T(8,128)(2,1)} %copy.292), calls=%async_computation.17 | async-start | bytes 1048576 | tf_op jit(solution)/shard_map/all_to_all | solution.py:27
  110.4 13.0 %all-to-all-start.18 = ((bf16[8,16,16,128]{3,1,2,0:T(8,128)(2,1)}), bf16[8,16,16,128]{3,1,2,0:T(8,128)(2,1)S(1)}, u32[]{:S(2)}, u32[]{:S(2)}) async-start(bf16[8,16,16,128]{3,1,2,0:T(8,128)(2,1)} %copy.300), calls=%async_computation.18 | async-start | bytes 1048576 | tf_op jit(solution)/shard_map/all_to_all | solution.py:27
  114.1 33.3 %all-gather.17.cloned.1.call-start = ((), (), s32[]{:S(2)}) async-start(), calls=%async_computation.41 | async-start | bytes 1310720 | tf_op jit(solution)/shard_map/all_gather | solution.py:114
  115.1 38.7 %collective-permute-start.13 = (bf16[2,4,128,128]{2,3,1,0:T(8,128)(2,1)}, bf16[2,4,128,128]{2,3,1,0:T(8,128)(2,1)}, u32[]{:S(2)}, u32[]{:S(2)}) collective-permute-start(bf16[2,4,128,128]{2,3,1,0:T(8,128)(2,1)} %pad_maximum_fusion.31), channel_id=1, source_target_pairs={{0,8},{8,0},{16,24},{24,16},{1,9},{9,1},{17,25},{25,17},{2,10},{10... | collective-permute-start | bytes 786440 | tf_op jit(solution)/shard_map/ppermute | solution.py:106
  116.5 37.3 %collective-permute-start.14 = (bf16[2,4,128,128]{2,3,1,0:T(8,128)(2,1)}, bf16[2,4,128,128]{2,3,1,0:T(8,128)(2,1)}, u32[]{:S(2)}, u32[]{:S(2)}) collective-permute-start(bf16[2,4,128,128]{2,3,1,0:T(8,128)(2,1)} %pad_maximum_fusion.32), channel_id=1, source_target_pairs={{0,16},{8,24},{16,0},{24,8},{1,17},{9,25},{17,1},{25,9},{2,18},{10... | collective-permute-start | bytes 786440 | tf_op jit(solution)/shard_map/ppermute | solution.py:106
  119.2 34.6 %collective-permute-start.15 = (bf16[2,4,128,128]{2,3,1,0:T(8,128)(2,1)}, bf16[2,4,128,128]{2,3,1,0:T(8,128)(2,1)}, u32[]{:S(2)}, u32[]{:S(2)}) collective-permute-start(bf16[2,4,128,128]{2,3,1,0:T(8,128)(2,1)} %pad_maximum_fusion.33), channel_id=1, source_target_pairs={{0,24},{8,16},{16,8},{24,0},{1,25},{9,17},{17,9},{25,1},{2,26},{10... | collective-permute-start | bytes 786440 | tf_op jit(solution)/shard_map/ppermute | solution.py:106
  125.3 14.5 %all-to-all-start.19 = ((bf16[8,16,16,128]{3,2,1,0:T(8,128)(2,1)}), bf16[8,16,16,128]{3,2,1,0:T(8,128)(2,1)S(1)}, u32[]{:S(2)}, u32[]{:S(2)}) async-start(bf16[8,16,16,128]{3,2,1,0:T(8,128)(2,1)} %copy.303), calls=%async_computation.19 | async-start | bytes 1048576 | tf_op jit(solution)/shard_map/all_to_all | solution.py:27
  150.1 12.9 %all-to-all-start.20 = ((bf16[8,16,16,128]{3,1,2,0:T(8,128)(2,1)}), bf16[8,16,16,128]{3,1,2,0:T(8,128)(2,1)S(1)}, u32[]{:S(2)}, u32[]{:S(2)}) async-start(bf16[8,16,16,128]{3,1,2,0:T(8,128)(2,1)} %copy.311), calls=%async_computation.20 | async-start | bytes 1048576 | tf_op jit(solution)/shard_map/all_to_all | solution.py:27
  153.7 30.6 %all-gather.19.cloned.1.call-start = ((), (), s32[]{:S(2)}) async-start(), calls=%async_computation.42 | async-start | bytes 1310720 | tf_op jit(solution)/shard_map/all_gather | solution.py:114
  186.9 12.9 %all-to-all-start.22 = ((bf16[8,16,16,128]{3,1,2,0:T(8,128)(2,1)}), bf16[8,16,16,128]{3,1,2,0:T(8,128)(2,1)S(1)}, u32[]{:S(2)}, u32[]{:S(2)}) async-start(bf16[8,16,16,128]{3,1,2,0:T(8,128)(2,1)} %copy.330), calls=%async_computation.22 | async-start | bytes 1048576 | tf_op jit(solution)/shard_map/all_to_all | solution.py:27
  190.6 30.7 %all-gather.21.cloned.1.call-start = ((), (), s32[]{:S(2)}) async-start(), calls=%async_computation.43 | async-start | bytes 1310720 | tf_op jit(solution)/shard_map/all_gather | solution.py:114
  223.9 12.9 %all-to-all-start.24 = ((bf16[8,16,16,128]{3,1,2,0:T(8,128)(2,1)}), bf16[8,16,16,128]{3,1,2,0:T(8,128)(2,1)S(1)}, u32[]{:S(2)}, u32[]{:S(2)}) async-start(bf16[8,16,16,128]{3,1,2,0:T(8,128)(2,1)} %copy.341), calls=%async_computation.24 | async-start | bytes 1048576 | tf_op jit(solution)/shard_map/all_to_all | solution.py:27
  227.5 30.7 %all-gather.23.cloned.1.call-start = ((), (), s32[]{:S(2)}) async-start(), calls=%async_computation.44 | async-start | bytes 1310720 | tf_op jit(solution)/shard_map/all_gather | solution.py:114
  238.7 12.7 %all-to-all-start.25 = ((bf16[8,16,16,128]{3,2,1,0:T(8,128)(2,1)}), bf16[8,16,16,128]{3,2,1,0:T(8,128)(2,1)S(1)}, u32[]{:S(2)}, u32[]{:S(2)}) async-start(bf16[8,16,16,128]{3,2,1,0:T(8,128)(2,1)} %copy.344), calls=%async_computation.25 | async-start | bytes 1048576 | tf_op jit(solution)/shard_map/all_to_all | solution.py:27
  260.8 12.9 %all-to-all-start.26 = ((bf16[8,16,16,128]{3,1,2,0:T(8,128)(2,1)}), bf16[8,16,16,128]{3,1,2,0:T(8,128)(2,1)S(1)}, u32[]{:S(2)}, u32[]{:S(2)}) async-start(bf16[8,16,16,128]{3,1,2,0:T(8,128)(2,1)} %copy.352), calls=%async_computation.26 | async-start | bytes 1048576 | tf_op jit(solution)/shard_map/all_to_all | solution.py:27
  264.5 30.7 %all-gather.25.cloned.1.call-start = ((), (), s32[]{:S(2)}) async-start(), calls=%async_computation.45 | async-start | bytes 1310720 | tf_op jit(solution)/shard_map/all_gather | solution.py:114
  275.6 13.1 %all-to-all-start.27 = ((bf16[8,16,16,128]{3,2,1,0:T(8,128)(2,1)}), bf16[8,16,16,128]{3,2,1,0:T(8,128)(2,1)S(1)}, u32[]{:S(2)}, u32[]{:S(2)}) async-start(bf16[8,16,16,128]{3,2,1,0:T(8,128)(2,1)} %copy.355), calls=%async_computation.27 | async-start | bytes 1048576 | tf_op jit(solution)/shard_map/all_to_all | solution.py:27
  298.6 12.9 %all-to-all-start.28 = ((bf16[8,16,16,128]{3,1,2,0:T(8,128)(2,1)}), bf16[8,16,16,128]{3,1,2,0:T(8,128)(2,1)S(1)}, u32[]{:S(2)}, u32[]{:S(2)}) async-start(bf16[8,16,16,128]{3,1,2,0:T(8,128)(2,1)} %copy.363), calls=%async_computation.28 | async-start | bytes 1048576 | tf_op jit(solution)/shard_map/all_to_all | solution.py:27
  302.2 34.9 %all-gather.27.cloned.1.call-start = ((), (), s32[]{:S(2)}) async-start(), calls=%async_computation.46 | async-start | bytes 1310720 | tf_op jit(solution)/shard_map/all_gather | solution.py:114
  313.4 13.4 %all-to-all-start.29 = ((bf16[8,16,16,128]{3,2,1,0:T(8,128)(2,1)}), bf16[8,16,16,128]{3,2,1,0:T(8,128)(2,1)}, u32[]{:S(2)}, u32[]{:S(2)}) async-start(bf16[8,16,16,128]{3,2,1,0:T(8,128)(2,1)} %copy.366), calls=%async_computation.29 | async-start | bytes 1048576 | tf_op jit(solution)/shard_map/all_to_all | solution.py:27
  329.7 16.1 %collective-permute-start.20 = (bf16[4,128,128]{1,2,0:T(8,128)(2,1)S(1)}, bf16[4,128,128]{1,2,0:T(8,128)(2,1)S(1)}, u32[]{:S(2)}, u32[]{:S(2)}) collective-permute-start(bf16[4,128,128]{1,2,0:T(8,128)(2,1)S(1)} %bitcast.1252), channel_id=1, source_target_pairs={{0,0},{2,8},{4,16},{6,24},{8,2},{10,10},{12,18},{14,26},{16,4},{18... | collective-permute-start | bytes 393224 | tf_op jit(solution)/shard_map/ppermute | solution.py:76
  330.6 15.3 %collective-permute-start.21 = (bf16[4,128,128]{1,2,0:T(8,128)(2,1)S(1)}, bf16[4,128,128]{1,2,0:T(8,128)(2,1)S(1)}, u32[]{:S(2)}, u32[]{:S(2)}) collective-permute-start(bf16[4,128,128]{1,2,0:T(8,128)(2,1)S(1)} %bitcast.1253), channel_id=1, source_target_pairs={{0,8},{2,0},{4,24},{6,16},{8,10},{10,2},{12,26},{14,18},{16,12},{1... | collective-permute-start | bytes 393224 | tf_op jit(solution)/shard_map/ppermute | solution.py:76
  333.5 22.2 %collective-permute-start.22 = (bf16[4,128,128]{1,2,0:T(8,128)(2,1)S(1)}, bf16[4,128,128]{1,2,0:T(8,128)(2,1)S(1)}, u32[]{:S(2)}, u32[]{:S(2)}) collective-permute-start(bf16[4,128,128]{1,2,0:T(8,128)(2,1)S(1)} %bitcast.1254), channel_id=1, source_target_pairs={{0,16},{2,24},{4,0},{6,8},{8,18},{10,26},{12,2},{14,10},{16,20},{1... | collective-permute-start | bytes 393224 | tf_op jit(solution)/shard_map/ppermute | solution.py:76
  336.2 19.5 %collective-permute-start.23 = (bf16[4,128,128]{1,2,0:T(8,128)(2,1)S(1)}, bf16[4,128,128]{1,2,0:T(8,128)(2,1)S(1)}, u32[]{:S(2)}, u32[]{:S(2)}) collective-permute-start(bf16[4,128,128]{1,2,0:T(8,128)(2,1)S(1)} %bitcast.1257), channel_id=1, source_target_pairs={{0,24},{2,16},{4,8},{6,0},{8,26},{10,18},{12,10},{14,2},{16,28},{1... | collective-permute-start | bytes 393224 | tf_op jit(solution)/shard_map/ppermute | solution.py:76
  339.8 16.2 %all-to-all-start.30 = ((bf16[8,16,16,128]{3,1,2,0:T(8,128)(2,1)}), bf16[8,16,16,128]{3,1,2,0:T(8,128)(2,1)S(1)}, u32[]{:S(2)}, u32[]{:S(2)}) async-start(bf16[8,16,16,128]{3,1,2,0:T(8,128)(2,1)} %copy.373), calls=%async_computation.30 | async-start | bytes 1048576 | tf_op jit(solution)/shard_map/all_to_all | solution.py:27
  357.9 14.1 %all-to-all-start.31 = ((bf16[8,16,16,128]{3,2,1,0:T(8,128)(2,1)}), bf16[8,16,16,128]{3,2,1,0:T(8,128)(2,1)}, u32[]{:S(2)}, u32[]{:S(2)}) async-start(bf16[8,16,16,128]{3,2,1,0:T(8,128)(2,1)} %copy.376), calls=%async_computation.31 | async-start | bytes 1048576 | tf_op jit(solution)/shard_map/all_to_all | solution.py:27
  362.6 153.1 %reduce-scatter.5.cloned.1.call-start = ((), (), s32[]{:S(2)}) async-start(), calls=%async_computation.36 | async-start | bytes 2621440 | tf_op jit(solution)/shard_map/reduce_scatter | solution.py:133
  384.0 12.7 %all-to-all-start = ((bf16[8,16,16,128]{3,2,1,0:T(8,128)(2,1)}), bf16[8,16,16,128]{3,2,1,0:T(8,128)(2,1)S(1)}, u32[]{:S(2)}, u32[]{:S(2)}) async-start(bf16[8,16,16,128]{3,2,1,0:T(8,128)(2,1)} %bitcast.922), calls=%async_computation | async-start | bytes 1048576 | tf_op jit(solution)/shard_map/while/body/all_to_all | solution.py:27
  448.2 133.2 %reduce-scatter.7.cloned.1.call-start = ((), (), s32[]{:S(2)}) async-start(), calls=%async_computation.37 | async-start | bytes 2621440 | tf_op jit(solution)/shard_map/reduce_scatter | solution.py:133
  451.4 12.7 %all-to-all-start.4 = ((bf16[8,16,16,128]{3,2,1,0:T(8,128)(2,1)}), bf16[8,16,16,128]{3,2,1,0:T(8,128)(2,1)S(1)}, u32[]{:S(2)}, u32[]{:S(2)}) async-start(bf16[8,16,16,128]{3,2,1,0:T(8,128)(2,1)} %bitcast.963), calls=%async_computation.4 | async-start | bytes 1048576 | tf_op jit(solution)/shard_map/while/body/all_to_all | solution.py:27
  515.7 206.5 %reduce-scatter.9.cloned.1.call-start = ((), (), s32[]{:S(2)}) async-start(), calls=%async_computation.38 | async-start | bytes 2621440 | tf_op jit(solution)/shard_map/reduce_scatter | solution.py:133
  651.5 108.8 %reduce-scatter.11.cloned.1.call-start = ((), (), s32[]{:S(2)}) async-start(), calls=%async_computation.39 | async-start | bytes 2621440 | tf_op jit(solution)/shard_map/reduce_scatter | solution.py:133
  661.0 14.2 %collective-permute-start.19 = (bf16[4,128,128]{2,1,0:T(8,128)(2,1)S(1)}, bf16[4,128,128]{2,1,0:T(8,128)(2,1)S(1)}, u32[]{:S(2)}, u32[]{:S(2)}) collective-permute-start(bf16[4,128,128]{2,1,0:T(8,128)(2,1)S(1)} %bitcast.1263), channel_id=1, source_target_pairs={{0,6},{2,14},{4,22},{6,30},{8,4},{10,12},{12,20},{14,28},{16,2},{1... | collective-permute-start | bytes 393224 | tf_op jit(solution)/shard_map/ppermute | solution.py:76
  675.6 38.9 %collective-permute-start.34 = (bf16[2,4,128,128]{3,2,1,0:T(8,128)(2,1)S(1)}, bf16[2,4,128,128]{3,2,1,0:T(8,128)(2,1)S(1)}, u32[]{:S(2)}, u32[]{:S(2)}) collective-permute-start(bf16[2,4,128,128]{3,2,1,0:T(8,128)(2,1)S(1)} %pad_maximum_fusion.34), channel_id=1, source_target_pairs={{0,8},{8,0},{16,24},{24,16},{1,9},{9,1},{17,25},{25,17},{2,10},{10... | collective-permute-start | bytes 786440 | tf_op jit(solution)/shard_map/ppermute | solution.py:106
  677.7 23.2 %collective-permute-start.24 = (bf16[4,128,128]{2,1,0:T(8,128)(2,1)S(1)}, bf16[4,128,128]{2,1,0:T(8,128)(2,1)S(1)}, u32[]{:S(2)}, u32[]{:S(2)}) collective-permute-start(bf16[4,128,128]{2,1,0:T(8,128)(2,1)S(1)} %bitcast.1259), channel_id=1, source_target_pairs={{0,0},{2,8},{4,16},{6,24},{8,2},{10,10},{12,18},{14,26},{16,4},{18... | collective-permute-start | bytes 393224 | tf_op jit(solution)/shard_map/ppermute | solution.py:76
  678.5 34.1 %collective-permute-start.25 = (bf16[4,128,128]{2,1,0:T(8,128)(2,1)S(1)}, bf16[4,128,128]{2,1,0:T(8,128)(2,1)S(1)}, u32[]{:S(2)}, u32[]{:S(2)}) collective-permute-start(bf16[4,128,128]{2,1,0:T(8,128)(2,1)S(1)} %bitcast.1256), channel_id=1, source_target_pairs={{0,2},{2,10},{4,18},{6,26},{8,0},{10,8},{12,16},{14,24},{16,6},{18... | collective-permute-start | bytes 393224 | tf_op jit(solution)/shard_map/ppermute | solution.py:76
  693.9 18.7 %collective-permute-start.26 = (bf16[4,128,128]{2,1,0:T(8,128)(2,1)S(1)}, bf16[4,128,128]{2,1,0:T(8,128)(2,1)S(1)}, u32[]{:S(2)}, u32[]{:S(2)}) collective-permute-start(bf16[4,128,128]{2,1,0:T(8,128)(2,1)S(1)} %bitcast.1255), channel_id=1, source_target_pairs={{0,4},{2,12},{4,20},{6,28},{8,6},{10,14},{12,22},{14,30},{16,0},{1... | collective-permute-start | bytes 393224 | tf_op jit(solution)/shard_map/ppermute | solution.py:76
  700.9 17.4 %collective-permute-start.35 = (bf16[2,4,128,128]{3,2,1,0:T(8,128)(2,1)S(1)}, bf16[2,4,128,128]{3,2,1,0:T(8,128)(2,1)S(1)}, u32[]{:S(2)}, u32[]{:S(2)}) collective-permute-start(bf16[2,4,128,128]{3,2,1,0:T(8,128)(2,1)S(1)} %pad_maximum_fusion.35), channel_id=1, source_target_pairs={{0,16},{8,24},{16,0},{24,8},{1,17},{9,25},{17,1},{25,9},{2,18},{10... | collective-permute-start | bytes 786440 | tf_op jit(solution)/shard_map/ppermute | solution.py:106
  (52 other events, 813.9 us)
Sparse Core Ops, SparseCore 0:
  72.0 35.7 all-gather.14
  119.7 27.7 all-gather.16
  156.4 27.9 all-gather.18
  193.3 27.9 all-gather.20
  230.2 27.9 all-gather.22
  267.1 27.9 all-gather.24
  307.8 27.8 all-gather.26
  448.3 42.7 reduce-scatter.4
  515.8 42.7 reduce-scatter.6
  651.6 55.2 reduce-scatter.8
  709.9 50.3 reduce-scatter.10

commit v12 on v11

--- a/solution.py
+++ b/solution.py
@@ -92,8 +92,10 @@
     def settled(parts):
         return jnp.einsum("aj,bjr->bar", order, parts, preferred_element_type=F32).astype(BF16)
 
+    def unsettled(acts):
+        return jnp.einsum("aj,bar->bjr", order, acts, preferred_element_type=F32).astype(BF16)
+
     def leave(acts):
-        acts = jnp.einsum("aj,bar->bjr", order, acts, preferred_element_type=F32).astype(BF16)
         parts = acts.reshape(own, size, micros, rows).transpose(2, 0, 1, 3)
         parts = turned(parts.reshape(sections, sub, size, rows), s_index, line, outof)
         return parts.reshape(1, held * size, rows)
@@ -113,9 +115,6 @@
     def gathered(part):
         return lax.all_gather(part, "t", axis=0, tiled=False)
 
-    def pair_of(full):
-        return [full[:, f].reshape(own, size, size) for f in range(2)]
-
     def around(value_of):
         moved = [value_of(0)]
         for mask in range(1, groups):
@@ -141,29 +140,51 @@
     parts = [ordered(part) for part in scattered(rights[0], lefts[0])]
     current = arriving(inputs)
     current, parts[0] = lax.optimization_barrier((current, parts[0]))
-    first = [gathered_directly(parts[0][f]) for f in range(2)]
-    later, first[0] = lax.optimization_barrier(((rights[1:], lefts[1:]), first[0]))
-    rights, lefts = later
-    weights = [jnp.stack(first, axis=1)]
-    for loop in range(loops - 1):
-        parts.extend(ordered(part) for part in scattered(rights[loop], lefts[loop]))
-
+    once = 1 + s_index // sections
+    first = jnp.stack([gathered_directly(parts[0][f]) for f in range(2)], axis=1)[:, None]
+    starts = [0, 1] + list(range(PAIRED, layers, PAIRED)) + [layers]
+    ahead = gathered(jnp.stack(parts[1:2]))
+    weights = {}
+    stored = {}
     current = settled(current)
-    kept = [jnp.zeros((layers, own, size, micros * rows), BF16) for _ in range(2)]
-    for layer in range(layers):
-        if layer + 1 < layers:
-            current, parts[layer + 1] = lax.optimization_barrier((current, parts[layer + 1]))
-            weights.append(gathered(parts[layer + 1]))
-        else:
+
+    def factors_of(layer):
+        full, step = weights[layer]
+        return [full[:, step, f].reshape(own, size, size) for f in range(2)]
+
+    def forward_stretch(stretch):
+        def run(_, carry):
+            acts = carry[0]
+            saved = []
+            for layer in stretch:
+                acts, pair = forward_layer(acts, *factors_of(layer))
+                saved += pair
+            return (acts, *saved[1:])
+
+        return run
+
+    for begin, end in zip(starts, starts[1:]):
+        stretch = range(begin, end)
+        full = ahead if begin else first
+        if begin:
+            coming = range(end, min(end + PAIRED, layers))
+            if begin == 1:
+                current, rights, lefts = lax.optimization_barrier((current, rights[1:], lefts[1:]))
+                for loop in range(loops - 1):
+                    parts.extend(ordered(part) for part in scattered(rights[loop], lefts[loop]))
+            if coming:
+                ahead = gathered(jnp.stack([parts[layer] for layer in coming]))
+        weights.update((layer, (full, layer - begin)) for layer in stretch)
+        if end + PAIRED == layers:
             current, cotangent = lax.optimization_barrier((current, cotangent))
             grad = settled(arriving(cotangent))
-        factors = pair_of(weights[layer]) if layer else [one.reshape(own, size, size) for one in first]
-        current, saved = forward_layer(current, *factors)
-        kept = [lax.dynamic_update_index_in_dim(all_of, one, layer, 0) for all_of, one in zip(kept, saved)]
-        current, kept = lax.optimization_barrier((current, kept))
-    outputs = leave(current)
-
-    once = 1 + s_index // sections
+        blanks = [jnp.zeros(current.shape, BF16) for _ in range(2 * len(stretch) - 1)]
+        entered = current
+        current, *saved = lax.fori_loop(0, once, forward_stretch(stretch), (current, *blanks))
+        saved = [entered] + saved
+        stored.update((layer, saved[2 * step : 2 * step + 2]) for step, layer in enumerate(stretch))
+    outputs = leave(unsettled(current))
+
     sums = [None] * layers
 
     def backward_pair(top):
@@ -171,8 +192,7 @@
             grad, _ = carry
             terms = []
             for layer in range(top, top - PAIRED, -1):
-                saved = [all_of[layer] for all_of in kept]
-                grad, *pair = backward_layer(grad, *pair_of(weights[layer]), saved)
+                grad, *pair = backward_layer(grad, *factors_of(layer), stored[layer])
                 terms += pair
             return grad, laid_out(*terms)
 
@@ -186,6 +206,9 @@
             asked = totals[top + 2 * PAIRED]
             grad, terms, totals[top + 2 * PAIRED] = lax.optimization_barrier((grad, terms, asked))
         totals[top] = summed(terms)
+    grad = lax.fori_loop(0, once, lambda _, acts: unsettled(acts), grad)
+    if 2 * PAIRED <= layers:
+        grad, totals[2 * PAIRED - 1] = lax.optimization_barrier((grad, totals[2 * PAIRED - 1]))
     for top, total in totals.items():
         for step in range(PAIRED):
             sums[top - step] = [total[2 * step], total[2 * step + 1]]

time: 799 us -> 758 us (0.949)
  the two profiles are of different devices: /device:TPU:0 before, /device:TPU:17 now
where the time goes in v12:
time: 758 us; the launch traced here: 747 us
  waiting for transfers between devices  218 us (29%)
  blocking collectives  180 us (24%)
  local copies, waits for them, and re-layouts  127 us (17%)
  starting transfers between devices  119 us (16%)
  matrix products  59.9 us (8%)
  other arithmetic  24.2 us (3%)
  between operations  15.8 us (2%)
    all_to_all x15, blocking collectives, exchange(): lax.all_to_all(pieces, WIDE, split_axis=0, concat_axis=0, tiled=True)  180 us
    all_to_all x17, waiting for transfers between devices, exchange(): lax.all_to_all(pieces, WIDE, split_axis=0, concat_axis=0, tiled=True)  103 us
    all_to_all x17, starting transfers between devices, exchange(): lax.all_to_all(pieces, WIDE, split_axis=0, concat_axis=0, tiled=True)  67.4 us
    ppermute x16, waiting for transfers between devices, turned(): moved.append(lax.ppermute(pick(parts, send_by ^ mask), ('s', 't'), pairs))  55.3 us
    ppermute x15, waiting for transfers between devices, scattered(): moved.append(lax.ppermute(value, 's', pairs))  33.4 us
    ppermute x16, starting transfers between devices, turned(): moved.append(lax.ppermute(pick(parts, send_by ^ mask), ('s', 't'), pairs))  30.7 us
    ppermute x6, waiting for transfers between devices, around(): lax.ppermute(value_of(mask), 't', [(t, t ^ mask) for t in range(groups)])  25.7 us
    while x15, local copies, waits for them, and re-layouts, body(): grad, terms = lax.fori_loop(0, once, backward_pair(top), (grad, blank))  24 us
  transfers between devices with their start and end apart: 62, of which 43 were waited for; matrix products, arithmetic and copies ran while one was open for 20% of the time, Pallas kernels for 0%

profile of v12, /device:TPU:17, one launch (start us, length us, event | category | flops | bytes accessed | tf_op | source)
XLA Modules:
  0.0 747.0 jit_solution(5643364293458426558)
XLA Ops:
  21.2 9.9 %collective-permute-done.6 = bf16[2,4,128,128]{2,3,1,0:T(8,128)(2,1)S(1)} collective-permute-done((bf16[2,4,128,128]{2,3,1,0:T(8,128)(2,1)S(1)}, bf16[2,4,128,128]{2,3,1,0:T(8,128)(2,1)S(1)}, u32[]{:S(2)}, u32[]{:S(2)}) %collective-permute-start.6) | collective-permute-done | bytes 262176 | tf_op jit(solution)/shard_map/ppermute | solution.py:108
  58.0 12.4 %collective-permute-done.9 = bf16[4,128,128]{2,1,0:T(8,128)(2,1)} collective-permute-done((bf16[4,128,128]{2,1,0:T(8,128)(2,1)}, bf16[4,128,128]{2,1,0:T(8,128)(2,1)}, u32[]{:S(2)}, u32[]{:S(2)}) %collective-permute-start.9) | collective-permute-done | bytes 131104 | tf_op jit(solution)/shard_map/ppermute | solution.py:121
  71.6 6.0 collective-permute-done.11
  83.4 28.0 %while.131 = (s32[]{:T(128)}, bf16[16,128,128]{2,1,0:T(8,128)(2,1)S(1)}, bf16[16,128,128]{2,0,1:T(8,128)(2,1)}, s32[]{:T(128)}, bf16[4,1,2,4,128,128]{4,5,3,0,2,1:T(8,128)(2,1)S(1)}, /*index=5*/s32[]{:T(128)}) while((s32[]{:T(128)}, bf16[16,128,128]{2,1,0:T(8,128)(2,1)S(1)}, bf16[16,128,128]{2,0,1:T(8,128)(2,1)}, s32[]{:T(128)}, ...), condition=%wide.region_1.2_spmd, body=%wide.region_0.1_spmd.sunk | while | flops 137363456 | bytes 16777344 | solution.py:183
  83.9 13.5 %all_to_all.192 = bf16[8,16,16,128]{3,1,2,0:T(8,128)(2,1)S(1)} all-to-all(bf16[8,16,16,128]{3,1,2,0:T(8,128)(2,1)S(1)} %copy.470), channel_id=1, replica_groups=mesh['s'=4,'t'=4,'x'=2] {'s','x'}, dimensions={0} | all-to-all | bytes 1048576 | tf_op jit(solution)/shard_map/while/body/all_to_all | solution.py:27
  102.4 8.6 %all-to-all-done.1 = bf16[8,16,16,128]{3,1,2,0:T(8,128)(2,1)S(1)} async-done(((bf16[8,16,16,128]{3,1,2,0:T(8,128)(2,1)}), bf16[8,16,16,128]{3,1,2,0:T(8,128)(2,1)S(1)}, u32[]{:S(2)}, u32[]{:S(2)}) %all-to-all-start.1) | async-done | bytes 524320 | tf_op jit(solution)/shard_map/while/body/all_to_all | solution.py:27
  116.5 5.7 collective-permute-done.14
  122.2 5.6 collective-permute-done.15
  134.2 26.4 %while.132 = (s32[]{:T(128)}, bf16[16,128,128]{2,1,0:T(8,128)(2,1)S(1)}, bf16[16,128,128]{2,0,1:T(8,128)(2,1)}, s32[]{:T(128)}, bf16[4,1,2,4,128,128]{4,5,3,0,2,1:T(8,128)(2,1)S(1)}, /*index=5*/s32[]{:T(128)}) while((s32[]{:T(128)}, bf16[16,128,128]{2,1,0:T(8,128)(2,1)S(1)}, bf16[16,128,128]{2,0,1:T(8,128)(2,1)}, s32[]{:T(128)}, ...), condition=%wide.region_3.4_spmd, body=%wide.region_2.3_spmd.sunk | while | flops 137363456 | bytes 16777344 | solution.py:183
  134.8 11.8 %all_to_all.193 = bf16[8,16,16,128]{3,1,2,0:T(8,128)(2,1)S(1)} all-to-all(bf16[8,16,16,128]{3,1,2,0:T(8,128)(2,1)S(1)} %copy.474), channel_id=1, replica_groups=mesh['s'=4,'t'=4,'x'=2] {'s','x'}, dimensions={0} | all-to-all | bytes 1048576 | tf_op jit(solution)/shard_map/while/body/all_to_all | solution.py:27
  151.7 8.4 %all-to-all-done.3 = bf16[8,16,16,128]{3,1,2,0:T(8,128)(2,1)S(1)} async-done(((bf16[8,16,16,128]{3,1,2,0:T(8,128)(2,1)}), bf16[8,16,16,128]{3,1,2,0:T(8,128)(2,1)S(1)}, u32[]{:S(2)}, u32[]{:S(2)}) %all-to-all-start.3) | async-done | bytes 524320 | tf_op jit(solution)/shard_map/while/body/all_to_all | solution.py:27
  166.5 52.9 %while.133 = (s32[]{:T(128)}, bf16[16,128,128]{2,1,0:T(8,128)(2,1)S(1)}, bf16[16,128,128]{2,0,1:T(8,128)(2,1)}, bf16[16,128,128]{2,1,0:T(8,128)(2,1)}, bf16[16,1...) while((s32[]{:T(128)}, ...), condition=%wide.region_5.6_spmd, body=%wide.region_4.5_spmd.sunk | while | flops 274726912 | bytes 35127496 | solution.py:183
  167.1 12.1 %all_to_all.194 = bf16[8,16,16,128]{3,1,2,0:T(8,128)(2,1)S(1)} all-to-all(bf16[8,16,16,128]{3,1,2,0:T(8,128)(2,1)S(1)} %copy.480), channel_id=1, replica_groups=mesh['s'=4,'t'=4,'x'=2] {'s','x'}, dimensions={0} | all-to-all | bytes 1048576 | tf_op jit(solution)/shard_map/while/body/all_to_all | solution.py:27
  180.4 11.7 %all_to_all.195 = bf16[8,16,16,128]{3,1,2,0:T(8,128)(2,1)S(1)} all-to-all(bf16[8,16,16,128]{3,1,2,0:T(8,128)(2,1)S(1)} %copy.481), channel_id=1, replica_groups=mesh['s'=4,'t'=4,'x'=2] {'s','x'}, dimensions={0} | all-to-all | bytes 1048576 | tf_op jit(solution)/shard_map/while/body/all_to_all | solution.py:27
  192.9 11.9 %all_to_all.196 = bf16[8,16,16,128]{3,1,2,0:T(8,128)(2,1)S(1)} all-to-all(bf16[8,16,16,128]{3,1,2,0:T(8,128)(2,1)S(1)} %copy.482), channel_id=1, replica_groups=mesh['s'=4,'t'=4,'x'=2] {'s','x'}, dimensions={0} | all-to-all | bytes 1048576 | tf_op jit(solution)/shard_map/while/body/all_to_all | solution.py:27
  210.3 8.6 %all-to-all-done.7 = bf16[8,16,16,128]{3,1,2,0:T(8,128)(2,1)S(1)} async-done(((bf16[8,16,16,128]{3,1,2,0:T(8,128)(2,1)}), bf16[8,16,16,128]{3,1,2,0:T(8,128)(2,1)S(1)}, u32[]{:S(2)}, u32[]{:S(2)}) %all-to-all-start.7) | async-done | bytes 524320 | tf_op jit(solution)/shard_map/while/body/all_to_all | solution.py:27
  234.4 6.3 collective-permute-done.20
  263.0 53.7 %while.134 = (s32[]{:T(128)}, bf16[16,128,128]{2,1,0:T(8,128)(2,1)S(1)}, bf16[16,128,128]{2,0,1:T(8,128)(2,1)}, bf16[16,128,128]{2,1,0:T(8,128)(2,1)}, bf16[16,1...) while((s32[]{:T(128)}, bf16[16,128,128]{2,1,0:T(8,128)(2,1)S(1)}, ...), condition=%wide.region_7.8_spmd, body=%wide.region_6.7_spmd.sunk | while | flops 274726912 | bytes 35127496 | solution.py:183
  265.3 12.3 %all_to_all.197 = bf16[8,16,16,128]{3,1,2,0:T(8,128)(2,1)S(1)} all-to-all(bf16[8,16,16,128]{3,1,2,0:T(8,128)(2,1)S(1)} %copy.488), channel_id=1, replica_groups=mesh['s'=4,'t'=4,'x'=2] {'s','x'}, dimensions={0} | all-to-all | bytes 1048576 | tf_op jit(solution)/shard_map/while/body/all_to_all | solution.py:27
  278.3 11.7 %all_to_all.198 = bf16[8,16,16,128]{3,1,2,0:T(8,128)(2,1)S(1)} all-to-all(bf16[8,16,16,128]{3,1,2,0:T(8,128)(2,1)S(1)} %copy.489), channel_id=1, replica_groups=mesh['s'=4,'t'=4,'x'=2] {'s','x'}, dimensions={0} | all-to-all | bytes 1048576 | tf_op jit(solution)/shard_map/while/body/all_to_all | solution.py:27
  290.9 11.7 %all_to_all.199 = bf16[8,16,16,128]{3,1,2,0:T(8,128)(2,1)S(1)} all-to-all(bf16[8,16,16,128]{3,1,2,0:T(8,128)(2,1)S(1)} %copy.490), channel_id=1, replica_groups=mesh['s'=4,'t'=4,'x'=2] {'s','x'}, dimensions={0} | all-to-all | bytes 1048576 | tf_op jit(solution)/shard_map/while/body/all_to_all | solution.py:27
  307.8 8.4 %all-to-all-done.11 = bf16[8,16,16,128]{3,1,2,0:T(8,128)(2,1)S(1)} async-done(((bf16[8,16,16,128]{3,1,2,0:T(8,128)(2,1)}), bf16[8,16,16,128]{3,1,2,0:T(8,128)(2,1)S(1)}, u32[]{:S(2)}, u32[]{:S(2)}) %all-to-all-start.11) | async-done | bytes 524320 | tf_op jit(solution)/shard_map/while/body/all_to_all | solution.py:27
  319.4 53.2 %while.135 = (s32[]{:T(128)}, bf16[16,128,128]{2,1,0:T(8,128)(2,1)S(1)}, bf16[16,128,128]{2,0,1:T(8,128)(2,1)}, bf16[16,128,128]{2,1,0:T(8,128)(2,1)}, bf16[16,1...) while((s32[]{:T(128)}, ...), condition=%wide.region_9.10_spmd, body=%wide.region_8.9_spmd.sunk | while | flops 274726912 | bytes 35127496 | solution.py:183
  321.4 12.1 %all_to_all.200 = bf16[8,16,16,128]{3,1,2,0:T(8,128)(2,1)S(1)} all-to-all(bf16[8,16,16,128]{3,1,2,0:T(8,128)(2,1)S(1)} %copy.496), channel_id=1, replica_groups=mesh['s'=4,'t'=4,'x'=2] {'s','x'}, dimensions={0} | all-to-all | bytes 1048576 | tf_op jit(solution)/shard_map/while/body/all_to_all | solution.py:27
  334.2 11.7 %all_to_all.201 = bf16[8,16,16,128]{3,1,2,0:T(8,128)(2,1)S(1)} all-to-all(bf16[8,16,16,128]{3,1,2,0:T(8,128)(2,1)S(1)} %copy.497), channel_id=1, replica_groups=mesh['s'=4,'t'=4,'x'=2] {'s','x'}, dimensions={0} | all-to-all | bytes 1048576 | tf_op jit(solution)/shard_map/while/body/all_to_all | solution.py:27
  346.8 11.7 %all_to_all.202 = bf16[8,16,16,128]{3,1,2,0:T(8,128)(2,1)S(1)} all-to-all(bf16[8,16,16,128]{3,1,2,0:T(8,128)(2,1)S(1)} %copy.498), channel_id=1, replica_groups=mesh['s'=4,'t'=4,'x'=2] {'s','x'}, dimensions={0} | all-to-all | bytes 1048576 | tf_op jit(solution)/shard_map/while/body/all_to_all | solution.py:27
  363.7 8.4 %all-to-all-done.15 = bf16[8,16,16,128]{3,1,2,0:T(8,128)(2,1)S(1)} async-done(((bf16[8,16,16,128]{3,1,2,0:T(8,128)(2,1)}), bf16[8,16,16,128]{3,1,2,0:T(8,128)(2,1)S(1)}, u32[]{:S(2)}, u32[]{:S(2)}) %all-to-all-start.15) | async-done | bytes 524320 | tf_op jit(solution)/shard_map/while/body/all_to_all | solution.py:27
  380.6 61.3 %while.136 = (s32[]{:T(128)}, bf16[16,128,128]{2,1,0:T(8,128)(2,1)S(1)}, bf16[4,4,4,128,128]{3,4,2,0,1:T(8,128)(2,1)}, s32[]{:T(128)}, bf16[4,2,2,4,128,128]{5,4...) while((s32[]{:T(128)}, ...), condition=%wide.region_11.12_spmd, body=%wide.region_10.11_spmd.sunk | while | flops 551026688 | bytes 51904876 | solution.py:204
  389.2 5.8 all-to-all-done.16
  397.0 12.1 %all_to_all.203 = bf16[8,16,16,128]{3,1,2,0:T(8,128)(2,1)S(1)} all-to-all(bf16[8,16,16,128]{3,1,2,0:T(8,128)(2,1)S(1)} %copy.502), channel_id=1, replica_groups=mesh['s'=4,'t'=4,'x'=2] {'s','x'}, dimensions={0} | all-to-all | bytes 1048576 | tf_op jit(solution)/shard_map/while/body/all_to_all | solution.py:27
  433.1 5.3 all-to-all-done.19
  448.0 61.0 %while.137 = (s32[]{:T(128)}, bf16[16,128,128]{2,1,0:T(8,128)(2,1)S(1)}, bf16[4,4,4,128,128]{3,4,2,0,1:T(8,128)(2,1)}, s32[]{:T(128)}, bf16[4,2,2,4,128,128]{5,4...) while((s32[]{:T(128)}, ...), condition=%wide.region_13.14_spmd, body=%wide.region_12.13_spmd.sunk | while | flops 551026688 | bytes 51904876 | solution.py:204
  456.2 5.9 all-to-all-done.20
  464.2 12.0 %all_to_all.204 = bf16[8,16,16,128]{3,1,2,0:T(8,128)(2,1)S(1)} all-to-all(bf16[8,16,16,128]{3,1,2,0:T(8,128)(2,1)S(1)} %copy.512), channel_id=1, replica_groups=mesh['s'=4,'t'=4,'x'=2] {'s','x'}, dimensions={0} | all-to-all | bytes 1048576 | tf_op jit(solution)/shard_map/while/body/all_to_all | solution.py:27
  500.2 5.3 all-to-all-done.23
  518.1 61.1 %while.138 = (s32[]{:T(128)}, bf16[16,128,128]{2,1,0:T(8,128)(2,1)S(1)}, bf16[4,4,4,128,128]{3,4,2,0,1:T(8,128)(2,1)}, s32[]{:T(128)}, bf16[4,2,2,4,128,128]{5,4...) while((s32[]{:T(128)}, ...), condition=%wide.region_15.16_spmd, body=%wide.region_14.15_spmd.sunk | while | flops 551026688 | bytes 51904876 | solution.py:204
  526.5 5.8 all-to-all-done.24
  534.3 12.0 %all_to_all.205 = bf16[8,16,16,128]{3,1,2,0:T(8,128)(2,1)S(1)} all-to-all(bf16[8,16,16,128]{3,1,2,0:T(8,128)(2,1)S(1)} %copy.522), channel_id=1, replica_groups=mesh['s'=4,'t'=4,'x'=2] {'s','x'}, dimensions={0} | all-to-all | bytes 1048576 | tf_op jit(solution)/shard_map/while/body/all_to_all | solution.py:27
  570.4 5.3 all-to-all-done.27
  587.7 61.1 %while.139 = (s32[]{:T(128)}, bf16[16,128,128]{2,1,0:T(8,128)(2,1)S(1)}, bf16[4,4,4,128,128]{3,4,2,0,1:T(8,128)(2,1)}, s32[]{:T(128)}, bf16[4,1,2,4,128,128]{5,4...) while((s32[]{:T(128)}, ...), condition=%wide.region_18.19_spmd, body=%wide.region_17.18_spmd.sunk | while | flops 551026688 | bytes 51904884 | solution.py:204
  596.0 5.9 all-to-all-done.28
  604.0 12.0 %all_to_all.206 = bf16[8,16,16,128]{3,1,2,0:T(8,128)(2,1)S(1)} all-to-all(bf16[8,16,16,128]{3,1,2,0:T(8,128)(2,1)S(1)} %copy.532), channel_id=1, replica_groups=mesh['s'=4,'t'=4,'x'=2] {'s','x'}, dimensions={0} | all-to-all | bytes 1048576 | tf_op jit(solution)/shard_map/while/body/all_to_all | solution.py:27
  640.0 5.3 all-to-all-done.31
  664.0 11.6 %collective-permute-done.16 = bf16[4,128,128]{2,1,0:T(8,128)(2,1)S(1)} collective-permute-done((bf16[4,128,128]{2,1,0:T(8,128)(2,1)S(1)}, bf16[4,128,128]{2,1,0:T(8,128)(2,1)S(1)}, u32[]{:S(2)}, u32[]{:S(2)}) %collective-permute-start.16) | collective-permute-done | bytes 131104 | tf_op jit(solution)/shard_map/ppermute | solution.py:76
  675.6 7.4 collective-permute-done.17
  683.0 8.1 %collective-permute-done.19 = bf16[4,128,128]{2,1,0:T(8,128)(2,1)S(1)} collective-permute-done((bf16[4,128,128]{2,1,0:T(8,128)(2,1)S(1)}, bf16[4,128,128]{2,1,0:T(8,128)(2,1)S(1)}, u32[]{:S(2)}, u32[]{:S(2)}) %collective-permute-start.19) | collective-permute-done | bytes 131104 | tf_op jit(solution)/shard_map/ppermute | solution.py:76
  699.5 6.2 collective-permute-done.36
  716.2 5.0 collective-permute-start.24
  (539 shorter events, 377.6 us)
Async XLA Ops:
  7.2 124.5 %all-gather.9.cloned.1.call-start = ((), (), s32[]{:S(2)}) async-start(), calls=%async_computation.40 | async-start | bytes 1310720 | tf_op jit(solution)/shard_map/all_gather | solution.py:116
  12.6 18.4 %collective-permute-start.6 = (bf16[2,4,128,128]{2,3,1,0:T(8,128)(2,1)S(1)}, bf16[2,4,128,128]{2,3,1,0:T(8,128)(2,1)S(1)}, u32[]{:S(2)}, u32[]{:S(2)}) collective-permute-start(bf16[2,4,128,128]{2,3,1,0:T(8,128)(2,1)S(1)} %pad_maximum_fusion.31), channel_id=1, source_target_pairs={{0,24},{8,16},{16,8},{24,0},{1,25},{9,17},{17,9},{25,1},{2,26},{10... | collective-permute-start | bytes 786440 | tf_op jit(solution)/shard_map/ppermute | solution.py:108
  13.8 19.7 %collective-permute-start = (bf16[4,128,128]{2,1,0:T(8,128)(2,1)}, bf16[4,128,128]{2,1,0:T(8,128)(2,1)S(1)}, u32[]{:S(2)}, u32[]{:S(2)}) collective-permute-start(bf16[4,128,128]{2,1,0:T(8,128)(2,1)} %get-tuple-element.957), channel_id=1, source_target_pairs={{0,0},{2,8},{4,16},{6,24},{8,2},{10,10},{12,18},{14,26},{16,4},{18... | collective-permute-start | bytes 393224 | tf_op jit(solution)/shard_map/ppermute | solution.py:76
  17.0 17.3 %collective-permute-start.1 = (bf16[4,128,128]{2,1,0:T(8,128)(2,1)}, bf16[4,128,128]{2,1,0:T(8,128)(2,1)}, u32[]{:S(2)}, u32[]{:S(2)}) collective-permute-start(bf16[4,128,128]{2,1,0:T(8,128)(2,1)} %get-tuple-element.960), channel_id=1, source_target_pairs={{0,8},{2,0},{4,24},{6,16},{8,10},{10,2},{12,26},{14,18},{16,12},{1... | collective-permute-start | bytes 393224 | tf_op jit(solution)/shard_map/ppermute | solution.py:76
  19.6 17.4 %collective-permute-start.2 = (bf16[4,128,128]{2,1,0:T(8,128)(2,1)}, bf16[4,128,128]{2,1,0:T(8,128)(2,1)S(1)}, u32[]{:S(2)}, u32[]{:S(2)}) collective-permute-start(bf16[4,128,128]{2,1,0:T(8,128)(2,1)} %get-tuple-element.959), channel_id=1, source_target_pairs={{0,16},{2,24},{4,0},{6,8},{8,18},{10,26},{12,2},{14,10},{16,20},{1... | collective-permute-start | bytes 393224 | tf_op jit(solution)/shard_map/ppermute | solution.py:76
  19.7 20.1 %collective-permute-start.3 = (bf16[4,128,128]{2,1,0:T(8,128)(2,1)}, bf16[4,128,128]{2,1,0:T(8,128)(2,1)S(1)}, u32[]{:S(2)}, u32[]{:S(2)}) collective-permute-start(bf16[4,128,128]{2,1,0:T(8,128)(2,1)} %get-tuple-element.958), channel_id=1, source_target_pairs={{0,24},{2,16},{4,8},{6,0},{8,26},{10,18},{12,10},{14,2},{16,28},{1... | collective-permute-start | bytes 393224 | tf_op jit(solution)/shard_map/ppermute | solution.py:76
  32.4 128.3 %all-gather.11.cloned.1.call-start = ((), (), s32[]{:S(2)}) async-start(), calls=%async_computation.41 | async-start | bytes 2621440 | tf_op jit(solution)/shard_map/all_gather | solution.py:116
  42.2 12.3 %collective-permute-start.7 = (bf16[4,128,128]{2,1,0:T(8,128)(2,1)}, bf16[4,128,128]{2,1,0:T(8,128)(2,1)}, u32[]{:S(2)}, u32[]{:S(2)}) collective-permute-start(bf16[4,128,128]{2,1,0:T(8,128)(2,1)} %get-tuple-element.962), channel_id=1, source_target_pairs={{0,2},{2,0},{4,6},{6,4},{1,3},{3,1},{5,7},{7,5},{8,10},{10,8},{12,... | collective-permute-start | bytes 393224 | tf_op jit(solution)/shard_map/ppermute | solution.py:121
  42.2 15.9 %collective-permute-start.8 = (bf16[4,128,128]{2,1,0:T(8,128)(2,1)}, bf16[4,128,128]{2,1,0:T(8,128)(2,1)}, u32[]{:S(2)}, u32[]{:S(2)}) collective-permute-start(bf16[4,128,128]{2,1,0:T(8,128)(2,1)} %get-tuple-element.962), channel_id=1, source_target_pairs={{0,4},{2,6},{4,0},{6,2},{1,5},{3,7},{5,1},{7,3},{8,12},{10,14},{12... | collective-permute-start | bytes 393224 | tf_op jit(solution)/shard_map/ppermute | solution.py:121
  45.3 25.1 %collective-permute-start.9 = (bf16[4,128,128]{2,1,0:T(8,128)(2,1)}, bf16[4,128,128]{2,1,0:T(8,128)(2,1)}, u32[]{:S(2)}, u32[]{:S(2)}) collective-permute-start(bf16[4,128,128]{2,1,0:T(8,128)(2,1)} %get-tuple-element.962), channel_id=1, source_target_pairs={{0,6},{2,4},{4,2},{6,0},{1,7},{3,5},{5,3},{7,1},{8,14},{10,12},{12... | collective-permute-start | bytes 393224 | tf_op jit(solution)/shard_map/ppermute | solution.py:121
  45.6 26.0 %collective-permute-start.10 = (bf16[4,128,128]{2,1,0:T(8,128)(2,1)S(1)}, bf16[4,128,128]{2,1,0:T(8,128)(2,1)}, u32[]{:S(2)}, u32[]{:S(2)}) collective-permute-start(bf16[4,128,128]{2,1,0:T(8,128)(2,1)S(1)} %get-tuple-element.963), channel_id=1, source_target_pairs={{0,2},{2,0},{4,6},{6,4},{1,3},{3,1},{5,7},{7,5},{8,10},{10,8},{12,... | collective-permute-start | bytes 393224 | tf_op jit(solution)/shard_map/ppermute | solution.py:121
  46.8 30.8 %collective-permute-start.11 = (bf16[4,128,128]{2,1,0:T(8,128)(2,1)S(1)}, bf16[4,128,128]{2,1,0:T(8,128)(2,1)}, u32[]{:S(2)}, u32[]{:S(2)}) collective-permute-start(bf16[4,128,128]{2,1,0:T(8,128)(2,1)S(1)} %get-tuple-element.963), channel_id=1, source_target_pairs={{0,4},{2,6},{4,0},{6,2},{1,5},{3,7},{5,1},{7,3},{8,12},{10,14},{12... | collective-permute-start | bytes 393224 | tf_op jit(solution)/shard_map/ppermute | solution.py:121
  51.4 197.4 %all-gather.15.cloned.1.call-start = ((), (), s32[]{:S(2)}) async-start(), calls=%async_computation.43 | async-start | bytes 2621440 | tf_op jit(solution)/shard_map/all_gather | solution.py:116
  54.5 26.0 %collective-permute-start.12 = (bf16[4,128,128]{2,1,0:T(8,128)(2,1)S(1)}, bf16[4,128,128]{2,1,0:T(8,128)(2,1)S(1)}, u32[]{:S(2)}, u32[]{:S(2)}) collective-permute-start(bf16[4,128,128]{2,1,0:T(8,128)(2,1)S(1)} %get-tuple-element.963), channel_id=1, source_target_pairs={{0,6},{2,4},{4,2},{6,0},{1,7},{3,5},{5,3},{7,1},{8,14},{10,12},{12... | collective-permute-start | bytes 393224 | tf_op jit(solution)/shard_map/ppermute | solution.py:121
  98.8 12.1 %all-to-all-start.1 = ((bf16[8,16,16,128]{3,1,2,0:T(8,128)(2,1)}), bf16[8,16,16,128]{3,1,2,0:T(8,128)(2,1)S(1)}, u32[]{:S(2)}, u32[]{:S(2)}) async-start(bf16[8,16,16,128]{3,1,2,0:T(8,128)(2,1)} %copy.471), calls=%async_computation.1 | async-start | bytes 1048576 | tf_op jit(solution)/shard_map/while/body/all_to_all | solution.py:27
  114.9 12.9 %collective-permute-start.15 = (bf16[2,4,128,128]{2,3,1,0:T(8,128)(2,1)S(1)}, bf16[2,4,128,128]{2,3,1,0:T(8,128)(2,1)S(1)}, u32[]{:S(2)}, u32[]{:S(2)}) collective-permute-start(bf16[2,4,128,128]{2,3,1,0:T(8,128)(2,1)S(1)} %pad_maximum_fusion.34), channel_id=1, source_target_pairs={{0,24},{8,16},{16,8},{24,0},{1,25},{9,17},{17,9},{25,1},{2,26},{10... | collective-permute-start | bytes 786440 | tf_op jit(solution)/shard_map/ppermute | solution.py:108
  129.7 124.9 %all-gather.13.cloned.1.call-start = ((), (), s32[]{:S(2)}) async-start(), calls=%async_computation.42 | async-start | bytes 2621440 | tf_op jit(solution)/shard_map/all_gather | solution.py:116
  131.6 381.7 %reduce-scatter.5.cloned.1.call-start = ((), (), s32[]{:S(2)}) async-start(), calls=%async_computation.36 | async-start | bytes 2621440 | tf_op jit(solution)/shard_map/reduce_scatter | solution.py:132
  206.7 12.1 %all-to-all-start.7 = ((bf16[8,16,16,128]{3,1,2,0:T(8,128)(2,1)}), bf16[8,16,16,128]{3,1,2,0:T(8,128)(2,1)S(1)}, u32[]{:S(2)}, u32[]{:S(2)}) async-start(bf16[8,16,16,128]{3,1,2,0:T(8,128)(2,1)} %copy.483), calls=%async_computation.7 | async-start | bytes 1048576 | tf_op jit(solution)/shard_map/while/body/all_to_all | solution.py:27
  220.9 19.8 %collective-permute-start.20 = (bf16[4,128,128]{1,2,0:T(8,128)(2,1)S(1)}, bf16[4,128,128]{1,2,0:T(8,128)(2,1)S(1)}, u32[]{:S(2)}, u32[]{:S(2)}) collective-permute-start(bf16[4,128,128]{1,2,0:T(8,128)(2,1)S(1)} %bitcast.1470), channel_id=1, source_target_pairs={{0,0},{2,8},{4,16},{6,24},{8,2},{10,10},{12,18},{14,26},{16,4},{18... | collective-permute-start | bytes 393224 | tf_op jit(solution)/shard_map/ppermute | solution.py:76
  224.8 17.5 %collective-permute-start.21 = (bf16[4,128,128]{1,2,0:T(8,128)(2,1)S(1)}, bf16[4,128,128]{1,2,0:T(8,128)(2,1)S(1)}, u32[]{:S(2)}, u32[]{:S(2)}) collective-permute-start(bf16[4,128,128]{1,2,0:T(8,128)(2,1)S(1)} %bitcast.1471), channel_id=1, source_target_pairs={{0,8},{2,0},{4,24},{6,16},{8,10},{10,2},{12,26},{14,18},{16,12},{1... | collective-permute-start | bytes 393224 | tf_op jit(solution)/shard_map/ppermute | solution.py:76
  225.1 20.1 %collective-permute-start.22 = (bf16[4,128,128]{1,2,0:T(8,128)(2,1)S(1)}, bf16[4,128,128]{1,2,0:T(8,128)(2,1)}, u32[]{:S(2)}, u32[]{:S(2)}) collective-permute-start(bf16[4,128,128]{1,2,0:T(8,128)(2,1)S(1)} %bitcast.1472), channel_id=1, source_target_pairs={{0,16},{2,24},{4,0},{6,8},{8,18},{10,26},{12,2},{14,10},{16,20},{1... | collective-permute-start | bytes 393224 | tf_op jit(solution)/shard_map/ppermute | solution.py:76
  225.3 21.7 %collective-permute-start.23 = (bf16[4,128,128]{1,2,0:T(8,128)(2,1)S(1)}, bf16[4,128,128]{1,2,0:T(8,128)(2,1)S(1)}, u32[]{:S(2)}, u32[]{:S(2)}) collective-permute-start(bf16[4,128,128]{1,2,0:T(8,128)(2,1)S(1)} %bitcast.1473), channel_id=1, source_target_pairs={{0,24},{2,16},{4,8},{6,0},{8,26},{10,18},{12,10},{14,2},{16,28},{1... | collective-permute-start | bytes 393224 | tf_op jit(solution)/shard_map/ppermute | solution.py:76
  304.0 12.2 %all-to-all-start.11 = ((bf16[8,16,16,128]{3,1,2,0:T(8,128)(2,1)}), bf16[8,16,16,128]{3,1,2,0:T(8,128)(2,1)S(1)}, u32[]{:S(2)}, u32[]{:S(2)}) async-start(bf16[8,16,16,128]{3,1,2,0:T(8,128)(2,1)} %copy.491), calls=%async_computation.11 | async-start | bytes 1048576 | tf_op jit(solution)/shard_map/while/body/all_to_all | solution.py:27
  359.9 12.2 %all-to-all-start.15 = ((bf16[8,16,16,128]{3,1,2,0:T(8,128)(2,1)}), bf16[8,16,16,128]{3,1,2,0:T(8,128)(2,1)S(1)}, u32[]{:S(2)}, u32[]{:S(2)}) async-start(bf16[8,16,16,128]{3,1,2,0:T(8,128)(2,1)} %copy.499), calls=%async_computation.15 | async-start | bytes 1048576 | tf_op jit(solution)/shard_map/while/body/all_to_all | solution.py:27
  382.2 12.7 %all-to-all-start.16 = ((bf16[8,16,16,128]{3,2,1,0:T(8,128)(2,1)}), bf16[8,16,16,128]{3,2,1,0:T(8,128)(2,1)S(1)}, u32[]{:S(2)}, u32[]{:S(2)}) async-start(bf16[8,16,16,128]{3,2,1,0:T(8,128)(2,1)} %bitcast.1140), calls=%async_computation.16 | async-start | bytes 1048576 | tf_op jit(solution)/shard_map/while/body/all_to_all | solution.py:27
  410.4 12.2 %all-to-all-start.18 = ((bf16[8,16,16,128]{3,1,2,0:T(8,128)(2,1)}), bf16[8,16,16,128]{3,1,2,0:T(8,128)(2,1)S(1)}, u32[]{:S(2)}, u32[]{:S(2)}) async-start(bf16[8,16,16,128]{3,1,2,0:T(8,128)(2,1)} %copy.504), calls=%async_computation.18 | async-start | bytes 1048576 | tf_op jit(solution)/shard_map/while/body/all_to_all | solution.py:27
  425.8 12.7 %all-to-all-start.19 = ((bf16[8,16,16,128]{3,2,1,0:T(8,128)(2,1)}), bf16[8,16,16,128]{3,2,1,0:T(8,128)(2,1)S(1)}, u32[]{:S(2)}, u32[]{:S(2)}) async-start(bf16[8,16,16,128]{3,2,1,0:T(8,128)(2,1)} %copy.506), calls=%async_computation.19 | async-start | bytes 1048576 | tf_op jit(solution)/shard_map/while/body/all_to_all | solution.py:27
  446.1 133.1 %reduce-scatter.7.cloned.1.call-start = ((), (), s32[]{:S(2)}) async-start(), calls=%async_computation.37 | async-start | bytes 2621440 | tf_op jit(solution)/shard_map/reduce_scatter | solution.py:132
  449.3 12.8 %all-to-all-start.20 = ((bf16[8,16,16,128]{3,2,1,0:T(8,128)(2,1)}), bf16[8,16,16,128]{3,2,1,0:T(8,128)(2,1)S(1)}, u32[]{:S(2)}, u32[]{:S(2)}) async-start(bf16[8,16,16,128]{3,2,1,0:T(8,128)(2,1)} %bitcast.1180), calls=%async_computation.20 | async-start | bytes 1048576 | tf_op jit(solution)/shard_map/while/body/all_to_all | solution.py:27
  477.5 12.2 %all-to-all-start.22 = ((bf16[8,16,16,128]{3,1,2,0:T(8,128)(2,1)}), bf16[8,16,16,128]{3,1,2,0:T(8,128)(2,1)S(1)}, u32[]{:S(2)}, u32[]{:S(2)}) async-start(bf16[8,16,16,128]{3,1,2,0:T(8,128)(2,1)} %copy.514), calls=%async_computation.22 | async-start | bytes 1048576 | tf_op jit(solution)/shard_map/while/body/all_to_all | solution.py:27
  492.9 12.7 %all-to-all-start.23 = ((bf16[8,16,16,128]{3,2,1,0:T(8,128)(2,1)}), bf16[8,16,16,128]{3,2,1,0:T(8,128)(2,1)S(1)}, u32[]{:S(2)}, u32[]{:S(2)}) async-start(bf16[8,16,16,128]{3,2,1,0:T(8,128)(2,1)} %copy.516), calls=%async_computation.23 | async-start | bytes 1048576 | tf_op jit(solution)/shard_map/while/body/all_to_all | solution.py:27
  513.2 192.9 %reduce-scatter.9.cloned.1.call-start = ((), (), s32[]{:S(2)}) async-start(), calls=%async_computation.38 | async-start | bytes 2621440 | tf_op jit(solution)/shard_map/reduce_scatter | solution.py:132
  519.4 12.8 %all-to-all-start.24 = ((bf16[8,16,16,128]{3,2,1,0:T(8,128)(2,1)}), bf16[8,16,16,128]{3,2,1,0:T(8,128)(2,1)S(1)}, u32[]{:S(2)}, u32[]{:S(2)}) async-start(bf16[8,16,16,128]{3,2,1,0:T(8,128)(2,1)} %bitcast.1220), calls=%async_computation.24 | async-start | bytes 1048576 | tf_op jit(solution)/shard_map/while/body/all_to_all | solution.py:27
  547.6 12.2 %all-to-all-start.26 = ((bf16[8,16,16,128]{3,1,2,0:T(8,128)(2,1)}), bf16[8,16,16,128]{3,1,2,0:T(8,128)(2,1)S(1)}, u32[]{:S(2)}, u32[]{:S(2)}) async-start(bf16[8,16,16,128]{3,1,2,0:T(8,128)(2,1)} %copy.524), calls=%async_computation.26 | async-start | bytes 1048576 | tf_op jit(solution)/shard_map/while/body/all_to_all | solution.py:27
  563.0 12.7 %all-to-all-start.27 = ((bf16[8,16,16,128]{3,2,1,0:T(8,128)(2,1)}), bf16[8,16,16,128]{3,2,1,0:T(8,128)(2,1)S(1)}, u32[]{:S(2)}, u32[]{:S(2)}) async-start(bf16[8,16,16,128]{3,2,1,0:T(8,128)(2,1)} %copy.526), calls=%async_computation.27 | async-start | bytes 1048576 | tf_op jit(solution)/shard_map/while/body/all_to_all | solution.py:27
  585.8 122.1 %reduce-scatter.11.cloned.1.call-start = ((), (), s32[]{:S(2)}) async-start(), calls=%async_computation.39 | async-start | bytes 2621440 | tf_op jit(solution)/shard_map/reduce_scatter | solution.py:132
  589.1 12.8 %all-to-all-start.28 = ((bf16[8,16,16,128]{3,2,1,0:T(8,128)(2,1)}), bf16[8,16,16,128]{3,2,1,0:T(8,128)(2,1)S(1)}, u32[]{:S(2)}, u32[]{:S(2)}) async-start(bf16[8,16,16,128]{3,2,1,0:T(8,128)(2,1)} %bitcast.1260), calls=%async_computation.28 | async-start | bytes 1048576 | tf_op jit(solution)/shard_map/while/body/all_to_all | solution.py:27
  617.3 12.2 %all-to-all-start.30 = ((bf16[8,16,16,128]{3,1,2,0:T(8,128)(2,1)}), bf16[8,16,16,128]{3,1,2,0:T(8,128)(2,1)S(1)}, u32[]{:S(2)}, u32[]{:S(2)}) async-start(bf16[8,16,16,128]{3,1,2,0:T(8,128)(2,1)} %copy.534), calls=%async_computation.30 | async-start | bytes 1048576 | tf_op jit(solution)/shard_map/while/body/all_to_all | solution.py:27
  632.6 12.7 %all-to-all-start.31 = ((bf16[8,16,16,128]{3,2,1,0:T(8,128)(2,1)}), bf16[8,16,16,128]{3,2,1,0:T(8,128)(2,1)S(1)}, u32[]{:S(2)}, u32[]{:S(2)}) async-start(bf16[8,16,16,128]{3,2,1,0:T(8,128)(2,1)} %copy.536), calls=%async_computation.31 | async-start | bytes 1048576 | tf_op jit(solution)/shard_map/while/body/all_to_all | solution.py:27
  654.6 21.0 %collective-permute-start.16 = (bf16[4,128,128]{2,1,0:T(8,128)(2,1)S(1)}, bf16[4,128,128]{2,1,0:T(8,128)(2,1)S(1)}, u32[]{:S(2)}, u32[]{:S(2)}) collective-permute-start(bf16[4,128,128]{2,1,0:T(8,128)(2,1)S(1)} %bitcast.1474), channel_id=1, source_target_pairs={{0,0},{2,8},{4,16},{6,24},{8,2},{10,10},{12,18},{14,26},{16,4},{18... | collective-permute-start | bytes 393224 | tf_op jit(solution)/shard_map/ppermute | solution.py:76
  657.9 25.0 %collective-permute-start.17 = (bf16[4,128,128]{2,1,0:T(8,128)(2,1)S(1)}, bf16[4,128,128]{2,1,0:T(8,128)(2,1)S(1)}, u32[]{:S(2)}, u32[]{:S(2)}) collective-permute-start(bf16[4,128,128]{2,1,0:T(8,128)(2,1)S(1)} %bitcast.1475), channel_id=1, source_target_pairs={{0,2},{2,10},{4,18},{6,26},{8,0},{10,8},{12,16},{14,24},{16,6},{18... | collective-permute-start | bytes 393224 | tf_op jit(solution)/shard_map/ppermute | solution.py:76
  661.2 21.7 %collective-permute-start.18 = (bf16[4,128,128]{2,1,0:T(8,128)(2,1)S(1)}, bf16[4,128,128]{2,1,0:T(8,128)(2,1)S(1)}, u32[]{:S(2)}, u32[]{:S(2)}) collective-permute-start(bf16[4,128,128]{2,1,0:T(8,128)(2,1)S(1)} %bitcast.1476), channel_id=1, source_target_pairs={{0,4},{2,12},{4,20},{6,28},{8,6},{10,14},{12,22},{14,30},{16,0},{1... | collective-permute-start | bytes 393224 | tf_op jit(solution)/shard_map/ppermute | solution.py:76
  661.4 29.6 %collective-permute-start.19 = (bf16[4,128,128]{2,1,0:T(8,128)(2,1)S(1)}, bf16[4,128,128]{2,1,0:T(8,128)(2,1)S(1)}, u32[]{:S(2)}, u32[]{:S(2)}) collective-permute-start(bf16[4,128,128]{2,1,0:T(8,128)(2,1)S(1)} %bitcast.1477), channel_id=1, source_target_pairs={{0,6},{2,14},{4,22},{6,30},{8,4},{10,12},{12,20},{14,28},{16,2},{1... | collective-permute-start | bytes 393224 | tf_op jit(solution)/shard_map/ppermute | solution.py:76
  692.1 13.6 %collective-permute-start.36 = (bf16[2,4,128,128]{3,2,1,0:T(8,128)(2,1)S(1)}, bf16[2,4,128,128]{3,2,1,0:T(8,128)(2,1)S(1)}, u32[]{:S(2)}, u32[]{:S(2)}) collective-permute-start(bf16[2,4,128,128]{3,2,1,0:T(8,128)(2,1)S(1)} %pad_maximum_fusion.37), channel_id=1, source_target_pairs={{0,24},{8,16},{16,8},{24,0},{1,25},{9,17},{17,9},{25,1},{2,26},{10... | collective-permute-start | bytes 786440 | tf_op jit(solution)/shard_map/ppermute | solution.py:108
  714.1 12.7 %collective-permute-start.33 = (bf16[1,4,128,128]{3,2,1,0:T(8,128)(2,1)S(1)}, bf16[1,4,128,128]{3,2,1,0:T(8,128)(2,1)S(1)}, u32[]{:S(2)}, u32[]{:S(2)}) collective-permute-start(bf16[1,4,128,128]{3,2,1,0:T(8,128)(2,1)S(1)} %get-tuple-element.886), channel_id=1, source_target_pairs={{0,24},{8,16},{16,8},{24,0},{1,25},{9,17},{17,9},{25,1},{2,26},{10... | collective-permute-start | bytes 393224 | tf_op jit(solution)/shard_map/ppermute | solution.py:108
  716.2 14.9 %collective-permute-start.24 = (bf16[4,128,128]{2,1,0:T(8,128)(2,1)S(1)}, bf16[4,128,128]{2,1,0:T(8,128)(2,1)S(1)}, u32[]{:S(2)}, u32[]{:S(2)}) collective-permute-start(bf16[4,128,128]{2,1,0:T(8,128)(2,1)S(1)} %bitcast.1469), channel_id=1, source_target_pairs={{0,0},{2,8},{4,16},{6,24},{8,2},{10,10},{12,18},{14,26},{16,4},{18... | collective-permute-start | bytes 393224 | tf_op jit(solution)/shard_map/ppermute | solution.py:76
  724.3 13.5 %collective-permute-start.27 = (bf16[4,128,128]{2,1,0:T(8,128)(2,1)S(1)}, bf16[4,128,128]{2,1,0:T(8,128)(2,1)S(1)}, u32[]{:S(2)}, u32[]{:S(2)}) collective-permute-start(bf16[4,128,128]{2,1,0:T(8,128)(2,1)S(1)} %bitcast.1466), channel_id=1, source_target_pairs={{0,6},{2,14},{4,22},{6,30},{8,4},{10,12},{12,20},{14,28},{16,2},{1... | collective-permute-start | bytes 393224 | tf_op jit(solution)/shard_map/ppermute | solution.py:76
  (80 other events, 747.3 us)
Sparse Core Ops, SparseCore 0:
  32.5 40.8 all-gather.8
  74.9 48.1 all-gather.10
  129.8 42.9 all-gather.14
  174.2 44.6 all-gather.12
  446.2 42.0 reduce-scatter.4
  513.3 42.0 reduce-scatter.6
  585.9 42.0 reduce-scatter.8
  653.1 51.9 reduce-scatter.10

commit v13 on v12

--- a/solution.py
+++ b/solution.py
@@ -143,6 +143,7 @@
     once = 1 + s_index // sections
     first = jnp.stack([gathered_directly(parts[0][f]) for f in range(2)], axis=1)[:, None]
     starts = [0, 1] + list(range(PAIRED, layers, PAIRED)) + [layers]
+    first, parts[1] = lax.optimization_barrier((first, parts[1]))
     ahead = gathered(jnp.stack(parts[1:2]))
     weights = {}
     stored = {}
@@ -168,16 +169,15 @@
         full = ahead if begin else first
         if begin:
             coming = range(end, min(end + PAIRED, layers))
-            if begin == 1:
-                current, rights, lefts = lax.optimization_barrier((current, rights[1:], lefts[1:]))
+            if begin == PAIRED:
+                later = (current, rights[1:], lefts[1:], cotangent)
+                current, rights, lefts, cotangent = lax.optimization_barrier(later)
                 for loop in range(loops - 1):
                     parts.extend(ordered(part) for part in scattered(rights[loop], lefts[loop]))
+                grad = settled(arriving(cotangent))
             if coming:
                 ahead = gathered(jnp.stack([parts[layer] for layer in coming]))
         weights.update((layer, (full, layer - begin)) for layer in stretch)
-        if end + PAIRED == layers:
-            current, cotangent = lax.optimization_barrier((current, cotangent))
-            grad = settled(arriving(cotangent))
         blanks = [jnp.zeros(current.shape, BF16) for _ in range(2 * len(stretch) - 1)]
         entered = current
         current, *saved = lax.fori_loop(0, once, forward_stretch(stretch), (current, *blanks))
@@ -187,31 +187,30 @@
 
     sums = [None] * layers
 
-    def backward_pair(top):
+    def backward_stretch(stretch):
         def run(_, carry):
             grad, _ = carry
             terms = []
-            for layer in range(top, top - PAIRED, -1):
+            for layer in stretch:
                 grad, *pair = backward_layer(grad, *factors_of(layer), stored[layer])
                 terms += pair
             return grad, laid_out(*terms)
 
         return run
 
-    totals = {}
-    for top in range(layers - 1, 0, -PAIRED):
-        blank = jnp.zeros((groups, 2 * PAIRED, sub, size, size), BF16)
-        grad, terms = lax.fori_loop(0, once, backward_pair(top), (grad, blank))
-        if top + 2 * PAIRED in totals:
-            asked = totals[top + 2 * PAIRED]
-            grad, terms, totals[top + 2 * PAIRED] = lax.optimization_barrier((grad, terms, asked))
-        totals[top] = summed(terms)
+    backward = [range(end - 1, begin - 1, -1) for begin, end in zip(starts, starts[1:])][::-1]
+    totals = []
+    for place, stretch in enumerate(backward):
+        blank = jnp.zeros((groups, 2 * len(stretch), sub, size, size), BF16)
+        grad, terms = lax.fori_loop(0, once, backward_stretch(stretch), (grad, blank))
+        if place >= 2 and len(stretch) == PAIRED:
+            grad, terms, totals[place - 2] = lax.optimization_barrier((grad, terms, totals[place - 2]))
+        totals.append(summed(terms))
     grad = lax.fori_loop(0, once, lambda _, acts: unsettled(acts), grad)
-    if 2 * PAIRED <= layers:
-        grad, totals[2 * PAIRED - 1] = lax.optimization_barrier((grad, totals[2 * PAIRED - 1]))
-    for top, total in totals.items():
-        for step in range(PAIRED):
-            sums[top - step] = [total[2 * step], total[2 * step + 1]]
+    grad, totals[1:-1] = lax.optimization_barrier((grad, totals[1:-1]))
+    for stretch, total in zip(backward, totals):
+        for step, layer in enumerate(stretch):
+            sums[layer] = [total[2 * step], total[2 * step + 1]]
     input_grad = leave(grad)
 
     def of_loop(loop, factor):
@@ -219,10 +218,7 @@
 
     halves = []
     for loop in range(loops):
-        if loop:
-            moved = jnp.stack(scattered(of_loop(loop, 0), of_loop(loop, 1)), axis=1)
-        else:
-            moved = jnp.stack([jnp.stack(scattered(of_loop(loop, factor)))[:, 0] for factor in range(2)])
+        moved = jnp.stack(scattered(of_loop(loop, 0), of_loop(loop, 1)), axis=1)
         halves.append(moved.reshape(2, 1, held, size, size))
     grads = jnp.stack(halves).astype(F32)
     return (outputs, input_grad, grads[:, 0], grads[:, 1])

time: 758 us -> 854 us (1.13)
  the two profiles are of different devices: /device:TPU:17 before, /device:TPU:0 now
where the time goes in v13:
time: 854 us; the launch traced here: 841 us
  waiting for transfers between devices  302 us (35%)
  blocking collectives  172 us (20%)
  starting transfers between devices  134 us (16%)
  local copies, waits for them, and re-layouts  132 us (15%)
  matrix products  58.2 us (7%)
  other arithmetic  25.7 us (3%)
  between operations  15.5 us (2%)
    all_to_all x14, blocking collectives, exchange(): lax.all_to_all(pieces, WIDE, split_axis=0, concat_axis=0, tiled=True)  172 us
    all_to_all x18, waiting for transfers between devices, exchange(): lax.all_to_all(pieces, WIDE, split_axis=0, concat_axis=0, tiled=True)  130 us
    reduce_scatter x5, waiting for transfers between devices, summed(): lax.psum_scatter(terms.reshape(-1, size, size), 't', scatter_dimension=0,...  76.6 us
    all_to_all x18, starting transfers between devices, exchange(): lax.all_to_all(pieces, WIDE, split_axis=0, concat_axis=0, tiled=True)  62.9 us
    ppermute x16, waiting for transfers between devices, turned(): moved.append(lax.ppermute(pick(parts, send_by ^ mask), ('s', 't'), pairs))  52.8 us
    while x18, local copies, waits for them, and re-layouts, body(): lax.fori_loop(0, once, backward_stretch(stretch), (grad, blank))  34.9 us
    ppermute x16, starting transfers between devices, turned(): moved.append(lax.ppermute(pick(parts, send_by ^ mask), ('s', 't'), pairs))  30.5 us
    ppermute x12, starting transfers between devices, scattered(): moved.append(lax.ppermute(value, 's', pairs))  30.3 us
  transfers between devices with their start and end apart: 61, of which 36 were waited for; matrix products, arithmetic and copies ran while one was open for 19% of the time, Pallas kernels for 0%

profile of v13, /device:TPU:0, one launch (start us, length us, event | category | flops | bytes accessed | tf_op | source)
XLA Modules:
  0.0 841.2 jit_solution(8388138562480414478)
XLA Ops:
  21.3 13.8 %collective-permute-start.5 = (bf16[2,4,128,128]{2,3,1,0:T(8,128)(2,1)S(1)}, bf16[2,4,128,128]{2,3,1,0:T(8,128)(2,1)S(1)}, u32[]{:S(2)}, u32[]{:S(2)}) collective-permute-start(bf16[2,4,128,128]{2,3,1,0:T(8,128)(2,1)S(1)} %pad_maximum_fusion.29), channel_id=1, source_target_pairs={{0,16},{8,24},{16,0},{24,8},{1,17},{9,25},{17,1},{25,9},{2,18},{10... | collective-permute-start | bytes 786440 | tf_op jit(solution)/shard_map/ppermute | solution.py:108
  60.9 9.8 %collective-permute-done.11 = bf16[4,128,128]{2,1,0:T(8,128)(2,1)S(1)} collective-permute-done((bf16[4,128,128]{2,1,0:T(8,128)(2,1)S(1)}, bf16[4,128,128]{2,1,0:T(8,128)(2,1)S(1)}, u32[]{:S(2)}, u32[]{:S(2)}) %collective-permute-start.11) | collective-permute-done | bytes 131104 | tf_op jit(solution)/shard_map/ppermute | solution.py:121
  77.0 28.1 %while.143 = (s32[]{:T(128)}, bf16[16,128,128]{2,1,0:T(8,128)(2,1)S(1)}, bf16[16,128,128]{2,0,1:T(8,128)(2,1)}, s32[]{:T(128)}, bf16[4,1,2,4,128,128]{4,5,3,0,2,1:T(8,128)(2,1)S(1)}, /*index=5*/s32[]{:T(128)}) while((s32[]{:T(128)}, bf16[16,128,128]{2,1,0:T(8,128)(2,1)S(1)}, bf16[16,128,128]{2,0,1:T(8,128)(2,1)}, s32[]{:T(128)}, ...), condition=%wide.region_1.2_spmd, body=%wide.region_0.1_spmd.sunk | while | flops 137363456 | bytes 16777344 | solution.py:183
  77.5 13.0 %all_to_all.192 = bf16[8,16,16,128]{3,1,2,0:T(8,128)(2,1)S(1)} all-to-all(bf16[8,16,16,128]{3,1,2,0:T(8,128)(2,1)S(1)} %copy.472), channel_id=1, replica_groups=mesh['s'=4,'t'=4,'x'=2] {'s','x'}, dimensions={0} | all-to-all | bytes 1048576 | tf_op jit(solution)/shard_map/while/body/all_to_all | solution.py:27
  95.4 9.2 %all-to-all-done.1 = bf16[8,16,16,128]{3,1,2,0:T(8,128)(2,1)S(1)} async-done(((bf16[8,16,16,128]{3,1,2,0:T(8,128)(2,1)}), bf16[8,16,16,128]{3,1,2,0:T(8,128)(2,1)S(1)}, u32[]{:S(2)}, u32[]{:S(2)}) %all-to-all-start.1) | async-done | bytes 524320 | tf_op jit(solution)/shard_map/while/body/all_to_all | solution.py:27
  107.8 26.8 %while.144 = (s32[]{:T(128)}, bf16[16,128,128]{2,1,0:T(8,128)(2,1)S(1)}, bf16[16,128,128]{2,0,1:T(8,128)(2,1)}, s32[]{:T(128)}, bf16[4,1,2,4,128,128]{4,5,3,0,2,1:T(8,128)(2,1)S(1)}, /*index=5*/s32[]{:T(128)}) while((s32[]{:T(128)}, bf16[16,128,128]{2,1,0:T(8,128)(2,1)S(1)}, bf16[16,128,128]{2,0,1:T(8,128)(2,1)}, s32[]{:T(128)}, ...), condition=%wide.region_3.4_spmd, body=%wide.region_2.3_spmd.sunk | while | flops 137363456 | bytes 16777344 | solution.py:183
  108.2 11.7 %all_to_all.193 = bf16[8,16,16,128]{3,1,2,0:T(8,128)(2,1)S(1)} all-to-all(bf16[8,16,16,128]{3,1,2,0:T(8,128)(2,1)S(1)} %copy.476), channel_id=1, replica_groups=mesh['s'=4,'t'=4,'x'=2] {'s','x'}, dimensions={0} | all-to-all | bytes 1048576 | tf_op jit(solution)/shard_map/while/body/all_to_all | solution.py:27
  124.9 9.2 %all-to-all-done.3 = bf16[8,16,16,128]{3,1,2,0:T(8,128)(2,1)S(1)} async-done(((bf16[8,16,16,128]{3,1,2,0:T(8,128)(2,1)}), bf16[8,16,16,128]{3,1,2,0:T(8,128)(2,1)S(1)}, u32[]{:S(2)}, u32[]{:S(2)}) %all-to-all-start.3) | async-done | bytes 524320 | tf_op jit(solution)/shard_map/while/body/all_to_all | solution.py:27
  139.1 6.5 collective-permute-done.14
  167.9 36.2 %collective-permute-done.22 = bf16[4,128,128]{1,2,0:T(8,128)(2,1)S(1)} collective-permute-done((bf16[4,128,128]{1,2,0:T(8,128)(2,1)S(1)}, bf16[4,128,128]{1,2,0:T(8,128)(2,1)S(1)}, u32[]{:S(2)}, u32[]{:S(2)}) %collective-permute-start.22) | collective-permute-done | bytes 131104 | tf_op jit(solution)/shard_map/ppermute | solution.py:76
  217.7 60.0 %while.145 = (s32[]{:T(128)}, bf16[16,128,128]{2,1,0:T(8,128)(2,1)S(1)}, bf16[16,128,128]{2,0,1:T(8,128)(2,1)}, bf16[16,128,128]{2,1,0:T(8,128)(2,1)}, bf16[16,1...) while((s32[]{:T(128)}, bf16[16,128,128]{2,1,0:T(8,128)(2,1)S(1)}, ...), condition=%wide.region_5.6_spmd, body=%wide.region_4.5_spmd.sunk | while | flops 274726912 | bytes 35127496 | solution.py:183
  219.7 18.5 %all_to_all.194 = bf16[8,16,16,128]{3,1,2,0:T(8,128)(2,1)S(1)} all-to-all(bf16[8,16,16,128]{3,1,2,0:T(8,128)(2,1)S(1)} %copy.482), channel_id=1, replica_groups=mesh['s'=4,'t'=4,'x'=2] {'s','x'}, dimensions={0} | all-to-all | bytes 1048576 | tf_op jit(solution)/shard_map/while/body/all_to_all | solution.py:27
  238.8 11.7 %all_to_all.195 = bf16[8,16,16,128]{3,1,2,0:T(8,128)(2,1)S(1)} all-to-all(bf16[8,16,16,128]{3,1,2,0:T(8,128)(2,1)S(1)} %copy.483), channel_id=1, replica_groups=mesh['s'=4,'t'=4,'x'=2] {'s','x'}, dimensions={0} | all-to-all | bytes 1048576 | tf_op jit(solution)/shard_map/while/body/all_to_all | solution.py:27
  251.4 11.7 %all_to_all.196 = bf16[8,16,16,128]{3,1,2,0:T(8,128)(2,1)S(1)} all-to-all(bf16[8,16,16,128]{3,1,2,0:T(8,128)(2,1)S(1)} %copy.484), channel_id=1, replica_groups=mesh['s'=4,'t'=4,'x'=2] {'s','x'}, dimensions={0} | all-to-all | bytes 1048576 | tf_op jit(solution)/shard_map/while/body/all_to_all | solution.py:27
  268.0 9.2 %all-to-all-done.7 = bf16[8,16,16,128]{3,1,2,0:T(8,128)(2,1)S(1)} async-done(((bf16[8,16,16,128]{3,1,2,0:T(8,128)(2,1)}), bf16[8,16,16,128]{3,1,2,0:T(8,128)(2,1)S(1)}, u32[]{:S(2)}, u32[]{:S(2)}) %all-to-all-start.7) | async-done | bytes 524320 | tf_op jit(solution)/shard_map/while/body/all_to_all | solution.py:27
  296.7 53.6 %while.146 = (s32[]{:T(128)}, bf16[16,128,128]{2,1,0:T(8,128)(2,1)S(1)}, bf16[16,128,128]{2,0,1:T(8,128)(2,1)}, bf16[16,128,128]{2,1,0:T(8,128)(2,1)}, bf16[16,1...) while((s32[]{:T(128)}, bf16[16,128,128]{2,1,0:T(8,128)(2,1)S(1)}, ...), condition=%wide.region_7.8_spmd, body=%wide.region_6.7_spmd.sunk | while | flops 274726912 | bytes 35127496 | solution.py:183
  298.7 11.7 %all_to_all.197 = bf16[8,16,16,128]{3,1,2,0:T(8,128)(2,1)S(1)} all-to-all(bf16[8,16,16,128]{3,1,2,0:T(8,128)(2,1)S(1)} %copy.490), channel_id=1, replica_groups=mesh['s'=4,'t'=4,'x'=2] {'s','x'}, dimensions={0} | all-to-all | bytes 1048576 | tf_op jit(solution)/shard_map/while/body/all_to_all | solution.py:27
  311.0 11.7 %all_to_all.198 = bf16[8,16,16,128]{3,1,2,0:T(8,128)(2,1)S(1)} all-to-all(bf16[8,16,16,128]{3,1,2,0:T(8,128)(2,1)S(1)} %copy.491), channel_id=1, replica_groups=mesh['s'=4,'t'=4,'x'=2] {'s','x'}, dimensions={0} | all-to-all | bytes 1048576 | tf_op jit(solution)/shard_map/while/body/all_to_all | solution.py:27
  323.6 11.7 %all_to_all.199 = bf16[8,16,16,128]{3,1,2,0:T(8,128)(2,1)S(1)} all-to-all(bf16[8,16,16,128]{3,1,2,0:T(8,128)(2,1)S(1)} %copy.492), channel_id=1, replica_groups=mesh['s'=4,'t'=4,'x'=2] {'s','x'}, dimensions={0} | all-to-all | bytes 1048576 | tf_op jit(solution)/shard_map/while/body/all_to_all | solution.py:27
  340.2 9.2 %all-to-all-done.11 = bf16[8,16,16,128]{3,1,2,0:T(8,128)(2,1)S(1)} async-done(((bf16[8,16,16,128]{3,1,2,0:T(8,128)(2,1)}), bf16[8,16,16,128]{3,1,2,0:T(8,128)(2,1)S(1)}, u32[]{:S(2)}, u32[]{:S(2)}) %all-to-all-start.11) | async-done | bytes 524320 | tf_op jit(solution)/shard_map/while/body/all_to_all | solution.py:27
  352.9 53.2 %while.147 = (s32[]{:T(128)}, bf16[16,128,128]{2,1,0:T(8,128)(2,1)S(1)}, bf16[16,128,128]{2,0,1:T(8,128)(2,1)}, bf16[16,128,128]{2,1,0:T(8,128)(2,1)}, bf16[16,1...) while((s32[]{:T(128)}, ...), condition=%wide.region_9.10_spmd, body=%wide.region_8.9_spmd.sunk | while | flops 274726912 | bytes 35127496 | solution.py:183
  355.0 11.7 %all_to_all.200 = bf16[8,16,16,128]{3,1,2,0:T(8,128)(2,1)S(1)} all-to-all(bf16[8,16,16,128]{3,1,2,0:T(8,128)(2,1)S(1)} %copy.498), channel_id=1, replica_groups=mesh['s'=4,'t'=4,'x'=2] {'s','x'}, dimensions={0} | all-to-all | bytes 1048576 | tf_op jit(solution)/shard_map/while/body/all_to_all | solution.py:27
  367.3 11.7 %all_to_all.201 = bf16[8,16,16,128]{3,1,2,0:T(8,128)(2,1)S(1)} all-to-all(bf16[8,16,16,128]{3,1,2,0:T(8,128)(2,1)S(1)} %copy.499), channel_id=1, replica_groups=mesh['s'=4,'t'=4,'x'=2] {'s','x'}, dimensions={0} | all-to-all | bytes 1048576 | tf_op jit(solution)/shard_map/while/body/all_to_all | solution.py:27
  379.8 11.7 %all_to_all.202 = bf16[8,16,16,128]{3,1,2,0:T(8,128)(2,1)S(1)} all-to-all(bf16[8,16,16,128]{3,1,2,0:T(8,128)(2,1)S(1)} %copy.500), channel_id=1, replica_groups=mesh['s'=4,'t'=4,'x'=2] {'s','x'}, dimensions={0} | all-to-all | bytes 1048576 | tf_op jit(solution)/shard_map/while/body/all_to_all | solution.py:27
  396.5 9.2 %all-to-all-done.15 = bf16[8,16,16,128]{3,1,2,0:T(8,128)(2,1)S(1)} async-done(((bf16[8,16,16,128]{3,1,2,0:T(8,128)(2,1)}), bf16[8,16,16,128]{3,1,2,0:T(8,128)(2,1)S(1)}, u32[]{:S(2)}, u32[]{:S(2)}) %all-to-all-start.15) | async-done | bytes 524320 | tf_op jit(solution)/shard_map/while/body/all_to_all | solution.py:27
  414.2 60.9 %while.148 = (s32[]{:T(128)}, bf16[16,128,128]{2,1,0:T(8,128)(2,1)S(1)}, bf16[4,4,4,128,128]{3,4,2,0,1:T(8,128)(2,1)}, s32[]{:T(128)}, bf16[4,2,2,4,128,128]{5,4...) while((s32[]{:T(128)}, ...), condition=%wide.region_11.12_spmd, body=%wide.region_10.11_spmd.sunk | while | flops 551026688 | bytes 51904876 | solution.py:205
  421.5 6.5 all-to-all-done.16
  430.1 11.7 %all_to_all.203 = bf16[8,16,16,128]{3,1,2,0:T(8,128)(2,1)S(1)} all-to-all(bf16[8,16,16,128]{3,1,2,0:T(8,128)(2,1)S(1)} %copy.504), channel_id=1, replica_groups=mesh['s'=4,'t'=4,'x'=2] {'s','x'}, dimensions={0} | all-to-all | bytes 1048576 | tf_op jit(solution)/shard_map/while/body/all_to_all | solution.py:27
  465.5 6.1 all-to-all-done.19
  481.1 61.1 %while.149 = (s32[]{:T(128)}, bf16[16,128,128]{2,1,0:T(8,128)(2,1)S(1)}, bf16[4,4,4,128,128]{3,4,2,0,1:T(8,128)(2,1)}, s32[]{:T(128)}, bf16[4,2,2,4,128,128]{5,4...) while((s32[]{:T(128)}, ...), condition=%wide.region_13.14_spmd, body=%wide.region_12.13_spmd.sunk | while | flops 551026688 | bytes 51904876 | solution.py:205
  488.7 6.4 all-to-all-done.20
  497.2 11.7 %all_to_all.204 = bf16[8,16,16,128]{3,1,2,0:T(8,128)(2,1)S(1)} all-to-all(bf16[8,16,16,128]{3,1,2,0:T(8,128)(2,1)S(1)} %copy.514), channel_id=1, replica_groups=mesh['s'=4,'t'=4,'x'=2] {'s','x'}, dimensions={0} | all-to-all | bytes 1048576 | tf_op jit(solution)/shard_map/while/body/all_to_all | solution.py:27
  532.6 6.0 all-to-all-done.23
  551.2 61.1 %while.150 = (s32[]{:T(128)}, bf16[16,128,128]{2,1,0:T(8,128)(2,1)S(1)}, bf16[4,4,4,128,128]{3,4,2,0,1:T(8,128)(2,1)}, s32[]{:T(128)}, bf16[4,2,2,4,128,128]{5,4...) while((s32[]{:T(128)}, ...), condition=%wide.region_15.16_spmd, body=%wide.region_14.15_spmd.sunk | while | flops 551026688 | bytes 51904876 | solution.py:205
  558.8 6.5 all-to-all-done.24
  567.4 11.7 %all_to_all.205 = bf16[8,16,16,128]{3,1,2,0:T(8,128)(2,1)S(1)} all-to-all(bf16[8,16,16,128]{3,1,2,0:T(8,128)(2,1)S(1)} %copy.524), channel_id=1, replica_groups=mesh['s'=4,'t'=4,'x'=2] {'s','x'}, dimensions={0} | all-to-all | bytes 1048576 | tf_op jit(solution)/shard_map/while/body/all_to_all | solution.py:27
  602.8 6.1 all-to-all-done.27
  613.9 31.6 %while.151 = (s32[]{:T(128)}, bf16[16,128,128]{1,2,0:T(8,128)(2,1)S(1)}, bf16[4,2,4,128,128]{3,4,2,0,1:T(8,128)(2,1)}, s32[]{:T(128)}, bf16[4,1,2,4,128,128]{5,4...) while((s32[]{:T(128)}, ...), condition=%wide.region_18.19_spmd, body=%wide.region_17.18_spmd.sunk | while | flops 274464768 | bytes 19923092 | solution.py:205
  619.8 7.9 all-to-all-done.28
  635.8 7.4 all-to-all-done.29
  646.7 32.1 %while.152 = (s32[]{:T(128)}, bf16[16,128,128]{1,2,0:T(8,128)(2,1)S(1)}, bf16[4,2,4,128,128]{3,4,2,0,1:T(8,128)(2,1)}, s32[]{:T(128)}, bf16[4,1,2,4,128,128]{5,4...) while((s32[]{:T(128)}, ...), condition=%wide.region_20.21_spmd, body=%wide.region_19.20_spmd.sunk | while | flops 274464768 | bytes 28311784 | solution.py:205
  652.5 8.3 all-to-all-done.30
  668.0 8.5 %all-to-all-done.31 = bf16[8,16,16,128]{3,2,1,0:T(8,128)(2,1)S(1)} async-done(((bf16[8,16,16,128]{3,2,1,0:T(8,128)(2,1)}), bf16[8,16,16,128]{3,2,1,0:T(8,128)(2,1)S(1)}, u32[]{:S(2)}, u32[]{:S(2)}) %all-to-all-start.31) | async-done | bytes 524320 | tf_op jit(solution)/shard_map/while/body/all_to_all | solution.py:27
  697.4 5.6 collective-permute-done.18
  716.2 28.6 %reduce-scatter.12.cloned.1.call-done = bf16[8,128,128]{2,1,0:T(8,128)(2,1)} async-done(((bf16[32,128,128]{2,1,0:T(8,128)(2,1)}), bf16[8,128,128]{2,1,0:T(8,128)(2,1)}) %reduce-scatter.12.cloned.1.call-update) | async-done | bytes 262160 | tf_op jit(solution)/shard_map/reduce_scatter | solution.py:132
  746.3 44.0 %reduce-scatter.10.cloned.1.call-done = bf16[16,128,128]{2,1,0:T(8,128)(2,1)} async-done(((bf16[64,128,128]{2,1,0:T(8,128)(2,1)}), bf16[16,128,128]{2,1,0:T(8,128)(2,1)}) %reduce-scatter.10.cloned.1.call-update) | async-done | bytes 524304 | tf_op jit(solution)/shard_map/reduce_scatter | solution.py:132
  803.2 7.1 collective-permute-start.29
  823.2 5.5 collective-permute-done.32
  (541 shorter events, 379.5 us)
Async XLA Ops:
  7.2 98.0 %all-gather.9.cloned.1.call-start = ((), (), s32[]{:S(2)}) async-start(), calls=%async_computation.42 | async-start | bytes 1310720 | tf_op jit(solution)/shard_map/all_gather | solution.py:116
  10.7 28.7 %collective-permute-start.4 = (bf16[2,4,128,128]{2,3,1,0:T(8,128)(2,1)S(1)}, bf16[2,4,128,128]{2,3,1,0:T(8,128)(2,1)S(1)}, u32[]{:S(2)}, u32[]{:S(2)}) collective-permute-start(bf16[2,4,128,128]{2,3,1,0:T(8,128)(2,1)S(1)} %pad_maximum_fusion.28), channel_id=1, source_target_pairs={{0,8},{8,0},{16,24},{24,16},{1,9},{9,1},{17,25},{25,17},{2,10},{10... | collective-permute-start | bytes 786440 | tf_op jit(solution)/shard_map/ppermute | solution.py:108
  12.0 23.1 %collective-permute-start.1 = (bf16[4,128,128]{2,1,0:T(8,128)(2,1)S(1)}, bf16[4,128,128]{2,1,0:T(8,128)(2,1)S(1)}, u32[]{:S(2)}, u32[]{:S(2)}) collective-permute-start(bf16[4,128,128]{2,1,0:T(8,128)(2,1)S(1)} %get-tuple-element.983), channel_id=1, source_target_pairs={{0,8},{2,0},{4,24},{6,16},{8,10},{10,2},{12,26},{14,18},{16,12},{1... | collective-permute-start | bytes 393224 | tf_op jit(solution)/shard_map/ppermute | solution.py:76
  16.0 23.2 %collective-permute-start.2 = (bf16[4,128,128]{2,1,0:T(8,128)(2,1)S(1)}, bf16[4,128,128]{2,1,0:T(8,128)(2,1)S(1)}, u32[]{:S(2)}, u32[]{:S(2)}) collective-permute-start(bf16[4,128,128]{2,1,0:T(8,128)(2,1)S(1)} %get-tuple-element.982), channel_id=1, source_target_pairs={{0,16},{2,24},{4,0},{6,8},{8,18},{10,26},{12,2},{14,10},{16,20},{1... | collective-permute-start | bytes 393224 | tf_op jit(solution)/shard_map/ppermute | solution.py:76
  19.5 19.7 %collective-permute-start.3 = (bf16[4,128,128]{2,1,0:T(8,128)(2,1)S(1)}, bf16[4,128,128]{2,1,0:T(8,128)(2,1)S(1)}, u32[]{:S(2)}, u32[]{:S(2)}) collective-permute-start(bf16[4,128,128]{2,1,0:T(8,128)(2,1)S(1)} %get-tuple-element.981), channel_id=1, source_target_pairs={{0,24},{2,16},{4,8},{6,0},{8,26},{10,18},{12,10},{14,2},{16,28},{1... | collective-permute-start | bytes 393224 | tf_op jit(solution)/shard_map/ppermute | solution.py:76
  21.3 20.0 %collective-permute-start.5 = (bf16[2,4,128,128]{2,3,1,0:T(8,128)(2,1)S(1)}, bf16[2,4,128,128]{2,3,1,0:T(8,128)(2,1)S(1)}, u32[]{:S(2)}, u32[]{:S(2)}) collective-permute-start(bf16[2,4,128,128]{2,3,1,0:T(8,128)(2,1)S(1)} %pad_maximum_fusion.29), channel_id=1, source_target_pairs={{0,16},{8,24},{16,0},{24,8},{1,17},{9,25},{17,1},{25,9},{2,18},{10... | collective-permute-start | bytes 786440 | tf_op jit(solution)/shard_map/ppermute | solution.py:108
  51.3 19.4 %collective-permute-start.11 = (bf16[4,128,128]{2,1,0:T(8,128)(2,1)S(1)}, bf16[4,128,128]{2,1,0:T(8,128)(2,1)S(1)}, u32[]{:S(2)}, u32[]{:S(2)}) collective-permute-start(bf16[4,128,128]{2,1,0:T(8,128)(2,1)S(1)} %get-tuple-element.990), channel_id=1, source_target_pairs={{0,4},{2,6},{4,0},{6,2},{1,5},{3,7},{5,1},{7,3},{8,12},{10,14},{12... | collective-permute-start | bytes 393224 | tf_op jit(solution)/shard_map/ppermute | solution.py:121
  54.9 15.8 %collective-permute-start.12 = (bf16[4,128,128]{2,1,0:T(8,128)(2,1)S(1)}, bf16[4,128,128]{2,1,0:T(8,128)(2,1)S(1)}, u32[]{:S(2)}, u32[]{:S(2)}) collective-permute-start(bf16[4,128,128]{2,1,0:T(8,128)(2,1)S(1)} %get-tuple-element.990), channel_id=1, source_target_pairs={{0,6},{2,4},{4,2},{6,0},{1,7},{3,5},{5,3},{7,1},{8,14},{10,12},{12... | collective-permute-start | bytes 393224 | tf_op jit(solution)/shard_map/ppermute | solution.py:121
  71.2 136.6 %all-gather.11.cloned.1.call-start = ((), (), s32[]{:S(2)}) async-start(), calls=%async_computation.43 | async-start | bytes 2621440 | tf_op jit(solution)/shard_map/all_gather | solution.py:116
  75.4 205.5 %all-gather.15.cloned.1.call-start = ((), (), s32[]{:S(2)}) async-start(), calls=%async_computation.45 | async-start | bytes 2621440 | tf_op jit(solution)/shard_map/all_gather | solution.py:116
  91.9 12.7 %all-to-all-start.1 = ((bf16[8,16,16,128]{3,1,2,0:T(8,128)(2,1)}), bf16[8,16,16,128]{3,1,2,0:T(8,128)(2,1)S(1)}, u32[]{:S(2)}, u32[]{:S(2)}) async-start(bf16[8,16,16,128]{3,1,2,0:T(8,128)(2,1)} %copy.473), calls=%async_computation.1 | async-start | bytes 1048576 | tf_op jit(solution)/shard_map/while/body/all_to_all | solution.py:27
  121.4 12.7 %all-to-all-start.3 = ((bf16[8,16,16,128]{3,1,2,0:T(8,128)(2,1)}), bf16[8,16,16,128]{3,1,2,0:T(8,128)(2,1)S(1)}, u32[]{:S(2)}, u32[]{:S(2)}) async-start(bf16[8,16,16,128]{3,1,2,0:T(8,128)(2,1)} %copy.477), calls=%async_computation.3 | async-start | bytes 1048576 | tf_op jit(solution)/shard_map/while/body/all_to_all | solution.py:27
  138.1 12.4 %collective-permute-start.15 = (bf16[2,4,128,128]{2,3,1,0:T(8,128)(2,1)S(1)}, bf16[2,4,128,128]{2,3,1,0:T(8,128)(2,1)S(1)}, u32[]{:S(2)}, u32[]{:S(2)}) collective-permute-start(bf16[2,4,128,128]{2,3,1,0:T(8,128)(2,1)S(1)} %pad_maximum_fusion.33), channel_id=1, source_target_pairs={{0,24},{8,16},{16,8},{24,0},{1,25},{9,17},{17,9},{25,1},{2,26},{10... | collective-permute-start | bytes 786440 | tf_op jit(solution)/shard_map/ppermute | solution.py:108
  154.3 134.0 %all-gather.13.cloned.1.call-start = ((), (), s32[]{:S(2)}) async-start(), calls=%async_computation.44 | async-start | bytes 2621440 | tf_op jit(solution)/shard_map/all_gather | solution.py:116
  154.5 13.1 %collective-permute-start.20 = (bf16[4,128,128]{1,2,0:T(8,128)(2,1)S(1)}, bf16[4,128,128]{1,2,0:T(8,128)(2,1)S(1)}, u32[]{:S(2)}, u32[]{:S(2)}) collective-permute-start(bf16[4,128,128]{1,2,0:T(8,128)(2,1)S(1)} %bitcast.1468), channel_id=1, source_target_pairs={{0,0},{2,8},{4,16},{6,24},{8,2},{10,10},{12,18},{14,26},{16,4},{18... | collective-permute-start | bytes 393224 | tf_op jit(solution)/shard_map/ppermute | solution.py:76
  155.6 12.3 %collective-permute-start.21 = (bf16[4,128,128]{1,2,0:T(8,128)(2,1)S(1)}, bf16[4,128,128]{1,2,0:T(8,128)(2,1)}, u32[]{:S(2)}, u32[]{:S(2)}) collective-permute-start(bf16[4,128,128]{1,2,0:T(8,128)(2,1)S(1)} %bitcast.1469), channel_id=1, source_target_pairs={{0,8},{2,0},{4,24},{6,16},{8,10},{10,2},{12,26},{14,18},{16,12},{1... | collective-permute-start | bytes 393224 | tf_op jit(solution)/shard_map/ppermute | solution.py:76
  160.2 43.9 %collective-permute-start.22 = (bf16[4,128,128]{1,2,0:T(8,128)(2,1)S(1)}, bf16[4,128,128]{1,2,0:T(8,128)(2,1)S(1)}, u32[]{:S(2)}, u32[]{:S(2)}) collective-permute-start(bf16[4,128,128]{1,2,0:T(8,128)(2,1)S(1)} %bitcast.1470), channel_id=1, source_target_pairs={{0,16},{2,24},{4,0},{6,8},{8,18},{10,26},{12,2},{14,10},{16,20},{1... | collective-permute-start | bytes 393224 | tf_op jit(solution)/shard_map/ppermute | solution.py:76
  162.5 41.6 %collective-permute-start.23 = (bf16[4,128,128]{1,2,0:T(8,128)(2,1)S(1)}, bf16[4,128,128]{1,2,0:T(8,128)(2,1)S(1)}, u32[]{:S(2)}, u32[]{:S(2)}) collective-permute-start(bf16[4,128,128]{1,2,0:T(8,128)(2,1)S(1)} %bitcast.1471), channel_id=1, source_target_pairs={{0,24},{2,16},{4,8},{6,0},{8,26},{10,18},{12,10},{14,2},{16,28},{1... | collective-permute-start | bytes 393224 | tf_op jit(solution)/shard_map/ppermute | solution.py:76
  207.6 338.8 %reduce-scatter.6.cloned.1.call-start = ((), (), s32[]{:S(2)}) async-start(), calls=%async_computation.37 | async-start | bytes 2621440 | tf_op jit(solution)/shard_map/reduce_scatter | solution.py:132
  264.5 12.7 %all-to-all-start.7 = ((bf16[8,16,16,128]{3,1,2,0:T(8,128)(2,1)}), bf16[8,16,16,128]{3,1,2,0:T(8,128)(2,1)S(1)}, u32[]{:S(2)}, u32[]{:S(2)}) async-start(bf16[8,16,16,128]{3,1,2,0:T(8,128)(2,1)} %copy.485), calls=%async_computation.7 | async-start | bytes 1048576 | tf_op jit(solution)/shard_map/while/body/all_to_all | solution.py:27
  336.7 12.7 %all-to-all-start.11 = ((bf16[8,16,16,128]{3,1,2,0:T(8,128)(2,1)}), bf16[8,16,16,128]{3,1,2,0:T(8,128)(2,1)S(1)}, u32[]{:S(2)}, u32[]{:S(2)}) async-start(bf16[8,16,16,128]{3,1,2,0:T(8,128)(2,1)} %copy.493), calls=%async_computation.11 | async-start | bytes 1048576 | tf_op jit(solution)/shard_map/while/body/all_to_all | solution.py:27
  393.0 12.7 %all-to-all-start.15 = ((bf16[8,16,16,128]{3,1,2,0:T(8,128)(2,1)}), bf16[8,16,16,128]{3,1,2,0:T(8,128)(2,1)S(1)}, u32[]{:S(2)}, u32[]{:S(2)}) async-start(bf16[8,16,16,128]{3,1,2,0:T(8,128)(2,1)} %copy.501), calls=%async_computation.15 | async-start | bytes 1048576 | tf_op jit(solution)/shard_map/while/body/all_to_all | solution.py:27
  415.3 12.7 %all-to-all-start.16 = ((bf16[8,16,16,128]{3,2,1,0:T(8,128)(2,1)}), bf16[8,16,16,128]{3,2,1,0:T(8,128)(2,1)S(1)}, u32[]{:S(2)}, u32[]{:S(2)}) async-start(bf16[8,16,16,128]{3,2,1,0:T(8,128)(2,1)} %bitcast.1143), calls=%async_computation.16 | async-start | bytes 1048576 | tf_op jit(solution)/shard_map/while/body/all_to_all | solution.py:27
  443.1 12.7 %all-to-all-start.18 = ((bf16[8,16,16,128]{3,1,2,0:T(8,128)(2,1)}), bf16[8,16,16,128]{3,1,2,0:T(8,128)(2,1)S(1)}, u32[]{:S(2)}, u32[]{:S(2)}) async-start(bf16[8,16,16,128]{3,1,2,0:T(8,128)(2,1)} %copy.506), calls=%async_computation.18 | async-start | bytes 1048576 | tf_op jit(solution)/shard_map/while/body/all_to_all | solution.py:27
  458.9 12.7 %all-to-all-start.19 = ((bf16[8,16,16,128]{3,2,1,0:T(8,128)(2,1)}), bf16[8,16,16,128]{3,2,1,0:T(8,128)(2,1)S(1)}, u32[]{:S(2)}, u32[]{:S(2)}) async-start(bf16[8,16,16,128]{3,2,1,0:T(8,128)(2,1)} %copy.508), calls=%async_computation.19 | async-start | bytes 1048576 | tf_op jit(solution)/shard_map/while/body/all_to_all | solution.py:27
  479.2 229.4 %reduce-scatter.8.cloned.1.call-start = ((), (), s32[]{:S(2)}) async-start(), calls=%async_computation.38 | async-start | bytes 2621440 | tf_op jit(solution)/shard_map/reduce_scatter | solution.py:132
  482.4 12.7 %all-to-all-start.20 = ((bf16[8,16,16,128]{3,2,1,0:T(8,128)(2,1)}), bf16[8,16,16,128]{3,2,1,0:T(8,128)(2,1)S(1)}, u32[]{:S(2)}, u32[]{:S(2)}) async-start(bf16[8,16,16,128]{3,2,1,0:T(8,128)(2,1)} %bitcast.1183), calls=%async_computation.20 | async-start | bytes 1048576 | tf_op jit(solution)/shard_map/while/body/all_to_all | solution.py:27
  510.2 12.7 %all-to-all-start.22 = ((bf16[8,16,16,128]{3,1,2,0:T(8,128)(2,1)}), bf16[8,16,16,128]{3,1,2,0:T(8,128)(2,1)S(1)}, u32[]{:S(2)}, u32[]{:S(2)}) async-start(bf16[8,16,16,128]{3,1,2,0:T(8,128)(2,1)} %copy.516), calls=%async_computation.22 | async-start | bytes 1048576 | tf_op jit(solution)/shard_map/while/body/all_to_all | solution.py:27
  526.0 12.7 %all-to-all-start.23 = ((bf16[8,16,16,128]{3,2,1,0:T(8,128)(2,1)}), bf16[8,16,16,128]{3,2,1,0:T(8,128)(2,1)S(1)}, u32[]{:S(2)}, u32[]{:S(2)}) async-start(bf16[8,16,16,128]{3,2,1,0:T(8,128)(2,1)} %copy.518), calls=%async_computation.23 | async-start | bytes 1048576 | tf_op jit(solution)/shard_map/while/body/all_to_all | solution.py:27
  546.4 168.4 %reduce-scatter.14.cloned.1.call-start = ((), (), s32[]{:S(2)}) async-start(), calls=%async_computation.41 | async-start | bytes 1310720 | tf_op jit(solution)/shard_map/reduce_scatter | solution.py:132
  552.6 12.7 %all-to-all-start.24 = ((bf16[8,16,16,128]{3,2,1,0:T(8,128)(2,1)}), bf16[8,16,16,128]{3,2,1,0:T(8,128)(2,1)S(1)}, u32[]{:S(2)}, u32[]{:S(2)}) async-start(bf16[8,16,16,128]{3,2,1,0:T(8,128)(2,1)} %bitcast.1223), calls=%async_computation.24 | async-start | bytes 1048576 | tf_op jit(solution)/shard_map/while/body/all_to_all | solution.py:27
  580.3 12.7 %all-to-all-start.26 = ((bf16[8,16,16,128]{3,1,2,0:T(8,128)(2,1)}), bf16[8,16,16,128]{3,1,2,0:T(8,128)(2,1)S(1)}, u32[]{:S(2)}, u32[]{:S(2)}) async-start(bf16[8,16,16,128]{3,1,2,0:T(8,128)(2,1)} %copy.526), calls=%async_computation.26 | async-start | bytes 1048576 | tf_op jit(solution)/shard_map/while/body/all_to_all | solution.py:27
  596.2 12.7 %all-to-all-start.27 = ((bf16[8,16,16,128]{3,2,1,0:T(8,128)(2,1)}), bf16[8,16,16,128]{3,2,1,0:T(8,128)(2,1)S(1)}, u32[]{:S(2)}, u32[]{:S(2)}) async-start(bf16[8,16,16,128]{3,2,1,0:T(8,128)(2,1)} %copy.528), calls=%async_computation.27 | async-start | bytes 1048576 | tf_op jit(solution)/shard_map/while/body/all_to_all | solution.py:27
  615.0 12.7 %all-to-all-start.28 = ((bf16[8,16,16,128]{3,2,1,0:T(8,128)(2,1)}), bf16[8,16,16,128]{3,2,1,0:T(8,128)(2,1)S(1)}, u32[]{:S(2)}, u32[]{:S(2)}) async-start(bf16[8,16,16,128]{3,2,1,0:T(8,128)(2,1)} %bitcast.1249), calls=%async_computation.28 | async-start | bytes 1048576 | tf_op jit(solution)/shard_map/while/body/all_to_all | solution.py:27
  630.5 12.7 %all-to-all-start.29 = ((bf16[8,16,16,128]{3,2,1,0:T(8,128)(2,1)}), bf16[8,16,16,128]{3,2,1,0:T(8,128)(2,1)S(1)}, u32[]{:S(2)}, u32[]{:S(2)}) async-start(bf16[8,16,16,128]{3,2,1,0:T(8,128)(2,1)} %copy.534), calls=%async_computation.29 | async-start | bytes 1048576 | tf_op jit(solution)/shard_map/while/body/all_to_all | solution.py:27
  648.1 12.7 %all-to-all-start.30 = ((bf16[8,16,16,128]{3,2,1,0:T(8,128)(2,1)}), bf16[8,16,16,128]{3,2,1,0:T(8,128)(2,1)S(1)}, u32[]{:S(2)}, u32[]{:S(2)}) async-start(bf16[8,16,16,128]{3,2,1,0:T(8,128)(2,1)} %bitcast.1268), calls=%async_computation.30 | async-start | bytes 1048576 | tf_op jit(solution)/shard_map/while/body/all_to_all | solution.py:27
  663.8 12.7 %all-to-all-start.31 = ((bf16[8,16,16,128]{3,2,1,0:T(8,128)(2,1)}), bf16[8,16,16,128]{3,2,1,0:T(8,128)(2,1)S(1)}, u32[]{:S(2)}, u32[]{:S(2)}) async-start(bf16[8,16,16,128]{3,2,1,0:T(8,128)(2,1)} %copy.539), calls=%async_computation.31 | async-start | bytes 1048576 | tf_op jit(solution)/shard_map/while/body/all_to_all | solution.py:27
  681.0 63.8 %reduce-scatter.12.cloned.1.call-start = ((), (), s32[]{:S(2)}) async-start(), calls=%async_computation.40 | async-start | bytes 1310720 | tf_op jit(solution)/shard_map/reduce_scatter | solution.py:132
  683.5 106.8 %reduce-scatter.10.cloned.1.call-start = ((), (), s32[]{:S(2)}) async-start(), calls=%async_computation.39 | async-start | bytes 2621440 | tf_op jit(solution)/shard_map/reduce_scatter | solution.py:132
  691.1 11.9 %collective-permute-start.18 = (bf16[4,128,128]{2,1,0:T(8,128)(2,1)S(1)}, bf16[4,128,128]{2,1,0:T(8,128)(2,1)S(1)}, u32[]{:S(2)}, u32[]{:S(2)}) collective-permute-start(bf16[4,128,128]{2,1,0:T(8,128)(2,1)S(1)} %bitcast.1474), channel_id=1, source_target_pairs={{0,4},{2,12},{4,20},{6,28},{8,6},{10,14},{12,22},{14,30},{16,0},{1... | collective-permute-start | bytes 393224 | tf_op jit(solution)/shard_map/ppermute | solution.py:76
  694.0 14.4 %collective-permute-start.19 = (bf16[4,128,128]{2,1,0:T(8,128)(2,1)S(1)}, bf16[4,128,128]{2,1,0:T(8,128)(2,1)S(1)}, u32[]{:S(2)}, u32[]{:S(2)}) collective-permute-start(bf16[4,128,128]{2,1,0:T(8,128)(2,1)S(1)} %bitcast.1475), channel_id=1, source_target_pairs={{0,6},{2,14},{4,22},{6,30},{8,4},{10,12},{12,20},{14,28},{16,2},{1... | collective-permute-start | bytes 393224 | tf_op jit(solution)/shard_map/ppermute | solution.py:76
  793.0 23.8 %collective-permute-start.28 = (bf16[2,4,128,128]{3,2,1,0:T(8,128)(2,1)}, bf16[2,4,128,128]{3,2,1,0:T(8,128)(2,1)}, u32[]{:S(2)}, u32[]{:S(2)}) collective-permute-start(bf16[2,4,128,128]{3,2,1,0:T(8,128)(2,1)} %pad_maximum_fusion.34), channel_id=1, source_target_pairs={{0,8},{8,0},{16,24},{24,16},{1,9},{9,1},{17,25},{25,17},{2,10},{10... | collective-permute-start | bytes 786440 | tf_op jit(solution)/shard_map/ppermute | solution.py:108
  797.1 13.2 %collective-permute-start.25 = (bf16[4,128,128]{2,1,0:T(8,128)(2,1)}, bf16[4,128,128]{2,1,0:T(8,128)(2,1)}, u32[]{:S(2)}, u32[]{:S(2)}) collective-permute-start(bf16[4,128,128]{2,1,0:T(8,128)(2,1)} %bitcast.303), channel_id=1, source_target_pairs={{0,2},{2,10},{4,18},{6,26},{8,0},{10,8},{12,16},{14,24},{16,6},{18... | collective-permute-start | bytes 393224 | tf_op jit(solution)/shard_map/ppermute | solution.py:76
  803.2 14.6 %collective-permute-start.29 = (bf16[2,4,128,128]{3,2,1,0:T(8,128)(2,1)S(1)}, bf16[2,4,128,128]{3,2,1,0:T(8,128)(2,1)S(1)}, u32[]{:S(2)}, u32[]{:S(2)}) collective-permute-start(bf16[2,4,128,128]{3,2,1,0:T(8,128)(2,1)S(1)} %pad_maximum_fusion.35), channel_id=1, source_target_pairs={{0,16},{8,24},{16,0},{24,8},{1,17},{9,25},{17,1},{25,9},{2,18},{10... | collective-permute-start | bytes 786440 | tf_op jit(solution)/shard_map/ppermute | solution.py:108
  810.3 11.8 %collective-permute-start.30 = (bf16[2,4,128,128]{3,2,1,0:T(8,128)(2,1)S(1)}, bf16[2,4,128,128]{3,2,1,0:T(8,128)(2,1)S(1)}, u32[]{:S(2)}, u32[]{:S(2)}) collective-permute-start(bf16[2,4,128,128]{3,2,1,0:T(8,128)(2,1)S(1)} %pad_maximum_fusion.36), channel_id=1, source_target_pairs={{0,24},{8,16},{16,8},{24,0},{1,25},{9,17},{17,9},{25,1},{2,26},{10... | collective-permute-start | bytes 786440 | tf_op jit(solution)/shard_map/ppermute | solution.py:108
  810.3 12.9 %collective-permute-start.31 = (bf16[2,4,128,128]{3,2,1,0:T(8,128)(2,1)S(1)}, bf16[2,4,128,128]{3,2,1,0:T(8,128)(2,1)S(1)}, u32[]{:S(2)}, u32[]{:S(2)}) collective-permute-start(bf16[2,4,128,128]{3,2,1,0:T(8,128)(2,1)S(1)} %pad_maximum_fusion.37), channel_id=1, source_target_pairs={{0,8},{8,0},{16,24},{24,16},{1,9},{9,1},{17,25},{25,17},{2,10},{10... | collective-permute-start | bytes 786440 | tf_op jit(solution)/shard_map/ppermute | solution.py:108
  811.5 17.2 %collective-permute-start.32 = (bf16[2,4,128,128]{3,2,1,0:T(8,128)(2,1)S(1)}, bf16[2,4,128,128]{3,2,1,0:T(8,128)(2,1)S(1)}, u32[]{:S(2)}, u32[]{:S(2)}) collective-permute-start(bf16[2,4,128,128]{3,2,1,0:T(8,128)(2,1)S(1)} %pad_maximum_fusion.38), channel_id=1, source_target_pairs={{0,16},{8,24},{16,0},{24,8},{1,17},{9,25},{17,1},{25,9},{2,18},{10... | collective-permute-start | bytes 786440 | tf_op jit(solution)/shard_map/ppermute | solution.py:108
  816.8 14.2 %collective-permute-start.33 = (bf16[2,4,128,128]{3,2,1,0:T(8,128)(2,1)S(1)}, bf16[2,4,128,128]{3,2,1,0:T(8,128)(2,1)S(1)}, u32[]{:S(2)}, u32[]{:S(2)}) collective-permute-start(bf16[2,4,128,128]{3,2,1,0:T(8,128)(2,1)S(1)} %pad_maximum_fusion.39), channel_id=1, source_target_pairs={{0,24},{8,16},{16,8},{24,0},{1,25},{9,17},{17,9},{25,1},{2,26},{10... | collective-permute-start | bytes 786440 | tf_op jit(solution)/shard_map/ppermute | solution.py:108
  (76 other events, 683.2 us)
Sparse Core Ops, SparseCore 0:
  71.3 29.2 all-gather.8
  102.1 45.5 all-gather.10
  154.4 63.5 all-gather.14
  219.4 44.1 all-gather.12
  479.3 41.8 reduce-scatter.5
  546.5 41.8 reduce-scatter.7
  681.1 33.5 reduce-scatter.13
  717.1 27.6 reduce-scatter.11
  747.7 42.5 reduce-scatter.9

commit v14 on v13

--- a/solution.py
+++ b/solution.py
@@ -175,6 +175,7 @@
                 for loop in range(loops - 1):
                     parts.extend(ordered(part) for part in scattered(rights[loop], lefts[loop]))
                 grad = settled(arriving(cotangent))
+                grad, parts[end:] = lax.optimization_barrier((grad, parts[end:]))
             if coming:
                 ahead = gathered(jnp.stack([parts[layer] for layer in coming]))
         weights.update((layer, (full, layer - begin)) for layer in stretch)
@@ -189,25 +190,26 @@
 
     def backward_stretch(stretch):
         def run(_, carry):
-            grad, _ = carry
+            grad = carry[0]
             terms = []
             for layer in stretch:
                 grad, *pair = backward_layer(grad, *factors_of(layer), stored[layer])
                 terms += pair
-            return grad, laid_out(*terms)
+            return (grad, *terms)
 
         return run
 
-    backward = [range(end - 1, begin - 1, -1) for begin, end in zip(starts, starts[1:])][::-1]
+    backward = [range(top, top - PAIRED, -1) for top in range(layers - 1, 0, -PAIRED)]
     totals = []
     for place, stretch in enumerate(backward):
-        blank = jnp.zeros((groups, 2 * len(stretch), sub, size, size), BF16)
-        grad, terms = lax.fori_loop(0, once, backward_stretch(stretch), (grad, blank))
-        if place >= 2 and len(stretch) == PAIRED:
+        blanks = [jnp.zeros((own, size, size), BF16) for _ in range(2 * PAIRED)]
+        grad, *terms = lax.fori_loop(0, once, backward_stretch(stretch), (grad, *blanks))
+        if place >= 2:
             grad, terms, totals[place - 2] = lax.optimization_barrier((grad, terms, totals[place - 2]))
-        totals.append(summed(terms))
+        totals.append(summed(laid_out(*terms)))
     grad = lax.fori_loop(0, once, lambda _, acts: unsettled(acts), grad)
-    grad, totals[1:-1] = lax.optimization_barrier((grad, totals[1:-1]))
+    if len(totals) > 1:
+        grad, totals[-2] = lax.optimization_barrier((grad, totals[-2]))
     for stretch, total in zip(backward, totals):
         for step, layer in enumerate(stretch):
             sums[layer] = [total[2 * step], total[2 * step + 1]]

time: 854 us -> 895 us (1.048)
  starting transfers between devices: 134 us -> 157 us
  waiting for transfers between devices: 302 us -> 325 us
  local copies, waits for them, and re-layouts: 132 us -> 115 us
    reduce_scatter x5 -> x4, waiting for transfers between devices: 76.6 us -> 120 us  [summed(): lax.psum_scatter(terms.reshape(-1, size, size), 't', scatter_dimension=0,...]
    ppermute x16, waiting for transfers between devices: 52.8 us -> 17.4 us  [turned(): moved.append(lax.ppermute(pick(parts, send_by ^ mask), ('s', 't'), pairs))]
    ppermute x12, starting transfers between devices: 30.3 us -> 55.2 us  [scattered(): moved.append(lax.ppermute(value, 's', pairs))]
    all_gather x4, waiting for transfers between devices: 0.04 us -> 23.6 us  [gathered(): return lax.all_gather(part, 't', axis=0, tiled=False)]
    while x83 -> x64, local copies, waits for them, and re-layouts: 35.1 us -> 20.8 us  [the longest x17 20.7 us: body(): lax.fori_loop(0, once, backward_stretch(stretch), (grad, *blanks))]
    reshape x8 -> x0, local copies, waits for them, and re-layouts: 9.97 us -> none  [laid_out(): jnp.stack([term.reshape(groups, sub, size, size) for term in terms], axis=1)]
    all_to_all x18 -> x17, waiting for transfers between devices: 130 us -> 121 us  [exchange(): lax.all_to_all(pieces, WIDE, split_axis=0, concat_axis=0, tiled=True)]
    all_to_all x14 -> x15, blocking collectives: 172 us -> 179 us  [exchange(): lax.all_to_all(pieces, WIDE, split_axis=0, concat_axis=0, tiled=True)]
  transfers between devices with their start and end apart: 61 -> 59, of which waited for: 36 -> 36; matrix products, arithmetic and copies ran while one was open for 19% -> 11% of each run, Pallas kernels for 0% -> 0%
where the time goes in v14:
time: 895 us; the launch traced here: 884 us
  waiting for transfers between devices  325 us (36%)
  blocking collectives  179 us (20%)
  starting transfers between devices  157 us (18%)
  local copies, waits for them, and re-layouts  115 us (13%)
  matrix products  67 us (7%)
  other arithmetic  23 us (3%)
  between operations  15.9 us (2%)
    all_to_all x15, blocking collectives, exchange(): lax.all_to_all(pieces, WIDE, split_axis=0, concat_axis=0, tiled=True)  179 us
    all_to_all x17, waiting for transfers between devices, exchange(): lax.all_to_all(pieces, WIDE, split_axis=0, concat_axis=0, tiled=True)  121 us
    reduce_scatter x4, waiting for transfers between devices, summed(): lax.psum_scatter(terms.reshape(-1, size, size), 't', scatter_dimension=0,...  120 us
    all_to_all x17, starting transfers between devices, exchange(): lax.all_to_all(pieces, WIDE, split_axis=0, concat_axis=0, tiled=True)  59.5 us
    ppermute x12, starting transfers between devices, scattered(): moved.append(lax.ppermute(value, 's', pairs))  55.2 us
    ppermute x16, starting transfers between devices, turned(): moved.append(lax.ppermute(pick(parts, send_by ^ mask), ('s', 't'), pairs))  31.4 us
    ppermute x12, waiting for transfers between devices, scattered(): moved.append(lax.ppermute(value, 's', pairs))  28.5 us
    another operation x27, local copies, waits for them, and re-layouts  24.2 us
  transfers between devices with their start and end apart: 59, of which 36 were waited for; matrix products, arithmetic and copies ran while one was open for 11% of the time, Pallas kernels for 0%

profile of v14, /device:TPU:0, one launch (start us, length us, event | category | flops | bytes accessed | tf_op | source)
XLA Modules:
  0.0 883.7 jit_solution(2144835456204920084)
XLA Ops:
  21.3 13.8 %collective-permute-start.5 = (bf16[2,4,128,128]{2,3,1,0:T(8,128)(2,1)S(1)}, bf16[2,4,128,128]{2,3,1,0:T(8,128)(2,1)S(1)}, u32[]{:S(2)}, u32[]{:S(2)}) collective-permute-start(bf16[2,4,128,128]{2,3,1,0:T(8,128)(2,1)S(1)} %pad_maximum_fusion.28), channel_id=1, source_target_pairs={{0,16},{8,24},{16,0},{24,8},{1,17},{9,25},{17,1},{25,9},{2,18},{10... | collective-permute-start | bytes 786440 | tf_op jit(solution)/shard_map/ppermute | solution.py:108
  60.9 9.8 %collective-permute-done.11 = bf16[4,128,128]{2,1,0:T(8,128)(2,1)S(1)} collective-permute-done((bf16[4,128,128]{2,1,0:T(8,128)(2,1)S(1)}, bf16[4,128,128]{2,1,0:T(8,128)(2,1)S(1)}, u32[]{:S(2)}, u32[]{:S(2)}) %collective-permute-start.11) | collective-permute-done | bytes 131104 | tf_op jit(solution)/shard_map/ppermute | solution.py:121
  77.0 28.1 %while.155 = (s32[]{:T(128)}, bf16[16,128,128]{2,1,0:T(8,128)(2,1)S(1)}, bf16[16,128,128]{2,0,1:T(8,128)(2,1)}, s32[]{:T(128)}, bf16[4,1,2,4,128,128]{4,5,3,0,2,1:T(8,128)(2,1)S(1)}, /*index=5*/s32[]{:T(128)}) while((s32[]{:T(128)}, bf16[16,128,128]{2,1,0:T(8,128)(2,1)S(1)}, bf16[16,128,128]{2,0,1:T(8,128)(2,1)}, s32[]{:T(128)}, ...), condition=%wide.region_1.2_spmd, body=%wide.region_0.1_spmd.sunk | while | flops 137363456 | bytes 16777344 | solution.py:184
  77.5 13.0 %all_to_all.192 = bf16[8,16,16,128]{3,1,2,0:T(8,128)(2,1)S(1)} all-to-all(bf16[8,16,16,128]{3,1,2,0:T(8,128)(2,1)S(1)} %copy.502), channel_id=1, replica_groups=mesh['s'=4,'t'=4,'x'=2] {'s','x'}, dimensions={0} | all-to-all | bytes 1048576 | tf_op jit(solution)/shard_map/while/body/all_to_all | solution.py:27
  95.4 9.2 %all-to-all-done.1 = bf16[8,16,16,128]{3,1,2,0:T(8,128)(2,1)S(1)} async-done(((bf16[8,16,16,128]{3,1,2,0:T(8,128)(2,1)}), bf16[8,16,16,128]{3,1,2,0:T(8,128)(2,1)S(1)}, u32[]{:S(2)}, u32[]{:S(2)}) %all-to-all-start.1) | async-done | bytes 524320 | tf_op jit(solution)/shard_map/while/body/all_to_all | solution.py:27
  107.8 26.8 %while.156 = (s32[]{:T(128)}, bf16[16,128,128]{2,1,0:T(8,128)(2,1)S(1)}, bf16[16,128,128]{2,0,1:T(8,128)(2,1)}, s32[]{:T(128)}, bf16[4,1,2,4,128,128]{4,5,3,0,2,1:T(8,128)(2,1)S(1)}, /*index=5*/s32[]{:T(128)}) while((s32[]{:T(128)}, bf16[16,128,128]{2,1,0:T(8,128)(2,1)S(1)}, bf16[16,128,128]{2,0,1:T(8,128)(2,1)}, s32[]{:T(128)}, ...), condition=%wide.region_3.4_spmd, body=%wide.region_2.3_spmd.sunk | while | flops 137363456 | bytes 16777344 | solution.py:184
  108.3 11.7 %all_to_all.193 = bf16[8,16,16,128]{3,1,2,0:T(8,128)(2,1)S(1)} all-to-all(bf16[8,16,16,128]{3,1,2,0:T(8,128)(2,1)S(1)} %copy.506), channel_id=1, replica_groups=mesh['s'=4,'t'=4,'x'=2] {'s','x'}, dimensions={0} | all-to-all | bytes 1048576 | tf_op jit(solution)/shard_map/while/body/all_to_all | solution.py:27
  124.9 9.2 %all-to-all-done.3 = bf16[8,16,16,128]{3,1,2,0:T(8,128)(2,1)S(1)} async-done(((bf16[8,16,16,128]{3,1,2,0:T(8,128)(2,1)}), bf16[8,16,16,128]{3,1,2,0:T(8,128)(2,1)S(1)}, u32[]{:S(2)}, u32[]{:S(2)}) %all-to-all-start.3) | async-done | bytes 524320 | tf_op jit(solution)/shard_map/while/body/all_to_all | solution.py:27
  146.6 16.3 %collective-permute-start.18 = (bf16[2,4,128,128]{2,3,1,0:T(8,128)(2,1)S(1)}, bf16[2,4,128,128]{2,3,1,0:T(8,128)(2,1)S(1)}, u32[]{:S(2)}, u32[]{:S(2)}) collective-permute-start(bf16[2,4,128,128]{2,3,1,0:T(8,128)(2,1)S(1)} %pad_maximum_fusion.31), channel_id=1, source_target_pairs={{0,16},{8,24},{16,0},{24,8},{1,17},{9,25},{17,1},{25,9},{2,18},{10... | collective-permute-start | bytes 786440 | tf_op jit(solution)/shard_map/ppermute | solution.py:108
  184.0 54.9 %while.157 = (s32[]{:T(128)}, bf16[16,128,128]{2,1,0:T(8,128)(2,1)S(1)}, bf16[16,128,128]{2,0,1:T(8,128)(2,1)}, bf16[16,128,128]{2,1,0:T(8,128)(2,1)}, bf16[16,1...) while((s32[]{:T(128)}, bf16[16,128,128]{2,1,0:T(8,128)(2,1)S(1)}, ...), condition=%wide.region_5.6_spmd, body=%wide.region_4.5_spmd.sunk | while | flops 274726912 | bytes 35127496 | solution.py:184
  186.1 13.2 %all_to_all.194 = bf16[8,16,16,128]{3,1,2,0:T(8,128)(2,1)S(1)} all-to-all(bf16[8,16,16,128]{3,1,2,0:T(8,128)(2,1)S(1)} %copy.512), channel_id=1, replica_groups=mesh['s'=4,'t'=4,'x'=2] {'s','x'}, dimensions={0} | all-to-all | bytes 1048576 | tf_op jit(solution)/shard_map/while/body/all_to_all | solution.py:27
  200.0 11.7 %all_to_all.195 = bf16[8,16,16,128]{3,1,2,0:T(8,128)(2,1)S(1)} all-to-all(bf16[8,16,16,128]{3,1,2,0:T(8,128)(2,1)S(1)} %copy.513), channel_id=1, replica_groups=mesh['s'=4,'t'=4,'x'=2] {'s','x'}, dimensions={0} | all-to-all | bytes 1048576 | tf_op jit(solution)/shard_map/while/body/all_to_all | solution.py:27
  212.5 11.7 %all_to_all.196 = bf16[8,16,16,128]{3,1,2,0:T(8,128)(2,1)S(1)} all-to-all(bf16[8,16,16,128]{3,1,2,0:T(8,128)(2,1)S(1)} %copy.514), channel_id=1, replica_groups=mesh['s'=4,'t'=4,'x'=2] {'s','x'}, dimensions={0} | all-to-all | bytes 1048576 | tf_op jit(solution)/shard_map/while/body/all_to_all | solution.py:27
  229.2 9.2 %all-to-all-done.7 = bf16[8,16,16,128]{3,1,2,0:T(8,128)(2,1)S(1)} async-done(((bf16[8,16,16,128]{3,1,2,0:T(8,128)(2,1)}), bf16[8,16,16,128]{3,1,2,0:T(8,128)(2,1)S(1)}, u32[]{:S(2)}, u32[]{:S(2)}) %all-to-all-start.7) | async-done | bytes 524320 | tf_op jit(solution)/shard_map/while/body/all_to_all | solution.py:27
  246.4 23.5 %all-gather.13.cloned.1.call-done = bf16[8,2,4,128,128]{4,3,2,1,0:T(8,128)(2,1)} async-done(((bf16[2,2,4,128,128]{4,3,2,1,0:T(8,128)(2,1)}), bf16[8,2,4,128,128]{4,3,2,1,0:T(8,128)(2,1)}) %all-gather.13.cloned.1.call-update) | async-done | bytes 2097168 | tf_op jit(solution)/shard_map/all_gather | solution.py:116
  278.4 54.2 %while.158 = (s32[]{:T(128)}, bf16[16,128,128]{2,1,0:T(8,128)(2,1)S(1)}, bf16[16,128,128]{2,0,1:T(8,128)(2,1)}, bf16[16,128,128]{2,1,0:T(8,128)(2,1)}, bf16[16,1...) while((s32[]{:T(128)}, bf16[16,128,128]{2,1,0:T(8,128)(2,1)S(1)}, ...), condition=%wide.region_7.8_spmd, body=%wide.region_6.7_spmd.sunk | while | flops 274726912 | bytes 35127496 | solution.py:184
  280.4 12.7 %all_to_all.197 = bf16[8,16,16,128]{3,1,2,0:T(8,128)(2,1)S(1)} all-to-all(bf16[8,16,16,128]{3,1,2,0:T(8,128)(2,1)S(1)} %copy.520), channel_id=1, replica_groups=mesh['s'=4,'t'=4,'x'=2] {'s','x'}, dimensions={0} | all-to-all | bytes 1048576 | tf_op jit(solution)/shard_map/while/body/all_to_all | solution.py:27
  293.7 11.7 %all_to_all.198 = bf16[8,16,16,128]{3,1,2,0:T(8,128)(2,1)S(1)} all-to-all(bf16[8,16,16,128]{3,1,2,0:T(8,128)(2,1)S(1)} %copy.521), channel_id=1, replica_groups=mesh['s'=4,'t'=4,'x'=2] {'s','x'}, dimensions={0} | all-to-all | bytes 1048576 | tf_op jit(solution)/shard_map/while/body/all_to_all | solution.py:27
  306.3 11.7 %all_to_all.199 = bf16[8,16,16,128]{3,1,2,0:T(8,128)(2,1)S(1)} all-to-all(bf16[8,16,16,128]{3,1,2,0:T(8,128)(2,1)S(1)} %copy.522), channel_id=1, replica_groups=mesh['s'=4,'t'=4,'x'=2] {'s','x'}, dimensions={0} | all-to-all | bytes 1048576 | tf_op jit(solution)/shard_map/while/body/all_to_all | solution.py:27
  322.9 9.2 %all-to-all-done.11 = bf16[8,16,16,128]{3,1,2,0:T(8,128)(2,1)S(1)} async-done(((bf16[8,16,16,128]{3,1,2,0:T(8,128)(2,1)}), bf16[8,16,16,128]{3,1,2,0:T(8,128)(2,1)S(1)}, u32[]{:S(2)}, u32[]{:S(2)}) %all-to-all-start.11) | async-done | bytes 524320 | tf_op jit(solution)/shard_map/while/body/all_to_all | solution.py:27
  335.3 53.6 %while.159 = (s32[]{:T(128)}, bf16[16,128,128]{2,1,0:T(8,128)(2,1)S(1)}, bf16[16,128,128]{2,0,1:T(8,128)(2,1)}, bf16[16,128,128]{2,1,0:T(8,128)(2,1)}, bf16[16,1...) while((s32[]{:T(128)}, ...), condition=%wide.region_9.10_spmd, body=%wide.region_8.9_spmd.sunk | while | flops 274726912 | bytes 35127496 | solution.py:184
  337.7 11.7 %all_to_all.200 = bf16[8,16,16,128]{3,1,2,0:T(8,128)(2,1)S(1)} all-to-all(bf16[8,16,16,128]{3,1,2,0:T(8,128)(2,1)S(1)} %copy.528), channel_id=1, replica_groups=mesh['s'=4,'t'=4,'x'=2] {'s','x'}, dimensions={0} | all-to-all | bytes 1048576 | tf_op jit(solution)/shard_map/while/body/all_to_all | solution.py:27
  350.0 11.7 %all_to_all.201 = bf16[8,16,16,128]{3,1,2,0:T(8,128)(2,1)S(1)} all-to-all(bf16[8,16,16,128]{3,1,2,0:T(8,128)(2,1)S(1)} %copy.529), channel_id=1, replica_groups=mesh['s'=4,'t'=4,'x'=2] {'s','x'}, dimensions={0} | all-to-all | bytes 1048576 | tf_op jit(solution)/shard_map/while/body/all_to_all | solution.py:27
  362.6 11.7 %all_to_all.202 = bf16[8,16,16,128]{3,1,2,0:T(8,128)(2,1)S(1)} all-to-all(bf16[8,16,16,128]{3,1,2,0:T(8,128)(2,1)S(1)} %copy.530), channel_id=1, replica_groups=mesh['s'=4,'t'=4,'x'=2] {'s','x'}, dimensions={0} | all-to-all | bytes 1048576 | tf_op jit(solution)/shard_map/while/body/all_to_all | solution.py:27
  379.2 9.2 %all-to-all-done.15 = bf16[8,16,16,128]{3,1,2,0:T(8,128)(2,1)S(1)} async-done(((bf16[8,16,16,128]{3,1,2,0:T(8,128)(2,1)}), bf16[8,16,16,128]{3,1,2,0:T(8,128)(2,1)S(1)}, u32[]{:S(2)}, u32[]{:S(2)}) %all-to-all-start.15) | async-done | bytes 524320 | tf_op jit(solution)/shard_map/while/body/all_to_all | solution.py:27
  398.7 59.3 %while.160 = (s32[]{:T(128)}, bf16[16,128,128]{2,1,0:T(8,128)(2,1)S(1)}, bf16[16,128,128]{1,2,0:T(8,128)(2,1)}, bf16[16,128,128]{2,1,0:T(8,128)(2,1)}, bf16[16,1...) while((s32[]{:T(128)}, ...), condition=%wide.region_11.12_spmd, body=%wide.region_10.11_spmd.sunk | while | flops 547880960 | bytes 39321904 | solution.py:206
  406.1 6.5 all-to-all-done.16
  414.6 11.8 %all_to_all.203 = bf16[8,16,16,128]{3,1,2,0:T(8,128)(2,1)S(1)} all-to-all(bf16[8,16,16,128]{3,1,2,0:T(8,128)(2,1)S(1)} %copy.534), channel_id=1, replica_groups=mesh['s'=4,'t'=4,'x'=2] {'s','x'}, dimensions={0} | all-to-all | bytes 1048576 | tf_op jit(solution)/shard_map/while/body/all_to_all | solution.py:27
  433.6 6.8 all-to-all-done.18
  461.7 59.5 %while.161 = (s32[]{:T(128)}, bf16[16,128,128]{2,1,0:T(8,128)(2,1)S(1)}, bf16[16,128,128]{1,2,0:T(8,128)(2,1)}, bf16[16,128,128]{2,1,0:T(8,128)(2,1)}, bf16[16,1...) while((s32[]{:T(128)}, ...), condition=%wide.region_13.14_spmd, body=%wide.region_12.13_spmd.sunk | while | flops 547880960 | bytes 39321904 | solution.py:206
  469.3 6.4 all-to-all-done.20
  477.8 11.8 %all_to_all.204 = bf16[8,16,16,128]{3,1,2,0:T(8,128)(2,1)S(1)} all-to-all(bf16[8,16,16,128]{3,1,2,0:T(8,128)(2,1)S(1)} %copy.542), channel_id=1, replica_groups=mesh['s'=4,'t'=4,'x'=2] {'s','x'}, dimensions={0} | all-to-all | bytes 1048576 | tf_op jit(solution)/shard_map/while/body/all_to_all | solution.py:27
  496.9 6.7 all-to-all-done.22
  536.2 30.7 %reduce-scatter.7.cloned.1.call-done = bf16[16,128,128]{2,1,0:T(8,128)(2,1)} async-done(((bf16[64,128,128]{2,1,0:T(8,128)(2,1)}), bf16[16,128,128]{2,1,0:T(8,128)(2,1)}) %reduce-scatter.7.cloned.1.call-update) | async-done | bytes 524304 | tf_op jit(solution)/shard_map/reduce_scatter | solution.py:132
  569.5 43.5 %reduce-scatter.5.cloned.1.call-done = bf16[16,128,128]{2,1,0:T(8,128)(2,1)} async-done(((bf16[64,128,128]{2,1,0:T(8,128)(2,1)}), bf16[16,128,128]{2,1,0:T(8,128)(2,1)}) %reduce-scatter.5.cloned.1.call-update) | async-done | bytes 524304 | tf_op jit(solution)/shard_map/reduce_scatter | solution.py:132
  619.2 59.8 %while.162 = (s32[]{:T(128)}, bf16[16,128,128]{2,1,0:T(8,128)(2,1)S(1)}, bf16[16,128,128]{1,2,0:T(8,128)(2,1)}, bf16[16,128,128]{2,1,0:T(8,128)(2,1)}, bf16[16,1...) while((s32[]{:T(128)}, ...), condition=%wide.region_15.16_spmd, body=%wide.region_14.15_spmd.sunk | while | flops 547880960 | bytes 39321904 | solution.py:206
  626.9 6.6 all-to-all-done.24
  635.5 11.8 %all_to_all.205 = bf16[8,16,16,128]{3,1,2,0:T(8,128)(2,1)S(1)} all-to-all(bf16[8,16,16,128]{3,1,2,0:T(8,128)(2,1)S(1)} %copy.550), channel_id=1, replica_groups=mesh['s'=4,'t'=4,'x'=2] {'s','x'}, dimensions={0} | all-to-all | bytes 1048576 | tf_op jit(solution)/shard_map/while/body/all_to_all | solution.py:27
  654.6 6.8 all-to-all-done.26
  682.6 59.0 %while.163 = (s32[]{:T(128)}, bf16[16,128,128]{2,1,0:T(8,128)(2,1)S(1)}, bf16[16,128,128]{1,2,0:T(8,128)(2,1)}, bf16[16,128,128]{2,1,0:T(8,128)(2,1)}, bf16[16,1...) while((s32[]{:T(128)}, ...), condition=%wide.region_18.19_spmd, body=%wide.region_17.18_spmd.sunk | while | flops 547880960 | bytes 39321912 | solution.py:206
  689.9 6.5 all-to-all-done.28
  698.5 11.7 %all_to_all.206 = bf16[8,16,16,128]{3,1,2,0:T(8,128)(2,1)S(1)} all-to-all(bf16[8,16,16,128]{3,1,2,0:T(8,128)(2,1)S(1)} %copy.558), channel_id=1, replica_groups=mesh['s'=4,'t'=4,'x'=2] {'s','x'}, dimensions={0} | all-to-all | bytes 1048576 | tf_op jit(solution)/shard_map/while/body/all_to_all | solution.py:27
  717.2 6.9 all-to-all-done.30
  734.2 5.6 all-to-all-done.31
  772.8 11.2 %collective-permute-start.32 = (bf16[2,4,128,128]{3,2,1,0:T(8,128)(2,1)S(1)}, bf16[2,4,128,128]{3,2,1,0:T(8,128)(2,1)S(1)}, u32[]{:S(2)}, u32[]{:S(2)}) collective-permute-start(bf16[2,4,128,128]{3,2,1,0:T(8,128)(2,1)S(1)} %pad_maximum_fusion.37), channel_id=1, source_target_pairs={{0,16},{8,24},{16,0},{24,8},{1,17},{9,25},{17,1},{25,9},{2,18},{10... | collective-permute-start | bytes 786440 | tf_op jit(solution)/shard_map/ppermute | solution.py:108
  784.6 6.5 collective-permute-done.32
  798.2 45.8 %reduce-scatter.9.cloned.1.call-done = bf16[16,128,128]{2,1,0:T(8,128)(2,1)} async-done(((bf16[64,128,128]{2,1,0:T(8,128)(2,1)}), bf16[16,128,128]{2,1,0:T(8,128)(2,1)}) %reduce-scatter.9.cloned.1.call-update) | async-done | bytes 524304 | tf_op jit(solution)/shard_map/reduce_scatter | solution.py:132
  854.7 8.0 collective-permute-start.29
  (542 shorter events, 373.3 us)
Async XLA Ops:
  7.2 98.0 %all-gather.9.cloned.1.call-start = ((), (), s32[]{:S(2)}) async-start(), calls=%async_computation.40 | async-start | bytes 1310720 | tf_op jit(solution)/shard_map/all_gather | solution.py:116
  10.7 28.7 %collective-permute-start.4 = (bf16[2,4,128,128]{2,3,1,0:T(8,128)(2,1)S(1)}, bf16[2,4,128,128]{2,3,1,0:T(8,128)(2,1)S(1)}, u32[]{:S(2)}, u32[]{:S(2)}) collective-permute-start(bf16[2,4,128,128]{2,3,1,0:T(8,128)(2,1)S(1)} %pad_maximum_fusion.27), channel_id=1, source_target_pairs={{0,8},{8,0},{16,24},{24,16},{1,9},{9,1},{17,25},{25,17},{2,10},{10... | collective-permute-start | bytes 786440 | tf_op jit(solution)/shard_map/ppermute | solution.py:108
  12.0 23.1 %collective-permute-start.1 = (bf16[4,128,128]{2,1,0:T(8,128)(2,1)S(1)}, bf16[4,128,128]{2,1,0:T(8,128)(2,1)S(1)}, u32[]{:S(2)}, u32[]{:S(2)}) collective-permute-start(bf16[4,128,128]{2,1,0:T(8,128)(2,1)S(1)} %get-tuple-element.1112), channel_id=1, source_target_pairs={{0,8},{2,0},{4,24},{6,16},{8,10},{10,2},{12,26},{14,18},{16,12},{1... | collective-permute-start | bytes 393224 | tf_op jit(solution)/shard_map/ppermute | solution.py:76
  16.0 23.2 %collective-permute-start.2 = (bf16[4,128,128]{2,1,0:T(8,128)(2,1)S(1)}, bf16[4,128,128]{2,1,0:T(8,128)(2,1)S(1)}, u32[]{:S(2)}, u32[]{:S(2)}) collective-permute-start(bf16[4,128,128]{2,1,0:T(8,128)(2,1)S(1)} %get-tuple-element.1111), channel_id=1, source_target_pairs={{0,16},{2,24},{4,0},{6,8},{8,18},{10,26},{12,2},{14,10},{16,20},{1... | collective-permute-start | bytes 393224 | tf_op jit(solution)/shard_map/ppermute | solution.py:76
  19.5 19.7 %collective-permute-start.3 = (bf16[4,128,128]{2,1,0:T(8,128)(2,1)S(1)}, bf16[4,128,128]{2,1,0:T(8,128)(2,1)S(1)}, u32[]{:S(2)}, u32[]{:S(2)}) collective-permute-start(bf16[4,128,128]{2,1,0:T(8,128)(2,1)S(1)} %get-tuple-element.1110), channel_id=1, source_target_pairs={{0,24},{2,16},{4,8},{6,0},{8,26},{10,18},{12,10},{14,2},{16,28},{1... | collective-permute-start | bytes 393224 | tf_op jit(solution)/shard_map/ppermute | solution.py:76
  21.3 20.0 %collective-permute-start.5 = (bf16[2,4,128,128]{2,3,1,0:T(8,128)(2,1)S(1)}, bf16[2,4,128,128]{2,3,1,0:T(8,128)(2,1)S(1)}, u32[]{:S(2)}, u32[]{:S(2)}) collective-permute-start(bf16[2,4,128,128]{2,3,1,0:T(8,128)(2,1)S(1)} %pad_maximum_fusion.28), channel_id=1, source_target_pairs={{0,16},{8,24},{16,0},{24,8},{1,17},{9,25},{17,1},{25,9},{2,18},{10... | collective-permute-start | bytes 786440 | tf_op jit(solution)/shard_map/ppermute | solution.py:108
  49.4 11.4 %collective-permute-start.9 = (bf16[4,128,128]{2,1,0:T(8,128)(2,1)S(1)}, bf16[4,128,128]{2,1,0:T(8,128)(2,1)S(1)}, u32[]{:S(2)}, u32[]{:S(2)}) collective-permute-start(bf16[4,128,128]{2,1,0:T(8,128)(2,1)S(1)} %get-tuple-element.1114), channel_id=1, source_target_pairs={{0,6},{2,4},{4,2},{6,0},{1,7},{3,5},{5,3},{7,1},{8,14},{10,12},{12... | collective-permute-start | bytes 393224 | tf_op jit(solution)/shard_map/ppermute | solution.py:121
  50.7 10.2 %collective-permute-start.10 = (bf16[4,128,128]{2,1,0:T(8,128)(2,1)S(1)}, bf16[4,128,128]{2,1,0:T(8,128)(2,1)S(1)}, u32[]{:S(2)}, u32[]{:S(2)}) collective-permute-start(bf16[4,128,128]{2,1,0:T(8,128)(2,1)S(1)} %get-tuple-element.1115), channel_id=1, source_target_pairs={{0,2},{2,0},{4,6},{6,4},{1,3},{3,1},{5,7},{7,5},{8,10},{10,8},{12,... | collective-permute-start | bytes 393224 | tf_op jit(solution)/shard_map/ppermute | solution.py:121
  51.3 19.4 %collective-permute-start.11 = (bf16[4,128,128]{2,1,0:T(8,128)(2,1)S(1)}, bf16[4,128,128]{2,1,0:T(8,128)(2,1)S(1)}, u32[]{:S(2)}, u32[]{:S(2)}) collective-permute-start(bf16[4,128,128]{2,1,0:T(8,128)(2,1)S(1)} %get-tuple-element.1115), channel_id=1, source_target_pairs={{0,4},{2,6},{4,0},{6,2},{1,5},{3,7},{5,1},{7,3},{8,12},{10,14},{12... | collective-permute-start | bytes 393224 | tf_op jit(solution)/shard_map/ppermute | solution.py:121
  54.9 15.8 %collective-permute-start.12 = (bf16[4,128,128]{2,1,0:T(8,128)(2,1)S(1)}, bf16[4,128,128]{2,1,0:T(8,128)(2,1)S(1)}, u32[]{:S(2)}, u32[]{:S(2)}) collective-permute-start(bf16[4,128,128]{2,1,0:T(8,128)(2,1)S(1)} %get-tuple-element.1115), channel_id=1, source_target_pairs={{0,6},{2,4},{4,2},{6,0},{1,7},{3,5},{5,3},{7,1},{8,14},{10,12},{12... | collective-permute-start | bytes 393224 | tf_op jit(solution)/shard_map/ppermute | solution.py:121
  71.2 106.1 %all-gather.11.cloned.1.call-start = ((), (), s32[]{:S(2)}) async-start(), calls=%async_computation.41 | async-start | bytes 2621440 | tf_op jit(solution)/shard_map/all_gather | solution.py:116
  75.4 163.6 %all-gather.15.cloned.1.call-start = ((), (), s32[]{:S(2)}) async-start(), calls=%async_computation.43 | async-start | bytes 2621440 | tf_op jit(solution)/shard_map/all_gather | solution.py:116
  91.9 12.7 %all-to-all-start.1 = ((bf16[8,16,16,128]{3,1,2,0:T(8,128)(2,1)}), bf16[8,16,16,128]{3,1,2,0:T(8,128)(2,1)S(1)}, u32[]{:S(2)}, u32[]{:S(2)}) async-start(bf16[8,16,16,128]{3,1,2,0:T(8,128)(2,1)} %copy.503), calls=%async_computation.1 | async-start | bytes 1048576 | tf_op jit(solution)/shard_map/while/body/all_to_all | solution.py:27
  121.4 12.7 %all-to-all-start.3 = ((bf16[8,16,16,128]{3,1,2,0:T(8,128)(2,1)}), bf16[8,16,16,128]{3,1,2,0:T(8,128)(2,1)S(1)}, u32[]{:S(2)}, u32[]{:S(2)}) async-start(bf16[8,16,16,128]{3,1,2,0:T(8,128)(2,1)} %copy.507), calls=%async_computation.3 | async-start | bytes 1048576 | tf_op jit(solution)/shard_map/while/body/all_to_all | solution.py:27
  136.6 31.1 %collective-permute-start.17 = (bf16[2,4,128,128]{2,3,1,0:T(8,128)(2,1)S(1)}, bf16[2,4,128,128]{2,3,1,0:T(8,128)(2,1)}, u32[]{:S(2)}, u32[]{:S(2)}) collective-permute-start(bf16[2,4,128,128]{2,3,1,0:T(8,128)(2,1)S(1)} %pad_maximum_fusion.30), channel_id=1, source_target_pairs={{0,8},{8,0},{16,24},{24,16},{1,9},{9,1},{17,25},{25,17},{2,10},{10... | collective-permute-start | bytes 786440 | tf_op jit(solution)/shard_map/ppermute | solution.py:108
  138.0 25.0 %collective-permute-start.14 = (bf16[4,128,128]{1,2,0:T(8,128)(2,1)S(1)}, bf16[4,128,128]{1,2,0:T(8,128)(2,1)S(1)}, u32[]{:S(2)}, u32[]{:S(2)}) collective-permute-start(bf16[4,128,128]{1,2,0:T(8,128)(2,1)S(1)} %bitcast.1449), channel_id=1, source_target_pairs={{0,8},{2,0},{4,24},{6,16},{8,10},{10,2},{12,26},{14,18},{16,12},{1... | collective-permute-start | bytes 393224 | tf_op jit(solution)/shard_map/ppermute | solution.py:76
  142.5 24.6 %collective-permute-start.15 = (bf16[4,128,128]{1,2,0:T(8,128)(2,1)S(1)}, bf16[4,128,128]{1,2,0:T(8,128)(2,1)S(1)}, u32[]{:S(2)}, u32[]{:S(2)}) collective-permute-start(bf16[4,128,128]{1,2,0:T(8,128)(2,1)S(1)} %bitcast.1448), channel_id=1, source_target_pairs={{0,16},{2,24},{4,0},{6,8},{8,18},{10,26},{12,2},{14,10},{16,20},{1... | collective-permute-start | bytes 393224 | tf_op jit(solution)/shard_map/ppermute | solution.py:76
  145.7 21.4 %collective-permute-start.16 = (bf16[4,128,128]{1,2,0:T(8,128)(2,1)S(1)}, bf16[4,128,128]{1,2,0:T(8,128)(2,1)S(1)}, u32[]{:S(2)}, u32[]{:S(2)}) collective-permute-start(bf16[4,128,128]{1,2,0:T(8,128)(2,1)S(1)} %bitcast.1450), channel_id=1, source_target_pairs={{0,24},{2,16},{4,8},{6,0},{8,26},{10,18},{12,10},{14,2},{16,28},{1... | collective-permute-start | bytes 393224 | tf_op jit(solution)/shard_map/ppermute | solution.py:76
  146.6 22.5 %collective-permute-start.18 = (bf16[2,4,128,128]{2,3,1,0:T(8,128)(2,1)S(1)}, bf16[2,4,128,128]{2,3,1,0:T(8,128)(2,1)S(1)}, u32[]{:S(2)}, u32[]{:S(2)}) collective-permute-start(bf16[2,4,128,128]{2,3,1,0:T(8,128)(2,1)S(1)} %pad_maximum_fusion.31), channel_id=1, source_target_pairs={{0,16},{8,24},{16,0},{24,8},{1,17},{9,25},{17,1},{25,9},{2,18},{10... | collective-permute-start | bytes 786440 | tf_op jit(solution)/shard_map/ppermute | solution.py:108
  175.9 94.0 %all-gather.13.cloned.1.call-start = ((), (), s32[]{:S(2)}) async-start(), calls=%async_computation.42 | async-start | bytes 2621440 | tf_op jit(solution)/shard_map/all_gather | solution.py:116
  177.2 389.8 %reduce-scatter.7.cloned.1.call-start = ((), (), s32[]{:S(2)}) async-start(), calls=%async_computation.37 | async-start | bytes 2621440 | tf_op jit(solution)/shard_map/reduce_scatter | solution.py:132
  225.7 12.7 %all-to-all-start.7 = ((bf16[8,16,16,128]{3,1,2,0:T(8,128)(2,1)}), bf16[8,16,16,128]{3,1,2,0:T(8,128)(2,1)S(1)}, u32[]{:S(2)}, u32[]{:S(2)}) async-start(bf16[8,16,16,128]{3,1,2,0:T(8,128)(2,1)} %copy.515), calls=%async_computation.7 | async-start | bytes 1048576 | tf_op jit(solution)/shard_map/while/body/all_to_all | solution.py:27
  319.4 12.7 %all-to-all-start.11 = ((bf16[8,16,16,128]{3,1,2,0:T(8,128)(2,1)}), bf16[8,16,16,128]{3,1,2,0:T(8,128)(2,1)S(1)}, u32[]{:S(2)}, u32[]{:S(2)}) async-start(bf16[8,16,16,128]{3,1,2,0:T(8,128)(2,1)} %copy.523), calls=%async_computation.11 | async-start | bytes 1048576 | tf_op jit(solution)/shard_map/while/body/all_to_all | solution.py:27
  375.7 12.7 %all-to-all-start.15 = ((bf16[8,16,16,128]{3,1,2,0:T(8,128)(2,1)}), bf16[8,16,16,128]{3,1,2,0:T(8,128)(2,1)S(1)}, u32[]{:S(2)}, u32[]{:S(2)}) async-start(bf16[8,16,16,128]{3,1,2,0:T(8,128)(2,1)} %copy.531), calls=%async_computation.15 | async-start | bytes 1048576 | tf_op jit(solution)/shard_map/while/body/all_to_all | solution.py:27
  399.8 12.7 %all-to-all-start.16 = ((bf16[8,16,16,128]{3,2,1,0:T(8,128)(2,1)}), bf16[8,16,16,128]{3,2,1,0:T(8,128)(2,1)S(1)}, u32[]{:S(2)}, u32[]{:S(2)}) async-start(bf16[8,16,16,128]{3,2,1,0:T(8,128)(2,1)} %bitcast.1128), calls=%async_computation.16 | async-start | bytes 1048576 | tf_op jit(solution)/shard_map/while/body/all_to_all | solution.py:27
  427.7 12.7 %all-to-all-start.18 = ((bf16[8,16,16,128]{3,1,2,0:T(8,128)(2,1)}), bf16[8,16,16,128]{3,1,2,0:T(8,128)(2,1)S(1)}, u32[]{:S(2)}, u32[]{:S(2)}) async-start(bf16[8,16,16,128]{3,1,2,0:T(8,128)(2,1)} %copy.536), calls=%async_computation.18 | async-start | bytes 1048576 | tf_op jit(solution)/shard_map/while/body/all_to_all | solution.py:27
  443.7 12.7 %all-to-all-start.19 = ((bf16[8,16,16,128]{3,2,1,0:T(8,128)(2,1)}), bf16[8,16,16,128]{3,2,1,0:T(8,128)(2,1)S(1)}, u32[]{:S(2)}, u32[]{:S(2)}) async-start(bf16[8,16,16,128]{3,2,1,0:T(8,128)(2,1)} %copy.538), calls=%async_computation.19 | async-start | bytes 1048576 | tf_op jit(solution)/shard_map/while/body/all_to_all | solution.py:27
  463.0 12.7 %all-to-all-start.20 = ((bf16[8,16,16,128]{3,2,1,0:T(8,128)(2,1)}), bf16[8,16,16,128]{3,2,1,0:T(8,128)(2,1)S(1)}, u32[]{:S(2)}, u32[]{:S(2)}) async-start(bf16[8,16,16,128]{3,2,1,0:T(8,128)(2,1)} %bitcast.1166), calls=%async_computation.20 | async-start | bytes 1048576 | tf_op jit(solution)/shard_map/while/body/all_to_all | solution.py:27
  490.9 12.7 %all-to-all-start.22 = ((bf16[8,16,16,128]{3,1,2,0:T(8,128)(2,1)}), bf16[8,16,16,128]{3,1,2,0:T(8,128)(2,1)S(1)}, u32[]{:S(2)}, u32[]{:S(2)}) async-start(bf16[8,16,16,128]{3,1,2,0:T(8,128)(2,1)} %copy.544), calls=%async_computation.22 | async-start | bytes 1048576 | tf_op jit(solution)/shard_map/while/body/all_to_all | solution.py:27
  506.8 12.7 %all-to-all-start.23 = ((bf16[8,16,16,128]{3,2,1,0:T(8,128)(2,1)}), bf16[8,16,16,128]{3,2,1,0:T(8,128)(2,1)S(1)}, u32[]{:S(2)}, u32[]{:S(2)}) async-start(bf16[8,16,16,128]{3,2,1,0:T(8,128)(2,1)} %copy.546), calls=%async_computation.23 | async-start | bytes 1048576 | tf_op jit(solution)/shard_map/while/body/all_to_all | solution.py:27
  525.6 87.5 %reduce-scatter.5.cloned.1.call-start = ((), (), s32[]{:S(2)}) async-start(), calls=%async_computation.36 | async-start | bytes 2621440 | tf_op jit(solution)/shard_map/reduce_scatter | solution.py:132
  528.8 267.7 %reduce-scatter.11.cloned.1.call-start = ((), (), s32[]{:S(2)}) async-start(), calls=%async_computation.39 | async-start | bytes 2621440 | tf_op jit(solution)/shard_map/reduce_scatter | solution.py:132
  620.5 12.9 %all-to-all-start.24 = ((bf16[8,16,16,128]{3,2,1,0:T(8,128)(2,1)}), bf16[8,16,16,128]{3,2,1,0:T(8,128)(2,1)S(1)}, u32[]{:S(2)}, u32[]{:S(2)}) async-start(bf16[8,16,16,128]{3,2,1,0:T(8,128)(2,1)} %bitcast.1204), calls=%async_computation.24 | async-start | bytes 1048576 | tf_op jit(solution)/shard_map/while/body/all_to_all | solution.py:27
  648.6 12.7 %all-to-all-start.26 = ((bf16[8,16,16,128]{3,1,2,0:T(8,128)(2,1)}), bf16[8,16,16,128]{3,1,2,0:T(8,128)(2,1)S(1)}, u32[]{:S(2)}, u32[]{:S(2)}) async-start(bf16[8,16,16,128]{3,1,2,0:T(8,128)(2,1)} %copy.552), calls=%async_computation.26 | async-start | bytes 1048576 | tf_op jit(solution)/shard_map/while/body/all_to_all | solution.py:27
  664.6 12.7 %all-to-all-start.27 = ((bf16[8,16,16,128]{3,2,1,0:T(8,128)(2,1)}), bf16[8,16,16,128]{3,2,1,0:T(8,128)(2,1)S(1)}, u32[]{:S(2)}, u32[]{:S(2)}) async-start(bf16[8,16,16,128]{3,2,1,0:T(8,128)(2,1)} %copy.554), calls=%async_computation.27 | async-start | bytes 1048576 | tf_op jit(solution)/shard_map/while/body/all_to_all | solution.py:27
  683.7 12.7 %all-to-all-start.28 = ((bf16[8,16,16,128]{3,2,1,0:T(8,128)(2,1)}), bf16[8,16,16,128]{3,2,1,0:T(8,128)(2,1)S(1)}, u32[]{:S(2)}, u32[]{:S(2)}) async-start(bf16[8,16,16,128]{3,2,1,0:T(8,128)(2,1)} %bitcast.1242), calls=%async_computation.28 | async-start | bytes 1048576 | tf_op jit(solution)/shard_map/while/body/all_to_all | solution.py:27
  711.4 12.7 %all-to-all-start.30 = ((bf16[8,16,16,128]{3,1,2,0:T(8,128)(2,1)}), bf16[8,16,16,128]{3,1,2,0:T(8,128)(2,1)S(1)}, u32[]{:S(2)}, u32[]{:S(2)}) async-start(bf16[8,16,16,128]{3,1,2,0:T(8,128)(2,1)} %copy.560), calls=%async_computation.30 | async-start | bytes 1048576 | tf_op jit(solution)/shard_map/while/body/all_to_all | solution.py:27
  727.2 12.7 %all-to-all-start.31 = ((bf16[8,16,16,128]{3,2,1,0:T(8,128)(2,1)}), bf16[8,16,16,128]{3,2,1,0:T(8,128)(2,1)S(1)}, u32[]{:S(2)}, u32[]{:S(2)}) async-start(bf16[8,16,16,128]{3,2,1,0:T(8,128)(2,1)} %copy.562), calls=%async_computation.31 | async-start | bytes 1048576 | tf_op jit(solution)/shard_map/while/body/all_to_all | solution.py:27
  745.9 98.1 %reduce-scatter.9.cloned.1.call-start = ((), (), s32[]{:S(2)}) async-start(), calls=%async_computation.38 | async-start | bytes 2621440 | tf_op jit(solution)/shard_map/reduce_scatter | solution.py:132
  754.4 12.0 %collective-permute-start.22 = (bf16[4,128,128]{2,1,0:T(8,128)(2,1)S(1)}, bf16[4,128,128]{2,1,0:T(8,128)(2,1)S(1)}, u32[]{:S(2)}, u32[]{:S(2)}) collective-permute-start(bf16[4,128,128]{2,1,0:T(8,128)(2,1)S(1)} %bitcast.1458), channel_id=1, source_target_pairs={{0,4},{2,12},{4,20},{6,28},{8,6},{10,14},{12,22},{14,30},{16,0},{1... | collective-permute-start | bytes 393224 | tf_op jit(solution)/shard_map/ppermute | solution.py:76
  757.3 14.1 %collective-permute-start.23 = (bf16[4,128,128]{2,1,0:T(8,128)(2,1)S(1)}, bf16[4,128,128]{2,1,0:T(8,128)(2,1)S(1)}, u32[]{:S(2)}, u32[]{:S(2)}) collective-permute-start(bf16[4,128,128]{2,1,0:T(8,128)(2,1)S(1)} %bitcast.1459), channel_id=1, source_target_pairs={{0,6},{2,14},{4,22},{6,30},{8,4},{10,12},{12,20},{14,28},{16,2},{1... | collective-permute-start | bytes 393224 | tf_op jit(solution)/shard_map/ppermute | solution.py:76
  772.1 12.5 %collective-permute-start.31 = (bf16[2,4,128,128]{3,2,1,0:T(8,128)(2,1)S(1)}, bf16[2,4,128,128]{3,2,1,0:T(8,128)(2,1)S(1)}, u32[]{:S(2)}, u32[]{:S(2)}) collective-permute-start(bf16[2,4,128,128]{3,2,1,0:T(8,128)(2,1)S(1)} %pad_maximum_fusion.36), channel_id=1, source_target_pairs={{0,8},{8,0},{16,24},{24,16},{1,9},{9,1},{17,25},{25,17},{2,10},{10... | collective-permute-start | bytes 786440 | tf_op jit(solution)/shard_map/ppermute | solution.py:108
  772.8 18.3 %collective-permute-start.32 = (bf16[2,4,128,128]{3,2,1,0:T(8,128)(2,1)S(1)}, bf16[2,4,128,128]{3,2,1,0:T(8,128)(2,1)S(1)}, u32[]{:S(2)}, u32[]{:S(2)}) collective-permute-start(bf16[2,4,128,128]{3,2,1,0:T(8,128)(2,1)S(1)} %pad_maximum_fusion.37), channel_id=1, source_target_pairs={{0,16},{8,24},{16,0},{24,8},{1,17},{9,25},{17,1},{25,9},{2,18},{10... | collective-permute-start | bytes 786440 | tf_op jit(solution)/shard_map/ppermute | solution.py:108
  784.0 12.3 %collective-permute-start.33 = (bf16[2,4,128,128]{3,2,1,0:T(8,128)(2,1)S(1)}, bf16[2,4,128,128]{3,2,1,0:T(8,128)(2,1)S(1)}, u32[]{:S(2)}, u32[]{:S(2)}) collective-permute-start(bf16[2,4,128,128]{3,2,1,0:T(8,128)(2,1)S(1)} %pad_maximum_fusion.38), channel_id=1, source_target_pairs={{0,24},{8,16},{16,8},{24,0},{1,25},{9,17},{17,9},{25,1},{2,26},{10... | collective-permute-start | bytes 786440 | tf_op jit(solution)/shard_map/ppermute | solution.py:108
  846.7 17.9 %collective-permute-start.28 = (bf16[2,4,128,128]{3,2,1,0:T(8,128)(2,1)}, bf16[2,4,128,128]{3,2,1,0:T(8,128)(2,1)}, u32[]{:S(2)}, u32[]{:S(2)}) collective-permute-start(bf16[2,4,128,128]{3,2,1,0:T(8,128)(2,1)} %pad_maximum_fusion.33), channel_id=1, source_target_pairs={{0,8},{8,0},{16,24},{24,16},{1,9},{9,1},{17,25},{25,17},{2,10},{10... | collective-permute-start | bytes 786440 | tf_op jit(solution)/shard_map/ppermute | solution.py:108
  847.7 15.0 %collective-permute-start.25 = (bf16[4,128,128]{2,1,0:T(8,128)(2,1)S(1)}, bf16[4,128,128]{2,1,0:T(8,128)(2,1)S(1)}, u32[]{:S(2)}, u32[]{:S(2)}) collective-permute-start(bf16[4,128,128]{2,1,0:T(8,128)(2,1)S(1)} %bitcast.1453), channel_id=1, source_target_pairs={{0,2},{2,10},{4,18},{6,26},{8,0},{10,8},{12,16},{14,24},{16,6},{18... | collective-permute-start | bytes 393224 | tf_op jit(solution)/shard_map/ppermute | solution.py:76
  851.3 11.5 %collective-permute-start.26 = (bf16[4,128,128]{2,1,0:T(8,128)(2,1)S(1)}, bf16[4,128,128]{2,1,0:T(8,128)(2,1)S(1)}, u32[]{:S(2)}, u32[]{:S(2)}) collective-permute-start(bf16[4,128,128]{2,1,0:T(8,128)(2,1)S(1)} %bitcast.1452), channel_id=1, source_target_pairs={{0,4},{2,12},{4,20},{6,28},{8,6},{10,14},{12,22},{14,30},{16,0},{1... | collective-permute-start | bytes 393224 | tf_op jit(solution)/shard_map/ppermute | solution.py:76
  854.7 14.3 %collective-permute-start.29 = (bf16[2,4,128,128]{3,2,1,0:T(8,128)(2,1)S(1)}, bf16[2,4,128,128]{3,2,1,0:T(8,128)(2,1)S(1)}, u32[]{:S(2)}, u32[]{:S(2)}) collective-permute-start(bf16[2,4,128,128]{3,2,1,0:T(8,128)(2,1)S(1)} %pad_maximum_fusion.34), channel_id=1, source_target_pairs={{0,16},{8,24},{16,0},{24,8},{1,17},{9,25},{17,1},{25,9},{2,18},{10... | collective-permute-start | bytes 786440 | tf_op jit(solution)/shard_map/ppermute | solution.py:108
  (76 other events, 778.4 us)
Sparse Core Ops, SparseCore 0:
  71.3 29.2 all-gather.8
  102.7 58.6 all-gather.10
  176.0 47.1 all-gather.14
  225.2 44.6 all-gather.12
  525.7 41.2 reduce-scatter.6
  569.8 43.1 reduce-scatter.4
  746.1 50.1 reduce-scatter.10
  799.3 44.7 reduce-scatter.8

commit v15 on v12

--- a/solution.py
+++ b/solution.py
@@ -141,6 +141,9 @@
     current = arriving(inputs)
     current, parts[0] = lax.optimization_barrier((current, parts[0]))
     once = 1 + s_index // sections
+    parts[0], rights, lefts = lax.optimization_barrier((parts[0], rights[1:], lefts[1:]))
+    for loop in range(loops - 1):
+        parts.extend(ordered(part) for part in scattered(rights[loop], lefts[loop]))
     first = jnp.stack([gathered_directly(parts[0][f]) for f in range(2)], axis=1)[:, None]
     starts = [0, 1] + list(range(PAIRED, layers, PAIRED)) + [layers]
     ahead = gathered(jnp.stack(parts[1:2]))
@@ -168,21 +171,17 @@
         full = ahead if begin else first
         if begin:
             coming = range(end, min(end + PAIRED, layers))
-            if begin == 1:
-                current, rights, lefts = lax.optimization_barrier((current, rights[1:], lefts[1:]))
-                for loop in range(loops - 1):
-                    parts.extend(ordered(part) for part in scattered(rights[loop], lefts[loop]))
             if coming:
                 ahead = gathered(jnp.stack([parts[layer] for layer in coming]))
         weights.update((layer, (full, layer - begin)) for layer in stretch)
-        if end + PAIRED == layers:
-            current, cotangent = lax.optimization_barrier((current, cotangent))
-            grad = settled(arriving(cotangent))
         blanks = [jnp.zeros(current.shape, BF16) for _ in range(2 * len(stretch) - 1)]
         entered = current
         current, *saved = lax.fori_loop(0, once, forward_stretch(stretch), (current, *blanks))
+        current, ahead = lax.optimization_barrier((current, ahead))
         saved = [entered] + saved
         stored.update((layer, saved[2 * step : 2 * step + 2]) for step, layer in enumerate(stretch))
+    current, cotangent = lax.optimization_barrier((current, cotangent))
+    grad = settled(arriving(cotangent))
     outputs = leave(unsettled(current))
 
     sums = [None] * layers
@@ -219,10 +218,7 @@
 
     halves = []
     for loop in range(loops):
-        if loop:
-            moved = jnp.stack(scattered(of_loop(loop, 0), of_loop(loop, 1)), axis=1)
-        else:
-            moved = jnp.stack([jnp.stack(scattered(of_loop(loop, factor)))[:, 0] for factor in range(2)])
+        moved = jnp.stack(scattered(of_loop(loop, 0), of_loop(loop, 1)), axis=1)
         halves.append(moved.reshape(2, 1, held, size, size))
     grads = jnp.stack(halves).astype(F32)
     return (outputs, input_grad, grads[:, 0], grads[:, 1])

time: 758 us -> 778 us (1.026)
  the two profiles are of different devices: /device:TPU:17 before, /device:TPU:0 now
where the time goes in v15:
time: 778 us; the launch traced here: 767 us
  waiting for transfers between devices  223 us (29%)
  blocking collectives  176 us (23%)
  starting transfers between devices  136 us (17%)
  local copies, waits for them, and re-layouts  130 us (17%)
  matrix products  58.9 us (8%)
  other arithmetic  24.2 us (3%)
  between operations  15.9 us (2%)
    all_to_all x15, blocking collectives, exchange(): lax.all_to_all(pieces, WIDE, split_axis=0, concat_axis=0, tiled=True)  176 us
    all_to_all x17, waiting for transfers between devices, exchange(): lax.all_to_all(pieces, WIDE, split_axis=0, concat_axis=0, tiled=True)  108 us
    all_to_all x17, starting transfers between devices, exchange(): lax.all_to_all(pieces, WIDE, split_axis=0, concat_axis=0, tiled=True)  64.3 us
    ppermute x16, waiting for transfers between devices, turned(): moved.append(lax.ppermute(pick(parts, send_by ^ mask), ('s', 't'), pairs))  45 us
    ppermute x12, starting transfers between devices, scattered(): moved.append(lax.ppermute(value, 's', pairs))  39 us
    ppermute x12, waiting for transfers between devices, scattered(): moved.append(lax.ppermute(value, 's', pairs))  37.9 us
    ppermute x6, waiting for transfers between devices, around(): lax.ppermute(value_of(mask), 't', [(t, t ^ mask) for t in range(groups)])  32.6 us
    while x15, local copies, waits for them, and re-layouts, body(): grad, terms = lax.fori_loop(0, once, backward_pair(top), (grad, blank))  21.6 us
  transfers between devices with their start and end apart: 59, of which 32 were waited for; matrix products, arithmetic and copies ran while one was open for 21% of the time, Pallas kernels for 0%

profile of v15, /device:TPU:0, one launch (start us, length us, event | category | flops | bytes accessed | tf_op | source)
XLA Modules:
  0.0 767.0 jit_solution(15325141101072126529)
XLA Ops:
  18.3 5.9 collective-permute-done.5
  38.1 25.8 %collective-permute-done.2 = bf16[4,128,128]{2,1,0:T(8,128)(2,1)S(1)} collective-permute-done((bf16[4,128,128]{2,1,0:T(8,128)(2,1)S(1)}, bf16[4,128,128]{2,1,0:T(8,128)(2,1)S(1)}, u32[]{:S(2)}, u32[]{:S(2)}) %collective-permute-start.2) | collective-permute-done | bytes 131104 | tf_op jit(solution)/shard_map/ppermute | solution.py:76
  65.1 6.6 collective-permute-start.15
  76.8 8.8 %collective-permute-done.14 = bf16[2,4,128,128]{2,3,1,0:T(8,128)(2,1)S(1)} collective-permute-done((bf16[2,4,128,128]{2,3,1,0:T(8,128)(2,1)S(1)}, bf16[2,4,128,128]{2,3,1,0:T(8,128)(2,1)S(1)}, u32[]{:S(2)}, u32[]{:S(2)}) %collective-permute-start.14) | collective-permute-done | bytes 262176 | tf_op jit(solution)/shard_map/ppermute | solution.py:108
  99.3 9.3 %collective-permute-start.7 = (bf16[4,128,128]{2,1,0:T(8,128)(2,1)S(1)}, bf16[4,128,128]{2,1,0:T(8,128)(2,1)S(1)}, u32[]{:S(2)}, u32[]{:S(2)}) collective-permute-start(bf16[4,128,128]{2,1,0:T(8,128)(2,1)S(1)} %get-tuple-element.976), channel_id=1, source_target_pairs={{0,2},{2,0},{4,6},{6,4},{1,3},{3,1},{5,7},{7,5},{8,10},{10,8},{12,... | collective-permute-start | bytes 393224 | tf_op jit(solution)/shard_map/ppermute | solution.py:121
  108.6 14.3 %collective-permute-done.11 = bf16[4,128,128]{2,1,0:T(8,128)(2,1)S(1)} collective-permute-done((bf16[4,128,128]{2,1,0:T(8,128)(2,1)S(1)}, bf16[4,128,128]{2,1,0:T(8,128)(2,1)S(1)}, u32[]{:S(2)}, u32[]{:S(2)}) %collective-permute-start.11) | collective-permute-done | bytes 131104 | tf_op jit(solution)/shard_map/ppermute | solution.py:121
  123.9 16.3 %collective-permute-done.8 = bf16[4,128,128]{2,1,0:T(8,128)(2,1)} collective-permute-done((bf16[4,128,128]{2,1,0:T(8,128)(2,1)S(1)}, bf16[4,128,128]{2,1,0:T(8,128)(2,1)}, u32[]{:S(2)}, u32[]{:S(2)}) %collective-permute-start.8) | collective-permute-done | bytes 131104 | tf_op jit(solution)/shard_map/ppermute | solution.py:121
  145.8 27.8 %while.131 = (s32[]{:T(128)}, bf16[16,128,128]{2,1,0:T(8,128)(2,1)S(1)}, bf16[16,128,128]{2,0,1:T(8,128)(2,1)}, s32[]{:T(128)}, bf16[4,1,2,4,128,128]{4,5,3,0,2,1:T(8,128)(2,1)S(1)}, /*index=5*/s32[]{:T(128)}) while((s32[]{:T(128)}, bf16[16,128,128]{2,1,0:T(8,128)(2,1)S(1)}, bf16[16,128,128]{2,0,1:T(8,128)(2,1)}, s32[]{:T(128)}, ...), condition=%wide.region_1.2_spmd, body=%wide.region_0.1_spmd.sunk | while | flops 137363456 | bytes 16777344 | solution.py:179
  146.3 12.7 %all_to_all.192 = bf16[8,16,16,128]{3,1,2,0:T(8,128)(2,1)S(1)} all-to-all(bf16[8,16,16,128]{3,1,2,0:T(8,128)(2,1)S(1)} %copy.464), channel_id=1, replica_groups=mesh['s'=4,'t'=4,'x'=2] {'s','x'}, dimensions={0} | all-to-all | bytes 1048576 | tf_op jit(solution)/shard_map/while/body/all_to_all | solution.py:27
  164.0 9.2 %all-to-all-done.1 = bf16[8,16,16,128]{3,1,2,0:T(8,128)(2,1)S(1)} async-done(((bf16[8,16,16,128]{3,1,2,0:T(8,128)(2,1)}), bf16[8,16,16,128]{3,1,2,0:T(8,128)(2,1)S(1)}, u32[]{:S(2)}, u32[]{:S(2)}) %all-to-all-start.1) | async-done | bytes 524320 | tf_op jit(solution)/shard_map/while/body/all_to_all | solution.py:27
  176.3 27.0 %while.132 = (s32[]{:T(128)}, bf16[16,128,128]{2,1,0:T(8,128)(2,1)S(1)}, bf16[16,128,128]{2,0,1:T(8,128)(2,1)}, s32[]{:T(128)}, bf16[4,1,2,4,128,128]{4,5,3,0,2,1:T(8,128)(2,1)S(1)}, /*index=5*/s32[]{:T(128)}) while((s32[]{:T(128)}, bf16[16,128,128]{2,1,0:T(8,128)(2,1)S(1)}, bf16[16,128,128]{2,0,1:T(8,128)(2,1)}, s32[]{:T(128)}, ...), condition=%wide.region_3.4_spmd, body=%wide.region_2.3_spmd.sunk | while | flops 137363456 | bytes 16777344 | solution.py:179
  177.0 11.7 %all_to_all.193 = bf16[8,16,16,128]{3,1,2,0:T(8,128)(2,1)S(1)} all-to-all(bf16[8,16,16,128]{3,1,2,0:T(8,128)(2,1)S(1)} %copy.468), channel_id=1, replica_groups=mesh['s'=4,'t'=4,'x'=2] {'s','x'}, dimensions={0} | all-to-all | bytes 1048576 | tf_op jit(solution)/shard_map/while/body/all_to_all | solution.py:27
  193.7 9.2 %all-to-all-done.3 = bf16[8,16,16,128]{3,1,2,0:T(8,128)(2,1)S(1)} async-done(((bf16[8,16,16,128]{3,1,2,0:T(8,128)(2,1)}), bf16[8,16,16,128]{3,1,2,0:T(8,128)(2,1)S(1)}, u32[]{:S(2)}, u32[]{:S(2)}) %all-to-all-start.3) | async-done | bytes 524320 | tf_op jit(solution)/shard_map/while/body/all_to_all | solution.py:27
  209.2 52.8 %while.133 = (s32[]{:T(128)}, bf16[16,128,128]{2,1,0:T(8,128)(2,1)S(1)}, bf16[16,128,128]{2,0,1:T(8,128)(2,1)}, bf16[16,128,128]{2,1,0:T(8,128)(2,1)}, bf16[16,1...) while((s32[]{:T(128)}, ...), condition=%wide.region_5.6_spmd, body=%wide.region_4.5_spmd.sunk | while | flops 274726912 | bytes 35127496 | solution.py:179
  209.8 11.7 %all_to_all.194 = bf16[8,16,16,128]{3,1,2,0:T(8,128)(2,1)S(1)} all-to-all(bf16[8,16,16,128]{3,1,2,0:T(8,128)(2,1)S(1)} %copy.474), channel_id=1, replica_groups=mesh['s'=4,'t'=4,'x'=2] {'s','x'}, dimensions={0} | all-to-all | bytes 1048576 | tf_op jit(solution)/shard_map/while/body/all_to_all | solution.py:27
  222.6 11.7 %all_to_all.195 = bf16[8,16,16,128]{3,1,2,0:T(8,128)(2,1)S(1)} all-to-all(bf16[8,16,16,128]{3,1,2,0:T(8,128)(2,1)S(1)} %copy.475), channel_id=1, replica_groups=mesh['s'=4,'t'=4,'x'=2] {'s','x'}, dimensions={0} | all-to-all | bytes 1048576 | tf_op jit(solution)/shard_map/while/body/all_to_all | solution.py:27
  235.2 11.7 %all_to_all.196 = bf16[8,16,16,128]{3,1,2,0:T(8,128)(2,1)S(1)} all-to-all(bf16[8,16,16,128]{3,1,2,0:T(8,128)(2,1)S(1)} %copy.476), channel_id=1, replica_groups=mesh['s'=4,'t'=4,'x'=2] {'s','x'}, dimensions={0} | all-to-all | bytes 1048576 | tf_op jit(solution)/shard_map/while/body/all_to_all | solution.py:27
  252.3 9.2 %all-to-all-done.7 = bf16[8,16,16,128]{3,1,2,0:T(8,128)(2,1)S(1)} async-done(((bf16[8,16,16,128]{3,1,2,0:T(8,128)(2,1)}), bf16[8,16,16,128]{3,1,2,0:T(8,128)(2,1)S(1)}, u32[]{:S(2)}, u32[]{:S(2)}) %all-to-all-start.7) | async-done | bytes 524320 | tf_op jit(solution)/shard_map/while/body/all_to_all | solution.py:27
  267.8 52.8 %while.134 = (s32[]{:T(128)}, bf16[16,128,128]{2,1,0:T(8,128)(2,1)S(1)}, bf16[16,128,128]{2,0,1:T(8,128)(2,1)}, bf16[16,128,128]{2,1,0:T(8,128)(2,1)}, bf16[16,1...) while((s32[]{:T(128)}, ...), condition=%wide.region_7.8_spmd, body=%wide.region_6.7_spmd.sunk | while | flops 274726912 | bytes 35127496 | solution.py:179
  268.4 11.7 %all_to_all.197 = bf16[8,16,16,128]{3,1,2,0:T(8,128)(2,1)S(1)} all-to-all(bf16[8,16,16,128]{3,1,2,0:T(8,128)(2,1)S(1)} %copy.482), channel_id=1, replica_groups=mesh['s'=4,'t'=4,'x'=2] {'s','x'}, dimensions={0} | all-to-all | bytes 1048576 | tf_op jit(solution)/shard_map/while/body/all_to_all | solution.py:27
  281.2 11.7 %all_to_all.198 = bf16[8,16,16,128]{3,1,2,0:T(8,128)(2,1)S(1)} all-to-all(bf16[8,16,16,128]{3,1,2,0:T(8,128)(2,1)S(1)} %copy.483), channel_id=1, replica_groups=mesh['s'=4,'t'=4,'x'=2] {'s','x'}, dimensions={0} | all-to-all | bytes 1048576 | tf_op jit(solution)/shard_map/while/body/all_to_all | solution.py:27
  293.8 11.7 %all_to_all.199 = bf16[8,16,16,128]{3,1,2,0:T(8,128)(2,1)S(1)} all-to-all(bf16[8,16,16,128]{3,1,2,0:T(8,128)(2,1)S(1)} %copy.484), channel_id=1, replica_groups=mesh['s'=4,'t'=4,'x'=2] {'s','x'}, dimensions={0} | all-to-all | bytes 1048576 | tf_op jit(solution)/shard_map/while/body/all_to_all | solution.py:27
  310.9 9.2 %all-to-all-done.11 = bf16[8,16,16,128]{3,1,2,0:T(8,128)(2,1)S(1)} async-done(((bf16[8,16,16,128]{3,1,2,0:T(8,128)(2,1)}), bf16[8,16,16,128]{3,1,2,0:T(8,128)(2,1)S(1)}, u32[]{:S(2)}, u32[]{:S(2)}) %all-to-all-start.11) | async-done | bytes 524320 | tf_op jit(solution)/shard_map/while/body/all_to_all | solution.py:27
  327.4 53.5 %while.135 = (s32[]{:T(128)}, bf16[16,128,128]{2,1,0:T(8,128)(2,1)S(1)}, bf16[16,128,128]{2,0,1:T(8,128)(2,1)}, bf16[16,128,128]{2,1,0:T(8,128)(2,1)}, bf16[16,1...) while((s32[]{:T(128)}, ...), condition=%wide.region_9.10_spmd, body=%wide.region_8.9_spmd.sunk | while | flops 274726912 | bytes 35127496 | solution.py:179
  329.7 11.7 %all_to_all.200 = bf16[8,16,16,128]{3,1,2,0:T(8,128)(2,1)S(1)} all-to-all(bf16[8,16,16,128]{3,1,2,0:T(8,128)(2,1)S(1)} %copy.490), channel_id=1, replica_groups=mesh['s'=4,'t'=4,'x'=2] {'s','x'}, dimensions={0} | all-to-all | bytes 1048576 | tf_op jit(solution)/shard_map/while/body/all_to_all | solution.py:27
  342.0 11.7 %all_to_all.201 = bf16[8,16,16,128]{3,1,2,0:T(8,128)(2,1)S(1)} all-to-all(bf16[8,16,16,128]{3,1,2,0:T(8,128)(2,1)S(1)} %copy.491), channel_id=1, replica_groups=mesh['s'=4,'t'=4,'x'=2] {'s','x'}, dimensions={0} | all-to-all | bytes 1048576 | tf_op jit(solution)/shard_map/while/body/all_to_all | solution.py:27
  354.6 11.7 %all_to_all.202 = bf16[8,16,16,128]{3,1,2,0:T(8,128)(2,1)S(1)} all-to-all(bf16[8,16,16,128]{3,1,2,0:T(8,128)(2,1)S(1)} %copy.492), channel_id=1, replica_groups=mesh['s'=4,'t'=4,'x'=2] {'s','x'}, dimensions={0} | all-to-all | bytes 1048576 | tf_op jit(solution)/shard_map/while/body/all_to_all | solution.py:27
  371.2 9.2 %all-to-all-done.15 = bf16[8,16,16,128]{3,1,2,0:T(8,128)(2,1)S(1)} async-done(((bf16[8,16,16,128]{3,1,2,0:T(8,128)(2,1)}), bf16[8,16,16,128]{3,1,2,0:T(8,128)(2,1)S(1)}, u32[]{:S(2)}, u32[]{:S(2)}) %all-to-all-start.15) | async-done | bytes 524320 | tf_op jit(solution)/shard_map/while/body/all_to_all | solution.py:27
  406.0 65.6 %while.136 = (s32[]{:T(128)}, bf16[16,128,128]{2,1,0:T(8,128)(2,1)S(1)}, bf16[4,4,4,128,128]{3,4,2,0,1:T(8,128)(2,1)}, s32[]{:T(128)}, bf16[4,2,2,4,128,128]{5,4...) while((s32[]{:T(128)}, ...), condition=%wide.region_11.12_spmd, body=%wide.region_10.11_spmd.sunk | while | flops 551026688 | bytes 54002056 | solution.py:203
  407.6 8.4 %all-to-all-start.16 = ((bf16[8,16,16,128]{3,2,1,0:T(8,128)(2,1)}), bf16[8,16,16,128]{3,2,1,0:T(8,128)(2,1)S(1)}, u32[]{:S(2)}, u32[]{:S(2)}) async-start(bf16[8,16,16,128]{3,2,1,0:T(8,128)(2,1)} %bitcast.1138), calls=%async_computation.16 | async-start | bytes 1048576 | tf_op jit(solution)/shard_map/while/body/all_to_all | solution.py:27
  418.6 6.6 all-to-all-done.16
  427.3 11.7 %all_to_all.203 = bf16[8,16,16,128]{3,1,2,0:T(8,128)(2,1)S(1)} all-to-all(bf16[8,16,16,128]{3,1,2,0:T(8,128)(2,1)S(1)} %copy.496), channel_id=1, replica_groups=mesh['s'=4,'t'=4,'x'=2] {'s','x'}, dimensions={0} | all-to-all | bytes 1048576 | tf_op jit(solution)/shard_map/while/body/all_to_all | solution.py:27
  477.6 60.3 %while.137 = (s32[]{:T(128)}, bf16[16,128,128]{2,1,0:T(8,128)(2,1)S(1)}, bf16[4,4,4,128,128]{3,4,2,0,1:T(8,128)(2,1)}, s32[]{:T(128)}, bf16[4,2,2,4,128,128]{5,4...) while((s32[]{:T(128)}, ...), condition=%wide.region_13.14_spmd, body=%wide.region_12.13_spmd.sunk | while | flops 551026688 | bytes 54002056 | solution.py:203
  485.1 6.4 all-to-all-done.20
  493.6 11.7 %all_to_all.204 = bf16[8,16,16,128]{3,1,2,0:T(8,128)(2,1)S(1)} all-to-all(bf16[8,16,16,128]{3,1,2,0:T(8,128)(2,1)S(1)} %copy.506), channel_id=1, replica_groups=mesh['s'=4,'t'=4,'x'=2] {'s','x'}, dimensions={0} | all-to-all | bytes 1048576 | tf_op jit(solution)/shard_map/while/body/all_to_all | solution.py:27
  514.5 4.8 all-to-all-done.22
  546.9 60.4 %while.138 = (s32[]{:T(128)}, bf16[16,128,128]{2,1,0:T(8,128)(2,1)S(1)}, bf16[4,4,4,128,128]{3,4,2,0,1:T(8,128)(2,1)}, s32[]{:T(128)}, bf16[4,2,2,4,128,128]{5,4...) while((s32[]{:T(128)}, ...), condition=%wide.region_15.16_spmd, body=%wide.region_14.15_spmd.sunk | while | flops 551026688 | bytes 54002056 | solution.py:203
  554.5 6.5 all-to-all-done.24
  563.1 11.7 %all_to_all.205 = bf16[8,16,16,128]{3,1,2,0:T(8,128)(2,1)S(1)} all-to-all(bf16[8,16,16,128]{3,1,2,0:T(8,128)(2,1)S(1)} %copy.516), channel_id=1, replica_groups=mesh['s'=4,'t'=4,'x'=2] {'s','x'}, dimensions={0} | all-to-all | bytes 1048576 | tf_op jit(solution)/shard_map/while/body/all_to_all | solution.py:27
  615.8 60.4 %while.139 = (s32[]{:T(128)}, bf16[16,128,128]{2,1,0:T(8,128)(2,1)S(1)}, bf16[4,4,4,128,128]{3,4,2,0,1:T(8,128)(2,1)}, s32[]{:T(128)}, bf16[4,1,2,4,128,128]{5,4...) while((s32[]{:T(128)}, ...), condition=%wide.region_18.19_spmd, body=%wide.region_17.18_spmd.sunk | while | flops 551026688 | bytes 54002064 | solution.py:203
  623.4 6.5 all-to-all-done.28
  632.0 11.7 %all_to_all.206 = bf16[8,16,16,128]{3,1,2,0:T(8,128)(2,1)S(1)} all-to-all(bf16[8,16,16,128]{3,1,2,0:T(8,128)(2,1)S(1)} %copy.526), channel_id=1, replica_groups=mesh['s'=4,'t'=4,'x'=2] {'s','x'}, dimensions={0} | all-to-all | bytes 1048576 | tf_op jit(solution)/shard_map/while/body/all_to_all | solution.py:27
  652.8 4.8 all-to-all-done.30
  690.7 5.6 collective-permute-done.18
  702.7 17.0 %collective-permute-start.32 = (bf16[2,4,128,128]{3,2,1,0:T(8,128)(2,1)S(1)}, bf16[2,4,128,128]{3,2,1,0:T(8,128)(2,1)S(1)}, u32[]{:S(2)}, u32[]{:S(2)}) collective-permute-start(bf16[2,4,128,128]{3,2,1,0:T(8,128)(2,1)S(1)} %pad_maximum_fusion.37), channel_id=1, source_target_pairs={{0,16},{8,24},{16,0},{24,8},{1,17},{9,25},{17,1},{25,9},{2,18},{10... | collective-permute-start | bytes 786440 | tf_op jit(solution)/shard_map/ppermute | solution.py:108
  720.4 9.2 %collective-permute-done.32 = bf16[2,4,128,128]{3,2,1,0:T(8,128)(2,1)S(1)} collective-permute-done((bf16[2,4,128,128]{3,2,1,0:T(8,128)(2,1)S(1)}, bf16[2,4,128,128]{3,2,1,0:T(8,128)(2,1)S(1)}, u32[]{:S(2)}, u32[]{:S(2)}) %collective-permute-start.32) | collective-permute-done | bytes 262176 | tf_op jit(solution)/shard_map/ppermute | solution.py:108
  737.4 5.6 collective-permute-start.30
  750.8 5.6 collective-permute-done.29
  (551 shorter events, 352.7 us)
Async XLA Ops:
  7.2 166.5 %all-gather.9.cloned.1.call-start = ((), (), s32[]{:S(2)}) async-start(), calls=%async_computation.40 | async-start | bytes 1310720 | tf_op jit(solution)/shard_map/all_gather | solution.py:116
  11.9 12.3 %collective-permute-start.5 = (bf16[2,4,128,128]{2,3,1,0:T(8,128)(2,1)S(1)}, bf16[2,4,128,128]{2,3,1,0:T(8,128)(2,1)}, u32[]{:S(2)}, u32[]{:S(2)}) collective-permute-start(bf16[2,4,128,128]{2,3,1,0:T(8,128)(2,1)S(1)} %pad_maximum_fusion.28), channel_id=1, source_target_pairs={{0,16},{8,24},{16,0},{24,8},{1,17},{9,25},{17,1},{25,9},{2,18},{10... | collective-permute-start | bytes 786440 | tf_op jit(solution)/shard_map/ppermute | solution.py:108
  27.3 176.1 %all-gather.11.cloned.1.call-start = ((), (), s32[]{:S(2)}) async-start(), calls=%async_computation.41 | async-start | bytes 2621440 | tf_op jit(solution)/shard_map/all_gather | solution.py:116
  29.1 232.9 %all-gather.13.cloned.1.call-start = ((), (), s32[]{:S(2)}) async-start(), calls=%async_computation.42 | async-start | bytes 2621440 | tf_op jit(solution)/shard_map/all_gather | solution.py:116
  31.3 32.7 %collective-permute-start.2 = (bf16[4,128,128]{2,1,0:T(8,128)(2,1)S(1)}, bf16[4,128,128]{2,1,0:T(8,128)(2,1)S(1)}, u32[]{:S(2)}, u32[]{:S(2)}) collective-permute-start(bf16[4,128,128]{2,1,0:T(8,128)(2,1)S(1)} %get-tuple-element.973), channel_id=1, source_target_pairs={{0,16},{2,24},{4,0},{6,8},{8,18},{10,26},{12,2},{14,10},{16,20},{1... | collective-permute-start | bytes 393224 | tf_op jit(solution)/shard_map/ppermute | solution.py:76
  33.9 30.1 %collective-permute-start.1 = (bf16[4,128,128]{2,1,0:T(8,128)(2,1)S(1)}, bf16[4,128,128]{2,1,0:T(8,128)(2,1)S(1)}, u32[]{:S(2)}, u32[]{:S(2)}) collective-permute-start(bf16[4,128,128]{2,1,0:T(8,128)(2,1)S(1)} %get-tuple-element.974), channel_id=1, source_target_pairs={{0,8},{2,0},{4,24},{6,16},{8,10},{10,2},{12,26},{14,18},{16,12},{1... | collective-permute-start | bytes 393224 | tf_op jit(solution)/shard_map/ppermute | solution.py:76
  34.3 29.7 %collective-permute-start = (bf16[4,128,128]{2,1,0:T(8,128)(2,1)S(1)}, bf16[4,128,128]{2,1,0:T(8,128)(2,1)S(1)}, u32[]{:S(2)}, u32[]{:S(2)}) collective-permute-start(bf16[4,128,128]{2,1,0:T(8,128)(2,1)S(1)} %get-tuple-element.971), channel_id=1, source_target_pairs={{0,0},{2,8},{4,16},{6,24},{8,2},{10,10},{12,18},{14,26},{16,4},{18... | collective-permute-start | bytes 393224 | tf_op jit(solution)/shard_map/ppermute | solution.py:76
  65.1 11.8 %collective-permute-start.15 = (bf16[2,4,128,128]{2,3,1,0:T(8,128)(2,1)S(1)}, bf16[2,4,128,128]{2,3,1,0:T(8,128)(2,1)S(1)}, u32[]{:S(2)}, u32[]{:S(2)}) collective-permute-start(bf16[2,4,128,128]{2,3,1,0:T(8,128)(2,1)S(1)} %pad_maximum_fusion.32), channel_id=1, source_target_pairs={{0,24},{8,16},{16,8},{24,0},{1,25},{9,17},{17,9},{25,1},{2,26},{10... | collective-permute-start | bytes 786440 | tf_op jit(solution)/shard_map/ppermute | solution.py:108
  71.9 13.7 %collective-permute-start.14 = (bf16[2,4,128,128]{2,3,1,0:T(8,128)(2,1)S(1)}, bf16[2,4,128,128]{2,3,1,0:T(8,128)(2,1)S(1)}, u32[]{:S(2)}, u32[]{:S(2)}) collective-permute-start(bf16[2,4,128,128]{2,3,1,0:T(8,128)(2,1)S(1)} %pad_maximum_fusion.31), channel_id=1, source_target_pairs={{0,16},{8,24},{16,0},{24,8},{1,17},{9,25},{17,1},{25,9},{2,18},{10... | collective-permute-start | bytes 786440 | tf_op jit(solution)/shard_map/ppermute | solution.py:108
  87.6 233.0 %all-gather.15.cloned.1.call-start = ((), (), s32[]{:S(2)}) async-start(), calls=%async_computation.43 | async-start | bytes 2621440 | tf_op jit(solution)/shard_map/all_gather | solution.py:116
  92.2 30.7 %collective-permute-start.11 = (bf16[4,128,128]{2,1,0:T(8,128)(2,1)S(1)}, bf16[4,128,128]{2,1,0:T(8,128)(2,1)S(1)}, u32[]{:S(2)}, u32[]{:S(2)}) collective-permute-start(bf16[4,128,128]{2,1,0:T(8,128)(2,1)S(1)} %get-tuple-element.977), channel_id=1, source_target_pairs={{0,4},{2,6},{4,0},{6,2},{1,5},{3,7},{5,1},{7,3},{8,12},{10,14},{12... | collective-permute-start | bytes 393224 | tf_op jit(solution)/shard_map/ppermute | solution.py:121
  92.2 30.7 %collective-permute-start.10 = (bf16[4,128,128]{2,1,0:T(8,128)(2,1)S(1)}, bf16[4,128,128]{2,1,0:T(8,128)(2,1)}, u32[]{:S(2)}, u32[]{:S(2)}) collective-permute-start(bf16[4,128,128]{2,1,0:T(8,128)(2,1)S(1)} %get-tuple-element.977), channel_id=1, source_target_pairs={{0,2},{2,0},{4,6},{6,4},{1,3},{3,1},{5,7},{7,5},{8,10},{10,8},{12,... | collective-permute-start | bytes 393224 | tf_op jit(solution)/shard_map/ppermute | solution.py:121
  92.8 31.1 %collective-permute-start.9 = (bf16[4,128,128]{2,1,0:T(8,128)(2,1)S(1)}, bf16[4,128,128]{2,1,0:T(8,128)(2,1)S(1)}, u32[]{:S(2)}, u32[]{:S(2)}) collective-permute-start(bf16[4,128,128]{2,1,0:T(8,128)(2,1)S(1)} %get-tuple-element.976), channel_id=1, source_target_pairs={{0,6},{2,4},{4,2},{6,0},{1,7},{3,5},{5,3},{7,1},{8,14},{10,12},{12... | collective-permute-start | bytes 393224 | tf_op jit(solution)/shard_map/ppermute | solution.py:121
  96.6 43.6 %collective-permute-start.8 = (bf16[4,128,128]{2,1,0:T(8,128)(2,1)S(1)}, bf16[4,128,128]{2,1,0:T(8,128)(2,1)}, u32[]{:S(2)}, u32[]{:S(2)}) collective-permute-start(bf16[4,128,128]{2,1,0:T(8,128)(2,1)S(1)} %get-tuple-element.976), channel_id=1, source_target_pairs={{0,4},{2,6},{4,0},{6,2},{1,5},{3,7},{5,1},{7,3},{8,12},{10,14},{12... | collective-permute-start | bytes 393224 | tf_op jit(solution)/shard_map/ppermute | solution.py:121
  99.3 40.9 %collective-permute-start.7 = (bf16[4,128,128]{2,1,0:T(8,128)(2,1)S(1)}, bf16[4,128,128]{2,1,0:T(8,128)(2,1)S(1)}, u32[]{:S(2)}, u32[]{:S(2)}) collective-permute-start(bf16[4,128,128]{2,1,0:T(8,128)(2,1)S(1)} %get-tuple-element.976), channel_id=1, source_target_pairs={{0,2},{2,0},{4,6},{6,4},{1,3},{3,1},{5,7},{7,5},{8,10},{10,8},{12,... | collective-permute-start | bytes 393224 | tf_op jit(solution)/shard_map/ppermute | solution.py:121
  144.9 397.3 %reduce-scatter.5.cloned.1.call-start = ((), (), s32[]{:S(2)}) async-start(), calls=%async_computation.36 | async-start | bytes 2621440 | tf_op jit(solution)/shard_map/reduce_scatter | solution.py:132
  160.5 12.7 %all-to-all-start.1 = ((bf16[8,16,16,128]{3,1,2,0:T(8,128)(2,1)}), bf16[8,16,16,128]{3,1,2,0:T(8,128)(2,1)S(1)}, u32[]{:S(2)}, u32[]{:S(2)}) async-start(bf16[8,16,16,128]{3,1,2,0:T(8,128)(2,1)} %copy.465), calls=%async_computation.1 | async-start | bytes 1048576 | tf_op jit(solution)/shard_map/while/body/all_to_all | solution.py:27
  190.2 12.7 %all-to-all-start.3 = ((bf16[8,16,16,128]{3,1,2,0:T(8,128)(2,1)}), bf16[8,16,16,128]{3,1,2,0:T(8,128)(2,1)S(1)}, u32[]{:S(2)}, u32[]{:S(2)}) async-start(bf16[8,16,16,128]{3,1,2,0:T(8,128)(2,1)} %copy.469), calls=%async_computation.3 | async-start | bytes 1048576 | tf_op jit(solution)/shard_map/while/body/all_to_all | solution.py:27
  248.8 12.7 %all-to-all-start.7 = ((bf16[8,16,16,128]{3,1,2,0:T(8,128)(2,1)}), bf16[8,16,16,128]{3,1,2,0:T(8,128)(2,1)S(1)}, u32[]{:S(2)}, u32[]{:S(2)}) async-start(bf16[8,16,16,128]{3,1,2,0:T(8,128)(2,1)} %copy.477), calls=%async_computation.7 | async-start | bytes 1048576 | tf_op jit(solution)/shard_map/while/body/all_to_all | solution.py:27
  307.4 12.7 %all-to-all-start.11 = ((bf16[8,16,16,128]{3,1,2,0:T(8,128)(2,1)}), bf16[8,16,16,128]{3,1,2,0:T(8,128)(2,1)S(1)}, u32[]{:S(2)}, u32[]{:S(2)}) async-start(bf16[8,16,16,128]{3,1,2,0:T(8,128)(2,1)} %copy.485), calls=%async_computation.11 | async-start | bytes 1048576 | tf_op jit(solution)/shard_map/while/body/all_to_all | solution.py:27
  367.7 12.7 %all-to-all-start.15 = ((bf16[8,16,16,128]{3,1,2,0:T(8,128)(2,1)}), bf16[8,16,16,128]{3,1,2,0:T(8,128)(2,1)S(1)}, u32[]{:S(2)}, u32[]{:S(2)}) async-start(bf16[8,16,16,128]{3,1,2,0:T(8,128)(2,1)} %copy.493), calls=%async_computation.15 | async-start | bytes 1048576 | tf_op jit(solution)/shard_map/while/body/all_to_all | solution.py:27
  384.7 16.4 %collective-permute-start.23 = (bf16[4,128,128]{1,2,0:T(8,128)(2,1)}, bf16[4,128,128]{1,2,0:T(8,128)(2,1)}, u32[]{:S(2)}, u32[]{:S(2)}) collective-permute-start(bf16[4,128,128]{1,2,0:T(8,128)(2,1)} %bitcast.1469), channel_id=1, source_target_pairs={{0,24},{2,16},{4,8},{6,0},{8,26},{10,18},{12,10},{14,2},{16,28},{1... | collective-permute-start | bytes 393224 | tf_op jit(solution)/shard_map/ppermute | solution.py:76
  385.9 16.3 %collective-permute-start.22 = (bf16[4,128,128]{1,2,0:T(8,128)(2,1)}, bf16[4,128,128]{1,2,0:T(8,128)(2,1)}, u32[]{:S(2)}, u32[]{:S(2)}) collective-permute-start(bf16[4,128,128]{1,2,0:T(8,128)(2,1)} %bitcast.1470), channel_id=1, source_target_pairs={{0,16},{2,24},{4,0},{6,8},{8,18},{10,26},{12,2},{14,10},{16,20},{1... | collective-permute-start | bytes 393224 | tf_op jit(solution)/shard_map/ppermute | solution.py:76
  386.1 16.1 %collective-permute-start.21 = (bf16[4,128,128]{1,2,0:T(8,128)(2,1)S(1)}, bf16[4,128,128]{1,2,0:T(8,128)(2,1)}, u32[]{:S(2)}, u32[]{:S(2)}) collective-permute-start(bf16[4,128,128]{1,2,0:T(8,128)(2,1)S(1)} %bitcast.1471), channel_id=1, source_target_pairs={{0,8},{2,0},{4,24},{6,16},{8,10},{10,2},{12,26},{14,18},{16,12},{1... | collective-permute-start | bytes 393224 | tf_op jit(solution)/shard_map/ppermute | solution.py:76
  386.3 15.9 %collective-permute-start.20 = (bf16[4,128,128]{1,2,0:T(8,128)(2,1)S(1)}, bf16[4,128,128]{1,2,0:T(8,128)(2,1)S(1)}, u32[]{:S(2)}, u32[]{:S(2)}) collective-permute-start(bf16[4,128,128]{1,2,0:T(8,128)(2,1)S(1)} %bitcast.1472), channel_id=1, source_target_pairs={{0,0},{2,8},{4,16},{6,24},{8,2},{10,10},{12,18},{14,26},{16,4},{18... | collective-permute-start | bytes 393224 | tf_op jit(solution)/shard_map/ppermute | solution.py:76
  407.6 17.6 %all-to-all-start.16 = ((bf16[8,16,16,128]{3,2,1,0:T(8,128)(2,1)}), bf16[8,16,16,128]{3,2,1,0:T(8,128)(2,1)S(1)}, u32[]{:S(2)}, u32[]{:S(2)}) async-start(bf16[8,16,16,128]{3,2,1,0:T(8,128)(2,1)} %bitcast.1138), calls=%async_computation.16 | async-start | bytes 1048576 | tf_op jit(solution)/shard_map/while/body/all_to_all | solution.py:27
  440.2 12.7 %all-to-all-start.18 = ((bf16[8,16,16,128]{3,1,2,0:T(8,128)(2,1)}), bf16[8,16,16,128]{3,1,2,0:T(8,128)(2,1)S(1)}, u32[]{:S(2)}, u32[]{:S(2)}) async-start(bf16[8,16,16,128]{3,1,2,0:T(8,128)(2,1)} %copy.498), calls=%async_computation.18 | async-start | bytes 1048576 | tf_op jit(solution)/shard_map/while/body/all_to_all | solution.py:27
  456.0 12.7 %all-to-all-start.19 = ((bf16[8,16,16,128]{3,2,1,0:T(8,128)(2,1)}), bf16[8,16,16,128]{3,2,1,0:T(8,128)(2,1)S(1)}, u32[]{:S(2)}, u32[]{:S(2)}) async-start(bf16[8,16,16,128]{3,2,1,0:T(8,128)(2,1)} %copy.500), calls=%async_computation.19 | async-start | bytes 1048576 | tf_op jit(solution)/shard_map/while/body/all_to_all | solution.py:27
  475.7 131.6 %reduce-scatter.7.cloned.1.call-start = ((), (), s32[]{:S(2)}) async-start(), calls=%async_computation.37 | async-start | bytes 2621440 | tf_op jit(solution)/shard_map/reduce_scatter | solution.py:132
  478.9 12.7 %all-to-all-start.20 = ((bf16[8,16,16,128]{3,2,1,0:T(8,128)(2,1)}), bf16[8,16,16,128]{3,2,1,0:T(8,128)(2,1)S(1)}, u32[]{:S(2)}, u32[]{:S(2)}) async-start(bf16[8,16,16,128]{3,2,1,0:T(8,128)(2,1)} %bitcast.1178), calls=%async_computation.20 | async-start | bytes 1048576 | tf_op jit(solution)/shard_map/while/body/all_to_all | solution.py:27
  506.6 12.7 %all-to-all-start.22 = ((bf16[8,16,16,128]{3,1,2,0:T(8,128)(2,1)}), bf16[8,16,16,128]{3,1,2,0:T(8,128)(2,1)S(1)}, u32[]{:S(2)}, u32[]{:S(2)}) async-start(bf16[8,16,16,128]{3,1,2,0:T(8,128)(2,1)} %copy.508), calls=%async_computation.22 | async-start | bytes 1048576 | tf_op jit(solution)/shard_map/while/body/all_to_all | solution.py:27
  522.4 12.7 %all-to-all-start.23 = ((bf16[8,16,16,128]{3,2,1,0:T(8,128)(2,1)}), bf16[8,16,16,128]{3,2,1,0:T(8,128)(2,1)S(1)}, u32[]{:S(2)}, u32[]{:S(2)}) async-start(bf16[8,16,16,128]{3,2,1,0:T(8,128)(2,1)} %copy.510), calls=%async_computation.23 | async-start | bytes 1048576 | tf_op jit(solution)/shard_map/while/body/all_to_all | solution.py:27
  542.1 187.7 %reduce-scatter.9.cloned.1.call-start = ((), (), s32[]{:S(2)}) async-start(), calls=%async_computation.38 | async-start | bytes 2621440 | tf_op jit(solution)/shard_map/reduce_scatter | solution.py:132
  548.3 12.7 %all-to-all-start.24 = ((bf16[8,16,16,128]{3,2,1,0:T(8,128)(2,1)}), bf16[8,16,16,128]{3,2,1,0:T(8,128)(2,1)S(1)}, u32[]{:S(2)}, u32[]{:S(2)}) async-start(bf16[8,16,16,128]{3,2,1,0:T(8,128)(2,1)} %bitcast.1218), calls=%async_computation.24 | async-start | bytes 1048576 | tf_op jit(solution)/shard_map/while/body/all_to_all | solution.py:27
  576.0 12.7 %all-to-all-start.26 = ((bf16[8,16,16,128]{3,1,2,0:T(8,128)(2,1)}), bf16[8,16,16,128]{3,1,2,0:T(8,128)(2,1)S(1)}, u32[]{:S(2)}, u32[]{:S(2)}) async-start(bf16[8,16,16,128]{3,1,2,0:T(8,128)(2,1)} %copy.518), calls=%async_computation.26 | async-start | bytes 1048576 | tf_op jit(solution)/shard_map/while/body/all_to_all | solution.py:27
  591.8 12.7 %all-to-all-start.27 = ((bf16[8,16,16,128]{3,2,1,0:T(8,128)(2,1)}), bf16[8,16,16,128]{3,2,1,0:T(8,128)(2,1)S(1)}, u32[]{:S(2)}, u32[]{:S(2)}) async-start(bf16[8,16,16,128]{3,2,1,0:T(8,128)(2,1)} %copy.520), calls=%async_computation.27 | async-start | bytes 1048576 | tf_op jit(solution)/shard_map/while/body/all_to_all | solution.py:27
  614.0 121.4 %reduce-scatter.11.cloned.1.call-start = ((), (), s32[]{:S(2)}) async-start(), calls=%async_computation.39 | async-start | bytes 2621440 | tf_op jit(solution)/shard_map/reduce_scatter | solution.py:132
  617.2 12.7 %all-to-all-start.28 = ((bf16[8,16,16,128]{3,2,1,0:T(8,128)(2,1)}), bf16[8,16,16,128]{3,2,1,0:T(8,128)(2,1)S(1)}, u32[]{:S(2)}, u32[]{:S(2)}) async-start(bf16[8,16,16,128]{3,2,1,0:T(8,128)(2,1)} %bitcast.1258), calls=%async_computation.28 | async-start | bytes 1048576 | tf_op jit(solution)/shard_map/while/body/all_to_all | solution.py:27
  645.0 12.7 %all-to-all-start.30 = ((bf16[8,16,16,128]{3,1,2,0:T(8,128)(2,1)}), bf16[8,16,16,128]{3,1,2,0:T(8,128)(2,1)S(1)}, u32[]{:S(2)}, u32[]{:S(2)}) async-start(bf16[8,16,16,128]{3,1,2,0:T(8,128)(2,1)} %copy.528), calls=%async_computation.30 | async-start | bytes 1048576 | tf_op jit(solution)/shard_map/while/body/all_to_all | solution.py:27
  660.8 12.7 %all-to-all-start.31 = ((bf16[8,16,16,128]{3,2,1,0:T(8,128)(2,1)}), bf16[8,16,16,128]{3,2,1,0:T(8,128)(2,1)S(1)}, u32[]{:S(2)}, u32[]{:S(2)}) async-start(bf16[8,16,16,128]{3,2,1,0:T(8,128)(2,1)} %copy.530), calls=%async_computation.31 | async-start | bytes 1048576 | tf_op jit(solution)/shard_map/while/body/all_to_all | solution.py:27
  685.4 15.7 %collective-permute-start.17 = (bf16[4,128,128]{2,1,0:T(8,128)(2,1)S(1)}, bf16[4,128,128]{2,1,0:T(8,128)(2,1)S(1)}, u32[]{:S(2)}, u32[]{:S(2)}) collective-permute-start(bf16[4,128,128]{2,1,0:T(8,128)(2,1)S(1)} %bitcast.1475), channel_id=1, source_target_pairs={{0,2},{2,10},{4,18},{6,26},{8,0},{10,8},{12,16},{14,24},{16,6},{18... | collective-permute-start | bytes 393224 | tf_op jit(solution)/shard_map/ppermute | solution.py:76
  685.6 15.4 %collective-permute-start.16 = (bf16[4,128,128]{2,1,0:T(8,128)(2,1)S(1)}, bf16[4,128,128]{2,1,0:T(8,128)(2,1)S(1)}, u32[]{:S(2)}, u32[]{:S(2)}) collective-permute-start(bf16[4,128,128]{2,1,0:T(8,128)(2,1)S(1)} %bitcast.1476), channel_id=1, source_target_pairs={{0,0},{2,8},{4,16},{6,24},{8,2},{10,10},{12,18},{14,26},{16,4},{18... | collective-permute-start | bytes 393224 | tf_op jit(solution)/shard_map/ppermute | solution.py:76
  701.9 18.6 %collective-permute-start.33 = (bf16[2,4,128,128]{3,2,1,0:T(8,128)(2,1)S(1)}, bf16[2,4,128,128]{3,2,1,0:T(8,128)(2,1)S(1)}, u32[]{:S(2)}, u32[]{:S(2)}) collective-permute-start(bf16[2,4,128,128]{3,2,1,0:T(8,128)(2,1)S(1)} %pad_maximum_fusion.38), channel_id=1, source_target_pairs={{0,24},{8,16},{16,8},{24,0},{1,25},{9,17},{17,9},{25,1},{2,26},{10... | collective-permute-start | bytes 786440 | tf_op jit(solution)/shard_map/ppermute | solution.py:108
  702.7 26.9 %collective-permute-start.32 = (bf16[2,4,128,128]{3,2,1,0:T(8,128)(2,1)S(1)}, bf16[2,4,128,128]{3,2,1,0:T(8,128)(2,1)S(1)}, u32[]{:S(2)}, u32[]{:S(2)}) collective-permute-start(bf16[2,4,128,128]{3,2,1,0:T(8,128)(2,1)S(1)} %pad_maximum_fusion.37), channel_id=1, source_target_pairs={{0,16},{8,24},{16,0},{24,8},{1,17},{9,25},{17,1},{25,9},{2,18},{10... | collective-permute-start | bytes 786440 | tf_op jit(solution)/shard_map/ppermute | solution.py:108
  731.9 12.3 %collective-permute-start.26 = (bf16[4,128,128]{2,1,0:T(8,128)(2,1)S(1)}, bf16[4,128,128]{2,1,0:T(8,128)(2,1)S(1)}, u32[]{:S(2)}, u32[]{:S(2)}) collective-permute-start(bf16[4,128,128]{2,1,0:T(8,128)(2,1)S(1)} %bitcast.1466), channel_id=1, source_target_pairs={{0,4},{2,12},{4,20},{6,28},{8,6},{10,14},{12,22},{14,30},{16,0},{1... | collective-permute-start | bytes 393224 | tf_op jit(solution)/shard_map/ppermute | solution.py:76
  737.4 13.4 %collective-permute-start.30 = (bf16[2,4,128,128]{3,2,1,0:T(8,128)(2,1)S(1)}, bf16[2,4,128,128]{3,2,1,0:T(8,128)(2,1)S(1)}, u32[]{:S(2)}, u32[]{:S(2)}) collective-permute-start(bf16[2,4,128,128]{3,2,1,0:T(8,128)(2,1)S(1)} %pad_maximum_fusion.35), channel_id=1, source_target_pairs={{0,24},{8,16},{16,8},{24,0},{1,25},{9,17},{17,9},{25,1},{2,26},{10... | collective-permute-start | bytes 786440 | tf_op jit(solution)/shard_map/ppermute | solution.py:108
  743.1 13.3 %collective-permute-start.29 = (bf16[2,4,128,128]{3,2,1,0:T(8,128)(2,1)S(1)}, bf16[2,4,128,128]{3,2,1,0:T(8,128)(2,1)S(1)}, u32[]{:S(2)}, u32[]{:S(2)}) collective-permute-start(bf16[2,4,128,128]{3,2,1,0:T(8,128)(2,1)S(1)} %pad_maximum_fusion.34), channel_id=1, source_target_pairs={{0,16},{8,24},{16,0},{24,8},{1,17},{9,25},{17,1},{25,9},{2,18},{10... | collective-permute-start | bytes 786440 | tf_op jit(solution)/shard_map/ppermute | solution.py:108
  744.2 12.2 %collective-permute-start.28 = (bf16[2,4,128,128]{3,2,1,0:T(8,128)(2,1)S(1)}, bf16[2,4,128,128]{3,2,1,0:T(8,128)(2,1)S(1)}, u32[]{:S(2)}, u32[]{:S(2)}) collective-permute-start(bf16[2,4,128,128]{3,2,1,0:T(8,128)(2,1)S(1)} %pad_maximum_fusion.33), channel_id=1, source_target_pairs={{0,8},{8,0},{16,24},{24,16},{1,9},{9,1},{17,25},{25,17},{2,10},{10... | collective-permute-start | bytes 786440 | tf_op jit(solution)/shard_map/ppermute | solution.py:108
  (85 other events, 610.9 us)
Sparse Core Ops, SparseCore 0:
  27.4 44.6 all-gather.8
  74.2 68.4 all-gather.10
  144.3 44.6 all-gather.12
  191.0 44.6 all-gather.14
  475.8 42.5 reduce-scatter.4
  542.2 42.5 reduce-scatter.6
  614.1 42.5 reduce-scatter.8
  680.5 51.2 reduce-scatter.10

commit v16 on v15

--- a/solution.py
+++ b/solution.py
@@ -141,11 +141,9 @@
     current = arriving(inputs)
     current, parts[0] = lax.optimization_barrier((current, parts[0]))
     once = 1 + s_index // sections
-    parts[0], rights, lefts = lax.optimization_barrier((parts[0], rights[1:], lefts[1:]))
-    for loop in range(loops - 1):
-        parts.extend(ordered(part) for part in scattered(rights[loop], lefts[loop]))
     first = jnp.stack([gathered_directly(parts[0][f]) for f in range(2)], axis=1)[:, None]
     starts = [0, 1] + list(range(PAIRED, layers, PAIRED)) + [layers]
+    first, parts[1] = lax.optimization_barrier((first, parts[1]))
     ahead = gathered(jnp.stack(parts[1:2]))
     weights = {}
     stored = {}
@@ -171,6 +169,10 @@
         full = ahead if begin else first
         if begin:
             coming = range(end, min(end + PAIRED, layers))
+            if begin == PAIRED:
+                current, rights, lefts = lax.optimization_barrier((current, rights[1:], lefts[1:]))
+                for loop in range(loops - 1):
+                    parts.extend(ordered(part) for part in scattered(rights[loop], lefts[loop]))
             if coming:
                 ahead = gathered(jnp.stack([parts[layer] for layer in coming]))
         weights.update((layer, (full, layer - begin)) for layer in stretch)

time: 778 us -> 747 us (0.960)
  waiting for transfers between devices: 223 us -> 203 us
  starting transfers between devices: 136 us -> 124 us
    ppermute x16, waiting for transfers between devices: 45 us -> 23.3 us  [turned(): moved.append(lax.ppermute(pick(parts, send_by ^ mask), ('s', 't'), pairs))]
    ppermute x6, waiting for transfers between devices: 32.6 us -> 13 us  [around(): lax.ppermute(value_of(mask), 't', [(t, t ^ mask) for t in range(groups)])]
    all_gather x4, waiting for transfers between devices: 0.08 us -> 11.9 us  [gathered(): return lax.all_gather(part, 't', axis=0, tiled=False)]
    all_to_all x17, waiting for transfers between devices: 108 us -> 117 us  [exchange(): lax.all_to_all(pieces, WIDE, split_axis=0, concat_axis=0, tiled=True)]
  transfers between devices with their start and end apart: 59 -> 59, of which waited for: 32 -> 32; matrix products, arithmetic and copies ran while one was open for 21% -> 22% of each run, Pallas kernels for 0% -> 0%
where the time goes in v16:
time: 747 us; the launch traced here: 735 us
  waiting for transfers between devices  203 us (27%)
  blocking collectives  177 us (24%)
  starting transfers between devices  124 us (17%)
  local copies, waits for them, and re-layouts  124 us (17%)
  matrix products  62.8 us (8%)
  other arithmetic  26 us (3%)
  between operations  15.8 us (2%)
    all_to_all x15, blocking collectives, exchange(): lax.all_to_all(pieces, WIDE, split_axis=0, concat_axis=0, tiled=True)  177 us
    all_to_all x17, waiting for transfers between devices, exchange(): lax.all_to_all(pieces, WIDE, split_axis=0, concat_axis=0, tiled=True)  117 us
    all_to_all x17, starting transfers between devices, exchange(): lax.all_to_all(pieces, WIDE, split_axis=0, concat_axis=0, tiled=True)  64 us
    ppermute x12, waiting for transfers between devices, scattered(): moved.append(lax.ppermute(value, 's', pairs))  37.6 us
    ppermute x12, starting transfers between devices, scattered(): moved.append(lax.ppermute(value, 's', pairs))  32.7 us
    ppermute x16, waiting for transfers between devices, turned(): moved.append(lax.ppermute(pick(parts, send_by ^ mask), ('s', 't'), pairs))  23.3 us
    while x15, local copies, waits for them, and re-layouts, body(): grad, terms = lax.fori_loop(0, once, backward_pair(top), (grad, blank))  21.6 us
    another operation x15, local copies, waits for them, and re-layouts  17 us
  transfers between devices with their start and end apart: 59, of which 32 were waited for; matrix products, arithmetic and copies ran while one was open for 22% of the time, Pallas kernels for 0%

profile of v16, /device:TPU:0, one launch (start us, length us, event | category | flops | bytes accessed | tf_op | source)
XLA Modules:
  0.0 734.7 jit_solution(14303281613725197438)
XLA Ops:
  18.3 5.7 collective-permute-start.6
  31.6 7.7 %collective-permute-done.5 = bf16[2,4,128,128]{2,3,1,0:T(8,128)(2,1)S(1)} collective-permute-done((bf16[2,4,128,128]{2,3,1,0:T(8,128)(2,1)S(1)}, bf16[2,4,128,128]{2,3,1,0:T(8,128)(2,1)S(1)}, u32[]{:S(2)}, u32[]{:S(2)}) %collective-permute-start.5) | collective-permute-done | bytes 262176 | tf_op jit(solution)/shard_map/ppermute | solution.py:108
  51.7 7.9 %collective-permute-done.11 = bf16[4,128,128]{2,1,0:T(8,128)(2,1)S(1)} collective-permute-done((bf16[4,128,128]{2,1,0:T(8,128)(2,1)S(1)}, bf16[4,128,128]{2,1,0:T(8,128)(2,1)S(1)}, u32[]{:S(2)}, u32[]{:S(2)}) %collective-permute-start.11) | collective-permute-done | bytes 131104 | tf_op jit(solution)/shard_map/ppermute | solution.py:121
  71.1 27.8 %while.131 = (s32[]{:T(128)}, bf16[16,128,128]{2,1,0:T(8,128)(2,1)S(1)}, bf16[16,128,128]{2,0,1:T(8,128)(2,1)}, s32[]{:T(128)}, bf16[4,1,2,4,128,128]{4,5,3,0,2,1:T(8,128)(2,1)S(1)}, /*index=5*/s32[]{:T(128)}) while((s32[]{:T(128)}, bf16[16,128,128]{2,1,0:T(8,128)(2,1)S(1)}, bf16[16,128,128]{2,0,1:T(8,128)(2,1)}, s32[]{:T(128)}, ...), condition=%wide.region_1.2_spmd, body=%wide.region_0.1_spmd.sunk | while | flops 137363456 | bytes 16777344 | solution.py:181
  71.5 12.7 %all_to_all.192 = bf16[8,16,16,128]{3,1,2,0:T(8,128)(2,1)S(1)} all-to-all(bf16[8,16,16,128]{3,1,2,0:T(8,128)(2,1)S(1)} %copy.464), channel_id=1, replica_groups=mesh['s'=4,'t'=4,'x'=2] {'s','x'}, dimensions={0} | all-to-all | bytes 1048576 | tf_op jit(solution)/shard_map/while/body/all_to_all | solution.py:27
  89.2 9.2 %all-to-all-done.1 = bf16[8,16,16,128]{3,1,2,0:T(8,128)(2,1)S(1)} async-done(((bf16[8,16,16,128]{3,1,2,0:T(8,128)(2,1)}), bf16[8,16,16,128]{3,1,2,0:T(8,128)(2,1)S(1)}, u32[]{:S(2)}, u32[]{:S(2)}) %all-to-all-start.1) | async-done | bytes 524320 | tf_op jit(solution)/shard_map/while/body/all_to_all | solution.py:27
  101.6 26.8 %while.132 = (s32[]{:T(128)}, bf16[16,128,128]{2,1,0:T(8,128)(2,1)S(1)}, bf16[16,128,128]{2,0,1:T(8,128)(2,1)}, s32[]{:T(128)}, bf16[4,1,2,4,128,128]{4,5,3,0,2,1:T(8,128)(2,1)S(1)}, /*index=5*/s32[]{:T(128)}) while((s32[]{:T(128)}, bf16[16,128,128]{2,1,0:T(8,128)(2,1)S(1)}, bf16[16,128,128]{2,0,1:T(8,128)(2,1)}, s32[]{:T(128)}, ...), condition=%wide.region_3.4_spmd, body=%wide.region_2.3_spmd.sunk | while | flops 137363456 | bytes 16777344 | solution.py:181
  102.1 11.7 %all_to_all.193 = bf16[8,16,16,128]{3,1,2,0:T(8,128)(2,1)S(1)} all-to-all(bf16[8,16,16,128]{3,1,2,0:T(8,128)(2,1)S(1)} %copy.468), channel_id=1, replica_groups=mesh['s'=4,'t'=4,'x'=2] {'s','x'}, dimensions={0} | all-to-all | bytes 1048576 | tf_op jit(solution)/shard_map/while/body/all_to_all | solution.py:27
  118.7 9.2 %all-to-all-done.3 = bf16[8,16,16,128]{3,1,2,0:T(8,128)(2,1)S(1)} async-done(((bf16[8,16,16,128]{3,1,2,0:T(8,128)(2,1)}), bf16[8,16,16,128]{3,1,2,0:T(8,128)(2,1)S(1)}, u32[]{:S(2)}, u32[]{:S(2)}) %all-to-all-start.3) | async-done | bytes 524320 | tf_op jit(solution)/shard_map/while/body/all_to_all | solution.py:27
  128.4 11.9 %all-gather.11.cloned.1.call-done = bf16[8,2,4,128,128]{4,3,2,1,0:T(8,128)(2,1)} async-done(((bf16[2,2,4,128,128]{4,3,2,1,0:T(8,128)(2,1)}), bf16[8,2,4,128,128]{4,3,2,1,0:T(8,128)(2,1)}) %all-gather.11.cloned.1.call-update) | async-done | bytes 2097168 | tf_op jit(solution)/shard_map/all_gather | solution.py:116
  144.8 5.7 collective-permute-done.15
  150.5 5.6 collective-permute-done.14
  168.6 54.3 %while.133 = (s32[]{:T(128)}, bf16[16,128,128]{2,1,0:T(8,128)(2,1)S(1)}, bf16[16,128,128]{2,0,1:T(8,128)(2,1)}, bf16[16,128,128]{2,1,0:T(8,128)(2,1)}, bf16[16,1...) while((s32[]{:T(128)}, bf16[16,128,128]{2,1,0:T(8,128)(2,1)S(1)}, ...), condition=%wide.region_5.6_spmd, body=%wide.region_4.5_spmd.sunk | while | flops 274726912 | bytes 35127496 | solution.py:181
  170.7 12.7 %all_to_all.194 = bf16[8,16,16,128]{3,1,2,0:T(8,128)(2,1)S(1)} all-to-all(bf16[8,16,16,128]{3,1,2,0:T(8,128)(2,1)S(1)} %copy.474), channel_id=1, replica_groups=mesh['s'=4,'t'=4,'x'=2] {'s','x'}, dimensions={0} | all-to-all | bytes 1048576 | tf_op jit(solution)/shard_map/while/body/all_to_all | solution.py:27
  184.0 11.7 %all_to_all.195 = bf16[8,16,16,128]{3,1,2,0:T(8,128)(2,1)S(1)} all-to-all(bf16[8,16,16,128]{3,1,2,0:T(8,128)(2,1)S(1)} %copy.475), channel_id=1, replica_groups=mesh['s'=4,'t'=4,'x'=2] {'s','x'}, dimensions={0} | all-to-all | bytes 1048576 | tf_op jit(solution)/shard_map/while/body/all_to_all | solution.py:27
  196.6 11.7 %all_to_all.196 = bf16[8,16,16,128]{3,1,2,0:T(8,128)(2,1)S(1)} all-to-all(bf16[8,16,16,128]{3,1,2,0:T(8,128)(2,1)S(1)} %copy.476), channel_id=1, replica_groups=mesh['s'=4,'t'=4,'x'=2] {'s','x'}, dimensions={0} | all-to-all | bytes 1048576 | tf_op jit(solution)/shard_map/while/body/all_to_all | solution.py:27
  213.2 9.2 %all-to-all-done.7 = bf16[8,16,16,128]{3,1,2,0:T(8,128)(2,1)S(1)} async-done(((bf16[8,16,16,128]{3,1,2,0:T(8,128)(2,1)}), bf16[8,16,16,128]{3,1,2,0:T(8,128)(2,1)S(1)}, u32[]{:S(2)}, u32[]{:S(2)}) %all-to-all-start.7) | async-done | bytes 524320 | tf_op jit(solution)/shard_map/while/body/all_to_all | solution.py:27
  229.9 53.3 %while.134 = (s32[]{:T(128)}, bf16[16,128,128]{2,1,0:T(8,128)(2,1)S(1)}, bf16[16,128,128]{2,0,1:T(8,128)(2,1)}, bf16[16,128,128]{2,1,0:T(8,128)(2,1)}, bf16[16,1...) while((s32[]{:T(128)}, bf16[16,128,128]{2,1,0:T(8,128)(2,1)S(1)}, ...), condition=%wide.region_7.8_spmd, body=%wide.region_6.7_spmd.sunk | while | flops 274726912 | bytes 35127496 | solution.py:181
  231.9 11.7 %all_to_all.197 = bf16[8,16,16,128]{3,1,2,0:T(8,128)(2,1)S(1)} all-to-all(bf16[8,16,16,128]{3,1,2,0:T(8,128)(2,1)S(1)} %copy.482), channel_id=1, replica_groups=mesh['s'=4,'t'=4,'x'=2] {'s','x'}, dimensions={0} | all-to-all | bytes 1048576 | tf_op jit(solution)/shard_map/while/body/all_to_all | solution.py:27
  244.3 11.7 %all_to_all.198 = bf16[8,16,16,128]{3,1,2,0:T(8,128)(2,1)S(1)} all-to-all(bf16[8,16,16,128]{3,1,2,0:T(8,128)(2,1)S(1)} %copy.483), channel_id=1, replica_groups=mesh['s'=4,'t'=4,'x'=2] {'s','x'}, dimensions={0} | all-to-all | bytes 1048576 | tf_op jit(solution)/shard_map/while/body/all_to_all | solution.py:27
  256.8 11.7 %all_to_all.199 = bf16[8,16,16,128]{3,1,2,0:T(8,128)(2,1)S(1)} all-to-all(bf16[8,16,16,128]{3,1,2,0:T(8,128)(2,1)S(1)} %copy.484), channel_id=1, replica_groups=mesh['s'=4,'t'=4,'x'=2] {'s','x'}, dimensions={0} | all-to-all | bytes 1048576 | tf_op jit(solution)/shard_map/while/body/all_to_all | solution.py:27
  273.5 9.2 %all-to-all-done.11 = bf16[8,16,16,128]{3,1,2,0:T(8,128)(2,1)S(1)} async-done(((bf16[8,16,16,128]{3,1,2,0:T(8,128)(2,1)}), bf16[8,16,16,128]{3,1,2,0:T(8,128)(2,1)S(1)}, u32[]{:S(2)}, u32[]{:S(2)}) %all-to-all-start.11) | async-done | bytes 524320 | tf_op jit(solution)/shard_map/while/body/all_to_all | solution.py:27
  289.7 57.6 %while.135 = (s32[]{:T(128)}, bf16[16,128,128]{2,1,0:T(8,128)(2,1)}, bf16[16,128,128]{2,0,1:T(8,128)(2,1)}, bf16[16,128,128]{2,1,0:T(8,128)(2,1)}, bf16[16,128,1...) while((s32[]{:T(128)}, bf16[16,128,128]{2,1,0:T(8,128)(2,1)}, ...), condition=%wide.region_9.10_spmd, body=%wide.region_8.9_spmd.sunk | while | flops 274726912 | bytes 35127496 | solution.py:181
  291.6 11.7 %all_to_all.200 = bf16[8,16,16,128]{3,1,2,0:T(8,128)(2,1)S(1)} all-to-all(bf16[8,16,16,128]{3,1,2,0:T(8,128)(2,1)S(1)} %copy.490), channel_id=1, replica_groups=mesh['s'=4,'t'=4,'x'=2] {'s','x'}, dimensions={0} | all-to-all | bytes 1048576 | tf_op jit(solution)/shard_map/while/body/all_to_all | solution.py:27
  304.4 11.7 %all_to_all.201 = bf16[8,16,16,128]{3,1,2,0:T(8,128)(2,1)S(1)} all-to-all(bf16[8,16,16,128]{3,1,2,0:T(8,128)(2,1)S(1)} %copy.491), channel_id=1, replica_groups=mesh['s'=4,'t'=4,'x'=2] {'s','x'}, dimensions={0} | all-to-all | bytes 1048576 | tf_op jit(solution)/shard_map/while/body/all_to_all | solution.py:27
  317.9 11.7 %all_to_all.202 = bf16[8,16,16,128]{3,1,2,0:T(8,128)(2,1)S(1)} all-to-all(bf16[8,16,16,128]{3,1,2,0:T(8,128)(2,1)S(1)} %copy.492), channel_id=1, replica_groups=mesh['s'=4,'t'=4,'x'=2] {'s','x'}, dimensions={0} | all-to-all | bytes 1048576 | tf_op jit(solution)/shard_map/while/body/all_to_all | solution.py:27
  335.7 9.3 %all-to-all-done.15 = bf16[8,16,16,128]{3,1,2,0:T(8,128)(2,1)} async-done(((bf16[8,16,16,128]{3,1,2,0:T(8,128)(2,1)}), bf16[8,16,16,128]{3,1,2,0:T(8,128)(2,1)}, u32[]{:S(2)}, u32[]{:S(2)}) %all-to-all-start.15) | async-done | bytes 524320 | tf_op jit(solution)/shard_map/while/body/all_to_all | solution.py:27
  372.2 65.4 %while.136 = (s32[]{:T(128)}, bf16[16,128,128]{2,1,0:T(8,128)(2,1)S(1)}, bf16[4,4,4,128,128]{3,4,2,0,1:T(8,128)(2,1)}, s32[]{:T(128)}, bf16[4,2,2,4,128,128]{5,4...) while((s32[]{:T(128)}, ...), condition=%wide.region_11.12_spmd, body=%wide.region_10.11_spmd.sunk | while | flops 551026688 | bytes 51904876 | solution.py:205
  373.8 7.4 %all-to-all-start.16 = ((bf16[8,16,16,128]{3,2,1,0:T(8,128)(2,1)}), bf16[8,16,16,128]{3,2,1,0:T(8,128)(2,1)S(1)}, u32[]{:S(2)}, u32[]{:S(2)}) async-start(bf16[8,16,16,128]{3,2,1,0:T(8,128)(2,1)} %bitcast.1138), calls=%async_computation.16 | async-start | bytes 1048576 | tf_op jit(solution)/shard_map/while/body/all_to_all | solution.py:27
  384.0 6.6 all-to-all-done.16
  392.6 11.7 %all_to_all.203 = bf16[8,16,16,128]{3,1,2,0:T(8,128)(2,1)S(1)} all-to-all(bf16[8,16,16,128]{3,1,2,0:T(8,128)(2,1)S(1)} %copy.496), channel_id=1, replica_groups=mesh['s'=4,'t'=4,'x'=2] {'s','x'}, dimensions={0} | all-to-all | bytes 1048576 | tf_op jit(solution)/shard_map/while/body/all_to_all | solution.py:27
  428.0 6.1 all-to-all-done.19
  443.7 61.1 %while.137 = (s32[]{:T(128)}, bf16[16,128,128]{2,1,0:T(8,128)(2,1)S(1)}, bf16[4,4,4,128,128]{3,4,2,0,1:T(8,128)(2,1)}, s32[]{:T(128)}, bf16[4,2,2,4,128,128]{5,4...) while((s32[]{:T(128)}, ...), condition=%wide.region_13.14_spmd, body=%wide.region_12.13_spmd.sunk | while | flops 551026688 | bytes 51904876 | solution.py:205
  451.2 6.4 all-to-all-done.20
  459.8 11.7 %all_to_all.204 = bf16[8,16,16,128]{3,1,2,0:T(8,128)(2,1)S(1)} all-to-all(bf16[8,16,16,128]{3,1,2,0:T(8,128)(2,1)S(1)} %copy.506), channel_id=1, replica_groups=mesh['s'=4,'t'=4,'x'=2] {'s','x'}, dimensions={0} | all-to-all | bytes 1048576 | tf_op jit(solution)/shard_map/while/body/all_to_all | solution.py:27
  495.2 6.0 all-to-all-done.23
  513.9 61.2 %while.138 = (s32[]{:T(128)}, bf16[16,128,128]{2,1,0:T(8,128)(2,1)S(1)}, bf16[4,4,4,128,128]{3,4,2,0,1:T(8,128)(2,1)}, s32[]{:T(128)}, bf16[4,2,2,4,128,128]{5,4...) while((s32[]{:T(128)}, ...), condition=%wide.region_15.16_spmd, body=%wide.region_14.15_spmd.sunk | while | flops 551026688 | bytes 51904876 | solution.py:205
  521.5 6.4 all-to-all-done.24
  530.0 11.7 %all_to_all.205 = bf16[8,16,16,128]{3,1,2,0:T(8,128)(2,1)S(1)} all-to-all(bf16[8,16,16,128]{3,1,2,0:T(8,128)(2,1)S(1)} %copy.516), channel_id=1, replica_groups=mesh['s'=4,'t'=4,'x'=2] {'s','x'}, dimensions={0} | all-to-all | bytes 1048576 | tf_op jit(solution)/shard_map/while/body/all_to_all | solution.py:27
  565.4 6.0 all-to-all-done.27
  583.5 60.9 %while.139 = (s32[]{:T(128)}, bf16[16,128,128]{2,1,0:T(8,128)(2,1)S(1)}, bf16[4,4,4,128,128]{3,4,2,0,1:T(8,128)(2,1)}, s32[]{:T(128)}, bf16[4,1,2,4,128,128]{5,4...) while((s32[]{:T(128)}, ...), condition=%wide.region_18.19_spmd, body=%wide.region_17.18_spmd.sunk | while | flops 551026688 | bytes 43516164 | solution.py:205
  591.1 6.5 all-to-all-done.28
  599.3 11.7 %all_to_all.206 = bf16[8,16,16,128]{3,1,2,0:T(8,128)(2,1)S(1)} all-to-all(bf16[8,16,16,128]{3,1,2,0:T(8,128)(2,1)S(1)} %copy.526), channel_id=1, replica_groups=mesh['s'=4,'t'=4,'x'=2] {'s','x'}, dimensions={0} | all-to-all | bytes 1048576 | tf_op jit(solution)/shard_map/while/body/all_to_all | solution.py:27
  617.5 7.4 %all-to-all-done.30 = bf16[8,16,16,128]{3,1,2,0:T(8,128)(2,1)S(1)} async-done(((bf16[8,16,16,128]{3,1,2,0:T(8,128)(2,1)}), bf16[8,16,16,128]{3,1,2,0:T(8,128)(2,1)S(1)}, u32[]{:S(2)}, u32[]{:S(2)}) %all-to-all-start.30) | async-done | bytes 524320 | tf_op jit(solution)/shard_map/while/body/all_to_all | solution.py:27
  658.1 5.6 collective-permute-done.18
  672.6 14.6 %collective-permute-start.32 = (bf16[2,4,128,128]{3,2,1,0:T(8,128)(2,1)S(1)}, bf16[2,4,128,128]{3,2,1,0:T(8,128)(2,1)S(1)}, u32[]{:S(2)}, u32[]{:S(2)}) collective-permute-start(bf16[2,4,128,128]{3,2,1,0:T(8,128)(2,1)S(1)} %pad_maximum_fusion.37), channel_id=1, source_target_pairs={{0,16},{8,24},{16,0},{24,8},{1,17},{9,25},{17,1},{25,9},{2,18},{10... | collective-permute-start | bytes 786440 | tf_op jit(solution)/shard_map/ppermute | solution.py:108
  687.9 9.2 %collective-permute-done.32 = bf16[2,4,128,128]{3,2,1,0:T(8,128)(2,1)S(1)} collective-permute-done((bf16[2,4,128,128]{3,2,1,0:T(8,128)(2,1)S(1)}, bf16[2,4,128,128]{3,2,1,0:T(8,128)(2,1)S(1)}, u32[]{:S(2)}, u32[]{:S(2)}) %collective-permute-start.32) | collective-permute-done | bytes 262176 | tf_op jit(solution)/shard_map/ppermute | solution.py:108
  718.5 5.6 collective-permute-done.29
  (526 shorter events, 355.2 us)
Async XLA Ops:
  7.2 91.8 %all-gather.9.cloned.1.call-start = ((), (), s32[]{:S(2)}) async-start(), calls=%async_computation.40 | async-start | bytes 1310720 | tf_op jit(solution)/shard_map/all_gather | solution.py:116
  8.5 16.6 %collective-permute-start.3 = (bf16[4,128,128]{2,1,0:T(8,128)(2,1)S(1)}, bf16[4,128,128]{2,1,0:T(8,128)(2,1)S(1)}, u32[]{:S(2)}, u32[]{:S(2)}) collective-permute-start(bf16[4,128,128]{2,1,0:T(8,128)(2,1)S(1)} %get-tuple-element.976), channel_id=1, source_target_pairs={{0,24},{2,16},{4,8},{6,0},{8,26},{10,18},{12,10},{14,2},{16,28},{1... | collective-permute-start | bytes 393224 | tf_op jit(solution)/shard_map/ppermute | solution.py:76
  10.9 20.0 %collective-permute-start.2 = (bf16[4,128,128]{2,1,0:T(8,128)(2,1)S(1)}, bf16[4,128,128]{2,1,0:T(8,128)(2,1)S(1)}, u32[]{:S(2)}, u32[]{:S(2)}) collective-permute-start(bf16[4,128,128]{2,1,0:T(8,128)(2,1)S(1)} %get-tuple-element.977), channel_id=1, source_target_pairs={{0,16},{2,24},{4,0},{6,8},{8,18},{10,26},{12,2},{14,10},{16,20},{1... | collective-permute-start | bytes 393224 | tf_op jit(solution)/shard_map/ppermute | solution.py:76
  13.5 17.4 %collective-permute-start.1 = (bf16[4,128,128]{2,1,0:T(8,128)(2,1)S(1)}, bf16[4,128,128]{2,1,0:T(8,128)(2,1)S(1)}, u32[]{:S(2)}, u32[]{:S(2)}) collective-permute-start(bf16[4,128,128]{2,1,0:T(8,128)(2,1)S(1)} %get-tuple-element.978), channel_id=1, source_target_pairs={{0,8},{2,0},{4,24},{6,16},{8,10},{10,2},{12,26},{14,18},{16,12},{1... | collective-permute-start | bytes 393224 | tf_op jit(solution)/shard_map/ppermute | solution.py:76
  14.2 16.7 %collective-permute-start = (bf16[4,128,128]{2,1,0:T(8,128)(2,1)S(1)}, bf16[4,128,128]{2,1,0:T(8,128)(2,1)S(1)}, u32[]{:S(2)}, u32[]{:S(2)}) collective-permute-start(bf16[4,128,128]{2,1,0:T(8,128)(2,1)S(1)} %get-tuple-element.975), channel_id=1, source_target_pairs={{0,0},{2,8},{4,16},{6,24},{8,2},{10,10},{12,18},{14,26},{16,4},{18... | collective-permute-start | bytes 393224 | tf_op jit(solution)/shard_map/ppermute | solution.py:76
  18.3 13.3 %collective-permute-start.6 = (bf16[2,4,128,128]{2,3,1,0:T(8,128)(2,1)S(1)}, bf16[2,4,128,128]{2,3,1,0:T(8,128)(2,1)S(1)}, u32[]{:S(2)}, u32[]{:S(2)}) collective-permute-start(bf16[2,4,128,128]{2,3,1,0:T(8,128)(2,1)S(1)} %pad_maximum_fusion.29), channel_id=1, source_target_pairs={{0,24},{8,16},{16,8},{24,0},{1,25},{9,17},{17,9},{25,1},{2,26},{10... | collective-permute-start | bytes 786440 | tf_op jit(solution)/shard_map/ppermute | solution.py:108
  25.1 14.2 %collective-permute-start.5 = (bf16[2,4,128,128]{2,3,1,0:T(8,128)(2,1)S(1)}, bf16[2,4,128,128]{2,3,1,0:T(8,128)(2,1)S(1)}, u32[]{:S(2)}, u32[]{:S(2)}) collective-permute-start(bf16[2,4,128,128]{2,3,1,0:T(8,128)(2,1)S(1)} %pad_maximum_fusion.28), channel_id=1, source_target_pairs={{0,16},{8,24},{16,0},{24,8},{1,17},{9,25},{17,1},{25,9},{2,18},{10... | collective-permute-start | bytes 786440 | tf_op jit(solution)/shard_map/ppermute | solution.py:108
  43.7 15.9 %collective-permute-start.11 = (bf16[4,128,128]{2,1,0:T(8,128)(2,1)S(1)}, bf16[4,128,128]{2,1,0:T(8,128)(2,1)S(1)}, u32[]{:S(2)}, u32[]{:S(2)}) collective-permute-start(bf16[4,128,128]{2,1,0:T(8,128)(2,1)S(1)} %get-tuple-element.981), channel_id=1, source_target_pairs={{0,4},{2,6},{4,0},{6,2},{1,5},{3,7},{5,1},{7,3},{8,12},{10,14},{12... | collective-permute-start | bytes 393224 | tf_op jit(solution)/shard_map/ppermute | solution.py:121
  43.7 15.9 %collective-permute-start.10 = (bf16[4,128,128]{2,1,0:T(8,128)(2,1)S(1)}, bf16[4,128,128]{2,1,0:T(8,128)(2,1)S(1)}, u32[]{:S(2)}, u32[]{:S(2)}) collective-permute-start(bf16[4,128,128]{2,1,0:T(8,128)(2,1)S(1)} %get-tuple-element.981), channel_id=1, source_target_pairs={{0,2},{2,0},{4,6},{6,4},{1,3},{3,1},{5,7},{7,5},{8,10},{10,8},{12,... | collective-permute-start | bytes 393224 | tf_op jit(solution)/shard_map/ppermute | solution.py:121
  44.4 15.3 %collective-permute-start.9 = (bf16[4,128,128]{2,1,0:T(8,128)(2,1)S(1)}, bf16[4,128,128]{2,1,0:T(8,128)(2,1)S(1)}, u32[]{:S(2)}, u32[]{:S(2)}) collective-permute-start(bf16[4,128,128]{2,1,0:T(8,128)(2,1)S(1)} %get-tuple-element.980), channel_id=1, source_target_pairs={{0,6},{2,4},{4,2},{6,0},{1,7},{3,5},{5,3},{7,1},{8,14},{10,12},{12... | collective-permute-start | bytes 393224 | tf_op jit(solution)/shard_map/ppermute | solution.py:121
  48.1 16.8 %collective-permute-start.8 = (bf16[4,128,128]{2,1,0:T(8,128)(2,1)S(1)}, bf16[4,128,128]{2,1,0:T(8,128)(2,1)S(1)}, u32[]{:S(2)}, u32[]{:S(2)}) collective-permute-start(bf16[4,128,128]{2,1,0:T(8,128)(2,1)S(1)} %get-tuple-element.980), channel_id=1, source_target_pairs={{0,4},{2,6},{4,0},{6,2},{1,5},{3,7},{5,1},{7,3},{8,12},{10,14},{12... | collective-permute-start | bytes 393224 | tf_op jit(solution)/shard_map/ppermute | solution.py:121
  49.2 15.6 %collective-permute-start.7 = (bf16[4,128,128]{2,1,0:T(8,128)(2,1)S(1)}, bf16[4,128,128]{2,1,0:T(8,128)(2,1)S(1)}, u32[]{:S(2)}, u32[]{:S(2)}) collective-permute-start(bf16[4,128,128]{2,1,0:T(8,128)(2,1)S(1)} %get-tuple-element.980), channel_id=1, source_target_pairs={{0,2},{2,0},{4,6},{6,4},{1,3},{3,1},{5,7},{7,5},{8,10},{10,8},{12,... | collective-permute-start | bytes 393224 | tf_op jit(solution)/shard_map/ppermute | solution.py:121
  65.2 75.1 %all-gather.11.cloned.1.call-start = ((), (), s32[]{:S(2)}) async-start(), calls=%async_computation.41 | async-start | bytes 2621440 | tf_op jit(solution)/shard_map/all_gather | solution.py:116
  69.5 153.5 %all-gather.13.cloned.1.call-start = ((), (), s32[]{:S(2)}) async-start(), calls=%async_computation.42 | async-start | bytes 2621440 | tf_op jit(solution)/shard_map/all_gather | solution.py:116
  85.7 12.7 %all-to-all-start.1 = ((bf16[8,16,16,128]{3,1,2,0:T(8,128)(2,1)}), bf16[8,16,16,128]{3,1,2,0:T(8,128)(2,1)S(1)}, u32[]{:S(2)}, u32[]{:S(2)}) async-start(bf16[8,16,16,128]{3,1,2,0:T(8,128)(2,1)} %copy.465), calls=%async_computation.1 | async-start | bytes 1048576 | tf_op jit(solution)/shard_map/while/body/all_to_all | solution.py:27
  115.2 12.7 %all-to-all-start.3 = ((bf16[8,16,16,128]{3,1,2,0:T(8,128)(2,1)}), bf16[8,16,16,128]{3,1,2,0:T(8,128)(2,1)S(1)}, u32[]{:S(2)}, u32[]{:S(2)}) async-start(bf16[8,16,16,128]{3,1,2,0:T(8,128)(2,1)} %copy.469), calls=%async_computation.3 | async-start | bytes 1048576 | tf_op jit(solution)/shard_map/while/body/all_to_all | solution.py:27
  143.1 13.0 %collective-permute-start.14 = (bf16[2,4,128,128]{2,3,1,0:T(8,128)(2,1)S(1)}, bf16[2,4,128,128]{2,3,1,0:T(8,128)(2,1)S(1)}, u32[]{:S(2)}, u32[]{:S(2)}) collective-permute-start(bf16[2,4,128,128]{2,3,1,0:T(8,128)(2,1)S(1)} %pad_maximum_fusion.31), channel_id=1, source_target_pairs={{0,16},{8,24},{16,0},{24,8},{1,17},{9,25},{17,1},{25,9},{2,18},{10... | collective-permute-start | bytes 786440 | tf_op jit(solution)/shard_map/ppermute | solution.py:108
  159.7 123.5 %all-gather.15.cloned.1.call-start = ((), (), s32[]{:S(2)}) async-start(), calls=%async_computation.43 | async-start | bytes 2621440 | tf_op jit(solution)/shard_map/all_gather | solution.py:116
  165.9 343.1 %reduce-scatter.5.cloned.1.call-start = ((), (), s32[]{:S(2)}) async-start(), calls=%async_computation.36 | async-start | bytes 2621440 | tf_op jit(solution)/shard_map/reduce_scatter | solution.py:132
  209.7 12.7 %all-to-all-start.7 = ((bf16[8,16,16,128]{3,1,2,0:T(8,128)(2,1)}), bf16[8,16,16,128]{3,1,2,0:T(8,128)(2,1)S(1)}, u32[]{:S(2)}, u32[]{:S(2)}) async-start(bf16[8,16,16,128]{3,1,2,0:T(8,128)(2,1)} %copy.477), calls=%async_computation.7 | async-start | bytes 1048576 | tf_op jit(solution)/shard_map/while/body/all_to_all | solution.py:27
  270.0 12.7 %all-to-all-start.11 = ((bf16[8,16,16,128]{3,1,2,0:T(8,128)(2,1)}), bf16[8,16,16,128]{3,1,2,0:T(8,128)(2,1)S(1)}, u32[]{:S(2)}, u32[]{:S(2)}) async-start(bf16[8,16,16,128]{3,1,2,0:T(8,128)(2,1)} %copy.485), calls=%async_computation.11 | async-start | bytes 1048576 | tf_op jit(solution)/shard_map/while/body/all_to_all | solution.py:27
  331.6 13.4 %all-to-all-start.15 = ((bf16[8,16,16,128]{3,1,2,0:T(8,128)(2,1)}), bf16[8,16,16,128]{3,1,2,0:T(8,128)(2,1)}, u32[]{:S(2)}, u32[]{:S(2)}) async-start(bf16[8,16,16,128]{3,1,2,0:T(8,128)(2,1)} %copy.493), calls=%async_computation.15 | async-start | bytes 1048576 | tf_op jit(solution)/shard_map/while/body/all_to_all | solution.py:27
  348.7 17.1 %collective-permute-start.23 = (bf16[4,128,128]{1,2,0:T(8,128)(2,1)S(1)}, bf16[4,128,128]{1,2,0:T(8,128)(2,1)S(1)}, u32[]{:S(2)}, u32[]{:S(2)}) collective-permute-start(bf16[4,128,128]{1,2,0:T(8,128)(2,1)S(1)} %bitcast.1470), channel_id=1, source_target_pairs={{0,24},{2,16},{4,8},{6,0},{8,26},{10,18},{12,10},{14,2},{16,28},{1... | collective-permute-start | bytes 393224 | tf_op jit(solution)/shard_map/ppermute | solution.py:76
  349.3 19.3 %collective-permute-start.22 = (bf16[4,128,128]{1,2,0:T(8,128)(2,1)S(1)}, bf16[4,128,128]{1,2,0:T(8,128)(2,1)S(1)}, u32[]{:S(2)}, u32[]{:S(2)}) collective-permute-start(bf16[4,128,128]{1,2,0:T(8,128)(2,1)S(1)} %bitcast.1471), channel_id=1, source_target_pairs={{0,16},{2,24},{4,0},{6,8},{8,18},{10,26},{12,2},{14,10},{16,20},{1... | collective-permute-start | bytes 393224 | tf_op jit(solution)/shard_map/ppermute | solution.py:76
  350.6 18.0 %collective-permute-start.21 = (bf16[4,128,128]{1,2,0:T(8,128)(2,1)S(1)}, bf16[4,128,128]{1,2,0:T(8,128)(2,1)}, u32[]{:S(2)}, u32[]{:S(2)}) collective-permute-start(bf16[4,128,128]{1,2,0:T(8,128)(2,1)S(1)} %bitcast.1472), channel_id=1, source_target_pairs={{0,8},{2,0},{4,24},{6,16},{8,10},{10,2},{12,26},{14,18},{16,12},{1... | collective-permute-start | bytes 393224 | tf_op jit(solution)/shard_map/ppermute | solution.py:76
  351.0 17.6 %collective-permute-start.20 = (bf16[4,128,128]{1,2,0:T(8,128)(2,1)S(1)}, bf16[4,128,128]{1,2,0:T(8,128)(2,1)S(1)}, u32[]{:S(2)}, u32[]{:S(2)}) collective-permute-start(bf16[4,128,128]{1,2,0:T(8,128)(2,1)S(1)} %bitcast.1473), channel_id=1, source_target_pairs={{0,0},{2,8},{4,16},{6,24},{8,2},{10,10},{12,18},{14,26},{16,4},{18... | collective-permute-start | bytes 393224 | tf_op jit(solution)/shard_map/ppermute | solution.py:76
  373.8 16.7 %all-to-all-start.16 = ((bf16[8,16,16,128]{3,2,1,0:T(8,128)(2,1)}), bf16[8,16,16,128]{3,2,1,0:T(8,128)(2,1)S(1)}, u32[]{:S(2)}, u32[]{:S(2)}) async-start(bf16[8,16,16,128]{3,2,1,0:T(8,128)(2,1)} %bitcast.1138), calls=%async_computation.16 | async-start | bytes 1048576 | tf_op jit(solution)/shard_map/while/body/all_to_all | solution.py:27
  405.6 12.7 %all-to-all-start.18 = ((bf16[8,16,16,128]{3,1,2,0:T(8,128)(2,1)}), bf16[8,16,16,128]{3,1,2,0:T(8,128)(2,1)S(1)}, u32[]{:S(2)}, u32[]{:S(2)}) async-start(bf16[8,16,16,128]{3,1,2,0:T(8,128)(2,1)} %copy.498), calls=%async_computation.18 | async-start | bytes 1048576 | tf_op jit(solution)/shard_map/while/body/all_to_all | solution.py:27
  421.4 12.7 %all-to-all-start.19 = ((bf16[8,16,16,128]{3,2,1,0:T(8,128)(2,1)}), bf16[8,16,16,128]{3,2,1,0:T(8,128)(2,1)S(1)}, u32[]{:S(2)}, u32[]{:S(2)}) async-start(bf16[8,16,16,128]{3,2,1,0:T(8,128)(2,1)} %copy.500), calls=%async_computation.19 | async-start | bytes 1048576 | tf_op jit(solution)/shard_map/while/body/all_to_all | solution.py:27
  441.8 133.3 %reduce-scatter.7.cloned.1.call-start = ((), (), s32[]{:S(2)}) async-start(), calls=%async_computation.37 | async-start | bytes 2621440 | tf_op jit(solution)/shard_map/reduce_scatter | solution.py:132
  445.0 12.7 %all-to-all-start.20 = ((bf16[8,16,16,128]{3,2,1,0:T(8,128)(2,1)}), bf16[8,16,16,128]{3,2,1,0:T(8,128)(2,1)S(1)}, u32[]{:S(2)}, u32[]{:S(2)}) async-start(bf16[8,16,16,128]{3,2,1,0:T(8,128)(2,1)} %bitcast.1178), calls=%async_computation.20 | async-start | bytes 1048576 | tf_op jit(solution)/shard_map/while/body/all_to_all | solution.py:27
  472.7 12.7 %all-to-all-start.22 = ((bf16[8,16,16,128]{3,1,2,0:T(8,128)(2,1)}), bf16[8,16,16,128]{3,1,2,0:T(8,128)(2,1)S(1)}, u32[]{:S(2)}, u32[]{:S(2)}) async-start(bf16[8,16,16,128]{3,1,2,0:T(8,128)(2,1)} %copy.508), calls=%async_computation.22 | async-start | bytes 1048576 | tf_op jit(solution)/shard_map/while/body/all_to_all | solution.py:27
  488.5 12.7 %all-to-all-start.23 = ((bf16[8,16,16,128]{3,2,1,0:T(8,128)(2,1)}), bf16[8,16,16,128]{3,2,1,0:T(8,128)(2,1)S(1)}, u32[]{:S(2)}, u32[]{:S(2)}) async-start(bf16[8,16,16,128]{3,2,1,0:T(8,128)(2,1)} %copy.510), calls=%async_computation.23 | async-start | bytes 1048576 | tf_op jit(solution)/shard_map/while/body/all_to_all | solution.py:27
  509.0 188.2 %reduce-scatter.9.cloned.1.call-start = ((), (), s32[]{:S(2)}) async-start(), calls=%async_computation.38 | async-start | bytes 2621440 | tf_op jit(solution)/shard_map/reduce_scatter | solution.py:132
  515.2 12.7 %all-to-all-start.24 = ((bf16[8,16,16,128]{3,2,1,0:T(8,128)(2,1)}), bf16[8,16,16,128]{3,2,1,0:T(8,128)(2,1)S(1)}, u32[]{:S(2)}, u32[]{:S(2)}) async-start(bf16[8,16,16,128]{3,2,1,0:T(8,128)(2,1)} %bitcast.1218), calls=%async_computation.24 | async-start | bytes 1048576 | tf_op jit(solution)/shard_map/while/body/all_to_all | solution.py:27
  543.0 12.7 %all-to-all-start.26 = ((bf16[8,16,16,128]{3,1,2,0:T(8,128)(2,1)}), bf16[8,16,16,128]{3,1,2,0:T(8,128)(2,1)S(1)}, u32[]{:S(2)}, u32[]{:S(2)}) async-start(bf16[8,16,16,128]{3,1,2,0:T(8,128)(2,1)} %copy.518), calls=%async_computation.26 | async-start | bytes 1048576 | tf_op jit(solution)/shard_map/while/body/all_to_all | solution.py:27
  558.8 12.7 %all-to-all-start.27 = ((bf16[8,16,16,128]{3,2,1,0:T(8,128)(2,1)}), bf16[8,16,16,128]{3,2,1,0:T(8,128)(2,1)S(1)}, u32[]{:S(2)}, u32[]{:S(2)}) async-start(bf16[8,16,16,128]{3,2,1,0:T(8,128)(2,1)} %copy.520), calls=%async_computation.27 | async-start | bytes 1048576 | tf_op jit(solution)/shard_map/while/body/all_to_all | solution.py:27
  581.7 121.8 %reduce-scatter.11.cloned.1.call-start = ((), (), s32[]{:S(2)}) async-start(), calls=%async_computation.39 | async-start | bytes 2621440 | tf_op jit(solution)/shard_map/reduce_scatter | solution.py:132
  584.9 12.7 %all-to-all-start.28 = ((bf16[8,16,16,128]{3,2,1,0:T(8,128)(2,1)}), bf16[8,16,16,128]{3,2,1,0:T(8,128)(2,1)S(1)}, u32[]{:S(2)}, u32[]{:S(2)}) async-start(bf16[8,16,16,128]{3,2,1,0:T(8,128)(2,1)} %bitcast.1258), calls=%async_computation.28 | async-start | bytes 1048576 | tf_op jit(solution)/shard_map/while/body/all_to_all | solution.py:27
  612.3 12.7 %all-to-all-start.30 = ((bf16[8,16,16,128]{3,1,2,0:T(8,128)(2,1)}), bf16[8,16,16,128]{3,1,2,0:T(8,128)(2,1)S(1)}, u32[]{:S(2)}, u32[]{:S(2)}) async-start(bf16[8,16,16,128]{3,1,2,0:T(8,128)(2,1)} %copy.528), calls=%async_computation.30 | async-start | bytes 1048576 | tf_op jit(solution)/shard_map/while/body/all_to_all | solution.py:27
  628.2 12.7 %all-to-all-start.31 = ((bf16[8,16,16,128]{3,2,1,0:T(8,128)(2,1)}), bf16[8,16,16,128]{3,2,1,0:T(8,128)(2,1)S(1)}, u32[]{:S(2)}, u32[]{:S(2)}) async-start(bf16[8,16,16,128]{3,2,1,0:T(8,128)(2,1)} %copy.530), calls=%async_computation.31 | async-start | bytes 1048576 | tf_op jit(solution)/shard_map/while/body/all_to_all | solution.py:27
  652.9 16.0 %collective-permute-start.17 = (bf16[4,128,128]{2,1,0:T(8,128)(2,1)S(1)}, bf16[4,128,128]{2,1,0:T(8,128)(2,1)S(1)}, u32[]{:S(2)}, u32[]{:S(2)}) collective-permute-start(bf16[4,128,128]{2,1,0:T(8,128)(2,1)S(1)} %bitcast.1476), channel_id=1, source_target_pairs={{0,2},{2,10},{4,18},{6,26},{8,0},{10,8},{12,16},{14,24},{16,6},{18... | collective-permute-start | bytes 393224 | tf_op jit(solution)/shard_map/ppermute | solution.py:76
  653.1 15.8 %collective-permute-start.16 = (bf16[4,128,128]{2,1,0:T(8,128)(2,1)S(1)}, bf16[4,128,128]{2,1,0:T(8,128)(2,1)S(1)}, u32[]{:S(2)}, u32[]{:S(2)}) collective-permute-start(bf16[4,128,128]{2,1,0:T(8,128)(2,1)S(1)} %bitcast.1477), channel_id=1, source_target_pairs={{0,0},{2,8},{4,16},{6,24},{8,2},{10,10},{12,18},{14,26},{16,4},{18... | collective-permute-start | bytes 393224 | tf_op jit(solution)/shard_map/ppermute | solution.py:76
  669.6 18.2 %collective-permute-start.33 = (bf16[2,4,128,128]{3,2,1,0:T(8,128)(2,1)S(1)}, bf16[2,4,128,128]{3,2,1,0:T(8,128)(2,1)S(1)}, u32[]{:S(2)}, u32[]{:S(2)}) collective-permute-start(bf16[2,4,128,128]{3,2,1,0:T(8,128)(2,1)S(1)} %pad_maximum_fusion.38), channel_id=1, source_target_pairs={{0,24},{8,16},{16,8},{24,0},{1,25},{9,17},{17,9},{25,1},{2,26},{10... | collective-permute-start | bytes 786440 | tf_op jit(solution)/shard_map/ppermute | solution.py:108
  672.6 24.5 %collective-permute-start.32 = (bf16[2,4,128,128]{3,2,1,0:T(8,128)(2,1)S(1)}, bf16[2,4,128,128]{3,2,1,0:T(8,128)(2,1)S(1)}, u32[]{:S(2)}, u32[]{:S(2)}) collective-permute-start(bf16[2,4,128,128]{3,2,1,0:T(8,128)(2,1)S(1)} %pad_maximum_fusion.37), channel_id=1, source_target_pairs={{0,16},{8,24},{16,0},{24,8},{1,17},{9,25},{17,1},{25,9},{2,18},{10... | collective-permute-start | bytes 786440 | tf_op jit(solution)/shard_map/ppermute | solution.py:108
  699.3 12.8 %collective-permute-start.26 = (bf16[4,128,128]{2,1,0:T(8,128)(2,1)S(1)}, bf16[4,128,128]{2,1,0:T(8,128)(2,1)S(1)}, u32[]{:S(2)}, u32[]{:S(2)}) collective-permute-start(bf16[4,128,128]{2,1,0:T(8,128)(2,1)S(1)} %bitcast.1467), channel_id=1, source_target_pairs={{0,4},{2,12},{4,20},{6,28},{8,6},{10,14},{12,22},{14,30},{16,0},{1... | collective-permute-start | bytes 393224 | tf_op jit(solution)/shard_map/ppermute | solution.py:76
  705.5 13.1 %collective-permute-start.30 = (bf16[2,4,128,128]{3,2,1,0:T(8,128)(2,1)S(1)}, bf16[2,4,128,128]{3,2,1,0:T(8,128)(2,1)S(1)}, u32[]{:S(2)}, u32[]{:S(2)}) collective-permute-start(bf16[2,4,128,128]{3,2,1,0:T(8,128)(2,1)S(1)} %pad_maximum_fusion.35), channel_id=1, source_target_pairs={{0,24},{8,16},{16,8},{24,0},{1,25},{9,17},{17,9},{25,1},{2,26},{10... | collective-permute-start | bytes 786440 | tf_op jit(solution)/shard_map/ppermute | solution.py:108
  710.9 13.2 %collective-permute-start.29 = (bf16[2,4,128,128]{3,2,1,0:T(8,128)(2,1)S(1)}, bf16[2,4,128,128]{3,2,1,0:T(8,128)(2,1)S(1)}, u32[]{:S(2)}, u32[]{:S(2)}) collective-permute-start(bf16[2,4,128,128]{3,2,1,0:T(8,128)(2,1)S(1)} %pad_maximum_fusion.34), channel_id=1, source_target_pairs={{0,16},{8,24},{16,0},{24,8},{1,17},{9,25},{17,1},{25,9},{2,18},{10... | collective-permute-start | bytes 786440 | tf_op jit(solution)/shard_map/ppermute | solution.py:108
  (72 other events, 819.2 us)
Sparse Core Ops, SparseCore 0:
  65.4 27.2 all-gather.8
  94.8 45.4 all-gather.10
  159.8 44.6 all-gather.12
  206.5 44.5 all-gather.14
  441.9 41.8 reduce-scatter.4
  509.1 41.8 reduce-scatter.6
  581.8 41.7 reduce-scatter.8
  648.7 49.6 reduce-scatter.10

commit v17 on v16

--- a/solution.py
+++ b/solution.py
@@ -69,11 +69,14 @@
     def pick(parts, index):
         return lax.dynamic_index_in_dim(parts, index, 0, keepdims=False)
 
-    def turned(parts, send_by, place_by, target):
+    def sent(parts, send_by, target):
         moved = []
         for mask in range(sections):
             pairs = [(s * groups + t, target(s, t, mask)) for s in range(sections) for t in range(groups)]
             moved.append(lax.ppermute(pick(parts, send_by ^ mask), ("s", "t"), pairs))
+        return moved
+
+    def placed(moved, place_by):
         moved = jnp.stack(moved)
         return jnp.stack([pick(moved, place_by ^ part) for part in range(sections)])
 
@@ -85,8 +88,10 @@
         return (t * micros + line_to // groups) * groups + line_to % groups
 
     def arriving(acts):
-        parts = turned(acts.reshape(sections, sub, size, rows), line, s_index, into)
-        parts = parts.reshape(micros, own, size, rows).transpose(1, 2, 0, 3)
+        return sent(acts.reshape(sections, sub, size, rows), line, into)
+
+    def arrived(moved):
+        parts = placed(moved, s_index).reshape(micros, own, size, rows).transpose(1, 2, 0, 3)
         return parts.reshape(own, size, micros * rows)
 
     def settled(parts):
@@ -97,7 +102,7 @@
 
     def leave(acts):
         parts = acts.reshape(own, size, micros, rows).transpose(2, 0, 1, 3)
-        parts = turned(parts.reshape(sections, sub, size, rows), s_index, line, outof)
+        parts = placed(sent(parts.reshape(sections, sub, size, rows), s_index, outof), line)
         return parts.reshape(1, held * size, rows)
 
     def scattered(*kinds):
@@ -138,7 +143,7 @@
     rights = right_factor[:, 0].reshape(loops, sections, sub, size, size)
     lefts = left_factor[:, 0].reshape(loops, sections, sub, size, size)
     parts = [ordered(part) for part in scattered(rights[0], lefts[0])]
-    current = arriving(inputs)
+    current = arrived(arriving(inputs))
     current, parts[0] = lax.optimization_barrier((current, parts[0]))
     once = 1 + s_index // sections
     first = jnp.stack([gathered_directly(parts[0][f]) for f in range(2)], axis=1)[:, None]
@@ -166,15 +171,20 @@
 
     for begin, end in zip(starts, starts[1:]):
         stretch = range(begin, end)
-        full = ahead if begin else first
+        full = first
         if begin:
             coming = range(end, min(end + PAIRED, layers))
             if begin == PAIRED:
                 current, rights, lefts = lax.optimization_barrier((current, rights[1:], lefts[1:]))
                 for loop in range(loops - 1):
                     parts.extend(ordered(part) for part in scattered(rights[loop], lefts[loop]))
+                ahead, parts[end:] = lax.optimization_barrier((ahead, parts[end:]))
+            full = ahead
             if coming:
                 ahead = gathered(jnp.stack([parts[layer] for layer in coming]))
+        if end == layers:
+            current, cotangent = lax.optimization_barrier((current, cotangent))
+            moving = arriving(cotangent)
         weights.update((layer, (full, layer - begin)) for layer in stretch)
         blanks = [jnp.zeros(current.shape, BF16) for _ in range(2 * len(stretch) - 1)]
         entered = current
@@ -182,8 +192,8 @@
         current, ahead = lax.optimization_barrier((current, ahead))
         saved = [entered] + saved
         stored.update((layer, saved[2 * step : 2 * step + 2]) for step, layer in enumerate(stretch))
-    current, cotangent = lax.optimization_barrier((current, cotangent))
-    grad = settled(arriving(cotangent))
+    current, moving = lax.optimization_barrier((current, moving))
+    grad = settled(arrived(moving))
     outputs = leave(unsettled(current))
 
     sums = [None] * layers
@@ -209,7 +219,7 @@
         totals[top] = summed(terms)
     grad = lax.fori_loop(0, once, lambda _, acts: unsettled(acts), grad)
     if 2 * PAIRED <= layers:
-        grad, totals[2 * PAIRED - 1] = lax.optimization_barrier((grad, totals[2 * PAIRED - 1]))
+        _, totals[2 * PAIRED - 1] = lax.optimization_barrier((grad, totals[2 * PAIRED - 1]))
     for top, total in totals.items():
         for step in range(PAIRED):
             sums[top - step] = [total[2 * step], total[2 * step + 1]]

time: 747 us -> 751 us (level)
  waiting for transfers between devices: 203 us -> 184 us
  starting transfers between devices: 124 us -> 133 us
    ppermute x16, starting transfers between devices: 15.9 us -> 31.3 us  [sent(): moved.append(lax.ppermute(pick(parts, send_by ^ mask), ('s', 't'), pairs))]
    ppermute x12, waiting for transfers between devices: 37.6 us -> 23.6 us  [scattered(): moved.append(lax.ppermute(value, 's', pairs))]
    while x15, local copies, waits for them, and re-layouts: 21.6 us -> 29.7 us  [body(): grad, terms = lax.fori_loop(0, once, backward_pair(top), (grad, blank))]
  transfers between devices with their start and end apart: 59 -> 59, of which waited for: 32 -> 29; matrix products, arithmetic and copies ran while one was open for 22% -> 23% of each run, Pallas kernels for 0% -> 0%
where the time goes in v17:
time: 751 us; the launch traced here: 740 us
  waiting for transfers between devices  184 us (25%)
  blocking collectives  182 us (24%)
  starting transfers between devices  133 us (18%)
  local copies, waits for them, and re-layouts  130 us (17%)
  matrix products  64.3 us (9%)
  other arithmetic  28.7 us (4%)
  between operations  15.8 us (2%)
    all_to_all x15, blocking collectives, exchange(): lax.all_to_all(pieces, WIDE, split_axis=0, concat_axis=0, tiled=True)  182 us
    all_to_all x17, waiting for transfers between devices, exchange(): lax.all_to_all(pieces, WIDE, split_axis=0, concat_axis=0, tiled=True)  117 us
    all_to_all x17, starting transfers between devices, exchange(): lax.all_to_all(pieces, WIDE, split_axis=0, concat_axis=0, tiled=True)  60 us
    ppermute x16, starting transfers between devices, sent(): moved.append(lax.ppermute(pick(parts, send_by ^ mask), ('s', 't'), pairs))  31.3 us
    ppermute x12, starting transfers between devices, scattered(): moved.append(lax.ppermute(value, 's', pairs))  30.5 us
    while x15, local copies, waits for them, and re-layouts, body(): grad, terms = lax.fori_loop(0, once, backward_pair(top), (grad, blank))  29.7 us
    ppermute x12, waiting for transfers between devices, scattered(): moved.append(lax.ppermute(value, 's', pairs))  23.6 us
    ppermute x16, waiting for transfers between devices, sent(): moved.append(lax.ppermute(pick(parts, send_by ^ mask), ('s', 't'), pairs))  20.7 us
  transfers between devices with their start and end apart: 59, of which 29 were waited for; matrix products, arithmetic and copies ran while one was open for 23% of the time, Pallas kernels for 0%

profile of v17, /device:TPU:0, one launch (start us, length us, event | category | flops | bytes accessed | tf_op | source)
XLA Modules:
  0.0 739.5 jit_solution(8148425818587180664)
XLA Ops:
  18.3 5.7 collective-permute-start.6
  31.6 7.7 %collective-permute-done.5 = bf16[2,4,128,128]{2,3,1,0:T(8,128)(2,1)S(1)} collective-permute-done((bf16[2,4,128,128]{2,3,1,0:T(8,128)(2,1)S(1)}, bf16[2,4,128,128]{2,3,1,0:T(8,128)(2,1)S(1)}, u32[]{:S(2)}, u32[]{:S(2)}) %collective-permute-start.5) | collective-permute-done | bytes 262176 | tf_op jit(solution)/shard_map/ppermute | solution.py:113
  51.7 7.9 %collective-permute-done.11 = bf16[4,128,128]{2,1,0:T(8,128)(2,1)S(1)} collective-permute-done((bf16[4,128,128]{2,1,0:T(8,128)(2,1)S(1)}, bf16[4,128,128]{2,1,0:T(8,128)(2,1)S(1)}, u32[]{:S(2)}, u32[]{:S(2)}) %collective-permute-start.11) | collective-permute-done | bytes 131104 | tf_op jit(solution)/shard_map/ppermute | solution.py:126
  72.9 27.8 %while.131 = (s32[]{:T(128)}, bf16[16,128,128]{2,1,0:T(8,128)(2,1)S(1)}, bf16[16,128,128]{2,0,1:T(8,128)(2,1)}, s32[]{:T(128)}, bf16[4,1,2,4,128,128]{4,5,3,0,2,1:T(8,128)(2,1)S(1)}, /*index=5*/s32[]{:T(128)}) while((s32[]{:T(128)}, bf16[16,128,128]{2,1,0:T(8,128)(2,1)S(1)}, bf16[16,128,128]{2,0,1:T(8,128)(2,1)}, s32[]{:T(128)}, ...), condition=%wide.region_1.2_spmd, body=%wide.region_0.1_spmd.sunk | while | flops 137363456 | bytes 16777344 | solution.py:191
  73.3 12.7 %all_to_all.192 = bf16[8,16,16,128]{3,1,2,0:T(8,128)(2,1)S(1)} all-to-all(bf16[8,16,16,128]{3,1,2,0:T(8,128)(2,1)S(1)} %copy.464), channel_id=1, replica_groups=mesh['s'=4,'t'=4,'x'=2] {'s','x'}, dimensions={0} | all-to-all | bytes 1048576 | tf_op jit(solution)/shard_map/while/body/all_to_all | solution.py:27
  91.1 9.2 %all-to-all-done.1 = bf16[8,16,16,128]{3,1,2,0:T(8,128)(2,1)S(1)} async-done(((bf16[8,16,16,128]{3,1,2,0:T(8,128)(2,1)}), bf16[8,16,16,128]{3,1,2,0:T(8,128)(2,1)S(1)}, u32[]{:S(2)}, u32[]{:S(2)}) %all-to-all-start.1) | async-done | bytes 524320 | tf_op jit(solution)/shard_map/while/body/all_to_all | solution.py:27
  103.5 27.0 %while.132 = (s32[]{:T(128)}, bf16[16,128,128]{2,1,0:T(8,128)(2,1)S(1)}, bf16[16,128,128]{2,0,1:T(8,128)(2,1)}, s32[]{:T(128)}, bf16[4,1,2,4,128,128]{4,5,3,0,2,1:T(8,128)(2,1)S(1)}, /*index=5*/s32[]{:T(128)}) while((s32[]{:T(128)}, bf16[16,128,128]{2,1,0:T(8,128)(2,1)S(1)}, bf16[16,128,128]{2,0,1:T(8,128)(2,1)}, s32[]{:T(128)}, ...), condition=%wide.region_3.4_spmd, body=%wide.region_2.3_spmd.sunk | while | flops 137363456 | bytes 16777344 | solution.py:191
  103.9 11.7 %all_to_all.193 = bf16[8,16,16,128]{3,1,2,0:T(8,128)(2,1)S(1)} all-to-all(bf16[8,16,16,128]{3,1,2,0:T(8,128)(2,1)S(1)} %copy.468), channel_id=1, replica_groups=mesh['s'=4,'t'=4,'x'=2] {'s','x'}, dimensions={0} | all-to-all | bytes 1048576 | tf_op jit(solution)/shard_map/while/body/all_to_all | solution.py:27
  120.6 9.2 %all-to-all-done.3 = bf16[8,16,16,128]{3,1,2,0:T(8,128)(2,1)S(1)} async-done(((bf16[8,16,16,128]{3,1,2,0:T(8,128)(2,1)}), bf16[8,16,16,128]{3,1,2,0:T(8,128)(2,1)S(1)}, u32[]{:S(2)}, u32[]{:S(2)}) %all-to-all-start.3) | async-done | bytes 524320 | tf_op jit(solution)/shard_map/while/body/all_to_all | solution.py:27
  130.5 9.2 %all-gather.11.cloned.1.call-done = bf16[8,2,4,128,128]{4,3,2,1,0:T(8,128)(2,1)} async-done(((bf16[2,2,4,128,128]{4,3,2,1,0:T(8,128)(2,1)}), bf16[8,2,4,128,128]{4,3,2,1,0:T(8,128)(2,1)}) %all-gather.11.cloned.1.call-update) | async-done | bytes 2097168 | tf_op jit(solution)/shard_map/all_gather | solution.py:121
  150.8 5.6 collective-permute-done.14
  169.9 53.8 %while.133 = (s32[]{:T(128)}, bf16[16,128,128]{2,1,0:T(8,128)(2,1)S(1)}, bf16[16,128,128]{2,0,1:T(8,128)(2,1)}, bf16[16,128,128]{2,1,0:T(8,128)(2,1)}, bf16[16,1...) while((s32[]{:T(128)}, ...), condition=%wide.region_5.6_spmd, body=%wide.region_4.5_spmd.sunk | while | flops 274726912 | bytes 35127496 | solution.py:191
  170.5 12.7 %all_to_all.194 = bf16[8,16,16,128]{3,1,2,0:T(8,128)(2,1)S(1)} all-to-all(bf16[8,16,16,128]{3,1,2,0:T(8,128)(2,1)S(1)} %copy.474), channel_id=1, replica_groups=mesh['s'=4,'t'=4,'x'=2] {'s','x'}, dimensions={0} | all-to-all | bytes 1048576 | tf_op jit(solution)/shard_map/while/body/all_to_all | solution.py:27
  184.3 11.7 %all_to_all.195 = bf16[8,16,16,128]{3,1,2,0:T(8,128)(2,1)S(1)} all-to-all(bf16[8,16,16,128]{3,1,2,0:T(8,128)(2,1)S(1)} %copy.475), channel_id=1, replica_groups=mesh['s'=4,'t'=4,'x'=2] {'s','x'}, dimensions={0} | all-to-all | bytes 1048576 | tf_op jit(solution)/shard_map/while/body/all_to_all | solution.py:27
  196.8 11.7 %all_to_all.196 = bf16[8,16,16,128]{3,1,2,0:T(8,128)(2,1)S(1)} all-to-all(bf16[8,16,16,128]{3,1,2,0:T(8,128)(2,1)S(1)} %copy.476), channel_id=1, replica_groups=mesh['s'=4,'t'=4,'x'=2] {'s','x'}, dimensions={0} | all-to-all | bytes 1048576 | tf_op jit(solution)/shard_map/while/body/all_to_all | solution.py:27
  213.9 9.2 %all-to-all-done.7 = bf16[8,16,16,128]{3,1,2,0:T(8,128)(2,1)S(1)} async-done(((bf16[8,16,16,128]{3,1,2,0:T(8,128)(2,1)}), bf16[8,16,16,128]{3,1,2,0:T(8,128)(2,1)S(1)}, u32[]{:S(2)}, u32[]{:S(2)}) %all-to-all-start.7) | async-done | bytes 524320 | tf_op jit(solution)/shard_map/while/body/all_to_all | solution.py:27
  234.5 53.0 %while.134 = (s32[]{:T(128)}, bf16[16,128,128]{2,1,0:T(8,128)(2,1)S(1)}, bf16[16,128,128]{2,0,1:T(8,128)(2,1)}, bf16[16,128,128]{2,1,0:T(8,128)(2,1)}, bf16[16,1...) while((s32[]{:T(128)}, ...), condition=%wide.region_7.8_spmd, body=%wide.region_6.7_spmd.sunk | while | flops 274726912 | bytes 35127496 | solution.py:191
  235.1 11.7 %all_to_all.197 = bf16[8,16,16,128]{3,1,2,0:T(8,128)(2,1)S(1)} all-to-all(bf16[8,16,16,128]{3,1,2,0:T(8,128)(2,1)S(1)} %copy.482), channel_id=1, replica_groups=mesh['s'=4,'t'=4,'x'=2] {'s','x'}, dimensions={0} | all-to-all | bytes 1048576 | tf_op jit(solution)/shard_map/while/body/all_to_all | solution.py:27
  247.9 11.7 %all_to_all.198 = bf16[8,16,16,128]{3,1,2,0:T(8,128)(2,1)S(1)} all-to-all(bf16[8,16,16,128]{3,1,2,0:T(8,128)(2,1)S(1)} %copy.483), channel_id=1, replica_groups=mesh['s'=4,'t'=4,'x'=2] {'s','x'}, dimensions={0} | all-to-all | bytes 1048576 | tf_op jit(solution)/shard_map/while/body/all_to_all | solution.py:27
  260.4 11.7 %all_to_all.199 = bf16[8,16,16,128]{3,1,2,0:T(8,128)(2,1)S(1)} all-to-all(bf16[8,16,16,128]{3,1,2,0:T(8,128)(2,1)S(1)} %copy.484), channel_id=1, replica_groups=mesh['s'=4,'t'=4,'x'=2] {'s','x'}, dimensions={0} | all-to-all | bytes 1048576 | tf_op jit(solution)/shard_map/while/body/all_to_all | solution.py:27
  277.5 9.2 %all-to-all-done.11 = bf16[8,16,16,128]{3,1,2,0:T(8,128)(2,1)S(1)} async-done(((bf16[8,16,16,128]{3,1,2,0:T(8,128)(2,1)}), bf16[8,16,16,128]{3,1,2,0:T(8,128)(2,1)S(1)}, u32[]{:S(2)}, u32[]{:S(2)}) %all-to-all-start.11) | async-done | bytes 524320 | tf_op jit(solution)/shard_map/while/body/all_to_all | solution.py:27
  305.4 62.0 %while.135 = (s32[]{:T(128)}, bf16[16,128,128]{2,1,0:T(8,128)(2,1)}, bf16[16,128,128]{2,0,1:T(8,128)(2,1)}, bf16[16,128,128]{2,1,0:T(8,128)(2,1)}, bf16[16,128,1...) while((s32[]{:T(128)}, bf16[16,128,128]{2,1,0:T(8,128)(2,1)}, ...), condition=%wide.region_9.10_spmd, body=%wide.region_8.9_spmd.sunk | while | flops 274726912 | bytes 35127496 | solution.py:191
  307.0 15.6 %all_to_all.200 = bf16[8,16,16,128]{3,1,2,0:T(8,128)(2,1)S(1)} all-to-all(bf16[8,16,16,128]{3,1,2,0:T(8,128)(2,1)S(1)} %copy.490), channel_id=1, replica_groups=mesh['s'=4,'t'=4,'x'=2] {'s','x'}, dimensions={0} | all-to-all | bytes 1048576 | tf_op jit(solution)/shard_map/while/body/all_to_all | solution.py:27
  323.8 12.4 %all_to_all.201 = bf16[8,16,16,128]{3,1,2,0:T(8,128)(2,1)S(1)} all-to-all(bf16[8,16,16,128]{3,1,2,0:T(8,128)(2,1)S(1)} %copy.491), channel_id=1, replica_groups=mesh['s'=4,'t'=4,'x'=2] {'s','x'}, dimensions={0} | all-to-all | bytes 1048576 | tf_op jit(solution)/shard_map/while/body/all_to_all | solution.py:27
  338.1 11.7 %all_to_all.202 = bf16[8,16,16,128]{3,1,2,0:T(8,128)(2,1)S(1)} all-to-all(bf16[8,16,16,128]{3,1,2,0:T(8,128)(2,1)S(1)} %copy.492), channel_id=1, replica_groups=mesh['s'=4,'t'=4,'x'=2] {'s','x'}, dimensions={0} | all-to-all | bytes 1048576 | tf_op jit(solution)/shard_map/while/body/all_to_all | solution.py:27
  355.8 9.3 %all-to-all-done.15 = bf16[8,16,16,128]{3,1,2,0:T(8,128)(2,1)} async-done(((bf16[8,16,16,128]{3,1,2,0:T(8,128)(2,1)}), bf16[8,16,16,128]{3,1,2,0:T(8,128)(2,1)}, u32[]{:S(2)}, u32[]{:S(2)}) %all-to-all-start.15) | async-done | bytes 524320 | tf_op jit(solution)/shard_map/while/body/all_to_all | solution.py:27
  377.2 61.4 %while.136 = (s32[]{:T(128)}, bf16[16,128,128]{2,1,0:T(8,128)(2,1)S(1)}, bf16[4,4,4,128,128]{3,4,2,0,1:T(8,128)(2,1)}, s32[]{:T(128)}, bf16[4,2,2,4,128,128]{5,4...) while((s32[]{:T(128)}, ...), condition=%wide.region_11.12_spmd, body=%wide.region_10.11_spmd.sunk | while | flops 551026688 | bytes 51904876 | solution.py:215
  385.0 6.5 all-to-all-done.16
  393.6 11.7 %all_to_all.203 = bf16[8,16,16,128]{3,1,2,0:T(8,128)(2,1)S(1)} all-to-all(bf16[8,16,16,128]{3,1,2,0:T(8,128)(2,1)S(1)} %copy.496), channel_id=1, replica_groups=mesh['s'=4,'t'=4,'x'=2] {'s','x'}, dimensions={0} | all-to-all | bytes 1048576 | tf_op jit(solution)/shard_map/while/body/all_to_all | solution.py:27
  428.9 6.1 all-to-all-done.19
  444.6 61.1 %while.137 = (s32[]{:T(128)}, bf16[16,128,128]{2,1,0:T(8,128)(2,1)S(1)}, bf16[4,4,4,128,128]{3,4,2,0,1:T(8,128)(2,1)}, s32[]{:T(128)}, bf16[4,2,2,4,128,128]{5,4...) while((s32[]{:T(128)}, ...), condition=%wide.region_13.14_spmd, body=%wide.region_12.13_spmd.sunk | while | flops 551026688 | bytes 51904876 | solution.py:215
  452.1 6.5 all-to-all-done.20
  460.7 11.7 %all_to_all.204 = bf16[8,16,16,128]{3,1,2,0:T(8,128)(2,1)S(1)} all-to-all(bf16[8,16,16,128]{3,1,2,0:T(8,128)(2,1)S(1)} %copy.506), channel_id=1, replica_groups=mesh['s'=4,'t'=4,'x'=2] {'s','x'}, dimensions={0} | all-to-all | bytes 1048576 | tf_op jit(solution)/shard_map/while/body/all_to_all | solution.py:27
  496.1 6.1 all-to-all-done.23
  514.8 61.2 %while.138 = (s32[]{:T(128)}, bf16[16,128,128]{2,1,0:T(8,128)(2,1)S(1)}, bf16[4,4,4,128,128]{3,4,2,0,1:T(8,128)(2,1)}, s32[]{:T(128)}, bf16[4,2,2,4,128,128]{5,4...) while((s32[]{:T(128)}, ...), condition=%wide.region_15.16_spmd, body=%wide.region_14.15_spmd.sunk | while | flops 551026688 | bytes 51904876 | solution.py:215
  522.4 6.5 all-to-all-done.24
  530.9 11.7 %all_to_all.205 = bf16[8,16,16,128]{3,1,2,0:T(8,128)(2,1)S(1)} all-to-all(bf16[8,16,16,128]{3,1,2,0:T(8,128)(2,1)S(1)} %copy.516), channel_id=1, replica_groups=mesh['s'=4,'t'=4,'x'=2] {'s','x'}, dimensions={0} | all-to-all | bytes 1048576 | tf_op jit(solution)/shard_map/while/body/all_to_all | solution.py:27
  566.3 6.1 all-to-all-done.27
  584.4 61.0 %while.139 = (s32[]{:T(128)}, bf16[16,128,128]{2,1,0:T(8,128)(2,1)S(1)}, bf16[4,4,4,128,128]{3,4,2,0,1:T(8,128)(2,1)}, s32[]{:T(128)}, bf16[4,1,2,4,128,128]{5,4...) while((s32[]{:T(128)}, ...), condition=%wide.region_18.19_spmd, body=%wide.region_17.18_spmd.sunk | while | flops 551026688 | bytes 43516164 | solution.py:215
  592.0 6.5 all-to-all-done.28
  600.3 11.7 %all_to_all.206 = bf16[8,16,16,128]{3,1,2,0:T(8,128)(2,1)S(1)} all-to-all(bf16[8,16,16,128]{3,1,2,0:T(8,128)(2,1)S(1)} %copy.526), channel_id=1, replica_groups=mesh['s'=4,'t'=4,'x'=2] {'s','x'}, dimensions={0} | all-to-all | bytes 1048576 | tf_op jit(solution)/shard_map/while/body/all_to_all | solution.py:27
  618.5 7.4 %all-to-all-done.30 = bf16[8,16,16,128]{3,1,2,0:T(8,128)(2,1)S(1)} async-done(((bf16[8,16,16,128]{3,1,2,0:T(8,128)(2,1)}), bf16[8,16,16,128]{3,1,2,0:T(8,128)(2,1)S(1)}, u32[]{:S(2)}, u32[]{:S(2)}) %all-to-all-start.30) | async-done | bytes 524320 | tf_op jit(solution)/shard_map/while/body/all_to_all | solution.py:27
  658.2 5.6 collective-permute-done.22
  663.7 5.6 collective-permute-done.21
  675.7 9.6 %collective-permute-start.26 = (bf16[4,128,128]{2,1,0:T(8,128)(2,1)}, bf16[4,128,128]{2,1,0:T(8,128)(2,1)}, u32[]{:S(2)}, u32[]{:S(2)}) collective-permute-start(bf16[4,128,128]{2,1,0:T(8,128)(2,1)} %bitcast.300), channel_id=1, source_target_pairs={{0,4},{2,12},{4,20},{6,28},{8,6},{10,14},{12,22},{14,30},{16,0},{1... | collective-permute-start | bytes 393224 | tf_op jit(solution)/shard_map/ppermute | solution.py:76
  690.9 6.1 collective-permute-start.33
  707.9 7.2 collective-permute-start.30
  721.4 7.6 %collective-permute-done.29 = bf16[2,4,128,128]{3,2,1,0:T(8,128)(2,1)S(1)} collective-permute-done((bf16[2,4,128,128]{3,2,1,0:T(8,128)(2,1)S(1)}, bf16[2,4,128,128]{3,2,1,0:T(8,128)(2,1)S(1)}, u32[]{:S(2)}, u32[]{:S(2)}) %collective-permute-start.29) | collective-permute-done | bytes 262176 | tf_op jit(solution)/shard_map/ppermute | solution.py:113
  (516 shorter events, 364.2 us)
Async XLA Ops:
  7.2 93.6 %all-gather.9.cloned.1.call-start = ((), (), s32[]{:S(2)}) async-start(), calls=%async_computation.40 | async-start | bytes 1310720 | tf_op jit(solution)/shard_map/all_gather | solution.py:121
  8.5 16.6 %collective-permute-start.3 = (bf16[4,128,128]{2,1,0:T(8,128)(2,1)S(1)}, bf16[4,128,128]{2,1,0:T(8,128)(2,1)S(1)}, u32[]{:S(2)}, u32[]{:S(2)}) collective-permute-start(bf16[4,128,128]{2,1,0:T(8,128)(2,1)S(1)} %get-tuple-element.994), channel_id=1, source_target_pairs={{0,24},{2,16},{4,8},{6,0},{8,26},{10,18},{12,10},{14,2},{16,28},{1... | collective-permute-start | bytes 393224 | tf_op jit(solution)/shard_map/ppermute | solution.py:76
  10.9 20.0 %collective-permute-start.2 = (bf16[4,128,128]{2,1,0:T(8,128)(2,1)S(1)}, bf16[4,128,128]{2,1,0:T(8,128)(2,1)S(1)}, u32[]{:S(2)}, u32[]{:S(2)}) collective-permute-start(bf16[4,128,128]{2,1,0:T(8,128)(2,1)S(1)} %get-tuple-element.995), channel_id=1, source_target_pairs={{0,16},{2,24},{4,0},{6,8},{8,18},{10,26},{12,2},{14,10},{16,20},{1... | collective-permute-start | bytes 393224 | tf_op jit(solution)/shard_map/ppermute | solution.py:76
  13.5 17.4 %collective-permute-start.1 = (bf16[4,128,128]{2,1,0:T(8,128)(2,1)S(1)}, bf16[4,128,128]{2,1,0:T(8,128)(2,1)S(1)}, u32[]{:S(2)}, u32[]{:S(2)}) collective-permute-start(bf16[4,128,128]{2,1,0:T(8,128)(2,1)S(1)} %get-tuple-element.996), channel_id=1, source_target_pairs={{0,8},{2,0},{4,24},{6,16},{8,10},{10,2},{12,26},{14,18},{16,12},{1... | collective-permute-start | bytes 393224 | tf_op jit(solution)/shard_map/ppermute | solution.py:76
  14.2 16.7 %collective-permute-start = (bf16[4,128,128]{2,1,0:T(8,128)(2,1)S(1)}, bf16[4,128,128]{2,1,0:T(8,128)(2,1)S(1)}, u32[]{:S(2)}, u32[]{:S(2)}) collective-permute-start(bf16[4,128,128]{2,1,0:T(8,128)(2,1)S(1)} %get-tuple-element.993), channel_id=1, source_target_pairs={{0,0},{2,8},{4,16},{6,24},{8,2},{10,10},{12,18},{14,26},{16,4},{18... | collective-permute-start | bytes 393224 | tf_op jit(solution)/shard_map/ppermute | solution.py:76
  18.3 13.3 %collective-permute-start.6 = (bf16[2,4,128,128]{2,3,1,0:T(8,128)(2,1)S(1)}, bf16[2,4,128,128]{2,3,1,0:T(8,128)(2,1)S(1)}, u32[]{:S(2)}, u32[]{:S(2)}) collective-permute-start(bf16[2,4,128,128]{2,3,1,0:T(8,128)(2,1)S(1)} %pad_maximum_fusion.29), channel_id=1, source_target_pairs={{0,24},{8,16},{16,8},{24,0},{1,25},{9,17},{17,9},{25,1},{2,26},{10... | collective-permute-start | bytes 786440 | tf_op jit(solution)/shard_map/ppermute | solution.py:113
  25.1 14.2 %collective-permute-start.5 = (bf16[2,4,128,128]{2,3,1,0:T(8,128)(2,1)S(1)}, bf16[2,4,128,128]{2,3,1,0:T(8,128)(2,1)S(1)}, u32[]{:S(2)}, u32[]{:S(2)}) collective-permute-start(bf16[2,4,128,128]{2,3,1,0:T(8,128)(2,1)S(1)} %pad_maximum_fusion.28), channel_id=1, source_target_pairs={{0,16},{8,24},{16,0},{24,8},{1,17},{9,25},{17,1},{25,9},{2,18},{10... | collective-permute-start | bytes 786440 | tf_op jit(solution)/shard_map/ppermute | solution.py:113
  43.7 15.9 %collective-permute-start.11 = (bf16[4,128,128]{2,1,0:T(8,128)(2,1)S(1)}, bf16[4,128,128]{2,1,0:T(8,128)(2,1)S(1)}, u32[]{:S(2)}, u32[]{:S(2)}) collective-permute-start(bf16[4,128,128]{2,1,0:T(8,128)(2,1)S(1)} %get-tuple-element.999), channel_id=1, source_target_pairs={{0,4},{2,6},{4,0},{6,2},{1,5},{3,7},{5,1},{7,3},{8,12},{10,14},{12... | collective-permute-start | bytes 393224 | tf_op jit(solution)/shard_map/ppermute | solution.py:126
  43.7 15.9 %collective-permute-start.10 = (bf16[4,128,128]{2,1,0:T(8,128)(2,1)S(1)}, bf16[4,128,128]{2,1,0:T(8,128)(2,1)S(1)}, u32[]{:S(2)}, u32[]{:S(2)}) collective-permute-start(bf16[4,128,128]{2,1,0:T(8,128)(2,1)S(1)} %get-tuple-element.999), channel_id=1, source_target_pairs={{0,2},{2,0},{4,6},{6,4},{1,3},{3,1},{5,7},{7,5},{8,10},{10,8},{12,... | collective-permute-start | bytes 393224 | tf_op jit(solution)/shard_map/ppermute | solution.py:126
  44.4 15.3 %collective-permute-start.9 = (bf16[4,128,128]{2,1,0:T(8,128)(2,1)S(1)}, bf16[4,128,128]{2,1,0:T(8,128)(2,1)S(1)}, u32[]{:S(2)}, u32[]{:S(2)}) collective-permute-start(bf16[4,128,128]{2,1,0:T(8,128)(2,1)S(1)} %get-tuple-element.998), channel_id=1, source_target_pairs={{0,6},{2,4},{4,2},{6,0},{1,7},{3,5},{5,3},{7,1},{8,14},{10,12},{12... | collective-permute-start | bytes 393224 | tf_op jit(solution)/shard_map/ppermute | solution.py:126
  48.1 16.8 %collective-permute-start.8 = (bf16[4,128,128]{2,1,0:T(8,128)(2,1)S(1)}, bf16[4,128,128]{2,1,0:T(8,128)(2,1)S(1)}, u32[]{:S(2)}, u32[]{:S(2)}) collective-permute-start(bf16[4,128,128]{2,1,0:T(8,128)(2,1)S(1)} %get-tuple-element.998), channel_id=1, source_target_pairs={{0,4},{2,6},{4,0},{6,2},{1,5},{3,7},{5,1},{7,3},{8,12},{10,14},{12... | collective-permute-start | bytes 393224 | tf_op jit(solution)/shard_map/ppermute | solution.py:126
  49.2 15.6 %collective-permute-start.7 = (bf16[4,128,128]{2,1,0:T(8,128)(2,1)S(1)}, bf16[4,128,128]{2,1,0:T(8,128)(2,1)S(1)}, u32[]{:S(2)}, u32[]{:S(2)}) collective-permute-start(bf16[4,128,128]{2,1,0:T(8,128)(2,1)S(1)} %get-tuple-element.998), channel_id=1, source_target_pairs={{0,2},{2,0},{4,6},{6,4},{1,3},{3,1},{5,7},{7,5},{8,10},{10,8},{12,... | collective-permute-start | bytes 393224 | tf_op jit(solution)/shard_map/ppermute | solution.py:126
  65.2 74.5 %all-gather.11.cloned.1.call-start = ((), (), s32[]{:S(2)}) async-start(), calls=%async_computation.41 | async-start | bytes 2621440 | tf_op jit(solution)/shard_map/all_gather | solution.py:121
  71.3 157.5 %all-gather.13.cloned.1.call-start = ((), (), s32[]{:S(2)}) async-start(), calls=%async_computation.42 | async-start | bytes 2621440 | tf_op jit(solution)/shard_map/all_gather | solution.py:121
  87.6 12.7 %all-to-all-start.1 = ((bf16[8,16,16,128]{3,1,2,0:T(8,128)(2,1)}), bf16[8,16,16,128]{3,1,2,0:T(8,128)(2,1)S(1)}, u32[]{:S(2)}, u32[]{:S(2)}) async-start(bf16[8,16,16,128]{3,1,2,0:T(8,128)(2,1)} %copy.465), calls=%async_computation.1 | async-start | bytes 1048576 | tf_op jit(solution)/shard_map/while/body/all_to_all | solution.py:27
  117.1 12.7 %all-to-all-start.3 = ((bf16[8,16,16,128]{3,1,2,0:T(8,128)(2,1)}), bf16[8,16,16,128]{3,1,2,0:T(8,128)(2,1)S(1)}, u32[]{:S(2)}, u32[]{:S(2)}) async-start(bf16[8,16,16,128]{3,1,2,0:T(8,128)(2,1)} %copy.469), calls=%async_computation.3 | async-start | bytes 1048576 | tf_op jit(solution)/shard_map/while/body/all_to_all | solution.py:27
  167.2 120.3 %all-gather.15.cloned.1.call-start = ((), (), s32[]{:S(2)}) async-start(), calls=%async_computation.43 | async-start | bytes 2621440 | tf_op jit(solution)/shard_map/all_gather | solution.py:121
  210.4 12.7 %all-to-all-start.7 = ((bf16[8,16,16,128]{3,1,2,0:T(8,128)(2,1)}), bf16[8,16,16,128]{3,1,2,0:T(8,128)(2,1)S(1)}, u32[]{:S(2)}, u32[]{:S(2)}) async-start(bf16[8,16,16,128]{3,1,2,0:T(8,128)(2,1)} %copy.477), calls=%async_computation.7 | async-start | bytes 1048576 | tf_op jit(solution)/shard_map/while/body/all_to_all | solution.py:27
  228.7 281.3 %reduce-scatter.5.cloned.1.call-start = ((), (), s32[]{:S(2)}) async-start(), calls=%async_computation.36 | async-start | bytes 2621440 | tf_op jit(solution)/shard_map/reduce_scatter | solution.py:137
  274.0 12.7 %all-to-all-start.11 = ((bf16[8,16,16,128]{3,1,2,0:T(8,128)(2,1)}), bf16[8,16,16,128]{3,1,2,0:T(8,128)(2,1)S(1)}, u32[]{:S(2)}, u32[]{:S(2)}) async-start(bf16[8,16,16,128]{3,1,2,0:T(8,128)(2,1)} %copy.485), calls=%async_computation.11 | async-start | bytes 1048576 | tf_op jit(solution)/shard_map/while/body/all_to_all | solution.py:27
  296.3 77.1 %collective-permute-start.16 = (bf16[4,128,128]{1,2,0:T(8,128)(2,1)S(1)}, bf16[4,128,128]{1,2,0:T(8,128)(2,1)}, u32[]{:S(2)}, u32[]{:S(2)}) collective-permute-start(bf16[4,128,128]{1,2,0:T(8,128)(2,1)S(1)} %bitcast.1462), channel_id=1, source_target_pairs={{0,0},{2,8},{4,16},{6,24},{8,2},{10,10},{12,18},{14,26},{16,4},{18... | collective-permute-start | bytes 393224 | tf_op jit(solution)/shard_map/ppermute | solution.py:76
  298.4 75.0 %collective-permute-start.17 = (bf16[4,128,128]{1,2,0:T(8,128)(2,1)}, bf16[4,128,128]{1,2,0:T(8,128)(2,1)}, u32[]{:S(2)}, u32[]{:S(2)}) collective-permute-start(bf16[4,128,128]{1,2,0:T(8,128)(2,1)} %bitcast.270), channel_id=1, source_target_pairs={{0,8},{2,0},{4,24},{6,16},{8,10},{10,2},{12,26},{14,18},{16,12},{1... | collective-permute-start | bytes 393224 | tf_op jit(solution)/shard_map/ppermute | solution.py:76
  299.4 74.0 %collective-permute-start.18 = (bf16[4,128,128]{1,2,0:T(8,128)(2,1)}, bf16[4,128,128]{1,2,0:T(8,128)(2,1)}, u32[]{:S(2)}, u32[]{:S(2)}) collective-permute-start(bf16[4,128,128]{1,2,0:T(8,128)(2,1)} %bitcast.271), channel_id=1, source_target_pairs={{0,16},{2,24},{4,0},{6,8},{8,18},{10,26},{12,2},{14,10},{16,20},{1... | collective-permute-start | bytes 393224 | tf_op jit(solution)/shard_map/ppermute | solution.py:76
  302.5 71.0 %collective-permute-start.19 = (bf16[4,128,128]{1,2,0:T(8,128)(2,1)S(1)}, bf16[4,128,128]{1,2,0:T(8,128)(2,1)S(1)}, u32[]{:S(2)}, u32[]{:S(2)}) collective-permute-start(bf16[4,128,128]{1,2,0:T(8,128)(2,1)S(1)} %bitcast.1463), channel_id=1, source_target_pairs={{0,24},{2,16},{4,8},{6,0},{8,26},{10,18},{12,10},{14,2},{16,28},{1... | collective-permute-start | bytes 393224 | tf_op jit(solution)/shard_map/ppermute | solution.py:76
  351.7 13.4 %all-to-all-start.15 = ((bf16[8,16,16,128]{3,1,2,0:T(8,128)(2,1)}), bf16[8,16,16,128]{3,1,2,0:T(8,128)(2,1)}, u32[]{:S(2)}, u32[]{:S(2)}) async-start(bf16[8,16,16,128]{3,1,2,0:T(8,128)(2,1)} %copy.493), calls=%async_computation.15 | async-start | bytes 1048576 | tf_op jit(solution)/shard_map/while/body/all_to_all | solution.py:27
  378.8 12.7 %all-to-all-start.16 = ((bf16[8,16,16,128]{3,2,1,0:T(8,128)(2,1)}), bf16[8,16,16,128]{3,2,1,0:T(8,128)(2,1)S(1)}, u32[]{:S(2)}, u32[]{:S(2)}) async-start(bf16[8,16,16,128]{3,2,1,0:T(8,128)(2,1)} %bitcast.1134), calls=%async_computation.16 | async-start | bytes 1048576 | tf_op jit(solution)/shard_map/while/body/all_to_all | solution.py:27
  406.5 12.7 %all-to-all-start.18 = ((bf16[8,16,16,128]{3,1,2,0:T(8,128)(2,1)}), bf16[8,16,16,128]{3,1,2,0:T(8,128)(2,1)S(1)}, u32[]{:S(2)}, u32[]{:S(2)}) async-start(bf16[8,16,16,128]{3,1,2,0:T(8,128)(2,1)} %copy.498), calls=%async_computation.18 | async-start | bytes 1048576 | tf_op jit(solution)/shard_map/while/body/all_to_all | solution.py:27
  422.3 12.7 %all-to-all-start.19 = ((bf16[8,16,16,128]{3,2,1,0:T(8,128)(2,1)}), bf16[8,16,16,128]{3,2,1,0:T(8,128)(2,1)S(1)}, u32[]{:S(2)}, u32[]{:S(2)}) async-start(bf16[8,16,16,128]{3,2,1,0:T(8,128)(2,1)} %copy.500), calls=%async_computation.19 | async-start | bytes 1048576 | tf_op jit(solution)/shard_map/while/body/all_to_all | solution.py:27
  442.7 133.2 %reduce-scatter.7.cloned.1.call-start = ((), (), s32[]{:S(2)}) async-start(), calls=%async_computation.37 | async-start | bytes 2621440 | tf_op jit(solution)/shard_map/reduce_scatter | solution.py:137
  445.9 12.7 %all-to-all-start.20 = ((bf16[8,16,16,128]{3,2,1,0:T(8,128)(2,1)}), bf16[8,16,16,128]{3,2,1,0:T(8,128)(2,1)S(1)}, u32[]{:S(2)}, u32[]{:S(2)}) async-start(bf16[8,16,16,128]{3,2,1,0:T(8,128)(2,1)} %bitcast.1174), calls=%async_computation.20 | async-start | bytes 1048576 | tf_op jit(solution)/shard_map/while/body/all_to_all | solution.py:27
  473.7 12.7 %all-to-all-start.22 = ((bf16[8,16,16,128]{3,1,2,0:T(8,128)(2,1)}), bf16[8,16,16,128]{3,1,2,0:T(8,128)(2,1)S(1)}, u32[]{:S(2)}, u32[]{:S(2)}) async-start(bf16[8,16,16,128]{3,1,2,0:T(8,128)(2,1)} %copy.508), calls=%async_computation.22 | async-start | bytes 1048576 | tf_op jit(solution)/shard_map/while/body/all_to_all | solution.py:27
  489.5 12.7 %all-to-all-start.23 = ((bf16[8,16,16,128]{3,2,1,0:T(8,128)(2,1)}), bf16[8,16,16,128]{3,2,1,0:T(8,128)(2,1)S(1)}, u32[]{:S(2)}, u32[]{:S(2)}) async-start(bf16[8,16,16,128]{3,2,1,0:T(8,128)(2,1)} %copy.510), calls=%async_computation.23 | async-start | bytes 1048576 | tf_op jit(solution)/shard_map/while/body/all_to_all | solution.py:27
  509.9 194.2 %reduce-scatter.11.cloned.1.call-start = ((), (), s32[]{:S(2)}) async-start(), calls=%async_computation.39 | async-start | bytes 2621440 | tf_op jit(solution)/shard_map/reduce_scatter | solution.py:137
  516.2 12.7 %all-to-all-start.24 = ((bf16[8,16,16,128]{3,2,1,0:T(8,128)(2,1)}), bf16[8,16,16,128]{3,2,1,0:T(8,128)(2,1)S(1)}, u32[]{:S(2)}, u32[]{:S(2)}) async-start(bf16[8,16,16,128]{3,2,1,0:T(8,128)(2,1)} %bitcast.1214), calls=%async_computation.24 | async-start | bytes 1048576 | tf_op jit(solution)/shard_map/while/body/all_to_all | solution.py:27
  543.9 12.7 %all-to-all-start.26 = ((bf16[8,16,16,128]{3,1,2,0:T(8,128)(2,1)}), bf16[8,16,16,128]{3,1,2,0:T(8,128)(2,1)S(1)}, u32[]{:S(2)}, u32[]{:S(2)}) async-start(bf16[8,16,16,128]{3,1,2,0:T(8,128)(2,1)} %copy.518), calls=%async_computation.26 | async-start | bytes 1048576 | tf_op jit(solution)/shard_map/while/body/all_to_all | solution.py:27
  559.7 12.7 %all-to-all-start.27 = ((bf16[8,16,16,128]{3,2,1,0:T(8,128)(2,1)}), bf16[8,16,16,128]{3,2,1,0:T(8,128)(2,1)S(1)}, u32[]{:S(2)}, u32[]{:S(2)}) async-start(bf16[8,16,16,128]{3,2,1,0:T(8,128)(2,1)} %copy.520), calls=%async_computation.27 | async-start | bytes 1048576 | tf_op jit(solution)/shard_map/while/body/all_to_all | solution.py:27
  582.6 123.3 %reduce-scatter.9.cloned.1.call-start = ((), (), s32[]{:S(2)}) async-start(), calls=%async_computation.38 | async-start | bytes 2621440 | tf_op jit(solution)/shard_map/reduce_scatter | solution.py:137
  652.5 16.8 %collective-permute-start.21 = (bf16[4,128,128]{2,1,0:T(8,128)(2,1)S(1)}, bf16[4,128,128]{2,1,0:T(8,128)(2,1)S(1)}, u32[]{:S(2)}, u32[]{:S(2)}) collective-permute-start(bf16[4,128,128]{2,1,0:T(8,128)(2,1)S(1)} %bitcast.1467), channel_id=1, source_target_pairs={{0,2},{2,10},{4,18},{6,26},{8,0},{10,8},{12,16},{14,24},{16,6},{18... | collective-permute-start | bytes 393224 | tf_op jit(solution)/shard_map/ppermute | solution.py:76
  653.3 16.0 %collective-permute-start.20 = (bf16[4,128,128]{2,1,0:T(8,128)(2,1)S(1)}, bf16[4,128,128]{2,1,0:T(8,128)(2,1)S(1)}, u32[]{:S(2)}, u32[]{:S(2)}) collective-permute-start(bf16[4,128,128]{2,1,0:T(8,128)(2,1)S(1)} %bitcast.1468), channel_id=1, source_target_pairs={{0,0},{2,8},{4,16},{6,24},{8,2},{10,10},{12,18},{14,26},{16,4},{18... | collective-permute-start | bytes 393224 | tf_op jit(solution)/shard_map/ppermute | solution.py:76
  671.0 26.1 %collective-permute-start.27 = (bf16[4,128,128]{2,1,0:T(8,128)(2,1)}, bf16[4,128,128]{2,1,0:T(8,128)(2,1)}, u32[]{:S(2)}, u32[]{:S(2)}) collective-permute-start(bf16[4,128,128]{2,1,0:T(8,128)(2,1)} %bitcast.302), channel_id=1, source_target_pairs={{0,6},{2,14},{4,22},{6,30},{8,4},{10,12},{12,20},{14,28},{16,2},{1... | collective-permute-start | bytes 393224 | tf_op jit(solution)/shard_map/ppermute | solution.py:76
  675.7 26.4 %collective-permute-start.26 = (bf16[4,128,128]{2,1,0:T(8,128)(2,1)}, bf16[4,128,128]{2,1,0:T(8,128)(2,1)}, u32[]{:S(2)}, u32[]{:S(2)}) collective-permute-start(bf16[4,128,128]{2,1,0:T(8,128)(2,1)} %bitcast.300), channel_id=1, source_target_pairs={{0,4},{2,12},{4,20},{6,28},{8,6},{10,14},{12,22},{14,30},{16,0},{1... | collective-permute-start | bytes 393224 | tf_op jit(solution)/shard_map/ppermute | solution.py:76
  685.4 16.6 %collective-permute-start.25 = (bf16[4,128,128]{2,1,0:T(8,128)(2,1)S(1)}, bf16[4,128,128]{2,1,0:T(8,128)(2,1)}, u32[]{:S(2)}, u32[]{:S(2)}) collective-permute-start(bf16[4,128,128]{2,1,0:T(8,128)(2,1)S(1)} %bitcast.1464), channel_id=1, source_target_pairs={{0,2},{2,10},{4,18},{6,26},{8,0},{10,8},{12,16},{14,24},{16,6},{18... | collective-permute-start | bytes 393224 | tf_op jit(solution)/shard_map/ppermute | solution.py:76
  688.7 13.4 %collective-permute-start.24 = (bf16[4,128,128]{2,1,0:T(8,128)(2,1)}, bf16[4,128,128]{2,1,0:T(8,128)(2,1)S(1)}, u32[]{:S(2)}, u32[]{:S(2)}) collective-permute-start(bf16[4,128,128]{2,1,0:T(8,128)(2,1)} %bitcast.296), channel_id=1, source_target_pairs={{0,0},{2,8},{4,16},{6,24},{8,2},{10,10},{12,18},{14,26},{16,4},{18... | collective-permute-start | bytes 393224 | tf_op jit(solution)/shard_map/ppermute | solution.py:76
  690.9 28.2 %collective-permute-start.33 = (bf16[2,4,128,128]{3,2,1,0:T(8,128)(2,1)S(1)}, bf16[2,4,128,128]{3,2,1,0:T(8,128)(2,1)S(1)}, u32[]{:S(2)}, u32[]{:S(2)}) collective-permute-start(bf16[2,4,128,128]{3,2,1,0:T(8,128)(2,1)S(1)} %pad_maximum_fusion.38), channel_id=1, source_target_pairs={{0,24},{8,16},{16,8},{24,0},{1,25},{9,17},{17,9},{25,1},{2,26},{10... | collective-permute-start | bytes 786440 | tf_op jit(solution)/shard_map/ppermute | solution.py:113
  697.1 23.0 %collective-permute-start.32 = (bf16[2,4,128,128]{3,2,1,0:T(8,128)(2,1)S(1)}, bf16[2,4,128,128]{3,2,1,0:T(8,128)(2,1)}, u32[]{:S(2)}, u32[]{:S(2)}) collective-permute-start(bf16[2,4,128,128]{3,2,1,0:T(8,128)(2,1)S(1)} %pad_maximum_fusion.37), channel_id=1, source_target_pairs={{0,16},{8,24},{16,0},{24,8},{1,17},{9,25},{17,1},{25,9},{2,18},{10... | collective-permute-start | bytes 786440 | tf_op jit(solution)/shard_map/ppermute | solution.py:113
  702.0 18.1 %collective-permute-start.31 = (bf16[2,4,128,128]{3,2,1,0:T(8,128)(2,1)S(1)}, bf16[2,4,128,128]{3,2,1,0:T(8,128)(2,1)}, u32[]{:S(2)}, u32[]{:S(2)}) collective-permute-start(bf16[2,4,128,128]{3,2,1,0:T(8,128)(2,1)S(1)} %pad_maximum_fusion.36), channel_id=1, source_target_pairs={{0,8},{8,0},{16,24},{24,16},{1,9},{9,1},{17,25},{25,17},{2,10},{10... | collective-permute-start | bytes 786440 | tf_op jit(solution)/shard_map/ppermute | solution.py:113
  707.9 13.5 %collective-permute-start.30 = (bf16[2,4,128,128]{3,2,1,0:T(8,128)(2,1)S(1)}, bf16[2,4,128,128]{3,2,1,0:T(8,128)(2,1)S(1)}, u32[]{:S(2)}, u32[]{:S(2)}) collective-permute-start(bf16[2,4,128,128]{3,2,1,0:T(8,128)(2,1)S(1)} %pad_maximum_fusion.35), channel_id=1, source_target_pairs={{0,24},{8,16},{16,8},{24,0},{1,25},{9,17},{17,9},{25,1},{2,26},{10... | collective-permute-start | bytes 786440 | tf_op jit(solution)/shard_map/ppermute | solution.py:113
  715.1 13.9 %collective-permute-start.29 = (bf16[2,4,128,128]{3,2,1,0:T(8,128)(2,1)S(1)}, bf16[2,4,128,128]{3,2,1,0:T(8,128)(2,1)S(1)}, u32[]{:S(2)}, u32[]{:S(2)}) collective-permute-start(bf16[2,4,128,128]{3,2,1,0:T(8,128)(2,1)S(1)} %pad_maximum_fusion.34), channel_id=1, source_target_pairs={{0,16},{8,24},{16,0},{24,8},{1,17},{9,25},{17,1},{25,9},{2,18},{10... | collective-permute-start | bytes 786440 | tf_op jit(solution)/shard_map/ppermute | solution.py:113
  (67 other events, 790.9 us)
Sparse Core Ops, SparseCore 0:
  65.4 27.2 all-gather.8
  94.3 45.4 all-gather.10
  167.3 44.5 all-gather.12
  228.8 43.2 all-gather.14
  442.9 40.7 reduce-scatter.4
  510.0 40.7 reduce-scatter.6
  582.7 40.7 reduce-scatter.10
  649.7 54.6 reduce-scatter.8

commit v18 on v16

--- a/solution.py
+++ b/solution.py
@@ -100,14 +100,20 @@
         parts = turned(parts.reshape(sections, sub, size, rows), s_index, line, outof)
         return parts.reshape(1, held * size, rows)
 
-    def scattered(*kinds):
+    def dealt(*kinds):
         moved = [jnp.stack([pick(parts, s_index) for parts in kinds])]
         for mask in range(1, sections):
             pairs = [(s, s ^ mask) for s in range(sections)]
             value = jnp.stack([pick(parts, s_index ^ mask) for parts in kinds])
             moved.append(lax.ppermute(value, "s", pairs))
+        return moved
+
+    def collected(moved):
         moved = jnp.stack(moved)
         return [pick(moved, s_index ^ section) for section in range(sections)]
+
+    def scattered(*kinds):
+        return collected(dealt(*kinds))
 
     def ordered(part):
         return jnp.einsum("aj,fbjk,ck->fbac", order, part, order, preferred_element_type=F32).astype(BF16)
@@ -169,10 +175,9 @@
         full = ahead if begin else first
         if begin:
             coming = range(end, min(end + PAIRED, layers))
-            if begin == PAIRED:
+            if begin == 1:
                 current, rights, lefts = lax.optimization_barrier((current, rights[1:], lefts[1:]))
-                for loop in range(loops - 1):
-                    parts.extend(ordered(part) for part in scattered(rights[loop], lefts[loop]))
+                moving = [dealt(rights[loop], lefts[loop]) for loop in range(loops - 1)]
             if coming:
                 ahead = gathered(jnp.stack([parts[layer] for layer in coming]))
         weights.update((layer, (full, layer - begin)) for layer in stretch)
@@ -180,6 +185,9 @@
         entered = current
         current, *saved = lax.fori_loop(0, once, forward_stretch(stretch), (current, *blanks))
         current, ahead = lax.optimization_barrier((current, ahead))
+        if begin == 1:
+            current, moving = lax.optimization_barrier((current, moving))
+            parts.extend(ordered(part) for moved in moving for part in collected(moved))
         saved = [entered] + saved
         stored.update((layer, saved[2 * step : 2 * step + 2]) for step, layer in enumerate(stretch))
     current, cotangent = lax.optimization_barrier((current, cotangent))

time: 747 us -> 731 us (0.979)
  waiting for transfers between devices: 203 us -> 181 us
    ppermute x12, waiting for transfers between devices: 37.6 us -> 25.9 us  [dealt(): moved.append(lax.ppermute(value, 's', pairs))]
    all_gather x4, waiting for transfers between devices: 11.9 us -> 1.23 us  [gathered(): return lax.all_gather(part, 't', axis=0, tiled=False)]
  transfers between devices with their start and end apart: 59 -> 59, of which waited for: 32 -> 30; matrix products, arithmetic and copies ran while one was open for 22% -> 23% of each run, Pallas kernels for 0% -> 0%
where the time goes in v18:
time: 731 us; the launch traced here: 718 us
  blocking collectives  182 us (25%)
  waiting for transfers between devices  181 us (25%)
  local copies, waits for them, and re-layouts  124 us (17%)
  starting transfers between devices  122 us (17%)
  matrix products  62.7 us (9%)
  other arithmetic  28.5 us (4%)
  between operations  15.8 us (2%)
    all_to_all x15, blocking collectives, exchange(): lax.all_to_all(pieces, WIDE, split_axis=0, concat_axis=0, tiled=True)  182 us
    all_to_all x17, waiting for transfers between devices, exchange(): lax.all_to_all(pieces, WIDE, split_axis=0, concat_axis=0, tiled=True)  117 us
    all_to_all x17, starting transfers between devices, exchange(): lax.all_to_all(pieces, WIDE, split_axis=0, concat_axis=0, tiled=True)  64.1 us
    ppermute x12, starting transfers between devices, dealt(): moved.append(lax.ppermute(value, 's', pairs))  33 us
    ppermute x12, waiting for transfers between devices, dealt(): moved.append(lax.ppermute(value, 's', pairs))  25.9 us
    ppermute x16, waiting for transfers between devices, turned(): moved.append(lax.ppermute(pick(parts, send_by ^ mask), ('s', 't'), pairs))  23.6 us
    while x15, local copies, waits for them, and re-layouts, body(): grad, terms = lax.fori_loop(0, once, backward_pair(top), (grad, blank))  21.6 us
    another operation x15, local copies, waits for them, and re-layouts  17 us
  transfers between devices with their start and end apart: 59, of which 30 were waited for; matrix products, arithmetic and copies ran while one was open for 23% of the time, Pallas kernels for 0%

profile of v18, /device:TPU:0, one launch (start us, length us, event | category | flops | bytes accessed | tf_op | source)
XLA Modules:
  0.0 717.5 jit_solution(1567821930141524712)
XLA Ops:
  18.3 5.7 collective-permute-start.6
  25.6 5.4 collective-permute-done.2
  31.5 7.7 %collective-permute-done.5 = bf16[2,4,128,128]{2,3,1,0:T(8,128)(2,1)S(1)} collective-permute-done((bf16[2,4,128,128]{2,3,1,0:T(8,128)(2,1)S(1)}, bf16[2,4,128,128]{2,3,1,0:T(8,128)(2,1)S(1)}, u32[]{:S(2)}, u32[]{:S(2)}) %collective-permute-start.5) | collective-permute-done | bytes 262176 | tf_op jit(solution)/shard_map/ppermute | solution.py:108
  51.7 7.9 %collective-permute-done.11 = bf16[4,128,128]{2,1,0:T(8,128)(2,1)S(1)} collective-permute-done((bf16[4,128,128]{2,1,0:T(8,128)(2,1)S(1)}, bf16[4,128,128]{2,1,0:T(8,128)(2,1)S(1)}, u32[]{:S(2)}, u32[]{:S(2)}) %collective-permute-start.11) | collective-permute-done | bytes 131104 | tf_op jit(solution)/shard_map/ppermute | solution.py:127
  71.0 27.8 %while.131 = (s32[]{:T(128)}, bf16[16,128,128]{2,1,0:T(8,128)(2,1)S(1)}, bf16[16,128,128]{2,0,1:T(8,128)(2,1)}, s32[]{:T(128)}, bf16[4,1,2,4,128,128]{4,5,3,0,2,1:T(8,128)(2,1)S(1)}, /*index=5*/s32[]{:T(128)}) while((s32[]{:T(128)}, bf16[16,128,128]{2,1,0:T(8,128)(2,1)S(1)}, bf16[16,128,128]{2,0,1:T(8,128)(2,1)}, s32[]{:T(128)}, ...), condition=%wide.region_1.2_spmd, body=%wide.region_0.1_spmd.sunk | while | flops 137363456 | bytes 16777344 | solution.py:186
  71.5 12.7 %all_to_all.192 = bf16[8,16,16,128]{3,1,2,0:T(8,128)(2,1)S(1)} all-to-all(bf16[8,16,16,128]{3,1,2,0:T(8,128)(2,1)S(1)} %copy.464), channel_id=1, replica_groups=mesh['s'=4,'t'=4,'x'=2] {'s','x'}, dimensions={0} | all-to-all | bytes 1048576 | tf_op jit(solution)/shard_map/while/body/all_to_all | solution.py:27
  89.2 9.2 %all-to-all-done.1 = bf16[8,16,16,128]{3,1,2,0:T(8,128)(2,1)S(1)} async-done(((bf16[8,16,16,128]{3,1,2,0:T(8,128)(2,1)}), bf16[8,16,16,128]{3,1,2,0:T(8,128)(2,1)S(1)}, u32[]{:S(2)}, u32[]{:S(2)}) %all-to-all-start.1) | async-done | bytes 524320 | tf_op jit(solution)/shard_map/while/body/all_to_all | solution.py:27
  108.0 31.1 %while.132 = (s32[]{:T(128)}, bf16[16,128,128]{2,1,0:T(8,128)(2,1)S(1)}, bf16[16,128,128]{2,0,1:T(8,128)(2,1)}, s32[]{:T(128)}, bf16[4,1,2,4,128,128]{4,5,3,0,2,1:T(8,128)(2,1)S(1)}, /*index=5*/s32[]{:T(128)}) while((s32[]{:T(128)}, bf16[16,128,128]{2,1,0:T(8,128)(2,1)S(1)}, bf16[16,128,128]{2,0,1:T(8,128)(2,1)}, s32[]{:T(128)}, ...), condition=%wide.region_3.4_spmd, body=%wide.region_2.3_spmd.sunk | while | flops 137363456 | bytes 16777344 | solution.py:186
  108.5 16.0 %all_to_all.193 = bf16[8,16,16,128]{3,1,2,0:T(8,128)(2,1)S(1)} all-to-all(bf16[8,16,16,128]{3,1,2,0:T(8,128)(2,1)S(1)} %copy.468), channel_id=1, replica_groups=mesh['s'=4,'t'=4,'x'=2] {'s','x'}, dimensions={0} | all-to-all | bytes 1048576 | tf_op jit(solution)/shard_map/while/body/all_to_all | solution.py:27
  129.4 9.2 %all-to-all-done.3 = bf16[8,16,16,128]{3,1,2,0:T(8,128)(2,1)S(1)} async-done(((bf16[8,16,16,128]{3,1,2,0:T(8,128)(2,1)}), bf16[8,16,16,128]{3,1,2,0:T(8,128)(2,1)S(1)}, u32[]{:S(2)}, u32[]{:S(2)}) %all-to-all-start.3) | async-done | bytes 524320 | tf_op jit(solution)/shard_map/while/body/all_to_all | solution.py:27
  152.3 54.3 %while.133 = (s32[]{:T(128)}, bf16[16,128,128]{2,1,0:T(8,128)(2,1)S(1)}, bf16[16,128,128]{2,0,1:T(8,128)(2,1)}, bf16[16,128,128]{2,1,0:T(8,128)(2,1)}, bf16[16,1...) while((s32[]{:T(128)}, bf16[16,128,128]{2,1,0:T(8,128)(2,1)S(1)}, ...), condition=%wide.region_5.6_spmd, body=%wide.region_4.5_spmd.sunk | while | flops 274726912 | bytes 35127496 | solution.py:186
  154.3 12.7 %all_to_all.194 = bf16[8,16,16,128]{3,1,2,0:T(8,128)(2,1)S(1)} all-to-all(bf16[8,16,16,128]{3,1,2,0:T(8,128)(2,1)S(1)} %copy.474), channel_id=1, replica_groups=mesh['s'=4,'t'=4,'x'=2] {'s','x'}, dimensions={0} | all-to-all | bytes 1048576 | tf_op jit(solution)/shard_map/while/body/all_to_all | solution.py:27
  167.7 11.7 %all_to_all.195 = bf16[8,16,16,128]{3,1,2,0:T(8,128)(2,1)S(1)} all-to-all(bf16[8,16,16,128]{3,1,2,0:T(8,128)(2,1)S(1)} %copy.475), channel_id=1, replica_groups=mesh['s'=4,'t'=4,'x'=2] {'s','x'}, dimensions={0} | all-to-all | bytes 1048576 | tf_op jit(solution)/shard_map/while/body/all_to_all | solution.py:27
  180.2 11.7 %all_to_all.196 = bf16[8,16,16,128]{3,1,2,0:T(8,128)(2,1)S(1)} all-to-all(bf16[8,16,16,128]{3,1,2,0:T(8,128)(2,1)S(1)} %copy.476), channel_id=1, replica_groups=mesh['s'=4,'t'=4,'x'=2] {'s','x'}, dimensions={0} | all-to-all | bytes 1048576 | tf_op jit(solution)/shard_map/while/body/all_to_all | solution.py:27
  196.9 9.2 %all-to-all-done.7 = bf16[8,16,16,128]{3,1,2,0:T(8,128)(2,1)S(1)} async-done(((bf16[8,16,16,128]{3,1,2,0:T(8,128)(2,1)}), bf16[8,16,16,128]{3,1,2,0:T(8,128)(2,1)S(1)}, u32[]{:S(2)}, u32[]{:S(2)}) %all-to-all-start.7) | async-done | bytes 524320 | tf_op jit(solution)/shard_map/while/body/all_to_all | solution.py:27
  213.5 53.3 %while.134 = (s32[]{:T(128)}, bf16[16,128,128]{2,1,0:T(8,128)(2,1)S(1)}, bf16[16,128,128]{2,0,1:T(8,128)(2,1)}, bf16[16,128,128]{2,1,0:T(8,128)(2,1)}, bf16[16,1...) while((s32[]{:T(128)}, bf16[16,128,128]{2,1,0:T(8,128)(2,1)S(1)}, ...), condition=%wide.region_7.8_spmd, body=%wide.region_6.7_spmd.sunk | while | flops 274726912 | bytes 35127496 | solution.py:186
  215.5 11.7 %all_to_all.197 = bf16[8,16,16,128]{3,1,2,0:T(8,128)(2,1)S(1)} all-to-all(bf16[8,16,16,128]{3,1,2,0:T(8,128)(2,1)S(1)} %copy.482), channel_id=1, replica_groups=mesh['s'=4,'t'=4,'x'=2] {'s','x'}, dimensions={0} | all-to-all | bytes 1048576 | tf_op jit(solution)/shard_map/while/body/all_to_all | solution.py:27
  227.9 11.7 %all_to_all.198 = bf16[8,16,16,128]{3,1,2,0:T(8,128)(2,1)S(1)} all-to-all(bf16[8,16,16,128]{3,1,2,0:T(8,128)(2,1)S(1)} %copy.483), channel_id=1, replica_groups=mesh['s'=4,'t'=4,'x'=2] {'s','x'}, dimensions={0} | all-to-all | bytes 1048576 | tf_op jit(solution)/shard_map/while/body/all_to_all | solution.py:27
  240.4 11.7 %all_to_all.199 = bf16[8,16,16,128]{3,1,2,0:T(8,128)(2,1)S(1)} all-to-all(bf16[8,16,16,128]{3,1,2,0:T(8,128)(2,1)S(1)} %copy.484), channel_id=1, replica_groups=mesh['s'=4,'t'=4,'x'=2] {'s','x'}, dimensions={0} | all-to-all | bytes 1048576 | tf_op jit(solution)/shard_map/while/body/all_to_all | solution.py:27
  257.1 9.2 %all-to-all-done.11 = bf16[8,16,16,128]{3,1,2,0:T(8,128)(2,1)S(1)} async-done(((bf16[8,16,16,128]{3,1,2,0:T(8,128)(2,1)}), bf16[8,16,16,128]{3,1,2,0:T(8,128)(2,1)S(1)}, u32[]{:S(2)}, u32[]{:S(2)}) %all-to-all-start.11) | async-done | bytes 524320 | tf_op jit(solution)/shard_map/while/body/all_to_all | solution.py:27
  273.3 57.6 %while.135 = (s32[]{:T(128)}, bf16[16,128,128]{2,1,0:T(8,128)(2,1)}, bf16[16,128,128]{2,0,1:T(8,128)(2,1)}, bf16[16,128,128]{2,1,0:T(8,128)(2,1)}, bf16[16,128,1...) while((s32[]{:T(128)}, bf16[16,128,128]{2,1,0:T(8,128)(2,1)}, ...), condition=%wide.region_9.10_spmd, body=%wide.region_8.9_spmd.sunk | while | flops 274726912 | bytes 35127496 | solution.py:186
  275.2 11.7 %all_to_all.200 = bf16[8,16,16,128]{3,1,2,0:T(8,128)(2,1)S(1)} all-to-all(bf16[8,16,16,128]{3,1,2,0:T(8,128)(2,1)S(1)} %copy.490), channel_id=1, replica_groups=mesh['s'=4,'t'=4,'x'=2] {'s','x'}, dimensions={0} | all-to-all | bytes 1048576 | tf_op jit(solution)/shard_map/while/body/all_to_all | solution.py:27
  288.0 11.7 %all_to_all.201 = bf16[8,16,16,128]{3,1,2,0:T(8,128)(2,1)S(1)} all-to-all(bf16[8,16,16,128]{3,1,2,0:T(8,128)(2,1)S(1)} %copy.491), channel_id=1, replica_groups=mesh['s'=4,'t'=4,'x'=2] {'s','x'}, dimensions={0} | all-to-all | bytes 1048576 | tf_op jit(solution)/shard_map/while/body/all_to_all | solution.py:27
  301.5 11.7 %all_to_all.202 = bf16[8,16,16,128]{3,1,2,0:T(8,128)(2,1)S(1)} all-to-all(bf16[8,16,16,128]{3,1,2,0:T(8,128)(2,1)S(1)} %copy.492), channel_id=1, replica_groups=mesh['s'=4,'t'=4,'x'=2] {'s','x'}, dimensions={0} | all-to-all | bytes 1048576 | tf_op jit(solution)/shard_map/while/body/all_to_all | solution.py:27
  319.3 9.3 %all-to-all-done.15 = bf16[8,16,16,128]{3,1,2,0:T(8,128)(2,1)} async-done(((bf16[8,16,16,128]{3,1,2,0:T(8,128)(2,1)}), bf16[8,16,16,128]{3,1,2,0:T(8,128)(2,1)}, u32[]{:S(2)}, u32[]{:S(2)}) %all-to-all-start.15) | async-done | bytes 524320 | tf_op jit(solution)/shard_map/while/body/all_to_all | solution.py:27
  356.1 65.5 %while.136 = (s32[]{:T(128)}, bf16[16,128,128]{2,1,0:T(8,128)(2,1)S(1)}, bf16[4,4,4,128,128]{3,4,2,0,1:T(8,128)(2,1)}, s32[]{:T(128)}, bf16[4,2,2,4,128,128]{5,4...) while((s32[]{:T(128)}, ...), condition=%wide.region_11.12_spmd, body=%wide.region_10.11_spmd.sunk | while | flops 551026688 | bytes 51904876 | solution.py:213
  357.7 7.5 %all-to-all-start.16 = ((bf16[8,16,16,128]{3,2,1,0:T(8,128)(2,1)}), bf16[8,16,16,128]{3,2,1,0:T(8,128)(2,1)S(1)}, u32[]{:S(2)}, u32[]{:S(2)}) async-start(bf16[8,16,16,128]{3,2,1,0:T(8,128)(2,1)} %bitcast.1137), calls=%async_computation.16 | async-start | bytes 1048576 | tf_op jit(solution)/shard_map/while/body/all_to_all | solution.py:27
  367.9 6.6 all-to-all-done.16
  376.5 11.7 %all_to_all.203 = bf16[8,16,16,128]{3,1,2,0:T(8,128)(2,1)S(1)} all-to-all(bf16[8,16,16,128]{3,1,2,0:T(8,128)(2,1)S(1)} %copy.496), channel_id=1, replica_groups=mesh['s'=4,'t'=4,'x'=2] {'s','x'}, dimensions={0} | all-to-all | bytes 1048576 | tf_op jit(solution)/shard_map/while/body/all_to_all | solution.py:27
  411.9 6.1 all-to-all-done.19
  427.6 61.1 %while.137 = (s32[]{:T(128)}, bf16[16,128,128]{2,1,0:T(8,128)(2,1)S(1)}, bf16[4,4,4,128,128]{3,4,2,0,1:T(8,128)(2,1)}, s32[]{:T(128)}, bf16[4,2,2,4,128,128]{5,4...) while((s32[]{:T(128)}, ...), condition=%wide.region_13.14_spmd, body=%wide.region_12.13_spmd.sunk | while | flops 551026688 | bytes 51904876 | solution.py:213
  435.2 6.4 all-to-all-done.20
  443.7 11.7 %all_to_all.204 = bf16[8,16,16,128]{3,1,2,0:T(8,128)(2,1)S(1)} all-to-all(bf16[8,16,16,128]{3,1,2,0:T(8,128)(2,1)S(1)} %copy.506), channel_id=1, replica_groups=mesh['s'=4,'t'=4,'x'=2] {'s','x'}, dimensions={0} | all-to-all | bytes 1048576 | tf_op jit(solution)/shard_map/while/body/all_to_all | solution.py:27
  479.2 6.0 all-to-all-done.23
  497.8 61.1 %while.138 = (s32[]{:T(128)}, bf16[16,128,128]{2,1,0:T(8,128)(2,1)S(1)}, bf16[4,4,4,128,128]{3,4,2,0,1:T(8,128)(2,1)}, s32[]{:T(128)}, bf16[4,2,2,4,128,128]{5,4...) while((s32[]{:T(128)}, ...), condition=%wide.region_15.16_spmd, body=%wide.region_14.15_spmd.sunk | while | flops 551026688 | bytes 51904876 | solution.py:213
  505.5 6.4 all-to-all-done.24
  514.0 11.7 %all_to_all.205 = bf16[8,16,16,128]{3,1,2,0:T(8,128)(2,1)S(1)} all-to-all(bf16[8,16,16,128]{3,1,2,0:T(8,128)(2,1)S(1)} %copy.516), channel_id=1, replica_groups=mesh['s'=4,'t'=4,'x'=2] {'s','x'}, dimensions={0} | all-to-all | bytes 1048576 | tf_op jit(solution)/shard_map/while/body/all_to_all | solution.py:27
  549.4 6.0 all-to-all-done.27
  567.5 60.9 %while.139 = (s32[]{:T(128)}, bf16[16,128,128]{2,1,0:T(8,128)(2,1)S(1)}, bf16[4,4,4,128,128]{3,4,2,0,1:T(8,128)(2,1)}, s32[]{:T(128)}, bf16[4,1,2,4,128,128]{5,4...) while((s32[]{:T(128)}, ...), condition=%wide.region_18.19_spmd, body=%wide.region_17.18_spmd.sunk | while | flops 551026688 | bytes 43516164 | solution.py:213
  575.0 6.5 all-to-all-done.28
  583.3 11.7 %all_to_all.206 = bf16[8,16,16,128]{3,1,2,0:T(8,128)(2,1)S(1)} all-to-all(bf16[8,16,16,128]{3,1,2,0:T(8,128)(2,1)S(1)} %copy.526), channel_id=1, replica_groups=mesh['s'=4,'t'=4,'x'=2] {'s','x'}, dimensions={0} | all-to-all | bytes 1048576 | tf_op jit(solution)/shard_map/while/body/all_to_all | solution.py:27
  601.5 7.4 %all-to-all-done.30 = bf16[8,16,16,128]{3,1,2,0:T(8,128)(2,1)S(1)} async-done(((bf16[8,16,16,128]{3,1,2,0:T(8,128)(2,1)}), bf16[8,16,16,128]{3,1,2,0:T(8,128)(2,1)S(1)}, u32[]{:S(2)}, u32[]{:S(2)}) %all-to-all-start.30) | async-done | bytes 524320 | tf_op jit(solution)/shard_map/while/body/all_to_all | solution.py:27
  641.7 5.6 collective-permute-done.18
  647.3 5.1 collective-permute-done.17
  657.0 13.8 %collective-permute-start.32 = (bf16[2,4,128,128]{3,2,1,0:T(8,128)(2,1)S(1)}, bf16[2,4,128,128]{3,2,1,0:T(8,128)(2,1)}, u32[]{:S(2)}, u32[]{:S(2)}) collective-permute-start(bf16[2,4,128,128]{3,2,1,0:T(8,128)(2,1)S(1)} %pad_maximum_fusion.38), channel_id=1, source_target_pairs={{0,16},{8,24},{16,0},{24,8},{1,17},{9,25},{17,1},{25,9},{2,18},{10... | collective-permute-start | bytes 786440 | tf_op jit(solution)/shard_map/ppermute | solution.py:108
  671.5 9.3 %collective-permute-done.32 = bf16[2,4,128,128]{3,2,1,0:T(8,128)(2,1)} collective-permute-done((bf16[2,4,128,128]{3,2,1,0:T(8,128)(2,1)S(1)}, bf16[2,4,128,128]{3,2,1,0:T(8,128)(2,1)}, u32[]{:S(2)}, u32[]{:S(2)}) %collective-permute-start.32) | collective-permute-done | bytes 262176 | tf_op jit(solution)/shard_map/ppermute | solution.py:108
  688.4 5.1 collective-permute-start.30
  701.4 5.6 collective-permute-done.29
  (528 shorter events, 342.0 us)
Async XLA Ops:
  7.2 91.8 %all-gather.9.cloned.1.call-start = ((), (), s32[]{:S(2)}) async-start(), calls=%async_computation.40 | async-start | bytes 1310720 | tf_op jit(solution)/shard_map/all_gather | solution.py:122
  8.5 16.6 %collective-permute-start.3 = (bf16[4,128,128]{2,1,0:T(8,128)(2,1)S(1)}, bf16[4,128,128]{2,1,0:T(8,128)(2,1)S(1)}, u32[]{:S(2)}, u32[]{:S(2)}) collective-permute-start(bf16[4,128,128]{2,1,0:T(8,128)(2,1)S(1)} %get-tuple-element.986), channel_id=1, source_target_pairs={{0,24},{2,16},{4,8},{6,0},{8,26},{10,18},{12,10},{14,2},{16,28},{1... | collective-permute-start | bytes 393224 | tf_op jit(solution)/shard_map/ppermute | solution.py:76
  10.9 20.0 %collective-permute-start.2 = (bf16[4,128,128]{2,1,0:T(8,128)(2,1)S(1)}, bf16[4,128,128]{2,1,0:T(8,128)(2,1)S(1)}, u32[]{:S(2)}, u32[]{:S(2)}) collective-permute-start(bf16[4,128,128]{2,1,0:T(8,128)(2,1)S(1)} %get-tuple-element.987), channel_id=1, source_target_pairs={{0,16},{2,24},{4,0},{6,8},{8,18},{10,26},{12,2},{14,10},{16,20},{1... | collective-permute-start | bytes 393224 | tf_op jit(solution)/shard_map/ppermute | solution.py:76
  13.5 17.4 %collective-permute-start.1 = (bf16[4,128,128]{2,1,0:T(8,128)(2,1)S(1)}, bf16[4,128,128]{2,1,0:T(8,128)(2,1)S(1)}, u32[]{:S(2)}, u32[]{:S(2)}) collective-permute-start(bf16[4,128,128]{2,1,0:T(8,128)(2,1)S(1)} %get-tuple-element.988), channel_id=1, source_target_pairs={{0,8},{2,0},{4,24},{6,16},{8,10},{10,2},{12,26},{14,18},{16,12},{1... | collective-permute-start | bytes 393224 | tf_op jit(solution)/shard_map/ppermute | solution.py:76
  14.2 16.7 %collective-permute-start = (bf16[4,128,128]{2,1,0:T(8,128)(2,1)S(1)}, bf16[4,128,128]{2,1,0:T(8,128)(2,1)S(1)}, u32[]{:S(2)}, u32[]{:S(2)}) collective-permute-start(bf16[4,128,128]{2,1,0:T(8,128)(2,1)S(1)} %get-tuple-element.985), channel_id=1, source_target_pairs={{0,0},{2,8},{4,16},{6,24},{8,2},{10,10},{12,18},{14,26},{16,4},{18... | collective-permute-start | bytes 393224 | tf_op jit(solution)/shard_map/ppermute | solution.py:76
  18.3 13.3 %collective-permute-start.6 = (bf16[2,4,128,128]{2,3,1,0:T(8,128)(2,1)S(1)}, bf16[2,4,128,128]{2,3,1,0:T(8,128)(2,1)S(1)}, u32[]{:S(2)}, u32[]{:S(2)}) collective-permute-start(bf16[2,4,128,128]{2,3,1,0:T(8,128)(2,1)S(1)} %pad_maximum_fusion.29), channel_id=1, source_target_pairs={{0,24},{8,16},{16,8},{24,0},{1,25},{9,17},{17,9},{25,1},{2,26},{10... | collective-permute-start | bytes 786440 | tf_op jit(solution)/shard_map/ppermute | solution.py:108
  25.0 14.2 %collective-permute-start.5 = (bf16[2,4,128,128]{2,3,1,0:T(8,128)(2,1)S(1)}, bf16[2,4,128,128]{2,3,1,0:T(8,128)(2,1)S(1)}, u32[]{:S(2)}, u32[]{:S(2)}) collective-permute-start(bf16[2,4,128,128]{2,3,1,0:T(8,128)(2,1)S(1)} %pad_maximum_fusion.28), channel_id=1, source_target_pairs={{0,16},{8,24},{16,0},{24,8},{1,17},{9,25},{17,1},{25,9},{2,18},{10... | collective-permute-start | bytes 786440 | tf_op jit(solution)/shard_map/ppermute | solution.py:108
  43.7 15.9 %collective-permute-start.11 = (bf16[4,128,128]{2,1,0:T(8,128)(2,1)S(1)}, bf16[4,128,128]{2,1,0:T(8,128)(2,1)S(1)}, u32[]{:S(2)}, u32[]{:S(2)}) collective-permute-start(bf16[4,128,128]{2,1,0:T(8,128)(2,1)S(1)} %get-tuple-element.991), channel_id=1, source_target_pairs={{0,4},{2,6},{4,0},{6,2},{1,5},{3,7},{5,1},{7,3},{8,12},{10,14},{12... | collective-permute-start | bytes 393224 | tf_op jit(solution)/shard_map/ppermute | solution.py:127
  43.7 15.9 %collective-permute-start.10 = (bf16[4,128,128]{2,1,0:T(8,128)(2,1)S(1)}, bf16[4,128,128]{2,1,0:T(8,128)(2,1)S(1)}, u32[]{:S(2)}, u32[]{:S(2)}) collective-permute-start(bf16[4,128,128]{2,1,0:T(8,128)(2,1)S(1)} %get-tuple-element.991), channel_id=1, source_target_pairs={{0,2},{2,0},{4,6},{6,4},{1,3},{3,1},{5,7},{7,5},{8,10},{10,8},{12,... | collective-permute-start | bytes 393224 | tf_op jit(solution)/shard_map/ppermute | solution.py:127
  44.4 15.3 %collective-permute-start.9 = (bf16[4,128,128]{2,1,0:T(8,128)(2,1)S(1)}, bf16[4,128,128]{2,1,0:T(8,128)(2,1)S(1)}, u32[]{:S(2)}, u32[]{:S(2)}) collective-permute-start(bf16[4,128,128]{2,1,0:T(8,128)(2,1)S(1)} %get-tuple-element.990), channel_id=1, source_target_pairs={{0,6},{2,4},{4,2},{6,0},{1,7},{3,5},{5,3},{7,1},{8,14},{10,12},{12... | collective-permute-start | bytes 393224 | tf_op jit(solution)/shard_map/ppermute | solution.py:127
  48.0 16.8 %collective-permute-start.8 = (bf16[4,128,128]{2,1,0:T(8,128)(2,1)S(1)}, bf16[4,128,128]{2,1,0:T(8,128)(2,1)S(1)}, u32[]{:S(2)}, u32[]{:S(2)}) collective-permute-start(bf16[4,128,128]{2,1,0:T(8,128)(2,1)S(1)} %get-tuple-element.990), channel_id=1, source_target_pairs={{0,4},{2,6},{4,0},{6,2},{1,5},{3,7},{5,1},{7,3},{8,12},{10,14},{12... | collective-permute-start | bytes 393224 | tf_op jit(solution)/shard_map/ppermute | solution.py:127
  49.2 15.6 %collective-permute-start.7 = (bf16[4,128,128]{2,1,0:T(8,128)(2,1)S(1)}, bf16[4,128,128]{2,1,0:T(8,128)(2,1)S(1)}, u32[]{:S(2)}, u32[]{:S(2)}) collective-permute-start(bf16[4,128,128]{2,1,0:T(8,128)(2,1)S(1)} %get-tuple-element.990), channel_id=1, source_target_pairs={{0,2},{2,0},{4,6},{6,4},{1,3},{3,1},{5,7},{7,5},{8,10},{10,8},{12,... | collective-permute-start | bytes 393224 | tf_op jit(solution)/shard_map/ppermute | solution.py:127
  65.2 75.1 %all-gather.11.cloned.1.call-start = ((), (), s32[]{:S(2)}) async-start(), calls=%async_computation.41 | async-start | bytes 2621440 | tf_op jit(solution)/shard_map/all_gather | solution.py:122
  69.4 137.1 %all-gather.13.cloned.1.call-start = ((), (), s32[]{:S(2)}) async-start(), calls=%async_computation.42 | async-start | bytes 2621440 | tf_op jit(solution)/shard_map/all_gather | solution.py:122
  85.7 12.7 %all-to-all-start.1 = ((bf16[8,16,16,128]{3,1,2,0:T(8,128)(2,1)}), bf16[8,16,16,128]{3,1,2,0:T(8,128)(2,1)S(1)}, u32[]{:S(2)}, u32[]{:S(2)}) async-start(bf16[8,16,16,128]{3,1,2,0:T(8,128)(2,1)} %copy.465), calls=%async_computation.1 | async-start | bytes 1048576 | tf_op jit(solution)/shard_map/while/body/all_to_all | solution.py:27
  103.2 37.1 %collective-permute-start.13 = (bf16[2,4,128,128]{2,3,1,0:T(8,128)(2,1)S(1)}, bf16[2,4,128,128]{2,3,1,0:T(8,128)(2,1)}, u32[]{:S(2)}, u32[]{:S(2)}) collective-permute-start(bf16[2,4,128,128]{2,3,1,0:T(8,128)(2,1)S(1)} %pad_maximum_fusion.31), channel_id=1, source_target_pairs={{0,8},{8,0},{16,24},{24,16},{1,9},{9,1},{17,25},{25,17},{2,10},{10... | collective-permute-start | bytes 786440 | tf_op jit(solution)/shard_map/ppermute | solution.py:108
  104.3 36.0 %collective-permute-start.14 = (bf16[2,4,128,128]{2,3,1,0:T(8,128)(2,1)}, bf16[2,4,128,128]{2,3,1,0:T(8,128)(2,1)}, u32[]{:S(2)}, u32[]{:S(2)}) collective-permute-start(bf16[2,4,128,128]{2,3,1,0:T(8,128)(2,1)} %pad_maximum_fusion.32), channel_id=1, source_target_pairs={{0,16},{8,24},{16,0},{24,8},{1,17},{9,25},{17,1},{25,9},{2,18},{10... | collective-permute-start | bytes 786440 | tf_op jit(solution)/shard_map/ppermute | solution.py:108
  106.2 34.1 %collective-permute-start.15 = (bf16[2,4,128,128]{2,3,1,0:T(8,128)(2,1)}, bf16[2,4,128,128]{2,3,1,0:T(8,128)(2,1)}, u32[]{:S(2)}, u32[]{:S(2)}) collective-permute-start(bf16[2,4,128,128]{2,3,1,0:T(8,128)(2,1)} %pad_maximum_fusion.33), channel_id=1, source_target_pairs={{0,24},{8,16},{16,8},{24,0},{1,25},{9,17},{17,9},{25,1},{2,26},{10... | collective-permute-start | bytes 786440 | tf_op jit(solution)/shard_map/ppermute | solution.py:108
  125.9 12.7 %all-to-all-start.3 = ((bf16[8,16,16,128]{3,1,2,0:T(8,128)(2,1)}), bf16[8,16,16,128]{3,1,2,0:T(8,128)(2,1)S(1)}, u32[]{:S(2)}, u32[]{:S(2)}) async-start(bf16[8,16,16,128]{3,1,2,0:T(8,128)(2,1)} %copy.469), calls=%async_computation.3 | async-start | bytes 1048576 | tf_op jit(solution)/shard_map/while/body/all_to_all | solution.py:27
  143.4 123.4 %all-gather.15.cloned.1.call-start = ((), (), s32[]{:S(2)}) async-start(), calls=%async_computation.43 | async-start | bytes 2621440 | tf_op jit(solution)/shard_map/all_gather | solution.py:122
  149.6 343.4 %reduce-scatter.5.cloned.1.call-start = ((), (), s32[]{:S(2)}) async-start(), calls=%async_computation.36 | async-start | bytes 2621440 | tf_op jit(solution)/shard_map/reduce_scatter | solution.py:138
  193.4 12.7 %all-to-all-start.7 = ((bf16[8,16,16,128]{3,1,2,0:T(8,128)(2,1)}), bf16[8,16,16,128]{3,1,2,0:T(8,128)(2,1)S(1)}, u32[]{:S(2)}, u32[]{:S(2)}) async-start(bf16[8,16,16,128]{3,1,2,0:T(8,128)(2,1)} %copy.477), calls=%async_computation.7 | async-start | bytes 1048576 | tf_op jit(solution)/shard_map/while/body/all_to_all | solution.py:27
  253.6 12.7 %all-to-all-start.11 = ((bf16[8,16,16,128]{3,1,2,0:T(8,128)(2,1)}), bf16[8,16,16,128]{3,1,2,0:T(8,128)(2,1)S(1)}, u32[]{:S(2)}, u32[]{:S(2)}) async-start(bf16[8,16,16,128]{3,1,2,0:T(8,128)(2,1)} %copy.485), calls=%async_computation.11 | async-start | bytes 1048576 | tf_op jit(solution)/shard_map/while/body/all_to_all | solution.py:27
  315.1 13.4 %all-to-all-start.15 = ((bf16[8,16,16,128]{3,1,2,0:T(8,128)(2,1)}), bf16[8,16,16,128]{3,1,2,0:T(8,128)(2,1)}, u32[]{:S(2)}, u32[]{:S(2)}) async-start(bf16[8,16,16,128]{3,1,2,0:T(8,128)(2,1)} %copy.493), calls=%async_computation.15 | async-start | bytes 1048576 | tf_op jit(solution)/shard_map/while/body/all_to_all | solution.py:27
  332.2 17.0 %collective-permute-start.23 = (bf16[4,128,128]{1,2,0:T(8,128)(2,1)S(1)}, bf16[4,128,128]{1,2,0:T(8,128)(2,1)S(1)}, u32[]{:S(2)}, u32[]{:S(2)}) collective-permute-start(bf16[4,128,128]{1,2,0:T(8,128)(2,1)S(1)} %bitcast.1466), channel_id=1, source_target_pairs={{0,24},{2,16},{4,8},{6,0},{8,26},{10,18},{12,10},{14,2},{16,28},{1... | collective-permute-start | bytes 393224 | tf_op jit(solution)/shard_map/ppermute | solution.py:76
  332.9 19.6 %collective-permute-start.22 = (bf16[4,128,128]{1,2,0:T(8,128)(2,1)S(1)}, bf16[4,128,128]{1,2,0:T(8,128)(2,1)S(1)}, u32[]{:S(2)}, u32[]{:S(2)}) collective-permute-start(bf16[4,128,128]{1,2,0:T(8,128)(2,1)S(1)} %bitcast.1467), channel_id=1, source_target_pairs={{0,16},{2,24},{4,0},{6,8},{8,18},{10,26},{12,2},{14,10},{16,20},{1... | collective-permute-start | bytes 393224 | tf_op jit(solution)/shard_map/ppermute | solution.py:76
  334.2 18.3 %collective-permute-start.21 = (bf16[4,128,128]{1,2,0:T(8,128)(2,1)S(1)}, bf16[4,128,128]{1,2,0:T(8,128)(2,1)}, u32[]{:S(2)}, u32[]{:S(2)}) collective-permute-start(bf16[4,128,128]{1,2,0:T(8,128)(2,1)S(1)} %bitcast.1468), channel_id=1, source_target_pairs={{0,8},{2,0},{4,24},{6,16},{8,10},{10,2},{12,26},{14,18},{16,12},{1... | collective-permute-start | bytes 393224 | tf_op jit(solution)/shard_map/ppermute | solution.py:76
  334.6 17.9 %collective-permute-start.20 = (bf16[4,128,128]{1,2,0:T(8,128)(2,1)S(1)}, bf16[4,128,128]{1,2,0:T(8,128)(2,1)S(1)}, u32[]{:S(2)}, u32[]{:S(2)}) collective-permute-start(bf16[4,128,128]{1,2,0:T(8,128)(2,1)S(1)} %bitcast.1469), channel_id=1, source_target_pairs={{0,0},{2,8},{4,16},{6,24},{8,2},{10,10},{12,18},{14,26},{16,4},{18... | collective-permute-start | bytes 393224 | tf_op jit(solution)/shard_map/ppermute | solution.py:76
  357.7 16.8 %all-to-all-start.16 = ((bf16[8,16,16,128]{3,2,1,0:T(8,128)(2,1)}), bf16[8,16,16,128]{3,2,1,0:T(8,128)(2,1)S(1)}, u32[]{:S(2)}, u32[]{:S(2)}) async-start(bf16[8,16,16,128]{3,2,1,0:T(8,128)(2,1)} %bitcast.1137), calls=%async_computation.16 | async-start | bytes 1048576 | tf_op jit(solution)/shard_map/while/body/all_to_all | solution.py:27
  389.5 12.7 %all-to-all-start.18 = ((bf16[8,16,16,128]{3,1,2,0:T(8,128)(2,1)}), bf16[8,16,16,128]{3,1,2,0:T(8,128)(2,1)S(1)}, u32[]{:S(2)}, u32[]{:S(2)}) async-start(bf16[8,16,16,128]{3,1,2,0:T(8,128)(2,1)} %copy.498), calls=%async_computation.18 | async-start | bytes 1048576 | tf_op jit(solution)/shard_map/while/body/all_to_all | solution.py:27
  405.3 12.7 %all-to-all-start.19 = ((bf16[8,16,16,128]{3,2,1,0:T(8,128)(2,1)}), bf16[8,16,16,128]{3,2,1,0:T(8,128)(2,1)S(1)}, u32[]{:S(2)}, u32[]{:S(2)}) async-start(bf16[8,16,16,128]{3,2,1,0:T(8,128)(2,1)} %copy.500), calls=%async_computation.19 | async-start | bytes 1048576 | tf_op jit(solution)/shard_map/while/body/all_to_all | solution.py:27
  425.7 133.3 %reduce-scatter.7.cloned.1.call-start = ((), (), s32[]{:S(2)}) async-start(), calls=%async_computation.37 | async-start | bytes 2621440 | tf_op jit(solution)/shard_map/reduce_scatter | solution.py:138
  428.9 12.7 %all-to-all-start.20 = ((bf16[8,16,16,128]{3,2,1,0:T(8,128)(2,1)}), bf16[8,16,16,128]{3,2,1,0:T(8,128)(2,1)S(1)}, u32[]{:S(2)}, u32[]{:S(2)}) async-start(bf16[8,16,16,128]{3,2,1,0:T(8,128)(2,1)} %bitcast.1177), calls=%async_computation.20 | async-start | bytes 1048576 | tf_op jit(solution)/shard_map/while/body/all_to_all | solution.py:27
  456.7 12.7 %all-to-all-start.22 = ((bf16[8,16,16,128]{3,1,2,0:T(8,128)(2,1)}), bf16[8,16,16,128]{3,1,2,0:T(8,128)(2,1)S(1)}, u32[]{:S(2)}, u32[]{:S(2)}) async-start(bf16[8,16,16,128]{3,1,2,0:T(8,128)(2,1)} %copy.508), calls=%async_computation.22 | async-start | bytes 1048576 | tf_op jit(solution)/shard_map/while/body/all_to_all | solution.py:27
  472.5 12.7 %all-to-all-start.23 = ((bf16[8,16,16,128]{3,2,1,0:T(8,128)(2,1)}), bf16[8,16,16,128]{3,2,1,0:T(8,128)(2,1)S(1)}, u32[]{:S(2)}, u32[]{:S(2)}) async-start(bf16[8,16,16,128]{3,2,1,0:T(8,128)(2,1)} %copy.510), calls=%async_computation.23 | async-start | bytes 1048576 | tf_op jit(solution)/shard_map/while/body/all_to_all | solution.py:27
  492.9 189.0 %reduce-scatter.9.cloned.1.call-start = ((), (), s32[]{:S(2)}) async-start(), calls=%async_computation.38 | async-start | bytes 2621440 | tf_op jit(solution)/shard_map/reduce_scatter | solution.py:138
  499.2 12.7 %all-to-all-start.24 = ((bf16[8,16,16,128]{3,2,1,0:T(8,128)(2,1)}), bf16[8,16,16,128]{3,2,1,0:T(8,128)(2,1)S(1)}, u32[]{:S(2)}, u32[]{:S(2)}) async-start(bf16[8,16,16,128]{3,2,1,0:T(8,128)(2,1)} %bitcast.1217), calls=%async_computation.24 | async-start | bytes 1048576 | tf_op jit(solution)/shard_map/while/body/all_to_all | solution.py:27
  526.9 12.7 %all-to-all-start.26 = ((bf16[8,16,16,128]{3,1,2,0:T(8,128)(2,1)}), bf16[8,16,16,128]{3,1,2,0:T(8,128)(2,1)S(1)}, u32[]{:S(2)}, u32[]{:S(2)}) async-start(bf16[8,16,16,128]{3,1,2,0:T(8,128)(2,1)} %copy.518), calls=%async_computation.26 | async-start | bytes 1048576 | tf_op jit(solution)/shard_map/while/body/all_to_all | solution.py:27
  542.7 12.7 %all-to-all-start.27 = ((bf16[8,16,16,128]{3,2,1,0:T(8,128)(2,1)}), bf16[8,16,16,128]{3,2,1,0:T(8,128)(2,1)S(1)}, u32[]{:S(2)}, u32[]{:S(2)}) async-start(bf16[8,16,16,128]{3,2,1,0:T(8,128)(2,1)} %copy.520), calls=%async_computation.27 | async-start | bytes 1048576 | tf_op jit(solution)/shard_map/while/body/all_to_all | solution.py:27
  565.6 120.8 %reduce-scatter.11.cloned.1.call-start = ((), (), s32[]{:S(2)}) async-start(), calls=%async_computation.39 | async-start | bytes 2621440 | tf_op jit(solution)/shard_map/reduce_scatter | solution.py:138
  568.9 12.7 %all-to-all-start.28 = ((bf16[8,16,16,128]{3,2,1,0:T(8,128)(2,1)}), bf16[8,16,16,128]{3,2,1,0:T(8,128)(2,1)S(1)}, u32[]{:S(2)}, u32[]{:S(2)}) async-start(bf16[8,16,16,128]{3,2,1,0:T(8,128)(2,1)} %bitcast.1257), calls=%async_computation.28 | async-start | bytes 1048576 | tf_op jit(solution)/shard_map/while/body/all_to_all | solution.py:27
  596.2 12.7 %all-to-all-start.30 = ((bf16[8,16,16,128]{3,1,2,0:T(8,128)(2,1)}), bf16[8,16,16,128]{3,1,2,0:T(8,128)(2,1)S(1)}, u32[]{:S(2)}, u32[]{:S(2)}) async-start(bf16[8,16,16,128]{3,1,2,0:T(8,128)(2,1)} %copy.528), calls=%async_computation.30 | async-start | bytes 1048576 | tf_op jit(solution)/shard_map/while/body/all_to_all | solution.py:27
  636.5 16.0 %collective-permute-start.17 = (bf16[4,128,128]{2,1,0:T(8,128)(2,1)S(1)}, bf16[4,128,128]{2,1,0:T(8,128)(2,1)S(1)}, u32[]{:S(2)}, u32[]{:S(2)}) collective-permute-start(bf16[4,128,128]{2,1,0:T(8,128)(2,1)S(1)} %bitcast.1472), channel_id=1, source_target_pairs={{0,2},{2,10},{4,18},{6,26},{8,0},{10,8},{12,16},{14,24},{16,6},{18... | collective-permute-start | bytes 393224 | tf_op jit(solution)/shard_map/ppermute | solution.py:76
  636.7 15.7 %collective-permute-start.16 = (bf16[4,128,128]{2,1,0:T(8,128)(2,1)S(1)}, bf16[4,128,128]{2,1,0:T(8,128)(2,1)S(1)}, u32[]{:S(2)}, u32[]{:S(2)}) collective-permute-start(bf16[4,128,128]{2,1,0:T(8,128)(2,1)S(1)} %bitcast.1473), channel_id=1, source_target_pairs={{0,0},{2,8},{4,16},{6,24},{8,2},{10,10},{12,18},{14,26},{16,4},{18... | collective-permute-start | bytes 393224 | tf_op jit(solution)/shard_map/ppermute | solution.py:76
  653.2 18.3 %collective-permute-start.33 = (bf16[2,4,128,128]{3,2,1,0:T(8,128)(2,1)S(1)}, bf16[2,4,128,128]{3,2,1,0:T(8,128)(2,1)S(1)}, u32[]{:S(2)}, u32[]{:S(2)}) collective-permute-start(bf16[2,4,128,128]{3,2,1,0:T(8,128)(2,1)S(1)} %pad_maximum_fusion.39), channel_id=1, source_target_pairs={{0,24},{8,16},{16,8},{24,0},{1,25},{9,17},{17,9},{25,1},{2,26},{10... | collective-permute-start | bytes 786440 | tf_op jit(solution)/shard_map/ppermute | solution.py:108
  657.0 23.8 %collective-permute-start.32 = (bf16[2,4,128,128]{3,2,1,0:T(8,128)(2,1)S(1)}, bf16[2,4,128,128]{3,2,1,0:T(8,128)(2,1)}, u32[]{:S(2)}, u32[]{:S(2)}) collective-permute-start(bf16[2,4,128,128]{3,2,1,0:T(8,128)(2,1)S(1)} %pad_maximum_fusion.38), channel_id=1, source_target_pairs={{0,16},{8,24},{16,0},{24,8},{1,17},{9,25},{17,1},{25,9},{2,18},{10... | collective-permute-start | bytes 786440 | tf_op jit(solution)/shard_map/ppermute | solution.py:108
  688.4 12.9 %collective-permute-start.30 = (bf16[2,4,128,128]{3,2,1,0:T(8,128)(2,1)S(1)}, bf16[2,4,128,128]{3,2,1,0:T(8,128)(2,1)S(1)}, u32[]{:S(2)}, u32[]{:S(2)}) collective-permute-start(bf16[2,4,128,128]{3,2,1,0:T(8,128)(2,1)S(1)} %pad_maximum_fusion.36), channel_id=1, source_target_pairs={{0,24},{8,16},{16,8},{24,0},{1,25},{9,17},{17,9},{25,1},{2,26},{10... | collective-permute-start | bytes 786440 | tf_op jit(solution)/shard_map/ppermute | solution.py:108
  693.6 13.3 %collective-permute-start.29 = (bf16[2,4,128,128]{3,2,1,0:T(8,128)(2,1)S(1)}, bf16[2,4,128,128]{3,2,1,0:T(8,128)(2,1)S(1)}, u32[]{:S(2)}, u32[]{:S(2)}) collective-permute-start(bf16[2,4,128,128]{3,2,1,0:T(8,128)(2,1)S(1)} %pad_maximum_fusion.35), channel_id=1, source_target_pairs={{0,16},{8,24},{16,0},{24,8},{1,17},{9,25},{17,1},{25,9},{2,18},{10... | collective-permute-start | bytes 786440 | tf_op jit(solution)/shard_map/ppermute | solution.py:108
  (73 other events, 743.5 us)
Sparse Core Ops, SparseCore 0:
  65.3 27.2 all-gather.8
  94.8 45.4 all-gather.10
  143.5 44.6 all-gather.12
  190.2 44.5 all-gather.14
  425.9 41.4 reduce-scatter.4
  493.0 41.4 reduce-scatter.6
  565.7 41.4 reduce-scatter.8
  632.7 49.5 reduce-scatter.10

commit v19 on v18

--- a/solution.py
+++ b/solution.py
@@ -143,9 +143,10 @@
 
     rights = right_factor[:, 0].reshape(loops, sections, sub, size, size)
     lefts = left_factor[:, 0].reshape(loops, sections, sub, size, size)
-    parts = [ordered(part) for part in scattered(rights[0], lefts[0])]
+    moving = dealt(rights[0], lefts[0])
+    moving[0], inputs = lax.optimization_barrier((moving[0], inputs))
+    parts = [ordered(part) for part in collected(moving)]
     current = arriving(inputs)
-    current, parts[0] = lax.optimization_barrier((current, parts[0]))
     once = 1 + s_index // sections
     first = jnp.stack([gathered_directly(parts[0][f]) for f in range(2)], axis=1)[:, None]
     starts = [0, 1] + list(range(PAIRED, layers, PAIRED)) + [layers]
@@ -217,7 +218,7 @@
         totals[top] = summed(terms)
     grad = lax.fori_loop(0, once, lambda _, acts: unsettled(acts), grad)
     if 2 * PAIRED <= layers:
-        grad, totals[2 * PAIRED - 1] = lax.optimization_barrier((grad, totals[2 * PAIRED - 1]))
+        _, totals[2 * PAIRED - 1] = lax.optimization_barrier((grad, totals[2 * PAIRED - 1]))
     for top, total in totals.items():
         for step in range(PAIRED):
             sums[top - step] = [total[2 * step], total[2 * step + 1]]

time: 731 us -> 763 us (1.044)
  starting transfers between devices: 122 us -> 136 us
  waiting for transfers between devices: 181 us -> 189 us
    ppermute x16, starting transfers between devices: 13.9 us -> 33.5 us  [turned(): moved.append(lax.ppermute(pick(parts, send_by ^ mask), ('s', 't'), pairs))]
    ppermute x16, waiting for transfers between devices: 23.6 us -> 34.7 us  [turned(): moved.append(lax.ppermute(pick(parts, send_by ^ mask), ('s', 't'), pairs))]
    ppermute x12, starting transfers between devices: 33 us -> 22.9 us  [dealt(): moved.append(lax.ppermute(value, 's', pairs))]
    reduce_scatter x4, waiting for transfers between devices: 0.06 us -> 7.83 us  [summed(): lax.psum_scatter(terms.reshape(-1, size, size), 't', scatter_dimension=0,...]
  transfers between devices with their start and end apart: 59 -> 59, of which waited for: 30 -> 26; matrix products, arithmetic and copies ran while one was open for 23% -> 22% of each run, Pallas kernels for 0% -> 0%
where the time goes in v19:
time: 763 us; the launch traced here: 751 us
  waiting for transfers between devices  189 us (25%)
  blocking collectives  188 us (25%)
  starting transfers between devices  136 us (18%)
  local copies, waits for them, and re-layouts  126 us (17%)
  matrix products  62.8 us (8%)
  other arithmetic  29.8 us (4%)
  between operations  15.9 us (2%)
    all_to_all x15, blocking collectives, exchange(): lax.all_to_all(pieces, WIDE, split_axis=0, concat_axis=0, tiled=True)  188 us
    all_to_all x17, waiting for transfers between devices, exchange(): lax.all_to_all(pieces, WIDE, split_axis=0, concat_axis=0, tiled=True)  117 us
    all_to_all x17, starting transfers between devices, exchange(): lax.all_to_all(pieces, WIDE, split_axis=0, concat_axis=0, tiled=True)  64.1 us
    ppermute x16, waiting for transfers between devices, turned(): moved.append(lax.ppermute(pick(parts, send_by ^ mask), ('s', 't'), pairs))  34.7 us
    ppermute x16, starting transfers between devices, turned(): moved.append(lax.ppermute(pick(parts, send_by ^ mask), ('s', 't'), pairs))  33.5 us
    ppermute x12, starting transfers between devices, dealt(): moved.append(lax.ppermute(value, 's', pairs))  22.9 us
    while x15, local copies, waits for them, and re-layouts, body(): grad, terms = lax.fori_loop(0, once, backward_pair(top), (grad, blank))  21.7 us
    ppermute x12, waiting for transfers between devices, dealt(): moved.append(lax.ppermute(value, 's', pairs))  19.2 us
  transfers between devices with their start and end apart: 59, of which 26 were waited for; matrix products, arithmetic and copies ran while one was open for 22% of the time, Pallas kernels for 0%

profile of v19, /device:TPU:0, one launch (start us, length us, event | category | flops | bytes accessed | tf_op | source)
XLA Modules:
  0.0 750.6 jit_solution(5759213517843823145)
XLA Ops:
  19.9 5.8 collective-permute-done.5
  36.9 6.1 collective-permute-start.7
  44.2 6.1 collective-permute-done.11
  64.3 25.8 %collective-permute-done.2 = bf16[4,128,128]{1,2,0:T(8,128)(2,1)S(1)} collective-permute-done((bf16[4,128,128]{1,2,0:T(8,128)(2,1)S(1)}, bf16[4,128,128]{1,2,0:T(8,128)(2,1)S(1)}, u32[]{:S(2)}, u32[]{:S(2)}) %collective-permute-start.2) | collective-permute-done | bytes 131104 | tf_op jit(solution)/shard_map/ppermute | solution.py:76
  96.1 35.1 %while.131 = (s32[]{:T(128)}, bf16[16,128,128]{2,1,0:T(8,128)(2,1)S(1)}, bf16[16,128,128]{2,0,1:T(8,128)(2,1)}, s32[]{:T(128)}, bf16[4,1,2,4,128,128]{4,5,3,0,2,1:T(8,128)(2,1)S(1)}, /*index=5*/s32[]{:T(128)}) while((s32[]{:T(128)}, bf16[16,128,128]{2,1,0:T(8,128)(2,1)S(1)}, bf16[16,128,128]{2,0,1:T(8,128)(2,1)}, s32[]{:T(128)}, ...), condition=%wide.region_1.2_spmd, body=%wide.region_0.1_spmd.sunk | while | flops 137363456 | bytes 16777344 | solution.py:187
  96.5 20.0 %all_to_all.192 = bf16[8,16,16,128]{3,1,2,0:T(8,128)(2,1)S(1)} all-to-all(bf16[8,16,16,128]{3,1,2,0:T(8,128)(2,1)S(1)} %copy.473), channel_id=1, replica_groups=mesh['s'=4,'t'=4,'x'=2] {'s','x'}, dimensions={0} | all-to-all | bytes 1048576 | tf_op jit(solution)/shard_map/while/body/all_to_all | solution.py:27
  121.5 9.2 %all-to-all-done.1 = bf16[8,16,16,128]{3,1,2,0:T(8,128)(2,1)S(1)} async-done(((bf16[8,16,16,128]{3,1,2,0:T(8,128)(2,1)}), bf16[8,16,16,128]{3,1,2,0:T(8,128)(2,1)S(1)}, u32[]{:S(2)}, u32[]{:S(2)}) %all-to-all-start.1) | async-done | bytes 524320 | tf_op jit(solution)/shard_map/while/body/all_to_all | solution.py:27
  139.7 31.9 %while.132 = (s32[]{:T(128)}, bf16[16,128,128]{2,1,0:T(8,128)(2,1)S(1)}, bf16[16,128,128]{2,0,1:T(8,128)(2,1)}, s32[]{:T(128)}, bf16[4,1,2,4,128,128]{4,5,3,0,2,1:T(8,128)(2,1)S(1)}, /*index=5*/s32[]{:T(128)}) while((s32[]{:T(128)}, bf16[16,128,128]{2,1,0:T(8,128)(2,1)S(1)}, bf16[16,128,128]{2,0,1:T(8,128)(2,1)}, s32[]{:T(128)}, ...), condition=%wide.region_3.4_spmd, body=%wide.region_2.3_spmd.sunk | while | flops 137363456 | bytes 16777344 | solution.py:187
  140.2 16.6 %all_to_all.193 = bf16[8,16,16,128]{3,1,2,0:T(8,128)(2,1)S(1)} all-to-all(bf16[8,16,16,128]{3,1,2,0:T(8,128)(2,1)S(1)} %copy.477), channel_id=1, replica_groups=mesh['s'=4,'t'=4,'x'=2] {'s','x'}, dimensions={0} | all-to-all | bytes 1048576 | tf_op jit(solution)/shard_map/while/body/all_to_all | solution.py:27
  161.7 9.2 %all-to-all-done.3 = bf16[8,16,16,128]{3,1,2,0:T(8,128)(2,1)S(1)} async-done(((bf16[8,16,16,128]{3,1,2,0:T(8,128)(2,1)}), bf16[8,16,16,128]{3,1,2,0:T(8,128)(2,1)S(1)}, u32[]{:S(2)}, u32[]{:S(2)}) %all-to-all-start.3) | async-done | bytes 524320 | tf_op jit(solution)/shard_map/while/body/all_to_all | solution.py:27
  183.7 53.2 %while.133 = (s32[]{:T(128)}, bf16[16,128,128]{2,1,0:T(8,128)(2,1)S(1)}, bf16[16,128,128]{2,0,1:T(8,128)(2,1)}, bf16[16,128,128]{2,1,0:T(8,128)(2,1)}, bf16[16,1...) while((s32[]{:T(128)}, bf16[16,128,128]{2,1,0:T(8,128)(2,1)S(1)}, ...), condition=%wide.region_5.6_spmd, body=%wide.region_4.5_spmd.sunk | while | flops 274726912 | bytes 35127496 | solution.py:187
  185.7 11.7 %all_to_all.194 = bf16[8,16,16,128]{3,1,2,0:T(8,128)(2,1)S(1)} all-to-all(bf16[8,16,16,128]{3,1,2,0:T(8,128)(2,1)S(1)} %copy.483), channel_id=1, replica_groups=mesh['s'=4,'t'=4,'x'=2] {'s','x'}, dimensions={0} | all-to-all | bytes 1048576 | tf_op jit(solution)/shard_map/while/body/all_to_all | solution.py:27
  198.0 11.7 %all_to_all.195 = bf16[8,16,16,128]{3,1,2,0:T(8,128)(2,1)S(1)} all-to-all(bf16[8,16,16,128]{3,1,2,0:T(8,128)(2,1)S(1)} %copy.484), channel_id=1, replica_groups=mesh['s'=4,'t'=4,'x'=2] {'s','x'}, dimensions={0} | all-to-all | bytes 1048576 | tf_op jit(solution)/shard_map/while/body/all_to_all | solution.py:27
  210.6 11.7 %all_to_all.196 = bf16[8,16,16,128]{3,1,2,0:T(8,128)(2,1)S(1)} all-to-all(bf16[8,16,16,128]{3,1,2,0:T(8,128)(2,1)S(1)} %copy.485), channel_id=1, replica_groups=mesh['s'=4,'t'=4,'x'=2] {'s','x'}, dimensions={0} | all-to-all | bytes 1048576 | tf_op jit(solution)/shard_map/while/body/all_to_all | solution.py:27
  227.2 9.2 %all-to-all-done.7 = bf16[8,16,16,128]{3,1,2,0:T(8,128)(2,1)S(1)} async-done(((bf16[8,16,16,128]{3,1,2,0:T(8,128)(2,1)}), bf16[8,16,16,128]{3,1,2,0:T(8,128)(2,1)S(1)}, u32[]{:S(2)}, u32[]{:S(2)}) %all-to-all-start.7) | async-done | bytes 524320 | tf_op jit(solution)/shard_map/while/body/all_to_all | solution.py:27
  243.9 53.3 %while.134 = (s32[]{:T(128)}, bf16[16,128,128]{2,1,0:T(8,128)(2,1)S(1)}, bf16[16,128,128]{2,0,1:T(8,128)(2,1)}, bf16[16,128,128]{2,1,0:T(8,128)(2,1)}, bf16[16,1...) while((s32[]{:T(128)}, bf16[16,128,128]{2,1,0:T(8,128)(2,1)S(1)}, ...), condition=%wide.region_7.8_spmd, body=%wide.region_6.7_spmd.sunk | while | flops 274726912 | bytes 35127496 | solution.py:187
  245.9 11.7 %all_to_all.197 = bf16[8,16,16,128]{3,1,2,0:T(8,128)(2,1)S(1)} all-to-all(bf16[8,16,16,128]{3,1,2,0:T(8,128)(2,1)S(1)} %copy.491), channel_id=1, replica_groups=mesh['s'=4,'t'=4,'x'=2] {'s','x'}, dimensions={0} | all-to-all | bytes 1048576 | tf_op jit(solution)/shard_map/while/body/all_to_all | solution.py:27
  258.3 11.7 %all_to_all.198 = bf16[8,16,16,128]{3,1,2,0:T(8,128)(2,1)S(1)} all-to-all(bf16[8,16,16,128]{3,1,2,0:T(8,128)(2,1)S(1)} %copy.492), channel_id=1, replica_groups=mesh['s'=4,'t'=4,'x'=2] {'s','x'}, dimensions={0} | all-to-all | bytes 1048576 | tf_op jit(solution)/shard_map/while/body/all_to_all | solution.py:27
  270.8 11.7 %all_to_all.199 = bf16[8,16,16,128]{3,1,2,0:T(8,128)(2,1)S(1)} all-to-all(bf16[8,16,16,128]{3,1,2,0:T(8,128)(2,1)S(1)} %copy.493), channel_id=1, replica_groups=mesh['s'=4,'t'=4,'x'=2] {'s','x'}, dimensions={0} | all-to-all | bytes 1048576 | tf_op jit(solution)/shard_map/while/body/all_to_all | solution.py:27
  287.5 9.2 %all-to-all-done.11 = bf16[8,16,16,128]{3,1,2,0:T(8,128)(2,1)S(1)} async-done(((bf16[8,16,16,128]{3,1,2,0:T(8,128)(2,1)}), bf16[8,16,16,128]{3,1,2,0:T(8,128)(2,1)S(1)}, u32[]{:S(2)}, u32[]{:S(2)}) %all-to-all-start.11) | async-done | bytes 524320 | tf_op jit(solution)/shard_map/while/body/all_to_all | solution.py:27
  303.7 57.6 %while.135 = (s32[]{:T(128)}, bf16[16,128,128]{2,1,0:T(8,128)(2,1)}, bf16[16,128,128]{2,0,1:T(8,128)(2,1)}, bf16[16,128,128]{2,1,0:T(8,128)(2,1)}, bf16[16,128,1...) while((s32[]{:T(128)}, bf16[16,128,128]{2,1,0:T(8,128)(2,1)}, ...), condition=%wide.region_9.10_spmd, body=%wide.region_8.9_spmd.sunk | while | flops 274726912 | bytes 35127496 | solution.py:187
  305.6 11.7 %all_to_all.200 = bf16[8,16,16,128]{3,1,2,0:T(8,128)(2,1)S(1)} all-to-all(bf16[8,16,16,128]{3,1,2,0:T(8,128)(2,1)S(1)} %copy.499), channel_id=1, replica_groups=mesh['s'=4,'t'=4,'x'=2] {'s','x'}, dimensions={0} | all-to-all | bytes 1048576 | tf_op jit(solution)/shard_map/while/body/all_to_all | solution.py:27
  318.4 11.7 %all_to_all.201 = bf16[8,16,16,128]{3,1,2,0:T(8,128)(2,1)S(1)} all-to-all(bf16[8,16,16,128]{3,1,2,0:T(8,128)(2,1)S(1)} %copy.500), channel_id=1, replica_groups=mesh['s'=4,'t'=4,'x'=2] {'s','x'}, dimensions={0} | all-to-all | bytes 1048576 | tf_op jit(solution)/shard_map/while/body/all_to_all | solution.py:27
  331.9 11.7 %all_to_all.202 = bf16[8,16,16,128]{3,1,2,0:T(8,128)(2,1)S(1)} all-to-all(bf16[8,16,16,128]{3,1,2,0:T(8,128)(2,1)S(1)} %copy.501), channel_id=1, replica_groups=mesh['s'=4,'t'=4,'x'=2] {'s','x'}, dimensions={0} | all-to-all | bytes 1048576 | tf_op jit(solution)/shard_map/while/body/all_to_all | solution.py:27
  349.7 9.3 %all-to-all-done.15 = bf16[8,16,16,128]{3,1,2,0:T(8,128)(2,1)} async-done(((bf16[8,16,16,128]{3,1,2,0:T(8,128)(2,1)}), bf16[8,16,16,128]{3,1,2,0:T(8,128)(2,1)}, u32[]{:S(2)}, u32[]{:S(2)}) %all-to-all-start.15) | async-done | bytes 524320 | tf_op jit(solution)/shard_map/while/body/all_to_all | solution.py:27
  386.1 65.5 %while.136 = (s32[]{:T(128)}, bf16[16,128,128]{2,1,0:T(8,128)(2,1)S(1)}, bf16[4,4,4,128,128]{3,4,2,0,1:T(8,128)(2,1)}, s32[]{:T(128)}, bf16[4,2,2,4,128,128]{5,4...) while((s32[]{:T(128)}, ...), condition=%wide.region_11.12_spmd, body=%wide.region_10.11_spmd.sunk | while | flops 551026688 | bytes 51904876 | solution.py:214
  387.7 7.5 %all-to-all-start.16 = ((bf16[8,16,16,128]{3,2,1,0:T(8,128)(2,1)}), bf16[8,16,16,128]{3,2,1,0:T(8,128)(2,1)S(1)}, u32[]{:S(2)}, u32[]{:S(2)}) async-start(bf16[8,16,16,128]{3,2,1,0:T(8,128)(2,1)} %bitcast.1132), calls=%async_computation.16 | async-start | bytes 1048576 | tf_op jit(solution)/shard_map/while/body/all_to_all | solution.py:27
  397.9 6.6 all-to-all-done.16
  406.6 11.7 %all_to_all.203 = bf16[8,16,16,128]{3,1,2,0:T(8,128)(2,1)S(1)} all-to-all(bf16[8,16,16,128]{3,1,2,0:T(8,128)(2,1)S(1)} %copy.505), channel_id=1, replica_groups=mesh['s'=4,'t'=4,'x'=2] {'s','x'}, dimensions={0} | all-to-all | bytes 1048576 | tf_op jit(solution)/shard_map/while/body/all_to_all | solution.py:27
  441.9 6.1 all-to-all-done.19
  457.6 61.1 %while.137 = (s32[]{:T(128)}, bf16[16,128,128]{2,1,0:T(8,128)(2,1)S(1)}, bf16[4,4,4,128,128]{3,4,2,0,1:T(8,128)(2,1)}, s32[]{:T(128)}, bf16[4,2,2,4,128,128]{5,4...) while((s32[]{:T(128)}, ...), condition=%wide.region_13.14_spmd, body=%wide.region_12.13_spmd.sunk | while | flops 551026688 | bytes 51904876 | solution.py:214
  465.2 6.4 all-to-all-done.20
  473.7 11.7 %all_to_all.204 = bf16[8,16,16,128]{3,1,2,0:T(8,128)(2,1)S(1)} all-to-all(bf16[8,16,16,128]{3,1,2,0:T(8,128)(2,1)S(1)} %copy.515), channel_id=1, replica_groups=mesh['s'=4,'t'=4,'x'=2] {'s','x'}, dimensions={0} | all-to-all | bytes 1048576 | tf_op jit(solution)/shard_map/while/body/all_to_all | solution.py:27
  509.2 6.0 all-to-all-done.23
  527.7 61.2 %while.138 = (s32[]{:T(128)}, bf16[16,128,128]{2,1,0:T(8,128)(2,1)S(1)}, bf16[4,4,4,128,128]{3,4,2,0,1:T(8,128)(2,1)}, s32[]{:T(128)}, bf16[4,2,2,4,128,128]{5,4...) while((s32[]{:T(128)}, ...), condition=%wide.region_15.16_spmd, body=%wide.region_14.15_spmd.sunk | while | flops 551026688 | bytes 51904876 | solution.py:214
  535.4 6.4 all-to-all-done.24
  543.9 11.7 %all_to_all.205 = bf16[8,16,16,128]{3,1,2,0:T(8,128)(2,1)S(1)} all-to-all(bf16[8,16,16,128]{3,1,2,0:T(8,128)(2,1)S(1)} %copy.525), channel_id=1, replica_groups=mesh['s'=4,'t'=4,'x'=2] {'s','x'}, dimensions={0} | all-to-all | bytes 1048576 | tf_op jit(solution)/shard_map/while/body/all_to_all | solution.py:27
  579.3 6.0 all-to-all-done.27
  597.4 60.9 %while.139 = (s32[]{:T(128)}, bf16[16,128,128]{2,1,0:T(8,128)(2,1)S(1)}, bf16[4,4,4,128,128]{3,4,2,0,1:T(8,128)(2,1)}, s32[]{:T(128)}, bf16[4,1,2,4,128,128]{5,4...) while((s32[]{:T(128)}, ...), condition=%wide.region_18.19_spmd, body=%wide.region_17.18_spmd.sunk | while | flops 551026688 | bytes 43516164 | solution.py:214
  605.0 6.5 all-to-all-done.28
  613.2 11.7 %all_to_all.206 = bf16[8,16,16,128]{3,1,2,0:T(8,128)(2,1)S(1)} all-to-all(bf16[8,16,16,128]{3,1,2,0:T(8,128)(2,1)S(1)} %copy.535), channel_id=1, replica_groups=mesh['s'=4,'t'=4,'x'=2] {'s','x'}, dimensions={0} | all-to-all | bytes 1048576 | tf_op jit(solution)/shard_map/while/body/all_to_all | solution.py:27
  631.4 7.4 all-to-all-done.30
  676.9 6.4 collective-permute-start.26
  683.3 13.8 %collective-permute-start.25 = (bf16[4,128,128]{2,1,0:T(8,128)(2,1)S(1)}, bf16[4,128,128]{2,1,0:T(8,128)(2,1)S(1)}, u32[]{:S(2)}, u32[]{:S(2)}) collective-permute-start(bf16[4,128,128]{2,1,0:T(8,128)(2,1)S(1)} %bitcast.1463), channel_id=1, source_target_pairs={{0,2},{2,10},{4,18},{6,26},{8,0},{10,8},{12,16},{14,24},{16,6},{18... | collective-permute-start | bytes 393224 | tf_op jit(solution)/shard_map/ppermute | solution.py:76
  699.4 9.6 %collective-permute-start.32 = (bf16[2,4,128,128]{3,2,1,0:T(8,128)(2,1)S(1)}, bf16[2,4,128,128]{3,2,1,0:T(8,128)(2,1)S(1)}, u32[]{:S(2)}, u32[]{:S(2)}) collective-permute-start(bf16[2,4,128,128]{3,2,1,0:T(8,128)(2,1)S(1)} %pad_maximum_fusion.39), channel_id=1, source_target_pairs={{0,16},{8,24},{16,0},{24,8},{1,17},{9,25},{17,1},{25,9},{2,18},{10... | collective-permute-start | bytes 786440 | tf_op jit(solution)/shard_map/ppermute | solution.py:108
  712.6 7.8 %reduce-scatter.9.cloned.1.call-done = bf16[16,128,128]{2,1,0:T(8,128)(2,1)} async-done(((bf16[64,128,128]{2,1,0:T(8,128)(2,1)}), bf16[16,128,128]{2,1,0:T(8,128)(2,1)}) %reduce-scatter.9.cloned.1.call-update) | async-done | bytes 524304 | tf_op jit(solution)/shard_map/reduce_scatter | solution.py:138
  724.6 5.6 collective-permute-start.29
  731.5 8.6 %collective-permute-done.29 = bf16[2,4,128,128]{3,2,1,0:T(8,128)(2,1)S(1)} collective-permute-done((bf16[2,4,128,128]{3,2,1,0:T(8,128)(2,1)S(1)}, bf16[2,4,128,128]{3,2,1,0:T(8,128)(2,1)S(1)}, u32[]{:S(2)}, u32[]{:S(2)}) %collective-permute-start.29) | collective-permute-done | bytes 262176 | tf_op jit(solution)/shard_map/ppermute | solution.py:108
  (534 shorter events, 343.5 us)
Async XLA Ops:
  7.2 124.1 %all-gather.9.cloned.1.call-start = ((), (), s32[]{:S(2)}) async-start(), calls=%async_computation.40 | async-start | bytes 1310720 | tf_op jit(solution)/shard_map/all_gather | solution.py:122
  32.5 17.8 %collective-permute-start.11 = (bf16[4,128,128]{2,1,0:T(8,128)(2,1)S(1)}, bf16[4,128,128]{2,1,0:T(8,128)(2,1)S(1)}, u32[]{:S(2)}, u32[]{:S(2)}) collective-permute-start(bf16[4,128,128]{2,1,0:T(8,128)(2,1)S(1)} %get-tuple-element.989), channel_id=1, source_target_pairs={{0,4},{2,6},{4,0},{6,2},{1,5},{3,7},{5,1},{7,3},{8,12},{10,14},{12... | collective-permute-start | bytes 393224 | tf_op jit(solution)/shard_map/ppermute | solution.py:127
  32.5 17.8 %collective-permute-start.10 = (bf16[4,128,128]{2,1,0:T(8,128)(2,1)S(1)}, bf16[4,128,128]{2,1,0:T(8,128)(2,1)S(1)}, u32[]{:S(2)}, u32[]{:S(2)}) collective-permute-start(bf16[4,128,128]{2,1,0:T(8,128)(2,1)S(1)} %get-tuple-element.989), channel_id=1, source_target_pairs={{0,2},{2,0},{4,6},{6,4},{1,3},{3,1},{5,7},{7,5},{8,10},{10,8},{12,... | collective-permute-start | bytes 393224 | tf_op jit(solution)/shard_map/ppermute | solution.py:127
  33.1 17.2 %collective-permute-start.9 = (bf16[4,128,128]{2,1,0:T(8,128)(2,1)S(1)}, bf16[4,128,128]{2,1,0:T(8,128)(2,1)S(1)}, u32[]{:S(2)}, u32[]{:S(2)}) collective-permute-start(bf16[4,128,128]{2,1,0:T(8,128)(2,1)S(1)} %get-tuple-element.988), channel_id=1, source_target_pairs={{0,6},{2,4},{4,2},{6,0},{1,7},{3,5},{5,3},{7,1},{8,14},{10,12},{12... | collective-permute-start | bytes 393224 | tf_op jit(solution)/shard_map/ppermute | solution.py:127
  36.9 18.1 %collective-permute-start.8 = (bf16[4,128,128]{2,1,0:T(8,128)(2,1)S(1)}, bf16[4,128,128]{2,1,0:T(8,128)(2,1)S(1)}, u32[]{:S(2)}, u32[]{:S(2)}) collective-permute-start(bf16[4,128,128]{2,1,0:T(8,128)(2,1)S(1)} %get-tuple-element.988), channel_id=1, source_target_pairs={{0,4},{2,6},{4,0},{6,2},{1,5},{3,7},{5,1},{7,3},{8,12},{10,14},{12... | collective-permute-start | bytes 393224 | tf_op jit(solution)/shard_map/ppermute | solution.py:127
  36.9 18.1 %collective-permute-start.7 = (bf16[4,128,128]{2,1,0:T(8,128)(2,1)S(1)}, bf16[4,128,128]{2,1,0:T(8,128)(2,1)S(1)}, u32[]{:S(2)}, u32[]{:S(2)}) collective-permute-start(bf16[4,128,128]{2,1,0:T(8,128)(2,1)S(1)} %get-tuple-element.988), channel_id=1, source_target_pairs={{0,2},{2,0},{4,6},{6,4},{1,3},{3,1},{5,7},{7,5},{8,10},{10,8},{12,... | collective-permute-start | bytes 393224 | tf_op jit(solution)/shard_map/ppermute | solution.py:127
  55.5 116.2 %all-gather.11.cloned.1.call-start = ((), (), s32[]{:S(2)}) async-start(), calls=%async_computation.41 | async-start | bytes 2621440 | tf_op jit(solution)/shard_map/all_gather | solution.py:122
  57.1 33.1 %collective-permute-start.2 = (bf16[4,128,128]{1,2,0:T(8,128)(2,1)S(1)}, bf16[4,128,128]{1,2,0:T(8,128)(2,1)S(1)}, u32[]{:S(2)}, u32[]{:S(2)}) collective-permute-start(bf16[4,128,128]{1,2,0:T(8,128)(2,1)S(1)} %bitcast.1466), channel_id=1, source_target_pairs={{0,16},{2,24},{4,0},{6,8},{8,18},{10,26},{12,2},{14,10},{16,20},{1... | collective-permute-start | bytes 393224 | tf_op jit(solution)/shard_map/ppermute | solution.py:76
  58.4 31.7 %collective-permute-start.1 = (bf16[4,128,128]{1,2,0:T(8,128)(2,1)S(1)}, bf16[4,128,128]{1,2,0:T(8,128)(2,1)S(1)}, u32[]{:S(2)}, u32[]{:S(2)}) collective-permute-start(bf16[4,128,128]{1,2,0:T(8,128)(2,1)S(1)} %bitcast.1467), channel_id=1, source_target_pairs={{0,8},{2,0},{4,24},{6,16},{8,10},{10,2},{12,26},{14,18},{16,12},{1... | collective-permute-start | bytes 393224 | tf_op jit(solution)/shard_map/ppermute | solution.py:76
  58.6 31.5 %collective-permute-start = (bf16[4,128,128]{1,2,0:T(8,128)(2,1)S(1)}, bf16[4,128,128]{1,2,0:T(8,128)(2,1)S(1)}, u32[]{:S(2)}, u32[]{:S(2)}) collective-permute-start(bf16[4,128,128]{1,2,0:T(8,128)(2,1)S(1)} %bitcast.1469), channel_id=1, source_target_pairs={{0,0},{2,8},{4,16},{6,24},{8,2},{10,10},{12,18},{14,26},{16,4},{18... | collective-permute-start | bytes 393224 | tf_op jit(solution)/shard_map/ppermute | solution.py:76
  94.5 142.5 %all-gather.13.cloned.1.call-start = ((), (), s32[]{:S(2)}) async-start(), calls=%async_computation.42 | async-start | bytes 2621440 | tf_op jit(solution)/shard_map/all_gather | solution.py:122
  118.0 12.7 %all-to-all-start.1 = ((bf16[8,16,16,128]{3,1,2,0:T(8,128)(2,1)}), bf16[8,16,16,128]{3,1,2,0:T(8,128)(2,1)S(1)}, u32[]{:S(2)}, u32[]{:S(2)}) async-start(bf16[8,16,16,128]{3,1,2,0:T(8,128)(2,1)} %copy.474), calls=%async_computation.1 | async-start | bytes 1048576 | tf_op jit(solution)/shard_map/while/body/all_to_all | solution.py:27
  135.5 36.1 %collective-permute-start.13 = (bf16[2,4,128,128]{2,3,1,0:T(8,128)(2,1)S(1)}, bf16[2,4,128,128]{2,3,1,0:T(8,128)(2,1)}, u32[]{:S(2)}, u32[]{:S(2)}) collective-permute-start(bf16[2,4,128,128]{2,3,1,0:T(8,128)(2,1)S(1)} %pad_maximum_fusion.32), channel_id=1, source_target_pairs={{0,8},{8,0},{16,24},{24,16},{1,9},{9,1},{17,25},{25,17},{2,10},{10... | collective-permute-start | bytes 786440 | tf_op jit(solution)/shard_map/ppermute | solution.py:108
  136.6 35.1 %collective-permute-start.14 = (bf16[2,4,128,128]{2,3,1,0:T(8,128)(2,1)}, bf16[2,4,128,128]{2,3,1,0:T(8,128)(2,1)}, u32[]{:S(2)}, u32[]{:S(2)}) collective-permute-start(bf16[2,4,128,128]{2,3,1,0:T(8,128)(2,1)} %pad_maximum_fusion.33), channel_id=1, source_target_pairs={{0,16},{8,24},{16,0},{24,8},{1,17},{9,25},{17,1},{25,9},{2,18},{10... | collective-permute-start | bytes 786440 | tf_op jit(solution)/shard_map/ppermute | solution.py:108
  138.1 33.5 %collective-permute-start.15 = (bf16[2,4,128,128]{2,3,1,0:T(8,128)(2,1)S(1)}, bf16[2,4,128,128]{2,3,1,0:T(8,128)(2,1)}, u32[]{:S(2)}, u32[]{:S(2)}) collective-permute-start(bf16[2,4,128,128]{2,3,1,0:T(8,128)(2,1)S(1)} %pad_maximum_fusion.34), channel_id=1, source_target_pairs={{0,24},{8,16},{16,8},{24,0},{1,25},{9,17},{17,9},{25,1},{2,26},{10... | collective-permute-start | bytes 786440 | tf_op jit(solution)/shard_map/ppermute | solution.py:108
  158.2 12.7 %all-to-all-start.3 = ((bf16[8,16,16,128]{3,1,2,0:T(8,128)(2,1)}), bf16[8,16,16,128]{3,1,2,0:T(8,128)(2,1)S(1)}, u32[]{:S(2)}, u32[]{:S(2)}) async-start(bf16[8,16,16,128]{3,1,2,0:T(8,128)(2,1)} %copy.478), calls=%async_computation.3 | async-start | bytes 1048576 | tf_op jit(solution)/shard_map/while/body/all_to_all | solution.py:27
  174.9 122.3 %all-gather.15.cloned.1.call-start = ((), (), s32[]{:S(2)}) async-start(), calls=%async_computation.43 | async-start | bytes 2621440 | tf_op jit(solution)/shard_map/all_gather | solution.py:122
  180.9 342.1 %reduce-scatter.5.cloned.1.call-start = ((), (), s32[]{:S(2)}) async-start(), calls=%async_computation.36 | async-start | bytes 2621440 | tf_op jit(solution)/shard_map/reduce_scatter | solution.py:138
  223.7 12.7 %all-to-all-start.7 = ((bf16[8,16,16,128]{3,1,2,0:T(8,128)(2,1)}), bf16[8,16,16,128]{3,1,2,0:T(8,128)(2,1)S(1)}, u32[]{:S(2)}, u32[]{:S(2)}) async-start(bf16[8,16,16,128]{3,1,2,0:T(8,128)(2,1)} %copy.486), calls=%async_computation.7 | async-start | bytes 1048576 | tf_op jit(solution)/shard_map/while/body/all_to_all | solution.py:27
  284.0 12.7 %all-to-all-start.11 = ((bf16[8,16,16,128]{3,1,2,0:T(8,128)(2,1)}), bf16[8,16,16,128]{3,1,2,0:T(8,128)(2,1)S(1)}, u32[]{:S(2)}, u32[]{:S(2)}) async-start(bf16[8,16,16,128]{3,1,2,0:T(8,128)(2,1)} %copy.494), calls=%async_computation.11 | async-start | bytes 1048576 | tf_op jit(solution)/shard_map/while/body/all_to_all | solution.py:27
  345.5 13.4 %all-to-all-start.15 = ((bf16[8,16,16,128]{3,1,2,0:T(8,128)(2,1)}), bf16[8,16,16,128]{3,1,2,0:T(8,128)(2,1)}, u32[]{:S(2)}, u32[]{:S(2)}) async-start(bf16[8,16,16,128]{3,1,2,0:T(8,128)(2,1)} %copy.502), calls=%async_computation.15 | async-start | bytes 1048576 | tf_op jit(solution)/shard_map/while/body/all_to_all | solution.py:27
  362.7 15.9 %collective-permute-start.23 = (bf16[4,128,128]{1,2,0:T(8,128)(2,1)S(1)}, bf16[4,128,128]{1,2,0:T(8,128)(2,1)S(1)}, u32[]{:S(2)}, u32[]{:S(2)}) collective-permute-start(bf16[4,128,128]{1,2,0:T(8,128)(2,1)S(1)} %bitcast.1468), channel_id=1, source_target_pairs={{0,24},{2,16},{4,8},{6,0},{8,26},{10,18},{12,10},{14,2},{16,28},{1... | collective-permute-start | bytes 393224 | tf_op jit(solution)/shard_map/ppermute | solution.py:76
  363.3 19.1 %collective-permute-start.22 = (bf16[4,128,128]{1,2,0:T(8,128)(2,1)S(1)}, bf16[4,128,128]{1,2,0:T(8,128)(2,1)S(1)}, u32[]{:S(2)}, u32[]{:S(2)}) collective-permute-start(bf16[4,128,128]{1,2,0:T(8,128)(2,1)S(1)} %bitcast.1470), channel_id=1, source_target_pairs={{0,16},{2,24},{4,0},{6,8},{8,18},{10,26},{12,2},{14,10},{16,20},{1... | collective-permute-start | bytes 393224 | tf_op jit(solution)/shard_map/ppermute | solution.py:76
  363.6 18.9 %collective-permute-start.21 = (bf16[4,128,128]{1,2,0:T(8,128)(2,1)S(1)}, bf16[4,128,128]{1,2,0:T(8,128)(2,1)}, u32[]{:S(2)}, u32[]{:S(2)}) collective-permute-start(bf16[4,128,128]{1,2,0:T(8,128)(2,1)S(1)} %bitcast.1471), channel_id=1, source_target_pairs={{0,8},{2,0},{4,24},{6,16},{8,10},{10,2},{12,26},{14,18},{16,12},{1... | collective-permute-start | bytes 393224 | tf_op jit(solution)/shard_map/ppermute | solution.py:76
  363.8 18.7 %collective-permute-start.20 = (bf16[4,128,128]{1,2,0:T(8,128)(2,1)S(1)}, bf16[4,128,128]{1,2,0:T(8,128)(2,1)S(1)}, u32[]{:S(2)}, u32[]{:S(2)}) collective-permute-start(bf16[4,128,128]{1,2,0:T(8,128)(2,1)S(1)} %bitcast.1472), channel_id=1, source_target_pairs={{0,0},{2,8},{4,16},{6,24},{8,2},{10,10},{12,18},{14,26},{16,4},{18... | collective-permute-start | bytes 393224 | tf_op jit(solution)/shard_map/ppermute | solution.py:76
  387.7 16.8 %all-to-all-start.16 = ((bf16[8,16,16,128]{3,2,1,0:T(8,128)(2,1)}), bf16[8,16,16,128]{3,2,1,0:T(8,128)(2,1)S(1)}, u32[]{:S(2)}, u32[]{:S(2)}) async-start(bf16[8,16,16,128]{3,2,1,0:T(8,128)(2,1)} %bitcast.1132), calls=%async_computation.16 | async-start | bytes 1048576 | tf_op jit(solution)/shard_map/while/body/all_to_all | solution.py:27
  419.5 12.7 %all-to-all-start.18 = ((bf16[8,16,16,128]{3,1,2,0:T(8,128)(2,1)}), bf16[8,16,16,128]{3,1,2,0:T(8,128)(2,1)S(1)}, u32[]{:S(2)}, u32[]{:S(2)}) async-start(bf16[8,16,16,128]{3,1,2,0:T(8,128)(2,1)} %copy.507), calls=%async_computation.18 | async-start | bytes 1048576 | tf_op jit(solution)/shard_map/while/body/all_to_all | solution.py:27
  435.3 12.7 %all-to-all-start.19 = ((bf16[8,16,16,128]{3,2,1,0:T(8,128)(2,1)}), bf16[8,16,16,128]{3,2,1,0:T(8,128)(2,1)S(1)}, u32[]{:S(2)}, u32[]{:S(2)}) async-start(bf16[8,16,16,128]{3,2,1,0:T(8,128)(2,1)} %copy.509), calls=%async_computation.19 | async-start | bytes 1048576 | tf_op jit(solution)/shard_map/while/body/all_to_all | solution.py:27
  455.7 133.2 %reduce-scatter.7.cloned.1.call-start = ((), (), s32[]{:S(2)}) async-start(), calls=%async_computation.37 | async-start | bytes 2621440 | tf_op jit(solution)/shard_map/reduce_scatter | solution.py:138
  486.7 12.7 %all-to-all-start.22 = ((bf16[8,16,16,128]{3,1,2,0:T(8,128)(2,1)}), bf16[8,16,16,128]{3,1,2,0:T(8,128)(2,1)S(1)}, u32[]{:S(2)}, u32[]{:S(2)}) async-start(bf16[8,16,16,128]{3,1,2,0:T(8,128)(2,1)} %copy.517), calls=%async_computation.22 | async-start | bytes 1048576 | tf_op jit(solution)/shard_map/while/body/all_to_all | solution.py:27
  502.5 12.7 %all-to-all-start.23 = ((bf16[8,16,16,128]{3,2,1,0:T(8,128)(2,1)}), bf16[8,16,16,128]{3,2,1,0:T(8,128)(2,1)S(1)}, u32[]{:S(2)}, u32[]{:S(2)}) async-start(bf16[8,16,16,128]{3,2,1,0:T(8,128)(2,1)} %copy.519), calls=%async_computation.23 | async-start | bytes 1048576 | tf_op jit(solution)/shard_map/while/body/all_to_all | solution.py:27
  522.9 188.0 %reduce-scatter.11.cloned.1.call-start = ((), (), s32[]{:S(2)}) async-start(), calls=%async_computation.39 | async-start | bytes 2621440 | tf_op jit(solution)/shard_map/reduce_scatter | solution.py:138
  529.1 12.7 %all-to-all-start.24 = ((bf16[8,16,16,128]{3,2,1,0:T(8,128)(2,1)}), bf16[8,16,16,128]{3,2,1,0:T(8,128)(2,1)S(1)}, u32[]{:S(2)}, u32[]{:S(2)}) async-start(bf16[8,16,16,128]{3,2,1,0:T(8,128)(2,1)} %bitcast.1212), calls=%async_computation.24 | async-start | bytes 1048576 | tf_op jit(solution)/shard_map/while/body/all_to_all | solution.py:27
  556.8 12.7 %all-to-all-start.26 = ((bf16[8,16,16,128]{3,1,2,0:T(8,128)(2,1)}), bf16[8,16,16,128]{3,1,2,0:T(8,128)(2,1)S(1)}, u32[]{:S(2)}, u32[]{:S(2)}) async-start(bf16[8,16,16,128]{3,1,2,0:T(8,128)(2,1)} %copy.527), calls=%async_computation.26 | async-start | bytes 1048576 | tf_op jit(solution)/shard_map/while/body/all_to_all | solution.py:27
  572.6 12.7 %all-to-all-start.27 = ((bf16[8,16,16,128]{3,2,1,0:T(8,128)(2,1)}), bf16[8,16,16,128]{3,2,1,0:T(8,128)(2,1)S(1)}, u32[]{:S(2)}, u32[]{:S(2)}) async-start(bf16[8,16,16,128]{3,2,1,0:T(8,128)(2,1)} %copy.529), calls=%async_computation.27 | async-start | bytes 1048576 | tf_op jit(solution)/shard_map/while/body/all_to_all | solution.py:27
  595.5 124.9 %reduce-scatter.9.cloned.1.call-start = ((), (), s32[]{:S(2)}) async-start(), calls=%async_computation.38 | async-start | bytes 2621440 | tf_op jit(solution)/shard_map/reduce_scatter | solution.py:138
  598.8 12.7 %all-to-all-start.28 = ((bf16[8,16,16,128]{3,2,1,0:T(8,128)(2,1)}), bf16[8,16,16,128]{3,2,1,0:T(8,128)(2,1)S(1)}, u32[]{:S(2)}, u32[]{:S(2)}) async-start(bf16[8,16,16,128]{3,2,1,0:T(8,128)(2,1)} %bitcast.1252), calls=%async_computation.28 | async-start | bytes 1048576 | tf_op jit(solution)/shard_map/while/body/all_to_all | solution.py:27
  626.2 12.7 %all-to-all-start.30 = ((bf16[8,16,16,128]{3,1,2,0:T(8,128)(2,1)}), bf16[8,16,16,128]{3,1,2,0:T(8,128)(2,1)S(1)}, u32[]{:S(2)}, u32[]{:S(2)}) async-start(bf16[8,16,16,128]{3,1,2,0:T(8,128)(2,1)} %copy.537), calls=%async_computation.30 | async-start | bytes 1048576 | tf_op jit(solution)/shard_map/while/body/all_to_all | solution.py:27
  667.8 15.5 %collective-permute-start.18 = (bf16[4,128,128]{2,1,0:T(8,128)(2,1)}, bf16[4,128,128]{2,1,0:T(8,128)(2,1)}, u32[]{:S(2)}, u32[]{:S(2)}) collective-permute-start(bf16[4,128,128]{2,1,0:T(8,128)(2,1)} %bitcast.275), channel_id=1, source_target_pairs={{0,4},{2,12},{4,20},{6,28},{8,6},{10,14},{12,22},{14,30},{16,0},{1... | collective-permute-start | bytes 393224 | tf_op jit(solution)/shard_map/ppermute | solution.py:76
  668.5 28.6 %collective-permute-start.17 = (bf16[4,128,128]{2,1,0:T(8,128)(2,1)S(1)}, bf16[4,128,128]{2,1,0:T(8,128)(2,1)}, u32[]{:S(2)}, u32[]{:S(2)}) collective-permute-start(bf16[4,128,128]{2,1,0:T(8,128)(2,1)S(1)} %bitcast.1461), channel_id=1, source_target_pairs={{0,2},{2,10},{4,18},{6,26},{8,0},{10,8},{12,16},{14,24},{16,6},{18... | collective-permute-start | bytes 393224 | tf_op jit(solution)/shard_map/ppermute | solution.py:76
  668.7 29.3 %collective-permute-start.16 = (bf16[4,128,128]{2,1,0:T(8,128)(2,1)S(1)}, bf16[4,128,128]{2,1,0:T(8,128)(2,1)}, u32[]{:S(2)}, u32[]{:S(2)}) collective-permute-start(bf16[4,128,128]{2,1,0:T(8,128)(2,1)S(1)} %bitcast.1460), channel_id=1, source_target_pairs={{0,0},{2,8},{4,16},{6,24},{8,2},{10,10},{12,18},{14,26},{16,4},{18... | collective-permute-start | bytes 393224 | tf_op jit(solution)/shard_map/ppermute | solution.py:76
  670.2 29.2 %collective-permute-start.27 = (bf16[4,128,128]{2,1,0:T(8,128)(2,1)S(1)}, bf16[4,128,128]{2,1,0:T(8,128)(2,1)}, u32[]{:S(2)}, u32[]{:S(2)}) collective-permute-start(bf16[4,128,128]{2,1,0:T(8,128)(2,1)S(1)} %bitcast.1459), channel_id=1, source_target_pairs={{0,6},{2,14},{4,22},{6,30},{8,4},{10,12},{12,20},{14,28},{16,2},{1... | collective-permute-start | bytes 393224 | tf_op jit(solution)/shard_map/ppermute | solution.py:76
  676.9 32.1 %collective-permute-start.26 = (bf16[4,128,128]{2,1,0:T(8,128)(2,1)S(1)}, bf16[4,128,128]{2,1,0:T(8,128)(2,1)S(1)}, u32[]{:S(2)}, u32[]{:S(2)}) collective-permute-start(bf16[4,128,128]{2,1,0:T(8,128)(2,1)S(1)} %bitcast.1464), channel_id=1, source_target_pairs={{0,4},{2,12},{4,20},{6,28},{8,6},{10,14},{12,22},{14,30},{16,0},{1... | collective-permute-start | bytes 393224 | tf_op jit(solution)/shard_map/ppermute | solution.py:76
  683.3 25.7 %collective-permute-start.25 = (bf16[4,128,128]{2,1,0:T(8,128)(2,1)S(1)}, bf16[4,128,128]{2,1,0:T(8,128)(2,1)S(1)}, u32[]{:S(2)}, u32[]{:S(2)}) collective-permute-start(bf16[4,128,128]{2,1,0:T(8,128)(2,1)S(1)} %bitcast.1463), channel_id=1, source_target_pairs={{0,2},{2,10},{4,18},{6,26},{8,0},{10,8},{12,16},{14,24},{16,6},{18... | collective-permute-start | bytes 393224 | tf_op jit(solution)/shard_map/ppermute | solution.py:76
  698.1 32.2 %collective-permute-start.33 = (bf16[2,4,128,128]{3,2,1,0:T(8,128)(2,1)}, bf16[2,4,128,128]{3,2,1,0:T(8,128)(2,1)S(1)}, u32[]{:S(2)}, u32[]{:S(2)}) collective-permute-start(bf16[2,4,128,128]{3,2,1,0:T(8,128)(2,1)} %pad_maximum_fusion.40), channel_id=1, source_target_pairs={{0,24},{8,16},{16,8},{24,0},{1,25},{9,17},{17,9},{25,1},{2,26},{10... | collective-permute-start | bytes 786440 | tf_op jit(solution)/shard_map/ppermute | solution.py:108
  699.4 31.9 %collective-permute-start.32 = (bf16[2,4,128,128]{3,2,1,0:T(8,128)(2,1)S(1)}, bf16[2,4,128,128]{3,2,1,0:T(8,128)(2,1)S(1)}, u32[]{:S(2)}, u32[]{:S(2)}) collective-permute-start(bf16[2,4,128,128]{3,2,1,0:T(8,128)(2,1)S(1)} %pad_maximum_fusion.39), channel_id=1, source_target_pairs={{0,16},{8,24},{16,0},{24,8},{1,17},{9,25},{17,1},{25,9},{2,18},{10... | collective-permute-start | bytes 786440 | tf_op jit(solution)/shard_map/ppermute | solution.py:108
  709.0 22.3 %collective-permute-start.31 = (bf16[2,4,128,128]{3,2,1,0:T(8,128)(2,1)S(1)}, bf16[2,4,128,128]{3,2,1,0:T(8,128)(2,1)S(1)}, u32[]{:S(2)}, u32[]{:S(2)}) collective-permute-start(bf16[2,4,128,128]{3,2,1,0:T(8,128)(2,1)S(1)} %pad_maximum_fusion.38), channel_id=1, source_target_pairs={{0,8},{8,0},{16,24},{24,16},{1,9},{9,1},{17,25},{25,17},{2,10},{10... | collective-permute-start | bytes 786440 | tf_op jit(solution)/shard_map/ppermute | solution.py:108
  724.6 15.4 %collective-permute-start.29 = (bf16[2,4,128,128]{3,2,1,0:T(8,128)(2,1)S(1)}, bf16[2,4,128,128]{3,2,1,0:T(8,128)(2,1)S(1)}, u32[]{:S(2)}, u32[]{:S(2)}) collective-permute-start(bf16[2,4,128,128]{3,2,1,0:T(8,128)(2,1)S(1)} %pad_maximum_fusion.36), channel_id=1, source_target_pairs={{0,16},{8,24},{16,0},{24,8},{1,17},{9,25},{17,1},{25,9},{2,18},{10... | collective-permute-start | bytes 786440 | tf_op jit(solution)/shard_map/ppermute | solution.py:108
  (74 other events, 793.0 us)
Sparse Core Ops, SparseCore 0:
  55.6 40.8 all-gather.8
  98.6 48.8 all-gather.10
  175.0 44.1 all-gather.12
  221.3 44.6 all-gather.14
  455.9 41.5 reduce-scatter.4
  523.0 41.5 reduce-scatter.6
  595.6 41.5 reduce-scatter.10
  662.6 57.7 reduce-scatter.8
